TPU v7x, 32 devices: a whole 2x2x4 slice. The times are simulated.
32 devices in a mesh: groups: 2 (over y), lib: 4 (over x, core), qry: 4 (over z).
Axes of the slice: x: 2, y: 2, z: 4, core: 2. Of those that a mesh axis runs over, the one named last changes fastest.
Arguments:
- queries: bfloat16 [4096, 1024], P(('groups', 'lib', 'qry')), parts along dimension 0, may hold values from -24 to 24
- library_keys: bfloat16 [4096, 1024], P(('groups', 'lib', 'qry')), parts along dimension 0, may hold values from -6 to 6
- library_values: bfloat16 [4096, 512], P(('groups', 'lib', 'qry')), parts along dimension 0, may hold values from -6 to 6
- key_scale: bfloat16 [4096], P(('groups', 'lib', 'qry')), parts along dimension 0, may hold values from 0.29 to 3.1
- block_list: int32 [32, 4], P('groups'), parts along dimension 0, may hold values from 0 to 15, as said below
- block_count: int32 [32], P('groups'), parts along dimension 0, may hold values from 1 to 4, as said below
Outputs:
- retrieved: bfloat16 [4096, 512], P(('groups', 'lib', 'qry')), parts along dimension 0
There are 2 independent parts, one for each index of `groups`. A program takes and returns all parts, laid end to end along the dimension named above; each array names one. Nothing has to cross between parts.
Inputs may be any that keep to these rules, and one draw needn't show every extreme that they name: Row p holds block_list[p, 0] + k modulo 16 at position k (a run of consecutive blocks, all distinct); only the first block_count[p] are active. `block_count`: at least one panel has exactly 4.
All inputs are finite; a program needn't handle non-finite values.
Results may differ from a plain program's by a relative error of at most 0.004.
Values may be sent and summed in bfloat16 or wider, within the bound.
No kernel may reach another device: no remote copies, remote signals or barrier semaphores. Data moves between devices by JAX's collectives and lax.ppermute only.
A program may use at most 64 MiB of HBM per device.

v0:
```python
import math

import jax
import jax.numpy as jnp
from jax import lax
from jax.sharding import PartitionSpec as P

TILE = 128


MASKED_SCORE = -1e30


def from_behind(value, axis, by):
    length = lax.axis_size(axis)
    return lax.ppermute(value, axis, [(i, (i + by) % length) for i in range(length)])


def window_flags(block_list, block_count, first_panel, panel_count, tile_ids):
    window_lists = lax.dynamic_slice_in_dim(block_list, first_panel, panel_count, 0)
    window_counts = lax.dynamic_slice_in_dim(block_count, first_panel, panel_count, 0)
    in_window = jnp.arange(window_lists.shape[1], dtype=jnp.int32)[None, :] < window_counts[:, None]
    matches = (window_lists[:, :, None] == tile_ids[None, None, :]) & in_window[:, :, None]
    return jnp.any(matches, axis=1)


def tile_update(carried, query_rows, tile_keys, tile_scale, tile_values, active_tiles):
    running_max, running_sum, weighted = carried
    query_count = query_rows.shape[0]
    key_count = tile_keys.shape[0]
    panel_count, tile_count = active_tiles.shape
    active_rows = jnp.broadcast_to(
        active_tiles[:, None, :, None],
        (panel_count, query_count // panel_count, tile_count, key_count // tile_count),
    ).reshape(query_count, key_count)
    inverse_root = 1.0 / math.sqrt(query_rows.shape[1])
    scores = lax.dot_general(
        query_rows, tile_keys, (((1,), (1,)), ((), ())), preferred_element_type=jnp.float32
    )
    scores = scores * (tile_scale.astype(jnp.float32) * inverse_root)[None, :]
    scores = jnp.where(active_rows, scores, MASKED_SCORE)
    new_max = jnp.maximum(running_max, jnp.max(scores, axis=1))
    weights = jnp.where(active_rows, jnp.exp(scores - new_max[:, None]), 0.0)
    shrink = jnp.exp(running_max - new_max)
    running_sum = running_sum * shrink + jnp.sum(weights, axis=1)
    weight_high = weights.astype(jnp.bfloat16)
    weight_low = (weights - weight_high.astype(jnp.float32)).astype(jnp.bfloat16)
    added = jnp.dot(weight_high, tile_values, preferred_element_type=jnp.float32)
    added = added + jnp.dot(weight_low, tile_values, preferred_element_type=jnp.float32)
    weighted = weighted * shrink[:, None] + added
    return (new_max, running_sum, weighted)


def attend(carried, query_rows, first_panel, column, tile_ids, block_list, block_count):
    column_keys, column_values, column_scale = column
    panel_total = query_rows.shape[0] // TILE
    active_tiles = window_flags(block_list, block_count, first_panel, panel_total, tile_ids)
    return tile_update(carried, query_rows, column_keys, column_scale, column_values, active_tiles)


def body(queries, library_keys, library_values, key_scale, block_list, block_count):
    lib_index = lax.axis_index("lib")
    qry_index = lax.axis_index("qry")
    qry_count = lax.axis_size("qry")
    lib_count = lax.axis_size("lib")
    column = (
        lax.all_gather(library_keys, "lib", axis=0, tiled=True),
        lax.all_gather(library_values, "lib", axis=0, tiled=True),
        lax.all_gather(key_scale, "lib", axis=0, tiled=True),
    )
    per_device = library_keys.shape[0] // TILE
    position = jnp.arange(lib_count * per_device, dtype=jnp.int32)
    tile_ids = (position // per_device * qry_count + qry_index) * per_device + position % per_device
    query_count = queries.shape[0]
    value_width = library_values.shape[1]
    panels_here = query_count // TILE
    fresh = (
        jnp.full((query_count,), MASKED_SCORE, jnp.float32),
        jnp.zeros((query_count,), jnp.float32),
        jnp.zeros((query_count, value_width), jnp.float32),
    )

    def visit(step, carried):
        panel, partial_value = carried
        source = (qry_index - step) % qry_count
        first_panel = (lib_index * qry_count + source) * panels_here
        partial_value = attend(
            partial_value, panel, first_panel, column, tile_ids, block_list, block_count
        )
        partial_value = from_behind(
            (partial_value[0], partial_value[1], partial_value[2]), "qry", 1
        )
        panel = from_behind(panel, "qry", 1)
        return (panel, partial_value)

    moved, final = lax.fori_loop(0, qry_count, visit, (queries, fresh))
    running_max, running_sum, weighted = final
    return (weighted / running_sum[:, None]).astype(jnp.bfloat16)


def solution(mesh):
    in_specs = (
        P(("groups", "lib", "qry"), None),
        P(("groups", "lib", "qry"), None),
        P(("groups", "lib", "qry"), None),
        P(("groups", "lib", "qry")),
        P("groups", None),
        P("groups"),
    )
    out_specs = P(("groups", "lib", "qry"), None)
    return jax.shard_map(body, mesh=mesh, in_specs=in_specs, out_specs=out_specs, check_vma=False)
```

profile of v0, /device:TPU:0, one launch (start us, length us, event | category | flops | bytes accessed | tf_op | source)
XLA Modules:
  0.0 112.4 jit_solution(14631812113009457531)
XLA Ops:
  6.5 0.7 all-gather.3.cloned.1.call-update
  7.3 0.7 copy-done.2
  8.0 0.7 copy-done.3
  8.7 5.9 %all-gather = bf16[4,1,128]{2,1,0:T(2,128)(2,1)S(1)} all-gather(bf16[1,1,128]{2,1,0:T(2,128)(2,1)S(1)} %bitcast.26), channel_id=1, replica_groups=mesh['groups'=2,'lib'=4,'qry'=4] {'lib'}, dimensions={0}, use_global_device_ids=true | all-gather | bytes 1280 | tf_op jit(solution)/shard_map/all_gather | solution.py:69
  14.6 8.1 %all_gather.11 = bf16[512,512]{1,0:T(8,128)(2,1)S(1)} all-gather(bf16[128,512]{1,0:T(8,128)(2,1)S(1)} %copy-done.1), channel_id=1, replica_groups=mesh['groups'=2,'lib'=4,'qry'=4] {'lib'}, dimensions={0}, use_global_device_ids=true | all-gather | bytes 655360 | tf_op jit(solution)/shard_map/all_gather | solution.py:68
  22.8 5.8 %all-gather.3.cloned.1.call-done = bf16[512,1024]{1,0:T(8,128)(2,1)} async-done(((bf16[128,1024]{1,0:T(8,128)(2,1)}), bf16[512,1024]{1,0:T(8,128)(2,1)}) %all-gather.3.cloned.1.call-update) | async-done | bytes 1048592 | tf_op jit(solution)/shard_map/all_gather | solution.py:67
  29.3 75.5 %while.23 = (s32[]{:T(128)}, bf16[128,1024]{1,0:T(8,128)(2,1)S(1)}, f32[128]{0:T(128)S(1)}, f32[128]{0:T(128)S(1)}, f32[128,512]{1,0:T(8,128)S(1)}, /*index=5*/s...) while((s32[]{:T(128)}, bf16[128,1024]{1,0:T(8,128)(2,1)S(1)}, ...), condition=%wide.region_4.5_spmd.clone.clone, body=%wide.region_0.4_spmd.clone.clone.sunk | while | flops 269616448 | bytes 7097948 | solution.py:96
  29.3 0.6 dynamic_slice.32
  29.9 0.6 iota_compare_fusion.2
  30.7 1.8 %fusion.35 = (f32[128]{0:T(128)S(1)}, f32[128,512]{1,0:T(8,128)S(1)}) fusion(f32[512]{0:T(512)S(1)} %convert_multiply_fusion.2, bf16[128,1024]{1,0:T(8,128)(2,1)S(1)} %copy.17, bf16[512,1024]{1,0:T(8,128)(2,1)} %get-tuple-element.576, pred[512]{0:T(512)(128)(4,1)S(1)} %broadcast_bitcast_fusion.2), kind=kOutput, calls=%fused_computation.27.clone.1 | convolution fusion | flops 134414208 | bytes 1575936 | tf_op jit(solution)/shard_map/while/body/eval_jaxpr/dot_general | solution.py:37
  33.3 1.7 %collective-permute-start.3 = (f32[128,512]{1,0:T(8,128)S(1)}, f32[128,512]{1,0:T(8,128)S(1)}, u32[]{:S(2)}, u32[]{:S(2)}) collective-permute-start(f32[128,512]{1,0:T(8,128)S(1)} %fusion.38), channel_id=1, source_target_pairs={{0,1},{1,2},{2,3},{3,0},{4,5},{5,6},{6,7},{7,4},{8,9},{9,10},{10,1... | collective-permute-start | bytes 786440 | tf_op jit(solution)/shard_map/while/body/eval_jaxpr/ppermute | solution.py:16
  35.1 1.6 %collective-permute-start = (bf16[128,1024]{1,0:T(8,128)(2,1)S(1)}, bf16[128,1024]{1,0:T(8,128)(2,1)S(1)}, u32[]{:S(2)}, u32[]{:S(2)}) collective-permute-start(bf16[128,1024]{1,0:T(8,128)(2,1)S(1)} %copy.17), channel_id=1, source_target_pairs={{0,1},{1,2},{2,3},{3,0},{4,5},{5,6},{6,7},{7,4},{8,9},{9,10},{10,1... | collective-permute-start | bytes 786440 | tf_op jit(solution)/shard_map/while/body/eval_jaxpr/ppermute | solution.py:16
  36.6 1.6 %collective-permute-start.1 = (f32[128]{0:T(128)S(1)}, f32[128]{0:T(128)S(1)}, u32[]{:S(2)}, u32[]{:S(2)}) collective-permute-start(f32[128]{0:T(128)S(1)} %max.13), channel_id=1, source_target_pairs={{0,1},{1,2},{2,3},{3,0},{4,5},{5,6},{6,7},{7,4},{8,9},{9,10},{10,1... | collective-permute-start | bytes 1544 | tf_op jit(solution)/shard_map/while/body/eval_jaxpr/ppermute | solution.py:16
  38.4 11.1 %collective-permute-done.1 = f32[128]{0:T(128)S(1)} collective-permute-done((f32[128]{0:T(128)S(1)}, f32[128]{0:T(128)S(1)}, u32[]{:S(2)}, u32[]{:S(2)}) %collective-permute-start.1) | collective-permute-done | bytes 544 | tf_op jit(solution)/shard_map/while/body/eval_jaxpr/ppermute | solution.py:16
  49.5 0.6 dynamic_slice.32
  50.2 0.6 iota_compare_fusion.2
  51.0 1.8 %fusion.35 = (f32[128]{0:T(128)S(1)}, f32[128,512]{1,0:T(8,128)S(1)}) fusion(f32[512]{0:T(512)S(1)} %convert_multiply_fusion.2, bf16[128,1024]{1,0:T(8,128)(2,1)S(1)} %copy.17, bf16[512,1024]{1,0:T(8,128)(2,1)} %get-tuple-element.576, pred[512]{0:T(512)(128)(4,1)S(1)} %broadcast_bitcast_fusion.2), kind=kOutput, calls=%fused_computation.27.clone.1 | convolution fusion | flops 134414208 | bytes 1575936 | tf_op jit(solution)/shard_map/while/body/eval_jaxpr/dot_general | solution.py:37
  53.7 1.3 %collective-permute-start = (bf16[128,1024]{1,0:T(8,128)(2,1)S(1)}, bf16[128,1024]{1,0:T(8,128)(2,1)S(1)}, u32[]{:S(2)}, u32[]{:S(2)}) collective-permute-start(bf16[128,1024]{1,0:T(8,128)(2,1)S(1)} %copy.17), channel_id=1, source_target_pairs={{0,1},{1,2},{2,3},{3,0},{4,5},{5,6},{6,7},{7,4},{8,9},{9,10},{10,1... | collective-permute-start | bytes 786440 | tf_op jit(solution)/shard_map/while/body/eval_jaxpr/ppermute | solution.py:16
  55.0 1.6 %collective-permute-start.1 = (f32[128]{0:T(128)S(1)}, f32[128]{0:T(128)S(1)}, u32[]{:S(2)}, u32[]{:S(2)}) collective-permute-start(f32[128]{0:T(128)S(1)} %max.13), channel_id=1, source_target_pairs={{0,1},{1,2},{2,3},{3,0},{4,5},{5,6},{6,7},{7,4},{8,9},{9,10},{10,1... | collective-permute-start | bytes 1544 | tf_op jit(solution)/shard_map/while/body/eval_jaxpr/ppermute | solution.py:16
  56.6 2.1 %collective-permute-start.2 = (f32[128]{0:T(128)S(1)}, f32[128]{0:T(128)S(1)}, u32[]{:S(2)}, u32[]{:S(2)}) collective-permute-start(f32[128]{0:T(128)S(1)} %get-tuple-element.531), channel_id=1, source_target_pairs={{0,1},{1,2},{2,3},{3,0},{4,5},{5,6},{6,7},{7,4},{8,9},{9,10},{10,1... | collective-permute-start | bytes 1544 | tf_op jit(solution)/shard_map/while/body/eval_jaxpr/ppermute | solution.py:16
  58.6 10.3 %collective-permute-done.1 = f32[128]{0:T(128)S(1)} collective-permute-done((f32[128]{0:T(128)S(1)}, f32[128]{0:T(128)S(1)}, u32[]{:S(2)}, u32[]{:S(2)}) %collective-permute-start.1) | collective-permute-done | bytes 544 | tf_op jit(solution)/shard_map/while/body/eval_jaxpr/ppermute | solution.py:16
  69.0 0.6 dynamic_slice.32
  69.6 0.6 iota_compare_fusion.2
  70.5 1.8 %fusion.35 = (f32[128]{0:T(128)S(1)}, f32[128,512]{1,0:T(8,128)S(1)}) fusion(f32[512]{0:T(512)S(1)} %convert_multiply_fusion.2, bf16[128,1024]{1,0:T(8,128)(2,1)S(1)} %copy.17, bf16[512,1024]{1,0:T(8,128)(2,1)} %get-tuple-element.576, pred[512]{0:T(512)(128)(4,1)S(1)} %broadcast_bitcast_fusion.2), kind=kOutput, calls=%fused_computation.27.clone.1 | convolution fusion | flops 134414208 | bytes 1575936 | tf_op jit(solution)/shard_map/while/body/eval_jaxpr/dot_general | solution.py:37
  73.2 0.8 collective-permute-start.1
  74.0 4.0 %collective-permute-start.2 = (f32[128]{0:T(128)S(1)}, f32[128]{0:T(128)S(1)}, u32[]{:S(2)}, u32[]{:S(2)}) collective-permute-start(f32[128]{0:T(128)S(1)} %get-tuple-element.531), channel_id=1, source_target_pairs={{0,1},{1,2},{2,3},{3,0},{4,5},{5,6},{6,7},{7,4},{8,9},{9,10},{10,1... | collective-permute-start | bytes 1544 | tf_op jit(solution)/shard_map/while/body/eval_jaxpr/ppermute | solution.py:16
  78.1 9.3 %collective-permute-done.1 = f32[128]{0:T(128)S(1)} collective-permute-done((f32[128]{0:T(128)S(1)}, f32[128]{0:T(128)S(1)}, u32[]{:S(2)}, u32[]{:S(2)}) %collective-permute-start.1) | collective-permute-done | bytes 544 | tf_op jit(solution)/shard_map/while/body/eval_jaxpr/ppermute | solution.py:16
  87.4 0.6 dynamic_slice.32
  88.9 1.8 %fusion.35 = (f32[128]{0:T(128)S(1)}, f32[128,512]{1,0:T(8,128)S(1)}) fusion(f32[512]{0:T(512)S(1)} %convert_multiply_fusion.2, bf16[128,1024]{1,0:T(8,128)(2,1)S(1)} %copy.17, bf16[512,1024]{1,0:T(8,128)(2,1)} %get-tuple-element.576, pred[512]{0:T(512)(128)(4,1)S(1)} %broadcast_bitcast_fusion.2), kind=kOutput, calls=%fused_computation.27.clone.1 | convolution fusion | flops 134414208 | bytes 1575936 | tf_op jit(solution)/shard_map/while/body/eval_jaxpr/dot_general | solution.py:37
  92.2 4.3 %collective-permute-start.2 = (f32[128]{0:T(128)S(1)}, f32[128]{0:T(128)S(1)}, u32[]{:S(2)}, u32[]{:S(2)}) collective-permute-start(f32[128]{0:T(128)S(1)} %get-tuple-element.531), channel_id=1, source_target_pairs={{0,1},{1,2},{2,3},{3,0},{4,5},{5,6},{6,7},{7,4},{8,9},{9,10},{10,1... | collective-permute-start | bytes 1544 | tf_op jit(solution)/shard_map/while/body/eval_jaxpr/ppermute | solution.py:16
  96.5 8.3 %collective-permute-done.1 = f32[128]{0:T(128)S(1)} collective-permute-done((f32[128]{0:T(128)S(1)}, f32[128]{0:T(128)S(1)}, u32[]{:S(2)}, u32[]{:S(2)}) %collective-permute-start.1) | collective-permute-done | bytes 544 | tf_op jit(solution)/shard_map/while/body/eval_jaxpr/ppermute | solution.py:16
  104.8 0.7 divide_convert_fusion
  (78 shorter events, 6.4 us)
Async XLA Ops:
  6.5 22.1 %all-gather.3.cloned.1.call-start = ((), (), s32[]{:S(2)}) async-start(), calls=%async_computation | async-start | bytes 1310720 | tf_op jit(solution)/shard_map/all_gather | solution.py:67
  6.5 8.1 %copy-start.1 = (bf16[128,512]{1,0:T(8,128)(2,1)S(1)}, bf16[128,512]{1,0:T(8,128)(2,1)}, u32[]{:S(2)}) copy-start(bf16[128,512]{1,0:T(8,128)(2,1)} %param.10) | copy-start | bytes 393220
  7.3 0.7 copy-start.2
  8.0 0.7 copy-start.3
  22.8 5.9 %copy-start = (bf16[128,1024]{1,0:T(8,128)(2,1)S(1)}, bf16[128,1024]{1,0:T(8,128)(2,1)}, u32[]{:S(2)}) copy-start(bf16[128,1024]{1,0:T(8,128)(2,1)} %param.8) | copy-start | bytes 786436
  28.6 0.7 copy-start.4
  33.3 16.1 %collective-permute-start.3 = (f32[128,512]{1,0:T(8,128)S(1)}, f32[128,512]{1,0:T(8,128)S(1)}, u32[]{:S(2)}, u32[]{:S(2)}) collective-permute-start(f32[128,512]{1,0:T(8,128)S(1)} %fusion.38), channel_id=1, source_target_pairs={{0,1},{1,2},{2,3},{3,0},{4,5},{5,6},{6,7},{7,4},{8,9},{9,10},{10,1... | collective-permute-start | bytes 786440 | tf_op jit(solution)/shard_map/while/body/eval_jaxpr/ppermute | solution.py:16
  35.1 14.4 %collective-permute-start = (bf16[128,1024]{1,0:T(8,128)(2,1)S(1)}, bf16[128,1024]{1,0:T(8,128)(2,1)S(1)}, u32[]{:S(2)}, u32[]{:S(2)}) collective-permute-start(bf16[128,1024]{1,0:T(8,128)(2,1)S(1)} %copy.17), channel_id=1, source_target_pairs={{0,1},{1,2},{2,3},{3,0},{4,5},{5,6},{6,7},{7,4},{8,9},{9,10},{10,1... | collective-permute-start | bytes 786440 | tf_op jit(solution)/shard_map/while/body/eval_jaxpr/ppermute | solution.py:16
  36.6 12.8 %collective-permute-start.1 = (f32[128]{0:T(128)S(1)}, f32[128]{0:T(128)S(1)}, u32[]{:S(2)}, u32[]{:S(2)}) collective-permute-start(f32[128]{0:T(128)S(1)} %max.13), channel_id=1, source_target_pairs={{0,1},{1,2},{2,3},{3,0},{4,5},{5,6},{6,7},{7,4},{8,9},{9,10},{10,1... | collective-permute-start | bytes 1544 | tf_op jit(solution)/shard_map/while/body/eval_jaxpr/ppermute | solution.py:16
  38.2 11.3 %collective-permute-start.2 = (f32[128]{0:T(128)S(1)}, f32[128]{0:T(128)S(1)}, u32[]{:S(2)}, u32[]{:S(2)}) collective-permute-start(f32[128]{0:T(128)S(1)} %get-tuple-element.531), channel_id=1, source_target_pairs={{0,1},{1,2},{2,3},{3,0},{4,5},{5,6},{6,7},{7,4},{8,9},{9,10},{10,1... | collective-permute-start | bytes 1544 | tf_op jit(solution)/shard_map/while/body/eval_jaxpr/ppermute | solution.py:16
  53.6 15.3 %collective-permute-start.3 = (f32[128,512]{1,0:T(8,128)S(1)}, f32[128,512]{1,0:T(8,128)S(1)}, u32[]{:S(2)}, u32[]{:S(2)}) collective-permute-start(f32[128,512]{1,0:T(8,128)S(1)} %fusion.38), channel_id=1, source_target_pairs={{0,1},{1,2},{2,3},{3,0},{4,5},{5,6},{6,7},{7,4},{8,9},{9,10},{10,1... | collective-permute-start | bytes 786440 | tf_op jit(solution)/shard_map/while/body/eval_jaxpr/ppermute | solution.py:16
  53.7 15.2 %collective-permute-start = (bf16[128,1024]{1,0:T(8,128)(2,1)S(1)}, bf16[128,1024]{1,0:T(8,128)(2,1)S(1)}, u32[]{:S(2)}, u32[]{:S(2)}) collective-permute-start(bf16[128,1024]{1,0:T(8,128)(2,1)S(1)} %copy.17), channel_id=1, source_target_pairs={{0,1},{1,2},{2,3},{3,0},{4,5},{5,6},{6,7},{7,4},{8,9},{9,10},{10,1... | collective-permute-start | bytes 786440 | tf_op jit(solution)/shard_map/while/body/eval_jaxpr/ppermute | solution.py:16
  55.0 13.9 %collective-permute-start.1 = (f32[128]{0:T(128)S(1)}, f32[128]{0:T(128)S(1)}, u32[]{:S(2)}, u32[]{:S(2)}) collective-permute-start(f32[128]{0:T(128)S(1)} %max.13), channel_id=1, source_target_pairs={{0,1},{1,2},{2,3},{3,0},{4,5},{5,6},{6,7},{7,4},{8,9},{9,10},{10,1... | collective-permute-start | bytes 1544 | tf_op jit(solution)/shard_map/while/body/eval_jaxpr/ppermute | solution.py:16
  56.6 12.3 %collective-permute-start.2 = (f32[128]{0:T(128)S(1)}, f32[128]{0:T(128)S(1)}, u32[]{:S(2)}, u32[]{:S(2)}) collective-permute-start(f32[128]{0:T(128)S(1)} %get-tuple-element.531), channel_id=1, source_target_pairs={{0,1},{1,2},{2,3},{3,0},{4,5},{5,6},{6,7},{7,4},{8,9},{9,10},{10,1... | collective-permute-start | bytes 1544 | tf_op jit(solution)/shard_map/while/body/eval_jaxpr/ppermute | solution.py:16
  73.1 14.3 %collective-permute-start.3 = (f32[128,512]{1,0:T(8,128)S(1)}, f32[128,512]{1,0:T(8,128)S(1)}, u32[]{:S(2)}, u32[]{:S(2)}) collective-permute-start(f32[128,512]{1,0:T(8,128)S(1)} %fusion.38), channel_id=1, source_target_pairs={{0,1},{1,2},{2,3},{3,0},{4,5},{5,6},{6,7},{7,4},{8,9},{9,10},{10,1... | collective-permute-start | bytes 786440 | tf_op jit(solution)/shard_map/while/body/eval_jaxpr/ppermute | solution.py:16
  73.1 14.2 %collective-permute-start = (bf16[128,1024]{1,0:T(8,128)(2,1)S(1)}, bf16[128,1024]{1,0:T(8,128)(2,1)S(1)}, u32[]{:S(2)}, u32[]{:S(2)}) collective-permute-start(bf16[128,1024]{1,0:T(8,128)(2,1)S(1)} %copy.17), channel_id=1, source_target_pairs={{0,1},{1,2},{2,3},{3,0},{4,5},{5,6},{6,7},{7,4},{8,9},{9,10},{10,1... | collective-permute-start | bytes 786440 | tf_op jit(solution)/shard_map/while/body/eval_jaxpr/ppermute | solution.py:16
  73.2 14.1 %collective-permute-start.1 = (f32[128]{0:T(128)S(1)}, f32[128]{0:T(128)S(1)}, u32[]{:S(2)}, u32[]{:S(2)}) collective-permute-start(f32[128]{0:T(128)S(1)} %max.13), channel_id=1, source_target_pairs={{0,1},{1,2},{2,3},{3,0},{4,5},{5,6},{6,7},{7,4},{8,9},{9,10},{10,1... | collective-permute-start | bytes 1544 | tf_op jit(solution)/shard_map/while/body/eval_jaxpr/ppermute | solution.py:16
  74.0 13.3 %collective-permute-start.2 = (f32[128]{0:T(128)S(1)}, f32[128]{0:T(128)S(1)}, u32[]{:S(2)}, u32[]{:S(2)}) collective-permute-start(f32[128]{0:T(128)S(1)} %get-tuple-element.531), channel_id=1, source_target_pairs={{0,1},{1,2},{2,3},{3,0},{4,5},{5,6},{6,7},{7,4},{8,9},{9,10},{10,1... | collective-permute-start | bytes 1544 | tf_op jit(solution)/shard_map/while/body/eval_jaxpr/ppermute | solution.py:16
  91.5 13.3 %collective-permute-start.3 = (f32[128,512]{1,0:T(8,128)S(1)}, f32[128,512]{1,0:T(8,128)S(1)}, u32[]{:S(2)}, u32[]{:S(2)}) collective-permute-start(f32[128,512]{1,0:T(8,128)S(1)} %fusion.38), channel_id=1, source_target_pairs={{0,1},{1,2},{2,3},{3,0},{4,5},{5,6},{6,7},{7,4},{8,9},{9,10},{10,1... | collective-permute-start | bytes 786440 | tf_op jit(solution)/shard_map/while/body/eval_jaxpr/ppermute | solution.py:16
  91.6 13.2 %collective-permute-start = (bf16[128,1024]{1,0:T(8,128)(2,1)S(1)}, bf16[128,1024]{1,0:T(8,128)(2,1)S(1)}, u32[]{:S(2)}, u32[]{:S(2)}) collective-permute-start(bf16[128,1024]{1,0:T(8,128)(2,1)S(1)} %copy.17), channel_id=1, source_target_pairs={{0,1},{1,2},{2,3},{3,0},{4,5},{5,6},{6,7},{7,4},{8,9},{9,10},{10,1... | collective-permute-start | bytes 786440 | tf_op jit(solution)/shard_map/while/body/eval_jaxpr/ppermute | solution.py:16
  91.6 13.1 %collective-permute-start.1 = (f32[128]{0:T(128)S(1)}, f32[128]{0:T(128)S(1)}, u32[]{:S(2)}, u32[]{:S(2)}) collective-permute-start(f32[128]{0:T(128)S(1)} %max.13), channel_id=1, source_target_pairs={{0,1},{1,2},{2,3},{3,0},{4,5},{5,6},{6,7},{7,4},{8,9},{9,10},{10,1... | collective-permute-start | bytes 1544 | tf_op jit(solution)/shard_map/while/body/eval_jaxpr/ppermute | solution.py:16
  92.2 12.6 %collective-permute-start.2 = (f32[128]{0:T(128)S(1)}, f32[128]{0:T(128)S(1)}, u32[]{:S(2)}, u32[]{:S(2)}) collective-permute-start(f32[128]{0:T(128)S(1)} %get-tuple-element.531), channel_id=1, source_target_pairs={{0,1},{1,2},{2,3},{3,0},{4,5},{5,6},{6,7},{7,4},{8,9},{9,10},{10,1... | collective-permute-start | bytes 1544 | tf_op jit(solution)/shard_map/while/body/eval_jaxpr/ppermute | solution.py:16
Sparse Core Ops, SparseCore 0:
  8.9 19.6 all-gather.2
where the time goes:
time: 113 us; the launch traced here: 112 us
  waiting for transfers between devices  45.5 us (40%)
  starting transfers between devices  20 us (18%)
  blocking collectives  14.1 us (12%)
  between operations  13.4 us (12%)
  matrix products  9.45 us (8%)
  local copies, waits for them, and re-layouts  5.07 us (4%)
  other arithmetic  4.5 us (4%)
    ppermute x16, waiting for transfers between devices, from_behind(): lax.ppermute(value, axis, [(i, (i + by) % length) for i in range(length)])  38.9 us
    ppermute x16, starting transfers between devices, from_behind(): lax.ppermute(value, axis, [(i, (i + by) % length) for i in range(length)])  20 us
    all_gather x1, blocking collectives, body(): lax.all_gather(library_values, 'lib', axis=0, tiled=True)  8.12 us
    dot_general x4, matrix products, tile_update(): lax.dot_general(query_rows, tile_keys, (((1,), (1,)), ((), ())), preferre...  7.17 us
    all_gather x1, blocking collectives, body(): lax.all_gather(key_scale, 'lib', axis=0, tiled=True)  5.94 us
    all_gather x1, waiting for transfers between devices, body(): lax.all_gather(library_keys, 'lib', axis=0, tiled=True)  5.83 us
    dynamic_slice x4, local copies, waits for them, and re-layouts, window_flags(): lax.dynamic_slice_in_dim(block_count, first_panel, panel_count, 0)  2.59 us
    lt x4, other arithmetic, window_flags(): jnp.arange(window_lists.shape[1], dtype=jnp.int32)[None, :]  2.49 us
  transfers between devices with their start and end apart: 17, of which 5 were waited for; matrix products, arithmetic and copies ran while one was open for 0% of the time, Pallas kernels for 0%

commit v1 on v0

v1 whole, which is shorter than its diff:
```python
import functools
import math

import jax
import jax.numpy as jnp
from jax import lax
from jax.experimental import pallas as pl
from jax.experimental.pallas import tpu as pltpu
from jax.sharding import PartitionSpec as P

TILE = 128
LANES = 128
MASKED_SCORE = -1e30
VMEM_LIMIT = 48 * 1024 * 1024


def swap(value, axis, mask):
    length = lax.axis_size(axis)
    return lax.ppermute(value, axis, [(i, i ^ mask) for i in range(length)])


def split_three(value):
    high = value.astype(jnp.bfloat16)
    rest = value - high.astype(jnp.float32)
    middle = rest.astype(jnp.bfloat16)
    low = (rest - middle.astype(jnp.float32)).astype(jnp.bfloat16)
    return high, middle, low


def attend(masks, panel_mask, lists_ref, counts_ref, query_ref, key_refs, value_refs, score_ref, total_ref, mass_ref):
    lib_index = lax.axis_index("lib")
    qry_index = lax.axis_index("qry")
    qry_count = lax.axis_size("qry")
    block_total = lax.axis_size("lib") * qry_count
    panel = lib_index * qry_count + lax.bitwise_xor(qry_index, panel_mask)
    first = lists_ref[panel, 0]
    count = counts_ref[panel]
    width = query_ref.shape[1]
    value_width = total_ref.shape[1]
    inverse_root = 1.0 / math.sqrt(width)

    def active(lib_mask, qry_mask):
        block = lax.bitwise_xor(lib_index, lib_mask) * qry_count + lax.bitwise_xor(qry_index, qry_mask)
        return lax.rem(block - first + block_total, block_total) < count

    flags = [active(*mask) for mask in masks]
    score_ref[...] = jnp.full(score_ref.shape, MASKED_SCORE, jnp.float32)
    total_ref[...] = jnp.zeros(total_ref.shape, jnp.float32)
    mass_ref[...] = jnp.zeros(mass_ref.shape, jnp.float32)
    for at, flag in enumerate(flags):

        @pl.when(flag)
        def _(at=at):
            scale = value_refs[at][0:16, value_width : value_width + TILE].astype(jnp.float32)[0:1] * inverse_root
            product = lax.dot_general(
                query_ref[...], key_refs[at][...], (((1,), (1,)), ((), ())), preferred_element_type=jnp.float32
            )
            score_ref[at] = product * scale

    largest = score_ref[0]
    for at in range(1, len(flags)):
        largest = jnp.maximum(largest, score_ref[at])
    row_max = jnp.max(largest, axis=1, keepdims=True)
    for at, flag in enumerate(flags):

        @pl.when(flag)
        def _(at=at):
            weights = jnp.exp(score_ref[at] - row_max)
            mass_ref[...] += weights
            weight_high = weights.astype(jnp.bfloat16)
            weight_low = (weights - weight_high.astype(jnp.float32)).astype(jnp.bfloat16)
            values = value_refs[at][:, 0:value_width]
            added = jnp.dot(weight_high, values, preferred_element_type=jnp.float32)
            added = added + jnp.dot(weight_low, values, preferred_element_type=jnp.float32)
            total_ref[...] += added

    return row_max


def visit_kernel(masks, panel_mask, *refs):
    count = len(masks)
    lists_ref, counts_ref, query_ref = refs[:3]
    key_refs = refs[3 : 3 + count]
    value_refs = refs[3 + count : 3 + 2 * count]
    packed_ref, score_ref, total_ref, mass_ref = refs[3 + 2 * count :]
    row_max = attend(
        masks, panel_mask, lists_ref, counts_ref, query_ref, key_refs, value_refs, score_ref, total_ref, mass_ref
    )
    row_sum = jnp.sum(mass_ref[...], axis=1, keepdims=True)
    value_width = total_ref.shape[1]
    divisor = jnp.where(row_sum > 0.0, row_sum, 1.0)
    packed_ref[:, 0:value_width] = (total_ref[...] / divisor).astype(jnp.bfloat16)
    lane = lax.broadcasted_iota(jnp.int32, (TILE, LANES), 1)
    packed = jnp.zeros((TILE, LANES), jnp.float32)
    for at, part in enumerate(split_three(row_max) + split_three(row_sum)):
        packed = jnp.where(lane == at, part.astype(jnp.float32), packed)
    packed_ref[:, value_width:] = packed.astype(jnp.bfloat16)


def home_kernel(masks, *refs):
    count = len(masks)
    lists_ref, counts_ref, query_ref = refs[:3]
    key_refs = refs[3 : 3 + count]
    value_refs = refs[3 + count : 3 + 2 * count]
    total_ref, stats_ref, score_ref, mass_ref = refs[3 + 2 * count :]
    row_max = attend(masks, 0, lists_ref, counts_ref, query_ref, key_refs, value_refs, score_ref, total_ref, mass_ref)
    row_sum = jnp.sum(mass_ref[...], axis=1, keepdims=True)
    stats_ref[0] = jnp.broadcast_to(row_max, (TILE, LANES))
    stats_ref[1] = jnp.broadcast_to(row_sum, (TILE, LANES))


def merge_kernel(total_ref, stats_ref, *refs):
    packed_refs, out_ref = refs[:-1], refs[-1]
    value_width = total_ref.shape[1]
    lane = lax.broadcasted_iota(jnp.int32, (TILE, LANES), 1)
    maxima = [stats_ref[0]]
    sums = [stats_ref[1]]
    for packed_ref in packed_refs:
        packed = packed_ref[:, value_width:].astype(jnp.float32)

        def lanes_sum(low, packed=packed):
            picked = jnp.where((lane >= low) & (lane < low + 3), packed, 0.0)
            return jnp.broadcast_to(jnp.sum(picked, axis=1, keepdims=True), (TILE, LANES))

        maxima.append(lanes_sum(0))
        sums.append(lanes_sum(3))
    top = functools.reduce(jnp.maximum, maxima)
    factors = [jnp.exp(row_max - top) for row_max in maxima]
    masses = [factor * row_sum for factor, row_sum in zip(factors, sums)]
    inverse = 1.0 / functools.reduce(jnp.add, masses)
    scales = [factors[0] * inverse] + [mass * inverse for mass in masses[1:]]
    for at in range(0, value_width, LANES):
        merged = total_ref[:, at : at + LANES] * scales[0]
        for packed_ref, scale in zip(packed_refs, scales[1:]):
            merged = merged + packed_ref[:, at : at + LANES].astype(jnp.float32) * scale
        out_ref[:, at : at + LANES] = merged.astype(jnp.bfloat16)


def params():
    return pltpu.CompilerParams(vmem_limit_bytes=VMEM_LIMIT)


def pack_kernel(values_ref, scale_ref, packed_ref):
    value_width = values_ref.shape[1]
    packed_ref[:, 0:value_width] = values_ref[...]
    row = scale_ref[...].astype(jnp.float32)
    packed_ref[:, value_width:] = jnp.broadcast_to(row, (TILE, TILE)).astype(jnp.bfloat16)


def body(queries, library_keys, library_values, key_scale, block_list, block_count):
    qry_count = lax.axis_size("qry")
    lib_count = lax.axis_size("lib")
    value_width = library_values.shape[1]
    smem = pl.BlockSpec(memory_space=pltpu.SMEM)
    vmem = pl.BlockSpec(memory_space=pltpu.VMEM)

    values_packed = pl.pallas_call(
        pack_kernel,
        out_shape=jax.ShapeDtypeStruct((TILE, value_width + TILE), jnp.bfloat16),
        in_specs=[vmem, vmem],
        out_specs=vmem,
        compiler_params=params(),
    )(library_values, key_scale.reshape(1, TILE))

    steps = [("qry", 1)]
    mask = lib_count // 2
    while mask:
        steps.append(("lib", mask))
        mask //= 2
    pieces = [((0, 0), library_keys, values_packed)]
    for axis, mask in steps:
        arrived = []
        for (lib_mask, qry_mask), keys, values in pieces:
            place = (lib_mask, mask) if axis == "qry" else (lib_mask | mask, qry_mask)
            arrived.append((place, swap(keys, axis, mask), swap(values, axis, mask)))
        pieces = pieces + arrived
    masks = [piece[0] for piece in pieces]
    keys = [piece[1] for piece in pieces]
    values = [piece[2] for piece in pieces]
    count = len(pieces)

    cost = pl.CostEstimate(flops=2 * TILE * 4 * TILE * (1024 + 1024), bytes_accessed=count * 400 * 1024, transcendentals=0)
    scratch = [
        pltpu.VMEM((count, TILE, TILE), jnp.float32),
        pltpu.VMEM((TILE, value_width), jnp.float32),
        pltpu.VMEM((TILE, TILE), jnp.float32),
    ]
    returned = []
    visit_masks = [2 * at + 1 for at in range(1, qry_count // 2)]
    for visit_mask in visit_masks:
        visitor = swap(queries, "qry", visit_mask)
        packed = pl.pallas_call(
            functools.partial(visit_kernel, masks, visit_mask),
            out_shape=jax.ShapeDtypeStruct((TILE, value_width + LANES), jnp.bfloat16),
            in_specs=[smem, smem] + [vmem] * (1 + 2 * count),
            out_specs=vmem,
            scratch_shapes=scratch,
            compiler_params=params(),
            cost_estimate=cost,
        )(block_list, block_count, visitor, *keys, *values)
        returned.append(swap(packed, "qry", visit_mask))

    total, stats = pl.pallas_call(
        functools.partial(home_kernel, masks),
        out_shape=(
            jax.ShapeDtypeStruct((TILE, value_width), jnp.float32),
            jax.ShapeDtypeStruct((2, TILE, LANES), jnp.float32),
        ),
        in_specs=[smem, smem] + [vmem] * (1 + 2 * count),
        out_specs=(vmem, vmem),
        scratch_shapes=[scratch[0], scratch[2]],
        compiler_params=params(),
        cost_estimate=cost,
    )(block_list, block_count, queries, *keys, *values)

    return pl.pallas_call(
        merge_kernel,
        out_shape=jax.ShapeDtypeStruct((TILE, value_width), jnp.bfloat16),
        in_specs=[vmem] * (2 + len(returned)),
        out_specs=vmem,
        compiler_params=params(),
    )(total, stats, *returned)


def solution(mesh):
    in_specs = (
        P(("groups", "lib", "qry"), None),
        P(("groups", "lib", "qry"), None),
        P(("groups", "lib", "qry"), None),
        P(("groups", "lib", "qry")),
        P("groups", None),
        P("groups"),
    )
    out_specs = P(("groups", "lib", "qry"), None)
    return jax.shard_map(body, mesh=mesh, in_specs=in_specs, out_specs=out_specs, check_vma=False)
```

time: 113 us -> 42.3 us (0.37)
  waiting for transfers between devices: 45.5 us -> 17.2 us
  blocking collectives: 14.1 us -> 0 us
  between operations: 13.4 us -> 0.07 us
  matrix products: 9.45 us -> 0 us
  other arithmetic: 4.5 us -> 0 us
  Pallas kernels: 0 us -> 2.8 us
  local copies, waits for them, and re-layouts: 5.07 us -> 3.32 us
    ppermute x16, waiting for transfers between devices: 38.9 us -> 17.2 us  [swap(): return lax.ppermute(value, axis, [(i, i ^ mask) for i in range(length)])]
    all_gather x2 -> x0, blocking collectives: 14.1 us -> none  [the longest x1 8.12 us: body(): lax.all_gather(library_values, 'lib', axis=0, tiled=True)]
    dot_general x12 -> x0, matrix products: 9.45 us -> none  [the longest x4 7.17 us: tile_update(): lax.dot_general(query_rows, tile_keys, (((1,), (1,)), ((), ())), preferre...]
    all_gather x1 -> x0, waiting for transfers between devices: 5.83 us -> none  [body(): lax.all_gather(library_keys, 'lib', axis=0, tiled=True)]
    pallas_call x0 -> x4, Pallas kernels: none -> 2.8 us  [the longest x1 1 us: body(): pl.pallas_call(functools.partial(visit_kernel, masks, visit_mask), out_sh...]
    dynamic_slice x8 -> x0, local copies, waits for them, and re-layouts: 2.64 us -> none  [the longest x4 2.59 us: window_flags(): lax.dynamic_slice_in_dim(block_count, first_panel, panel_count, 0)]
    lt x4 -> x0, other arithmetic: 2.49 us -> none  [window_flags(): jnp.arange(window_lists.shape[1], dtype=jnp.int32)[None, :]]
    unnamed x11 -> x17, local copies, waits for them, and re-layouts: 2.04 us -> 3.32 us
  transfers between devices with their start and end apart: 17 -> 16, of which waited for: 5 -> 6; matrix products, arithmetic and copies ran while one was open for 0% -> 0% of each run, Pallas kernels for 0% -> 2%
where the time goes in v1:
time: 42.3 us; the launch traced here: 42.6 us
  starting transfers between devices  19.2 us (45%)
  waiting for transfers between devices  17.2 us (41%)
  local copies, waits for them, and re-layouts  3.32 us (8%)
  Pallas kernels  2.8 us (7%)
    ppermute x16, starting transfers between devices, swap(): return lax.ppermute(value, axis, [(i, i ^ mask) for i in range(length)])  19.2 us
    ppermute x16, waiting for transfers between devices, swap(): return lax.ppermute(value, axis, [(i, i ^ mask) for i in range(length)])  17.2 us
    unnamed x17, local copies, waits for them, and re-layouts  3.32 us
    pallas_call x1, Pallas kernels, body(): pl.pallas_call(functools.partial(visit_kernel, masks, visit_mask), out_sh...  1 us
    pallas_call x1, Pallas kernels, body(): pl.pallas_call(functools.partial(home_kernel, masks), out_shape=(jax.Shap...  0.97 us
  transfers between devices with their start and end apart: 16, of which 6 were waited for; matrix products, arithmetic and copies ran while one was open for 0% of the time, Pallas kernels for 2%

profile of v1, /device:TPU:0, one launch (start us, length us, event | category | flops | bytes accessed | tf_op | source)
XLA Modules:
  0.0 42.6 jit_solution(13786915773138832747)
XLA Ops:
  0.0 3.0 %collective-permute-start = (bf16[128,1024]{1,0:T(8,128)(2,1)}, bf16[128,1024]{1,0:T(8,128)(2,1)S(1)}, u32[]{:S(2)}, u32[]{:S(2)}) collective-permute-start(bf16[128,1024]{1,0:T(8,128)(2,1)} %refs_3_.3), channel_id=1, source_target_pairs={{0,1},{1,0},{2,3},{3,2},{4,5},{5,4},{6,7},{7,6},{8,9},{9,8},{10,11... | collective-permute-start | bytes 786440 | tf_op jit(solution)/shard_map/ppermute | solution.py:19
  3.0 0.9 %copy-done.4 = bf16[128,512]{1,0:T(8,128)(2,1)S(1)} copy-done((bf16[128,512]{1,0:T(8,128)(2,1)S(1)}, bf16[128,512]{1,0:T(8,128)(2,1)}, u32[]{:S(2)}) %copy-start.4) | copy-done | bytes 131096
  3.9 0.7 %copy-done.6 = bf16[128]{0:T(256)(128)(2,1)S(1)} copy-done((bf16[128]{0:T(256)(128)(2,1)S(1)}, bf16[128]{0:T(256)(128)(2,1)}, u32[]{:S(2)}) %copy-start.6) | copy-done | bytes 280
  4.6 0.0 copy-start.5
  4.6 0.1 collective-permute-start.10
  4.7 1.6 %collective-permute-start.8 = (bf16[128,640]{1,0:T(8,128)(2,1)S(1)}, bf16[128,640]{1,0:T(8,128)(2,1)S(1)}, u32[]{:S(2)}, u32[]{:S(2)}) collective-permute-start(bf16[128,640]{1,0:T(8,128)(2,1)S(1)} %shard_map.64.refs_11_), channel_id=1, source_target_pairs={{0,8},{4,12},{8,0},{12,4},{1,9},{5,13},{9,1},{13,5},{2,10},{6,14},... | collective-permute-start | bytes 491528 | tf_op jit(solution)/shard_map/ppermute | solution.py:19
  6.3 2.5 %collective-permute-start.14 = (bf16[128,1024]{1,0:T(8,128)(2,1)}, bf16[128,1024]{1,0:T(8,128)(2,1)S(1)}, u32[]{:S(2)}, u32[]{:S(2)}) collective-permute-start(bf16[128,1024]{1,0:T(8,128)(2,1)} %refs_2_.1), channel_id=1, source_target_pairs={{0,3},{1,2},{2,1},{3,0},{4,7},{5,6},{6,5},{7,4},{8,11},{9,10},{10,... | collective-permute-start | bytes 786440 | tf_op jit(solution)/shard_map/ppermute | solution.py:19
  8.7 0.0 collective-permute-start.3
  8.7 0.0 collective-permute-done.10.refs_15_
  8.7 0.6 %collective-permute-start.1 = (bf16[128,1024]{1,0:T(8,128)(2,1)S(1)}, bf16[128,1024]{1,0:T(8,128)(2,1)S(1)}, u32[]{:S(2)}, u32[]{:S(2)}) collective-permute-start(bf16[128,1024]{1,0:T(8,128)(2,1)S(1)} %copy-done), channel_id=1, source_target_pairs={{0,8},{4,12},{8,0},{12,4},{1,9},{5,13},{9,1},{13,5},{2,10},{6,14},... | collective-permute-start | bytes 786440 | tf_op jit(solution)/shard_map/ppermute | solution.py:19
  9.3 0.3 collective-permute-done.refs_4_
  9.6 1.6 %collective-permute-start.2 = (bf16[128,1024]{1,0:T(8,128)(2,1)S(1)}, bf16[128,1024]{1,0:T(8,128)(2,1)S(1)}, u32[]{:S(2)}, u32[]{:S(2)}) collective-permute-start(bf16[128,1024]{1,0:T(8,128)(2,1)S(1)} %collective-permute-done.refs_4_), channel_id=1, source_target_pairs={{0,8},{4,12},{8,0},{12,4},{1,9},{5,13},{9,1},{13,5},{2,10},{6,14},... | collective-permute-start | bytes 786440 | tf_op jit(solution)/shard_map/ppermute | solution.py:19
  11.2 0.1 collective-permute-done.8.refs_13_
  11.3 1.9 %collective-permute-start.7 = (bf16[128,640]{1,0:T(8,128)(2,1)S(1)}, bf16[128,640]{1,0:T(8,128)(2,1)S(1)}, u32[]{:S(2)}, u32[]{:S(2)}) collective-permute-start(bf16[128,640]{1,0:T(8,128)(2,1)S(1)} %shard_map.64.refs_11_), channel_id=1, source_target_pairs={{0,1},{1,0},{2,3},{3,2},{4,5},{5,4},{6,7},{7,6},{8,9},{9,8},{10,11... | collective-permute-start | bytes 491528 | tf_op jit(solution)/shard_map/ppermute | solution.py:19
  13.3 7.7 %collective-permute-done.7.refs_12_ = bf16[128,640]{1,0:T(8,128)(2,1)S(1)} collective-permute-done((bf16[128,640]{1,0:T(8,128)(2,1)S(1)}, bf16[128,640]{1,0:T(8,128)(2,1)S(1)}, u32[]{:S(2)}, u32[]{:S(2)}) %collective-permute-start.7) | collective-permute-done | bytes 163872 | tf_op jit(solution)/shard_map/ppermute | solution.py:19
  21.0 0.0 collective-permute-start.12
  21.0 0.0 collective-permute-done.14.refs_2_
  21.0 0.7 %copy-done.1 = bf16[128,1024]{1,0:T(8,128)(2,1)} copy-done((bf16[128,1024]{1,0:T(8,128)(2,1)}, bf16[128,1024]{1,0:T(8,128)(2,1)S(1)}, u32[]{:S(2)}) %copy-start.1) | copy-done | bytes 262168
  21.7 1.5 %collective-permute-start.9 = (bf16[128,640]{1,0:T(8,128)(2,1)S(1)}, bf16[128,640]{1,0:T(8,128)(2,1)S(1)}, u32[]{:S(2)}, u32[]{:S(2)}) collective-permute-start(bf16[128,640]{1,0:T(8,128)(2,1)S(1)} %collective-permute-done.7.refs_12_), channel_id=1, source_target_pairs={{0,8},{4,12},{8,0},{12,4},{1,9},{5,13},{9,1},{13,5},{2,10},{6,14},... | collective-permute-start | bytes 491528 | tf_op jit(solution)/shard_map/ppermute | solution.py:19
  23.2 0.2 collective-permute-start.4
  23.4 0.3 collective-permute-start.5
  23.7 0.2 collective-permute-start.6
  23.9 0.3 collective-permute-start.11
  24.2 4.1 %collective-permute-done.9.refs_14_ = bf16[128,640]{1,0:T(8,128)(2,1)S(1)} collective-permute-done((bf16[128,640]{1,0:T(8,128)(2,1)S(1)}, bf16[128,640]{1,0:T(8,128)(2,1)S(1)}, u32[]{:S(2)}, u32[]{:S(2)}) %collective-permute-start.9) | collective-permute-done | bytes 163872 | tf_op jit(solution)/shard_map/ppermute | solution.py:19
  28.3 0.1 copy.7.refs_0_
  28.4 1.3 %collective-permute-done.13.refs_18_ = bf16[128,640]{1,0:T(8,128)(2,1)S(1)} collective-permute-done((bf16[128,640]{1,0:T(8,128)(2,1)S(1)}, bf16[128,640]{1,0:T(8,128)(2,1)S(1)}, u32[]{:S(2)}, u32[]{:S(2)}) %collective-permute-start.13) | collective-permute-done | bytes 163872 | tf_op jit(solution)/shard_map/ppermute | solution.py:19
  29.7 0.9 %copy-done.2 = bf16[128,1024]{1,0:T(8,128)(2,1)S(1)} copy-done((bf16[128,1024]{1,0:T(8,128)(2,1)S(1)}, bf16[128,1024]{1,0:T(8,128)(2,1)}, u32[]{:S(2)}) %copy-start.2) | copy-done | bytes 262168
  30.7 1.0 %shard_map.66 = bf16[128,640]{1,0:T(8,128)(2,1)S(1)} custom-call(s32[16,4]{1,0:T(8,128)S(1)} %copy.7.refs_0_, s32[16]{0:T(128)S(1)} %copy-done.5, bf16[128,1024]{1,0:T(8,128)(2,1)S(1)} %copy-done.2, bf16[128,1024]{1,0:T(8,128)(2,1)S(1)} %copy-done, bf16[128,1024]{1,0:T(8,128)(2,1)S(1)} %collective-permute-done.refs_4_, ...), custom_call_target="tpu_custom_call" | custom-call | flops 268435456 | bytes 3276800 | tf_op jit(solution)/shard_map/pallas_call | solution.py:192
  31.7 5.4 %collective-permute-start.15 = (bf16[128,640]{1,0:T(8,128)(2,1)S(1)}, bf16[128,640]{1,0:T(8,128)(2,1)S(1)}, u32[]{:S(2)}, u32[]{:S(2)}) collective-permute-start(bf16[128,640]{1,0:T(8,128)(2,1)S(1)} %shard_map.66), channel_id=1, source_target_pairs={{0,3},{1,2},{2,1},{3,0},{4,7},{5,6},{6,5},{7,4},{8,11},{9,10},{10,... | collective-permute-start | bytes 491528 | tf_op jit(solution)/shard_map/ppermute | solution.py:19
  37.1 1.0 %shard_map.65 = (f32[128,512]{1,0:T(8,128)S(1)}, f32[2,128,128]{2,1,0:T(8,128)S(1)}) custom-call(s32[16,4]{1,0:T(8,128)S(1)} %copy.7.refs_0_, s32[16]{0:T(128)S(1)} %copy-done.5, bf16[128,1024]{1,0:T(8,128)(2,1)S(1)} %copy-done.3, bf16[128,1024]{1,0:T(8,128)(2,1)S(1)} %copy-done, bf16[128,1024]{1,0:T(8,128)(2,1)S(1)} %collective-permute-done.refs_4_, ...), custom_call_target="tpu_custom_call" | custom-call | flops 268435456 | bytes 3276800 | tf_op jit(solution)/shard_map/pallas_call | solution.py:203
  38.1 3.7 %collective-permute-done.15.refs_0_ = bf16[128,640]{1,0:T(8,128)(2,1)S(1)} collective-permute-done((bf16[128,640]{1,0:T(8,128)(2,1)S(1)}, bf16[128,640]{1,0:T(8,128)(2,1)S(1)}, u32[]{:S(2)}, u32[]{:S(2)}) %collective-permute-start.15) | collective-permute-done | bytes 163872 | tf_op jit(solution)/shard_map/ppermute | solution.py:19
  41.7 0.8 %shard_map.67 = bf16[128,512]{1,0:T(8,128)(2,1)} custom-call(f32[128,512]{1,0:T(8,128)S(1)} %get-tuple-element.7.total_ref, f32[2,128,128]{2,1,0:T(8,128)S(1)} %get-tuple-element.8.stats_ref, bf16[128,640]{1,0:T(8,128)(2,1)S(1)} %collective-permute-done.15.refs_0_), custom_call_target="tpu_custom_call" | custom-call | tf_op jit(solution)/shard_map/pallas_call | solution.py:216
  (21 shorter events, 0.1 us)
Async XLA Ops:
  0.0 8.7 %copy-start = (bf16[128,1024]{1,0:T(8,128)(2,1)S(1)}, bf16[128,1024]{1,0:T(8,128)(2,1)}, u32[]{:S(2)}) copy-start(bf16[128,1024]{1,0:T(8,128)(2,1)} %refs_3_.3) | copy-start | bytes 786436
  0.0 9.6 %collective-permute-start = (bf16[128,1024]{1,0:T(8,128)(2,1)}, bf16[128,1024]{1,0:T(8,128)(2,1)S(1)}, u32[]{:S(2)}, u32[]{:S(2)}) collective-permute-start(bf16[128,1024]{1,0:T(8,128)(2,1)} %refs_3_.3), channel_id=1, source_target_pairs={{0,1},{1,0},{2,3},{3,2},{4,5},{5,4},{6,7},{7,6},{8,9},{9,8},{10,11... | collective-permute-start | bytes 786440 | tf_op jit(solution)/shard_map/ppermute | solution.py:19
  3.0 0.9 %copy-start.4 = (bf16[128,512]{1,0:T(8,128)(2,1)S(1)}, bf16[128,512]{1,0:T(8,128)(2,1)}, u32[]{:S(2)}) copy-start(bf16[128,512]{1,0:T(8,128)(2,1)} %values_ref.1) | copy-start | bytes 393220
  3.9 0.7 %copy-start.6 = (bf16[128]{0:T(256)(128)(2,1)S(1)}, bf16[128]{0:T(256)(128)(2,1)}, u32[]{:S(2)}) copy-start(bf16[128]{0:T(256)(128)(2,1)} %param.9) | copy-start | bytes 772
  4.6 23.7 %copy-start.7 = (s32[16,4]{0,1:T(4,128)S(1)}, s32[16,4]{0,1:T(4,128)}, u32[]{:S(2)}) copy-start(s32[16,4]{0,1:T(4,128)} %param.10) | copy-start | bytes 772
  4.6 25.1 %copy-start.5 = (s32[16]{0:T(128)S(1)}, s32[16]{0:T(128)}, u32[]{:S(2)}) copy-start(s32[16]{0:T(128)} %refs_1_.3) | copy-start | bytes 196
  4.6 4.1 %collective-permute-start.10 = (bf16[128,640]{1,0:T(8,128)(2,1)S(1)}, bf16[128,640]{1,0:T(8,128)(2,1)S(1)}, u32[]{:S(2)}, u32[]{:S(2)}) collective-permute-start(bf16[128,640]{1,0:T(8,128)(2,1)S(1)} %shard_map.64.refs_11_), channel_id=1, source_target_pairs={{0,4},{4,0},{8,12},{12,8},{1,5},{5,1},{9,13},{13,9},{2,6},{6,2},{1... | collective-permute-start | bytes 491528 | tf_op jit(solution)/shard_map/ppermute | solution.py:19
  4.7 6.6 %collective-permute-start.8 = (bf16[128,640]{1,0:T(8,128)(2,1)S(1)}, bf16[128,640]{1,0:T(8,128)(2,1)S(1)}, u32[]{:S(2)}, u32[]{:S(2)}) collective-permute-start(bf16[128,640]{1,0:T(8,128)(2,1)S(1)} %shard_map.64.refs_11_), channel_id=1, source_target_pairs={{0,8},{4,12},{8,0},{12,4},{1,9},{5,13},{9,1},{13,5},{2,10},{6,14},... | collective-permute-start | bytes 491528 | tf_op jit(solution)/shard_map/ppermute | solution.py:19
  6.3 14.7 %collective-permute-start.14 = (bf16[128,1024]{1,0:T(8,128)(2,1)}, bf16[128,1024]{1,0:T(8,128)(2,1)S(1)}, u32[]{:S(2)}, u32[]{:S(2)}) collective-permute-start(bf16[128,1024]{1,0:T(8,128)(2,1)} %refs_2_.1), channel_id=1, source_target_pairs={{0,3},{1,2},{2,1},{3,0},{4,7},{5,6},{6,5},{7,4},{8,11},{9,10},{10,... | collective-permute-start | bytes 786440 | tf_op jit(solution)/shard_map/ppermute | solution.py:19
  8.7 14.5 %collective-permute-start.3 = (bf16[128,1024]{1,0:T(8,128)(2,1)S(1)}, bf16[128,1024]{1,0:T(8,128)(2,1)S(1)}, u32[]{:S(2)}, u32[]{:S(2)}) collective-permute-start(bf16[128,1024]{1,0:T(8,128)(2,1)S(1)} %copy-done), channel_id=1, source_target_pairs={{0,4},{4,0},{8,12},{12,8},{1,5},{5,1},{9,13},{13,9},{2,6},{6,2},{1... | collective-permute-start | bytes 786440 | tf_op jit(solution)/shard_map/ppermute | solution.py:19
  8.7 14.7 %collective-permute-start.1 = (bf16[128,1024]{1,0:T(8,128)(2,1)S(1)}, bf16[128,1024]{1,0:T(8,128)(2,1)S(1)}, u32[]{:S(2)}, u32[]{:S(2)}) collective-permute-start(bf16[128,1024]{1,0:T(8,128)(2,1)S(1)} %copy-done), channel_id=1, source_target_pairs={{0,8},{4,12},{8,0},{12,4},{1,9},{5,13},{9,1},{13,5},{2,10},{6,14},... | collective-permute-start | bytes 786440 | tf_op jit(solution)/shard_map/ppermute | solution.py:19
  9.6 14.1 %collective-permute-start.2 = (bf16[128,1024]{1,0:T(8,128)(2,1)S(1)}, bf16[128,1024]{1,0:T(8,128)(2,1)S(1)}, u32[]{:S(2)}, u32[]{:S(2)}) collective-permute-start(bf16[128,1024]{1,0:T(8,128)(2,1)S(1)} %collective-permute-done.refs_4_), channel_id=1, source_target_pairs={{0,8},{4,12},{8,0},{12,4},{1,9},{5,13},{9,1},{13,5},{2,10},{6,14},... | collective-permute-start | bytes 786440 | tf_op jit(solution)/shard_map/ppermute | solution.py:19
  11.3 9.6 %collective-permute-start.7 = (bf16[128,640]{1,0:T(8,128)(2,1)S(1)}, bf16[128,640]{1,0:T(8,128)(2,1)S(1)}, u32[]{:S(2)}, u32[]{:S(2)}) collective-permute-start(bf16[128,640]{1,0:T(8,128)(2,1)S(1)} %shard_map.64.refs_11_), channel_id=1, source_target_pairs={{0,1},{1,0},{2,3},{3,2},{4,5},{5,4},{6,7},{7,6},{8,9},{9,8},{10,11... | collective-permute-start | bytes 491528 | tf_op jit(solution)/shard_map/ppermute | solution.py:19
  21.0 3.0 %collective-permute-start.12 = (bf16[128,640]{1,0:T(8,128)(2,1)S(1)}, bf16[128,640]{1,0:T(8,128)(2,1)S(1)}, u32[]{:S(2)}, u32[]{:S(2)}) collective-permute-start(bf16[128,640]{1,0:T(8,128)(2,1)S(1)} %collective-permute-done.8.refs_13_), channel_id=1, source_target_pairs={{0,4},{4,0},{8,12},{12,8},{1,5},{5,1},{9,13},{13,9},{2,6},{6,2},{1... | collective-permute-start | bytes 491528 | tf_op jit(solution)/shard_map/ppermute | solution.py:19
  21.0 0.7 %copy-start.1 = (bf16[128,1024]{1,0:T(8,128)(2,1)}, bf16[128,1024]{1,0:T(8,128)(2,1)S(1)}, u32[]{:S(2)}) copy-start(bf16[128,1024]{1,0:T(8,128)(2,1)S(1)} %collective-permute-done.14.refs_2_) | copy-start | bytes 786436
  21.7 6.6 %collective-permute-start.9 = (bf16[128,640]{1,0:T(8,128)(2,1)S(1)}, bf16[128,640]{1,0:T(8,128)(2,1)S(1)}, u32[]{:S(2)}, u32[]{:S(2)}) collective-permute-start(bf16[128,640]{1,0:T(8,128)(2,1)S(1)} %collective-permute-done.7.refs_12_), channel_id=1, source_target_pairs={{0,8},{4,12},{8,0},{12,4},{1,9},{5,13},{9,1},{13,5},{2,10},{6,14},... | collective-permute-start | bytes 491528 | tf_op jit(solution)/shard_map/ppermute | solution.py:19
  23.2 6.5 %collective-permute-start.4 = (bf16[128,1024]{1,0:T(8,128)(2,1)S(1)}, bf16[128,1024]{1,0:T(8,128)(2,1)S(1)}, u32[]{:S(2)}, u32[]{:S(2)}) collective-permute-start(bf16[128,1024]{1,0:T(8,128)(2,1)S(1)} %collective-permute-done.refs_4_), channel_id=1, source_target_pairs={{0,4},{4,0},{8,12},{12,8},{1,5},{5,1},{9,13},{13,9},{2,6},{6,2},{1... | collective-permute-start | bytes 786440 | tf_op jit(solution)/shard_map/ppermute | solution.py:19
  23.4 6.3 %collective-permute-start.5 = (bf16[128,1024]{1,0:T(8,128)(2,1)S(1)}, bf16[128,1024]{1,0:T(8,128)(2,1)S(1)}, u32[]{:S(2)}, u32[]{:S(2)}) collective-permute-start(bf16[128,1024]{1,0:T(8,128)(2,1)S(1)} %collective-permute-done.1.refs_5_), channel_id=1, source_target_pairs={{0,4},{4,0},{8,12},{12,8},{1,5},{5,1},{9,13},{13,9},{2,6},{6,2},{1... | collective-permute-start | bytes 786440 | tf_op jit(solution)/shard_map/ppermute | solution.py:19
  23.7 6.0 %collective-permute-start.6 = (bf16[128,1024]{1,0:T(8,128)(2,1)S(1)}, bf16[128,1024]{1,0:T(8,128)(2,1)S(1)}, u32[]{:S(2)}, u32[]{:S(2)}) collective-permute-start(bf16[128,1024]{1,0:T(8,128)(2,1)S(1)} %collective-permute-done.2.refs_6_), channel_id=1, source_target_pairs={{0,4},{4,0},{8,12},{12,8},{1,5},{5,1},{9,13},{13,9},{2,6},{6,2},{1... | collective-permute-start | bytes 786440 | tf_op jit(solution)/shard_map/ppermute | solution.py:19
  23.9 4.5 %collective-permute-start.11 = (bf16[128,640]{1,0:T(8,128)(2,1)S(1)}, bf16[128,640]{1,0:T(8,128)(2,1)S(1)}, u32[]{:S(2)}, u32[]{:S(2)}) collective-permute-start(bf16[128,640]{1,0:T(8,128)(2,1)S(1)} %collective-permute-done.7.refs_12_), channel_id=1, source_target_pairs={{0,4},{4,0},{8,12},{12,8},{1,5},{5,1},{9,13},{13,9},{2,6},{6,2},{1... | collective-permute-start | bytes 491528 | tf_op jit(solution)/shard_map/ppermute | solution.py:19
  28.3 1.4 %collective-permute-start.13 = (bf16[128,640]{1,0:T(8,128)(2,1)S(1)}, bf16[128,640]{1,0:T(8,128)(2,1)S(1)}, u32[]{:S(2)}, u32[]{:S(2)}) collective-permute-start(bf16[128,640]{1,0:T(8,128)(2,1)S(1)} %collective-permute-done.9.refs_14_), channel_id=1, source_target_pairs={{0,4},{4,0},{8,12},{12,8},{1,5},{5,1},{9,13},{13,9},{2,6},{6,2},{1... | collective-permute-start | bytes 491528 | tf_op jit(solution)/shard_map/ppermute | solution.py:19
  29.7 1.0 %copy-start.2 = (bf16[128,1024]{1,0:T(8,128)(2,1)S(1)}, bf16[128,1024]{1,0:T(8,128)(2,1)}, u32[]{:S(2)}) copy-start(bf16[128,1024]{1,0:T(8,128)(2,1)} %copy-done.1) | copy-start | bytes 786436
  30.7 6.4 %copy-start.3 = (bf16[128,1024]{1,0:T(8,128)(2,1)S(1)}, bf16[128,1024]{1,0:T(8,128)(2,1)}, u32[]{:S(2)}) copy-start(bf16[128,1024]{1,0:T(8,128)(2,1)} %refs_2_.1) | copy-start | bytes 786436
  31.7 10.1 %collective-permute-start.15 = (bf16[128,640]{1,0:T(8,128)(2,1)S(1)}, bf16[128,640]{1,0:T(8,128)(2,1)S(1)}, u32[]{:S(2)}, u32[]{:S(2)}) collective-permute-start(bf16[128,640]{1,0:T(8,128)(2,1)S(1)} %shard_map.66), channel_id=1, source_target_pairs={{0,3},{1,2},{2,1},{3,0},{4,7},{5,6},{6,5},{7,4},{8,11},{9,10},{10,... | collective-permute-start | bytes 491528 | tf_op jit(solution)/shard_map/ppermute | solution.py:19

commit v2 on v1

v2 whole, which is shorter than its diff:
```python
import functools
import math

import jax
import jax.numpy as jnp
from jax import lax
from jax.experimental import pallas as pl
from jax.experimental.pallas import tpu as pltpu
from jax.sharding import PartitionSpec as P

TILE = 128
LANES = 128
EXTRA = 16
MASKED_SCORE = -1e30
SMEM = pl.BlockSpec(memory_space=pltpu.SMEM)
VMEM = pl.BlockSpec(memory_space=pltpu.VMEM)


def params(operand_bytes=0):
    return pltpu.CompilerParams(vmem_limit_bytes=operand_bytes * 3 // 2 + 6 * 1024 * 1024)


def swap(value, axis, mask):
    length = lax.axis_size(axis)
    return lax.ppermute(value, axis, [(i, i ^ mask) for i in range(length)])


def tie(*values):
    return lax.optimization_barrier(values)


def split_three(value):
    high = value.astype(jnp.bfloat16)
    rest = value - high.astype(jnp.float32)
    middle = rest.astype(jnp.bfloat16)
    low = (rest - middle.astype(jnp.float32)).astype(jnp.bfloat16)
    return high, middle, low


def pack_kernel(values_ref, scale_ref, packed_ref):
    value_width = values_ref.shape[1]
    packed_ref[0:TILE, :] = values_ref[...]
    row = scale_ref[...].astype(jnp.float32)
    packed_ref[TILE:, 0:TILE] = jnp.broadcast_to(row, (EXTRA, TILE)).astype(jnp.bfloat16)
    packed_ref[TILE:, TILE:] = jnp.zeros((EXTRA, value_width - TILE), jnp.bfloat16)


def bundle_kernel(*refs):
    bundle_ref, at = refs[-1], 0
    width = bundle_ref.shape[1]
    for ref in refs[:-1]:
        rows = ref.shape[0]
        for column in range(0, ref.shape[1], width):
            bundle_ref[at : at + rows, :] = ref[:, column : column + width]
            at += rows


class Piece:
    def __init__(self, place, keys_ref=None, values_ref=None, bundle_ref=None, first_row=0):
        self.place = place
        self.refs = (keys_ref, values_ref, bundle_ref)
        self.first_row = first_row

    def scores(self, query_ref, inverse_root):
        keys_ref, values_ref, bundle_ref = self.refs
        width = query_ref.shape[1]
        dims = (((1,), (1,)), ((), ()))
        if bundle_ref is None:
            product = lax.dot_general(query_ref[...], keys_ref[...], dims, preferred_element_type=jnp.float32)
            scale = values_ref[TILE : TILE + EXTRA, 0:TILE]
        else:
            group = bundle_ref.shape[1]
            product = 0.0
            for at in range(width // group):
                rows = pl.ds(self.first_row + at * TILE, TILE)
                product = product + lax.dot_general(
                    query_ref[:, at * group : (at + 1) * group],
                    bundle_ref[rows, :],
                    dims,
                    preferred_element_type=jnp.float32,
                )
            scale = bundle_ref[pl.ds(self.first_row + width // group * TILE + TILE, EXTRA), 0:TILE]
        return product * (scale.astype(jnp.float32)[0:1] * inverse_root)

    def values(self, width):
        keys_ref, values_ref, bundle_ref = self.refs
        if bundle_ref is None:
            return values_ref[0:TILE, :]
        return bundle_ref[pl.ds(self.first_row + width // bundle_ref.shape[1] * TILE, TILE), :]


def read_pieces(layout, width, refs):
    pieces = []
    for entry in layout:
        if entry[0] == "pair":
            pieces.append(Piece(entry[1], refs[0], refs[1]))
            refs = refs[2:]
        else:
            for at, place in enumerate(entry[1]):
                group = refs[0].shape[1]
                rows = (width // group + 1) * TILE + EXTRA
                pieces.append(Piece(place, bundle_ref=refs[0], first_row=at * rows))
            refs = refs[1:]
    return pieces, refs


def attend(pieces, panel_mask, lists_ref, counts_ref, query_ref, score_ref, total_ref, mass_ref):
    lib_index = lax.axis_index("lib")
    qry_index = lax.axis_index("qry")
    qry_count = lax.axis_size("qry")
    block_total = lax.axis_size("lib") * qry_count
    panel = lib_index * qry_count + lax.bitwise_xor(qry_index, panel_mask)
    first = lists_ref[panel, 0]
    count = counts_ref[panel]
    width = query_ref.shape[1]
    inverse_root = 1.0 / math.sqrt(width)

    def active(lib_mask, qry_mask):
        block = lax.bitwise_xor(lib_index, lib_mask) * qry_count + lax.bitwise_xor(qry_index, qry_mask)
        return lax.rem(block - first + block_total, block_total) < count

    flags = [active(*piece.place) for piece in pieces]
    score_ref[...] = jnp.full(score_ref.shape, MASKED_SCORE, jnp.float32)
    total_ref[...] = jnp.zeros(total_ref.shape, jnp.float32)
    mass_ref[...] = jnp.zeros(mass_ref.shape, jnp.float32)
    for at, (piece, flag) in enumerate(zip(pieces, flags)):

        @pl.when(flag)
        def _(at=at, piece=piece):
            score_ref[at] = piece.scores(query_ref, inverse_root)

    largest = score_ref[0]
    for at in range(1, len(flags)):
        largest = jnp.maximum(largest, score_ref[at])
    row_max = jnp.max(largest, axis=1, keepdims=True)
    for at, (piece, flag) in enumerate(zip(pieces, flags)):

        @pl.when(flag)
        def _(at=at, piece=piece):
            weights = jnp.exp(score_ref[at] - row_max)
            mass_ref[...] += weights
            weight_high = weights.astype(jnp.bfloat16)
            weight_low = (weights - weight_high.astype(jnp.float32)).astype(jnp.bfloat16)
            values = piece.values(width)
            added = jnp.dot(weight_high, values, preferred_element_type=jnp.float32)
            added = added + jnp.dot(weight_low, values, preferred_element_type=jnp.float32)
            total_ref[...] += added

    return row_max


def visit_kernel(layout, panel_mask, lists_ref, counts_ref, query_ref, *refs):
    pieces, refs = read_pieces(layout, query_ref.shape[1], refs)
    packed_ref, score_ref, total_ref, mass_ref = refs
    row_max = attend(pieces, panel_mask, lists_ref, counts_ref, query_ref, score_ref, total_ref, mass_ref)
    row_sum = jnp.sum(mass_ref[...], axis=1, keepdims=True)
    value_width = total_ref.shape[1]
    divisor = jnp.where(row_sum > 0.0, row_sum, 1.0)
    packed_ref[0:TILE, :] = (total_ref[...] / divisor).astype(jnp.bfloat16)
    row = lax.broadcasted_iota(jnp.int32, (EXTRA, LANES), 0)
    packed = jnp.zeros((EXTRA, LANES), jnp.float32)
    for first, column in ((0, row_max), (3, row_sum)):
        turned = jnp.transpose(jnp.broadcast_to(column, (TILE, LANES)))[0:EXTRA]
        for at, part in enumerate(split_three(turned)):
            packed = jnp.where(row == first + at, part.astype(jnp.float32), packed)
    packed_ref[TILE:, 0:LANES] = packed.astype(jnp.bfloat16)
    packed_ref[TILE:, LANES:] = jnp.zeros((EXTRA, value_width - LANES), jnp.bfloat16)


def home_kernel(layout, lists_ref, counts_ref, query_ref, *refs):
    pieces, refs = read_pieces(layout, query_ref.shape[1], refs)
    total_ref, stats_ref, score_ref, mass_ref = refs
    row_max = attend(pieces, 0, lists_ref, counts_ref, query_ref, score_ref, total_ref, mass_ref)
    row_sum = jnp.sum(mass_ref[...], axis=1, keepdims=True)
    stats_ref[0] = jnp.broadcast_to(row_max, (TILE, LANES))
    stats_ref[1] = jnp.broadcast_to(row_sum, (TILE, LANES))


def merge_kernel(total_ref, stats_ref, *refs):
    packed_refs, out_ref = refs[:-1], refs[-1]
    maxima = [stats_ref[0]]
    sums = [stats_ref[1]]
    for packed_ref in packed_refs:
        packed = packed_ref[TILE:, 0:LANES].astype(jnp.float32)
        for first, kept in ((0, maxima), (3, sums)):
            line = packed[first : first + 1] + packed[first + 1 : first + 2] + packed[first + 2 : first + 3]
            kept.append(jnp.transpose(jnp.broadcast_to(line, (TILE, LANES))))
    top = functools.reduce(jnp.maximum, maxima)
    factors = [jnp.exp(row_max - top) for row_max in maxima]
    masses = [factor * row_sum for factor, row_sum in zip(factors, sums)]
    inverse = 1.0 / functools.reduce(jnp.add, masses)
    scales = [factors[0] * inverse] + [mass * inverse for mass in masses[1:]]
    for at in range(0, total_ref.shape[1], LANES):
        merged = total_ref[:, at : at + LANES] * scales[0]
        for packed_ref, scale in zip(packed_refs, scales[1:]):
            merged = merged + packed_ref[0:TILE, at : at + LANES].astype(jnp.float32) * scale
        out_ref[:, at : at + LANES] = merged.astype(jnp.bfloat16)


def gather_library(keys, values):
    steps = [("qry", 1)]
    mask = lax.axis_size("lib") // 2
    while mask > 1:
        steps.append(("lib", mask))
        mask //= 2
    early, late = [((0, 0), keys, values)], []
    for axis, mask in steps:
        place = (0, mask) if axis == "qry" else (mask, 0)
        near = (place, swap(keys, axis, mask), swap(values, axis, mask))
        relayed = []
        for (lib_mask, qry_mask), far_keys, far_values in early[1:] + late:
            far_keys, _ = tie(far_keys, near[1])
            far_values, _ = tie(far_values, near[2])
            place = (lib_mask | mask, qry_mask)
            relayed.append((place, swap(far_keys, axis, mask), swap(far_values, axis, mask)))
        early, late = early + late + [near], relayed
    return early, late


def body(queries, library_keys, library_values, key_scale, block_list, block_count):
    qry_count = lax.axis_size("qry")
    width = library_keys.shape[1]
    value_width = library_values.shape[1]

    values = pl.pallas_call(
        pack_kernel,
        out_shape=jax.ShapeDtypeStruct((TILE + EXTRA, value_width), jnp.bfloat16),
        in_specs=[VMEM, VMEM],
        out_specs=VMEM,
        compiler_params=params(),
    )(library_values, key_scale.reshape(1, TILE))

    early, late = gather_library(library_keys, values)
    piece_rows = (width // value_width + 1) * TILE + EXTRA
    early_arrays = [array for piece in early for array in piece[1:]]
    bundle = pl.pallas_call(
        bundle_kernel,
        out_shape=jax.ShapeDtypeStruct((len(early) * piece_rows, value_width), jnp.bfloat16),
        in_specs=[VMEM] * len(early_arrays),
        out_specs=VMEM,
        compiler_params=params(2 * len(early) * piece_rows * value_width * 2),
    )(*early_arrays)
    bundle, *_ = tie(bundle, *(piece[1] for piece in late))
    bundle = swap(bundle, "lib", 1)
    layout = [("pair", piece[0]) for piece in early]
    layout.append(("bundle", [(lib_mask | 1, qry_mask) for (lib_mask, qry_mask), *_ in early]))
    arrays = early_arrays + [bundle]
    for (lib_mask, qry_mask), *pair in late:
        layout += [("pair", (lib_mask, qry_mask)), ("pair", (lib_mask | 1, qry_mask))]
        arrays += pair + [swap(array, "lib", 1) for array in pair]

    count = 2 * (len(early) + len(late))
    cost = pl.CostEstimate(flops=2 * TILE * 4 * TILE * width * 2, bytes_accessed=4 * 1024 * 1024, transcendentals=0)
    scratch = [
        pltpu.VMEM((count, TILE, TILE), jnp.float32),
        pltpu.VMEM((TILE, value_width), jnp.float32),
        pltpu.VMEM((TILE, TILE), jnp.float32),
    ]
    attend_params = params(count * piece_rows * value_width * 2)
    in_specs = [SMEM, SMEM] + [VMEM] * (1 + len(arrays))
    returned = []
    for at in range(1, qry_count // 2):
        visitors, *_ = tie(queries, early[1][1], early[1][2])
        visitors = swap(visitors, "qry", 2 * at + 1)
        packed = pl.pallas_call(
            functools.partial(visit_kernel, layout, 2 * at + 1),
            out_shape=jax.ShapeDtypeStruct((TILE + EXTRA, value_width), jnp.bfloat16),
            in_specs=in_specs,
            out_specs=VMEM,
            scratch_shapes=scratch,
            compiler_params=attend_params,
            cost_estimate=cost,
        )(block_list, block_count, visitors, *arrays)
        returned.append(swap(packed, "qry", 2 * at + 1))

    total, stats = pl.pallas_call(
        functools.partial(home_kernel, layout),
        out_shape=(
            jax.ShapeDtypeStruct((TILE, value_width), jnp.float32),
            jax.ShapeDtypeStruct((2, TILE, LANES), jnp.float32),
        ),
        in_specs=in_specs,
        out_specs=(VMEM, VMEM),
        scratch_shapes=[scratch[0], scratch[2]],
        compiler_params=attend_params,
        cost_estimate=cost,
    )(block_list, block_count, queries, *arrays)

    return pl.pallas_call(
        merge_kernel,
        out_shape=jax.ShapeDtypeStruct((TILE, value_width), jnp.bfloat16),
        in_specs=[VMEM] * (2 + len(returned)),
        out_specs=VMEM,
        compiler_params=params(),
    )(total, stats, *returned)


def solution(mesh):
    in_specs = (
        P(("groups", "lib", "qry"), None),
        P(("groups", "lib", "qry"), None),
        P(("groups", "lib", "qry"), None),
        P(("groups", "lib", "qry")),
        P("groups", None),
        P("groups"),
    )
    out_specs = P(("groups", "lib", "qry"), None)
    return jax.shard_map(body, mesh=mesh, in_specs=in_specs, out_specs=out_specs, check_vma=False)
```

time: 42.3 us -> 46.1 us (1.090)
  the two profiles are of different devices: /device:TPU:0 before, /device:TPU:20 now
where the time goes in v2:
time: 46.1 us; the launch traced here: 45.9 us
  waiting for transfers between devices  30.7 us (67%)
  starting transfers between devices  7.39 us (16%)
  Pallas kernels  5.16 us (11%)
  local copies, waits for them, and re-layouts  2.61 us (6%)
    ppermute x11, waiting for transfers between devices, swap(): return lax.ppermute(value, axis, [(i, i ^ mask) for i in range(length)])  30.7 us
    ppermute x11, starting transfers between devices, swap(): return lax.ppermute(value, axis, [(i, i ^ mask) for i in range(length)])  7.39 us
    unnamed x15, local copies, waits for them, and re-layouts  2.61 us
    pallas_call x1, Pallas kernels, body(): pl.pallas_call(functools.partial(visit_kernel, layout, 2 * at + 1), out_s...  2.21 us
    pallas_call x1, Pallas kernels, body(): pl.pallas_call(bundle_kernel, out_shape=jax.ShapeDtypeStruct((len(early)...  1.14 us
    pallas_call x1, Pallas kernels, body(): pl.pallas_call(functools.partial(home_kernel, layout), out_shape=(jax.Sha...  0.99 us
  transfers between devices with their start and end apart: 11, of which 8 were waited for; matrix products, arithmetic and copies ran while one was open for 0% of the time, Pallas kernels for 5%

profile of v2, /device:TPU:20, one launch (start us, length us, event | category | flops | bytes accessed | tf_op | source)
XLA Modules:
  0.0 45.9 jit_solution(3047114641703297845)
XLA Ops:
  0.0 1.6 %collective-permute-start = (bf16[128,1024]{1,0:T(8,128)(2,1)}, bf16[128,1024]{1,0:T(8,128)(2,1)S(1)}, u32[]{:S(2)}, u32[]{:S(2)}) collective-permute-start(bf16[128,1024]{1,0:T(8,128)(2,1)} %refs_0_.5), channel_id=1, source_target_pairs={{0,1},{1,0},{2,3},{3,2},{4,5},{5,4},{6,7},{7,6},{8,9},{9,8},{10,11... | collective-permute-start | bytes 786440 | tf_op jit(solution)/shard_map/ppermute | solution.py:25
  1.6 1.5 %collective-permute-start.2 = (bf16[128,1024]{1,0:T(8,128)(2,1)}, bf16[128,1024]{1,0:T(8,128)(2,1)S(1)}, u32[]{:S(2)}, u32[]{:S(2)}) collective-permute-start(bf16[128,1024]{1,0:T(8,128)(2,1)} %refs_0_.5), channel_id=1, source_target_pairs={{0,8},{4,12},{8,0},{12,4},{1,9},{5,13},{9,1},{13,5},{2,10},{6,14},... | collective-permute-start | bytes 786440 | tf_op jit(solution)/shard_map/ppermute | solution.py:25
  3.1 5.2 %collective-permute-done.refs_2_ = bf16[128,1024]{1,0:T(8,128)(2,1)S(1)} collective-permute-done((bf16[128,1024]{1,0:T(8,128)(2,1)}, bf16[128,1024]{1,0:T(8,128)(2,1)S(1)}, u32[]{:S(2)}, u32[]{:S(2)}) %collective-permute-start) | collective-permute-done | bytes 262176 | tf_op jit(solution)/shard_map/ppermute | solution.py:25
  8.3 1.3 %collective-permute-done.2.refs_4_ = bf16[128,1024]{1,0:T(8,128)(2,1)S(1)} collective-permute-done((bf16[128,1024]{1,0:T(8,128)(2,1)}, bf16[128,1024]{1,0:T(8,128)(2,1)S(1)}, u32[]{:S(2)}, u32[]{:S(2)}) %collective-permute-start.2) | collective-permute-done | bytes 262176 | tf_op jit(solution)/shard_map/ppermute | solution.py:25
  9.6 1.5 %collective-permute-start.4 = (bf16[128,1024]{1,0:T(8,128)(2,1)S(1)}, bf16[128,1024]{1,0:T(8,128)(2,1)S(1)}, u32[]{:S(2)}, u32[]{:S(2)}) collective-permute-start(bf16[128,1024]{1,0:T(8,128)(2,1)S(1)} %collective-permute-done.refs_2_), channel_id=1, source_target_pairs={{0,8},{4,12},{8,0},{12,4},{1,9},{5,13},{9,1},{13,5},{2,10},{6,14},... | collective-permute-start | bytes 786440 | tf_op jit(solution)/shard_map/ppermute | solution.py:25
  11.0 0.9 %copy-done.3 = bf16[128,512]{1,0:T(8,128)(2,1)S(1)} copy-done((bf16[128,512]{1,0:T(8,128)(2,1)S(1)}, bf16[128,512]{1,0:T(8,128)(2,1)}, u32[]{:S(2)}) %copy-start.3) | copy-done | bytes 131096
  12.0 0.7 %copy-done.5 = bf16[128]{0:T(256)(128)(2,1)S(1)} copy-done((bf16[128]{0:T(256)(128)(2,1)S(1)}, bf16[128]{0:T(256)(128)(2,1)}, u32[]{:S(2)}) %copy-start.5) | copy-done | bytes 280
  12.6 0.5 %collective-permute-start.1 = (bf16[144,512]{1,0:T(8,128)(2,1)S(1)}, bf16[144,512]{1,0:T(8,128)(2,1)S(1)}, u32[]{:S(2)}, u32[]{:S(2)}) collective-permute-start(bf16[144,512]{1,0:T(8,128)(2,1)S(1)} %shard_map.64.refs_1_), channel_id=1, source_target_pairs={{0,1},{1,0},{2,3},{3,2},{4,5},{5,4},{6,7},{7,6},{8,9},{9,8},{10,11... | collective-permute-start | bytes 442376 | tf_op jit(solution)/shard_map/ppermute | solution.py:25
  13.1 0.5 %collective-permute-start.3 = (bf16[144,512]{1,0:T(8,128)(2,1)S(1)}, bf16[144,512]{1,0:T(8,128)(2,1)S(1)}, u32[]{:S(2)}, u32[]{:S(2)}) collective-permute-start(bf16[144,512]{1,0:T(8,128)(2,1)S(1)} %shard_map.64.refs_1_), channel_id=1, source_target_pairs={{0,8},{4,12},{8,0},{12,4},{1,9},{5,13},{9,1},{13,5},{2,10},{6,14},... | collective-permute-start | bytes 442376 | tf_op jit(solution)/shard_map/ppermute | solution.py:25
  13.7 4.2 %collective-permute-done.1.refs_3_ = bf16[144,512]{1,0:T(8,128)(2,1)S(1)} collective-permute-done((bf16[144,512]{1,0:T(8,128)(2,1)S(1)}, bf16[144,512]{1,0:T(8,128)(2,1)S(1)}, u32[]{:S(2)}, u32[]{:S(2)}) %collective-permute-start.1) | collective-permute-done | bytes 147488 | tf_op jit(solution)/shard_map/ppermute | solution.py:25
  17.8 1.7 %collective-permute-done.3.refs_5_ = bf16[144,512]{1,0:T(8,128)(2,1)S(1)} collective-permute-done((bf16[144,512]{1,0:T(8,128)(2,1)S(1)}, bf16[144,512]{1,0:T(8,128)(2,1)S(1)}, u32[]{:S(2)}, u32[]{:S(2)}) %collective-permute-start.3) | collective-permute-done | bytes 147488 | tf_op jit(solution)/shard_map/ppermute | solution.py:25
  19.6 0.9 %copy-done = bf16[128,1024]{1,0:T(8,128)(2,1)S(1)} copy-done((bf16[128,1024]{1,0:T(8,128)(2,1)S(1)}, bf16[128,1024]{1,0:T(8,128)(2,1)}, u32[]{:S(2)}) %copy-start) | copy-done | bytes 262168
  20.5 1.1 %shard_map.65 = bf16[1200,512]{1,0:T(8,128)(2,1)} custom-call(bf16[128,1024]{1,0:T(8,128)(2,1)S(1)} %copy-done, bf16[144,512]{1,0:T(8,128)(2,1)S(1)} %shard_map.64.refs_1_, bf16[128,1024]{1,0:T(8,128)(2,1)S(1)} %collective-permute-done.refs_2_, bf16[144,512]{1,0:T(8,128)(2,1)S(1)} %collective-permute-done.1.refs_3_, ...), custom_call_target="tpu_custom_call" | custom-call | tf_op jit(solution)/shard_map/pallas_call | solution.py:236
  21.7 0.0 collective-permute-done.4.refs_7_
  21.7 0.0 collective-permute-start.5
  21.7 1.5 %collective-permute-start.6 = (bf16[144,512]{1,0:T(8,128)(2,1)S(1)}, bf16[144,512]{1,0:T(8,128)(2,1)S(1)}, u32[]{:S(2)}, u32[]{:S(2)}) collective-permute-start(bf16[144,512]{1,0:T(8,128)(2,1)S(1)} %collective-permute-done.1.refs_3_), channel_id=1, source_target_pairs={{0,8},{4,12},{8,0},{12,4},{1,9},{5,13},{9,1},{13,5},{2,10},{6,14},... | collective-permute-start | bytes 442376 | tf_op jit(solution)/shard_map/ppermute | solution.py:25
  23.2 0.0 copy-done.2
  23.2 0.0 collective-permute-start.9
  23.2 0.2 collective-permute-start.7
  23.4 4.5 %collective-permute-done.6.refs_8_ = bf16[144,512]{1,0:T(8,128)(2,1)S(1)} collective-permute-done((bf16[144,512]{1,0:T(8,128)(2,1)S(1)}, bf16[144,512]{1,0:T(8,128)(2,1)S(1)}, u32[]{:S(2)}, u32[]{:S(2)}) %collective-permute-start.6) | collective-permute-done | bytes 147488 | tf_op jit(solution)/shard_map/ppermute | solution.py:25
  27.9 0.0 collective-permute-start.8
  27.9 0.1 copy.7.lists_ref
  28.0 1.3 %collective-permute-done.8.refs_10_ = bf16[144,512]{1,0:T(8,128)(2,1)S(1)} collective-permute-done((bf16[144,512]{1,0:T(8,128)(2,1)S(1)}, bf16[144,512]{1,0:T(8,128)(2,1)S(1)}, u32[]{:S(2)}, u32[]{:S(2)}) %collective-permute-start.8) | collective-permute-done | bytes 147488 | tf_op jit(solution)/shard_map/ppermute | solution.py:25
  29.3 8.0 %collective-permute-done.9.query_ref = bf16[128,1024]{1,0:T(8,128)(2,1)} collective-permute-done((bf16[128,1024]{1,0:T(8,128)(2,1)S(1)}, bf16[128,1024]{1,0:T(8,128)(2,1)}, u32[]{:S(2)}, u32[]{:S(2)}) %collective-permute-start.9) | collective-permute-done | bytes 262176 | tf_op jit(solution)/shard_map/ppermute | solution.py:25
  37.3 0.0 collective-permute-done.7.refs_9_
  37.3 0.0 collective-permute-done.5.refs_6_
  37.3 0.0 copy-done.4
  37.3 2.2 %shard_map.67 = bf16[144,512]{1,0:T(8,128)(2,1)S(1)} custom-call(s32[16,4]{1,0:T(8,128)S(1)} %copy.7.lists_ref, s32[16]{0:T(128)S(1)} %copy-done.4, bf16[128,1024]{1,0:T(8,128)(2,1)} %collective-permute-done.9.query_ref, bf16[128,1024]{1,0:T(8,128)(2,1)S(1)} %copy-done.1, bf16[144,512]{1,0:T(8,128)(2,1)S(1)} %shard_map.64.refs_1_, ...), custom_call_target="tpu_custom_call" | custom-call | flops 268435456 | bytes 4194304 | tf_op jit(solution)/shard_map/pallas_call | solution.py:265
  39.6 0.1 collective-permute-start.10
  39.6 1.0 %shard_map.66 = (f32[128,512]{1,0:T(8,128)S(1)}, f32[2,128,128]{2,1,0:T(8,128)S(1)}) custom-call(s32[16,4]{1,0:T(8,128)S(1)} %copy.7.lists_ref, s32[16]{0:T(128)S(1)} %copy-done.4, bf16[128,1024]{1,0:T(8,128)(2,1)S(1)} %copy-done.2, bf16[128,1024]{1,0:T(8,128)(2,1)S(1)} %copy-done.1, bf16[144,512]{1,0:T(8,128)(2,1)S(1)} %shard_map.64.refs_1_, ...), custom_call_target="tpu_custom_call" | custom-call | flops 268435456 | bytes 4194304 | tf_op jit(solution)/shard_map/pallas_call | solution.py:276
  40.6 4.5 %collective-permute-done.10.refs_0_ = bf16[144,512]{1,0:T(8,128)(2,1)S(1)} collective-permute-done((bf16[144,512]{1,0:T(8,128)(2,1)S(1)}, bf16[144,512]{1,0:T(8,128)(2,1)S(1)}, u32[]{:S(2)}, u32[]{:S(2)}) %collective-permute-start.10) | collective-permute-done | bytes 147488 | tf_op jit(solution)/shard_map/ppermute | solution.py:25
  45.1 0.8 %shard_map.68 = bf16[128,512]{1,0:T(8,128)(2,1)} custom-call(f32[128,512]{1,0:T(8,128)S(1)} %get-tuple-element.14.total_ref, f32[2,128,128]{2,1,0:T(8,128)S(1)} %get-tuple-element.15.stats_ref, bf16[144,512]{1,0:T(8,128)(2,1)S(1)} %collective-permute-done.10.refs_0_), custom_call_target="tpu_custom_call" | custom-call | tf_op jit(solution)/shard_map/pallas_call | solution.py:289
  (10 shorter events, 0.0 us)
Async XLA Ops:
  0.0 8.3 %collective-permute-start = (bf16[128,1024]{1,0:T(8,128)(2,1)}, bf16[128,1024]{1,0:T(8,128)(2,1)S(1)}, u32[]{:S(2)}, u32[]{:S(2)}) collective-permute-start(bf16[128,1024]{1,0:T(8,128)(2,1)} %refs_0_.5), channel_id=1, source_target_pairs={{0,1},{1,0},{2,3},{3,2},{4,5},{5,4},{6,7},{7,6},{8,9},{9,8},{10,11... | collective-permute-start | bytes 786440 | tf_op jit(solution)/shard_map/ppermute | solution.py:25
  1.6 8.0 %collective-permute-start.2 = (bf16[128,1024]{1,0:T(8,128)(2,1)}, bf16[128,1024]{1,0:T(8,128)(2,1)S(1)}, u32[]{:S(2)}, u32[]{:S(2)}) collective-permute-start(bf16[128,1024]{1,0:T(8,128)(2,1)} %refs_0_.5), channel_id=1, source_target_pairs={{0,8},{4,12},{8,0},{12,4},{1,9},{5,13},{9,1},{13,5},{2,10},{6,14},... | collective-permute-start | bytes 786440 | tf_op jit(solution)/shard_map/ppermute | solution.py:25
  9.6 12.1 %collective-permute-start.4 = (bf16[128,1024]{1,0:T(8,128)(2,1)S(1)}, bf16[128,1024]{1,0:T(8,128)(2,1)S(1)}, u32[]{:S(2)}, u32[]{:S(2)}) collective-permute-start(bf16[128,1024]{1,0:T(8,128)(2,1)S(1)} %collective-permute-done.refs_2_), channel_id=1, source_target_pairs={{0,8},{4,12},{8,0},{12,4},{1,9},{5,13},{9,1},{13,5},{2,10},{6,14},... | collective-permute-start | bytes 786440 | tf_op jit(solution)/shard_map/ppermute | solution.py:25
  11.0 0.9 %copy-start.3 = (bf16[128,512]{1,0:T(8,128)(2,1)S(1)}, bf16[128,512]{1,0:T(8,128)(2,1)}, u32[]{:S(2)}) copy-start(bf16[128,512]{1,0:T(8,128)(2,1)} %values_ref.1) | copy-start | bytes 393220
  12.0 0.7 %copy-start.5 = (bf16[128]{0:T(256)(128)(2,1)S(1)}, bf16[128]{0:T(256)(128)(2,1)}, u32[]{:S(2)}) copy-start(bf16[128]{0:T(256)(128)(2,1)} %param.9) | copy-start | bytes 772
  12.6 15.3 %copy-start.6 = (s32[16,4]{0,1:T(4,128)S(1)}, s32[16,4]{0,1:T(4,128)}, u32[]{:S(2)}) copy-start(s32[16,4]{0,1:T(4,128)} %param.10) | copy-start | bytes 772
  12.6 24.7 %copy-start.1 = (bf16[128,1024]{1,0:T(8,128)(2,1)S(1)}, bf16[128,1024]{1,0:T(8,128)(2,1)}, u32[]{:S(2)}) copy-start(bf16[128,1024]{1,0:T(8,128)(2,1)} %refs_0_.5) | copy-start | bytes 786436
  12.6 24.7 %copy-start.4 = (s32[16]{0:T(128)S(1)}, s32[16]{0:T(128)}, u32[]{:S(2)}) copy-start(s32[16]{0:T(128)} %counts_ref.3) | copy-start | bytes 196
  12.6 5.2 %collective-permute-start.1 = (bf16[144,512]{1,0:T(8,128)(2,1)S(1)}, bf16[144,512]{1,0:T(8,128)(2,1)S(1)}, u32[]{:S(2)}, u32[]{:S(2)}) collective-permute-start(bf16[144,512]{1,0:T(8,128)(2,1)S(1)} %shard_map.64.refs_1_), channel_id=1, source_target_pairs={{0,1},{1,0},{2,3},{3,2},{4,5},{5,4},{6,7},{7,6},{8,9},{9,8},{10,11... | collective-permute-start | bytes 442376 | tf_op jit(solution)/shard_map/ppermute | solution.py:25
  13.1 6.4 %collective-permute-start.3 = (bf16[144,512]{1,0:T(8,128)(2,1)S(1)}, bf16[144,512]{1,0:T(8,128)(2,1)S(1)}, u32[]{:S(2)}, u32[]{:S(2)}) collective-permute-start(bf16[144,512]{1,0:T(8,128)(2,1)S(1)} %shard_map.64.refs_1_), channel_id=1, source_target_pairs={{0,8},{4,12},{8,0},{12,4},{1,9},{5,13},{9,1},{13,5},{2,10},{6,14},... | collective-permute-start | bytes 442376 | tf_op jit(solution)/shard_map/ppermute | solution.py:25
  19.6 1.0 %copy-start = (bf16[128,1024]{1,0:T(8,128)(2,1)S(1)}, bf16[128,1024]{1,0:T(8,128)(2,1)}, u32[]{:S(2)}) copy-start(bf16[128,1024]{1,0:T(8,128)(2,1)} %refs_0_.5) | copy-start | bytes 786436
  20.5 2.6 %copy-start.2 = (bf16[128,1024]{1,0:T(8,128)(2,1)S(1)}, bf16[128,1024]{1,0:T(8,128)(2,1)}, u32[]{:S(2)}) copy-start(bf16[128,1024]{1,0:T(8,128)(2,1)} %query_ref.1) | copy-start | bytes 786436
  21.7 15.7 %collective-permute-start.5 = (bf16[1200,512]{1,0:T(8,128)(2,1)}, bf16[1200,512]{1,0:T(8,128)(2,1)S(1)}, u32[]{:S(2)}, u32[]{:S(2)}) collective-permute-start(bf16[1200,512]{1,0:T(8,128)(2,1)} %shard_map.65), channel_id=1, source_target_pairs={{0,4},{4,0},{8,12},{12,8},{1,5},{5,1},{9,13},{13,9},{2,6},{6,2},{1... | collective-permute-start | bytes 3686408 | tf_op jit(solution)/shard_map/ppermute | solution.py:25
  21.7 6.3 %collective-permute-start.6 = (bf16[144,512]{1,0:T(8,128)(2,1)S(1)}, bf16[144,512]{1,0:T(8,128)(2,1)S(1)}, u32[]{:S(2)}, u32[]{:S(2)}) collective-permute-start(bf16[144,512]{1,0:T(8,128)(2,1)S(1)} %collective-permute-done.1.refs_3_), channel_id=1, source_target_pairs={{0,8},{4,12},{8,0},{12,4},{1,9},{5,13},{9,1},{13,5},{2,10},{6,14},... | collective-permute-start | bytes 442376 | tf_op jit(solution)/shard_map/ppermute | solution.py:25
  23.2 14.2 %collective-permute-start.9 = (bf16[128,1024]{1,0:T(8,128)(2,1)S(1)}, bf16[128,1024]{1,0:T(8,128)(2,1)}, u32[]{:S(2)}, u32[]{:S(2)}) collective-permute-start(bf16[128,1024]{1,0:T(8,128)(2,1)S(1)} %copy-done.2), channel_id=1, source_target_pairs={{0,3},{1,2},{2,1},{3,0},{4,7},{5,6},{6,5},{7,4},{8,11},{9,10},{10,... | collective-permute-start | bytes 786440 | tf_op jit(solution)/shard_map/ppermute | solution.py:25
  23.2 14.2 %collective-permute-start.7 = (bf16[128,1024]{1,0:T(8,128)(2,1)S(1)}, bf16[128,1024]{1,0:T(8,128)(2,1)S(1)}, u32[]{:S(2)}, u32[]{:S(2)}) collective-permute-start(bf16[128,1024]{1,0:T(8,128)(2,1)S(1)} %collective-permute-done.4.refs_7_), channel_id=1, source_target_pairs={{0,4},{4,0},{8,12},{12,8},{1,5},{5,1},{9,13},{13,9},{2,6},{6,2},{1... | collective-permute-start | bytes 786440 | tf_op jit(solution)/shard_map/ppermute | solution.py:25
  27.9 1.4 %collective-permute-start.8 = (bf16[144,512]{1,0:T(8,128)(2,1)S(1)}, bf16[144,512]{1,0:T(8,128)(2,1)S(1)}, u32[]{:S(2)}, u32[]{:S(2)}) collective-permute-start(bf16[144,512]{1,0:T(8,128)(2,1)S(1)} %collective-permute-done.6.refs_8_), channel_id=1, source_target_pairs={{0,4},{4,0},{8,12},{12,8},{1,5},{5,1},{9,13},{13,9},{2,6},{6,2},{1... | collective-permute-start | bytes 442376 | tf_op jit(solution)/shard_map/ppermute | solution.py:25
  39.6 5.6 %collective-permute-start.10 = (bf16[144,512]{1,0:T(8,128)(2,1)S(1)}, bf16[144,512]{1,0:T(8,128)(2,1)S(1)}, u32[]{:S(2)}, u32[]{:S(2)}) collective-permute-start(bf16[144,512]{1,0:T(8,128)(2,1)S(1)} %shard_map.67), channel_id=1, source_target_pairs={{0,3},{1,2},{2,1},{3,0},{4,7},{5,6},{6,5},{7,4},{8,11},{9,10},{10,... | collective-permute-start | bytes 442376 | tf_op jit(solution)/shard_map/ppermute | solution.py:25

commit v3 on v2

--- a/solution.py
+++ b/solution.py
@@ -25,6 +25,12 @@
     return lax.ppermute(value, axis, [(i, i ^ mask) for i in range(length)])
 
 
+def swap_some(value, axis, mask, inner):
+    length = lax.axis_size(axis)
+    pairs = [(i, i ^ mask) for i in range(length) if (abs(i - (i ^ mask)) * 2 <= mask) == inner]
+    return lax.ppermute(value, axis, pairs)
+
+
 def tie(*values):
     return lax.optimization_barrier(values)
 
@@ -37,12 +43,19 @@
     return high, middle, low
 
 
-def pack_kernel(values_ref, scale_ref, packed_ref):
+def pack_kernel(values_ref, scale_ref, packed_ref, row_ref, sems):
     value_width = values_ref.shape[1]
-    packed_ref[0:TILE, :] = values_ref[...]
-    row = scale_ref[...].astype(jnp.float32)
+    copies = (
+        pltpu.make_async_copy(values_ref, packed_ref.at[pl.ds(0, TILE)], sems.at[0]),
+        pltpu.make_async_copy(scale_ref, row_ref, sems.at[1]),
+    )
+    for copy in copies:
+        copy.start()
+    packed_ref[TILE:, TILE:] = jnp.zeros((EXTRA, value_width - TILE), jnp.bfloat16)
+    for copy in reversed(copies):
+        copy.wait()
+    row = row_ref[...].astype(jnp.float32)
     packed_ref[TILE:, 0:TILE] = jnp.broadcast_to(row, (EXTRA, TILE)).astype(jnp.bfloat16)
-    packed_ref[TILE:, TILE:] = jnp.zeros((EXTRA, value_width - TILE), jnp.bfloat16)
 
 
 def bundle_kernel(*refs):
@@ -104,7 +117,7 @@
     return pieces, refs
 
 
-def attend(pieces, panel_mask, lists_ref, counts_ref, query_ref, score_ref, total_ref, mass_ref):
+def attend(pieces, panel_mask, lists_ref, counts_ref, query_ref, score_ref, total_ref, mass_ref, before=None):
     lib_index = lax.axis_index("lib")
     qry_index = lax.axis_index("qry")
     qry_count = lax.axis_size("qry")
@@ -121,8 +134,6 @@
 
     flags = [active(*piece.place) for piece in pieces]
     score_ref[...] = jnp.full(score_ref.shape, MASKED_SCORE, jnp.float32)
-    total_ref[...] = jnp.zeros(total_ref.shape, jnp.float32)
-    mass_ref[...] = jnp.zeros(mass_ref.shape, jnp.float32)
     for at, (piece, flag) in enumerate(zip(pieces, flags)):
 
         @pl.when(flag)
@@ -133,6 +144,18 @@
     for at in range(1, len(flags)):
         largest = jnp.maximum(largest, score_ref[at])
     row_max = jnp.max(largest, axis=1, keepdims=True)
+    if before is None:
+        total_ref[...] = jnp.zeros(total_ref.shape, jnp.float32)
+        mass_ref[...] = jnp.zeros(mass_ref.shape, jnp.float32)
+    else:
+        old_total_ref, old_mass_ref, old_max_ref = before
+        old_max = old_max_ref[...]
+        new_max = jnp.maximum(old_max, row_max)
+        shrink = jnp.exp(old_max - new_max)
+        row_max = new_max[:, 0:1]
+        mass_ref[...] = old_mass_ref[...] * shrink
+        for at in range(0, total_ref.shape[1], LANES):
+            total_ref[:, at : at + LANES] = old_total_ref[:, at : at + LANES] * shrink
     for at, (piece, flag) in enumerate(zip(pieces, flags)):
 
         @pl.when(flag)
@@ -149,14 +172,37 @@
     return row_max
 
 
-def visit_kernel(layout, panel_mask, lists_ref, counts_ref, query_ref, *refs):
+def is_inner(mask):
+    index = lax.axis_index("qry")
+    return jnp.abs(index - lax.bitwise_xor(index, mask)) * 2 <= mask
+
+
+def early_kernel(layout, panel_mask, lists_ref, counts_ref, inner_ref, outer_ref, *refs):
+    pieces, refs = read_pieces(layout, inner_ref.shape[1], refs)
+    query_ref, total_ref, mass_ref, max_ref, score_ref = refs
+    inner = is_inner(panel_mask)
+
+    @pl.when(inner)
+    def _():
+        query_ref[...] = inner_ref[...]
+
+    @pl.when(jnp.logical_not(inner))
+    def _():
+        query_ref[...] = outer_ref[...]
+
+    row_max = attend(pieces, panel_mask, lists_ref, counts_ref, query_ref, score_ref, total_ref, mass_ref)
+    max_ref[...] = jnp.broadcast_to(row_max, max_ref.shape)
+
+
+def late_kernel(layout, panel_mask, lists_ref, counts_ref, query_ref, *refs):
+    before, refs = refs[:3], refs[3:]
     pieces, refs = read_pieces(layout, query_ref.shape[1], refs)
     packed_ref, score_ref, total_ref, mass_ref = refs
-    row_max = attend(pieces, panel_mask, lists_ref, counts_ref, query_ref, score_ref, total_ref, mass_ref)
+    row_max = attend(pieces, panel_mask, lists_ref, counts_ref, query_ref, score_ref, total_ref, mass_ref, before)
     row_sum = jnp.sum(mass_ref[...], axis=1, keepdims=True)
     value_width = total_ref.shape[1]
-    divisor = jnp.where(row_sum > 0.0, row_sum, 1.0)
-    packed_ref[0:TILE, :] = (total_ref[...] / divisor).astype(jnp.bfloat16)
+    inverse = 1.0 / jnp.where(row_sum > 0.0, row_sum, 1.0)
+    packed_ref[0:TILE, :] = (total_ref[...] * inverse).astype(jnp.bfloat16)
     row = lax.broadcasted_iota(jnp.int32, (EXTRA, LANES), 0)
     packed = jnp.zeros((EXTRA, LANES), jnp.float32)
     for first, column in ((0, row_max), (3, row_sum)):
@@ -197,7 +243,7 @@
         out_ref[:, at : at + LANES] = merged.astype(jnp.bfloat16)
 
 
-def gather_library(keys, values):
+def gather_library(keys, values, first_arrivals):
     steps = [("qry", 1)]
     mask = lax.axis_size("lib") // 2
     while mask > 1:
@@ -209,14 +255,21 @@
         near = (place, swap(keys, axis, mask), swap(values, axis, mask))
         relayed = []
         for (lib_mask, qry_mask), far_keys, far_values in early[1:] + late:
-            far_keys, _ = tie(far_keys, near[1])
-            far_values, _ = tie(far_values, near[2])
+            far_keys, far_values, *_ = tie(far_keys, far_values, near[1], near[2], *first_arrivals)
             place = (lib_mask | mask, qry_mask)
             relayed.append((place, swap(far_keys, axis, mask), swap(far_values, axis, mask)))
         early, late = early + late + [near], relayed
     return early, late
 
 
+def both_cores(pieces):
+    layout, arrays = [], []
+    for (lib_mask, qry_mask), *pair in pieces:
+        layout += [("pair", (lib_mask, qry_mask)), ("pair", (lib_mask | 1, qry_mask))]
+        arrays += pair + [swap(array, "lib", 1) for array in pair]
+    return layout, arrays
+
+
 def body(queries, library_keys, library_values, key_scale, block_list, block_count):
     qry_count = lax.axis_size("qry")
     width = library_keys.shape[1]
@@ -225,66 +278,68 @@
     values = pl.pallas_call(
         pack_kernel,
         out_shape=jax.ShapeDtypeStruct((TILE + EXTRA, value_width), jnp.bfloat16),
-        in_specs=[VMEM, VMEM],
+        in_specs=[pl.BlockSpec(memory_space=pl.ANY)] * 2,
         out_specs=VMEM,
+        scratch_shapes=[pltpu.VMEM((1, TILE), jnp.bfloat16), pltpu.SemaphoreType.DMA((2,))],
         compiler_params=params(),
     )(library_values, key_scale.reshape(1, TILE))
 
-    early, late = gather_library(library_keys, values)
+    masks = [2 * at + 1 for at in range(1, qry_count // 2)]
+    inner = [swap_some(queries, "qry", mask, True) for mask in masks]
+    early, late = gather_library(library_keys, values, inner)
     piece_rows = (width // value_width + 1) * TILE + EXTRA
-    early_arrays = [array for piece in early for array in piece[1:]]
-    bundle = pl.pallas_call(
-        bundle_kernel,
-        out_shape=jax.ShapeDtypeStruct((len(early) * piece_rows, value_width), jnp.bfloat16),
-        in_specs=[VMEM] * len(early_arrays),
-        out_specs=VMEM,
-        compiler_params=params(2 * len(early) * piece_rows * value_width * 2),
-    )(*early_arrays)
-    bundle, *_ = tie(bundle, *(piece[1] for piece in late))
-    bundle = swap(bundle, "lib", 1)
-    layout = [("pair", piece[0]) for piece in early]
-    layout.append(("bundle", [(lib_mask | 1, qry_mask) for (lib_mask, qry_mask), *_ in early]))
-    arrays = early_arrays + [bundle]
-    for (lib_mask, qry_mask), *pair in late:
-        layout += [("pair", (lib_mask, qry_mask)), ("pair", (lib_mask | 1, qry_mask))]
-        arrays += pair + [swap(array, "lib", 1) for array in pair]
-
-    count = 2 * (len(early) + len(late))
+    (early_layout, early_arrays), (late_layout, late_arrays) = both_cores(early), both_cores(late)
+    count_early, count_late = 2 * len(early), 2 * len(late)
+
     cost = pl.CostEstimate(flops=2 * TILE * 4 * TILE * width * 2, bytes_accessed=4 * 1024 * 1024, transcendentals=0)
-    scratch = [
-        pltpu.VMEM((count, TILE, TILE), jnp.float32),
-        pltpu.VMEM((TILE, value_width), jnp.float32),
-        pltpu.VMEM((TILE, TILE), jnp.float32),
-    ]
-    attend_params = params(count * piece_rows * value_width * 2)
-    in_specs = [SMEM, SMEM] + [VMEM] * (1 + len(arrays))
+    total_shape = jax.ShapeDtypeStruct((TILE, value_width), jnp.float32)
+    line_shape = jax.ShapeDtypeStruct((TILE, LANES), jnp.float32)
+    attend_params = params((count_early + count_late) * piece_rows * value_width * 2)
     returned = []
-    for at in range(1, qry_count // 2):
-        visitors, *_ = tie(queries, early[1][1], early[1][2])
-        visitors = swap(visitors, "qry", 2 * at + 1)
-        packed = pl.pallas_call(
-            functools.partial(visit_kernel, layout, 2 * at + 1),
-            out_shape=jax.ShapeDtypeStruct((TILE + EXTRA, value_width), jnp.bfloat16),
-            in_specs=in_specs,
-            out_specs=VMEM,
-            scratch_shapes=scratch,
+    for mask, inner_queries in zip(masks, inner):
+        waiting, *_ = tie(queries, early[1][1], early[1][2])
+        *state, = pl.pallas_call(
+            functools.partial(early_kernel, early_layout, mask),
+            out_shape=(jax.ShapeDtypeStruct(queries.shape, queries.dtype), total_shape, line_shape, line_shape),
+            in_specs=[SMEM, SMEM] + [VMEM] * (2 + len(early_arrays)),
+            out_specs=(VMEM,) * 4,
+            scratch_shapes=[pltpu.VMEM((count_early, TILE, TILE), jnp.float32)],
             compiler_params=attend_params,
             cost_estimate=cost,
-        )(block_list, block_count, visitors, *arrays)
-        returned.append(swap(packed, "qry", 2 * at + 1))
+        )(
+            block_list,
+            block_count,
+            inner_queries,
+            swap_some(waiting, "qry", mask, False),
+            *early_arrays,
+        )
+        packed = pl.pallas_call(
+            functools.partial(late_kernel, late_layout, mask),
+            out_shape=jax.ShapeDtypeStruct((TILE + EXTRA, value_width), jnp.bfloat16),
+            in_specs=[SMEM, SMEM] + [VMEM] * (4 + len(late_arrays)),
+            out_specs=VMEM,
+            scratch_shapes=[
+                pltpu.VMEM((count_late, TILE, TILE), jnp.float32),
+                pltpu.VMEM((TILE, value_width), jnp.float32),
+                pltpu.VMEM((TILE, TILE), jnp.float32),
+            ],
+            compiler_params=attend_params,
+            cost_estimate=cost,
+        )(block_list, block_count, *state, *late_arrays)
+        returned.append(swap(packed, "qry", mask))
 
     total, stats = pl.pallas_call(
-        functools.partial(home_kernel, layout),
-        out_shape=(
-            jax.ShapeDtypeStruct((TILE, value_width), jnp.float32),
-            jax.ShapeDtypeStruct((2, TILE, LANES), jnp.float32),
-        ),
-        in_specs=in_specs,
+        functools.partial(home_kernel, early_layout + late_layout),
+        out_shape=(total_shape, jax.ShapeDtypeStruct((2, TILE, LANES), jnp.float32)),
+        in_specs=[SMEM, SMEM] + [VMEM] * (1 + len(early_arrays) + len(late_arrays)),
         out_specs=(VMEM, VMEM),
-        scratch_shapes=[scratch[0], scratch[2]],
+        scratch_shapes=[
+            pltpu.VMEM((count_early + count_late, TILE, TILE), jnp.float32),
+            pltpu.VMEM((TILE, TILE), jnp.float32),
+        ],
         compiler_params=attend_params,
         cost_estimate=cost,
-    )(block_list, block_count, queries, *arrays)
+    )(block_list, block_count, queries, *early_arrays, *late_arrays)
 
     return pl.pallas_call(
         merge_kernel,

time: 46.1 us -> 43 us (0.933)
  the two profiles are of different devices: /device:TPU:20 before, /device:TPU:0 now
where the time goes in v3:
time: 43 us; the launch traced here: 43.1 us
  waiting for transfers between devices  19.6 us (46%)
  starting transfers between devices  16.6 us (39%)
  Pallas kernels  5.03 us (12%)
  local copies, waits for them, and re-layouts  1.65 us (4%)
    ppermute x15, waiting for transfers between devices, swap(): return lax.ppermute(value, axis, [(i, i ^ mask) for i in range(length)])  14.1 us
    ppermute x15, starting transfers between devices, swap(): return lax.ppermute(value, axis, [(i, i ^ mask) for i in range(length)])  13.1 us
    ppermute x2, waiting for transfers between devices, swap_some(): return lax.ppermute(value, axis, pairs)  5.52 us
    ppermute x2, starting transfers between devices, swap_some(): return lax.ppermute(value, axis, pairs)  3.48 us
    unnamed x13, local copies, waits for them, and re-layouts  1.65 us
    pallas_call x1, Pallas kernels, body(): pl.pallas_call(functools.partial(early_kernel, early_layout, mask), out_s...  1.61 us
    pallas_call x1, Pallas kernels, body(): pl.pallas_call(functools.partial(late_kernel, late_layout, mask), out_sha...  1.49 us
    pallas_call x1, Pallas kernels, body(): pl.pallas_call(functools.partial(home_kernel, early_layout + late_layout)...  0.95 us
  transfers between devices with their start and end apart: 17, of which 7 were waited for; matrix products, arithmetic and copies ran while one was open for 0% of the time, Pallas kernels for 6%

profile of v3, /device:TPU:0, one launch (start us, length us, event | category | flops | bytes accessed | tf_op | source)
XLA Modules:
  0.0 43.1 jit_solution(10502200693138818182)
XLA Ops:
  0.0 3.0 %collective-permute-start.2 = (bf16[128,1024]{1,0:T(8,128)(2,1)}, bf16[128,1024]{1,0:T(8,128)(2,1)S(1)}, u32[]{:S(2)}, u32[]{:S(2)}) collective-permute-start(bf16[128,1024]{1,0:T(8,128)(2,1)} %refs_0_.3), channel_id=1, source_target_pairs={{0,1},{1,0},{2,3},{3,2},{4,5},{5,4},{6,7},{7,6},{8,9},{9,8},{10,11... | collective-permute-start | bytes 786440 | tf_op jit(solution)/shard_map/ppermute | solution.py:25
  3.0 1.5 %collective-permute-start.6 = (bf16[128,1024]{1,0:T(8,128)(2,1)}, bf16[128,1024]{1,0:T(8,128)(2,1)S(1)}, u32[]{:S(2)}, u32[]{:S(2)}) collective-permute-start(bf16[128,1024]{1,0:T(8,128)(2,1)} %refs_0_.3), channel_id=1, source_target_pairs={{0,8},{4,12},{8,0},{12,4},{1,9},{5,13},{9,1},{13,5},{2,10},{6,14},... | collective-permute-start | bytes 786440 | tf_op jit(solution)/shard_map/ppermute | solution.py:25
  4.5 0.7 %collective-permute-start.10 = (bf16[128,1024]{1,0:T(8,128)(2,1)}, bf16[128,1024]{1,0:T(8,128)(2,1)S(1)}, u32[]{:S(2)}, u32[]{:S(2)}) collective-permute-start(bf16[128,1024]{1,0:T(8,128)(2,1)} %query_ref.1), channel_id=1, source_target_pairs={{1,2},{2,1},{5,6},{6,5},{9,10},{10,9},{13,14},{14,13},{17,18},{18,... | collective-permute-start | bytes 786440 | tf_op jit(solution)/shard_map/ppermute | solution.py:31
  5.2 0.9 %copy-done.2 = bf16[128,512]{1,0:T(8,128)(2,1)S(1)} copy-done((bf16[128,512]{1,0:T(8,128)(2,1)S(1)}, bf16[128,512]{1,0:T(8,128)(2,1)}, u32[]{:S(2)}) %copy-start.2) | copy-done | bytes 131096
  6.1 0.7 %copy-done.4 = bf16[128]{0:T(256)(128)(2,1)S(1)} copy-done((bf16[128]{0:T(256)(128)(2,1)S(1)}, bf16[128]{0:T(256)(128)(2,1)}, u32[]{:S(2)}) %copy-start.4) | copy-done | bytes 280
  6.8 0.2 shard_map.64.refs_1_
  6.9 0.0 copy-start.3
  6.9 4.5 %collective-permute-start.3 = (bf16[144,512]{1,0:T(8,128)(2,1)S(1)}, bf16[144,512]{1,0:T(8,128)(2,1)S(1)}, u32[]{:S(2)}, u32[]{:S(2)}) collective-permute-start(bf16[144,512]{1,0:T(8,128)(2,1)S(1)} %shard_map.64.refs_1_), channel_id=1, source_target_pairs={{0,1},{1,0},{2,3},{3,2},{4,5},{5,4},{6,7},{7,6},{8,9},{9,8},{10,11... | collective-permute-start | bytes 442376 | tf_op jit(solution)/shard_map/ppermute | solution.py:25
  11.4 0.5 %collective-permute-start.7 = (bf16[144,512]{1,0:T(8,128)(2,1)S(1)}, bf16[144,512]{1,0:T(8,128)(2,1)S(1)}, u32[]{:S(2)}, u32[]{:S(2)}) collective-permute-start(bf16[144,512]{1,0:T(8,128)(2,1)S(1)} %shard_map.64.refs_1_), channel_id=1, source_target_pairs={{0,8},{4,12},{8,0},{12,4},{1,9},{5,13},{9,1},{13,5},{2,10},{6,14},... | collective-permute-start | bytes 442376 | tf_op jit(solution)/shard_map/ppermute | solution.py:25
  11.9 2.6 %collective-permute-done.3.refs_5_ = bf16[144,512]{1,0:T(8,128)(2,1)S(1)} collective-permute-done((bf16[144,512]{1,0:T(8,128)(2,1)S(1)}, bf16[144,512]{1,0:T(8,128)(2,1)S(1)}, u32[]{:S(2)}, u32[]{:S(2)}) %collective-permute-start.3) | collective-permute-done | bytes 147488 | tf_op jit(solution)/shard_map/ppermute | solution.py:25
  14.5 0.0 collective-permute-start
  14.5 2.0 %collective-permute-done.7.refs_9_ = bf16[144,512]{1,0:T(8,128)(2,1)S(1)} collective-permute-done((bf16[144,512]{1,0:T(8,128)(2,1)S(1)}, bf16[144,512]{1,0:T(8,128)(2,1)S(1)}, u32[]{:S(2)}, u32[]{:S(2)}) %collective-permute-start.7) | collective-permute-done | bytes 147488 | tf_op jit(solution)/shard_map/ppermute | solution.py:25
  16.5 0.0 collective-permute-done.2.refs_4_
  16.5 0.0 collective-permute-done.6.refs_8_
  16.6 0.6 %collective-permute-start.11 = (bf16[128,1024]{1,0:T(8,128)(2,1)S(1)}, bf16[128,1024]{1,0:T(8,128)(2,1)S(1)}, u32[]{:S(2)}, u32[]{:S(2)}) collective-permute-start(bf16[128,1024]{1,0:T(8,128)(2,1)S(1)} %collective-permute-done.2.refs_4_), channel_id=1, source_target_pairs={{0,8},{4,12},{8,0},{12,4},{1,9},{5,13},{9,1},{13,5},{2,10},{6,14},... | collective-permute-start | bytes 786440 | tf_op jit(solution)/shard_map/ppermute | solution.py:25
  17.2 0.5 %collective-permute-start.5 = (bf16[144,512]{1,0:T(8,128)(2,1)S(1)}, bf16[144,512]{1,0:T(8,128)(2,1)S(1)}, u32[]{:S(2)}, u32[]{:S(2)}) collective-permute-start(bf16[144,512]{1,0:T(8,128)(2,1)S(1)} %collective-permute-done.3.refs_5_), channel_id=1, source_target_pairs={{0,4},{4,0},{8,12},{12,8},{1,5},{5,1},{9,13},{13,9},{2,6},{6,2},{1... | collective-permute-start | bytes 442376 | tf_op jit(solution)/shard_map/ppermute | solution.py:25
  17.7 0.9 %collective-permute-done.1.refs_3_ = bf16[144,512]{1,0:T(8,128)(2,1)S(1)} collective-permute-done((bf16[144,512]{1,0:T(8,128)(2,1)S(1)}, bf16[144,512]{1,0:T(8,128)(2,1)S(1)}, u32[]{:S(2)}, u32[]{:S(2)}) %collective-permute-start.1) | collective-permute-done | bytes 147488 | tf_op jit(solution)/shard_map/ppermute | solution.py:25
  18.5 1.5 %collective-permute-start.12 = (bf16[144,512]{1,0:T(8,128)(2,1)S(1)}, bf16[144,512]{1,0:T(8,128)(2,1)S(1)}, u32[]{:S(2)}, u32[]{:S(2)}) collective-permute-start(bf16[144,512]{1,0:T(8,128)(2,1)S(1)} %collective-permute-done.3.refs_5_), channel_id=1, source_target_pairs={{0,8},{4,12},{8,0},{12,4},{1,9},{5,13},{9,1},{13,5},{2,10},{6,14},... | collective-permute-start | bytes 442376 | tf_op jit(solution)/shard_map/ppermute | solution.py:25
  20.0 2.8 %collective-permute-start.15 = (bf16[128,1024]{1,0:T(8,128)(2,1)}, bf16[128,1024]{1,0:T(8,128)(2,1)}, u32[]{:S(2)}, u32[]{:S(2)}) collective-permute-start(bf16[128,1024]{1,0:T(8,128)(2,1)} %query_ref.1), channel_id=1, source_target_pairs={{0,3},{3,0},{4,7},{7,4},{8,11},{11,8},{12,15},{15,12},{16,19},{19,... | collective-permute-start | bytes 786440 | tf_op jit(solution)/shard_map/ppermute | solution.py:31
  22.8 0.1 collective-permute-start.4
  22.9 0.5 %collective-permute-start.8 = (bf16[128,1024]{1,0:T(8,128)(2,1)S(1)}, bf16[128,1024]{1,0:T(8,128)(2,1)S(1)}, u32[]{:S(2)}, u32[]{:S(2)}) collective-permute-start(bf16[128,1024]{1,0:T(8,128)(2,1)S(1)} %collective-permute-done.6.refs_8_), channel_id=1, source_target_pairs={{0,4},{4,0},{8,12},{12,8},{1,5},{5,1},{9,13},{13,9},{2,6},{6,2},{1... | collective-permute-start | bytes 786440 | tf_op jit(solution)/shard_map/ppermute | solution.py:25
  23.4 1.5 %collective-permute-done.11.refs_12_.refs_3_ = bf16[128,1024]{1,0:T(8,128)(2,1)S(1)} collective-permute-done((bf16[128,1024]{1,0:T(8,128)(2,1)S(1)}, bf16[128,1024]{1,0:T(8,128)(2,1)S(1)}, u32[]{:S(2)}, u32[]{:S(2)}) %collective-permute-start.11) | collective-permute-done | bytes 262176 | tf_op jit(solution)/shard_map/ppermute | solution.py:25
  24.9 1.6 %collective-permute-done.12.refs_13_.refs_4_ = bf16[144,512]{1,0:T(8,128)(2,1)S(1)} collective-permute-done((bf16[144,512]{1,0:T(8,128)(2,1)S(1)}, bf16[144,512]{1,0:T(8,128)(2,1)S(1)}, u32[]{:S(2)}, u32[]{:S(2)}) %collective-permute-start.12) | collective-permute-done | bytes 147488 | tf_op jit(solution)/shard_map/ppermute | solution.py:25
  26.5 0.1 copy.7.lists_ref
  26.6 5.5 %collective-permute-done.15.outer_ref = bf16[128,1024]{1,0:T(8,128)(2,1)} collective-permute-done((bf16[128,1024]{1,0:T(8,128)(2,1)}, bf16[128,1024]{1,0:T(8,128)(2,1)}, u32[]{:S(2)}, u32[]{:S(2)}) %collective-permute-start.15) | collective-permute-done | bytes 262176 | tf_op jit(solution)/shard_map/ppermute | solution.py:31
  32.1 1.6 %shard_map.66 = (bf16[128,1024]{1,0:T(8,128)(2,1)S(1)}, f32[128,512]{1,0:T(8,128)S(1)}, f32[128,128]{1,0:T(8,128)S(1)}, f32[128,128]{1,0:T(8,128)S(1)}) custom-call(s32[16,4]{1,0:T(8,128)S(1)} %copy.7.lists_ref, s32[16]{0:T(128)S(1)} %copy-done.3, bf16[128,1024]{1,0:T(8,128)(2,1)S(1)} %collective-permute-done.10.inner_ref, ...), custom_call_target="tpu_custom_call" | custom-call | flops 268435456 | bytes 4194304 | tf_op jit(solution)/shard_map/pallas_call | solution.py:301
  33.7 0.0 copy-start.1
  33.8 1.5 %shard_map.67 = bf16[144,512]{1,0:T(8,128)(2,1)S(1)} custom-call(s32[16,4]{1,0:T(8,128)S(1)} %copy.7.lists_ref, s32[16]{0:T(128)S(1)} %copy-done.3, bf16[128,1024]{1,0:T(8,128)(2,1)S(1)} %get-tuple-element.19.query_ref, f32[128,512]{1,0:T(8,128)S(1)} %get-tuple-element.20.refs_0_, f32[128,128]{1,0:T(8,128)S(1)} %get-tuple-element.21.refs_1_, ...), custom_call_target="tpu_custom_call" | custom-call | flops 268435456 | bytes 4194304 | tf_op jit(solution)/shard_map/pallas_call | solution.py:316
  35.3 0.5 %collective-permute-start.16 = (bf16[144,512]{1,0:T(8,128)(2,1)S(1)}, bf16[144,512]{1,0:T(8,128)(2,1)S(1)}, u32[]{:S(2)}, u32[]{:S(2)}) collective-permute-start(bf16[144,512]{1,0:T(8,128)(2,1)S(1)} %shard_map.67), channel_id=1, source_target_pairs={{0,3},{1,2},{2,1},{3,0},{4,7},{5,6},{6,5},{7,4},{8,11},{9,10},{10,... | collective-permute-start | bytes 442376 | tf_op jit(solution)/shard_map/ppermute | solution.py:25
  35.7 0.9 %shard_map.65 = (f32[128,512]{1,0:T(8,128)S(1)}, f32[2,128,128]{2,1,0:T(8,128)S(1)}) custom-call(s32[16,4]{1,0:T(8,128)S(1)} %copy.7.lists_ref, s32[16]{0:T(128)S(1)} %copy-done.3, bf16[128,1024]{1,0:T(8,128)(2,1)S(1)} %copy-done.1, bf16[128,1024]{1,0:T(8,128)(2,1)S(1)} %copy-done, bf16[144,512]{1,0:T(8,128)(2,1)S(1)} %shard_map.64.refs_1_, ...), custom_call_target="tpu_custom_call" | custom-call | flops 268435456 | bytes 4194304 | tf_op jit(solution)/shard_map/pallas_call | solution.py:331
  36.7 5.6 %collective-permute-done.16.refs_0_ = bf16[144,512]{1,0:T(8,128)(2,1)S(1)} collective-permute-done((bf16[144,512]{1,0:T(8,128)(2,1)S(1)}, bf16[144,512]{1,0:T(8,128)(2,1)S(1)}, u32[]{:S(2)}, u32[]{:S(2)}) %collective-permute-start.16) | collective-permute-done | bytes 147488 | tf_op jit(solution)/shard_map/ppermute | solution.py:25
  42.3 0.8 %shard_map.68 = bf16[128,512]{1,0:T(8,128)(2,1)} custom-call(f32[128,512]{1,0:T(8,128)S(1)} %get-tuple-element.16.total_ref, f32[2,128,128]{2,1,0:T(8,128)S(1)} %get-tuple-element.17.stats_ref, bf16[144,512]{1,0:T(8,128)(2,1)S(1)} %collective-permute-done.16.refs_0_), custom_call_target="tpu_custom_call" | custom-call | tf_op jit(solution)/shard_map/pallas_call | solution.py:344
  (20 shorter events, 0.0 us)
Async XLA Ops:
  0.0 14.5 %copy-start = (bf16[128,1024]{1,0:T(8,128)(2,1)S(1)}, bf16[128,1024]{1,0:T(8,128)(2,1)}, u32[]{:S(2)}) copy-start(bf16[128,1024]{1,0:T(8,128)(2,1)} %refs_0_.3) | copy-start | bytes 786436
  0.0 16.5 %collective-permute-start.2 = (bf16[128,1024]{1,0:T(8,128)(2,1)}, bf16[128,1024]{1,0:T(8,128)(2,1)S(1)}, u32[]{:S(2)}, u32[]{:S(2)}) collective-permute-start(bf16[128,1024]{1,0:T(8,128)(2,1)} %refs_0_.3), channel_id=1, source_target_pairs={{0,1},{1,0},{2,3},{3,2},{4,5},{5,4},{6,7},{7,6},{8,9},{9,8},{10,11... | collective-permute-start | bytes 786440 | tf_op jit(solution)/shard_map/ppermute | solution.py:25
  3.0 13.5 %collective-permute-start.6 = (bf16[128,1024]{1,0:T(8,128)(2,1)}, bf16[128,1024]{1,0:T(8,128)(2,1)S(1)}, u32[]{:S(2)}, u32[]{:S(2)}) collective-permute-start(bf16[128,1024]{1,0:T(8,128)(2,1)} %refs_0_.3), channel_id=1, source_target_pairs={{0,8},{4,12},{8,0},{12,4},{1,9},{5,13},{9,1},{13,5},{2,10},{6,14},... | collective-permute-start | bytes 786440 | tf_op jit(solution)/shard_map/ppermute | solution.py:25
  4.5 12.0 %collective-permute-start.10 = (bf16[128,1024]{1,0:T(8,128)(2,1)}, bf16[128,1024]{1,0:T(8,128)(2,1)S(1)}, u32[]{:S(2)}, u32[]{:S(2)}) collective-permute-start(bf16[128,1024]{1,0:T(8,128)(2,1)} %query_ref.1), channel_id=1, source_target_pairs={{1,2},{2,1},{5,6},{6,5},{9,10},{10,9},{13,14},{14,13},{17,18},{18,... | collective-permute-start | bytes 786440 | tf_op jit(solution)/shard_map/ppermute | solution.py:31
  5.2 0.9 %copy-start.2 = (bf16[128,512]{1,0:T(8,128)(2,1)S(1)}, bf16[128,512]{1,0:T(8,128)(2,1)}, u32[]{:S(2)}) copy-start(bf16[128,512]{1,0:T(8,128)(2,1)} %values_ref.1) | copy-start | bytes 393220
  6.1 0.7 %copy-start.4 = (bf16[128]{0:T(256)(128)(2,1)S(1)}, bf16[128]{0:T(256)(128)(2,1)}, u32[]{:S(2)}) copy-start(bf16[128]{0:T(256)(128)(2,1)} %param.9) | copy-start | bytes 772
  6.8 19.7 %copy-start.5 = (s32[16,4]{0,1:T(4,128)S(1)}, s32[16,4]{0,1:T(4,128)}, u32[]{:S(2)}) copy-start(s32[16,4]{0,1:T(4,128)} %param.10) | copy-start | bytes 772
  6.9 25.2 %copy-start.3 = (s32[16]{0:T(128)S(1)}, s32[16]{0:T(128)}, u32[]{:S(2)}) copy-start(s32[16]{0:T(128)} %counts_ref.5) | copy-start | bytes 196
  6.9 7.6 %collective-permute-start.3 = (bf16[144,512]{1,0:T(8,128)(2,1)S(1)}, bf16[144,512]{1,0:T(8,128)(2,1)S(1)}, u32[]{:S(2)}, u32[]{:S(2)}) collective-permute-start(bf16[144,512]{1,0:T(8,128)(2,1)S(1)} %shard_map.64.refs_1_), channel_id=1, source_target_pairs={{0,1},{1,0},{2,3},{3,2},{4,5},{5,4},{6,7},{7,6},{8,9},{9,8},{10,11... | collective-permute-start | bytes 442376 | tf_op jit(solution)/shard_map/ppermute | solution.py:25
  11.4 5.1 %collective-permute-start.7 = (bf16[144,512]{1,0:T(8,128)(2,1)S(1)}, bf16[144,512]{1,0:T(8,128)(2,1)S(1)}, u32[]{:S(2)}, u32[]{:S(2)}) collective-permute-start(bf16[144,512]{1,0:T(8,128)(2,1)S(1)} %shard_map.64.refs_1_), channel_id=1, source_target_pairs={{0,8},{4,12},{8,0},{12,4},{1,9},{5,13},{9,1},{13,5},{2,10},{6,14},... | collective-permute-start | bytes 442376 | tf_op jit(solution)/shard_map/ppermute | solution.py:25
  14.5 5.5 %collective-permute-start = (bf16[128,1024]{1,0:T(8,128)(2,1)S(1)}, bf16[128,1024]{1,0:T(8,128)(2,1)S(1)}, u32[]{:S(2)}, u32[]{:S(2)}) collective-permute-start(bf16[128,1024]{1,0:T(8,128)(2,1)S(1)} %copy-done), channel_id=1, source_target_pairs={{0,4},{4,0},{8,12},{12,8},{1,5},{5,1},{9,13},{13,9},{2,6},{6,2},{1... | collective-permute-start | bytes 786440 | tf_op jit(solution)/shard_map/ppermute | solution.py:25
  16.6 8.4 %collective-permute-start.11 = (bf16[128,1024]{1,0:T(8,128)(2,1)S(1)}, bf16[128,1024]{1,0:T(8,128)(2,1)S(1)}, u32[]{:S(2)}, u32[]{:S(2)}) collective-permute-start(bf16[128,1024]{1,0:T(8,128)(2,1)S(1)} %collective-permute-done.2.refs_4_), channel_id=1, source_target_pairs={{0,8},{4,12},{8,0},{12,4},{1,9},{5,13},{9,1},{13,5},{2,10},{6,14},... | collective-permute-start | bytes 786440 | tf_op jit(solution)/shard_map/ppermute | solution.py:25
  17.2 1.4 %collective-permute-start.1 = (bf16[144,512]{1,0:T(8,128)(2,1)S(1)}, bf16[144,512]{1,0:T(8,128)(2,1)S(1)}, u32[]{:S(2)}, u32[]{:S(2)}) collective-permute-start(bf16[144,512]{1,0:T(8,128)(2,1)S(1)} %shard_map.64.refs_1_), channel_id=1, source_target_pairs={{0,4},{4,0},{8,12},{12,8},{1,5},{5,1},{9,13},{13,9},{2,6},{6,2},{1... | collective-permute-start | bytes 442376 | tf_op jit(solution)/shard_map/ppermute | solution.py:25
  17.2 5.7 %collective-permute-start.5 = (bf16[144,512]{1,0:T(8,128)(2,1)S(1)}, bf16[144,512]{1,0:T(8,128)(2,1)S(1)}, u32[]{:S(2)}, u32[]{:S(2)}) collective-permute-start(bf16[144,512]{1,0:T(8,128)(2,1)S(1)} %collective-permute-done.3.refs_5_), channel_id=1, source_target_pairs={{0,4},{4,0},{8,12},{12,8},{1,5},{5,1},{9,13},{13,9},{2,6},{6,2},{1... | collective-permute-start | bytes 442376 | tf_op jit(solution)/shard_map/ppermute | solution.py:25
  17.7 5.3 %collective-permute-start.9 = (bf16[144,512]{1,0:T(8,128)(2,1)S(1)}, bf16[144,512]{1,0:T(8,128)(2,1)S(1)}, u32[]{:S(2)}, u32[]{:S(2)}) collective-permute-start(bf16[144,512]{1,0:T(8,128)(2,1)S(1)} %collective-permute-done.7.refs_9_), channel_id=1, source_target_pairs={{0,4},{4,0},{8,12},{12,8},{1,5},{5,1},{9,13},{13,9},{2,6},{6,2},{1... | collective-permute-start | bytes 442376 | tf_op jit(solution)/shard_map/ppermute | solution.py:25
  18.5 8.0 %collective-permute-start.12 = (bf16[144,512]{1,0:T(8,128)(2,1)S(1)}, bf16[144,512]{1,0:T(8,128)(2,1)S(1)}, u32[]{:S(2)}, u32[]{:S(2)}) collective-permute-start(bf16[144,512]{1,0:T(8,128)(2,1)S(1)} %collective-permute-done.3.refs_5_), channel_id=1, source_target_pairs={{0,8},{4,12},{8,0},{12,4},{1,9},{5,13},{9,1},{13,5},{2,10},{6,14},... | collective-permute-start | bytes 442376 | tf_op jit(solution)/shard_map/ppermute | solution.py:25
  20.0 12.1 %collective-permute-start.15 = (bf16[128,1024]{1,0:T(8,128)(2,1)}, bf16[128,1024]{1,0:T(8,128)(2,1)}, u32[]{:S(2)}, u32[]{:S(2)}) collective-permute-start(bf16[128,1024]{1,0:T(8,128)(2,1)} %query_ref.1), channel_id=1, source_target_pairs={{0,3},{3,0},{4,7},{7,4},{8,11},{11,8},{12,15},{15,12},{16,19},{19,... | collective-permute-start | bytes 786440 | tf_op jit(solution)/shard_map/ppermute | solution.py:31
  22.8 9.3 %collective-permute-start.4 = (bf16[128,1024]{1,0:T(8,128)(2,1)S(1)}, bf16[128,1024]{1,0:T(8,128)(2,1)S(1)}, u32[]{:S(2)}, u32[]{:S(2)}) collective-permute-start(bf16[128,1024]{1,0:T(8,128)(2,1)S(1)} %collective-permute-done.2.refs_4_), channel_id=1, source_target_pairs={{0,4},{4,0},{8,12},{12,8},{1,5},{5,1},{9,13},{13,9},{2,6},{6,2},{1... | collective-permute-start | bytes 786440 | tf_op jit(solution)/shard_map/ppermute | solution.py:25
  22.9 9.2 %collective-permute-start.8 = (bf16[128,1024]{1,0:T(8,128)(2,1)S(1)}, bf16[128,1024]{1,0:T(8,128)(2,1)S(1)}, u32[]{:S(2)}, u32[]{:S(2)}) collective-permute-start(bf16[128,1024]{1,0:T(8,128)(2,1)S(1)} %collective-permute-done.6.refs_8_), channel_id=1, source_target_pairs={{0,4},{4,0},{8,12},{12,8},{1,5},{5,1},{9,13},{13,9},{2,6},{6,2},{1... | collective-permute-start | bytes 786440 | tf_op jit(solution)/shard_map/ppermute | solution.py:25
  24.9 8.8 %collective-permute-start.13 = (bf16[128,1024]{1,0:T(8,128)(2,1)S(1)}, bf16[128,1024]{1,0:T(8,128)(2,1)S(1)}, u32[]{:S(2)}, u32[]{:S(2)}) collective-permute-start(bf16[128,1024]{1,0:T(8,128)(2,1)S(1)} %collective-permute-done.11.refs_12_.refs_3_), channel_id=1, source_target_pairs={{0,4},{4,0},{8,12},{12,8},{1,5},{5,1},{9,13},{13,9},{2,6},{6,2},{1... | collective-permute-start | bytes 786440 | tf_op jit(solution)/shard_map/ppermute | solution.py:25
  26.5 7.2 %collective-permute-start.14 = (bf16[144,512]{1,0:T(8,128)(2,1)S(1)}, bf16[144,512]{1,0:T(8,128)(2,1)S(1)}, u32[]{:S(2)}, u32[]{:S(2)}) collective-permute-start(bf16[144,512]{1,0:T(8,128)(2,1)S(1)} %collective-permute-done.12.refs_13_.refs_4_), channel_id=1, source_target_pairs={{0,4},{4,0},{8,12},{12,8},{1,5},{5,1},{9,13},{13,9},{2,6},{6,2},{1... | collective-permute-start | bytes 442376 | tf_op jit(solution)/shard_map/ppermute | solution.py:25
  33.7 2.0 %copy-start.1 = (bf16[128,1024]{1,0:T(8,128)(2,1)S(1)}, bf16[128,1024]{1,0:T(8,128)(2,1)}, u32[]{:S(2)}) copy-start(bf16[128,1024]{1,0:T(8,128)(2,1)} %query_ref.1) | copy-start | bytes 786436
  35.3 7.0 %collective-permute-start.16 = (bf16[144,512]{1,0:T(8,128)(2,1)S(1)}, bf16[144,512]{1,0:T(8,128)(2,1)S(1)}, u32[]{:S(2)}, u32[]{:S(2)}) collective-permute-start(bf16[144,512]{1,0:T(8,128)(2,1)S(1)} %shard_map.67), channel_id=1, source_target_pairs={{0,3},{1,2},{2,1},{3,0},{4,7},{5,6},{6,5},{7,4},{8,11},{9,10},{10,... | collective-permute-start | bytes 442376 | tf_op jit(solution)/shard_map/ppermute | solution.py:25

commit v4 on v3

--- a/solution.py
+++ b/solution.py
@@ -43,78 +43,51 @@
     return high, middle, low
 
 
-def pack_kernel(values_ref, scale_ref, packed_ref, row_ref, sems):
-    value_width = values_ref.shape[1]
-    copies = (
-        pltpu.make_async_copy(values_ref, packed_ref.at[pl.ds(0, TILE)], sems.at[0]),
-        pltpu.make_async_copy(scale_ref, row_ref, sems.at[1]),
-    )
+def pack_kernel(keys_ref, values_ref, scale_ref, packed_ref, row_ref, last_ref, sems):
+    width = packed_ref.shape[1]
+    groups = keys_ref.shape[1] // width
+    row_copy = pltpu.make_async_copy(scale_ref, row_ref, sems.at[0])
+    row_copy.start()
+    copies = []
+    for at in range(groups):
+        columns = keys_ref.at[:, pl.ds(at * width, width)]
+        copies.append(pltpu.make_async_copy(columns, packed_ref.at[pl.ds(at * TILE, TILE)], sems.at[1 + at]))
+    copies.append(pltpu.make_async_copy(values_ref, packed_ref.at[pl.ds(groups * TILE, TILE)], sems.at[1 + groups]))
     for copy in copies:
         copy.start()
-    packed_ref[TILE:, TILE:] = jnp.zeros((EXTRA, value_width - TILE), jnp.bfloat16)
-    for copy in reversed(copies):
+    last_ref[:, TILE:] = jnp.zeros((EXTRA, width - TILE), jnp.bfloat16)
+    row_copy.wait()
+    row = row_ref[...].astype(jnp.float32)
+    last_ref[:, 0:TILE] = jnp.broadcast_to(row, (EXTRA, TILE)).astype(jnp.bfloat16)
+    last_rows = packed_ref.at[pl.ds((groups + 1) * TILE, EXTRA)]
+    last_copy = pltpu.make_async_copy(last_ref, last_rows, sems.at[2 + groups])
+    last_copy.start()
+    for copy in copies + [last_copy]:
         copy.wait()
-    row = row_ref[...].astype(jnp.float32)
-    packed_ref[TILE:, 0:TILE] = jnp.broadcast_to(row, (EXTRA, TILE)).astype(jnp.bfloat16)
-
-
-def bundle_kernel(*refs):
-    bundle_ref, at = refs[-1], 0
-    width = bundle_ref.shape[1]
-    for ref in refs[:-1]:
-        rows = ref.shape[0]
-        for column in range(0, ref.shape[1], width):
-            bundle_ref[at : at + rows, :] = ref[:, column : column + width]
-            at += rows
 
 
 class Piece:
-    def __init__(self, place, keys_ref=None, values_ref=None, bundle_ref=None, first_row=0):
+    def __init__(self, place, ref):
         self.place = place
-        self.refs = (keys_ref, values_ref, bundle_ref)
-        self.first_row = first_row
+        self.ref = ref
 
     def scores(self, query_ref, inverse_root):
-        keys_ref, values_ref, bundle_ref = self.refs
-        width = query_ref.shape[1]
-        dims = (((1,), (1,)), ((), ()))
-        if bundle_ref is None:
-            product = lax.dot_general(query_ref[...], keys_ref[...], dims, preferred_element_type=jnp.float32)
-            scale = values_ref[TILE : TILE + EXTRA, 0:TILE]
-        else:
-            group = bundle_ref.shape[1]
-            product = 0.0
-            for at in range(width // group):
-                rows = pl.ds(self.first_row + at * TILE, TILE)
-                product = product + lax.dot_general(
-                    query_ref[:, at * group : (at + 1) * group],
-                    bundle_ref[rows, :],
-                    dims,
-                    preferred_element_type=jnp.float32,
-                )
-            scale = bundle_ref[pl.ds(self.first_row + width // group * TILE + TILE, EXTRA), 0:TILE]
-        return product * (scale.astype(jnp.float32)[0:1] * inverse_root)
+        group = self.ref.shape[1]
+        groups = query_ref.shape[1] // group
+        product = 0.0
+        for at in range(groups):
+            product = product + lax.dot_general(
+                query_ref[:, at * group : (at + 1) * group],
+                self.ref[at * TILE : (at + 1) * TILE, :],
+                (((1,), (1,)), ((), ())),
+                preferred_element_type=jnp.float32,
+            )
+        scale = self.ref[(groups + 1) * TILE :, 0:TILE].astype(jnp.float32)[0:1]
+        return product * (scale * inverse_root)
 
     def values(self, width):
-        keys_ref, values_ref, bundle_ref = self.refs
-        if bundle_ref is None:
-            return values_ref[0:TILE, :]
-        return bundle_ref[pl.ds(self.first_row + width // bundle_ref.shape[1] * TILE, TILE), :]
-
-
-def read_pieces(layout, width, refs):
-    pieces = []
-    for entry in layout:
-        if entry[0] == "pair":
-            pieces.append(Piece(entry[1], refs[0], refs[1]))
-            refs = refs[2:]
-        else:
-            for at, place in enumerate(entry[1]):
-                group = refs[0].shape[1]
-                rows = (width // group + 1) * TILE + EXTRA
-                pieces.append(Piece(place, bundle_ref=refs[0], first_row=at * rows))
-            refs = refs[1:]
-    return pieces, refs
+        first = width // self.ref.shape[1] * TILE
+        return self.ref[first : first + TILE, :]
 
 
 def attend(pieces, panel_mask, lists_ref, counts_ref, query_ref, score_ref, total_ref, mass_ref, before=None):
@@ -177,8 +150,13 @@
     return jnp.abs(index - lax.bitwise_xor(index, mask)) * 2 <= mask
 
 
-def early_kernel(layout, panel_mask, lists_ref, counts_ref, inner_ref, outer_ref, *refs):
-    pieces, refs = read_pieces(layout, inner_ref.shape[1], refs)
+def read_pieces(places, refs):
+    count = len(places)
+    return [Piece(place, ref) for place, ref in zip(places, refs)], refs[count:]
+
+
+def early_kernel(places, panel_mask, lists_ref, counts_ref, inner_ref, outer_ref, *refs):
+    pieces, refs = read_pieces(places, refs)
     query_ref, total_ref, mass_ref, max_ref, score_ref = refs
     inner = is_inner(panel_mask)
 
@@ -194,9 +172,9 @@
     max_ref[...] = jnp.broadcast_to(row_max, max_ref.shape)
 
 
-def late_kernel(layout, panel_mask, lists_ref, counts_ref, query_ref, *refs):
+def late_kernel(places, panel_mask, lists_ref, counts_ref, query_ref, *refs):
     before, refs = refs[:3], refs[3:]
-    pieces, refs = read_pieces(layout, query_ref.shape[1], refs)
+    pieces, refs = read_pieces(places, refs)
     packed_ref, score_ref, total_ref, mass_ref = refs
     row_max = attend(pieces, panel_mask, lists_ref, counts_ref, query_ref, score_ref, total_ref, mass_ref, before)
     row_sum = jnp.sum(mass_ref[...], axis=1, keepdims=True)
@@ -213,8 +191,8 @@
     packed_ref[TILE:, LANES:] = jnp.zeros((EXTRA, value_width - LANES), jnp.bfloat16)
 
 
-def home_kernel(layout, lists_ref, counts_ref, query_ref, *refs):
-    pieces, refs = read_pieces(layout, query_ref.shape[1], refs)
+def home_kernel(places, lists_ref, counts_ref, query_ref, *refs):
+    pieces, refs = read_pieces(places, refs)
     total_ref, stats_ref, score_ref, mass_ref = refs
     row_max = attend(pieces, 0, lists_ref, counts_ref, query_ref, score_ref, total_ref, mass_ref)
     row_sum = jnp.sum(mass_ref[...], axis=1, keepdims=True)
@@ -243,63 +221,73 @@
         out_ref[:, at : at + LANES] = merged.astype(jnp.bfloat16)
 
 
-def gather_library(keys, values, first_arrivals):
+def gather_library(block, queries, masks):
     steps = [("qry", 1)]
     mask = lax.axis_size("lib") // 2
     while mask > 1:
         steps.append(("lib", mask))
         mask //= 2
-    early, late = [((0, 0), keys, values)], []
+    own_places, own_arrays = both_cores([((0, 0), block)])
+    nearer, _ = tie(queries, own_arrays[1])
+    inner = [swap_some(nearer, "qry", mask, True) for mask in masks]
+    early, late = [], []
     for axis, mask in steps:
         place = (0, mask) if axis == "qry" else (mask, 0)
-        near = (place, swap(keys, axis, mask), swap(values, axis, mask))
+        near = (place, swap(block, axis, mask))
         relayed = []
-        for (lib_mask, qry_mask), far_keys, far_values in early[1:] + late:
-            far_keys, far_values, *_ = tie(far_keys, far_values, near[1], near[2], *first_arrivals)
-            place = (lib_mask | mask, qry_mask)
-            relayed.append((place, swap(far_keys, axis, mask), swap(far_values, axis, mask)))
+        for (lib_mask, qry_mask), far in early + late:
+            far, *_ = tie(far, near[1], *inner)
+            relayed.append(((lib_mask | mask, qry_mask), swap(far, axis, mask)))
         early, late = early + late + [near], relayed
-    return early, late
-
-
-def both_cores(pieces):
-    layout, arrays = [], []
-    for (lib_mask, qry_mask), *pair in pieces:
-        layout += [("pair", (lib_mask, qry_mask)), ("pair", (lib_mask | 1, qry_mask))]
-        arrays += pair + [swap(array, "lib", 1) for array in pair]
-    return layout, arrays
+    farther, _ = tie(queries, early[0][1])
+    outer = [swap_some(farther, "qry", mask, False) for mask in masks]
+    early_places, early_arrays = both_cores(early)
+    late_places, late_arrays = both_cores(late, outer)
+    early = (own_places + early_places, own_arrays + early_arrays)
+    return early, (late_places, late_arrays), list(zip(masks, inner, outer))
+
+
+def both_cores(pieces, arrivals=()):
+    places, arrays = [], []
+    for (lib_mask, qry_mask), block in pieces:
+        sent, *_ = tie(block, *arrivals)
+        places += [(lib_mask, qry_mask), (lib_mask | 1, qry_mask)]
+        arrays += [block, swap(sent, "lib", 1)]
+    return places, arrays
 
 
 def body(queries, library_keys, library_values, key_scale, block_list, block_count):
     qry_count = lax.axis_size("qry")
     width = library_keys.shape[1]
     value_width = library_values.shape[1]
-
-    values = pl.pallas_call(
+    piece_rows = (width // value_width + 1) * TILE + EXTRA
+    piece_bytes = piece_rows * value_width * 2
+
+    block = pl.pallas_call(
         pack_kernel,
-        out_shape=jax.ShapeDtypeStruct((TILE + EXTRA, value_width), jnp.bfloat16),
-        in_specs=[pl.BlockSpec(memory_space=pl.ANY)] * 2,
-        out_specs=VMEM,
-        scratch_shapes=[pltpu.VMEM((1, TILE), jnp.bfloat16), pltpu.SemaphoreType.DMA((2,))],
-        compiler_params=params(),
-    )(library_values, key_scale.reshape(1, TILE))
+        out_shape=jax.ShapeDtypeStruct((piece_rows, value_width), jnp.bfloat16),
+        in_specs=[pl.BlockSpec(memory_space=pl.ANY)] * 3,
+        out_specs=pl.BlockSpec(memory_space=pl.ANY),
+        scratch_shapes=[
+            pltpu.VMEM((1, TILE), jnp.bfloat16),
+            pltpu.VMEM((EXTRA, value_width), jnp.bfloat16),
+            pltpu.SemaphoreType.DMA((width // value_width + 3,)),
+        ],
+        compiler_params=pltpu.CompilerParams(vmem_limit_bytes=60 * 1024 * 1024),
+    )(library_keys, library_values, key_scale.reshape(1, TILE))
 
     masks = [2 * at + 1 for at in range(1, qry_count // 2)]
-    inner = [swap_some(queries, "qry", mask, True) for mask in masks]
-    early, late = gather_library(library_keys, values, inner)
-    piece_rows = (width // value_width + 1) * TILE + EXTRA
-    (early_layout, early_arrays), (late_layout, late_arrays) = both_cores(early), both_cores(late)
-    count_early, count_late = 2 * len(early), 2 * len(late)
+    (early_places, early_arrays), (late_places, late_arrays), visitors = gather_library(block, queries, masks)
+    count_early, count_late = len(early_places), len(late_places)
 
     cost = pl.CostEstimate(flops=2 * TILE * 4 * TILE * width * 2, bytes_accessed=4 * 1024 * 1024, transcendentals=0)
     total_shape = jax.ShapeDtypeStruct((TILE, value_width), jnp.float32)
     line_shape = jax.ShapeDtypeStruct((TILE, LANES), jnp.float32)
-    attend_params = params((count_early + count_late) * piece_rows * value_width * 2)
+    attend_params = params((count_early + count_late) * piece_bytes)
     returned = []
-    for mask, inner_queries in zip(masks, inner):
-        waiting, *_ = tie(queries, early[1][1], early[1][2])
+    for mask, inner_queries, outer_queries in visitors:
         *state, = pl.pallas_call(
-            functools.partial(early_kernel, early_layout, mask),
+            functools.partial(early_kernel, early_places, mask),
             out_shape=(jax.ShapeDtypeStruct(queries.shape, queries.dtype), total_shape, line_shape, line_shape),
             in_specs=[SMEM, SMEM] + [VMEM] * (2 + len(early_arrays)),
             out_specs=(VMEM,) * 4,
@@ -310,11 +298,11 @@
             block_list,
             block_count,
             inner_queries,
-            swap_some(waiting, "qry", mask, False),
+            outer_queries,
             *early_arrays,
         )
         packed = pl.pallas_call(
-            functools.partial(late_kernel, late_layout, mask),
+            functools.partial(late_kernel, late_places, mask),
             out_shape=jax.ShapeDtypeStruct((TILE + EXTRA, value_width), jnp.bfloat16),
             in_specs=[SMEM, SMEM] + [VMEM] * (4 + len(late_arrays)),
             out_specs=VMEM,
@@ -329,7 +317,7 @@
         returned.append(swap(packed, "qry", mask))
 
     total, stats = pl.pallas_call(
-        functools.partial(home_kernel, early_layout + late_layout),
+        functools.partial(home_kernel, early_places + late_places),
         out_shape=(total_shape, jax.ShapeDtypeStruct((2, TILE, LANES), jnp.float32)),
         in_specs=[SMEM, SMEM] + [VMEM] * (1 + len(early_arrays) + len(late_arrays)),
         out_specs=(VMEM, VMEM),

time: 43 us -> 52.8 us (1.23)
  Pallas kernels: 5.03 us -> 17.1 us
  starting transfers between devices: 16.6 us -> 14.9 us
  local copies, waits for them, and re-layouts: 1.65 us -> 1.1 us
    pallas_call x4, Pallas kernels: 4.22 us -> 16.3 us  [the longest x1 13.1 us: body(): pl.pallas_call(pack_kernel, out_shape=jax.ShapeDtypeStruct((piece_rows, v...]
    ppermute x15 -> x8, starting transfers between devices: 13.1 us -> 9.9 us  [swap(): return lax.ppermute(value, axis, [(i, i ^ mask) for i in range(length)])]
    ppermute x2, starting transfers between devices: 3.48 us -> 5.04 us  [swap_some(): return lax.ppermute(value, axis, pairs)]
    ppermute x15 -> x8, waiting for transfers between devices: 14.1 us -> 13.3 us  [swap(): return lax.ppermute(value, axis, [(i, i ^ mask) for i in range(length)])]
    unnamed x13, local copies, waits for them, and re-layouts: 1.65 us -> 1.1 us
  transfers between devices with their start and end apart: 17 -> 10, of which waited for: 7 -> 4; matrix products, arithmetic and copies ran while one was open for 0% -> 0% of each run, Pallas kernels for 6% -> 4%
where the time goes in v4:
time: 52.8 us; the launch traced here: 52.5 us
  waiting for transfers between devices  19.3 us (37%)
  Pallas kernels  17.1 us (32%)
  starting transfers between devices  14.9 us (28%)
  local copies, waits for them, and re-layouts  1.1 us (2%)
    ppermute x8, waiting for transfers between devices, swap(): return lax.ppermute(value, axis, [(i, i ^ mask) for i in range(length)])  13.3 us
    pallas_call x1, Pallas kernels, body(): pl.pallas_call(pack_kernel, out_shape=jax.ShapeDtypeStruct((piece_rows, v...  13.1 us
    ppermute x8, starting transfers between devices, swap(): return lax.ppermute(value, axis, [(i, i ^ mask) for i in range(length)])  9.9 us
    ppermute x2, waiting for transfers between devices, swap_some(): return lax.ppermute(value, axis, pairs)  5.99 us
    ppermute x2, starting transfers between devices, swap_some(): return lax.ppermute(value, axis, pairs)  5.04 us
    pallas_call x1, Pallas kernels, body(): pl.pallas_call(functools.partial(early_kernel, early_places, mask), out_s...  1.3 us
    unnamed x13, local copies, waits for them, and re-layouts  1.1 us
  transfers between devices with their start and end apart: 10, of which 4 were waited for; matrix products, arithmetic and copies ran while one was open for 0% of the time, Pallas kernels for 4%

profile of v4, /device:TPU:0, one launch (start us, length us, event | category | flops | bytes accessed | tf_op | source)
XLA Modules:
  0.0 52.5 jit_solution(13151942963068486319)
XLA Ops:
  0.0 13.1 %shard_map.64.refs_0_ = bf16[400,512]{1,0:T(8,128)(2,1)} custom-call(bf16[128,1024]{1,0:T(8,128)(2,1)} %keys_ref.1, bf16[128,512]{1,0:T(8,128)(2,1)} %values_ref.1, bf16[1,128]{1,0:T(2,128)(2,1)} %bitcast.1), custom_call_target="tpu_custom_call" | custom-call | tf_op jit(solution)/shard_map/pallas_call | solution.py:266
  13.1 0.0 copy-start.4
  13.1 0.5 collective-permute-start
  13.6 2.6 %collective-permute-start.1 = (bf16[400,512]{1,0:T(8,128)(2,1)}, bf16[400,512]{1,0:T(8,128)(2,1)S(1)}, u32[]{:S(2)}, u32[]{:S(2)}) collective-permute-start(bf16[400,512]{1,0:T(8,128)(2,1)} %shard_map.64.refs_0_), channel_id=1, source_target_pairs={{0,1},{1,0},{2,3},{3,2},{4,5},{5,4},{6,7},{7,6},{8,9},{9,8},{10,11... | collective-permute-start | bytes 1228808 | tf_op jit(solution)/shard_map/ppermute | solution.py:25
  16.2 1.5 %collective-permute-start.3 = (bf16[400,512]{1,0:T(8,128)(2,1)}, bf16[400,512]{1,0:T(8,128)(2,1)S(1)}, u32[]{:S(2)}, u32[]{:S(2)}) collective-permute-start(bf16[400,512]{1,0:T(8,128)(2,1)} %shard_map.64.refs_0_), channel_id=1, source_target_pairs={{0,8},{4,12},{8,0},{12,4},{1,9},{5,13},{9,1},{13,5},{2,10},{6,14},... | collective-permute-start | bytes 1228808 | tf_op jit(solution)/shard_map/ppermute | solution.py:25
  17.7 0.0 collective-permute-done.refs_1_
  17.7 0.7 %collective-permute-start.5 = (bf16[128,1024]{1,0:T(8,128)(2,1)S(1)}, bf16[128,1024]{1,0:T(8,128)(2,1)S(1)}, u32[]{:S(2)}, u32[]{:S(2)}) collective-permute-start(bf16[128,1024]{1,0:T(8,128)(2,1)S(1)} %copy-done.2), channel_id=1, source_target_pairs={{1,2},{2,1},{5,6},{6,5},{9,10},{10,9},{13,14},{14,13},{17,18},{18,... | collective-permute-start | bytes 786440 | tf_op jit(solution)/shard_map/ppermute | solution.py:31
  18.4 8.1 %collective-permute-done.1.refs_2_ = bf16[400,512]{1,0:T(8,128)(2,1)S(1)} collective-permute-done((bf16[400,512]{1,0:T(8,128)(2,1)}, bf16[400,512]{1,0:T(8,128)(2,1)S(1)}, u32[]{:S(2)}, u32[]{:S(2)}) %collective-permute-start.1) | collective-permute-done | bytes 409632 | tf_op jit(solution)/shard_map/ppermute | solution.py:25
  26.5 1.5 %collective-permute-done.3.refs_4_ = bf16[400,512]{1,0:T(8,128)(2,1)S(1)} collective-permute-done((bf16[400,512]{1,0:T(8,128)(2,1)}, bf16[400,512]{1,0:T(8,128)(2,1)S(1)}, u32[]{:S(2)}, u32[]{:S(2)}) %collective-permute-start.3) | collective-permute-done | bytes 409632 | tf_op jit(solution)/shard_map/ppermute | solution.py:25
  28.0 0.0 collective-permute-done.5.inner_ref
  28.0 1.5 %collective-permute-start.6 = (bf16[400,512]{1,0:T(8,128)(2,1)S(1)}, bf16[400,512]{1,0:T(8,128)(2,1)S(1)}, u32[]{:S(2)}, u32[]{:S(2)}) collective-permute-start(bf16[400,512]{1,0:T(8,128)(2,1)S(1)} %collective-permute-done.1.refs_2_), channel_id=1, source_target_pairs={{0,8},{4,12},{8,0},{12,4},{1,9},{5,13},{9,1},{13,5},{2,10},{6,14},... | collective-permute-start | bytes 1228808 | tf_op jit(solution)/shard_map/ppermute | solution.py:25
  29.5 4.4 %collective-permute-start.7 = (bf16[128,1024]{1,0:T(8,128)(2,1)S(1)}, bf16[128,1024]{1,0:T(8,128)(2,1)S(1)}, u32[]{:S(2)}, u32[]{:S(2)}) collective-permute-start(bf16[128,1024]{1,0:T(8,128)(2,1)S(1)} %copy-done.2), channel_id=1, source_target_pairs={{0,3},{3,0},{4,7},{7,4},{8,11},{11,8},{12,15},{15,12},{16,19},{19,... | collective-permute-start | bytes 786440 | tf_op jit(solution)/shard_map/ppermute | solution.py:31
  33.9 0.1 collective-permute-start.2
  34.0 0.5 collective-permute-start.4
  34.4 6.0 %collective-permute-done.7.outer_ref = bf16[128,1024]{1,0:T(8,128)(2,1)S(1)} collective-permute-done((bf16[128,1024]{1,0:T(8,128)(2,1)S(1)}, bf16[128,1024]{1,0:T(8,128)(2,1)S(1)}, u32[]{:S(2)}, u32[]{:S(2)}) %collective-permute-start.7) | collective-permute-done | bytes 262176 | tf_op jit(solution)/shard_map/ppermute | solution.py:31
  40.4 0.0 collective-permute-done.6.refs_6_.refs_3_
  40.4 0.0 collective-permute-start.8
  40.5 0.1 copy.7.lists_ref
  40.5 0.0 collective-permute-done.2.refs_3_
  40.5 0.0 collective-permute-done.4.refs_5_
  40.5 0.0 copy-done.4
  40.6 1.0 %copy-done = bf16[400,512]{1,0:T(8,128)(2,1)S(1)} copy-done((bf16[400,512]{1,0:T(8,128)(2,1)S(1)}, bf16[400,512]{1,0:T(8,128)(2,1)}, u32[]{:S(2)}) %copy-start) | copy-done | bytes 409624
  41.6 1.3 %shard_map.66 = (bf16[128,1024]{1,0:T(8,128)(2,1)S(1)}, f32[128,512]{1,0:T(8,128)S(1)}, f32[128,128]{1,0:T(8,128)S(1)}, f32[128,128]{1,0:T(8,128)S(1)}) custom-call(s32[16,4]{1,0:T(8,128)S(1)} %copy.7.lists_ref, s32[16]{0:T(128)S(1)} %copy-done.4, bf16[128,1024]{1,0:T(8,128)(2,1)S(1)} %collective-permute-done.5.inner_ref, ...), custom_call_target="tpu_custom_call" | custom-call | flops 268435456 | bytes 4194304 | tf_op jit(solution)/shard_map/pallas_call | solution.py:289
  42.9 0.0 collective-permute-done.8.refs_7_.refs_4_
  42.9 0.0 copy-start.1
  42.9 0.0 copy-start.3
  42.9 1.0 %shard_map.67 = bf16[144,512]{1,0:T(8,128)(2,1)S(1)} custom-call(s32[16,4]{1,0:T(8,128)S(1)} %copy.7.lists_ref, s32[16]{0:T(128)S(1)} %copy-done.4, bf16[128,1024]{1,0:T(8,128)(2,1)S(1)} %get-tuple-element.21.query_ref, f32[128,512]{1,0:T(8,128)S(1)} %get-tuple-element.22.refs_0_, f32[128,128]{1,0:T(8,128)S(1)} %get-tuple-element.23.refs_1_, ...), custom_call_target="tpu_custom_call" | custom-call | flops 268435456 | bytes 4194304 | tf_op jit(solution)/shard_map/pallas_call | solution.py:304
  43.9 3.2 %collective-permute-start.9 = (bf16[144,512]{1,0:T(8,128)(2,1)S(1)}, bf16[144,512]{1,0:T(8,128)(2,1)S(1)}, u32[]{:S(2)}, u32[]{:S(2)}) collective-permute-start(bf16[144,512]{1,0:T(8,128)(2,1)S(1)} %shard_map.67), channel_id=1, source_target_pairs={{0,3},{1,2},{2,1},{3,0},{4,7},{5,6},{6,5},{7,4},{8,11},{9,10},{10,... | collective-permute-start | bytes 442376 | tf_op jit(solution)/shard_map/ppermute | solution.py:25
  47.1 0.0 copy-done.3
  47.1 0.9 %shard_map.65 = (f32[128,512]{1,0:T(8,128)S(1)}, f32[2,128,128]{2,1,0:T(8,128)S(1)}) custom-call(s32[16,4]{1,0:T(8,128)S(1)} %copy.7.lists_ref, s32[16]{0:T(128)S(1)} %copy-done.4, bf16[128,1024]{1,0:T(8,128)(2,1)S(1)} %copy-done.3, bf16[400,512]{1,0:T(8,128)(2,1)S(1)} %copy-done.1, bf16[400,512]{1,0:T(8,128)(2,1)S(1)} %collective-permute-done.refs_1_, ...), custom_call_target="tpu_custom_call" | custom-call | flops 268435456 | bytes 4194304 | tf_op jit(solution)/shard_map/pallas_call | solution.py:319
  48.0 3.7 %collective-permute-done.9.refs_0_ = bf16[144,512]{1,0:T(8,128)(2,1)S(1)} collective-permute-done((bf16[144,512]{1,0:T(8,128)(2,1)S(1)}, bf16[144,512]{1,0:T(8,128)(2,1)S(1)}, u32[]{:S(2)}, u32[]{:S(2)}) %collective-permute-start.9) | collective-permute-done | bytes 147488 | tf_op jit(solution)/shard_map/ppermute | solution.py:25
  51.7 0.8 %shard_map.68 = bf16[128,512]{1,0:T(8,128)(2,1)} custom-call(f32[128,512]{1,0:T(8,128)S(1)} %get-tuple-element.19.total_ref, f32[2,128,128]{2,1,0:T(8,128)S(1)} %get-tuple-element.20.stats_ref, bf16[144,512]{1,0:T(8,128)(2,1)S(1)} %collective-permute-done.9.refs_0_), custom_call_target="tpu_custom_call" | custom-call | tf_op jit(solution)/shard_map/pallas_call | solution.py:332
  (6 shorter events, 0.0 us)
Async XLA Ops:
  0.0 17.7 %copy-start.2 = (bf16[128,1024]{1,0:T(8,128)(2,1)S(1)}, bf16[128,1024]{1,0:T(8,128)(2,1)}, u32[]{:S(2)}) copy-start(bf16[128,1024]{1,0:T(8,128)(2,1)} %query_ref.1) | copy-start | bytes 786436
  0.0 40.4 %copy-start.5 = (s32[16,4]{0,1:T(4,128)S(1)}, s32[16,4]{0,1:T(4,128)}, u32[]{:S(2)}) copy-start(s32[16,4]{0,1:T(4,128)} %param.10) | copy-start | bytes 772
  13.1 27.5 %copy-start.4 = (s32[16]{0:T(128)S(1)}, s32[16]{0:T(128)}, u32[]{:S(2)}) copy-start(s32[16]{0:T(128)} %counts_ref.5) | copy-start | bytes 196
  13.1 4.7 %collective-permute-start = (bf16[400,512]{1,0:T(8,128)(2,1)}, bf16[400,512]{1,0:T(8,128)(2,1)S(1)}, u32[]{:S(2)}, u32[]{:S(2)}) collective-permute-start(bf16[400,512]{1,0:T(8,128)(2,1)} %shard_map.64.refs_0_), channel_id=1, source_target_pairs={{0,4},{4,0},{8,12},{12,8},{1,5},{5,1},{9,13},{13,9},{2,6},{6,2},{1... | collective-permute-start | bytes 1228808 | tf_op jit(solution)/shard_map/ppermute | solution.py:25
  13.6 12.9 %collective-permute-start.1 = (bf16[400,512]{1,0:T(8,128)(2,1)}, bf16[400,512]{1,0:T(8,128)(2,1)S(1)}, u32[]{:S(2)}, u32[]{:S(2)}) collective-permute-start(bf16[400,512]{1,0:T(8,128)(2,1)} %shard_map.64.refs_0_), channel_id=1, source_target_pairs={{0,1},{1,0},{2,3},{3,2},{4,5},{5,4},{6,7},{7,6},{8,9},{9,8},{10,11... | collective-permute-start | bytes 1228808 | tf_op jit(solution)/shard_map/ppermute | solution.py:25
  16.2 11.7 %collective-permute-start.3 = (bf16[400,512]{1,0:T(8,128)(2,1)}, bf16[400,512]{1,0:T(8,128)(2,1)S(1)}, u32[]{:S(2)}, u32[]{:S(2)}) collective-permute-start(bf16[400,512]{1,0:T(8,128)(2,1)} %shard_map.64.refs_0_), channel_id=1, source_target_pairs={{0,8},{4,12},{8,0},{12,4},{1,9},{5,13},{9,1},{13,5},{2,10},{6,14},... | collective-permute-start | bytes 1228808 | tf_op jit(solution)/shard_map/ppermute | solution.py:25
  17.7 10.3 %collective-permute-start.5 = (bf16[128,1024]{1,0:T(8,128)(2,1)S(1)}, bf16[128,1024]{1,0:T(8,128)(2,1)S(1)}, u32[]{:S(2)}, u32[]{:S(2)}) collective-permute-start(bf16[128,1024]{1,0:T(8,128)(2,1)S(1)} %copy-done.2), channel_id=1, source_target_pairs={{1,2},{2,1},{5,6},{6,5},{9,10},{10,9},{13,14},{14,13},{17,18},{18,... | collective-permute-start | bytes 786440 | tf_op jit(solution)/shard_map/ppermute | solution.py:31
  28.0 12.4 %collective-permute-start.6 = (bf16[400,512]{1,0:T(8,128)(2,1)S(1)}, bf16[400,512]{1,0:T(8,128)(2,1)S(1)}, u32[]{:S(2)}, u32[]{:S(2)}) collective-permute-start(bf16[400,512]{1,0:T(8,128)(2,1)S(1)} %collective-permute-done.1.refs_2_), channel_id=1, source_target_pairs={{0,8},{4,12},{8,0},{12,4},{1,9},{5,13},{9,1},{13,5},{2,10},{6,14},... | collective-permute-start | bytes 1228808 | tf_op jit(solution)/shard_map/ppermute | solution.py:25
  29.5 10.9 %collective-permute-start.7 = (bf16[128,1024]{1,0:T(8,128)(2,1)S(1)}, bf16[128,1024]{1,0:T(8,128)(2,1)S(1)}, u32[]{:S(2)}, u32[]{:S(2)}) collective-permute-start(bf16[128,1024]{1,0:T(8,128)(2,1)S(1)} %copy-done.2), channel_id=1, source_target_pairs={{0,3},{3,0},{4,7},{7,4},{8,11},{11,8},{12,15},{15,12},{16,19},{19,... | collective-permute-start | bytes 786440 | tf_op jit(solution)/shard_map/ppermute | solution.py:31
  33.9 6.7 %collective-permute-start.2 = (bf16[400,512]{1,0:T(8,128)(2,1)S(1)}, bf16[400,512]{1,0:T(8,128)(2,1)S(1)}, u32[]{:S(2)}, u32[]{:S(2)}) collective-permute-start(bf16[400,512]{1,0:T(8,128)(2,1)S(1)} %collective-permute-done.1.refs_2_), channel_id=1, source_target_pairs={{0,4},{4,0},{8,12},{12,8},{1,5},{5,1},{9,13},{13,9},{2,6},{6,2},{1... | collective-permute-start | bytes 1228808 | tf_op jit(solution)/shard_map/ppermute | solution.py:25
  34.0 6.6 %collective-permute-start.4 = (bf16[400,512]{1,0:T(8,128)(2,1)S(1)}, bf16[400,512]{1,0:T(8,128)(2,1)S(1)}, u32[]{:S(2)}, u32[]{:S(2)}) collective-permute-start(bf16[400,512]{1,0:T(8,128)(2,1)S(1)} %collective-permute-done.3.refs_4_), channel_id=1, source_target_pairs={{0,4},{4,0},{8,12},{12,8},{1,5},{5,1},{9,13},{13,9},{2,6},{6,2},{1... | collective-permute-start | bytes 1228808 | tf_op jit(solution)/shard_map/ppermute | solution.py:25
  40.4 2.4 %collective-permute-start.8 = (bf16[400,512]{1,0:T(8,128)(2,1)S(1)}, bf16[400,512]{1,0:T(8,128)(2,1)S(1)}, u32[]{:S(2)}, u32[]{:S(2)}) collective-permute-start(bf16[400,512]{1,0:T(8,128)(2,1)S(1)} %collective-permute-done.6.refs_6_.refs_3_), channel_id=1, source_target_pairs={{0,4},{4,0},{8,12},{12,8},{1,5},{5,1},{9,13},{13,9},{2,6},{6,2},{1... | collective-permute-start | bytes 1228808 | tf_op jit(solution)/shard_map/ppermute | solution.py:25
  40.5 1.0 %copy-start = (bf16[400,512]{1,0:T(8,128)(2,1)S(1)}, bf16[400,512]{1,0:T(8,128)(2,1)}, u32[]{:S(2)}) copy-start(bf16[400,512]{1,0:T(8,128)(2,1)} %shard_map.64.refs_0_) | copy-start | bytes 1228804
  42.9 4.2 %copy-start.1 = (bf16[400,512]{1,0:T(8,128)(2,1)S(1)}, bf16[400,512]{1,0:T(8,128)(2,1)}, u32[]{:S(2)}) copy-start(bf16[400,512]{1,0:T(8,128)(2,1)} %shard_map.64.refs_0_) | copy-start | bytes 1228804
  42.9 4.2 %copy-start.3 = (bf16[128,1024]{1,0:T(8,128)(2,1)S(1)}, bf16[128,1024]{1,0:T(8,128)(2,1)}, u32[]{:S(2)}) copy-start(bf16[128,1024]{1,0:T(8,128)(2,1)} %query_ref.1) | copy-start | bytes 786436
  43.9 7.8 %collective-permute-start.9 = (bf16[144,512]{1,0:T(8,128)(2,1)S(1)}, bf16[144,512]{1,0:T(8,128)(2,1)S(1)}, u32[]{:S(2)}, u32[]{:S(2)}) collective-permute-start(bf16[144,512]{1,0:T(8,128)(2,1)S(1)} %shard_map.67), channel_id=1, source_target_pairs={{0,3},{1,2},{2,1},{3,0},{4,7},{5,6},{6,5},{7,4},{8,11},{9,10},{10,... | collective-permute-start | bytes 442376 | tf_op jit(solution)/shard_map/ppermute | solution.py:25

commit v5 on v3

--- a/solution.py
+++ b/solution.py
@@ -243,31 +243,42 @@
         out_ref[:, at : at + LANES] = merged.astype(jnp.bfloat16)
 
 
-def gather_library(keys, values, first_arrivals):
+def both_cores(pieces, arrivals=()):
+    places, arrays = [], []
+    for (lib_mask, qry_mask), *pair in pieces:
+        sent = tie(*pair, *arrivals)[:2]
+        places += [("pair", (lib_mask, qry_mask)), ("pair", (lib_mask | 1, qry_mask))]
+        arrays += pair + [swap(array, "lib", 1) for array in sent]
+    return places, arrays
+
+
+def gather_library(keys, partner_keys, values, queries, masks):
     steps = [("qry", 1)]
     mask = lax.axis_size("lib") // 2
     while mask > 1:
         steps.append(("lib", mask))
         mask //= 2
-    early, late = [((0, 0), keys, values)], []
+    own_places = [("pair", (0, 0)), ("pair", (1, 0))]
+    own_arrays = [keys, values, partner_keys, swap(values, "lib", 1)]
+    nearer, _ = tie(queries, values)
+    inner = [swap_some(nearer, "qry", mask, True) for mask in masks]
+    early, late = [], []
     for axis, mask in steps:
         place = (0, mask) if axis == "qry" else (mask, 0)
         near = (place, swap(keys, axis, mask), swap(values, axis, mask))
         relayed = []
-        for (lib_mask, qry_mask), far_keys, far_values in early[1:] + late:
-            far_keys, far_values, *_ = tie(far_keys, far_values, near[1], near[2], *first_arrivals)
+        for (lib_mask, qry_mask), far_keys, far_values in early + late:
+            far_keys, _ = tie(far_keys, near[1])
+            far_values, *_ = tie(far_values, near[2], *inner)
             place = (lib_mask | mask, qry_mask)
             relayed.append((place, swap(far_keys, axis, mask), swap(far_values, axis, mask)))
         early, late = early + late + [near], relayed
-    return early, late
-
-
-def both_cores(pieces):
-    layout, arrays = [], []
-    for (lib_mask, qry_mask), *pair in pieces:
-        layout += [("pair", (lib_mask, qry_mask)), ("pair", (lib_mask | 1, qry_mask))]
-        arrays += pair + [swap(array, "lib", 1) for array in pair]
-    return layout, arrays
+    farther, *_ = tie(queries, *early[0][1:])
+    outer = [swap_some(farther, "qry", mask, False) for mask in masks]
+    early_places, early_arrays = both_cores(early)
+    late_places, late_arrays = both_cores(late, outer)
+    early = (own_places + early_places, own_arrays + early_arrays)
+    return early, (late_places, late_arrays), list(zip(masks, inner, outer))
 
 
 def body(queries, library_keys, library_values, key_scale, block_list, block_count):
@@ -275,6 +286,8 @@
     width = library_keys.shape[1]
     value_width = library_values.shape[1]
 
+    partner_keys = swap(library_keys, "lib", 1)
+    own_values, _ = tie(library_values, partner_keys)
     values = pl.pallas_call(
         pack_kernel,
         out_shape=jax.ShapeDtypeStruct((TILE + EXTRA, value_width), jnp.bfloat16),
@@ -282,24 +295,23 @@
         out_specs=VMEM,
         scratch_shapes=[pltpu.VMEM((1, TILE), jnp.bfloat16), pltpu.SemaphoreType.DMA((2,))],
         compiler_params=params(),
-    )(library_values, key_scale.reshape(1, TILE))
+    )(own_values, key_scale.reshape(1, TILE))
 
     masks = [2 * at + 1 for at in range(1, qry_count // 2)]
-    inner = [swap_some(queries, "qry", mask, True) for mask in masks]
-    early, late = gather_library(library_keys, values, inner)
+    (early_places, early_arrays), (late_places, late_arrays), visitors = gather_library(
+        library_keys, partner_keys, values, queries, masks
+    )
     piece_rows = (width // value_width + 1) * TILE + EXTRA
-    (early_layout, early_arrays), (late_layout, late_arrays) = both_cores(early), both_cores(late)
-    count_early, count_late = 2 * len(early), 2 * len(late)
+    count_early, count_late = len(early_places), len(late_places)
 
     cost = pl.CostEstimate(flops=2 * TILE * 4 * TILE * width * 2, bytes_accessed=4 * 1024 * 1024, transcendentals=0)
     total_shape = jax.ShapeDtypeStruct((TILE, value_width), jnp.float32)
     line_shape = jax.ShapeDtypeStruct((TILE, LANES), jnp.float32)
     attend_params = params((count_early + count_late) * piece_rows * value_width * 2)
     returned = []
-    for mask, inner_queries in zip(masks, inner):
-        waiting, *_ = tie(queries, early[1][1], early[1][2])
+    for mask, inner_queries, outer_queries in visitors:
         *state, = pl.pallas_call(
-            functools.partial(early_kernel, early_layout, mask),
+            functools.partial(early_kernel, early_places, mask),
             out_shape=(jax.ShapeDtypeStruct(queries.shape, queries.dtype), total_shape, line_shape, line_shape),
             in_specs=[SMEM, SMEM] + [VMEM] * (2 + len(early_arrays)),
             out_specs=(VMEM,) * 4,
@@ -310,11 +322,11 @@
             block_list,
             block_count,
             inner_queries,
-            swap_some(waiting, "qry", mask, False),
+            outer_queries,
             *early_arrays,
         )
         packed = pl.pallas_call(
-            functools.partial(late_kernel, late_layout, mask),
+            functools.partial(late_kernel, late_places, mask),
             out_shape=jax.ShapeDtypeStruct((TILE + EXTRA, value_width), jnp.bfloat16),
             in_specs=[SMEM, SMEM] + [VMEM] * (4 + len(late_arrays)),
             out_specs=VMEM,
@@ -329,7 +341,7 @@
         returned.append(swap(packed, "qry", mask))
 
     total, stats = pl.pallas_call(
-        functools.partial(home_kernel, early_layout + late_layout),
+        functools.partial(home_kernel, early_places + late_places),
         out_shape=(total_shape, jax.ShapeDtypeStruct((2, TILE, LANES), jnp.float32)),
         in_specs=[SMEM, SMEM] + [VMEM] * (1 + len(early_arrays) + len(late_arrays)),
         out_specs=(VMEM, VMEM),

time: 43 us -> 40.6 us (0.944); the launches traced: 43.1 us -> 40.2 us
  waiting for transfers between devices: 19.6 us -> 11.3 us
  starting transfers between devices: 16.6 us -> 20.3 us
  local copies, waits for them, and re-layouts: 1.65 us -> 3.31 us
    ppermute x15, waiting for transfers between devices: 14.1 us -> 7.11 us  [swap(): return lax.ppermute(value, axis, [(i, i ^ mask) for i in range(length)])]
    ppermute x2, starting transfers between devices: 3.48 us -> 5.76 us  [swap_some(): return lax.ppermute(value, axis, pairs)]
    unnamed x13 -> x17, local copies, waits for them, and re-layouts: 1.65 us -> 3.31 us
    ppermute x15, starting transfers between devices: 13.1 us -> 14.6 us  [swap(): return lax.ppermute(value, axis, [(i, i ^ mask) for i in range(length)])]
    ppermute x2, waiting for transfers between devices: 5.52 us -> 4.23 us  [swap_some(): return lax.ppermute(value, axis, pairs)]
  transfers between devices with their start and end apart: 17 -> 17, of which waited for: 7 -> 5; matrix products, arithmetic and copies ran while one was open for 0% -> 0% of each run, Pallas kernels for 6% -> 8%
where the time goes in v5:
time: 40.6 us; the launch traced here: 40.2 us
  starting transfers between devices  20.3 us (50%)
  waiting for transfers between devices  11.3 us (28%)
  Pallas kernels  5.11 us (13%)
  local copies, waits for them, and re-layouts  3.31 us (8%)
    ppermute x15, starting transfers between devices, swap(): return lax.ppermute(value, axis, [(i, i ^ mask) for i in range(length)])  14.6 us
    ppermute x15, waiting for transfers between devices, swap(): return lax.ppermute(value, axis, [(i, i ^ mask) for i in range(length)])  7.11 us
    ppermute x2, starting transfers between devices, swap_some(): return lax.ppermute(value, axis, pairs)  5.76 us
    ppermute x2, waiting for transfers between devices, swap_some(): return lax.ppermute(value, axis, pairs)  4.23 us
    unnamed x17, local copies, waits for them, and re-layouts  3.31 us
    pallas_call x1, Pallas kernels, body(): pl.pallas_call(functools.partial(home_kernel, early_places + late_places)...  1.82 us
    pallas_call x1, Pallas kernels, body(): pl.pallas_call(functools.partial(early_kernel, early_places, mask), out_s...  1.31 us
    pallas_call x1, Pallas kernels, body(): pl.pallas_call(functools.partial(late_kernel, late_places, mask), out_sha...  0.99 us
  transfers between devices with their start and end apart: 17, of which 5 were waited for; matrix products, arithmetic and copies ran while one was open for 0% of the time, Pallas kernels for 8%

profile of v5, /device:TPU:0, one launch (start us, length us, event | category | flops | bytes accessed | tf_op | source)
XLA Modules:
  0.0 40.2 jit_solution(1766155276891370455)
XLA Ops:
  0.0 0.5 %collective-permute-start = (bf16[128,1024]{1,0:T(8,128)(2,1)}, bf16[128,1024]{1,0:T(8,128)(2,1)S(1)}, u32[]{:S(2)}, u32[]{:S(2)}) collective-permute-start(bf16[128,1024]{1,0:T(8,128)(2,1)} %refs_0_.3), channel_id=1, source_target_pairs={{0,4},{4,0},{8,12},{12,8},{1,5},{5,1},{9,13},{13,9},{2,6},{6,2},{1... | collective-permute-start | bytes 786440 | tf_op jit(solution)/shard_map/ppermute | solution.py:25
  0.5 2.6 %collective-permute-start.2 = (bf16[128,1024]{1,0:T(8,128)(2,1)}, bf16[128,1024]{1,0:T(8,128)(2,1)S(1)}, u32[]{:S(2)}, u32[]{:S(2)}) collective-permute-start(bf16[128,1024]{1,0:T(8,128)(2,1)} %refs_0_.3), channel_id=1, source_target_pairs={{0,1},{1,0},{2,3},{3,2},{4,5},{5,4},{6,7},{7,6},{8,9},{9,8},{10,11... | collective-permute-start | bytes 786440 | tf_op jit(solution)/shard_map/ppermute | solution.py:25
  3.1 1.5 %collective-permute-start.6 = (bf16[128,1024]{1,0:T(8,128)(2,1)}, bf16[128,1024]{1,0:T(8,128)(2,1)S(1)}, u32[]{:S(2)}, u32[]{:S(2)}) collective-permute-start(bf16[128,1024]{1,0:T(8,128)(2,1)} %refs_0_.3), channel_id=1, source_target_pairs={{0,8},{4,12},{8,0},{12,4},{1,9},{5,13},{9,1},{13,5},{2,10},{6,14},... | collective-permute-start | bytes 786440 | tf_op jit(solution)/shard_map/ppermute | solution.py:25
  4.6 0.9 %copy-done.4 = bf16[128,512]{1,0:T(8,128)(2,1)S(1)} copy-done((bf16[128,512]{1,0:T(8,128)(2,1)S(1)}, bf16[128,512]{1,0:T(8,128)(2,1)}, u32[]{:S(2)}) %copy-start.4) | copy-done | bytes 131096
  5.5 0.7 %copy-done.6 = bf16[128]{0:T(256)(128)(2,1)S(1)} copy-done((bf16[128]{0:T(256)(128)(2,1)S(1)}, bf16[128]{0:T(256)(128)(2,1)}, u32[]{:S(2)}) %copy-start.6) | copy-done | bytes 280
  6.1 0.2 shard_map.64.refs_1_
  6.3 0.0 copy-start.5
  6.3 0.5 %collective-permute-start.3 = (bf16[144,512]{1,0:T(8,128)(2,1)S(1)}, bf16[144,512]{1,0:T(8,128)(2,1)S(1)}, u32[]{:S(2)}, u32[]{:S(2)}) collective-permute-start(bf16[144,512]{1,0:T(8,128)(2,1)S(1)} %shard_map.64.refs_1_), channel_id=1, source_target_pairs={{0,1},{1,0},{2,3},{3,2},{4,5},{5,4},{6,7},{7,6},{8,9},{9,8},{10,11... | collective-permute-start | bytes 442376 | tf_op jit(solution)/shard_map/ppermute | solution.py:25
  6.9 0.7 %collective-permute-start.11 = (bf16[128,1024]{1,0:T(8,128)(2,1)}, bf16[128,1024]{1,0:T(8,128)(2,1)S(1)}, u32[]{:S(2)}, u32[]{:S(2)}) collective-permute-start(bf16[128,1024]{1,0:T(8,128)(2,1)} %query_ref.1), channel_id=1, source_target_pairs={{1,2},{2,1},{5,6},{6,5},{9,10},{10,9},{13,14},{14,13},{17,18},{18,... | collective-permute-start | bytes 786440 | tf_op jit(solution)/shard_map/ppermute | solution.py:31
  7.5 1.3 %collective-permute-start.7 = (bf16[144,512]{1,0:T(8,128)(2,1)S(1)}, bf16[144,512]{1,0:T(8,128)(2,1)S(1)}, u32[]{:S(2)}, u32[]{:S(2)}) collective-permute-start(bf16[144,512]{1,0:T(8,128)(2,1)S(1)} %shard_map.64.refs_1_), channel_id=1, source_target_pairs={{0,8},{4,12},{8,0},{12,4},{1,9},{5,13},{9,1},{13,5},{2,10},{6,14},... | collective-permute-start | bytes 442376 | tf_op jit(solution)/shard_map/ppermute | solution.py:25
  8.8 1.6 %collective-permute-done.2.refs_4_ = bf16[128,1024]{1,0:T(8,128)(2,1)S(1)} collective-permute-done((bf16[128,1024]{1,0:T(8,128)(2,1)}, bf16[128,1024]{1,0:T(8,128)(2,1)S(1)}, u32[]{:S(2)}, u32[]{:S(2)}) %collective-permute-start.2) | collective-permute-done | bytes 262176 | tf_op jit(solution)/shard_map/ppermute | solution.py:25
  10.5 2.0 %collective-permute-done.6.refs_8_ = bf16[128,1024]{1,0:T(8,128)(2,1)S(1)} collective-permute-done((bf16[128,1024]{1,0:T(8,128)(2,1)}, bf16[128,1024]{1,0:T(8,128)(2,1)S(1)}, u32[]{:S(2)}, u32[]{:S(2)}) %collective-permute-start.6) | collective-permute-done | bytes 262176 | tf_op jit(solution)/shard_map/ppermute | solution.py:25
  12.5 1.5 %collective-permute-start.10 = (bf16[128,1024]{1,0:T(8,128)(2,1)S(1)}, bf16[128,1024]{1,0:T(8,128)(2,1)S(1)}, u32[]{:S(2)}, u32[]{:S(2)}) collective-permute-start(bf16[128,1024]{1,0:T(8,128)(2,1)S(1)} %collective-permute-done.2.refs_4_), channel_id=1, source_target_pairs={{0,8},{4,12},{8,0},{12,4},{1,9},{5,13},{9,1},{13,5},{2,10},{6,14},... | collective-permute-start | bytes 786440 | tf_op jit(solution)/shard_map/ppermute | solution.py:25
  13.9 5.1 %collective-permute-start.13 = (bf16[128,1024]{1,0:T(8,128)(2,1)}, bf16[128,1024]{1,0:T(8,128)(2,1)S(1)}, u32[]{:S(2)}, u32[]{:S(2)}) collective-permute-start(bf16[128,1024]{1,0:T(8,128)(2,1)} %query_ref.1), channel_id=1, source_target_pairs={{0,3},{3,0},{4,7},{7,4},{8,11},{11,8},{12,15},{15,12},{16,19},{19,... | collective-permute-start | bytes 786440 | tf_op jit(solution)/shard_map/ppermute | solution.py:31
  19.1 1.6 %collective-permute-start.12 = (bf16[144,512]{1,0:T(8,128)(2,1)S(1)}, bf16[144,512]{1,0:T(8,128)(2,1)S(1)}, u32[]{:S(2)}, u32[]{:S(2)}) collective-permute-start(bf16[144,512]{1,0:T(8,128)(2,1)S(1)} %collective-permute-done.3.refs_5_), channel_id=1, source_target_pairs={{0,8},{4,12},{8,0},{12,4},{1,9},{5,13},{9,1},{13,5},{2,10},{6,14},... | collective-permute-start | bytes 442376 | tf_op jit(solution)/shard_map/ppermute | solution.py:25
  20.6 0.5 %collective-permute-start.5 = (bf16[144,512]{1,0:T(8,128)(2,1)S(1)}, bf16[144,512]{1,0:T(8,128)(2,1)S(1)}, u32[]{:S(2)}, u32[]{:S(2)}) collective-permute-start(bf16[144,512]{1,0:T(8,128)(2,1)S(1)} %collective-permute-done.3.refs_5_), channel_id=1, source_target_pairs={{0,4},{4,0},{8,12},{12,8},{1,5},{5,1},{9,13},{13,9},{2,6},{6,2},{1... | collective-permute-start | bytes 442376 | tf_op jit(solution)/shard_map/ppermute | solution.py:25
  21.1 0.0 collective-permute-start.4
  21.1 4.2 %collective-permute-done.13.outer_ref = bf16[128,1024]{1,0:T(8,128)(2,1)S(1)} collective-permute-done((bf16[128,1024]{1,0:T(8,128)(2,1)}, bf16[128,1024]{1,0:T(8,128)(2,1)S(1)}, u32[]{:S(2)}, u32[]{:S(2)}) %collective-permute-start.13) | collective-permute-done | bytes 262176 | tf_op jit(solution)/shard_map/ppermute | solution.py:31
  25.4 0.7 %copy-done.1 = bf16[128,1024]{1,0:T(8,128)(2,1)} copy-done((bf16[128,1024]{1,0:T(8,128)(2,1)}, bf16[128,1024]{1,0:T(8,128)(2,1)S(1)}, u32[]{:S(2)}) %copy-start.1) | copy-done | bytes 262168
  26.1 0.5 %collective-permute-start.14 = (bf16[128,1024]{1,0:T(8,128)(2,1)S(1)}, bf16[128,1024]{1,0:T(8,128)(2,1)S(1)}, u32[]{:S(2)}, u32[]{:S(2)}) collective-permute-start(bf16[128,1024]{1,0:T(8,128)(2,1)S(1)} %collective-permute-done.10.refs_12_.refs_3_), channel_id=1, source_target_pairs={{0,4},{4,0},{8,12},{12,8},{1,5},{5,1},{9,13},{13,9},{2,6},{6,2},{1... | collective-permute-start | bytes 786440 | tf_op jit(solution)/shard_map/ppermute | solution.py:25
  26.6 0.1 collective-permute-start.9
  26.7 0.4 %collective-permute-start.15 = (bf16[144,512]{1,0:T(8,128)(2,1)S(1)}, bf16[144,512]{1,0:T(8,128)(2,1)S(1)}, u32[]{:S(2)}, u32[]{:S(2)}) collective-permute-start(bf16[144,512]{1,0:T(8,128)(2,1)S(1)} %collective-permute-done.12.refs_13_.refs_4_), channel_id=1, source_target_pairs={{0,4},{4,0},{8,12},{12,8},{1,5},{5,1},{9,13},{13,9},{2,6},{6,2},{1... | collective-permute-start | bytes 442376 | tf_op jit(solution)/shard_map/ppermute | solution.py:25
  27.1 0.1 copy.7.lists_ref
  27.2 1.0 %collective-permute-done.9.refs_11_ = bf16[144,512]{1,0:T(8,128)(2,1)S(1)} collective-permute-done((bf16[144,512]{1,0:T(8,128)(2,1)S(1)}, bf16[144,512]{1,0:T(8,128)(2,1)S(1)}, u32[]{:S(2)}, u32[]{:S(2)}) %collective-permute-start.9) | collective-permute-done | bytes 147488 | tf_op jit(solution)/shard_map/ppermute | solution.py:25
  28.2 0.9 %copy-done.2 = bf16[128,1024]{1,0:T(8,128)(2,1)S(1)} copy-done((bf16[128,1024]{1,0:T(8,128)(2,1)S(1)}, bf16[128,1024]{1,0:T(8,128)(2,1)}, u32[]{:S(2)}) %copy-start.2) | copy-done | bytes 262168
  29.2 1.3 %shard_map.66 = (bf16[128,1024]{1,0:T(8,128)(2,1)S(1)}, f32[128,512]{1,0:T(8,128)S(1)}, f32[128,128]{1,0:T(8,128)S(1)}, f32[128,128]{1,0:T(8,128)S(1)}) custom-call(s32[16,4]{1,0:T(8,128)S(1)} %copy.7.lists_ref, s32[16]{0:T(128)S(1)} %copy-done.5, bf16[128,1024]{1,0:T(8,128)(2,1)S(1)} %collective-permute-done.11.inner_ref, bf16[128,1024]{1,0:T(8,128)(2,1)S(1)} %copy-done.2, ...), custom_call_target="tpu_custom_call" | custom-call | flops 268435456 | bytes 4194304 | tf_op jit(solution)/shard_map/pallas_call | solution.py:313
  30.5 0.0 copy-start.3
  30.5 1.0 %shard_map.67 = bf16[144,512]{1,0:T(8,128)(2,1)S(1)} custom-call(s32[16,4]{1,0:T(8,128)S(1)} %copy.7.lists_ref, s32[16]{0:T(128)S(1)} %copy-done.5, bf16[128,1024]{1,0:T(8,128)(2,1)S(1)} %get-tuple-element.35.query_ref, f32[128,512]{1,0:T(8,128)S(1)} %get-tuple-element.36.refs_0_, f32[128,128]{1,0:T(8,128)S(1)} %get-tuple-element.37.refs_1_, ...), custom_call_target="tpu_custom_call" | custom-call | flops 268435456 | bytes 4194304 | tf_op jit(solution)/shard_map/pallas_call | solution.py:328
  31.5 3.6 %collective-permute-start.16 = (bf16[144,512]{1,0:T(8,128)(2,1)S(1)}, bf16[144,512]{1,0:T(8,128)(2,1)S(1)}, u32[]{:S(2)}, u32[]{:S(2)}) collective-permute-start(bf16[144,512]{1,0:T(8,128)(2,1)S(1)} %shard_map.67), channel_id=1, source_target_pairs={{0,3},{1,2},{2,1},{3,0},{4,7},{5,6},{6,5},{7,4},{8,11},{9,10},{10,... | collective-permute-start | bytes 442376 | tf_op jit(solution)/shard_map/ppermute | solution.py:25
  35.1 1.8 %shard_map.65 = (f32[128,512]{1,0:T(8,128)S(1)}, f32[2,128,128]{2,1,0:T(8,128)S(1)}) custom-call(s32[16,4]{1,0:T(8,128)S(1)} %copy.7.lists_ref, s32[16]{0:T(128)S(1)} %copy-done.5, bf16[128,1024]{1,0:T(8,128)(2,1)S(1)} %copy-done.3, bf16[128,1024]{1,0:T(8,128)(2,1)S(1)} %copy-done, bf16[144,512]{1,0:T(8,128)(2,1)S(1)} %shard_map.64.refs_1_, ...), custom_call_target="tpu_custom_call" | custom-call | flops 268435456 | bytes 4194304 | tf_op jit(solution)/shard_map/pallas_call | solution.py:343
  37.0 2.4 %collective-permute-done.16.refs_0_ = bf16[144,512]{1,0:T(8,128)(2,1)S(1)} collective-permute-done((bf16[144,512]{1,0:T(8,128)(2,1)S(1)}, bf16[144,512]{1,0:T(8,128)(2,1)S(1)}, u32[]{:S(2)}, u32[]{:S(2)}) %collective-permute-start.16) | collective-permute-done | bytes 147488 | tf_op jit(solution)/shard_map/ppermute | solution.py:25
  39.4 0.8 %shard_map.68 = bf16[128,512]{1,0:T(8,128)(2,1)} custom-call(f32[128,512]{1,0:T(8,128)S(1)} %get-tuple-element.33.total_ref, f32[2,128,128]{2,1,0:T(8,128)S(1)} %get-tuple-element.34.stats_ref, bf16[144,512]{1,0:T(8,128)(2,1)S(1)} %collective-permute-done.16.refs_0_), custom_call_target="tpu_custom_call" | custom-call | tf_op jit(solution)/shard_map/pallas_call | solution.py:356
  (24 shorter events, 0.1 us)
Async XLA Ops:
  0.0 28.2 %copy-start = (bf16[128,1024]{1,0:T(8,128)(2,1)S(1)}, bf16[128,1024]{1,0:T(8,128)(2,1)}, u32[]{:S(2)}) copy-start(bf16[128,1024]{1,0:T(8,128)(2,1)} %refs_0_.3) | copy-start | bytes 786436
  0.0 4.6 %collective-permute-start = (bf16[128,1024]{1,0:T(8,128)(2,1)}, bf16[128,1024]{1,0:T(8,128)(2,1)S(1)}, u32[]{:S(2)}, u32[]{:S(2)}) collective-permute-start(bf16[128,1024]{1,0:T(8,128)(2,1)} %refs_0_.3), channel_id=1, source_target_pairs={{0,4},{4,0},{8,12},{12,8},{1,5},{5,1},{9,13},{13,9},{2,6},{6,2},{1... | collective-permute-start | bytes 786440 | tf_op jit(solution)/shard_map/ppermute | solution.py:25
  0.5 10.0 %collective-permute-start.2 = (bf16[128,1024]{1,0:T(8,128)(2,1)}, bf16[128,1024]{1,0:T(8,128)(2,1)S(1)}, u32[]{:S(2)}, u32[]{:S(2)}) collective-permute-start(bf16[128,1024]{1,0:T(8,128)(2,1)} %refs_0_.3), channel_id=1, source_target_pairs={{0,1},{1,0},{2,3},{3,2},{4,5},{5,4},{6,7},{7,6},{8,9},{9,8},{10,11... | collective-permute-start | bytes 786440 | tf_op jit(solution)/shard_map/ppermute | solution.py:25
  3.1 9.4 %collective-permute-start.6 = (bf16[128,1024]{1,0:T(8,128)(2,1)}, bf16[128,1024]{1,0:T(8,128)(2,1)S(1)}, u32[]{:S(2)}, u32[]{:S(2)}) collective-permute-start(bf16[128,1024]{1,0:T(8,128)(2,1)} %refs_0_.3), channel_id=1, source_target_pairs={{0,8},{4,12},{8,0},{12,4},{1,9},{5,13},{9,1},{13,5},{2,10},{6,14},... | collective-permute-start | bytes 786440 | tf_op jit(solution)/shard_map/ppermute | solution.py:25
  4.6 0.9 %copy-start.4 = (bf16[128,512]{1,0:T(8,128)(2,1)S(1)}, bf16[128,512]{1,0:T(8,128)(2,1)}, u32[]{:S(2)}) copy-start(bf16[128,512]{1,0:T(8,128)(2,1)} %values_ref) | copy-start | bytes 393220
  5.5 0.7 %copy-start.6 = (bf16[128]{0:T(256)(128)(2,1)S(1)}, bf16[128]{0:T(256)(128)(2,1)}, u32[]{:S(2)}) copy-start(bf16[128]{0:T(256)(128)(2,1)} %param.9) | copy-start | bytes 772
  6.1 21.0 %copy-start.7 = (s32[16,4]{0,1:T(4,128)S(1)}, s32[16,4]{0,1:T(4,128)}, u32[]{:S(2)}) copy-start(s32[16,4]{0,1:T(4,128)} %param.10) | copy-start | bytes 772
  6.3 21.9 %copy-start.5 = (s32[16]{0:T(128)S(1)}, s32[16]{0:T(128)}, u32[]{:S(2)}) copy-start(s32[16]{0:T(128)} %counts_ref.5) | copy-start | bytes 196
  6.3 7.6 %collective-permute-start.3 = (bf16[144,512]{1,0:T(8,128)(2,1)S(1)}, bf16[144,512]{1,0:T(8,128)(2,1)S(1)}, u32[]{:S(2)}, u32[]{:S(2)}) collective-permute-start(bf16[144,512]{1,0:T(8,128)(2,1)S(1)} %shard_map.64.refs_1_), channel_id=1, source_target_pairs={{0,1},{1,0},{2,3},{3,2},{4,5},{5,4},{6,7},{7,6},{8,9},{9,8},{10,11... | collective-permute-start | bytes 442376 | tf_op jit(solution)/shard_map/ppermute | solution.py:25
  6.9 12.2 %collective-permute-start.11 = (bf16[128,1024]{1,0:T(8,128)(2,1)}, bf16[128,1024]{1,0:T(8,128)(2,1)S(1)}, u32[]{:S(2)}, u32[]{:S(2)}) collective-permute-start(bf16[128,1024]{1,0:T(8,128)(2,1)} %query_ref.1), channel_id=1, source_target_pairs={{1,2},{2,1},{5,6},{6,5},{9,10},{10,9},{13,14},{14,13},{17,18},{18,... | collective-permute-start | bytes 786440 | tf_op jit(solution)/shard_map/ppermute | solution.py:31
  7.5 11.5 %collective-permute-start.7 = (bf16[144,512]{1,0:T(8,128)(2,1)S(1)}, bf16[144,512]{1,0:T(8,128)(2,1)S(1)}, u32[]{:S(2)}, u32[]{:S(2)}) collective-permute-start(bf16[144,512]{1,0:T(8,128)(2,1)S(1)} %shard_map.64.refs_1_), channel_id=1, source_target_pairs={{0,8},{4,12},{8,0},{12,4},{1,9},{5,13},{9,1},{13,5},{2,10},{6,14},... | collective-permute-start | bytes 442376 | tf_op jit(solution)/shard_map/ppermute | solution.py:25
  12.5 8.7 %collective-permute-start.10 = (bf16[128,1024]{1,0:T(8,128)(2,1)S(1)}, bf16[128,1024]{1,0:T(8,128)(2,1)S(1)}, u32[]{:S(2)}, u32[]{:S(2)}) collective-permute-start(bf16[128,1024]{1,0:T(8,128)(2,1)S(1)} %collective-permute-done.2.refs_4_), channel_id=1, source_target_pairs={{0,8},{4,12},{8,0},{12,4},{1,9},{5,13},{9,1},{13,5},{2,10},{6,14},... | collective-permute-start | bytes 786440 | tf_op jit(solution)/shard_map/ppermute | solution.py:25
  13.9 11.4 %collective-permute-start.13 = (bf16[128,1024]{1,0:T(8,128)(2,1)}, bf16[128,1024]{1,0:T(8,128)(2,1)S(1)}, u32[]{:S(2)}, u32[]{:S(2)}) collective-permute-start(bf16[128,1024]{1,0:T(8,128)(2,1)} %query_ref.1), channel_id=1, source_target_pairs={{0,3},{3,0},{4,7},{7,4},{8,11},{11,8},{12,15},{15,12},{16,19},{19,... | collective-permute-start | bytes 786440 | tf_op jit(solution)/shard_map/ppermute | solution.py:31
  19.1 7.0 %collective-permute-start.12 = (bf16[144,512]{1,0:T(8,128)(2,1)S(1)}, bf16[144,512]{1,0:T(8,128)(2,1)S(1)}, u32[]{:S(2)}, u32[]{:S(2)}) collective-permute-start(bf16[144,512]{1,0:T(8,128)(2,1)S(1)} %collective-permute-done.3.refs_5_), channel_id=1, source_target_pairs={{0,8},{4,12},{8,0},{12,4},{1,9},{5,13},{9,1},{13,5},{2,10},{6,14},... | collective-permute-start | bytes 442376 | tf_op jit(solution)/shard_map/ppermute | solution.py:25
  20.6 6.0 %collective-permute-start.1 = (bf16[144,512]{1,0:T(8,128)(2,1)S(1)}, bf16[144,512]{1,0:T(8,128)(2,1)S(1)}, u32[]{:S(2)}, u32[]{:S(2)}) collective-permute-start(bf16[144,512]{1,0:T(8,128)(2,1)S(1)} %shard_map.64.refs_1_), channel_id=1, source_target_pairs={{0,4},{4,0},{8,12},{12,8},{1,5},{5,1},{9,13},{13,9},{2,6},{6,2},{1... | collective-permute-start | bytes 442376 | tf_op jit(solution)/shard_map/ppermute | solution.py:25
  20.6 6.0 %collective-permute-start.5 = (bf16[144,512]{1,0:T(8,128)(2,1)S(1)}, bf16[144,512]{1,0:T(8,128)(2,1)S(1)}, u32[]{:S(2)}, u32[]{:S(2)}) collective-permute-start(bf16[144,512]{1,0:T(8,128)(2,1)S(1)} %collective-permute-done.3.refs_5_), channel_id=1, source_target_pairs={{0,4},{4,0},{8,12},{12,8},{1,5},{5,1},{9,13},{13,9},{2,6},{6,2},{1... | collective-permute-start | bytes 442376 | tf_op jit(solution)/shard_map/ppermute | solution.py:25
  21.1 7.1 %collective-permute-start.4 = (bf16[128,1024]{1,0:T(8,128)(2,1)S(1)}, bf16[128,1024]{1,0:T(8,128)(2,1)S(1)}, u32[]{:S(2)}, u32[]{:S(2)}) collective-permute-start(bf16[128,1024]{1,0:T(8,128)(2,1)S(1)} %collective-permute-done.2.refs_4_), channel_id=1, source_target_pairs={{0,4},{4,0},{8,12},{12,8},{1,5},{5,1},{9,13},{13,9},{2,6},{6,2},{1... | collective-permute-start | bytes 786440 | tf_op jit(solution)/shard_map/ppermute | solution.py:25
  25.4 0.7 %copy-start.1 = (bf16[128,1024]{1,0:T(8,128)(2,1)}, bf16[128,1024]{1,0:T(8,128)(2,1)S(1)}, u32[]{:S(2)}) copy-start(bf16[128,1024]{1,0:T(8,128)(2,1)S(1)} %collective-permute-done.13.outer_ref) | copy-start | bytes 786436
  26.1 2.1 %collective-permute-start.8 = (bf16[128,1024]{1,0:T(8,128)(2,1)S(1)}, bf16[128,1024]{1,0:T(8,128)(2,1)S(1)}, u32[]{:S(2)}, u32[]{:S(2)}) collective-permute-start(bf16[128,1024]{1,0:T(8,128)(2,1)S(1)} %collective-permute-done.6.refs_8_), channel_id=1, source_target_pairs={{0,4},{4,0},{8,12},{12,8},{1,5},{5,1},{9,13},{13,9},{2,6},{6,2},{1... | collective-permute-start | bytes 786440 | tf_op jit(solution)/shard_map/ppermute | solution.py:25
  26.1 4.4 %collective-permute-start.14 = (bf16[128,1024]{1,0:T(8,128)(2,1)S(1)}, bf16[128,1024]{1,0:T(8,128)(2,1)S(1)}, u32[]{:S(2)}, u32[]{:S(2)}) collective-permute-start(bf16[128,1024]{1,0:T(8,128)(2,1)S(1)} %collective-permute-done.10.refs_12_.refs_3_), channel_id=1, source_target_pairs={{0,4},{4,0},{8,12},{12,8},{1,5},{5,1},{9,13},{13,9},{2,6},{6,2},{1... | collective-permute-start | bytes 786440 | tf_op jit(solution)/shard_map/ppermute | solution.py:25
  26.6 1.6 %collective-permute-start.9 = (bf16[144,512]{1,0:T(8,128)(2,1)S(1)}, bf16[144,512]{1,0:T(8,128)(2,1)S(1)}, u32[]{:S(2)}, u32[]{:S(2)}) collective-permute-start(bf16[144,512]{1,0:T(8,128)(2,1)S(1)} %collective-permute-done.7.refs_9_), channel_id=1, source_target_pairs={{0,4},{4,0},{8,12},{12,8},{1,5},{5,1},{9,13},{13,9},{2,6},{6,2},{1... | collective-permute-start | bytes 442376 | tf_op jit(solution)/shard_map/ppermute | solution.py:25
  26.7 3.8 %collective-permute-start.15 = (bf16[144,512]{1,0:T(8,128)(2,1)S(1)}, bf16[144,512]{1,0:T(8,128)(2,1)S(1)}, u32[]{:S(2)}, u32[]{:S(2)}) collective-permute-start(bf16[144,512]{1,0:T(8,128)(2,1)S(1)} %collective-permute-done.12.refs_13_.refs_4_), channel_id=1, source_target_pairs={{0,4},{4,0},{8,12},{12,8},{1,5},{5,1},{9,13},{13,9},{2,6},{6,2},{1... | collective-permute-start | bytes 442376 | tf_op jit(solution)/shard_map/ppermute | solution.py:25
  28.2 1.0 %copy-start.2 = (bf16[128,1024]{1,0:T(8,128)(2,1)S(1)}, bf16[128,1024]{1,0:T(8,128)(2,1)}, u32[]{:S(2)}) copy-start(bf16[128,1024]{1,0:T(8,128)(2,1)} %copy-done.1) | copy-start | bytes 786436
  30.5 4.6 %copy-start.3 = (bf16[128,1024]{1,0:T(8,128)(2,1)S(1)}, bf16[128,1024]{1,0:T(8,128)(2,1)}, u32[]{:S(2)}) copy-start(bf16[128,1024]{1,0:T(8,128)(2,1)} %query_ref.1) | copy-start | bytes 786436
  31.5 7.9 %collective-permute-start.16 = (bf16[144,512]{1,0:T(8,128)(2,1)S(1)}, bf16[144,512]{1,0:T(8,128)(2,1)S(1)}, u32[]{:S(2)}, u32[]{:S(2)}) collective-permute-start(bf16[144,512]{1,0:T(8,128)(2,1)S(1)} %shard_map.67), channel_id=1, source_target_pairs={{0,3},{1,2},{2,1},{3,0},{4,7},{5,6},{6,5},{7,4},{8,11},{9,10},{10,... | collective-permute-start | bytes 442376 | tf_op jit(solution)/shard_map/ppermute | solution.py:25

commit v6 on v5

--- a/solution.py
+++ b/solution.py
@@ -23,12 +23,6 @@
 def swap(value, axis, mask):
     length = lax.axis_size(axis)
     return lax.ppermute(value, axis, [(i, i ^ mask) for i in range(length)])
-
-
-def swap_some(value, axis, mask, inner):
-    length = lax.axis_size(axis)
-    pairs = [(i, i ^ mask) for i in range(length) if (abs(i - (i ^ mask)) * 2 <= mask) == inner]
-    return lax.ppermute(value, axis, pairs)
 
 
 def tie(*values):
@@ -58,62 +52,32 @@
     packed_ref[TILE:, 0:TILE] = jnp.broadcast_to(row, (EXTRA, TILE)).astype(jnp.bfloat16)
 
 
-def bundle_kernel(*refs):
-    bundle_ref, at = refs[-1], 0
-    width = bundle_ref.shape[1]
-    for ref in refs[:-1]:
-        rows = ref.shape[0]
-        for column in range(0, ref.shape[1], width):
-            bundle_ref[at : at + rows, :] = ref[:, column : column + width]
-            at += rows
-
-
 class Piece:
-    def __init__(self, place, keys_ref=None, values_ref=None, bundle_ref=None, first_row=0):
+    def __init__(self, place, keys_ref, values_ref, copy=None):
         self.place = place
-        self.refs = (keys_ref, values_ref, bundle_ref)
-        self.first_row = first_row
+        self.refs = (keys_ref, values_ref)
+        self.copy = copy
 
     def scores(self, query_ref, inverse_root):
-        keys_ref, values_ref, bundle_ref = self.refs
-        width = query_ref.shape[1]
-        dims = (((1,), (1,)), ((), ()))
-        if bundle_ref is None:
-            product = lax.dot_general(query_ref[...], keys_ref[...], dims, preferred_element_type=jnp.float32)
-            scale = values_ref[TILE : TILE + EXTRA, 0:TILE]
-        else:
-            group = bundle_ref.shape[1]
-            product = 0.0
-            for at in range(width // group):
-                rows = pl.ds(self.first_row + at * TILE, TILE)
-                product = product + lax.dot_general(
-                    query_ref[:, at * group : (at + 1) * group],
-                    bundle_ref[rows, :],
-                    dims,
-                    preferred_element_type=jnp.float32,
-                )
-            scale = bundle_ref[pl.ds(self.first_row + width // group * TILE + TILE, EXTRA), 0:TILE]
+        keys_ref, values_ref = self.refs
+        product = lax.dot_general(
+            query_ref[...], keys_ref[...], (((1,), (1,)), ((), ())), preferred_element_type=jnp.float32
+        )
+        scale = values_ref[TILE : TILE + EXTRA, 0:TILE]
         return product * (scale.astype(jnp.float32)[0:1] * inverse_root)
 
-    def values(self, width):
-        keys_ref, values_ref, bundle_ref = self.refs
-        if bundle_ref is None:
-            return values_ref[0:TILE, :]
-        return bundle_ref[pl.ds(self.first_row + width // bundle_ref.shape[1] * TILE, TILE), :]
-
-
-def read_pieces(layout, width, refs):
-    pieces = []
-    for entry in layout:
-        if entry[0] == "pair":
-            pieces.append(Piece(entry[1], refs[0], refs[1]))
-            refs = refs[2:]
-        else:
-            for at, place in enumerate(entry[1]):
-                group = refs[0].shape[1]
-                rows = (width // group + 1) * TILE + EXTRA
-                pieces.append(Piece(place, bundle_ref=refs[0], first_row=at * rows))
-            refs = refs[1:]
+    def values(self):
+        return self.refs[1][0:TILE, :]
+
+
+def read_pieces(places, refs, own=None):
+    pieces = [Piece(place, refs[2 * at], refs[2 * at + 1]) for at, place in enumerate(places)]
+    refs = refs[2 * len(places) :]
+    if own is not None:
+        keys_ref, values_ref, *refs, held_ref, sem = refs
+        copy = pltpu.make_async_copy(keys_ref, held_ref, sem)
+        copy.start()
+        pieces.append(Piece((0, 0), held_ref, values_ref, copy))
     return pieces, refs
 
 
@@ -135,6 +99,8 @@
     flags = [active(*piece.place) for piece in pieces]
     score_ref[...] = jnp.full(score_ref.shape, MASKED_SCORE, jnp.float32)
     for at, (piece, flag) in enumerate(zip(pieces, flags)):
+        if piece.copy is not None:
+            piece.copy.wait()
 
         @pl.when(flag)
         def _(at=at, piece=piece):
@@ -164,7 +130,7 @@
             mass_ref[...] += weights
             weight_high = weights.astype(jnp.bfloat16)
             weight_low = (weights - weight_high.astype(jnp.float32)).astype(jnp.bfloat16)
-            values = piece.values(width)
+            values = piece.values()
             added = jnp.dot(weight_high, values, preferred_element_type=jnp.float32)
             added = added + jnp.dot(weight_low, values, preferred_element_type=jnp.float32)
             total_ref[...] += added
@@ -172,31 +138,16 @@
     return row_max
 
 
-def is_inner(mask):
-    index = lax.axis_index("qry")
-    return jnp.abs(index - lax.bitwise_xor(index, mask)) * 2 <= mask
-
-
-def early_kernel(layout, panel_mask, lists_ref, counts_ref, inner_ref, outer_ref, *refs):
-    pieces, refs = read_pieces(layout, inner_ref.shape[1], refs)
-    query_ref, total_ref, mass_ref, max_ref, score_ref = refs
-    inner = is_inner(panel_mask)
-
-    @pl.when(inner)
-    def _():
-        query_ref[...] = inner_ref[...]
-
-    @pl.when(jnp.logical_not(inner))
-    def _():
-        query_ref[...] = outer_ref[...]
-
+def early_kernel(places, panel_mask, lists_ref, counts_ref, query_ref, *refs):
+    pieces, refs = read_pieces(places, refs, own=True)
+    total_ref, mass_ref, max_ref, score_ref = refs
     row_max = attend(pieces, panel_mask, lists_ref, counts_ref, query_ref, score_ref, total_ref, mass_ref)
     max_ref[...] = jnp.broadcast_to(row_max, max_ref.shape)
 
 
-def late_kernel(layout, panel_mask, lists_ref, counts_ref, query_ref, *refs):
+def late_kernel(places, panel_mask, lists_ref, counts_ref, query_ref, *refs):
     before, refs = refs[:3], refs[3:]
-    pieces, refs = read_pieces(layout, query_ref.shape[1], refs)
+    pieces, refs = read_pieces(places, refs)
     packed_ref, score_ref, total_ref, mass_ref = refs
     row_max = attend(pieces, panel_mask, lists_ref, counts_ref, query_ref, score_ref, total_ref, mass_ref, before)
     row_sum = jnp.sum(mass_ref[...], axis=1, keepdims=True)
@@ -213,8 +164,8 @@
     packed_ref[TILE:, LANES:] = jnp.zeros((EXTRA, value_width - LANES), jnp.bfloat16)
 
 
-def home_kernel(layout, lists_ref, counts_ref, query_ref, *refs):
-    pieces, refs = read_pieces(layout, query_ref.shape[1], refs)
+def home_kernel(places, lists_ref, counts_ref, query_ref, *refs):
+    pieces, refs = read_pieces(places, refs, own=True)
     total_ref, stats_ref, score_ref, mass_ref = refs
     row_max = attend(pieces, 0, lists_ref, counts_ref, query_ref, score_ref, total_ref, mass_ref)
     row_sum = jnp.sum(mass_ref[...], axis=1, keepdims=True)
@@ -247,7 +198,7 @@
     places, arrays = [], []
     for (lib_mask, qry_mask), *pair in pieces:
         sent = tie(*pair, *arrivals)[:2]
-        places += [("pair", (lib_mask, qry_mask)), ("pair", (lib_mask | 1, qry_mask))]
+        places += [(lib_mask, qry_mask), (lib_mask | 1, qry_mask)]
         arrays += pair + [swap(array, "lib", 1) for array in sent]
     return places, arrays
 
@@ -258,27 +209,24 @@
     while mask > 1:
         steps.append(("lib", mask))
         mask //= 2
-    own_places = [("pair", (0, 0)), ("pair", (1, 0))]
-    own_arrays = [keys, values, partner_keys, swap(values, "lib", 1)]
-    nearer, _ = tie(queries, values)
-    inner = [swap_some(nearer, "qry", mask, True) for mask in masks]
+    own_places = [(1, 0)]
+    own_arrays = [partner_keys, swap(values, "lib", 1)]
+    leaving, _ = tie(queries, values)
+    visitors = [swap(leaving, "qry", mask) for mask in masks]
     early, late = [], []
     for axis, mask in steps:
         place = (0, mask) if axis == "qry" else (mask, 0)
         near = (place, swap(keys, axis, mask), swap(values, axis, mask))
         relayed = []
         for (lib_mask, qry_mask), far_keys, far_values in early + late:
-            far_keys, _ = tie(far_keys, near[1])
-            far_values, *_ = tie(far_values, near[2], *inner)
+            far_keys, far_values, *_ = tie(far_keys, far_values, *near[1:])
             place = (lib_mask | mask, qry_mask)
             relayed.append((place, swap(far_keys, axis, mask), swap(far_values, axis, mask)))
         early, late = early + late + [near], relayed
-    farther, *_ = tie(queries, *early[0][1:])
-    outer = [swap_some(farther, "qry", mask, False) for mask in masks]
     early_places, early_arrays = both_cores(early)
-    late_places, late_arrays = both_cores(late, outer)
+    late_places, late_arrays = both_cores(late, visitors)
     early = (own_places + early_places, own_arrays + early_arrays)
-    return early, (late_places, late_arrays), list(zip(masks, inner, outer))
+    return early, (late_places, late_arrays), list(zip(masks, visitors))
 
 
 def body(queries, library_keys, library_values, key_scale, block_list, block_count):
@@ -302,29 +250,25 @@
         library_keys, partner_keys, values, queries, masks
     )
     piece_rows = (width // value_width + 1) * TILE + EXTRA
-    count_early, count_late = len(early_places), len(late_places)
+    count_early, count_late = len(early_places) + 1, len(late_places)
 
     cost = pl.CostEstimate(flops=2 * TILE * 4 * TILE * width * 2, bytes_accessed=4 * 1024 * 1024, transcendentals=0)
     total_shape = jax.ShapeDtypeStruct((TILE, value_width), jnp.float32)
     line_shape = jax.ShapeDtypeStruct((TILE, LANES), jnp.float32)
     attend_params = params((count_early + count_late) * piece_rows * value_width * 2)
+    own_specs = [pl.BlockSpec(memory_space=pl.ANY), VMEM]
+    own_scratch = [pltpu.VMEM(library_keys.shape, library_keys.dtype), pltpu.SemaphoreType.DMA]
     returned = []
-    for mask, inner_queries, outer_queries in visitors:
+    for mask, visiting in visitors:
         *state, = pl.pallas_call(
             functools.partial(early_kernel, early_places, mask),
-            out_shape=(jax.ShapeDtypeStruct(queries.shape, queries.dtype), total_shape, line_shape, line_shape),
-            in_specs=[SMEM, SMEM] + [VMEM] * (2 + len(early_arrays)),
-            out_specs=(VMEM,) * 4,
-            scratch_shapes=[pltpu.VMEM((count_early, TILE, TILE), jnp.float32)],
+            out_shape=(total_shape, line_shape, line_shape),
+            in_specs=[SMEM, SMEM] + [VMEM] * (1 + len(early_arrays)) + own_specs,
+            out_specs=(VMEM,) * 3,
+            scratch_shapes=[pltpu.VMEM((count_early, TILE, TILE), jnp.float32)] + own_scratch,
             compiler_params=attend_params,
             cost_estimate=cost,
-        )(
-            block_list,
-            block_count,
-            inner_queries,
-            outer_queries,
-            *early_arrays,
-        )
+        )(block_list, block_count, visiting, *early_arrays, library_keys, values)
         packed = pl.pallas_call(
             functools.partial(late_kernel, late_places, mask),
             out_shape=jax.ShapeDtypeStruct((TILE + EXTRA, value_width), jnp.bfloat16),
@@ -337,21 +281,22 @@
             ],
             compiler_params=attend_params,
             cost_estimate=cost,
-        )(block_list, block_count, *state, *late_arrays)
+        )(block_list, block_count, visiting, *state, *late_arrays)
         returned.append(swap(packed, "qry", mask))
 
     total, stats = pl.pallas_call(
         functools.partial(home_kernel, early_places + late_places),
         out_shape=(total_shape, jax.ShapeDtypeStruct((2, TILE, LANES), jnp.float32)),
-        in_specs=[SMEM, SMEM] + [VMEM] * (1 + len(early_arrays) + len(late_arrays)),
+        in_specs=[SMEM, SMEM] + [VMEM] * (1 + len(early_arrays) + len(late_arrays)) + own_specs,
         out_specs=(VMEM, VMEM),
         scratch_shapes=[
             pltpu.VMEM((count_early + count_late, TILE, TILE), jnp.float32),
             pltpu.VMEM((TILE, TILE), jnp.float32),
-        ],
+        ]
+        + own_scratch,
         compiler_params=attend_params,
         cost_estimate=cost,
-    )(block_list, block_count, queries, *early_arrays, *late_arrays)
+    )(block_list, block_count, queries, *early_arrays, *late_arrays, library_keys, values)
 
     return pl.pallas_call(
         merge_kernel,

time: 40.6 us -> 40.5 us (level)
  waiting for transfers between devices: 11.3 us -> 16.4 us
  starting transfers between devices: 20.3 us -> 18 us
  local copies, waits for them, and re-layouts: 3.31 us -> 1.66 us
  Pallas kernels: 5.11 us -> 4.32 us
    ppermute x15 -> x16, waiting for transfers between devices: 7.11 us -> 16.4 us  [swap(): return lax.ppermute(value, axis, [(i, i ^ mask) for i in range(length)])]
    ppermute x2 -> x0, starting transfers between devices: 5.76 us -> none  [swap_some(): return lax.ppermute(value, axis, pairs)]
    ppermute x2 -> x0, waiting for transfers between devices: 4.23 us -> none  [swap_some(): return lax.ppermute(value, axis, pairs)]
    ppermute x15 -> x16, starting transfers between devices: 14.6 us -> 18 us  [swap(): return lax.ppermute(value, axis, [(i, i ^ mask) for i in range(length)])]
    unnamed x17 -> x13, local copies, waits for them, and re-layouts: 3.31 us -> 1.66 us
    pallas_call x1, Pallas kernels: 1.82 us -> 0.98 us  [body(): pl.pallas_call(functools.partial(home_kernel, early_places + late_places)...]
    pallas_call x1, Pallas kernels: 0.99 us -> 1.49 us  [body(): pl.pallas_call(functools.partial(late_kernel, late_places, mask), out_sha...]
    pallas_call x1, Pallas kernels: 1.31 us -> 0.87 us  [body(): pl.pallas_call(functools.partial(early_kernel, early_places, mask), out_s...]
  transfers between devices with their start and end apart: 17 -> 16, of which waited for: 5 -> 7; matrix products, arithmetic and copies ran while one was open for 0% -> 0% of each run, Pallas kernels for 8% -> 5%
where the time goes in v6:
time: 40.5 us; the launch traced here: 40.4 us
  starting transfers between devices  18 us (44%)
  waiting for transfers between devices  16.4 us (40%)
  Pallas kernels  4.32 us (11%)
  local copies, waits for them, and re-layouts  1.66 us (4%)
    ppermute x16, starting transfers between devices, swap(): return lax.ppermute(value, axis, [(i, i ^ mask) for i in range(length)])  18 us
    ppermute x16, waiting for transfers between devices, swap(): return lax.ppermute(value, axis, [(i, i ^ mask) for i in range(length)])  16.4 us
    unnamed x13, local copies, waits for them, and re-layouts  1.66 us
    pallas_call x1, Pallas kernels, body(): pl.pallas_call(functools.partial(late_kernel, late_places, mask), out_sha...  1.49 us
    pallas_call x1, Pallas kernels, body(): pl.pallas_call(functools.partial(home_kernel, early_places + late_places)...  0.98 us
    pallas_call x1, Pallas kernels, body(): pl.pallas_call(functools.partial(early_kernel, early_places, mask), out_s...  0.87 us
    pallas_call x1, Pallas kernels, body(): pl.pallas_call(merge_kernel, out_shape=jax.ShapeDtypeStruct((TILE, value_...  0.81 us
  transfers between devices with their start and end apart: 16, of which 7 were waited for; matrix products, arithmetic and copies ran while one was open for 0% of the time, Pallas kernels for 5%

profile of v6, /device:TPU:0, one launch (start us, length us, event | category | flops | bytes accessed | tf_op | source)
XLA Modules:
  0.0 40.4 jit_solution(1350613456867792805)
XLA Ops:
  0.0 0.5 %collective-permute-start = (bf16[128,1024]{1,0:T(8,128)(2,1)}, bf16[128,1024]{1,0:T(8,128)(2,1)S(1)}, u32[]{:S(2)}, u32[]{:S(2)}) collective-permute-start(bf16[128,1024]{1,0:T(8,128)(2,1)} %refs_10_.1), channel_id=1, source_target_pairs={{0,4},{4,0},{8,12},{12,8},{1,5},{5,1},{9,13},{13,9},{2,6},{6,2},{1... | collective-permute-start | bytes 786440 | tf_op jit(solution)/shard_map/ppermute | solution.py:25
  0.5 2.6 %collective-permute-start.2 = (bf16[128,1024]{1,0:T(8,128)(2,1)}, bf16[128,1024]{1,0:T(8,128)(2,1)S(1)}, u32[]{:S(2)}, u32[]{:S(2)}) collective-permute-start(bf16[128,1024]{1,0:T(8,128)(2,1)} %refs_10_.1), channel_id=1, source_target_pairs={{0,1},{1,0},{2,3},{3,2},{4,5},{5,4},{6,7},{7,6},{8,9},{9,8},{10,11... | collective-permute-start | bytes 786440 | tf_op jit(solution)/shard_map/ppermute | solution.py:25
  3.1 1.5 %collective-permute-start.6 = (bf16[128,1024]{1,0:T(8,128)(2,1)}, bf16[128,1024]{1,0:T(8,128)(2,1)S(1)}, u32[]{:S(2)}, u32[]{:S(2)}) collective-permute-start(bf16[128,1024]{1,0:T(8,128)(2,1)} %refs_10_.1), channel_id=1, source_target_pairs={{0,8},{4,12},{8,0},{12,4},{1,9},{5,13},{9,1},{13,5},{2,10},{6,14},... | collective-permute-start | bytes 786440 | tf_op jit(solution)/shard_map/ppermute | solution.py:25
  4.6 0.9 %copy-done.2 = bf16[128,512]{1,0:T(8,128)(2,1)S(1)} copy-done((bf16[128,512]{1,0:T(8,128)(2,1)S(1)}, bf16[128,512]{1,0:T(8,128)(2,1)}, u32[]{:S(2)}) %copy-start.2) | copy-done | bytes 131096
  5.5 0.7 %copy-done.4 = bf16[128]{0:T(256)(128)(2,1)S(1)} copy-done((bf16[128]{0:T(256)(128)(2,1)S(1)}, bf16[128]{0:T(256)(128)(2,1)}, u32[]{:S(2)}) %copy-start.4) | copy-done | bytes 280
  6.1 0.2 shard_map.64.refs_15_.refs_11_
  6.3 0.0 copy-start.3
  6.3 0.5 %collective-permute-start.3 = (bf16[144,512]{1,0:T(8,128)(2,1)S(1)}, bf16[144,512]{1,0:T(8,128)(2,1)S(1)}, u32[]{:S(2)}, u32[]{:S(2)}) collective-permute-start(bf16[144,512]{1,0:T(8,128)(2,1)S(1)} %shard_map.64.refs_15_.refs_11_), channel_id=1, source_target_pairs={{0,1},{1,0},{2,3},{3,2},{4,5},{5,4},{6,7},{7,6},{8,9},{9,8},{10,11... | collective-permute-start | bytes 442376 | tf_op jit(solution)/shard_map/ppermute | solution.py:25
  6.9 1.2 %collective-permute-start.7 = (bf16[144,512]{1,0:T(8,128)(2,1)S(1)}, bf16[144,512]{1,0:T(8,128)(2,1)S(1)}, u32[]{:S(2)}, u32[]{:S(2)}) collective-permute-start(bf16[144,512]{1,0:T(8,128)(2,1)S(1)} %shard_map.64.refs_15_.refs_11_), channel_id=1, source_target_pairs={{0,8},{4,12},{8,0},{12,4},{1,9},{5,13},{9,1},{13,5},{2,10},{6,14},... | collective-permute-start | bytes 442376 | tf_op jit(solution)/shard_map/ppermute | solution.py:25
  8.1 2.9 %collective-permute-start.12 = (bf16[128,1024]{1,0:T(8,128)(2,1)}, bf16[128,1024]{1,0:T(8,128)(2,1)S(1)}, u32[]{:S(2)}, u32[]{:S(2)}) collective-permute-start(bf16[128,1024]{1,0:T(8,128)(2,1)} %query_ref.1), channel_id=1, source_target_pairs={{0,3},{1,2},{2,1},{3,0},{4,7},{5,6},{6,5},{7,4},{8,11},{9,10},{10,... | collective-permute-start | bytes 786440 | tf_op jit(solution)/shard_map/ppermute | solution.py:25
  11.0 1.5 %collective-permute-done.6.refs_6_ = bf16[128,1024]{1,0:T(8,128)(2,1)S(1)} collective-permute-done((bf16[128,1024]{1,0:T(8,128)(2,1)}, bf16[128,1024]{1,0:T(8,128)(2,1)S(1)}, u32[]{:S(2)}, u32[]{:S(2)}) %collective-permute-start.6) | collective-permute-done | bytes 262176 | tf_op jit(solution)/shard_map/ppermute | solution.py:25
  12.5 0.9 %collective-permute-done.3.refs_3_ = bf16[144,512]{1,0:T(8,128)(2,1)S(1)} collective-permute-done((bf16[144,512]{1,0:T(8,128)(2,1)S(1)}, bf16[144,512]{1,0:T(8,128)(2,1)S(1)}, u32[]{:S(2)}, u32[]{:S(2)}) %collective-permute-start.3) | collective-permute-done | bytes 147488 | tf_op jit(solution)/shard_map/ppermute | solution.py:25
  13.4 1.5 %collective-permute-done.7.refs_7_ = bf16[144,512]{1,0:T(8,128)(2,1)S(1)} collective-permute-done((bf16[144,512]{1,0:T(8,128)(2,1)S(1)}, bf16[144,512]{1,0:T(8,128)(2,1)S(1)}, u32[]{:S(2)}, u32[]{:S(2)}) %collective-permute-start.7) | collective-permute-done | bytes 147488 | tf_op jit(solution)/shard_map/ppermute | solution.py:25
  14.8 1.5 %collective-permute-start.10 = (bf16[128,1024]{1,0:T(8,128)(2,1)S(1)}, bf16[128,1024]{1,0:T(8,128)(2,1)S(1)}, u32[]{:S(2)}, u32[]{:S(2)}) collective-permute-start(bf16[128,1024]{1,0:T(8,128)(2,1)S(1)} %collective-permute-done.2.refs_2_), channel_id=1, source_target_pairs={{0,8},{4,12},{8,0},{12,4},{1,9},{5,13},{9,1},{13,5},{2,10},{6,14},... | collective-permute-start | bytes 786440 | tf_op jit(solution)/shard_map/ppermute | solution.py:25
  16.3 0.5 %collective-permute-start.11 = (bf16[144,512]{1,0:T(8,128)(2,1)S(1)}, bf16[144,512]{1,0:T(8,128)(2,1)S(1)}, u32[]{:S(2)}, u32[]{:S(2)}) collective-permute-start(bf16[144,512]{1,0:T(8,128)(2,1)S(1)} %collective-permute-done.3.refs_3_), channel_id=1, source_target_pairs={{0,8},{4,12},{8,0},{12,4},{1,9},{5,13},{9,1},{13,5},{2,10},{6,14},... | collective-permute-start | bytes 442376 | tf_op jit(solution)/shard_map/ppermute | solution.py:25
  16.9 0.0 collective-permute-start.1
  16.9 0.5 %collective-permute-start.5 = (bf16[144,512]{1,0:T(8,128)(2,1)S(1)}, bf16[144,512]{1,0:T(8,128)(2,1)S(1)}, u32[]{:S(2)}, u32[]{:S(2)}) collective-permute-start(bf16[144,512]{1,0:T(8,128)(2,1)S(1)} %collective-permute-done.3.refs_3_), channel_id=1, source_target_pairs={{0,4},{4,0},{8,12},{12,8},{1,5},{5,1},{9,13},{13,9},{2,6},{6,2},{1... | collective-permute-start | bytes 442376 | tf_op jit(solution)/shard_map/ppermute | solution.py:25
  17.4 3.9 %collective-permute-done.12.query_ref = bf16[128,1024]{1,0:T(8,128)(2,1)S(1)} collective-permute-done((bf16[128,1024]{1,0:T(8,128)(2,1)}, bf16[128,1024]{1,0:T(8,128)(2,1)S(1)}, u32[]{:S(2)}, u32[]{:S(2)}) %collective-permute-start.12) | collective-permute-done | bytes 262176 | tf_op jit(solution)/shard_map/ppermute | solution.py:25
  21.3 4.2 %collective-permute-done.11.refs_11_.refs_4_ = bf16[144,512]{1,0:T(8,128)(2,1)S(1)} collective-permute-done((bf16[144,512]{1,0:T(8,128)(2,1)S(1)}, bf16[144,512]{1,0:T(8,128)(2,1)S(1)}, u32[]{:S(2)}, u32[]{:S(2)}) %collective-permute-start.11) | collective-permute-done | bytes 147488 | tf_op jit(solution)/shard_map/ppermute | solution.py:25
  25.6 0.5 %collective-permute-start.13 = (bf16[128,1024]{1,0:T(8,128)(2,1)S(1)}, bf16[128,1024]{1,0:T(8,128)(2,1)S(1)}, u32[]{:S(2)}, u32[]{:S(2)}) collective-permute-start(bf16[128,1024]{1,0:T(8,128)(2,1)S(1)} %collective-permute-done.10.refs_10_.refs_3_), channel_id=1, source_target_pairs={{0,4},{4,0},{8,12},{12,8},{1,5},{5,1},{9,13},{13,9},{2,6},{6,2},{1... | collective-permute-start | bytes 786440 | tf_op jit(solution)/shard_map/ppermute | solution.py:25
  26.1 0.1 collective-permute-start.9
  26.1 0.4 %collective-permute-start.14 = (bf16[144,512]{1,0:T(8,128)(2,1)S(1)}, bf16[144,512]{1,0:T(8,128)(2,1)S(1)}, u32[]{:S(2)}, u32[]{:S(2)}) collective-permute-start(bf16[144,512]{1,0:T(8,128)(2,1)S(1)} %collective-permute-done.11.refs_11_.refs_4_), channel_id=1, source_target_pairs={{0,4},{4,0},{8,12},{12,8},{1,5},{5,1},{9,13},{13,9},{2,6},{6,2},{1... | collective-permute-start | bytes 442376 | tf_op jit(solution)/shard_map/ppermute | solution.py:25
  26.6 0.1 copy.7.lists_ref
  26.7 1.0 %collective-permute-done.9.refs_9_ = bf16[144,512]{1,0:T(8,128)(2,1)S(1)} collective-permute-done((bf16[144,512]{1,0:T(8,128)(2,1)S(1)}, bf16[144,512]{1,0:T(8,128)(2,1)S(1)}, u32[]{:S(2)}, u32[]{:S(2)}) %collective-permute-start.9) | collective-permute-done | bytes 147488 | tf_op jit(solution)/shard_map/ppermute | solution.py:25
  27.7 0.0 collective-permute-done.4.refs_4_
  27.7 0.9 %shard_map.66 = (f32[128,512]{1,0:T(8,128)S(1)}, f32[128,128]{1,0:T(8,128)S(1)}, f32[128,128]{1,0:T(8,128)S(1)}) custom-call(s32[16,4]{1,0:T(8,128)S(1)} %copy.7.lists_ref, s32[16]{0:T(128)S(1)} %copy-done.3, bf16[128,1024]{1,0:T(8,128)(2,1)S(1)} %collective-permute-done.12.query_ref, bf16[128,1024]{1,0:T(8,128)(2,1)S(1)} %collective-permute-done.refs_0_, ...), custom_call_target="tpu_custom_call" | custom-call | flops 268435456 | bytes 4194304 | tf_op jit(solution)/shard_map/pallas_call | solution.py:263
  28.6 0.0 copy-start.1
  28.6 1.5 %shard_map.67 = bf16[144,512]{1,0:T(8,128)(2,1)S(1)} custom-call(s32[16,4]{1,0:T(8,128)S(1)} %copy.7.lists_ref, s32[16]{0:T(128)S(1)} %copy-done.3, bf16[128,1024]{1,0:T(8,128)(2,1)S(1)} %collective-permute-done.12.query_ref, f32[128,512]{1,0:T(8,128)S(1)} %get-tuple-element.32.refs_0_, f32[128,128]{1,0:T(8,128)S(1)} %get-tuple-element.33.refs_1_, ...), custom_call_target="tpu_custom_call" | custom-call | flops 268435456 | bytes 4194304 | tf_op jit(solution)/shard_map/pallas_call | solution.py:272
  30.1 5.2 %collective-permute-start.15 = (bf16[144,512]{1,0:T(8,128)(2,1)S(1)}, bf16[144,512]{1,0:T(8,128)(2,1)S(1)}, u32[]{:S(2)}, u32[]{:S(2)}) collective-permute-start(bf16[144,512]{1,0:T(8,128)(2,1)S(1)} %shard_map.67), channel_id=1, source_target_pairs={{0,3},{1,2},{2,1},{3,0},{4,7},{5,6},{6,5},{7,4},{8,11},{9,10},{10,... | collective-permute-start | bytes 442376 | tf_op jit(solution)/shard_map/ppermute | solution.py:25
  35.3 1.0 %shard_map.65 = (f32[128,512]{1,0:T(8,128)S(1)}, f32[2,128,128]{2,1,0:T(8,128)S(1)}) custom-call(s32[16,4]{1,0:T(8,128)S(1)} %copy.7.lists_ref, s32[16]{0:T(128)S(1)} %copy-done.3, bf16[128,1024]{1,0:T(8,128)(2,1)S(1)} %copy-done.1, bf16[128,1024]{1,0:T(8,128)(2,1)S(1)} %collective-permute-done.refs_0_, bf16[144,512]{1,0:T(8,128)(2,1)S(1)} %collective-permute-done.1.refs_1_, ...), custom_call_target="tpu_custom_call" | custom-call | flops 268435456 | bytes 4194304 | tf_op jit(solution)/shard_map/pallas_call | solution.py:287
  36.3 3.3 %collective-permute-done.15.refs_0_ = bf16[144,512]{1,0:T(8,128)(2,1)S(1)} collective-permute-done((bf16[144,512]{1,0:T(8,128)(2,1)S(1)}, bf16[144,512]{1,0:T(8,128)(2,1)S(1)}, u32[]{:S(2)}, u32[]{:S(2)}) %collective-permute-start.15) | collective-permute-done | bytes 147488 | tf_op jit(solution)/shard_map/ppermute | solution.py:25
  39.6 0.8 %shard_map.68 = bf16[128,512]{1,0:T(8,128)(2,1)} custom-call(f32[128,512]{1,0:T(8,128)S(1)} %get-tuple-element.30.total_ref, f32[2,128,128]{2,1,0:T(8,128)S(1)} %get-tuple-element.31.stats_ref, bf16[144,512]{1,0:T(8,128)(2,1)S(1)} %collective-permute-done.15.refs_0_), custom_call_target="tpu_custom_call" | custom-call | tf_op jit(solution)/shard_map/pallas_call | solution.py:301
  (18 shorter events, 0.0 us)
Async XLA Ops:
  0.0 27.7 %copy-start = (bf16[128,1024]{1,0:T(8,128)(2,1)S(1)}, bf16[128,1024]{1,0:T(8,128)(2,1)}, u32[]{:S(2)}) copy-start(bf16[128,1024]{1,0:T(8,128)(2,1)} %refs_10_.1) | copy-start | bytes 786436
  0.0 4.6 %collective-permute-start = (bf16[128,1024]{1,0:T(8,128)(2,1)}, bf16[128,1024]{1,0:T(8,128)(2,1)S(1)}, u32[]{:S(2)}, u32[]{:S(2)}) collective-permute-start(bf16[128,1024]{1,0:T(8,128)(2,1)} %refs_10_.1), channel_id=1, source_target_pairs={{0,4},{4,0},{8,12},{12,8},{1,5},{5,1},{9,13},{13,9},{2,6},{6,2},{1... | collective-permute-start | bytes 786440 | tf_op jit(solution)/shard_map/ppermute | solution.py:25
  0.5 10.5 %collective-permute-start.2 = (bf16[128,1024]{1,0:T(8,128)(2,1)}, bf16[128,1024]{1,0:T(8,128)(2,1)S(1)}, u32[]{:S(2)}, u32[]{:S(2)}) collective-permute-start(bf16[128,1024]{1,0:T(8,128)(2,1)} %refs_10_.1), channel_id=1, source_target_pairs={{0,1},{1,0},{2,3},{3,2},{4,5},{5,4},{6,7},{7,6},{8,9},{9,8},{10,11... | collective-permute-start | bytes 786440 | tf_op jit(solution)/shard_map/ppermute | solution.py:25
  3.1 9.4 %collective-permute-start.6 = (bf16[128,1024]{1,0:T(8,128)(2,1)}, bf16[128,1024]{1,0:T(8,128)(2,1)S(1)}, u32[]{:S(2)}, u32[]{:S(2)}) collective-permute-start(bf16[128,1024]{1,0:T(8,128)(2,1)} %refs_10_.1), channel_id=1, source_target_pairs={{0,8},{4,12},{8,0},{12,4},{1,9},{5,13},{9,1},{13,5},{2,10},{6,14},... | collective-permute-start | bytes 786440 | tf_op jit(solution)/shard_map/ppermute | solution.py:25
  4.6 0.9 %copy-start.2 = (bf16[128,512]{1,0:T(8,128)(2,1)S(1)}, bf16[128,512]{1,0:T(8,128)(2,1)}, u32[]{:S(2)}) copy-start(bf16[128,512]{1,0:T(8,128)(2,1)} %values_ref) | copy-start | bytes 393220
  5.5 0.7 %copy-start.4 = (bf16[128]{0:T(256)(128)(2,1)S(1)}, bf16[128]{0:T(256)(128)(2,1)}, u32[]{:S(2)}) copy-start(bf16[128]{0:T(256)(128)(2,1)} %param.9) | copy-start | bytes 772
  6.1 20.4 %copy-start.5 = (s32[16,4]{0,1:T(4,128)S(1)}, s32[16,4]{0,1:T(4,128)}, u32[]{:S(2)}) copy-start(s32[16,4]{0,1:T(4,128)} %param.10) | copy-start | bytes 772
  6.3 21.4 %copy-start.3 = (s32[16]{0:T(128)S(1)}, s32[16]{0:T(128)}, u32[]{:S(2)}) copy-start(s32[16]{0:T(128)} %counts_ref.5) | copy-start | bytes 196
  6.3 7.0 %collective-permute-start.3 = (bf16[144,512]{1,0:T(8,128)(2,1)S(1)}, bf16[144,512]{1,0:T(8,128)(2,1)S(1)}, u32[]{:S(2)}, u32[]{:S(2)}) collective-permute-start(bf16[144,512]{1,0:T(8,128)(2,1)S(1)} %shard_map.64.refs_15_.refs_11_), channel_id=1, source_target_pairs={{0,1},{1,0},{2,3},{3,2},{4,5},{5,4},{6,7},{7,6},{8,9},{9,8},{10,11... | collective-permute-start | bytes 442376 | tf_op jit(solution)/shard_map/ppermute | solution.py:25
  6.9 8.0 %collective-permute-start.7 = (bf16[144,512]{1,0:T(8,128)(2,1)S(1)}, bf16[144,512]{1,0:T(8,128)(2,1)S(1)}, u32[]{:S(2)}, u32[]{:S(2)}) collective-permute-start(bf16[144,512]{1,0:T(8,128)(2,1)S(1)} %shard_map.64.refs_15_.refs_11_), channel_id=1, source_target_pairs={{0,8},{4,12},{8,0},{12,4},{1,9},{5,13},{9,1},{13,5},{2,10},{6,14},... | collective-permute-start | bytes 442376 | tf_op jit(solution)/shard_map/ppermute | solution.py:25
  8.1 13.2 %collective-permute-start.12 = (bf16[128,1024]{1,0:T(8,128)(2,1)}, bf16[128,1024]{1,0:T(8,128)(2,1)S(1)}, u32[]{:S(2)}, u32[]{:S(2)}) collective-permute-start(bf16[128,1024]{1,0:T(8,128)(2,1)} %query_ref.1), channel_id=1, source_target_pairs={{0,3},{1,2},{2,1},{3,0},{4,7},{5,6},{6,5},{7,4},{8,11},{9,10},{10,... | collective-permute-start | bytes 786440 | tf_op jit(solution)/shard_map/ppermute | solution.py:25
  14.8 10.7 %collective-permute-start.10 = (bf16[128,1024]{1,0:T(8,128)(2,1)S(1)}, bf16[128,1024]{1,0:T(8,128)(2,1)S(1)}, u32[]{:S(2)}, u32[]{:S(2)}) collective-permute-start(bf16[128,1024]{1,0:T(8,128)(2,1)S(1)} %collective-permute-done.2.refs_2_), channel_id=1, source_target_pairs={{0,8},{4,12},{8,0},{12,4},{1,9},{5,13},{9,1},{13,5},{2,10},{6,14},... | collective-permute-start | bytes 786440 | tf_op jit(solution)/shard_map/ppermute | solution.py:25
  16.3 9.2 %collective-permute-start.11 = (bf16[144,512]{1,0:T(8,128)(2,1)S(1)}, bf16[144,512]{1,0:T(8,128)(2,1)S(1)}, u32[]{:S(2)}, u32[]{:S(2)}) collective-permute-start(bf16[144,512]{1,0:T(8,128)(2,1)S(1)} %collective-permute-done.3.refs_3_), channel_id=1, source_target_pairs={{0,8},{4,12},{8,0},{12,4},{1,9},{5,13},{9,1},{13,5},{2,10},{6,14},... | collective-permute-start | bytes 442376 | tf_op jit(solution)/shard_map/ppermute | solution.py:25
  16.9 9.2 %collective-permute-start.1 = (bf16[144,512]{1,0:T(8,128)(2,1)S(1)}, bf16[144,512]{1,0:T(8,128)(2,1)S(1)}, u32[]{:S(2)}, u32[]{:S(2)}) collective-permute-start(bf16[144,512]{1,0:T(8,128)(2,1)S(1)} %shard_map.64.refs_15_.refs_11_), channel_id=1, source_target_pairs={{0,4},{4,0},{8,12},{12,8},{1,5},{5,1},{9,13},{13,9},{2,6},{6,2},{1... | collective-permute-start | bytes 442376 | tf_op jit(solution)/shard_map/ppermute | solution.py:25
  16.9 9.3 %collective-permute-start.5 = (bf16[144,512]{1,0:T(8,128)(2,1)S(1)}, bf16[144,512]{1,0:T(8,128)(2,1)S(1)}, u32[]{:S(2)}, u32[]{:S(2)}) collective-permute-start(bf16[144,512]{1,0:T(8,128)(2,1)S(1)} %collective-permute-done.3.refs_3_), channel_id=1, source_target_pairs={{0,4},{4,0},{8,12},{12,8},{1,5},{5,1},{9,13},{13,9},{2,6},{6,2},{1... | collective-permute-start | bytes 442376 | tf_op jit(solution)/shard_map/ppermute | solution.py:25
  21.3 6.4 %collective-permute-start.4 = (bf16[128,1024]{1,0:T(8,128)(2,1)S(1)}, bf16[128,1024]{1,0:T(8,128)(2,1)S(1)}, u32[]{:S(2)}, u32[]{:S(2)}) collective-permute-start(bf16[128,1024]{1,0:T(8,128)(2,1)S(1)} %collective-permute-done.2.refs_2_), channel_id=1, source_target_pairs={{0,4},{4,0},{8,12},{12,8},{1,5},{5,1},{9,13},{13,9},{2,6},{6,2},{1... | collective-permute-start | bytes 786440 | tf_op jit(solution)/shard_map/ppermute | solution.py:25
  25.5 2.1 %collective-permute-start.8 = (bf16[128,1024]{1,0:T(8,128)(2,1)S(1)}, bf16[128,1024]{1,0:T(8,128)(2,1)S(1)}, u32[]{:S(2)}, u32[]{:S(2)}) collective-permute-start(bf16[128,1024]{1,0:T(8,128)(2,1)S(1)} %collective-permute-done.6.refs_6_), channel_id=1, source_target_pairs={{0,4},{4,0},{8,12},{12,8},{1,5},{5,1},{9,13},{13,9},{2,6},{6,2},{1... | collective-permute-start | bytes 786440 | tf_op jit(solution)/shard_map/ppermute | solution.py:25
  25.6 3.0 %collective-permute-start.13 = (bf16[128,1024]{1,0:T(8,128)(2,1)S(1)}, bf16[128,1024]{1,0:T(8,128)(2,1)S(1)}, u32[]{:S(2)}, u32[]{:S(2)}) collective-permute-start(bf16[128,1024]{1,0:T(8,128)(2,1)S(1)} %collective-permute-done.10.refs_10_.refs_3_), channel_id=1, source_target_pairs={{0,4},{4,0},{8,12},{12,8},{1,5},{5,1},{9,13},{13,9},{2,6},{6,2},{1... | collective-permute-start | bytes 786440 | tf_op jit(solution)/shard_map/ppermute | solution.py:25
  26.1 1.6 %collective-permute-start.9 = (bf16[144,512]{1,0:T(8,128)(2,1)S(1)}, bf16[144,512]{1,0:T(8,128)(2,1)S(1)}, u32[]{:S(2)}, u32[]{:S(2)}) collective-permute-start(bf16[144,512]{1,0:T(8,128)(2,1)S(1)} %collective-permute-done.7.refs_7_), channel_id=1, source_target_pairs={{0,4},{4,0},{8,12},{12,8},{1,5},{5,1},{9,13},{13,9},{2,6},{6,2},{1... | collective-permute-start | bytes 442376 | tf_op jit(solution)/shard_map/ppermute | solution.py:25
  26.1 2.4 %collective-permute-start.14 = (bf16[144,512]{1,0:T(8,128)(2,1)S(1)}, bf16[144,512]{1,0:T(8,128)(2,1)S(1)}, u32[]{:S(2)}, u32[]{:S(2)}) collective-permute-start(bf16[144,512]{1,0:T(8,128)(2,1)S(1)} %collective-permute-done.11.refs_11_.refs_4_), channel_id=1, source_target_pairs={{0,4},{4,0},{8,12},{12,8},{1,5},{5,1},{9,13},{13,9},{2,6},{6,2},{1... | collective-permute-start | bytes 442376 | tf_op jit(solution)/shard_map/ppermute | solution.py:25
  28.6 6.7 %copy-start.1 = (bf16[128,1024]{1,0:T(8,128)(2,1)S(1)}, bf16[128,1024]{1,0:T(8,128)(2,1)}, u32[]{:S(2)}) copy-start(bf16[128,1024]{1,0:T(8,128)(2,1)} %query_ref.1) | copy-start | bytes 786436
  30.1 9.5 %collective-permute-start.15 = (bf16[144,512]{1,0:T(8,128)(2,1)S(1)}, bf16[144,512]{1,0:T(8,128)(2,1)S(1)}, u32[]{:S(2)}, u32[]{:S(2)}) collective-permute-start(bf16[144,512]{1,0:T(8,128)(2,1)S(1)} %shard_map.67), channel_id=1, source_target_pairs={{0,3},{1,2},{2,1},{3,0},{4,7},{5,6},{6,5},{7,4},{8,11},{9,10},{10,... | collective-permute-start | bytes 442376 | tf_op jit(solution)/shard_map/ppermute | solution.py:25

commit v7 on v6

--- a/solution.py
+++ b/solution.py
@@ -194,23 +194,12 @@
         out_ref[:, at : at + LANES] = merged.astype(jnp.bfloat16)
 
 
-def both_cores(pieces, arrivals=()):
-    places, arrays = [], []
-    for (lib_mask, qry_mask), *pair in pieces:
-        sent = tie(*pair, *arrivals)[:2]
-        places += [(lib_mask, qry_mask), (lib_mask | 1, qry_mask)]
-        arrays += pair + [swap(array, "lib", 1) for array in sent]
-    return places, arrays
-
-
-def gather_library(keys, partner_keys, values, queries, masks):
+def gather_library(keys, values, queries, masks):
     steps = [("qry", 1)]
     mask = lax.axis_size("lib") // 2
     while mask > 1:
         steps.append(("lib", mask))
         mask //= 2
-    own_places = [(1, 0)]
-    own_arrays = [partner_keys, swap(values, "lib", 1)]
     leaving, _ = tie(queries, values)
     visitors = [swap(leaving, "qry", mask) for mask in masks]
     early, late = [], []
@@ -219,14 +208,28 @@
         near = (place, swap(keys, axis, mask), swap(values, axis, mask))
         relayed = []
         for (lib_mask, qry_mask), far_keys, far_values in early + late:
-            far_keys, far_values, *_ = tie(far_keys, far_values, *near[1:])
+            far_keys, *_ = tie(far_keys, near[1], values)
+            far_values, _ = tie(far_values, near[2])
             place = (lib_mask | mask, qry_mask)
             relayed.append((place, swap(far_keys, axis, mask), swap(far_values, axis, mask)))
         early, late = early + late + [near], relayed
-    early_places, early_arrays = both_cores(early)
-    late_places, late_arrays = both_cores(late, visitors)
-    early = (own_places + early_places, own_arrays + early_arrays)
-    return early, (late_places, late_arrays), list(zip(masks, visitors))
+    return early, late, list(zip(masks, visitors))
+
+
+def cross_cores(pieces, arrivals=()):
+    crossed = []
+    for (lib_mask, qry_mask), *pair in pieces:
+        pair = tie(*pair, *arrivals)[:2]
+        crossed.append(((lib_mask | 1, qry_mask), *(swap(array, "lib", 1) for array in pair)))
+    return crossed
+
+
+def places_of(pieces):
+    return [piece[0] for piece in pieces]
+
+
+def arrays_of(pieces):
+    return [array for piece in pieces for array in piece[1:]]
 
 
 def body(queries, library_keys, library_values, key_scale, block_list, block_count):
@@ -246,36 +249,40 @@
     )(own_values, key_scale.reshape(1, TILE))
 
     masks = [2 * at + 1 for at in range(1, qry_count // 2)]
-    (early_places, early_arrays), (late_places, late_arrays), visitors = gather_library(
-        library_keys, partner_keys, values, queries, masks
-    )
+    early, relayed, visitors = gather_library(library_keys, values, queries, masks)
     piece_rows = (width // value_width + 1) * TILE + EXTRA
-    count_early, count_late = len(early_places) + 1, len(late_places)
-
     cost = pl.CostEstimate(flops=2 * TILE * 4 * TILE * width * 2, bytes_accessed=4 * 1024 * 1024, transcendentals=0)
     total_shape = jax.ShapeDtypeStruct((TILE, value_width), jnp.float32)
     line_shape = jax.ShapeDtypeStruct((TILE, LANES), jnp.float32)
-    attend_params = params((count_early + count_late) * piece_rows * value_width * 2)
+    pieces_total = 2 * (1 + len(early) + len(relayed))
+    attend_params = params(pieces_total * piece_rows * value_width * 2)
     own_specs = [pl.BlockSpec(memory_space=pl.ANY), VMEM]
     own_scratch = [pltpu.VMEM(library_keys.shape, library_keys.dtype), pltpu.SemaphoreType.DMA]
-    returned = []
+    early_arrays = arrays_of(early)
+    states = []
     for mask, visiting in visitors:
-        *state, = pl.pallas_call(
-            functools.partial(early_kernel, early_places, mask),
+        state = pl.pallas_call(
+            functools.partial(early_kernel, places_of(early), mask),
             out_shape=(total_shape, line_shape, line_shape),
             in_specs=[SMEM, SMEM] + [VMEM] * (1 + len(early_arrays)) + own_specs,
             out_specs=(VMEM,) * 3,
-            scratch_shapes=[pltpu.VMEM((count_early, TILE, TILE), jnp.float32)] + own_scratch,
+            scratch_shapes=[pltpu.VMEM((len(early) + 1, TILE, TILE), jnp.float32)] + own_scratch,
             compiler_params=attend_params,
             cost_estimate=cost,
         )(block_list, block_count, visiting, *early_arrays, library_keys, values)
+        states.append(state)
+
+    late = [((1, 0), partner_keys, swap(values, "lib", 1))] + cross_cores(early) + relayed + cross_cores(relayed, [state[2] for state in states])
+    late_arrays = arrays_of(late)
+    returned = []
+    for (mask, visiting), state in zip(visitors, states):
         packed = pl.pallas_call(
-            functools.partial(late_kernel, late_places, mask),
+            functools.partial(late_kernel, places_of(late), mask),
             out_shape=jax.ShapeDtypeStruct((TILE + EXTRA, value_width), jnp.bfloat16),
             in_specs=[SMEM, SMEM] + [VMEM] * (4 + len(late_arrays)),
             out_specs=VMEM,
             scratch_shapes=[
-                pltpu.VMEM((count_late, TILE, TILE), jnp.float32),
+                pltpu.VMEM((len(late), TILE, TILE), jnp.float32),
                 pltpu.VMEM((TILE, value_width), jnp.float32),
                 pltpu.VMEM((TILE, TILE), jnp.float32),
             ],
@@ -285,12 +292,12 @@
         returned.append(swap(packed, "qry", mask))
 
     total, stats = pl.pallas_call(
-        functools.partial(home_kernel, early_places + late_places),
+        functools.partial(home_kernel, places_of(early + late)),
         out_shape=(total_shape, jax.ShapeDtypeStruct((2, TILE, LANES), jnp.float32)),
         in_specs=[SMEM, SMEM] + [VMEM] * (1 + len(early_arrays) + len(late_arrays)) + own_specs,
         out_specs=(VMEM, VMEM),
         scratch_shapes=[
-            pltpu.VMEM((count_early + count_late, TILE, TILE), jnp.float32),
+            pltpu.VMEM((pieces_total, TILE, TILE), jnp.float32),
             pltpu.VMEM((TILE, TILE), jnp.float32),
         ]
         + own_scratch,

time: 40.5 us -> 36.3 us (0.90)
  waiting for transfers between devices: 16.4 us -> 11.6 us
  Pallas kernels: 4.32 us -> 5.11 us
    ppermute x16, waiting for transfers between devices: 16.4 us -> 11.6 us  [swap(): return lax.ppermute(value, axis, [(i, i ^ mask) for i in range(length)])]
    pallas_call x3, Pallas kernels: 3.34 us -> 4.12 us  [the longest x1 1.84 us: body(): pl.pallas_call(functools.partial(home_kernel, places_of(early + late)), o...]
  transfers between devices with their start and end apart: 16 -> 16, of which waited for: 7 -> 7; matrix products, arithmetic and copies ran while one was open for 0% -> 0% of each run, Pallas kernels for 5% -> 9%
where the time goes in v7:
time: 36.3 us; the launch traced here: 36.2 us
  starting transfers between devices  17.8 us (49%)
  waiting for transfers between devices  11.6 us (32%)
  Pallas kernels  5.11 us (14%)
  local copies, waits for them, and re-layouts  1.66 us (5%)
    ppermute x16, starting transfers between devices, swap(): return lax.ppermute(value, axis, [(i, i ^ mask) for i in range(length)])  17.8 us
    ppermute x16, waiting for transfers between devices, swap(): return lax.ppermute(value, axis, [(i, i ^ mask) for i in range(length)])  11.6 us
    pallas_call x1, Pallas kernels, body(): pl.pallas_call(functools.partial(home_kernel, places_of(early + late)), o...  1.84 us
    unnamed x13, local copies, waits for them, and re-layouts  1.66 us
    pallas_call x1, Pallas kernels, body(): pl.pallas_call(functools.partial(early_kernel, places_of(early), mask), o...  1.26 us
    pallas_call x1, Pallas kernels, body(): pl.pallas_call(functools.partial(late_kernel, places_of(late), mask), out...  1.03 us
    pallas_call x1, Pallas kernels, body(): pl.pallas_call(merge_kernel, out_shape=jax.ShapeDtypeStruct((TILE, value_...  0.81 us
  transfers between devices with their start and end apart: 16, of which 7 were waited for; matrix products, arithmetic and copies ran while one was open for 0% of the time, Pallas kernels for 9%

profile of v7, /device:TPU:0, one launch (start us, length us, event | category | flops | bytes accessed | tf_op | source)
XLA Modules:
  0.0 36.2 jit_solution(9075550674542951969)
XLA Ops:
  0.0 0.5 %collective-permute-start.1 = (bf16[128,1024]{1,0:T(8,128)(2,1)}, bf16[128,1024]{1,0:T(8,128)(2,1)S(1)}, u32[]{:S(2)}, u32[]{:S(2)}) collective-permute-start(bf16[128,1024]{1,0:T(8,128)(2,1)} %refs_14_.1), channel_id=1, source_target_pairs={{0,4},{4,0},{8,12},{12,8},{1,5},{5,1},{9,13},{13,9},{2,6},{6,2},{1... | collective-permute-start | bytes 786440 | tf_op jit(solution)/shard_map/ppermute | solution.py:25
  0.5 2.6 %collective-permute-start = (bf16[128,1024]{1,0:T(8,128)(2,1)}, bf16[128,1024]{1,0:T(8,128)(2,1)S(1)}, u32[]{:S(2)}, u32[]{:S(2)}) collective-permute-start(bf16[128,1024]{1,0:T(8,128)(2,1)} %refs_14_.1), channel_id=1, source_target_pairs={{0,1},{1,0},{2,3},{3,2},{4,5},{5,4},{6,7},{7,6},{8,9},{9,8},{10,11... | collective-permute-start | bytes 786440 | tf_op jit(solution)/shard_map/ppermute | solution.py:25
  3.1 1.5 %collective-permute-start.3 = (bf16[128,1024]{1,0:T(8,128)(2,1)}, bf16[128,1024]{1,0:T(8,128)(2,1)S(1)}, u32[]{:S(2)}, u32[]{:S(2)}) collective-permute-start(bf16[128,1024]{1,0:T(8,128)(2,1)} %refs_14_.1), channel_id=1, source_target_pairs={{0,8},{4,12},{8,0},{12,4},{1,9},{5,13},{9,1},{13,5},{2,10},{6,14},... | collective-permute-start | bytes 786440 | tf_op jit(solution)/shard_map/ppermute | solution.py:25
  4.6 0.0 collective-permute-done.1.refs_4_.refs_3_
  4.6 0.9 %copy-done.2 = bf16[128,512]{1,0:T(8,128)(2,1)S(1)} copy-done((bf16[128,512]{1,0:T(8,128)(2,1)S(1)}, bf16[128,512]{1,0:T(8,128)(2,1)}, u32[]{:S(2)}) %copy-start.2) | copy-done | bytes 131096
  5.5 0.7 %copy-done.4 = bf16[128]{0:T(256)(128)(2,1)S(1)} copy-done((bf16[128]{0:T(256)(128)(2,1)S(1)}, bf16[128]{0:T(256)(128)(2,1)}, u32[]{:S(2)}) %copy-start.4) | copy-done | bytes 280
  6.1 0.2 shard_map.64.refs_5_.refs_15_
  6.3 0.0 copy-start.3
  6.3 0.5 %collective-permute-start.2 = (bf16[144,512]{1,0:T(8,128)(2,1)S(1)}, bf16[144,512]{1,0:T(8,128)(2,1)S(1)}, u32[]{:S(2)}, u32[]{:S(2)}) collective-permute-start(bf16[144,512]{1,0:T(8,128)(2,1)S(1)} %shard_map.64.refs_5_.refs_15_), channel_id=1, source_target_pairs={{0,1},{1,0},{2,3},{3,2},{4,5},{5,4},{6,7},{7,6},{8,9},{9,8},{10,11... | collective-permute-start | bytes 442376 | tf_op jit(solution)/shard_map/ppermute | solution.py:25
  6.9 1.2 %collective-permute-start.4 = (bf16[144,512]{1,0:T(8,128)(2,1)S(1)}, bf16[144,512]{1,0:T(8,128)(2,1)S(1)}, u32[]{:S(2)}, u32[]{:S(2)}) collective-permute-start(bf16[144,512]{1,0:T(8,128)(2,1)S(1)} %shard_map.64.refs_5_.refs_15_), channel_id=1, source_target_pairs={{0,8},{4,12},{8,0},{12,4},{1,9},{5,13},{9,1},{13,5},{2,10},{6,14},... | collective-permute-start | bytes 442376 | tf_op jit(solution)/shard_map/ppermute | solution.py:25
  8.1 2.9 %collective-permute-start.12 = (bf16[128,1024]{1,0:T(8,128)(2,1)}, bf16[128,1024]{1,0:T(8,128)(2,1)S(1)}, u32[]{:S(2)}, u32[]{:S(2)}) collective-permute-start(bf16[128,1024]{1,0:T(8,128)(2,1)} %query_ref.1), channel_id=1, source_target_pairs={{0,3},{1,2},{2,1},{3,0},{4,7},{5,6},{6,5},{7,4},{8,11},{9,10},{10,... | collective-permute-start | bytes 786440 | tf_op jit(solution)/shard_map/ppermute | solution.py:25
  11.0 1.5 %collective-permute-done.3.refs_2_ = bf16[128,1024]{1,0:T(8,128)(2,1)S(1)} collective-permute-done((bf16[128,1024]{1,0:T(8,128)(2,1)}, bf16[128,1024]{1,0:T(8,128)(2,1)S(1)}, u32[]{:S(2)}, u32[]{:S(2)}) %collective-permute-start.3) | collective-permute-done | bytes 262176 | tf_op jit(solution)/shard_map/ppermute | solution.py:25
  12.5 1.5 %collective-permute-start.10 = (bf16[128,1024]{1,0:T(8,128)(2,1)S(1)}, bf16[128,1024]{1,0:T(8,128)(2,1)S(1)}, u32[]{:S(2)}, u32[]{:S(2)}) collective-permute-start(bf16[128,1024]{1,0:T(8,128)(2,1)S(1)} %collective-permute-done.refs_0_), channel_id=1, source_target_pairs={{0,8},{4,12},{8,0},{12,4},{1,9},{5,13},{9,1},{13,5},{2,10},{6,14},... | collective-permute-start | bytes 786440 | tf_op jit(solution)/shard_map/ppermute | solution.py:25
  13.9 1.7 %collective-permute-done.4.refs_3_ = bf16[144,512]{1,0:T(8,128)(2,1)S(1)} collective-permute-done((bf16[144,512]{1,0:T(8,128)(2,1)S(1)}, bf16[144,512]{1,0:T(8,128)(2,1)S(1)}, u32[]{:S(2)}, u32[]{:S(2)}) %collective-permute-start.4) | collective-permute-done | bytes 147488 | tf_op jit(solution)/shard_map/ppermute | solution.py:25
  15.6 1.5 %collective-permute-start.11 = (bf16[144,512]{1,0:T(8,128)(2,1)S(1)}, bf16[144,512]{1,0:T(8,128)(2,1)S(1)}, u32[]{:S(2)}, u32[]{:S(2)}) collective-permute-start(bf16[144,512]{1,0:T(8,128)(2,1)S(1)} %collective-permute-done.2.refs_1_), channel_id=1, source_target_pairs={{0,8},{4,12},{8,0},{12,4},{1,9},{5,13},{9,1},{13,5},{2,10},{6,14},... | collective-permute-start | bytes 442376 | tf_op jit(solution)/shard_map/ppermute | solution.py:25
  17.1 0.5 %collective-permute-start.7 = (bf16[144,512]{1,0:T(8,128)(2,1)S(1)}, bf16[144,512]{1,0:T(8,128)(2,1)S(1)}, u32[]{:S(2)}, u32[]{:S(2)}) collective-permute-start(bf16[144,512]{1,0:T(8,128)(2,1)S(1)} %collective-permute-done.2.refs_1_), channel_id=1, source_target_pairs={{0,4},{4,0},{8,12},{12,8},{1,5},{5,1},{9,13},{13,9},{2,6},{6,2},{1... | collective-permute-start | bytes 442376 | tf_op jit(solution)/shard_map/ppermute | solution.py:25
  17.6 0.1 copy.8.lists_ref
  17.7 3.6 %collective-permute-done.12.query_ref = bf16[128,1024]{1,0:T(8,128)(2,1)S(1)} collective-permute-done((bf16[128,1024]{1,0:T(8,128)(2,1)}, bf16[128,1024]{1,0:T(8,128)(2,1)S(1)}, u32[]{:S(2)}, u32[]{:S(2)}) %collective-permute-start.12) | collective-permute-done | bytes 262176 | tf_op jit(solution)/shard_map/ppermute | solution.py:25
  21.3 0.0 collective-permute-start.6
  21.3 1.3 %shard_map.65 = (f32[128,512]{1,0:T(8,128)S(1)}, f32[128,128]{1,0:T(8,128)S(1)}, f32[128,128]{1,0:T(8,128)S(1)}) custom-call(s32[16,4]{1,0:T(8,128)S(1)} %copy.8.lists_ref, s32[16]{0:T(128)S(1)} %copy-done.3, bf16[128,1024]{1,0:T(8,128)(2,1)S(1)} %collective-permute-done.12.query_ref, bf16[128,1024]{1,0:T(8,128)(2,1)S(1)} %collective-permute-done.refs_0_, ...), custom_call_target="tpu_custom_call" | custom-call | flops 268435456 | bytes 4194304 | tf_op jit(solution)/shard_map/pallas_call | solution.py:264
  22.6 0.0 collective-permute-done.10.refs_10_.refs_9_
  22.6 0.1 collective-permute-start.8
  22.7 0.9 %collective-permute-done.11.refs_11_.refs_10_ = bf16[144,512]{1,0:T(8,128)(2,1)S(1)} collective-permute-done((bf16[144,512]{1,0:T(8,128)(2,1)S(1)}, bf16[144,512]{1,0:T(8,128)(2,1)S(1)}, u32[]{:S(2)}, u32[]{:S(2)}) %collective-permute-start.11) | collective-permute-done | bytes 147488 | tf_op jit(solution)/shard_map/ppermute | solution.py:25
  23.6 0.5 %collective-permute-start.9 = (bf16[144,512]{1,0:T(8,128)(2,1)S(1)}, bf16[144,512]{1,0:T(8,128)(2,1)S(1)}, u32[]{:S(2)}, u32[]{:S(2)}) collective-permute-start(bf16[144,512]{1,0:T(8,128)(2,1)S(1)} %collective-permute-done.4.refs_3_), channel_id=1, source_target_pairs={{0,4},{4,0},{8,12},{12,8},{1,5},{5,1},{9,13},{13,9},{2,6},{6,2},{1... | collective-permute-start | bytes 442376 | tf_op jit(solution)/shard_map/ppermute | solution.py:25
  24.1 0.1 collective-permute-start.14
  24.2 1.2 %collective-permute-done.9.refs_9_.refs_8_ = bf16[144,512]{1,0:T(8,128)(2,1)S(1)} collective-permute-done((bf16[144,512]{1,0:T(8,128)(2,1)S(1)}, bf16[144,512]{1,0:T(8,128)(2,1)S(1)}, u32[]{:S(2)}, u32[]{:S(2)}) %collective-permute-start.9) | collective-permute-done | bytes 147488 | tf_op jit(solution)/shard_map/ppermute | solution.py:25
  25.4 0.2 collective-permute-done.14.refs_13_.refs_12_
  25.6 1.0 %shard_map.67 = bf16[144,512]{1,0:T(8,128)(2,1)S(1)} custom-call(s32[16,4]{1,0:T(8,128)S(1)} %copy.8.lists_ref, s32[16]{0:T(128)S(1)} %copy-done.3, bf16[128,1024]{1,0:T(8,128)(2,1)S(1)} %collective-permute-done.12.query_ref, f32[128,512]{1,0:T(8,128)S(1)} %get-tuple-element.33.refs_0_, f32[128,128]{1,0:T(8,128)S(1)} %get-tuple-element.34.refs_1_, ...), custom_call_target="tpu_custom_call" | custom-call | flops 268435456 | bytes 4194304 | tf_op jit(solution)/shard_map/pallas_call | solution.py:279
  26.6 4.4 %collective-permute-start.15 = (bf16[144,512]{1,0:T(8,128)(2,1)S(1)}, bf16[144,512]{1,0:T(8,128)(2,1)S(1)}, u32[]{:S(2)}, u32[]{:S(2)}) collective-permute-start(bf16[144,512]{1,0:T(8,128)(2,1)S(1)} %shard_map.67), channel_id=1, source_target_pairs={{0,3},{1,2},{2,1},{3,0},{4,7},{5,6},{6,5},{7,4},{8,11},{9,10},{10,... | collective-permute-start | bytes 442376 | tf_op jit(solution)/shard_map/ppermute | solution.py:25
  31.0 1.8 %shard_map.66 = (f32[128,512]{1,0:T(8,128)S(1)}, f32[2,128,128]{2,1,0:T(8,128)S(1)}) custom-call(s32[16,4]{1,0:T(8,128)S(1)} %copy.8.lists_ref, s32[16]{0:T(128)S(1)} %copy-done.3, bf16[128,1024]{1,0:T(8,128)(2,1)S(1)} %copy-done.1, bf16[128,1024]{1,0:T(8,128)(2,1)S(1)} %collective-permute-done.refs_0_, bf16[144,512]{1,0:T(8,128)(2,1)S(1)} %collective-permute-done.2.refs_1_, ...), custom_call_target="tpu_custom_call" | custom-call | flops 268435456 | bytes 4194304 | tf_op jit(solution)/shard_map/pallas_call | solution.py:294
  32.8 2.6 %collective-permute-done.15.refs_0_ = bf16[144,512]{1,0:T(8,128)(2,1)S(1)} collective-permute-done((bf16[144,512]{1,0:T(8,128)(2,1)S(1)}, bf16[144,512]{1,0:T(8,128)(2,1)S(1)}, u32[]{:S(2)}, u32[]{:S(2)}) %collective-permute-start.15) | collective-permute-done | bytes 147488 | tf_op jit(solution)/shard_map/ppermute | solution.py:25
  35.4 0.8 %shard_map.68 = bf16[128,512]{1,0:T(8,128)(2,1)} custom-call(f32[128,512]{1,0:T(8,128)S(1)} %get-tuple-element.31.total_ref, f32[2,128,128]{2,1,0:T(8,128)S(1)} %get-tuple-element.32.stats_ref, bf16[144,512]{1,0:T(8,128)(2,1)S(1)} %collective-permute-done.15.refs_0_), custom_call_target="tpu_custom_call" | custom-call | tf_op jit(solution)/shard_map/pallas_call | solution.py:308
  (18 shorter events, 0.0 us)
Async XLA Ops:
  0.0 21.3 %copy-start = (bf16[128,1024]{1,0:T(8,128)(2,1)S(1)}, bf16[128,1024]{1,0:T(8,128)(2,1)}, u32[]{:S(2)}) copy-start(bf16[128,1024]{1,0:T(8,128)(2,1)} %refs_14_.1) | copy-start | bytes 786436
  0.0 4.6 %collective-permute-start.1 = (bf16[128,1024]{1,0:T(8,128)(2,1)}, bf16[128,1024]{1,0:T(8,128)(2,1)S(1)}, u32[]{:S(2)}, u32[]{:S(2)}) collective-permute-start(bf16[128,1024]{1,0:T(8,128)(2,1)} %refs_14_.1), channel_id=1, source_target_pairs={{0,4},{4,0},{8,12},{12,8},{1,5},{5,1},{9,13},{13,9},{2,6},{6,2},{1... | collective-permute-start | bytes 786440 | tf_op jit(solution)/shard_map/ppermute | solution.py:25
  0.5 10.5 %collective-permute-start = (bf16[128,1024]{1,0:T(8,128)(2,1)}, bf16[128,1024]{1,0:T(8,128)(2,1)S(1)}, u32[]{:S(2)}, u32[]{:S(2)}) collective-permute-start(bf16[128,1024]{1,0:T(8,128)(2,1)} %refs_14_.1), channel_id=1, source_target_pairs={{0,1},{1,0},{2,3},{3,2},{4,5},{5,4},{6,7},{7,6},{8,9},{9,8},{10,11... | collective-permute-start | bytes 786440 | tf_op jit(solution)/shard_map/ppermute | solution.py:25
  3.1 9.4 %collective-permute-start.3 = (bf16[128,1024]{1,0:T(8,128)(2,1)}, bf16[128,1024]{1,0:T(8,128)(2,1)S(1)}, u32[]{:S(2)}, u32[]{:S(2)}) collective-permute-start(bf16[128,1024]{1,0:T(8,128)(2,1)} %refs_14_.1), channel_id=1, source_target_pairs={{0,8},{4,12},{8,0},{12,4},{1,9},{5,13},{9,1},{13,5},{2,10},{6,14},... | collective-permute-start | bytes 786440 | tf_op jit(solution)/shard_map/ppermute | solution.py:25
  4.6 0.9 %copy-start.2 = (bf16[128,512]{1,0:T(8,128)(2,1)S(1)}, bf16[128,512]{1,0:T(8,128)(2,1)}, u32[]{:S(2)}) copy-start(bf16[128,512]{1,0:T(8,128)(2,1)} %values_ref) | copy-start | bytes 393220
  5.5 0.7 %copy-start.4 = (bf16[128]{0:T(256)(128)(2,1)S(1)}, bf16[128]{0:T(256)(128)(2,1)}, u32[]{:S(2)}) copy-start(bf16[128]{0:T(256)(128)(2,1)} %param.9) | copy-start | bytes 772
  6.1 11.5 %copy-start.5 = (s32[16,4]{0,1:T(4,128)S(1)}, s32[16,4]{0,1:T(4,128)}, u32[]{:S(2)}) copy-start(s32[16,4]{0,1:T(4,128)} %param.10) | copy-start | bytes 772
  6.3 15.0 %copy-start.3 = (s32[16]{0:T(128)S(1)}, s32[16]{0:T(128)}, u32[]{:S(2)}) copy-start(s32[16]{0:T(128)} %counts_ref.5) | copy-start | bytes 196
  6.3 7.6 %collective-permute-start.2 = (bf16[144,512]{1,0:T(8,128)(2,1)S(1)}, bf16[144,512]{1,0:T(8,128)(2,1)S(1)}, u32[]{:S(2)}, u32[]{:S(2)}) collective-permute-start(bf16[144,512]{1,0:T(8,128)(2,1)S(1)} %shard_map.64.refs_5_.refs_15_), channel_id=1, source_target_pairs={{0,1},{1,0},{2,3},{3,2},{4,5},{5,4},{6,7},{7,6},{8,9},{9,8},{10,11... | collective-permute-start | bytes 442376 | tf_op jit(solution)/shard_map/ppermute | solution.py:25
  6.9 8.8 %collective-permute-start.4 = (bf16[144,512]{1,0:T(8,128)(2,1)S(1)}, bf16[144,512]{1,0:T(8,128)(2,1)S(1)}, u32[]{:S(2)}, u32[]{:S(2)}) collective-permute-start(bf16[144,512]{1,0:T(8,128)(2,1)S(1)} %shard_map.64.refs_5_.refs_15_), channel_id=1, source_target_pairs={{0,8},{4,12},{8,0},{12,4},{1,9},{5,13},{9,1},{13,5},{2,10},{6,14},... | collective-permute-start | bytes 442376 | tf_op jit(solution)/shard_map/ppermute | solution.py:25
  8.1 13.2 %collective-permute-start.12 = (bf16[128,1024]{1,0:T(8,128)(2,1)}, bf16[128,1024]{1,0:T(8,128)(2,1)S(1)}, u32[]{:S(2)}, u32[]{:S(2)}) collective-permute-start(bf16[128,1024]{1,0:T(8,128)(2,1)} %query_ref.1), channel_id=1, source_target_pairs={{0,3},{1,2},{2,1},{3,0},{4,7},{5,6},{6,5},{7,4},{8,11},{9,10},{10,... | collective-permute-start | bytes 786440 | tf_op jit(solution)/shard_map/ppermute | solution.py:25
  12.5 10.1 %collective-permute-start.10 = (bf16[128,1024]{1,0:T(8,128)(2,1)S(1)}, bf16[128,1024]{1,0:T(8,128)(2,1)S(1)}, u32[]{:S(2)}, u32[]{:S(2)}) collective-permute-start(bf16[128,1024]{1,0:T(8,128)(2,1)S(1)} %collective-permute-done.refs_0_), channel_id=1, source_target_pairs={{0,8},{4,12},{8,0},{12,4},{1,9},{5,13},{9,1},{13,5},{2,10},{6,14},... | collective-permute-start | bytes 786440 | tf_op jit(solution)/shard_map/ppermute | solution.py:25
  15.6 8.0 %collective-permute-start.11 = (bf16[144,512]{1,0:T(8,128)(2,1)S(1)}, bf16[144,512]{1,0:T(8,128)(2,1)S(1)}, u32[]{:S(2)}, u32[]{:S(2)}) collective-permute-start(bf16[144,512]{1,0:T(8,128)(2,1)S(1)} %collective-permute-done.2.refs_1_), channel_id=1, source_target_pairs={{0,8},{4,12},{8,0},{12,4},{1,9},{5,13},{9,1},{13,5},{2,10},{6,14},... | collective-permute-start | bytes 442376 | tf_op jit(solution)/shard_map/ppermute | solution.py:25
  17.1 6.5 %collective-permute-start.5 = (bf16[144,512]{1,0:T(8,128)(2,1)S(1)}, bf16[144,512]{1,0:T(8,128)(2,1)S(1)}, u32[]{:S(2)}, u32[]{:S(2)}) collective-permute-start(bf16[144,512]{1,0:T(8,128)(2,1)S(1)} %shard_map.64.refs_5_.refs_15_), channel_id=1, source_target_pairs={{0,4},{4,0},{8,12},{12,8},{1,5},{5,1},{9,13},{13,9},{2,6},{6,2},{1... | collective-permute-start | bytes 442376 | tf_op jit(solution)/shard_map/ppermute | solution.py:25
  17.1 7.0 %collective-permute-start.7 = (bf16[144,512]{1,0:T(8,128)(2,1)S(1)}, bf16[144,512]{1,0:T(8,128)(2,1)S(1)}, u32[]{:S(2)}, u32[]{:S(2)}) collective-permute-start(bf16[144,512]{1,0:T(8,128)(2,1)S(1)} %collective-permute-done.2.refs_1_), channel_id=1, source_target_pairs={{0,4},{4,0},{8,12},{12,8},{1,5},{5,1},{9,13},{13,9},{2,6},{6,2},{1... | collective-permute-start | bytes 442376 | tf_op jit(solution)/shard_map/ppermute | solution.py:25
  21.3 4.1 %collective-permute-start.6 = (bf16[128,1024]{1,0:T(8,128)(2,1)S(1)}, bf16[128,1024]{1,0:T(8,128)(2,1)S(1)}, u32[]{:S(2)}, u32[]{:S(2)}) collective-permute-start(bf16[128,1024]{1,0:T(8,128)(2,1)S(1)} %collective-permute-done.refs_0_), channel_id=1, source_target_pairs={{0,4},{4,0},{8,12},{12,8},{1,5},{5,1},{9,13},{13,9},{2,6},{6,2},{1... | collective-permute-start | bytes 786440 | tf_op jit(solution)/shard_map/ppermute | solution.py:25
  22.6 2.8 %collective-permute-start.8 = (bf16[128,1024]{1,0:T(8,128)(2,1)S(1)}, bf16[128,1024]{1,0:T(8,128)(2,1)S(1)}, u32[]{:S(2)}, u32[]{:S(2)}) collective-permute-start(bf16[128,1024]{1,0:T(8,128)(2,1)S(1)} %collective-permute-done.3.refs_2_), channel_id=1, source_target_pairs={{0,4},{4,0},{8,12},{12,8},{1,5},{5,1},{9,13},{13,9},{2,6},{6,2},{1... | collective-permute-start | bytes 786440 | tf_op jit(solution)/shard_map/ppermute | solution.py:25
  23.6 2.0 %collective-permute-start.13 = (bf16[128,1024]{1,0:T(8,128)(2,1)S(1)}, bf16[128,1024]{1,0:T(8,128)(2,1)S(1)}, u32[]{:S(2)}, u32[]{:S(2)}) collective-permute-start(bf16[128,1024]{1,0:T(8,128)(2,1)S(1)} %collective-permute-done.10.refs_10_.refs_9_), channel_id=1, source_target_pairs={{0,4},{4,0},{8,12},{12,8},{1,5},{5,1},{9,13},{13,9},{2,6},{6,2},{1... | collective-permute-start | bytes 786440 | tf_op jit(solution)/shard_map/ppermute | solution.py:25
  23.6 1.7 %collective-permute-start.9 = (bf16[144,512]{1,0:T(8,128)(2,1)S(1)}, bf16[144,512]{1,0:T(8,128)(2,1)S(1)}, u32[]{:S(2)}, u32[]{:S(2)}) collective-permute-start(bf16[144,512]{1,0:T(8,128)(2,1)S(1)} %collective-permute-done.4.refs_3_), channel_id=1, source_target_pairs={{0,4},{4,0},{8,12},{12,8},{1,5},{5,1},{9,13},{13,9},{2,6},{6,2},{1... | collective-permute-start | bytes 442376 | tf_op jit(solution)/shard_map/ppermute | solution.py:25
  24.1 1.4 %collective-permute-start.14 = (bf16[144,512]{1,0:T(8,128)(2,1)S(1)}, bf16[144,512]{1,0:T(8,128)(2,1)S(1)}, u32[]{:S(2)}, u32[]{:S(2)}) collective-permute-start(bf16[144,512]{1,0:T(8,128)(2,1)S(1)} %collective-permute-done.11.refs_11_.refs_10_), channel_id=1, source_target_pairs={{0,4},{4,0},{8,12},{12,8},{1,5},{5,1},{9,13},{13,9},{2,6},{6,2},{1... | collective-permute-start | bytes 442376 | tf_op jit(solution)/shard_map/ppermute | solution.py:25
  25.6 5.4 %copy-start.1 = (bf16[128,1024]{1,0:T(8,128)(2,1)S(1)}, bf16[128,1024]{1,0:T(8,128)(2,1)}, u32[]{:S(2)}) copy-start(bf16[128,1024]{1,0:T(8,128)(2,1)} %query_ref.1) | copy-start | bytes 786436
  26.6 8.8 %collective-permute-start.15 = (bf16[144,512]{1,0:T(8,128)(2,1)S(1)}, bf16[144,512]{1,0:T(8,128)(2,1)S(1)}, u32[]{:S(2)}, u32[]{:S(2)}) collective-permute-start(bf16[144,512]{1,0:T(8,128)(2,1)S(1)} %shard_map.67), channel_id=1, source_target_pairs={{0,3},{1,2},{2,1},{3,0},{4,7},{5,6},{6,5},{7,4},{8,11},{9,10},{10,... | collective-permute-start | bytes 442376 | tf_op jit(solution)/shard_map/ppermute | solution.py:25

commit v8 on v7

--- a/solution.py
+++ b/solution.py
@@ -248,7 +248,7 @@
         compiler_params=params(),
     )(own_values, key_scale.reshape(1, TILE))
 
-    masks = [2 * at + 1 for at in range(1, qry_count // 2)]
+    masks = [2 * at for at in range(1, qry_count // 2)]
     early, relayed, visitors = gather_library(library_keys, values, queries, masks)
     piece_rows = (width // value_width + 1) * TILE + EXTRA
     cost = pl.CostEstimate(flops=2 * TILE * 4 * TILE * width * 2, bytes_accessed=4 * 1024 * 1024, transcendentals=0)

time: 36.3 us -> 38.6 us (1.063)
  starting transfers between devices: 17.8 us -> 19.5 us
  waiting for transfers between devices: 11.6 us -> 12.6 us
  Pallas kernels: 5.11 us -> 4.32 us
    ppermute x16, starting transfers between devices: 17.8 us -> 19.5 us  [swap(): return lax.ppermute(value, axis, [(i, i ^ mask) for i in range(length)])]
    ppermute x16, waiting for transfers between devices: 11.6 us -> 12.6 us  [swap(): return lax.ppermute(value, axis, [(i, i ^ mask) for i in range(length)])]
    pallas_call x1, Pallas kernels: 1.84 us -> 0.98 us  [body(): pl.pallas_call(functools.partial(home_kernel, places_of(early + late)), o...]
    pallas_call x1, Pallas kernels: 1.03 us -> 1.52 us  [body(): pl.pallas_call(functools.partial(late_kernel, places_of(late), mask), out...]
    pallas_call x1, Pallas kernels: 1.26 us -> 0.83 us  [body(): pl.pallas_call(functools.partial(early_kernel, places_of(early), mask), o...]
  transfers between devices with their start and end apart: 16 -> 16, of which waited for: 7 -> 7; matrix products, arithmetic and copies ran while one was open for 0% -> 0% of each run, Pallas kernels for 9% -> 5%
where the time goes in v8:
time: 38.6 us; the launch traced here: 38.2 us
  starting transfers between devices  19.5 us (51%)
  waiting for transfers between devices  12.6 us (33%)
  Pallas kernels  4.32 us (11%)
  local copies, waits for them, and re-layouts  1.66 us (4%)
    ppermute x16, starting transfers between devices, swap(): return lax.ppermute(value, axis, [(i, i ^ mask) for i in range(length)])  19.5 us
    ppermute x16, waiting for transfers between devices, swap(): return lax.ppermute(value, axis, [(i, i ^ mask) for i in range(length)])  12.6 us
    unnamed x13, local copies, waits for them, and re-layouts  1.66 us
    pallas_call x1, Pallas kernels, body(): pl.pallas_call(functools.partial(late_kernel, places_of(late), mask), out...  1.52 us
    pallas_call x1, Pallas kernels, body(): pl.pallas_call(functools.partial(home_kernel, places_of(early + late)), o...  0.98 us
    pallas_call x1, Pallas kernels, body(): pl.pallas_call(functools.partial(early_kernel, places_of(early), mask), o...  0.83 us
    pallas_call x1, Pallas kernels, body(): pl.pallas_call(merge_kernel, out_shape=jax.ShapeDtypeStruct((TILE, value_...  0.81 us
  transfers between devices with their start and end apart: 16, of which 7 were waited for; matrix products, arithmetic and copies ran while one was open for 0% of the time, Pallas kernels for 5%

profile of v8, /device:TPU:0, one launch (start us, length us, event | category | flops | bytes accessed | tf_op | source)
XLA Modules:
  0.0 38.2 jit_solution(656292799559565511)
XLA Ops:
  0.0 0.5 %collective-permute-start.1 = (bf16[128,1024]{1,0:T(8,128)(2,1)}, bf16[128,1024]{1,0:T(8,128)(2,1)S(1)}, u32[]{:S(2)}, u32[]{:S(2)}) collective-permute-start(bf16[128,1024]{1,0:T(8,128)(2,1)} %refs_14_.1), channel_id=1, source_target_pairs={{0,4},{4,0},{8,12},{12,8},{1,5},{5,1},{9,13},{13,9},{2,6},{6,2},{1... | collective-permute-start | bytes 786440 | tf_op jit(solution)/shard_map/ppermute | solution.py:25
  0.5 2.6 %collective-permute-start = (bf16[128,1024]{1,0:T(8,128)(2,1)}, bf16[128,1024]{1,0:T(8,128)(2,1)S(1)}, u32[]{:S(2)}, u32[]{:S(2)}) collective-permute-start(bf16[128,1024]{1,0:T(8,128)(2,1)} %refs_14_.1), channel_id=1, source_target_pairs={{0,1},{1,0},{2,3},{3,2},{4,5},{5,4},{6,7},{7,6},{8,9},{9,8},{10,11... | collective-permute-start | bytes 786440 | tf_op jit(solution)/shard_map/ppermute | solution.py:25
  3.1 1.5 %collective-permute-start.3 = (bf16[128,1024]{1,0:T(8,128)(2,1)}, bf16[128,1024]{1,0:T(8,128)(2,1)S(1)}, u32[]{:S(2)}, u32[]{:S(2)}) collective-permute-start(bf16[128,1024]{1,0:T(8,128)(2,1)} %refs_14_.1), channel_id=1, source_target_pairs={{0,8},{4,12},{8,0},{12,4},{1,9},{5,13},{9,1},{13,5},{2,10},{6,14},... | collective-permute-start | bytes 786440 | tf_op jit(solution)/shard_map/ppermute | solution.py:25
  4.6 0.0 collective-permute-done.1.refs_4_.refs_3_
  4.6 0.9 %copy-done.2 = bf16[128,512]{1,0:T(8,128)(2,1)S(1)} copy-done((bf16[128,512]{1,0:T(8,128)(2,1)S(1)}, bf16[128,512]{1,0:T(8,128)(2,1)}, u32[]{:S(2)}) %copy-start.2) | copy-done | bytes 131096
  5.5 0.7 %copy-done.4 = bf16[128]{0:T(256)(128)(2,1)S(1)} copy-done((bf16[128]{0:T(256)(128)(2,1)S(1)}, bf16[128]{0:T(256)(128)(2,1)}, u32[]{:S(2)}) %copy-start.4) | copy-done | bytes 280
  6.1 0.2 shard_map.64.refs_5_.refs_15_
  6.3 0.0 copy-start.3
  6.3 0.5 %collective-permute-start.2 = (bf16[144,512]{1,0:T(8,128)(2,1)S(1)}, bf16[144,512]{1,0:T(8,128)(2,1)S(1)}, u32[]{:S(2)}, u32[]{:S(2)}) collective-permute-start(bf16[144,512]{1,0:T(8,128)(2,1)S(1)} %shard_map.64.refs_5_.refs_15_), channel_id=1, source_target_pairs={{0,1},{1,0},{2,3},{3,2},{4,5},{5,4},{6,7},{7,6},{8,9},{9,8},{10,11... | collective-permute-start | bytes 442376 | tf_op jit(solution)/shard_map/ppermute | solution.py:25
  6.9 1.2 %collective-permute-start.4 = (bf16[144,512]{1,0:T(8,128)(2,1)S(1)}, bf16[144,512]{1,0:T(8,128)(2,1)S(1)}, u32[]{:S(2)}, u32[]{:S(2)}) collective-permute-start(bf16[144,512]{1,0:T(8,128)(2,1)S(1)} %shard_map.64.refs_5_.refs_15_), channel_id=1, source_target_pairs={{0,8},{4,12},{8,0},{12,4},{1,9},{5,13},{9,1},{13,5},{2,10},{6,14},... | collective-permute-start | bytes 442376 | tf_op jit(solution)/shard_map/ppermute | solution.py:25
  8.1 2.6 %collective-permute-start.12 = (bf16[128,1024]{1,0:T(8,128)(2,1)}, bf16[128,1024]{1,0:T(8,128)(2,1)S(1)}, u32[]{:S(2)}, u32[]{:S(2)}) collective-permute-start(bf16[128,1024]{1,0:T(8,128)(2,1)} %query_ref.1), channel_id=1, source_target_pairs={{0,2},{1,3},{2,0},{3,1},{4,6},{5,7},{6,4},{7,5},{8,10},{9,11},{10,... | collective-permute-start | bytes 786440 | tf_op jit(solution)/shard_map/ppermute | solution.py:25
  10.7 1.8 %collective-permute-done.3.refs_2_ = bf16[128,1024]{1,0:T(8,128)(2,1)S(1)} collective-permute-done((bf16[128,1024]{1,0:T(8,128)(2,1)}, bf16[128,1024]{1,0:T(8,128)(2,1)S(1)}, u32[]{:S(2)}, u32[]{:S(2)}) %collective-permute-start.3) | collective-permute-done | bytes 262176 | tf_op jit(solution)/shard_map/ppermute | solution.py:25
  12.5 4.9 %collective-permute-start.10 = (bf16[128,1024]{1,0:T(8,128)(2,1)S(1)}, bf16[128,1024]{1,0:T(8,128)(2,1)S(1)}, u32[]{:S(2)}, u32[]{:S(2)}) collective-permute-start(bf16[128,1024]{1,0:T(8,128)(2,1)S(1)} %collective-permute-done.refs_0_), channel_id=1, source_target_pairs={{0,8},{4,12},{8,0},{12,4},{1,9},{5,13},{9,1},{13,5},{2,10},{6,14},... | collective-permute-start | bytes 786440 | tf_op jit(solution)/shard_map/ppermute | solution.py:25
  17.3 0.3 collective-permute-done.2.refs_1_
  17.6 0.0 collective-permute-done.4.refs_3_
  17.6 2.6 %collective-permute-start.11 = (bf16[144,512]{1,0:T(8,128)(2,1)S(1)}, bf16[144,512]{1,0:T(8,128)(2,1)S(1)}, u32[]{:S(2)}, u32[]{:S(2)}) collective-permute-start(bf16[144,512]{1,0:T(8,128)(2,1)S(1)} %collective-permute-done.2.refs_1_), channel_id=1, source_target_pairs={{0,8},{4,12},{8,0},{12,4},{1,9},{5,13},{9,1},{13,5},{2,10},{6,14},... | collective-permute-start | bytes 442376 | tf_op jit(solution)/shard_map/ppermute | solution.py:25
  20.2 0.0 collective-permute-start.5
  20.2 0.5 %collective-permute-start.7 = (bf16[144,512]{1,0:T(8,128)(2,1)S(1)}, bf16[144,512]{1,0:T(8,128)(2,1)S(1)}, u32[]{:S(2)}, u32[]{:S(2)}) collective-permute-start(bf16[144,512]{1,0:T(8,128)(2,1)S(1)} %collective-permute-done.2.refs_1_), channel_id=1, source_target_pairs={{0,4},{4,0},{8,12},{12,8},{1,5},{5,1},{9,13},{13,9},{2,6},{6,2},{1... | collective-permute-start | bytes 442376 | tf_op jit(solution)/shard_map/ppermute | solution.py:25
  20.8 0.1 copy.8.lists_ref
  20.8 1.8 %collective-permute-done.12.query_ref = bf16[128,1024]{1,0:T(8,128)(2,1)S(1)} collective-permute-done((bf16[128,1024]{1,0:T(8,128)(2,1)}, bf16[128,1024]{1,0:T(8,128)(2,1)S(1)}, u32[]{:S(2)}, u32[]{:S(2)}) %collective-permute-start.12) | collective-permute-done | bytes 262176 | tf_op jit(solution)/shard_map/ppermute | solution.py:25
  22.7 0.8 %shard_map.65 = (f32[128,512]{1,0:T(8,128)S(1)}, f32[128,128]{1,0:T(8,128)S(1)}, f32[128,128]{1,0:T(8,128)S(1)}) custom-call(s32[16,4]{1,0:T(8,128)S(1)} %copy.8.lists_ref, s32[16]{0:T(128)S(1)} %copy-done.3, bf16[128,1024]{1,0:T(8,128)(2,1)S(1)} %collective-permute-done.12.query_ref, bf16[128,1024]{1,0:T(8,128)(2,1)S(1)} %collective-permute-done.refs_0_, ...), custom_call_target="tpu_custom_call" | custom-call | flops 268435456 | bytes 4194304 | tf_op jit(solution)/shard_map/pallas_call | solution.py:264
  23.5 0.6 %collective-permute-start.8 = (bf16[128,1024]{1,0:T(8,128)(2,1)S(1)}, bf16[128,1024]{1,0:T(8,128)(2,1)S(1)}, u32[]{:S(2)}, u32[]{:S(2)}) collective-permute-start(bf16[128,1024]{1,0:T(8,128)(2,1)S(1)} %collective-permute-done.3.refs_2_), channel_id=1, source_target_pairs={{0,4},{4,0},{8,12},{12,8},{1,5},{5,1},{9,13},{13,9},{2,6},{6,2},{1... | collective-permute-start | bytes 786440 | tf_op jit(solution)/shard_map/ppermute | solution.py:25
  24.1 0.8 %collective-permute-done.11.refs_11_.refs_10_ = bf16[144,512]{1,0:T(8,128)(2,1)S(1)} collective-permute-done((bf16[144,512]{1,0:T(8,128)(2,1)S(1)}, bf16[144,512]{1,0:T(8,128)(2,1)S(1)}, u32[]{:S(2)}, u32[]{:S(2)}) %collective-permute-start.11) | collective-permute-done | bytes 147488 | tf_op jit(solution)/shard_map/ppermute | solution.py:25
  24.9 0.5 %collective-permute-start.9 = (bf16[144,512]{1,0:T(8,128)(2,1)S(1)}, bf16[144,512]{1,0:T(8,128)(2,1)S(1)}, u32[]{:S(2)}, u32[]{:S(2)}) collective-permute-start(bf16[144,512]{1,0:T(8,128)(2,1)S(1)} %collective-permute-done.4.refs_3_), channel_id=1, source_target_pairs={{0,4},{4,0},{8,12},{12,8},{1,5},{5,1},{9,13},{13,9},{2,6},{6,2},{1... | collective-permute-start | bytes 442376 | tf_op jit(solution)/shard_map/ppermute | solution.py:25
  25.4 0.1 collective-permute-start.14
  25.4 1.2 %collective-permute-done.9.refs_9_.refs_8_ = bf16[144,512]{1,0:T(8,128)(2,1)S(1)} collective-permute-done((bf16[144,512]{1,0:T(8,128)(2,1)S(1)}, bf16[144,512]{1,0:T(8,128)(2,1)S(1)}, u32[]{:S(2)}, u32[]{:S(2)}) %collective-permute-start.9) | collective-permute-done | bytes 147488 | tf_op jit(solution)/shard_map/ppermute | solution.py:25
  26.6 0.2 collective-permute-done.14.refs_13_.refs_12_
  26.8 1.5 %shard_map.67 = bf16[144,512]{1,0:T(8,128)(2,1)S(1)} custom-call(s32[16,4]{1,0:T(8,128)S(1)} %copy.8.lists_ref, s32[16]{0:T(128)S(1)} %copy-done.3, bf16[128,1024]{1,0:T(8,128)(2,1)S(1)} %collective-permute-done.12.query_ref, f32[128,512]{1,0:T(8,128)S(1)} %get-tuple-element.33.refs_0_, f32[128,128]{1,0:T(8,128)S(1)} %get-tuple-element.34.refs_1_, ...), custom_call_target="tpu_custom_call" | custom-call | flops 268435456 | bytes 4194304 | tf_op jit(solution)/shard_map/pallas_call | solution.py:279
  28.4 1.4 %collective-permute-start.15 = (bf16[144,512]{1,0:T(8,128)(2,1)S(1)}, bf16[144,512]{1,0:T(8,128)(2,1)S(1)}, u32[]{:S(2)}, u32[]{:S(2)}) collective-permute-start(bf16[144,512]{1,0:T(8,128)(2,1)S(1)} %shard_map.67), channel_id=1, source_target_pairs={{0,2},{1,3},{2,0},{3,1},{4,6},{5,7},{6,4},{7,5},{8,10},{9,11},{10,... | collective-permute-start | bytes 442376 | tf_op jit(solution)/shard_map/ppermute | solution.py:25
  29.8 1.0 %shard_map.66 = (f32[128,512]{1,0:T(8,128)S(1)}, f32[2,128,128]{2,1,0:T(8,128)S(1)}) custom-call(s32[16,4]{1,0:T(8,128)S(1)} %copy.8.lists_ref, s32[16]{0:T(128)S(1)} %copy-done.3, bf16[128,1024]{1,0:T(8,128)(2,1)S(1)} %copy-done.1, bf16[128,1024]{1,0:T(8,128)(2,1)S(1)} %collective-permute-done.refs_0_, bf16[144,512]{1,0:T(8,128)(2,1)S(1)} %collective-permute-done.2.refs_1_, ...), custom_call_target="tpu_custom_call" | custom-call | flops 268435456 | bytes 4194304 | tf_op jit(solution)/shard_map/pallas_call | solution.py:294
  30.8 6.6 %collective-permute-done.15.refs_0_ = bf16[144,512]{1,0:T(8,128)(2,1)S(1)} collective-permute-done((bf16[144,512]{1,0:T(8,128)(2,1)S(1)}, bf16[144,512]{1,0:T(8,128)(2,1)S(1)}, u32[]{:S(2)}, u32[]{:S(2)}) %collective-permute-start.15) | collective-permute-done | bytes 147488 | tf_op jit(solution)/shard_map/ppermute | solution.py:25
  37.3 0.8 %shard_map.68 = bf16[128,512]{1,0:T(8,128)(2,1)} custom-call(f32[128,512]{1,0:T(8,128)S(1)} %get-tuple-element.31.total_ref, f32[2,128,128]{2,1,0:T(8,128)S(1)} %get-tuple-element.32.stats_ref, bf16[144,512]{1,0:T(8,128)(2,1)S(1)} %collective-permute-done.15.refs_0_), custom_call_target="tpu_custom_call" | custom-call | tf_op jit(solution)/shard_map/pallas_call | solution.py:308
  (18 shorter events, 0.0 us)
Async XLA Ops:
  0.0 22.7 %copy-start = (bf16[128,1024]{1,0:T(8,128)(2,1)S(1)}, bf16[128,1024]{1,0:T(8,128)(2,1)}, u32[]{:S(2)}) copy-start(bf16[128,1024]{1,0:T(8,128)(2,1)} %refs_14_.1) | copy-start | bytes 786436
  0.0 4.6 %collective-permute-start.1 = (bf16[128,1024]{1,0:T(8,128)(2,1)}, bf16[128,1024]{1,0:T(8,128)(2,1)S(1)}, u32[]{:S(2)}, u32[]{:S(2)}) collective-permute-start(bf16[128,1024]{1,0:T(8,128)(2,1)} %refs_14_.1), channel_id=1, source_target_pairs={{0,4},{4,0},{8,12},{12,8},{1,5},{5,1},{9,13},{13,9},{2,6},{6,2},{1... | collective-permute-start | bytes 786440 | tf_op jit(solution)/shard_map/ppermute | solution.py:25
  0.5 10.2 %collective-permute-start = (bf16[128,1024]{1,0:T(8,128)(2,1)}, bf16[128,1024]{1,0:T(8,128)(2,1)S(1)}, u32[]{:S(2)}, u32[]{:S(2)}) collective-permute-start(bf16[128,1024]{1,0:T(8,128)(2,1)} %refs_14_.1), channel_id=1, source_target_pairs={{0,1},{1,0},{2,3},{3,2},{4,5},{5,4},{6,7},{7,6},{8,9},{9,8},{10,11... | collective-permute-start | bytes 786440 | tf_op jit(solution)/shard_map/ppermute | solution.py:25
  3.1 9.4 %collective-permute-start.3 = (bf16[128,1024]{1,0:T(8,128)(2,1)}, bf16[128,1024]{1,0:T(8,128)(2,1)S(1)}, u32[]{:S(2)}, u32[]{:S(2)}) collective-permute-start(bf16[128,1024]{1,0:T(8,128)(2,1)} %refs_14_.1), channel_id=1, source_target_pairs={{0,8},{4,12},{8,0},{12,4},{1,9},{5,13},{9,1},{13,5},{2,10},{6,14},... | collective-permute-start | bytes 786440 | tf_op jit(solution)/shard_map/ppermute | solution.py:25
  4.6 0.9 %copy-start.2 = (bf16[128,512]{1,0:T(8,128)(2,1)S(1)}, bf16[128,512]{1,0:T(8,128)(2,1)}, u32[]{:S(2)}) copy-start(bf16[128,512]{1,0:T(8,128)(2,1)} %values_ref) | copy-start | bytes 393220
  5.5 0.7 %copy-start.4 = (bf16[128]{0:T(256)(128)(2,1)S(1)}, bf16[128]{0:T(256)(128)(2,1)}, u32[]{:S(2)}) copy-start(bf16[128]{0:T(256)(128)(2,1)} %param.9) | copy-start | bytes 772
  6.1 14.6 %copy-start.5 = (s32[16,4]{0,1:T(4,128)S(1)}, s32[16,4]{0,1:T(4,128)}, u32[]{:S(2)}) copy-start(s32[16,4]{0,1:T(4,128)} %param.10) | copy-start | bytes 772
  6.3 16.3 %copy-start.3 = (s32[16]{0:T(128)S(1)}, s32[16]{0:T(128)}, u32[]{:S(2)}) copy-start(s32[16]{0:T(128)} %counts_ref.5) | copy-start | bytes 196
  6.3 11.3 %collective-permute-start.2 = (bf16[144,512]{1,0:T(8,128)(2,1)S(1)}, bf16[144,512]{1,0:T(8,128)(2,1)S(1)}, u32[]{:S(2)}, u32[]{:S(2)}) collective-permute-start(bf16[144,512]{1,0:T(8,128)(2,1)S(1)} %shard_map.64.refs_5_.refs_15_), channel_id=1, source_target_pairs={{0,1},{1,0},{2,3},{3,2},{4,5},{5,4},{6,7},{7,6},{8,9},{9,8},{10,11... | collective-permute-start | bytes 442376 | tf_op jit(solution)/shard_map/ppermute | solution.py:25
  6.9 10.8 %collective-permute-start.4 = (bf16[144,512]{1,0:T(8,128)(2,1)S(1)}, bf16[144,512]{1,0:T(8,128)(2,1)S(1)}, u32[]{:S(2)}, u32[]{:S(2)}) collective-permute-start(bf16[144,512]{1,0:T(8,128)(2,1)S(1)} %shard_map.64.refs_5_.refs_15_), channel_id=1, source_target_pairs={{0,8},{4,12},{8,0},{12,4},{1,9},{5,13},{9,1},{13,5},{2,10},{6,14},... | collective-permute-start | bytes 442376 | tf_op jit(solution)/shard_map/ppermute | solution.py:25
  8.1 14.6 %collective-permute-start.12 = (bf16[128,1024]{1,0:T(8,128)(2,1)}, bf16[128,1024]{1,0:T(8,128)(2,1)S(1)}, u32[]{:S(2)}, u32[]{:S(2)}) collective-permute-start(bf16[128,1024]{1,0:T(8,128)(2,1)} %query_ref.1), channel_id=1, source_target_pairs={{0,2},{1,3},{2,0},{3,1},{4,6},{5,7},{6,4},{7,5},{8,10},{9,11},{10,... | collective-permute-start | bytes 786440 | tf_op jit(solution)/shard_map/ppermute | solution.py:25
  12.5 11.0 %collective-permute-start.10 = (bf16[128,1024]{1,0:T(8,128)(2,1)S(1)}, bf16[128,1024]{1,0:T(8,128)(2,1)S(1)}, u32[]{:S(2)}, u32[]{:S(2)}) collective-permute-start(bf16[128,1024]{1,0:T(8,128)(2,1)S(1)} %collective-permute-done.refs_0_), channel_id=1, source_target_pairs={{0,8},{4,12},{8,0},{12,4},{1,9},{5,13},{9,1},{13,5},{2,10},{6,14},... | collective-permute-start | bytes 786440 | tf_op jit(solution)/shard_map/ppermute | solution.py:25
  17.6 7.2 %collective-permute-start.11 = (bf16[144,512]{1,0:T(8,128)(2,1)S(1)}, bf16[144,512]{1,0:T(8,128)(2,1)S(1)}, u32[]{:S(2)}, u32[]{:S(2)}) collective-permute-start(bf16[144,512]{1,0:T(8,128)(2,1)S(1)} %collective-permute-done.2.refs_1_), channel_id=1, source_target_pairs={{0,8},{4,12},{8,0},{12,4},{1,9},{5,13},{9,1},{13,5},{2,10},{6,14},... | collective-permute-start | bytes 442376 | tf_op jit(solution)/shard_map/ppermute | solution.py:25
  20.2 4.6 %collective-permute-start.5 = (bf16[144,512]{1,0:T(8,128)(2,1)S(1)}, bf16[144,512]{1,0:T(8,128)(2,1)S(1)}, u32[]{:S(2)}, u32[]{:S(2)}) collective-permute-start(bf16[144,512]{1,0:T(8,128)(2,1)S(1)} %shard_map.64.refs_5_.refs_15_), channel_id=1, source_target_pairs={{0,4},{4,0},{8,12},{12,8},{1,5},{5,1},{9,13},{13,9},{2,6},{6,2},{1... | collective-permute-start | bytes 442376 | tf_op jit(solution)/shard_map/ppermute | solution.py:25
  20.2 5.1 %collective-permute-start.7 = (bf16[144,512]{1,0:T(8,128)(2,1)S(1)}, bf16[144,512]{1,0:T(8,128)(2,1)S(1)}, u32[]{:S(2)}, u32[]{:S(2)}) collective-permute-start(bf16[144,512]{1,0:T(8,128)(2,1)S(1)} %collective-permute-done.2.refs_1_), channel_id=1, source_target_pairs={{0,4},{4,0},{8,12},{12,8},{1,5},{5,1},{9,13},{13,9},{2,6},{6,2},{1... | collective-permute-start | bytes 442376 | tf_op jit(solution)/shard_map/ppermute | solution.py:25
  22.6 4.0 %collective-permute-start.6 = (bf16[128,1024]{1,0:T(8,128)(2,1)S(1)}, bf16[128,1024]{1,0:T(8,128)(2,1)S(1)}, u32[]{:S(2)}, u32[]{:S(2)}) collective-permute-start(bf16[128,1024]{1,0:T(8,128)(2,1)S(1)} %collective-permute-done.refs_0_), channel_id=1, source_target_pairs={{0,4},{4,0},{8,12},{12,8},{1,5},{5,1},{9,13},{13,9},{2,6},{6,2},{1... | collective-permute-start | bytes 786440 | tf_op jit(solution)/shard_map/ppermute | solution.py:25
  23.5 3.1 %collective-permute-start.8 = (bf16[128,1024]{1,0:T(8,128)(2,1)S(1)}, bf16[128,1024]{1,0:T(8,128)(2,1)S(1)}, u32[]{:S(2)}, u32[]{:S(2)}) collective-permute-start(bf16[128,1024]{1,0:T(8,128)(2,1)S(1)} %collective-permute-done.3.refs_2_), channel_id=1, source_target_pairs={{0,4},{4,0},{8,12},{12,8},{1,5},{5,1},{9,13},{13,9},{2,6},{6,2},{1... | collective-permute-start | bytes 786440 | tf_op jit(solution)/shard_map/ppermute | solution.py:25
  24.9 2.0 %collective-permute-start.13 = (bf16[128,1024]{1,0:T(8,128)(2,1)S(1)}, bf16[128,1024]{1,0:T(8,128)(2,1)S(1)}, u32[]{:S(2)}, u32[]{:S(2)}) collective-permute-start(bf16[128,1024]{1,0:T(8,128)(2,1)S(1)} %collective-permute-done.10.refs_10_.refs_9_), channel_id=1, source_target_pairs={{0,4},{4,0},{8,12},{12,8},{1,5},{5,1},{9,13},{13,9},{2,6},{6,2},{1... | collective-permute-start | bytes 786440 | tf_op jit(solution)/shard_map/ppermute | solution.py:25
  24.9 1.7 %collective-permute-start.9 = (bf16[144,512]{1,0:T(8,128)(2,1)S(1)}, bf16[144,512]{1,0:T(8,128)(2,1)S(1)}, u32[]{:S(2)}, u32[]{:S(2)}) collective-permute-start(bf16[144,512]{1,0:T(8,128)(2,1)S(1)} %collective-permute-done.4.refs_3_), channel_id=1, source_target_pairs={{0,4},{4,0},{8,12},{12,8},{1,5},{5,1},{9,13},{13,9},{2,6},{6,2},{1... | collective-permute-start | bytes 442376 | tf_op jit(solution)/shard_map/ppermute | solution.py:25
  25.4 1.4 %collective-permute-start.14 = (bf16[144,512]{1,0:T(8,128)(2,1)S(1)}, bf16[144,512]{1,0:T(8,128)(2,1)S(1)}, u32[]{:S(2)}, u32[]{:S(2)}) collective-permute-start(bf16[144,512]{1,0:T(8,128)(2,1)S(1)} %collective-permute-done.11.refs_11_.refs_10_), channel_id=1, source_target_pairs={{0,4},{4,0},{8,12},{12,8},{1,5},{5,1},{9,13},{13,9},{2,6},{6,2},{1... | collective-permute-start | bytes 442376 | tf_op jit(solution)/shard_map/ppermute | solution.py:25
  26.8 2.9 %copy-start.1 = (bf16[128,1024]{1,0:T(8,128)(2,1)S(1)}, bf16[128,1024]{1,0:T(8,128)(2,1)}, u32[]{:S(2)}) copy-start(bf16[128,1024]{1,0:T(8,128)(2,1)} %query_ref.1) | copy-start | bytes 786436
  28.4 9.0 %collective-permute-start.15 = (bf16[144,512]{1,0:T(8,128)(2,1)S(1)}, bf16[144,512]{1,0:T(8,128)(2,1)S(1)}, u32[]{:S(2)}, u32[]{:S(2)}) collective-permute-start(bf16[144,512]{1,0:T(8,128)(2,1)S(1)} %shard_map.67), channel_id=1, source_target_pairs={{0,2},{1,3},{2,0},{3,1},{4,6},{5,7},{6,4},{7,5},{8,10},{9,11},{10,... | collective-permute-start | bytes 442376 | tf_op jit(solution)/shard_map/ppermute | solution.py:25

commit v9 on v7

--- a/solution.py
+++ b/solution.py
@@ -194,7 +194,7 @@
         out_ref[:, at : at + LANES] = merged.astype(jnp.bfloat16)
 
 
-def gather_library(keys, values, queries, masks):
+def gather_library(keys, partner_keys, values, queries, masks):
     steps = [("qry", 1)]
     mask = lax.axis_size("lib") // 2
     while mask > 1:
@@ -205,7 +205,8 @@
     early, late = [], []
     for axis, mask in steps:
         place = (0, mask) if axis == "qry" else (mask, 0)
-        near = (place, swap(keys, axis, mask), swap(values, axis, mask))
+        leaving_keys = tie(keys, partner_keys)[0] if axis == "qry" else keys
+        near = (place, swap(leaving_keys, axis, mask), swap(values, axis, mask))
         relayed = []
         for (lib_mask, qry_mask), far_keys, far_values in early + late:
             far_keys, *_ = tie(far_keys, near[1], values)
@@ -249,7 +250,7 @@
     )(own_values, key_scale.reshape(1, TILE))
 
     masks = [2 * at + 1 for at in range(1, qry_count // 2)]
-    early, relayed, visitors = gather_library(library_keys, values, queries, masks)
+    early, relayed, visitors = gather_library(library_keys, partner_keys, values, queries, masks)
     piece_rows = (width // value_width + 1) * TILE + EXTRA
     cost = pl.CostEstimate(flops=2 * TILE * 4 * TILE * width * 2, bytes_accessed=4 * 1024 * 1024, transcendentals=0)
     total_shape = jax.ShapeDtypeStruct((TILE, value_width), jnp.float32)
@@ -258,21 +259,23 @@
     attend_params = params(pieces_total * piece_rows * value_width * 2)
     own_specs = [pl.BlockSpec(memory_space=pl.ANY), VMEM]
     own_scratch = [pltpu.VMEM(library_keys.shape, library_keys.dtype), pltpu.SemaphoreType.DMA]
-    early_arrays = arrays_of(early)
+    near = early + cross_cores(early[:-1])
+    near_arrays = arrays_of(near)
     states = []
     for mask, visiting in visitors:
         state = pl.pallas_call(
-            functools.partial(early_kernel, places_of(early), mask),
+            functools.partial(early_kernel, places_of(near), mask),
             out_shape=(total_shape, line_shape, line_shape),
-            in_specs=[SMEM, SMEM] + [VMEM] * (1 + len(early_arrays)) + own_specs,
+            in_specs=[SMEM, SMEM] + [VMEM] * (1 + len(near_arrays)) + own_specs,
             out_specs=(VMEM,) * 3,
-            scratch_shapes=[pltpu.VMEM((len(early) + 1, TILE, TILE), jnp.float32)] + own_scratch,
+            scratch_shapes=[pltpu.VMEM((len(near) + 1, TILE, TILE), jnp.float32)] + own_scratch,
             compiler_params=attend_params,
             cost_estimate=cost,
-        )(block_list, block_count, visiting, *early_arrays, library_keys, values)
+        )(block_list, block_count, visiting, *near_arrays, library_keys, values)
         states.append(state)
 
-    late = [((1, 0), partner_keys, swap(values, "lib", 1))] + cross_cores(early) + relayed + cross_cores(relayed, [state[2] for state in states])
+    late = [((1, 0), partner_keys, swap(values, "lib", 1))] + cross_cores(early[-1:]) + relayed
+    late += cross_cores(relayed, [state[2] for state in states])
     late_arrays = arrays_of(late)
     returned = []
     for (mask, visiting), state in zip(visitors, states):
@@ -292,9 +295,9 @@
         returned.append(swap(packed, "qry", mask))
 
     total, stats = pl.pallas_call(
-        functools.partial(home_kernel, places_of(early + late)),
+        functools.partial(home_kernel, places_of(near + late)),
         out_shape=(total_shape, jax.ShapeDtypeStruct((2, TILE, LANES), jnp.float32)),
-        in_specs=[SMEM, SMEM] + [VMEM] * (1 + len(early_arrays) + len(late_arrays)) + own_specs,
+        in_specs=[SMEM, SMEM] + [VMEM] * (1 + len(near_arrays) + len(late_arrays)) + own_specs,
         out_specs=(VMEM, VMEM),
         scratch_shapes=[
             pltpu.VMEM((pieces_total, TILE, TILE), jnp.float32),
@@ -303,7 +306,7 @@
         + own_scratch,
         compiler_params=attend_params,
         cost_estimate=cost,
-    )(block_list, block_count, queries, *early_arrays, *late_arrays, library_keys, values)
+    )(block_list, block_count, queries, *near_arrays, *late_arrays, library_keys, values)
 
     return pl.pallas_call(
         merge_kernel,

time: 36.3 us -> 44.5 us (1.23)
  starting transfers between devices: 17.8 us -> 22.3 us
  waiting for transfers between devices: 11.6 us -> 15.1 us
    ppermute x16, starting transfers between devices: 17.8 us -> 22.3 us  [swap(): return lax.ppermute(value, axis, [(i, i ^ mask) for i in range(length)])]
    ppermute x16, waiting for transfers between devices: 11.6 us -> 15.1 us  [swap(): return lax.ppermute(value, axis, [(i, i ^ mask) for i in range(length)])]
    pallas_call x1, Pallas kernels: 1.03 us -> 1.51 us  [body(): pl.pallas_call(functools.partial(late_kernel, places_of(late), mask), out...]
  transfers between devices with their start and end apart: 16 -> 16, of which waited for: 7 -> 8; matrix products, arithmetic and copies ran while one was open for 0% -> 0% of each run, Pallas kernels for 9% -> 6%
where the time goes in v9:
time: 44.5 us; the launch traced here: 44.3 us
  starting transfers between devices  22.3 us (50%)
  waiting for transfers between devices  15.1 us (34%)
  Pallas kernels  5.19 us (12%)
  local copies, waits for them, and re-layouts  1.66 us (4%)
    ppermute x16, starting transfers between devices, swap(): return lax.ppermute(value, axis, [(i, i ^ mask) for i in range(length)])  22.3 us
    ppermute x16, waiting for transfers between devices, swap(): return lax.ppermute(value, axis, [(i, i ^ mask) for i in range(length)])  15.1 us
    unnamed x13, local copies, waits for them, and re-layouts  1.66 us
    pallas_call x1, Pallas kernels, body(): pl.pallas_call(functools.partial(late_kernel, places_of(late), mask), out...  1.51 us
    pallas_call x1, Pallas kernels, body(): pl.pallas_call(functools.partial(home_kernel, places_of(near + late)), ou...  1.42 us
    pallas_call x1, Pallas kernels, body(): pl.pallas_call(functools.partial(early_kernel, places_of(near), mask), ou...  1.28 us
  transfers between devices with their start and end apart: 16, of which 8 were waited for; matrix products, arithmetic and copies ran while one was open for 0% of the time, Pallas kernels for 6%

profile of v9, /device:TPU:0, one launch (start us, length us, event | category | flops | bytes accessed | tf_op | source)
XLA Modules:
  0.0 44.3 jit_solution(15048891211706257892)
XLA Ops:
  0.0 0.5 %collective-permute-start = (bf16[128,1024]{1,0:T(8,128)(2,1)}, bf16[128,1024]{1,0:T(8,128)(2,1)S(1)}, u32[]{:S(2)}, u32[]{:S(2)}) collective-permute-start(bf16[128,1024]{1,0:T(8,128)(2,1)} %refs_14_.1), channel_id=1, source_target_pairs={{0,4},{4,0},{8,12},{12,8},{1,5},{5,1},{9,13},{13,9},{2,6},{6,2},{1... | collective-permute-start | bytes 786440 | tf_op jit(solution)/shard_map/ppermute | solution.py:25
  0.5 1.4 %collective-permute-done.refs_6_.refs_3_ = bf16[128,1024]{1,0:T(8,128)(2,1)S(1)} collective-permute-done((bf16[128,1024]{1,0:T(8,128)(2,1)}, bf16[128,1024]{1,0:T(8,128)(2,1)S(1)}, u32[]{:S(2)}, u32[]{:S(2)}) %collective-permute-start) | collective-permute-done | bytes 262176 | tf_op jit(solution)/shard_map/ppermute | solution.py:25
  1.8 2.9 %collective-permute-start.1 = (bf16[128,1024]{1,0:T(8,128)(2,1)}, bf16[128,1024]{1,0:T(8,128)(2,1)S(1)}, u32[]{:S(2)}, u32[]{:S(2)}) collective-permute-start(bf16[128,1024]{1,0:T(8,128)(2,1)} %refs_14_.1), channel_id=1, source_target_pairs={{0,1},{1,0},{2,3},{3,2},{4,5},{5,4},{6,7},{7,6},{8,9},{9,8},{10,11... | collective-permute-start | bytes 786440 | tf_op jit(solution)/shard_map/ppermute | solution.py:25
  4.8 1.5 %collective-permute-start.3 = (bf16[128,1024]{1,0:T(8,128)(2,1)}, bf16[128,1024]{1,0:T(8,128)(2,1)S(1)}, u32[]{:S(2)}, u32[]{:S(2)}) collective-permute-start(bf16[128,1024]{1,0:T(8,128)(2,1)} %refs_14_.1), channel_id=1, source_target_pairs={{0,8},{4,12},{8,0},{12,4},{1,9},{5,13},{9,1},{13,5},{2,10},{6,14},... | collective-permute-start | bytes 786440 | tf_op jit(solution)/shard_map/ppermute | solution.py:25
  6.3 0.9 %copy-done.2 = bf16[128,512]{1,0:T(8,128)(2,1)S(1)} copy-done((bf16[128,512]{1,0:T(8,128)(2,1)S(1)}, bf16[128,512]{1,0:T(8,128)(2,1)}, u32[]{:S(2)}) %copy-start.2) | copy-done | bytes 131096
  7.2 0.7 %copy-done.4 = bf16[128]{0:T(256)(128)(2,1)S(1)} copy-done((bf16[128]{0:T(256)(128)(2,1)S(1)}, bf16[128]{0:T(256)(128)(2,1)}, u32[]{:S(2)}) %copy-start.4) | copy-done | bytes 280
  7.8 0.2 shard_map.64.refs_7_.refs_15_
  8.0 0.0 copy-start.3
  8.0 0.5 %collective-permute-start.2 = (bf16[144,512]{1,0:T(8,128)(2,1)S(1)}, bf16[144,512]{1,0:T(8,128)(2,1)S(1)}, u32[]{:S(2)}, u32[]{:S(2)}) collective-permute-start(bf16[144,512]{1,0:T(8,128)(2,1)S(1)} %shard_map.64.refs_7_.refs_15_), channel_id=1, source_target_pairs={{0,1},{1,0},{2,3},{3,2},{4,5},{5,4},{6,7},{7,6},{8,9},{9,8},{10,11... | collective-permute-start | bytes 442376 | tf_op jit(solution)/shard_map/ppermute | solution.py:25
  8.5 0.2 collective-permute-start.4
  8.7 4.0 %collective-permute-start.12 = (bf16[128,1024]{1,0:T(8,128)(2,1)}, bf16[128,1024]{1,0:T(8,128)(2,1)S(1)}, u32[]{:S(2)}, u32[]{:S(2)}) collective-permute-start(bf16[128,1024]{1,0:T(8,128)(2,1)} %query_ref.1), channel_id=1, source_target_pairs={{0,3},{1,2},{2,1},{3,0},{4,7},{5,6},{6,5},{7,4},{8,11},{9,10},{10,... | collective-permute-start | bytes 786440 | tf_op jit(solution)/shard_map/ppermute | solution.py:25
  12.7 2.1 %collective-permute-done.2.refs_1_ = bf16[144,512]{1,0:T(8,128)(2,1)S(1)} collective-permute-done((bf16[144,512]{1,0:T(8,128)(2,1)S(1)}, bf16[144,512]{1,0:T(8,128)(2,1)S(1)}, u32[]{:S(2)}, u32[]{:S(2)}) %collective-permute-start.2) | collective-permute-done | bytes 147488 | tf_op jit(solution)/shard_map/ppermute | solution.py:25
  14.8 0.0 collective-permute-done.3.refs_2_
  14.8 1.7 %collective-permute-start.10 = (bf16[128,1024]{1,0:T(8,128)(2,1)S(1)}, bf16[128,1024]{1,0:T(8,128)(2,1)S(1)}, u32[]{:S(2)}, u32[]{:S(2)}) collective-permute-start(bf16[128,1024]{1,0:T(8,128)(2,1)S(1)} %collective-permute-done.1.refs_0_), channel_id=1, source_target_pairs={{0,8},{4,12},{8,0},{12,4},{1,9},{5,13},{9,1},{13,5},{2,10},{6,14},... | collective-permute-start | bytes 786440 | tf_op jit(solution)/shard_map/ppermute | solution.py:25
  16.5 0.2 collective-permute-start.6
  16.6 0.0 collective-permute-done.4.refs_3_
  16.6 1.1 %collective-permute-start.11 = (bf16[144,512]{1,0:T(8,128)(2,1)S(1)}, bf16[144,512]{1,0:T(8,128)(2,1)S(1)}, u32[]{:S(2)}, u32[]{:S(2)}) collective-permute-start(bf16[144,512]{1,0:T(8,128)(2,1)S(1)} %collective-permute-done.2.refs_1_), channel_id=1, source_target_pairs={{0,8},{4,12},{8,0},{12,4},{1,9},{5,13},{9,1},{13,5},{2,10},{6,14},... | collective-permute-start | bytes 442376 | tf_op jit(solution)/shard_map/ppermute | solution.py:25
  17.7 0.1 copy.8.lists_ref
  17.8 4.9 %collective-permute-done.12.query_ref = bf16[128,1024]{1,0:T(8,128)(2,1)S(1)} collective-permute-done((bf16[128,1024]{1,0:T(8,128)(2,1)}, bf16[128,1024]{1,0:T(8,128)(2,1)S(1)}, u32[]{:S(2)}, u32[]{:S(2)}) %collective-permute-start.12) | collective-permute-done | bytes 262176 | tf_op jit(solution)/shard_map/ppermute | solution.py:25
  22.7 1.3 %shard_map.65 = (f32[128,512]{1,0:T(8,128)S(1)}, f32[128,128]{1,0:T(8,128)S(1)}, f32[128,128]{1,0:T(8,128)S(1)}) custom-call(s32[16,4]{1,0:T(8,128)S(1)} %copy.8.lists_ref, s32[16]{0:T(128)S(1)} %copy-done.3, bf16[128,1024]{1,0:T(8,128)(2,1)S(1)} %collective-permute-done.12.query_ref, bf16[128,1024]{1,0:T(8,128)(2,1)S(1)} %collective-permute-done.1.refs_0_, ...), custom_call_target="tpu_custom_call" | custom-call | flops 268435456 | bytes 4194304 | tf_op jit(solution)/shard_map/pallas_call | solution.py:266
  24.0 2.7 %collective-permute-done.11.refs_11_.refs_8_ = bf16[144,512]{1,0:T(8,128)(2,1)S(1)} collective-permute-done((bf16[144,512]{1,0:T(8,128)(2,1)S(1)}, bf16[144,512]{1,0:T(8,128)(2,1)S(1)}, u32[]{:S(2)}, u32[]{:S(2)}) %collective-permute-start.11) | collective-permute-done | bytes 147488 | tf_op jit(solution)/shard_map/ppermute | solution.py:25
  26.7 0.5 %collective-permute-start.7 = (bf16[144,512]{1,0:T(8,128)(2,1)S(1)}, bf16[144,512]{1,0:T(8,128)(2,1)S(1)}, u32[]{:S(2)}, u32[]{:S(2)}) collective-permute-start(bf16[144,512]{1,0:T(8,128)(2,1)S(1)} %shard_map.64.refs_7_.refs_15_), channel_id=1, source_target_pairs={{0,4},{4,0},{8,12},{12,8},{1,5},{5,1},{9,13},{13,9},{2,6},{6,2},{1... | collective-permute-start | bytes 442376 | tf_op jit(solution)/shard_map/ppermute | solution.py:25
  27.2 0.0 collective-permute-start.9
  27.2 0.5 %collective-permute-start.14 = (bf16[144,512]{1,0:T(8,128)(2,1)S(1)}, bf16[144,512]{1,0:T(8,128)(2,1)S(1)}, u32[]{:S(2)}, u32[]{:S(2)}) collective-permute-start(bf16[144,512]{1,0:T(8,128)(2,1)S(1)} %collective-permute-done.11.refs_11_.refs_8_), channel_id=1, source_target_pairs={{0,4},{4,0},{8,12},{12,8},{1,5},{5,1},{9,13},{13,9},{2,6},{6,2},{1... | collective-permute-start | bytes 442376 | tf_op jit(solution)/shard_map/ppermute | solution.py:25
  27.7 0.7 %collective-permute-done.7.refs_7_.refs_4_ = bf16[144,512]{1,0:T(8,128)(2,1)S(1)} collective-permute-done((bf16[144,512]{1,0:T(8,128)(2,1)S(1)}, bf16[144,512]{1,0:T(8,128)(2,1)S(1)}, u32[]{:S(2)}, u32[]{:S(2)}) %collective-permute-start.7) | collective-permute-done | bytes 147488 | tf_op jit(solution)/shard_map/ppermute | solution.py:25
  28.5 0.2 collective-permute-done.9.refs_9_.refs_6_
  28.7 0.2 collective-permute-done.14.refs_13_.refs_10_
  28.9 1.5 %shard_map.67 = bf16[144,512]{1,0:T(8,128)(2,1)S(1)} custom-call(s32[16,4]{1,0:T(8,128)S(1)} %copy.8.lists_ref, s32[16]{0:T(128)S(1)} %copy-done.3, bf16[128,1024]{1,0:T(8,128)(2,1)S(1)} %collective-permute-done.12.query_ref, f32[128,512]{1,0:T(8,128)S(1)} %get-tuple-element.35.refs_0_, f32[128,128]{1,0:T(8,128)S(1)} %get-tuple-element.36.refs_1_, ...), custom_call_target="tpu_custom_call" | custom-call | flops 268435456 | bytes 4194304 | tf_op jit(solution)/shard_map/pallas_call | solution.py:282
  30.4 8.9 %collective-permute-start.15 = (bf16[144,512]{1,0:T(8,128)(2,1)S(1)}, bf16[144,512]{1,0:T(8,128)(2,1)S(1)}, u32[]{:S(2)}, u32[]{:S(2)}) collective-permute-start(bf16[144,512]{1,0:T(8,128)(2,1)S(1)} %shard_map.67), channel_id=1, source_target_pairs={{0,3},{1,2},{2,1},{3,0},{4,7},{5,6},{6,5},{7,4},{8,11},{9,10},{10,... | collective-permute-start | bytes 442376 | tf_op jit(solution)/shard_map/ppermute | solution.py:25
  39.3 1.4 %shard_map.66 = (f32[128,512]{1,0:T(8,128)S(1)}, f32[2,128,128]{2,1,0:T(8,128)S(1)}) custom-call(s32[16,4]{1,0:T(8,128)S(1)} %copy.8.lists_ref, s32[16]{0:T(128)S(1)} %copy-done.3, bf16[128,1024]{1,0:T(8,128)(2,1)S(1)} %copy-done.1, bf16[128,1024]{1,0:T(8,128)(2,1)S(1)} %collective-permute-done.1.refs_0_, ...), custom_call_target="tpu_custom_call" | custom-call | flops 268435456 | bytes 4194304 | tf_op jit(solution)/shard_map/pallas_call | solution.py:297
  40.7 2.8 %collective-permute-done.15.refs_0_ = bf16[144,512]{1,0:T(8,128)(2,1)S(1)} collective-permute-done((bf16[144,512]{1,0:T(8,128)(2,1)S(1)}, bf16[144,512]{1,0:T(8,128)(2,1)S(1)}, u32[]{:S(2)}, u32[]{:S(2)}) %collective-permute-start.15) | collective-permute-done | bytes 147488 | tf_op jit(solution)/shard_map/ppermute | solution.py:25
  43.5 0.8 %shard_map.68 = bf16[128,512]{1,0:T(8,128)(2,1)} custom-call(f32[128,512]{1,0:T(8,128)S(1)} %get-tuple-element.33.total_ref, f32[2,128,128]{2,1,0:T(8,128)S(1)} %get-tuple-element.34.stats_ref, bf16[144,512]{1,0:T(8,128)(2,1)S(1)} %collective-permute-done.15.refs_0_), custom_call_target="tpu_custom_call" | custom-call | tf_op jit(solution)/shard_map/pallas_call | solution.py:311
  (18 shorter events, 0.0 us)
Async XLA Ops:
  0.0 22.7 %copy-start = (bf16[128,1024]{1,0:T(8,128)(2,1)S(1)}, bf16[128,1024]{1,0:T(8,128)(2,1)}, u32[]{:S(2)}) copy-start(bf16[128,1024]{1,0:T(8,128)(2,1)} %refs_14_.1) | copy-start | bytes 786436
  0.0 1.8 %collective-permute-start = (bf16[128,1024]{1,0:T(8,128)(2,1)}, bf16[128,1024]{1,0:T(8,128)(2,1)S(1)}, u32[]{:S(2)}, u32[]{:S(2)}) collective-permute-start(bf16[128,1024]{1,0:T(8,128)(2,1)} %refs_14_.1), channel_id=1, source_target_pairs={{0,4},{4,0},{8,12},{12,8},{1,5},{5,1},{9,13},{13,9},{2,6},{6,2},{1... | collective-permute-start | bytes 786440 | tf_op jit(solution)/shard_map/ppermute | solution.py:25
  1.8 13.0 %collective-permute-start.1 = (bf16[128,1024]{1,0:T(8,128)(2,1)}, bf16[128,1024]{1,0:T(8,128)(2,1)S(1)}, u32[]{:S(2)}, u32[]{:S(2)}) collective-permute-start(bf16[128,1024]{1,0:T(8,128)(2,1)} %refs_14_.1), channel_id=1, source_target_pairs={{0,1},{1,0},{2,3},{3,2},{4,5},{5,4},{6,7},{7,6},{8,9},{9,8},{10,11... | collective-permute-start | bytes 786440 | tf_op jit(solution)/shard_map/ppermute | solution.py:25
  4.8 10.0 %collective-permute-start.3 = (bf16[128,1024]{1,0:T(8,128)(2,1)}, bf16[128,1024]{1,0:T(8,128)(2,1)S(1)}, u32[]{:S(2)}, u32[]{:S(2)}) collective-permute-start(bf16[128,1024]{1,0:T(8,128)(2,1)} %refs_14_.1), channel_id=1, source_target_pairs={{0,8},{4,12},{8,0},{12,4},{1,9},{5,13},{9,1},{13,5},{2,10},{6,14},... | collective-permute-start | bytes 786440 | tf_op jit(solution)/shard_map/ppermute | solution.py:25
  6.3 0.9 %copy-start.2 = (bf16[128,512]{1,0:T(8,128)(2,1)S(1)}, bf16[128,512]{1,0:T(8,128)(2,1)}, u32[]{:S(2)}) copy-start(bf16[128,512]{1,0:T(8,128)(2,1)} %values_ref) | copy-start | bytes 393220
  7.2 0.7 %copy-start.4 = (bf16[128]{0:T(256)(128)(2,1)S(1)}, bf16[128]{0:T(256)(128)(2,1)}, u32[]{:S(2)}) copy-start(bf16[128]{0:T(256)(128)(2,1)} %param.9) | copy-start | bytes 772
  7.8 9.9 %copy-start.5 = (s32[16,4]{0,1:T(4,128)S(1)}, s32[16,4]{0,1:T(4,128)}, u32[]{:S(2)}) copy-start(s32[16,4]{0,1:T(4,128)} %param.10) | copy-start | bytes 772
  8.0 14.7 %copy-start.3 = (s32[16]{0:T(128)S(1)}, s32[16]{0:T(128)}, u32[]{:S(2)}) copy-start(s32[16]{0:T(128)} %counts_ref.5) | copy-start | bytes 196
  8.0 6.8 %collective-permute-start.2 = (bf16[144,512]{1,0:T(8,128)(2,1)S(1)}, bf16[144,512]{1,0:T(8,128)(2,1)S(1)}, u32[]{:S(2)}, u32[]{:S(2)}) collective-permute-start(bf16[144,512]{1,0:T(8,128)(2,1)S(1)} %shard_map.64.refs_7_.refs_15_), channel_id=1, source_target_pairs={{0,1},{1,0},{2,3},{3,2},{4,5},{5,4},{6,7},{7,6},{8,9},{9,8},{10,11... | collective-permute-start | bytes 442376 | tf_op jit(solution)/shard_map/ppermute | solution.py:25
  8.5 8.1 %collective-permute-start.4 = (bf16[144,512]{1,0:T(8,128)(2,1)S(1)}, bf16[144,512]{1,0:T(8,128)(2,1)S(1)}, u32[]{:S(2)}, u32[]{:S(2)}) collective-permute-start(bf16[144,512]{1,0:T(8,128)(2,1)S(1)} %shard_map.64.refs_7_.refs_15_), channel_id=1, source_target_pairs={{0,8},{4,12},{8,0},{12,4},{1,9},{5,13},{9,1},{13,5},{2,10},{6,14},... | collective-permute-start | bytes 442376 | tf_op jit(solution)/shard_map/ppermute | solution.py:25
  8.7 14.0 %collective-permute-start.12 = (bf16[128,1024]{1,0:T(8,128)(2,1)}, bf16[128,1024]{1,0:T(8,128)(2,1)S(1)}, u32[]{:S(2)}, u32[]{:S(2)}) collective-permute-start(bf16[128,1024]{1,0:T(8,128)(2,1)} %query_ref.1), channel_id=1, source_target_pairs={{0,3},{1,2},{2,1},{3,0},{4,7},{5,6},{6,5},{7,4},{8,11},{9,10},{10,... | collective-permute-start | bytes 786440 | tf_op jit(solution)/shard_map/ppermute | solution.py:25
  14.8 7.9 %collective-permute-start.5 = (bf16[128,1024]{1,0:T(8,128)(2,1)S(1)}, bf16[128,1024]{1,0:T(8,128)(2,1)S(1)}, u32[]{:S(2)}, u32[]{:S(2)}) collective-permute-start(bf16[128,1024]{1,0:T(8,128)(2,1)S(1)} %collective-permute-done.1.refs_0_), channel_id=1, source_target_pairs={{0,4},{4,0},{8,12},{12,8},{1,5},{5,1},{9,13},{13,9},{2,6},{6,2},{1... | collective-permute-start | bytes 786440 | tf_op jit(solution)/shard_map/ppermute | solution.py:25
  14.8 11.9 %collective-permute-start.10 = (bf16[128,1024]{1,0:T(8,128)(2,1)S(1)}, bf16[128,1024]{1,0:T(8,128)(2,1)S(1)}, u32[]{:S(2)}, u32[]{:S(2)}) collective-permute-start(bf16[128,1024]{1,0:T(8,128)(2,1)S(1)} %collective-permute-done.1.refs_0_), channel_id=1, source_target_pairs={{0,8},{4,12},{8,0},{12,4},{1,9},{5,13},{9,1},{13,5},{2,10},{6,14},... | collective-permute-start | bytes 786440 | tf_op jit(solution)/shard_map/ppermute | solution.py:25
  16.5 6.2 %collective-permute-start.6 = (bf16[144,512]{1,0:T(8,128)(2,1)S(1)}, bf16[144,512]{1,0:T(8,128)(2,1)S(1)}, u32[]{:S(2)}, u32[]{:S(2)}) collective-permute-start(bf16[144,512]{1,0:T(8,128)(2,1)S(1)} %collective-permute-done.2.refs_1_), channel_id=1, source_target_pairs={{0,4},{4,0},{8,12},{12,8},{1,5},{5,1},{9,13},{13,9},{2,6},{6,2},{1... | collective-permute-start | bytes 442376 | tf_op jit(solution)/shard_map/ppermute | solution.py:25
  16.6 10.1 %collective-permute-start.11 = (bf16[144,512]{1,0:T(8,128)(2,1)S(1)}, bf16[144,512]{1,0:T(8,128)(2,1)S(1)}, u32[]{:S(2)}, u32[]{:S(2)}) collective-permute-start(bf16[144,512]{1,0:T(8,128)(2,1)S(1)} %collective-permute-done.2.refs_1_), channel_id=1, source_target_pairs={{0,8},{4,12},{8,0},{12,4},{1,9},{5,13},{9,1},{13,5},{2,10},{6,14},... | collective-permute-start | bytes 442376 | tf_op jit(solution)/shard_map/ppermute | solution.py:25
  22.7 6.0 %collective-permute-start.8 = (bf16[128,1024]{1,0:T(8,128)(2,1)S(1)}, bf16[128,1024]{1,0:T(8,128)(2,1)S(1)}, u32[]{:S(2)}, u32[]{:S(2)}) collective-permute-start(bf16[128,1024]{1,0:T(8,128)(2,1)S(1)} %collective-permute-done.3.refs_2_), channel_id=1, source_target_pairs={{0,4},{4,0},{8,12},{12,8},{1,5},{5,1},{9,13},{13,9},{2,6},{6,2},{1... | collective-permute-start | bytes 786440 | tf_op jit(solution)/shard_map/ppermute | solution.py:25
  26.7 2.2 %collective-permute-start.13 = (bf16[128,1024]{1,0:T(8,128)(2,1)S(1)}, bf16[128,1024]{1,0:T(8,128)(2,1)S(1)}, u32[]{:S(2)}, u32[]{:S(2)}) collective-permute-start(bf16[128,1024]{1,0:T(8,128)(2,1)S(1)} %collective-permute-done.10.refs_10_.refs_7_), channel_id=1, source_target_pairs={{0,4},{4,0},{8,12},{12,8},{1,5},{5,1},{9,13},{13,9},{2,6},{6,2},{1... | collective-permute-start | bytes 786440 | tf_op jit(solution)/shard_map/ppermute | solution.py:25
  26.7 1.7 %collective-permute-start.7 = (bf16[144,512]{1,0:T(8,128)(2,1)S(1)}, bf16[144,512]{1,0:T(8,128)(2,1)S(1)}, u32[]{:S(2)}, u32[]{:S(2)}) collective-permute-start(bf16[144,512]{1,0:T(8,128)(2,1)S(1)} %shard_map.64.refs_7_.refs_15_), channel_id=1, source_target_pairs={{0,4},{4,0},{8,12},{12,8},{1,5},{5,1},{9,13},{13,9},{2,6},{6,2},{1... | collective-permute-start | bytes 442376 | tf_op jit(solution)/shard_map/ppermute | solution.py:25
  27.2 1.4 %collective-permute-start.9 = (bf16[144,512]{1,0:T(8,128)(2,1)S(1)}, bf16[144,512]{1,0:T(8,128)(2,1)S(1)}, u32[]{:S(2)}, u32[]{:S(2)}) collective-permute-start(bf16[144,512]{1,0:T(8,128)(2,1)S(1)} %collective-permute-done.4.refs_3_), channel_id=1, source_target_pairs={{0,4},{4,0},{8,12},{12,8},{1,5},{5,1},{9,13},{13,9},{2,6},{6,2},{1... | collective-permute-start | bytes 442376 | tf_op jit(solution)/shard_map/ppermute | solution.py:25
  27.2 1.7 %collective-permute-start.14 = (bf16[144,512]{1,0:T(8,128)(2,1)S(1)}, bf16[144,512]{1,0:T(8,128)(2,1)S(1)}, u32[]{:S(2)}, u32[]{:S(2)}) collective-permute-start(bf16[144,512]{1,0:T(8,128)(2,1)S(1)} %collective-permute-done.11.refs_11_.refs_8_), channel_id=1, source_target_pairs={{0,4},{4,0},{8,12},{12,8},{1,5},{5,1},{9,13},{13,9},{2,6},{6,2},{1... | collective-permute-start | bytes 442376 | tf_op jit(solution)/shard_map/ppermute | solution.py:25
  28.9 10.4 %copy-start.1 = (bf16[128,1024]{1,0:T(8,128)(2,1)S(1)}, bf16[128,1024]{1,0:T(8,128)(2,1)}, u32[]{:S(2)}) copy-start(bf16[128,1024]{1,0:T(8,128)(2,1)} %query_ref.1) | copy-start | bytes 786436
  30.4 13.1 %collective-permute-start.15 = (bf16[144,512]{1,0:T(8,128)(2,1)S(1)}, bf16[144,512]{1,0:T(8,128)(2,1)S(1)}, u32[]{:S(2)}, u32[]{:S(2)}) collective-permute-start(bf16[144,512]{1,0:T(8,128)(2,1)S(1)} %shard_map.67), channel_id=1, source_target_pairs={{0,3},{1,2},{2,1},{3,0},{4,7},{5,6},{6,5},{7,4},{8,11},{9,10},{10,... | collective-permute-start | bytes 442376 | tf_op jit(solution)/shard_map/ppermute | solution.py:25

commit v10 on v7

--- a/solution.py
+++ b/solution.py
@@ -194,7 +194,7 @@
         out_ref[:, at : at + LANES] = merged.astype(jnp.bfloat16)
 
 
-def gather_library(keys, values, queries, masks):
+def gather_library(keys, partner_keys, values, queries, masks):
     steps = [("qry", 1)]
     mask = lax.axis_size("lib") // 2
     while mask > 1:
@@ -205,7 +205,8 @@
     early, late = [], []
     for axis, mask in steps:
         place = (0, mask) if axis == "qry" else (mask, 0)
-        near = (place, swap(keys, axis, mask), swap(values, axis, mask))
+        leaving_keys = tie(keys, partner_keys)[0] if axis == "qry" else keys
+        near = (place, swap(leaving_keys, axis, mask), swap(values, axis, mask))
         relayed = []
         for (lib_mask, qry_mask), far_keys, far_values in early + late:
             far_keys, *_ = tie(far_keys, near[1], values)
@@ -249,7 +250,7 @@
     )(own_values, key_scale.reshape(1, TILE))
 
     masks = [2 * at + 1 for at in range(1, qry_count // 2)]
-    early, relayed, visitors = gather_library(library_keys, values, queries, masks)
+    early, relayed, visitors = gather_library(library_keys, partner_keys, values, queries, masks)
     piece_rows = (width // value_width + 1) * TILE + EXTRA
     cost = pl.CostEstimate(flops=2 * TILE * 4 * TILE * width * 2, bytes_accessed=4 * 1024 * 1024, transcendentals=0)
     total_shape = jax.ShapeDtypeStruct((TILE, value_width), jnp.float32)

time: 36.3 us -> 38.1 us (1.050)
  starting transfers between devices: 17.8 us -> 20.1 us
  waiting for transfers between devices: 11.6 us -> 10.9 us
    ppermute x16, starting transfers between devices: 17.8 us -> 20.1 us  [swap(): return lax.ppermute(value, axis, [(i, i ^ mask) for i in range(length)])]
    ppermute x16, waiting for transfers between devices: 11.6 us -> 10.9 us  [swap(): return lax.ppermute(value, axis, [(i, i ^ mask) for i in range(length)])]
    pallas_call x1, Pallas kernels: 1.26 us -> 1.7 us  [body(): pl.pallas_call(functools.partial(early_kernel, places_of(early), mask), o...]
    pallas_call x1, Pallas kernels: 1.84 us -> 1.44 us  [body(): pl.pallas_call(functools.partial(home_kernel, places_of(early + late)), o...]
  transfers between devices with their start and end apart: 16 -> 16, of which waited for: 7 -> 6; matrix products, arithmetic and copies ran while one was open for 0% -> 0% of each run, Pallas kernels for 9% -> 9%
where the time goes in v10:
time: 38.1 us; the launch traced here: 37.9 us
  starting transfers between devices  20.1 us (53%)
  waiting for transfers between devices  10.9 us (29%)
  Pallas kernels  5.15 us (14%)
  local copies, waits for them, and re-layouts  1.66 us (4%)
    ppermute x16, starting transfers between devices, swap(): return lax.ppermute(value, axis, [(i, i ^ mask) for i in range(length)])  20.1 us
    ppermute x16, waiting for transfers between devices, swap(): return lax.ppermute(value, axis, [(i, i ^ mask) for i in range(length)])  10.9 us
    pallas_call x1, Pallas kernels, body(): pl.pallas_call(functools.partial(early_kernel, places_of(early), mask), o...  1.7 us
    unnamed x13, local copies, waits for them, and re-layouts  1.66 us
    pallas_call x1, Pallas kernels, body(): pl.pallas_call(functools.partial(home_kernel, places_of(early + late)), o...  1.44 us
    pallas_call x1, Pallas kernels, body(): pl.pallas_call(functools.partial(late_kernel, places_of(late), mask), out...  1.03 us
    pallas_call x1, Pallas kernels, body(): pl.pallas_call(merge_kernel, out_shape=jax.ShapeDtypeStruct((TILE, value_...  0.81 us
  transfers between devices with their start and end apart: 16, of which 6 were waited for; matrix products, arithmetic and copies ran while one was open for 0% of the time, Pallas kernels for 9%

profile of v10, /device:TPU:0, one launch (start us, length us, event | category | flops | bytes accessed | tf_op | source)
XLA Modules:
  0.0 37.9 jit_solution(14881144460085748720)
XLA Ops:
  0.0 0.5 %collective-permute-start = (bf16[128,1024]{1,0:T(8,128)(2,1)}, bf16[128,1024]{1,0:T(8,128)(2,1)S(1)}, u32[]{:S(2)}, u32[]{:S(2)}) collective-permute-start(bf16[128,1024]{1,0:T(8,128)(2,1)} %refs_14_.1), channel_id=1, source_target_pairs={{0,4},{4,0},{8,12},{12,8},{1,5},{5,1},{9,13},{13,9},{2,6},{6,2},{1... | collective-permute-start | bytes 786440 | tf_op jit(solution)/shard_map/ppermute | solution.py:25
  0.5 2.5 %collective-permute-start.3 = (bf16[128,1024]{1,0:T(8,128)(2,1)}, bf16[128,1024]{1,0:T(8,128)(2,1)S(1)}, u32[]{:S(2)}, u32[]{:S(2)}) collective-permute-start(bf16[128,1024]{1,0:T(8,128)(2,1)} %refs_14_.1), channel_id=1, source_target_pairs={{0,8},{4,12},{8,0},{12,4},{1,9},{5,13},{9,1},{13,5},{2,10},{6,14},... | collective-permute-start | bytes 786440 | tf_op jit(solution)/shard_map/ppermute | solution.py:25
  3.0 1.8 %collective-permute-start.1 = (bf16[128,1024]{1,0:T(8,128)(2,1)}, bf16[128,1024]{1,0:T(8,128)(2,1)S(1)}, u32[]{:S(2)}, u32[]{:S(2)}) collective-permute-start(bf16[128,1024]{1,0:T(8,128)(2,1)} %refs_14_.1), channel_id=1, source_target_pairs={{0,1},{1,0},{2,3},{3,2},{4,5},{5,4},{6,7},{7,6},{8,9},{9,8},{10,11... | collective-permute-start | bytes 786440 | tf_op jit(solution)/shard_map/ppermute | solution.py:25
  4.8 0.9 %copy-done.2 = bf16[128,512]{1,0:T(8,128)(2,1)S(1)} copy-done((bf16[128,512]{1,0:T(8,128)(2,1)S(1)}, bf16[128,512]{1,0:T(8,128)(2,1)}, u32[]{:S(2)}) %copy-start.2) | copy-done | bytes 131096
  5.7 0.7 %copy-done.4 = bf16[128]{0:T(256)(128)(2,1)S(1)} copy-done((bf16[128]{0:T(256)(128)(2,1)S(1)}, bf16[128]{0:T(256)(128)(2,1)}, u32[]{:S(2)}) %copy-start.4) | copy-done | bytes 280
  6.3 0.2 shard_map.64.refs_5_.refs_15_
  6.5 0.0 copy-start.3
  6.5 0.3 collective-permute-start.2
  6.9 1.7 %collective-permute-start.4 = (bf16[144,512]{1,0:T(8,128)(2,1)S(1)}, bf16[144,512]{1,0:T(8,128)(2,1)S(1)}, u32[]{:S(2)}, u32[]{:S(2)}) collective-permute-start(bf16[144,512]{1,0:T(8,128)(2,1)S(1)} %shard_map.64.refs_5_.refs_15_), channel_id=1, source_target_pairs={{0,8},{4,12},{8,0},{12,4},{1,9},{5,13},{9,1},{13,5},{2,10},{6,14},... | collective-permute-start | bytes 442376 | tf_op jit(solution)/shard_map/ppermute | solution.py:25
  8.5 3.6 %collective-permute-start.12 = (bf16[128,1024]{1,0:T(8,128)(2,1)}, bf16[128,1024]{1,0:T(8,128)(2,1)S(1)}, u32[]{:S(2)}, u32[]{:S(2)}) collective-permute-start(bf16[128,1024]{1,0:T(8,128)(2,1)} %query_ref.1), channel_id=1, source_target_pairs={{0,3},{1,2},{2,1},{3,0},{4,7},{5,6},{6,5},{7,4},{8,11},{9,10},{10,... | collective-permute-start | bytes 786440 | tf_op jit(solution)/shard_map/ppermute | solution.py:25
  12.1 0.2 collective-permute-done.1.refs_0_
  12.4 1.7 %collective-permute-start.10 = (bf16[128,1024]{1,0:T(8,128)(2,1)S(1)}, bf16[128,1024]{1,0:T(8,128)(2,1)S(1)}, u32[]{:S(2)}, u32[]{:S(2)}) collective-permute-start(bf16[128,1024]{1,0:T(8,128)(2,1)S(1)} %collective-permute-done.1.refs_0_), channel_id=1, source_target_pairs={{0,8},{4,12},{8,0},{12,4},{1,9},{5,13},{9,1},{13,5},{2,10},{6,14},... | collective-permute-start | bytes 786440 | tf_op jit(solution)/shard_map/ppermute | solution.py:25
  14.0 0.8 %collective-permute-done.2.refs_1_ = bf16[144,512]{1,0:T(8,128)(2,1)S(1)} collective-permute-done((bf16[144,512]{1,0:T(8,128)(2,1)S(1)}, bf16[144,512]{1,0:T(8,128)(2,1)S(1)}, u32[]{:S(2)}, u32[]{:S(2)}) %collective-permute-start.2) | collective-permute-done | bytes 147488 | tf_op jit(solution)/shard_map/ppermute | solution.py:25
  14.8 0.0 collective-permute-done.4.refs_3_
  14.8 1.6 %collective-permute-start.11 = (bf16[144,512]{1,0:T(8,128)(2,1)S(1)}, bf16[144,512]{1,0:T(8,128)(2,1)S(1)}, u32[]{:S(2)}, u32[]{:S(2)}) collective-permute-start(bf16[144,512]{1,0:T(8,128)(2,1)S(1)} %collective-permute-done.2.refs_1_), channel_id=1, source_target_pairs={{0,8},{4,12},{8,0},{12,4},{1,9},{5,13},{9,1},{13,5},{2,10},{6,14},... | collective-permute-start | bytes 442376 | tf_op jit(solution)/shard_map/ppermute | solution.py:25
  16.4 0.5 %collective-permute-start.9 = (bf16[144,512]{1,0:T(8,128)(2,1)S(1)}, bf16[144,512]{1,0:T(8,128)(2,1)S(1)}, u32[]{:S(2)}, u32[]{:S(2)}) collective-permute-start(bf16[144,512]{1,0:T(8,128)(2,1)S(1)} %collective-permute-done.4.refs_3_), channel_id=1, source_target_pairs={{0,4},{4,0},{8,12},{12,8},{1,5},{5,1},{9,13},{13,9},{2,6},{6,2},{1... | collective-permute-start | bytes 442376 | tf_op jit(solution)/shard_map/ppermute | solution.py:25
  16.9 0.1 copy.8.lists_ref
  17.0 5.7 %collective-permute-done.12.query_ref = bf16[128,1024]{1,0:T(8,128)(2,1)S(1)} collective-permute-done((bf16[128,1024]{1,0:T(8,128)(2,1)}, bf16[128,1024]{1,0:T(8,128)(2,1)S(1)}, u32[]{:S(2)}, u32[]{:S(2)}) %collective-permute-start.12) | collective-permute-done | bytes 262176 | tf_op jit(solution)/shard_map/ppermute | solution.py:25
  22.7 0.0 collective-permute-start.8
  22.7 1.7 %shard_map.65 = (f32[128,512]{1,0:T(8,128)S(1)}, f32[128,128]{1,0:T(8,128)S(1)}, f32[128,128]{1,0:T(8,128)S(1)}) custom-call(s32[16,4]{1,0:T(8,128)S(1)} %copy.8.lists_ref, s32[16]{0:T(128)S(1)} %copy-done.3, bf16[128,1024]{1,0:T(8,128)(2,1)S(1)} %collective-permute-done.12.query_ref, bf16[128,1024]{1,0:T(8,128)(2,1)S(1)} %collective-permute-done.1.refs_0_, ...), custom_call_target="tpu_custom_call" | custom-call | flops 268435456 | bytes 4194304 | tf_op jit(solution)/shard_map/pallas_call | solution.py:265
  24.4 0.0 collective-permute-done.11.refs_11_.refs_10_
  24.4 0.1 collective-permute-start.6
  24.5 0.5 %collective-permute-start.13 = (bf16[128,1024]{1,0:T(8,128)(2,1)S(1)}, bf16[128,1024]{1,0:T(8,128)(2,1)S(1)}, u32[]{:S(2)}, u32[]{:S(2)}) collective-permute-start(bf16[128,1024]{1,0:T(8,128)(2,1)S(1)} %collective-permute-done.10.refs_10_.refs_9_), channel_id=1, source_target_pairs={{0,4},{4,0},{8,12},{12,8},{1,5},{5,1},{9,13},{13,9},{2,6},{6,2},{1... | collective-permute-start | bytes 786440 | tf_op jit(solution)/shard_map/ppermute | solution.py:25
  25.0 0.1 collective-permute-start.7
  25.1 0.4 %collective-permute-start.14 = (bf16[144,512]{1,0:T(8,128)(2,1)S(1)}, bf16[144,512]{1,0:T(8,128)(2,1)S(1)}, u32[]{:S(2)}, u32[]{:S(2)}) collective-permute-start(bf16[144,512]{1,0:T(8,128)(2,1)S(1)} %collective-permute-done.11.refs_11_.refs_10_), channel_id=1, source_target_pairs={{0,4},{4,0},{8,12},{12,8},{1,5},{5,1},{9,13},{13,9},{2,6},{6,2},{1... | collective-permute-start | bytes 442376 | tf_op jit(solution)/shard_map/ppermute | solution.py:25
  25.5 1.1 %collective-permute-done.7.refs_7_.refs_6_ = bf16[144,512]{1,0:T(8,128)(2,1)S(1)} collective-permute-done((bf16[144,512]{1,0:T(8,128)(2,1)S(1)}, bf16[144,512]{1,0:T(8,128)(2,1)S(1)}, u32[]{:S(2)}, u32[]{:S(2)}) %collective-permute-start.7) | collective-permute-done | bytes 147488 | tf_op jit(solution)/shard_map/ppermute | solution.py:25
  26.6 0.2 collective-permute-done.14.refs_13_.refs_12_
  26.8 1.0 %shard_map.67 = bf16[144,512]{1,0:T(8,128)(2,1)S(1)} custom-call(s32[16,4]{1,0:T(8,128)S(1)} %copy.8.lists_ref, s32[16]{0:T(128)S(1)} %copy-done.3, bf16[128,1024]{1,0:T(8,128)(2,1)S(1)} %collective-permute-done.12.query_ref, f32[128,512]{1,0:T(8,128)S(1)} %get-tuple-element.35.refs_0_, f32[128,128]{1,0:T(8,128)S(1)} %get-tuple-element.36.refs_1_, ...), custom_call_target="tpu_custom_call" | custom-call | flops 268435456 | bytes 4194304 | tf_op jit(solution)/shard_map/pallas_call | solution.py:280
  27.8 4.9 %collective-permute-start.15 = (bf16[144,512]{1,0:T(8,128)(2,1)S(1)}, bf16[144,512]{1,0:T(8,128)(2,1)S(1)}, u32[]{:S(2)}, u32[]{:S(2)}) collective-permute-start(bf16[144,512]{1,0:T(8,128)(2,1)S(1)} %shard_map.67), channel_id=1, source_target_pairs={{0,3},{1,2},{2,1},{3,0},{4,7},{5,6},{6,5},{7,4},{8,11},{9,10},{10,... | collective-permute-start | bytes 442376 | tf_op jit(solution)/shard_map/ppermute | solution.py:25
  32.7 1.4 %shard_map.66 = (f32[128,512]{1,0:T(8,128)S(1)}, f32[2,128,128]{2,1,0:T(8,128)S(1)}) custom-call(s32[16,4]{1,0:T(8,128)S(1)} %copy.8.lists_ref, s32[16]{0:T(128)S(1)} %copy-done.3, bf16[128,1024]{1,0:T(8,128)(2,1)S(1)} %copy-done.1, bf16[128,1024]{1,0:T(8,128)(2,1)S(1)} %collective-permute-done.1.refs_0_, ...), custom_call_target="tpu_custom_call" | custom-call | flops 268435456 | bytes 4194304 | tf_op jit(solution)/shard_map/pallas_call | solution.py:295
  34.2 2.9 %collective-permute-done.15.refs_0_ = bf16[144,512]{1,0:T(8,128)(2,1)S(1)} collective-permute-done((bf16[144,512]{1,0:T(8,128)(2,1)S(1)}, bf16[144,512]{1,0:T(8,128)(2,1)S(1)}, u32[]{:S(2)}, u32[]{:S(2)}) %collective-permute-start.15) | collective-permute-done | bytes 147488 | tf_op jit(solution)/shard_map/ppermute | solution.py:25
  37.1 0.8 %shard_map.68 = bf16[128,512]{1,0:T(8,128)(2,1)} custom-call(f32[128,512]{1,0:T(8,128)S(1)} %get-tuple-element.33.total_ref, f32[2,128,128]{2,1,0:T(8,128)S(1)} %get-tuple-element.34.stats_ref, bf16[144,512]{1,0:T(8,128)(2,1)S(1)} %collective-permute-done.15.refs_0_), custom_call_target="tpu_custom_call" | custom-call | tf_op jit(solution)/shard_map/pallas_call | solution.py:309
  (18 shorter events, 0.0 us)
Async XLA Ops:
  0.0 22.7 %copy-start = (bf16[128,1024]{1,0:T(8,128)(2,1)S(1)}, bf16[128,1024]{1,0:T(8,128)(2,1)}, u32[]{:S(2)}) copy-start(bf16[128,1024]{1,0:T(8,128)(2,1)} %refs_14_.1) | copy-start | bytes 786436
  0.0 3.0 %collective-permute-start = (bf16[128,1024]{1,0:T(8,128)(2,1)}, bf16[128,1024]{1,0:T(8,128)(2,1)S(1)}, u32[]{:S(2)}, u32[]{:S(2)}) collective-permute-start(bf16[128,1024]{1,0:T(8,128)(2,1)} %refs_14_.1), channel_id=1, source_target_pairs={{0,4},{4,0},{8,12},{12,8},{1,5},{5,1},{9,13},{13,9},{2,6},{6,2},{1... | collective-permute-start | bytes 786440 | tf_op jit(solution)/shard_map/ppermute | solution.py:25
  0.5 11.7 %collective-permute-start.3 = (bf16[128,1024]{1,0:T(8,128)(2,1)}, bf16[128,1024]{1,0:T(8,128)(2,1)S(1)}, u32[]{:S(2)}, u32[]{:S(2)}) collective-permute-start(bf16[128,1024]{1,0:T(8,128)(2,1)} %refs_14_.1), channel_id=1, source_target_pairs={{0,8},{4,12},{8,0},{12,4},{1,9},{5,13},{9,1},{13,5},{2,10},{6,14},... | collective-permute-start | bytes 786440 | tf_op jit(solution)/shard_map/ppermute | solution.py:25
  3.0 9.4 %collective-permute-start.1 = (bf16[128,1024]{1,0:T(8,128)(2,1)}, bf16[128,1024]{1,0:T(8,128)(2,1)S(1)}, u32[]{:S(2)}, u32[]{:S(2)}) collective-permute-start(bf16[128,1024]{1,0:T(8,128)(2,1)} %refs_14_.1), channel_id=1, source_target_pairs={{0,1},{1,0},{2,3},{3,2},{4,5},{5,4},{6,7},{7,6},{8,9},{9,8},{10,11... | collective-permute-start | bytes 786440 | tf_op jit(solution)/shard_map/ppermute | solution.py:25
  4.8 0.9 %copy-start.2 = (bf16[128,512]{1,0:T(8,128)(2,1)S(1)}, bf16[128,512]{1,0:T(8,128)(2,1)}, u32[]{:S(2)}) copy-start(bf16[128,512]{1,0:T(8,128)(2,1)} %values_ref) | copy-start | bytes 393220
  5.7 0.7 %copy-start.4 = (bf16[128]{0:T(256)(128)(2,1)S(1)}, bf16[128]{0:T(256)(128)(2,1)}, u32[]{:S(2)}) copy-start(bf16[128]{0:T(256)(128)(2,1)} %param.9) | copy-start | bytes 772
  6.3 10.6 %copy-start.5 = (s32[16,4]{0,1:T(4,128)S(1)}, s32[16,4]{0,1:T(4,128)}, u32[]{:S(2)}) copy-start(s32[16,4]{0,1:T(4,128)} %param.10) | copy-start | bytes 772
  6.5 16.2 %copy-start.3 = (s32[16]{0:T(128)S(1)}, s32[16]{0:T(128)}, u32[]{:S(2)}) copy-start(s32[16]{0:T(128)} %counts_ref.5) | copy-start | bytes 196
  6.5 8.3 %collective-permute-start.2 = (bf16[144,512]{1,0:T(8,128)(2,1)S(1)}, bf16[144,512]{1,0:T(8,128)(2,1)S(1)}, u32[]{:S(2)}, u32[]{:S(2)}) collective-permute-start(bf16[144,512]{1,0:T(8,128)(2,1)S(1)} %shard_map.64.refs_5_.refs_15_), channel_id=1, source_target_pairs={{0,1},{1,0},{2,3},{3,2},{4,5},{5,4},{6,7},{7,6},{8,9},{9,8},{10,11... | collective-permute-start | bytes 442376 | tf_op jit(solution)/shard_map/ppermute | solution.py:25
  6.9 8.0 %collective-permute-start.4 = (bf16[144,512]{1,0:T(8,128)(2,1)S(1)}, bf16[144,512]{1,0:T(8,128)(2,1)S(1)}, u32[]{:S(2)}, u32[]{:S(2)}) collective-permute-start(bf16[144,512]{1,0:T(8,128)(2,1)S(1)} %shard_map.64.refs_5_.refs_15_), channel_id=1, source_target_pairs={{0,8},{4,12},{8,0},{12,4},{1,9},{5,13},{9,1},{13,5},{2,10},{6,14},... | collective-permute-start | bytes 442376 | tf_op jit(solution)/shard_map/ppermute | solution.py:25
  8.5 14.1 %collective-permute-start.12 = (bf16[128,1024]{1,0:T(8,128)(2,1)}, bf16[128,1024]{1,0:T(8,128)(2,1)S(1)}, u32[]{:S(2)}, u32[]{:S(2)}) collective-permute-start(bf16[128,1024]{1,0:T(8,128)(2,1)} %query_ref.1), channel_id=1, source_target_pairs={{0,3},{1,2},{2,1},{3,0},{4,7},{5,6},{6,5},{7,4},{8,11},{9,10},{10,... | collective-permute-start | bytes 786440 | tf_op jit(solution)/shard_map/ppermute | solution.py:25
  12.4 12.1 %collective-permute-start.10 = (bf16[128,1024]{1,0:T(8,128)(2,1)S(1)}, bf16[128,1024]{1,0:T(8,128)(2,1)S(1)}, u32[]{:S(2)}, u32[]{:S(2)}) collective-permute-start(bf16[128,1024]{1,0:T(8,128)(2,1)S(1)} %collective-permute-done.1.refs_0_), channel_id=1, source_target_pairs={{0,8},{4,12},{8,0},{12,4},{1,9},{5,13},{9,1},{13,5},{2,10},{6,14},... | collective-permute-start | bytes 786440 | tf_op jit(solution)/shard_map/ppermute | solution.py:25
  14.8 9.6 %collective-permute-start.11 = (bf16[144,512]{1,0:T(8,128)(2,1)S(1)}, bf16[144,512]{1,0:T(8,128)(2,1)S(1)}, u32[]{:S(2)}, u32[]{:S(2)}) collective-permute-start(bf16[144,512]{1,0:T(8,128)(2,1)S(1)} %collective-permute-done.2.refs_1_), channel_id=1, source_target_pairs={{0,8},{4,12},{8,0},{12,4},{1,9},{5,13},{9,1},{13,5},{2,10},{6,14},... | collective-permute-start | bytes 442376 | tf_op jit(solution)/shard_map/ppermute | solution.py:25
  16.4 8.6 %collective-permute-start.5 = (bf16[144,512]{1,0:T(8,128)(2,1)S(1)}, bf16[144,512]{1,0:T(8,128)(2,1)S(1)}, u32[]{:S(2)}, u32[]{:S(2)}) collective-permute-start(bf16[144,512]{1,0:T(8,128)(2,1)S(1)} %shard_map.64.refs_5_.refs_15_), channel_id=1, source_target_pairs={{0,4},{4,0},{8,12},{12,8},{1,5},{5,1},{9,13},{13,9},{2,6},{6,2},{1... | collective-permute-start | bytes 442376 | tf_op jit(solution)/shard_map/ppermute | solution.py:25
  16.4 8.7 %collective-permute-start.9 = (bf16[144,512]{1,0:T(8,128)(2,1)S(1)}, bf16[144,512]{1,0:T(8,128)(2,1)S(1)}, u32[]{:S(2)}, u32[]{:S(2)}) collective-permute-start(bf16[144,512]{1,0:T(8,128)(2,1)S(1)} %collective-permute-done.4.refs_3_), channel_id=1, source_target_pairs={{0,4},{4,0},{8,12},{12,8},{1,5},{5,1},{9,13},{13,9},{2,6},{6,2},{1... | collective-permute-start | bytes 442376 | tf_op jit(solution)/shard_map/ppermute | solution.py:25
  22.7 3.9 %collective-permute-start.8 = (bf16[128,1024]{1,0:T(8,128)(2,1)S(1)}, bf16[128,1024]{1,0:T(8,128)(2,1)S(1)}, u32[]{:S(2)}, u32[]{:S(2)}) collective-permute-start(bf16[128,1024]{1,0:T(8,128)(2,1)S(1)} %collective-permute-done.3.refs_2_), channel_id=1, source_target_pairs={{0,4},{4,0},{8,12},{12,8},{1,5},{5,1},{9,13},{13,9},{2,6},{6,2},{1... | collective-permute-start | bytes 786440 | tf_op jit(solution)/shard_map/ppermute | solution.py:25
  24.4 2.2 %collective-permute-start.6 = (bf16[128,1024]{1,0:T(8,128)(2,1)S(1)}, bf16[128,1024]{1,0:T(8,128)(2,1)S(1)}, u32[]{:S(2)}, u32[]{:S(2)}) collective-permute-start(bf16[128,1024]{1,0:T(8,128)(2,1)S(1)} %collective-permute-done.1.refs_0_), channel_id=1, source_target_pairs={{0,4},{4,0},{8,12},{12,8},{1,5},{5,1},{9,13},{13,9},{2,6},{6,2},{1... | collective-permute-start | bytes 786440 | tf_op jit(solution)/shard_map/ppermute | solution.py:25
  24.5 2.3 %collective-permute-start.13 = (bf16[128,1024]{1,0:T(8,128)(2,1)S(1)}, bf16[128,1024]{1,0:T(8,128)(2,1)S(1)}, u32[]{:S(2)}, u32[]{:S(2)}) collective-permute-start(bf16[128,1024]{1,0:T(8,128)(2,1)S(1)} %collective-permute-done.10.refs_10_.refs_9_), channel_id=1, source_target_pairs={{0,4},{4,0},{8,12},{12,8},{1,5},{5,1},{9,13},{13,9},{2,6},{6,2},{1... | collective-permute-start | bytes 786440 | tf_op jit(solution)/shard_map/ppermute | solution.py:25
  25.0 1.6 %collective-permute-start.7 = (bf16[144,512]{1,0:T(8,128)(2,1)S(1)}, bf16[144,512]{1,0:T(8,128)(2,1)S(1)}, u32[]{:S(2)}, u32[]{:S(2)}) collective-permute-start(bf16[144,512]{1,0:T(8,128)(2,1)S(1)} %collective-permute-done.2.refs_1_), channel_id=1, source_target_pairs={{0,4},{4,0},{8,12},{12,8},{1,5},{5,1},{9,13},{13,9},{2,6},{6,2},{1... | collective-permute-start | bytes 442376 | tf_op jit(solution)/shard_map/ppermute | solution.py:25
  25.1 1.7 %collective-permute-start.14 = (bf16[144,512]{1,0:T(8,128)(2,1)S(1)}, bf16[144,512]{1,0:T(8,128)(2,1)S(1)}, u32[]{:S(2)}, u32[]{:S(2)}) collective-permute-start(bf16[144,512]{1,0:T(8,128)(2,1)S(1)} %collective-permute-done.11.refs_11_.refs_10_), channel_id=1, source_target_pairs={{0,4},{4,0},{8,12},{12,8},{1,5},{5,1},{9,13},{13,9},{2,6},{6,2},{1... | collective-permute-start | bytes 442376 | tf_op jit(solution)/shard_map/ppermute | solution.py:25
  26.8 5.9 %copy-start.1 = (bf16[128,1024]{1,0:T(8,128)(2,1)S(1)}, bf16[128,1024]{1,0:T(8,128)(2,1)}, u32[]{:S(2)}) copy-start(bf16[128,1024]{1,0:T(8,128)(2,1)} %query_ref.1) | copy-start | bytes 786436
  27.8 9.2 %collective-permute-start.15 = (bf16[144,512]{1,0:T(8,128)(2,1)S(1)}, bf16[144,512]{1,0:T(8,128)(2,1)S(1)}, u32[]{:S(2)}, u32[]{:S(2)}) collective-permute-start(bf16[144,512]{1,0:T(8,128)(2,1)S(1)} %shard_map.67), channel_id=1, source_target_pairs={{0,3},{1,2},{2,1},{3,0},{4,7},{5,6},{6,5},{7,4},{8,11},{9,10},{10,... | collective-permute-start | bytes 442376 | tf_op jit(solution)/shard_map/ppermute | solution.py:25

commit v11 on v7

--- a/solution.py
+++ b/solution.py
@@ -23,6 +23,12 @@
 def swap(value, axis, mask):
     length = lax.axis_size(axis)
     return lax.ppermute(value, axis, [(i, i ^ mask) for i in range(length)])
+
+
+def swap_some(value, axis, mask, inner):
+    length = lax.axis_size(axis)
+    pairs = [(i, i ^ mask) for i in range(length) if (abs(i - (i ^ mask)) * 2 <= mask) == inner]
+    return lax.ppermute(value, axis, pairs)
 
 
 def tie(*values):
@@ -138,9 +144,24 @@
     return row_max
 
 
-def early_kernel(places, panel_mask, lists_ref, counts_ref, query_ref, *refs):
+def is_inner(mask):
+    index = lax.axis_index("qry")
+    return jnp.abs(index - lax.bitwise_xor(index, mask)) * 2 <= mask
+
+
+def early_kernel(places, panel_mask, lists_ref, counts_ref, inner_ref, outer_ref, *refs):
     pieces, refs = read_pieces(places, refs, own=True)
-    total_ref, mass_ref, max_ref, score_ref = refs
+    query_ref, total_ref, mass_ref, max_ref, score_ref = refs
+    inner = is_inner(panel_mask)
+
+    @pl.when(inner)
+    def _():
+        query_ref[...] = inner_ref[...]
+
+    @pl.when(jnp.logical_not(inner))
+    def _():
+        query_ref[...] = outer_ref[...]
+
     row_max = attend(pieces, panel_mask, lists_ref, counts_ref, query_ref, score_ref, total_ref, mass_ref)
     max_ref[...] = jnp.broadcast_to(row_max, max_ref.shape)
 
@@ -201,7 +222,7 @@
         steps.append(("lib", mask))
         mask //= 2
     leaving, _ = tie(queries, values)
-    visitors = [swap(leaving, "qry", mask) for mask in masks]
+    inner = [swap_some(leaving, "qry", mask, True) for mask in masks]
     early, late = [], []
     for axis, mask in steps:
         place = (0, mask) if axis == "qry" else (mask, 0)
@@ -213,7 +234,9 @@
             place = (lib_mask | mask, qry_mask)
             relayed.append((place, swap(far_keys, axis, mask), swap(far_values, axis, mask)))
         early, late = early + late + [near], relayed
-    return early, late, list(zip(masks, visitors))
+    leaving, _ = tie(queries, early[0][1])
+    outer = [swap_some(leaving, "qry", mask, False) for mask in masks]
+    return early, late, list(zip(masks, inner, outer))
 
 
 def cross_cores(pieces, arrivals=()):
@@ -260,22 +283,22 @@
     own_scratch = [pltpu.VMEM(library_keys.shape, library_keys.dtype), pltpu.SemaphoreType.DMA]
     early_arrays = arrays_of(early)
     states = []
-    for mask, visiting in visitors:
+    for mask, inner, outer in visitors:
         state = pl.pallas_call(
             functools.partial(early_kernel, places_of(early), mask),
-            out_shape=(total_shape, line_shape, line_shape),
-            in_specs=[SMEM, SMEM] + [VMEM] * (1 + len(early_arrays)) + own_specs,
-            out_specs=(VMEM,) * 3,
+            out_shape=(jax.ShapeDtypeStruct(queries.shape, queries.dtype), total_shape, line_shape, line_shape),
+            in_specs=[SMEM, SMEM] + [VMEM] * (2 + len(early_arrays)) + own_specs,
+            out_specs=(VMEM,) * 4,
             scratch_shapes=[pltpu.VMEM((len(early) + 1, TILE, TILE), jnp.float32)] + own_scratch,
             compiler_params=attend_params,
             cost_estimate=cost,
-        )(block_list, block_count, visiting, *early_arrays, library_keys, values)
+        )(block_list, block_count, inner, outer, *early_arrays, library_keys, values)
         states.append(state)
 
-    late = [((1, 0), partner_keys, swap(values, "lib", 1))] + cross_cores(early) + relayed + cross_cores(relayed, [state[2] for state in states])
+    late = [((1, 0), partner_keys, swap(values, "lib", 1))] + cross_cores(early) + relayed + cross_cores(relayed, [state[3] for state in states])
     late_arrays = arrays_of(late)
     returned = []
-    for (mask, visiting), state in zip(visitors, states):
+    for (mask, *_), state in zip(visitors, states):
         packed = pl.pallas_call(
             functools.partial(late_kernel, places_of(late), mask),
             out_shape=jax.ShapeDtypeStruct((TILE + EXTRA, value_width), jnp.bfloat16),
@@ -288,7 +311,7 @@
             ],
             compiler_params=attend_params,
             cost_estimate=cost,
-        )(block_list, block_count, visiting, *state, *late_arrays)
+        )(block_list, block_count, *state, *late_arrays)
         returned.append(swap(packed, "qry", mask))
 
     total, stats = pl.pallas_call(

time: 36.3 us -> 39.1 us (1.077)
  waiting for transfers between devices: 11.6 us -> 15.4 us
  starting transfers between devices: 17.8 us -> 16.9 us
    ppermute x16 -> x15, starting transfers between devices: 17.8 us -> 10.4 us  [swap(): return lax.ppermute(value, axis, [(i, i ^ mask) for i in range(length)])]
    ppermute x0 -> x2, starting transfers between devices: none -> 6.54 us  [swap_some(): return lax.ppermute(value, axis, pairs)]
    ppermute x0 -> x2, waiting for transfers between devices: none -> 3.28 us  [swap_some(): return lax.ppermute(value, axis, pairs)]
    ppermute x16 -> x15, waiting for transfers between devices: 11.6 us -> 12.1 us  [swap(): return lax.ppermute(value, axis, [(i, i ^ mask) for i in range(length)])]
    pallas_call x1, Pallas kernels: 1.03 us -> 1.53 us  [body(): pl.pallas_call(functools.partial(late_kernel, places_of(late), mask), out...]
    pallas_call x1, Pallas kernels: 1.84 us -> 1.41 us  [body(): pl.pallas_call(functools.partial(home_kernel, places_of(early + late)), o...]
    pallas_call x1, Pallas kernels: 1.26 us -> 0.86 us  [body(): pl.pallas_call(functools.partial(early_kernel, places_of(early), mask), o...]
  transfers between devices with their start and end apart: 16 -> 17, of which waited for: 7 -> 7; matrix products, arithmetic and copies ran while one was open for 0% -> 0% of each run, Pallas kernels for 9% -> 6%
where the time goes in v11:
time: 39.1 us; the launch traced here: 38.9 us
  starting transfers between devices  16.9 us (43%)
  waiting for transfers between devices  15.4 us (39%)
  Pallas kernels  4.79 us (12%)
  local copies, waits for them, and re-layouts  1.66 us (4%)
    ppermute x15, waiting for transfers between devices, swap(): return lax.ppermute(value, axis, [(i, i ^ mask) for i in range(length)])  12.1 us
    ppermute x15, starting transfers between devices, swap(): return lax.ppermute(value, axis, [(i, i ^ mask) for i in range(length)])  10.4 us
    ppermute x2, starting transfers between devices, swap_some(): return lax.ppermute(value, axis, pairs)  6.54 us
    ppermute x2, waiting for transfers between devices, swap_some(): return lax.ppermute(value, axis, pairs)  3.28 us
    unnamed x13, local copies, waits for them, and re-layouts  1.66 us
    pallas_call x1, Pallas kernels, body(): pl.pallas_call(functools.partial(late_kernel, places_of(late), mask), out...  1.53 us
    pallas_call x1, Pallas kernels, body(): pl.pallas_call(functools.partial(home_kernel, places_of(early + late)), o...  1.41 us
    pallas_call x1, Pallas kernels, body(): pl.pallas_call(functools.partial(early_kernel, places_of(early), mask), o...  0.86 us
  transfers between devices with their start and end apart: 17, of which 7 were waited for; matrix products, arithmetic and copies ran while one was open for 0% of the time, Pallas kernels for 6%

profile of v11, /device:TPU:0, one launch (start us, length us, event | category | flops | bytes accessed | tf_op | source)
XLA Modules:
  0.0 38.9 jit_solution(9366783884246252361)
XLA Ops:
  0.0 0.5 %collective-permute-start.1 = (bf16[128,1024]{1,0:T(8,128)(2,1)}, bf16[128,1024]{1,0:T(8,128)(2,1)S(1)}, u32[]{:S(2)}, u32[]{:S(2)}) collective-permute-start(bf16[128,1024]{1,0:T(8,128)(2,1)} %refs_14_.1), channel_id=1, source_target_pairs={{0,4},{4,0},{8,12},{12,8},{1,5},{5,1},{9,13},{13,9},{2,6},{6,2},{1... | collective-permute-start | bytes 786440 | tf_op jit(solution)/shard_map/ppermute | solution.py:25
  0.5 2.6 %collective-permute-start = (bf16[128,1024]{1,0:T(8,128)(2,1)}, bf16[128,1024]{1,0:T(8,128)(2,1)S(1)}, u32[]{:S(2)}, u32[]{:S(2)}) collective-permute-start(bf16[128,1024]{1,0:T(8,128)(2,1)} %refs_14_.1), channel_id=1, source_target_pairs={{0,1},{1,0},{2,3},{3,2},{4,5},{5,4},{6,7},{7,6},{8,9},{9,8},{10,11... | collective-permute-start | bytes 786440 | tf_op jit(solution)/shard_map/ppermute | solution.py:25
  3.1 1.5 %collective-permute-start.3 = (bf16[128,1024]{1,0:T(8,128)(2,1)}, bf16[128,1024]{1,0:T(8,128)(2,1)S(1)}, u32[]{:S(2)}, u32[]{:S(2)}) collective-permute-start(bf16[128,1024]{1,0:T(8,128)(2,1)} %refs_14_.1), channel_id=1, source_target_pairs={{0,8},{4,12},{8,0},{12,4},{1,9},{5,13},{9,1},{13,5},{2,10},{6,14},... | collective-permute-start | bytes 786440 | tf_op jit(solution)/shard_map/ppermute | solution.py:25
  4.6 0.0 collective-permute-done.1.refs_4_.refs_3_
  4.6 0.9 %copy-done.2 = bf16[128,512]{1,0:T(8,128)(2,1)S(1)} copy-done((bf16[128,512]{1,0:T(8,128)(2,1)S(1)}, bf16[128,512]{1,0:T(8,128)(2,1)}, u32[]{:S(2)}) %copy-start.2) | copy-done | bytes 131096
  5.5 0.7 %copy-done.4 = bf16[128]{0:T(256)(128)(2,1)S(1)} copy-done((bf16[128]{0:T(256)(128)(2,1)S(1)}, bf16[128]{0:T(256)(128)(2,1)}, u32[]{:S(2)}) %copy-start.4) | copy-done | bytes 280
  6.1 0.2 shard_map.64.refs_5_.refs_15_
  6.3 0.0 copy-start.3
  6.3 0.5 %collective-permute-start.2 = (bf16[144,512]{1,0:T(8,128)(2,1)S(1)}, bf16[144,512]{1,0:T(8,128)(2,1)S(1)}, u32[]{:S(2)}, u32[]{:S(2)}) collective-permute-start(bf16[144,512]{1,0:T(8,128)(2,1)S(1)} %shard_map.64.refs_5_.refs_15_), channel_id=1, source_target_pairs={{0,1},{1,0},{2,3},{3,2},{4,5},{5,4},{6,7},{7,6},{8,9},{9,8},{10,11... | collective-permute-start | bytes 442376 | tf_op jit(solution)/shard_map/ppermute | solution.py:25
  6.9 1.2 %collective-permute-start.4 = (bf16[144,512]{1,0:T(8,128)(2,1)S(1)}, bf16[144,512]{1,0:T(8,128)(2,1)S(1)}, u32[]{:S(2)}, u32[]{:S(2)}) collective-permute-start(bf16[144,512]{1,0:T(8,128)(2,1)S(1)} %shard_map.64.refs_5_.refs_15_), channel_id=1, source_target_pairs={{0,8},{4,12},{8,0},{12,4},{1,9},{5,13},{9,1},{13,5},{2,10},{6,14},... | collective-permute-start | bytes 442376 | tf_op jit(solution)/shard_map/ppermute | solution.py:25
  8.1 0.7 %collective-permute-start.12 = (bf16[128,1024]{1,0:T(8,128)(2,1)}, bf16[128,1024]{1,0:T(8,128)(2,1)S(1)}, u32[]{:S(2)}, u32[]{:S(2)}) collective-permute-start(bf16[128,1024]{1,0:T(8,128)(2,1)} %query_ref.1), channel_id=1, source_target_pairs={{1,2},{2,1},{5,6},{6,5},{9,10},{10,9},{13,14},{14,13},{17,18},{18,... | collective-permute-start | bytes 786440 | tf_op jit(solution)/shard_map/ppermute | solution.py:31
  8.8 1.7 %collective-permute-done.refs_0_ = bf16[128,1024]{1,0:T(8,128)(2,1)S(1)} collective-permute-done((bf16[128,1024]{1,0:T(8,128)(2,1)}, bf16[128,1024]{1,0:T(8,128)(2,1)S(1)}, u32[]{:S(2)}, u32[]{:S(2)}) %collective-permute-start) | collective-permute-done | bytes 262176 | tf_op jit(solution)/shard_map/ppermute | solution.py:25
  10.5 5.9 %collective-permute-start.13 = (bf16[128,1024]{1,0:T(8,128)(2,1)}, bf16[128,1024]{1,0:T(8,128)(2,1)S(1)}, u32[]{:S(2)}, u32[]{:S(2)}) collective-permute-start(bf16[128,1024]{1,0:T(8,128)(2,1)} %query_ref.1), channel_id=1, source_target_pairs={{0,3},{3,0},{4,7},{7,4},{8,11},{11,8},{12,15},{15,12},{16,19},{19,... | collective-permute-start | bytes 786440 | tf_op jit(solution)/shard_map/ppermute | solution.py:31
  16.4 1.6 %collective-permute-start.10 = (bf16[128,1024]{1,0:T(8,128)(2,1)S(1)}, bf16[128,1024]{1,0:T(8,128)(2,1)S(1)}, u32[]{:S(2)}, u32[]{:S(2)}) collective-permute-start(bf16[128,1024]{1,0:T(8,128)(2,1)S(1)} %collective-permute-done.refs_0_), channel_id=1, source_target_pairs={{0,8},{4,12},{8,0},{12,4},{1,9},{5,13},{9,1},{13,5},{2,10},{6,14},... | collective-permute-start | bytes 786440 | tf_op jit(solution)/shard_map/ppermute | solution.py:25
  17.9 0.0 collective-permute-done.2.refs_1_
  17.9 0.5 %collective-permute-start.11 = (bf16[144,512]{1,0:T(8,128)(2,1)S(1)}, bf16[144,512]{1,0:T(8,128)(2,1)S(1)}, u32[]{:S(2)}, u32[]{:S(2)}) collective-permute-start(bf16[144,512]{1,0:T(8,128)(2,1)S(1)} %collective-permute-done.2.refs_1_), channel_id=1, source_target_pairs={{0,8},{4,12},{8,0},{12,4},{1,9},{5,13},{9,1},{13,5},{2,10},{6,14},... | collective-permute-start | bytes 442376 | tf_op jit(solution)/shard_map/ppermute | solution.py:25
  18.5 0.5 %collective-permute-start.7 = (bf16[144,512]{1,0:T(8,128)(2,1)S(1)}, bf16[144,512]{1,0:T(8,128)(2,1)S(1)}, u32[]{:S(2)}, u32[]{:S(2)}) collective-permute-start(bf16[144,512]{1,0:T(8,128)(2,1)S(1)} %collective-permute-done.2.refs_1_), channel_id=1, source_target_pairs={{0,4},{4,0},{8,12},{12,8},{1,5},{5,1},{9,13},{13,9},{2,6},{6,2},{1... | collective-permute-start | bytes 442376 | tf_op jit(solution)/shard_map/ppermute | solution.py:25
  19.0 0.1 copy.8.lists_ref
  19.1 3.3 %collective-permute-done.13.outer_ref = bf16[128,1024]{1,0:T(8,128)(2,1)S(1)} collective-permute-done((bf16[128,1024]{1,0:T(8,128)(2,1)}, bf16[128,1024]{1,0:T(8,128)(2,1)S(1)}, u32[]{:S(2)}, u32[]{:S(2)}) %collective-permute-start.13) | collective-permute-done | bytes 262176 | tf_op jit(solution)/shard_map/ppermute | solution.py:31
  22.3 0.9 %shard_map.65 = (bf16[128,1024]{1,0:T(8,128)(2,1)S(1)}, f32[128,512]{1,0:T(8,128)S(1)}, f32[128,128]{1,0:T(8,128)S(1)}, f32[128,128]{1,0:T(8,128)S(1)}) custom-call(s32[16,4]{1,0:T(8,128)S(1)} %copy.8.lists_ref, s32[16]{0:T(128)S(1)} %copy-done.3, bf16[128,1024]{1,0:T(8,128)(2,1)S(1)} %collective-permute-done.12.inner_ref, ...), custom_call_target="tpu_custom_call" | custom-call | flops 268435456 | bytes 4194304 | tf_op jit(solution)/shard_map/pallas_call | solution.py:287
  23.2 1.9 %collective-permute-done.10.refs_10_.refs_9_ = bf16[128,1024]{1,0:T(8,128)(2,1)S(1)} collective-permute-done((bf16[128,1024]{1,0:T(8,128)(2,1)S(1)}, bf16[128,1024]{1,0:T(8,128)(2,1)S(1)}, u32[]{:S(2)}, u32[]{:S(2)}) %collective-permute-start.10) | collective-permute-done | bytes 262176 | tf_op jit(solution)/shard_map/ppermute | solution.py:25
  25.1 0.0 collective-permute-start.8
  25.1 1.6 %collective-permute-done.11.refs_11_.refs_10_ = bf16[144,512]{1,0:T(8,128)(2,1)S(1)} collective-permute-done((bf16[144,512]{1,0:T(8,128)(2,1)S(1)}, bf16[144,512]{1,0:T(8,128)(2,1)S(1)}, u32[]{:S(2)}, u32[]{:S(2)}) %collective-permute-start.11) | collective-permute-done | bytes 147488 | tf_op jit(solution)/shard_map/ppermute | solution.py:25
  26.7 0.5 %collective-permute-start.9 = (bf16[144,512]{1,0:T(8,128)(2,1)S(1)}, bf16[144,512]{1,0:T(8,128)(2,1)S(1)}, u32[]{:S(2)}, u32[]{:S(2)}) collective-permute-start(bf16[144,512]{1,0:T(8,128)(2,1)S(1)} %collective-permute-done.4.refs_3_), channel_id=1, source_target_pairs={{0,4},{4,0},{8,12},{12,8},{1,5},{5,1},{9,13},{13,9},{2,6},{6,2},{1... | collective-permute-start | bytes 442376 | tf_op jit(solution)/shard_map/ppermute | solution.py:25
  27.2 0.1 collective-permute-start.15
  27.3 1.2 %collective-permute-done.9.refs_9_.refs_8_ = bf16[144,512]{1,0:T(8,128)(2,1)S(1)} collective-permute-done((bf16[144,512]{1,0:T(8,128)(2,1)S(1)}, bf16[144,512]{1,0:T(8,128)(2,1)S(1)}, u32[]{:S(2)}, u32[]{:S(2)}) %collective-permute-start.9) | collective-permute-done | bytes 147488 | tf_op jit(solution)/shard_map/ppermute | solution.py:25
  28.5 0.2 collective-permute-done.15.refs_13_.refs_12_
  28.7 1.5 %shard_map.67 = bf16[144,512]{1,0:T(8,128)(2,1)S(1)} custom-call(s32[16,4]{1,0:T(8,128)S(1)} %copy.8.lists_ref, s32[16]{0:T(128)S(1)} %copy-done.3, bf16[128,1024]{1,0:T(8,128)(2,1)S(1)} %get-tuple-element.36.query_ref, f32[128,512]{1,0:T(8,128)S(1)} %get-tuple-element.37.refs_0_, f32[128,128]{1,0:T(8,128)S(1)} %get-tuple-element.38.refs_1_, ...), custom_call_target="tpu_custom_call" | custom-call | flops 268435456 | bytes 4194304 | tf_op jit(solution)/shard_map/pallas_call | solution.py:302
  30.2 0.9 %collective-permute-start.16 = (bf16[144,512]{1,0:T(8,128)(2,1)S(1)}, bf16[144,512]{1,0:T(8,128)(2,1)S(1)}, u32[]{:S(2)}, u32[]{:S(2)}) collective-permute-start(bf16[144,512]{1,0:T(8,128)(2,1)S(1)} %shard_map.67), channel_id=1, source_target_pairs={{0,3},{1,2},{2,1},{3,0},{4,7},{5,6},{6,5},{7,4},{8,11},{9,10},{10,... | collective-permute-start | bytes 442376 | tf_op jit(solution)/shard_map/ppermute | solution.py:25
  31.1 1.4 %shard_map.66 = (f32[128,512]{1,0:T(8,128)S(1)}, f32[2,128,128]{2,1,0:T(8,128)S(1)}) custom-call(s32[16,4]{1,0:T(8,128)S(1)} %copy.8.lists_ref, s32[16]{0:T(128)S(1)} %copy-done.3, bf16[128,1024]{1,0:T(8,128)(2,1)S(1)} %copy-done.1, bf16[128,1024]{1,0:T(8,128)(2,1)S(1)} %collective-permute-done.refs_0_, bf16[144,512]{1,0:T(8,128)(2,1)S(1)} %collective-permute-done.2.refs_1_, ...), custom_call_target="tpu_custom_call" | custom-call | flops 268435456 | bytes 4194304 | tf_op jit(solution)/shard_map/pallas_call | solution.py:317
  32.5 5.5 %collective-permute-done.16.refs_0_ = bf16[144,512]{1,0:T(8,128)(2,1)S(1)} collective-permute-done((bf16[144,512]{1,0:T(8,128)(2,1)S(1)}, bf16[144,512]{1,0:T(8,128)(2,1)S(1)}, u32[]{:S(2)}, u32[]{:S(2)}) %collective-permute-start.16) | collective-permute-done | bytes 147488 | tf_op jit(solution)/shard_map/ppermute | solution.py:25
  38.1 0.8 %shard_map.68 = bf16[128,512]{1,0:T(8,128)(2,1)} custom-call(f32[128,512]{1,0:T(8,128)S(1)} %get-tuple-element.34.total_ref, f32[2,128,128]{2,1,0:T(8,128)S(1)} %get-tuple-element.35.stats_ref, bf16[144,512]{1,0:T(8,128)(2,1)S(1)} %collective-permute-done.16.refs_0_), custom_call_target="tpu_custom_call" | custom-call | tf_op jit(solution)/shard_map/pallas_call | solution.py:331
  (20 shorter events, 0.0 us)
Async XLA Ops:
  0.0 22.3 %copy-start = (bf16[128,1024]{1,0:T(8,128)(2,1)S(1)}, bf16[128,1024]{1,0:T(8,128)(2,1)}, u32[]{:S(2)}) copy-start(bf16[128,1024]{1,0:T(8,128)(2,1)} %refs_14_.1) | copy-start | bytes 786436
  0.0 4.6 %collective-permute-start.1 = (bf16[128,1024]{1,0:T(8,128)(2,1)}, bf16[128,1024]{1,0:T(8,128)(2,1)S(1)}, u32[]{:S(2)}, u32[]{:S(2)}) collective-permute-start(bf16[128,1024]{1,0:T(8,128)(2,1)} %refs_14_.1), channel_id=1, source_target_pairs={{0,4},{4,0},{8,12},{12,8},{1,5},{5,1},{9,13},{13,9},{2,6},{6,2},{1... | collective-permute-start | bytes 786440 | tf_op jit(solution)/shard_map/ppermute | solution.py:25
  0.5 10.0 %collective-permute-start = (bf16[128,1024]{1,0:T(8,128)(2,1)}, bf16[128,1024]{1,0:T(8,128)(2,1)S(1)}, u32[]{:S(2)}, u32[]{:S(2)}) collective-permute-start(bf16[128,1024]{1,0:T(8,128)(2,1)} %refs_14_.1), channel_id=1, source_target_pairs={{0,1},{1,0},{2,3},{3,2},{4,5},{5,4},{6,7},{7,6},{8,9},{9,8},{10,11... | collective-permute-start | bytes 786440 | tf_op jit(solution)/shard_map/ppermute | solution.py:25
  3.1 13.3 %collective-permute-start.3 = (bf16[128,1024]{1,0:T(8,128)(2,1)}, bf16[128,1024]{1,0:T(8,128)(2,1)S(1)}, u32[]{:S(2)}, u32[]{:S(2)}) collective-permute-start(bf16[128,1024]{1,0:T(8,128)(2,1)} %refs_14_.1), channel_id=1, source_target_pairs={{0,8},{4,12},{8,0},{12,4},{1,9},{5,13},{9,1},{13,5},{2,10},{6,14},... | collective-permute-start | bytes 786440 | tf_op jit(solution)/shard_map/ppermute | solution.py:25
  4.6 0.9 %copy-start.2 = (bf16[128,512]{1,0:T(8,128)(2,1)S(1)}, bf16[128,512]{1,0:T(8,128)(2,1)}, u32[]{:S(2)}) copy-start(bf16[128,512]{1,0:T(8,128)(2,1)} %values_ref) | copy-start | bytes 393220
  5.5 0.7 %copy-start.4 = (bf16[128]{0:T(256)(128)(2,1)S(1)}, bf16[128]{0:T(256)(128)(2,1)}, u32[]{:S(2)}) copy-start(bf16[128]{0:T(256)(128)(2,1)} %param.9) | copy-start | bytes 772
  6.1 12.8 %copy-start.5 = (s32[16,4]{0,1:T(4,128)S(1)}, s32[16,4]{0,1:T(4,128)}, u32[]{:S(2)}) copy-start(s32[16,4]{0,1:T(4,128)} %param.10) | copy-start | bytes 772
  6.3 16.0 %copy-start.3 = (s32[16]{0:T(128)S(1)}, s32[16]{0:T(128)}, u32[]{:S(2)}) copy-start(s32[16]{0:T(128)} %counts_ref.5) | copy-start | bytes 196
  6.3 11.6 %collective-permute-start.2 = (bf16[144,512]{1,0:T(8,128)(2,1)S(1)}, bf16[144,512]{1,0:T(8,128)(2,1)S(1)}, u32[]{:S(2)}, u32[]{:S(2)}) collective-permute-start(bf16[144,512]{1,0:T(8,128)(2,1)S(1)} %shard_map.64.refs_5_.refs_15_), channel_id=1, source_target_pairs={{0,1},{1,0},{2,3},{3,2},{4,5},{5,4},{6,7},{7,6},{8,9},{9,8},{10,11... | collective-permute-start | bytes 442376 | tf_op jit(solution)/shard_map/ppermute | solution.py:25
  6.9 11.1 %collective-permute-start.4 = (bf16[144,512]{1,0:T(8,128)(2,1)S(1)}, bf16[144,512]{1,0:T(8,128)(2,1)S(1)}, u32[]{:S(2)}, u32[]{:S(2)}) collective-permute-start(bf16[144,512]{1,0:T(8,128)(2,1)S(1)} %shard_map.64.refs_5_.refs_15_), channel_id=1, source_target_pairs={{0,8},{4,12},{8,0},{12,4},{1,9},{5,13},{9,1},{13,5},{2,10},{6,14},... | collective-permute-start | bytes 442376 | tf_op jit(solution)/shard_map/ppermute | solution.py:25
  8.1 10.4 %collective-permute-start.12 = (bf16[128,1024]{1,0:T(8,128)(2,1)}, bf16[128,1024]{1,0:T(8,128)(2,1)S(1)}, u32[]{:S(2)}, u32[]{:S(2)}) collective-permute-start(bf16[128,1024]{1,0:T(8,128)(2,1)} %query_ref.1), channel_id=1, source_target_pairs={{1,2},{2,1},{5,6},{6,5},{9,10},{10,9},{13,14},{14,13},{17,18},{18,... | collective-permute-start | bytes 786440 | tf_op jit(solution)/shard_map/ppermute | solution.py:31
  10.5 11.9 %collective-permute-start.13 = (bf16[128,1024]{1,0:T(8,128)(2,1)}, bf16[128,1024]{1,0:T(8,128)(2,1)S(1)}, u32[]{:S(2)}, u32[]{:S(2)}) collective-permute-start(bf16[128,1024]{1,0:T(8,128)(2,1)} %query_ref.1), channel_id=1, source_target_pairs={{0,3},{3,0},{4,7},{7,4},{8,11},{11,8},{12,15},{15,12},{16,19},{19,... | collective-permute-start | bytes 786440 | tf_op jit(solution)/shard_map/ppermute | solution.py:31
  16.4 8.8 %collective-permute-start.10 = (bf16[128,1024]{1,0:T(8,128)(2,1)S(1)}, bf16[128,1024]{1,0:T(8,128)(2,1)S(1)}, u32[]{:S(2)}, u32[]{:S(2)}) collective-permute-start(bf16[128,1024]{1,0:T(8,128)(2,1)S(1)} %collective-permute-done.refs_0_), channel_id=1, source_target_pairs={{0,8},{4,12},{8,0},{12,4},{1,9},{5,13},{9,1},{13,5},{2,10},{6,14},... | collective-permute-start | bytes 786440 | tf_op jit(solution)/shard_map/ppermute | solution.py:25
  17.9 8.8 %collective-permute-start.11 = (bf16[144,512]{1,0:T(8,128)(2,1)S(1)}, bf16[144,512]{1,0:T(8,128)(2,1)S(1)}, u32[]{:S(2)}, u32[]{:S(2)}) collective-permute-start(bf16[144,512]{1,0:T(8,128)(2,1)S(1)} %collective-permute-done.2.refs_1_), channel_id=1, source_target_pairs={{0,8},{4,12},{8,0},{12,4},{1,9},{5,13},{9,1},{13,5},{2,10},{6,14},... | collective-permute-start | bytes 442376 | tf_op jit(solution)/shard_map/ppermute | solution.py:25
  18.5 8.3 %collective-permute-start.5 = (bf16[144,512]{1,0:T(8,128)(2,1)S(1)}, bf16[144,512]{1,0:T(8,128)(2,1)S(1)}, u32[]{:S(2)}, u32[]{:S(2)}) collective-permute-start(bf16[144,512]{1,0:T(8,128)(2,1)S(1)} %shard_map.64.refs_5_.refs_15_), channel_id=1, source_target_pairs={{0,4},{4,0},{8,12},{12,8},{1,5},{5,1},{9,13},{13,9},{2,6},{6,2},{1... | collective-permute-start | bytes 442376 | tf_op jit(solution)/shard_map/ppermute | solution.py:25
  18.5 8.8 %collective-permute-start.7 = (bf16[144,512]{1,0:T(8,128)(2,1)S(1)}, bf16[144,512]{1,0:T(8,128)(2,1)S(1)}, u32[]{:S(2)}, u32[]{:S(2)}) collective-permute-start(bf16[144,512]{1,0:T(8,128)(2,1)S(1)} %collective-permute-done.2.refs_1_), channel_id=1, source_target_pairs={{0,4},{4,0},{8,12},{12,8},{1,5},{5,1},{9,13},{13,9},{2,6},{6,2},{1... | collective-permute-start | bytes 442376 | tf_op jit(solution)/shard_map/ppermute | solution.py:25
  22.3 6.1 %collective-permute-start.6 = (bf16[128,1024]{1,0:T(8,128)(2,1)S(1)}, bf16[128,1024]{1,0:T(8,128)(2,1)S(1)}, u32[]{:S(2)}, u32[]{:S(2)}) collective-permute-start(bf16[128,1024]{1,0:T(8,128)(2,1)S(1)} %collective-permute-done.refs_0_), channel_id=1, source_target_pairs={{0,4},{4,0},{8,12},{12,8},{1,5},{5,1},{9,13},{13,9},{2,6},{6,2},{1... | collective-permute-start | bytes 786440 | tf_op jit(solution)/shard_map/ppermute | solution.py:25
  25.1 3.3 %collective-permute-start.8 = (bf16[128,1024]{1,0:T(8,128)(2,1)S(1)}, bf16[128,1024]{1,0:T(8,128)(2,1)S(1)}, u32[]{:S(2)}, u32[]{:S(2)}) collective-permute-start(bf16[128,1024]{1,0:T(8,128)(2,1)S(1)} %collective-permute-done.3.refs_2_), channel_id=1, source_target_pairs={{0,4},{4,0},{8,12},{12,8},{1,5},{5,1},{9,13},{13,9},{2,6},{6,2},{1... | collective-permute-start | bytes 786440 | tf_op jit(solution)/shard_map/ppermute | solution.py:25
  26.7 2.0 %collective-permute-start.14 = (bf16[128,1024]{1,0:T(8,128)(2,1)S(1)}, bf16[128,1024]{1,0:T(8,128)(2,1)S(1)}, u32[]{:S(2)}, u32[]{:S(2)}) collective-permute-start(bf16[128,1024]{1,0:T(8,128)(2,1)S(1)} %collective-permute-done.10.refs_10_.refs_9_), channel_id=1, source_target_pairs={{0,4},{4,0},{8,12},{12,8},{1,5},{5,1},{9,13},{13,9},{2,6},{6,2},{1... | collective-permute-start | bytes 786440 | tf_op jit(solution)/shard_map/ppermute | solution.py:25
  26.7 1.7 %collective-permute-start.9 = (bf16[144,512]{1,0:T(8,128)(2,1)S(1)}, bf16[144,512]{1,0:T(8,128)(2,1)S(1)}, u32[]{:S(2)}, u32[]{:S(2)}) collective-permute-start(bf16[144,512]{1,0:T(8,128)(2,1)S(1)} %collective-permute-done.4.refs_3_), channel_id=1, source_target_pairs={{0,4},{4,0},{8,12},{12,8},{1,5},{5,1},{9,13},{13,9},{2,6},{6,2},{1... | collective-permute-start | bytes 442376 | tf_op jit(solution)/shard_map/ppermute | solution.py:25
  27.2 1.4 %collective-permute-start.15 = (bf16[144,512]{1,0:T(8,128)(2,1)S(1)}, bf16[144,512]{1,0:T(8,128)(2,1)S(1)}, u32[]{:S(2)}, u32[]{:S(2)}) collective-permute-start(bf16[144,512]{1,0:T(8,128)(2,1)S(1)} %collective-permute-done.11.refs_11_.refs_10_), channel_id=1, source_target_pairs={{0,4},{4,0},{8,12},{12,8},{1,5},{5,1},{9,13},{13,9},{2,6},{6,2},{1... | collective-permute-start | bytes 442376 | tf_op jit(solution)/shard_map/ppermute | solution.py:25
  28.7 2.4 %copy-start.1 = (bf16[128,1024]{1,0:T(8,128)(2,1)S(1)}, bf16[128,1024]{1,0:T(8,128)(2,1)}, u32[]{:S(2)}) copy-start(bf16[128,1024]{1,0:T(8,128)(2,1)} %query_ref.1) | copy-start | bytes 786436
  30.2 7.9 %collective-permute-start.16 = (bf16[144,512]{1,0:T(8,128)(2,1)S(1)}, bf16[144,512]{1,0:T(8,128)(2,1)S(1)}, u32[]{:S(2)}, u32[]{:S(2)}) collective-permute-start(bf16[144,512]{1,0:T(8,128)(2,1)S(1)} %shard_map.67), channel_id=1, source_target_pairs={{0,3},{1,2},{2,1},{3,0},{4,7},{5,6},{6,5},{7,4},{8,11},{9,10},{10,... | collective-permute-start | bytes 442376 | tf_op jit(solution)/shard_map/ppermute | solution.py:25

commit v12 on v7

--- a/solution.py
+++ b/solution.py
@@ -200,7 +200,8 @@
     while mask > 1:
         steps.append(("lib", mask))
         mask //= 2
-    leaving, _ = tie(queries, values)
+    partner_values = swap(values, "lib", 1)
+    leaving, _ = tie(queries, partner_values)
     visitors = [swap(leaving, "qry", mask) for mask in masks]
     early, late = [], []
     for axis, mask in steps:
@@ -213,7 +214,7 @@
             place = (lib_mask | mask, qry_mask)
             relayed.append((place, swap(far_keys, axis, mask), swap(far_values, axis, mask)))
         early, late = early + late + [near], relayed
-    return early, late, list(zip(masks, visitors))
+    return early, late, partner_values, list(zip(masks, visitors))
 
 
 def cross_cores(pieces, arrivals=()):
@@ -249,7 +250,7 @@
     )(own_values, key_scale.reshape(1, TILE))
 
     masks = [2 * at + 1 for at in range(1, qry_count // 2)]
-    early, relayed, visitors = gather_library(library_keys, values, queries, masks)
+    early, relayed, partner_values, visitors = gather_library(library_keys, values, queries, masks)
     piece_rows = (width // value_width + 1) * TILE + EXTRA
     cost = pl.CostEstimate(flops=2 * TILE * 4 * TILE * width * 2, bytes_accessed=4 * 1024 * 1024, transcendentals=0)
     total_shape = jax.ShapeDtypeStruct((TILE, value_width), jnp.float32)
@@ -272,7 +273,7 @@
         )(block_list, block_count, visiting, *early_arrays, library_keys, values)
         states.append(state)
 
-    late = [((1, 0), partner_keys, swap(values, "lib", 1))] + cross_cores(early) + relayed + cross_cores(relayed, [state[2] for state in states])
+    late = [((1, 0), partner_keys, partner_values)] + cross_cores(early) + relayed + cross_cores(relayed, [state[2] for state in states])
     late_arrays = arrays_of(late)
     returned = []
     for (mask, visiting), state in zip(visitors, states):

time: 36.3 us -> 36.2 us (level)
  Pallas kernels: 5.11 us -> 4.26 us
  waiting for transfers between devices: 11.6 us -> 12.4 us
    ppermute x16, waiting for transfers between devices: 11.6 us -> 12.4 us  [swap(): return lax.ppermute(value, axis, [(i, i ^ mask) for i in range(length)])]
    pallas_call x1, Pallas kernels: 1.26 us -> 0.83 us  [body(): pl.pallas_call(functools.partial(early_kernel, places_of(early), mask), o...]
    pallas_call x1, Pallas kernels: 1.84 us -> 1.42 us  [body(): pl.pallas_call(functools.partial(home_kernel, places_of(early + late)), o...]
  transfers between devices with their start and end apart: 16 -> 16, of which waited for: 7 -> 7; matrix products, arithmetic and copies ran while one was open for 0% -> 0% of each run, Pallas kernels for 9% -> 7%
where the time goes in v12:
time: 36.2 us; the launch traced here: 36 us
  starting transfers between devices  17.7 us (49%)
  waiting for transfers between devices  12.4 us (34%)
  Pallas kernels  4.26 us (12%)
  local copies, waits for them, and re-layouts  1.66 us (5%)
    ppermute x16, starting transfers between devices, swap(): return lax.ppermute(value, axis, [(i, i ^ mask) for i in range(length)])  17.7 us
    ppermute x16, waiting for transfers between devices, swap(): return lax.ppermute(value, axis, [(i, i ^ mask) for i in range(length)])  12.4 us
    unnamed x13, local copies, waits for them, and re-layouts  1.66 us
    pallas_call x1, Pallas kernels, body(): pl.pallas_call(functools.partial(home_kernel, places_of(early + late)), o...  1.42 us
    pallas_call x1, Pallas kernels, body(): pl.pallas_call(functools.partial(late_kernel, places_of(late), mask), out...  1.03 us
    pallas_call x1, Pallas kernels, body(): pl.pallas_call(functools.partial(early_kernel, places_of(early), mask), o...  0.83 us
    pallas_call x1, Pallas kernels, body(): pl.pallas_call(merge_kernel, out_shape=jax.ShapeDtypeStruct((TILE, value_...  0.81 us
  transfers between devices with their start and end apart: 16, of which 7 were waited for; matrix products, arithmetic and copies ran while one was open for 0% of the time, Pallas kernels for 7%

profile of v12, /device:TPU:0, one launch (start us, length us, event | category | flops | bytes accessed | tf_op | source)
XLA Modules:
  0.0 36.0 jit_solution(6402393518485797096)
XLA Ops:
  0.0 0.5 %collective-permute-start.1 = (bf16[128,1024]{1,0:T(8,128)(2,1)}, bf16[128,1024]{1,0:T(8,128)(2,1)S(1)}, u32[]{:S(2)}, u32[]{:S(2)}) collective-permute-start(bf16[128,1024]{1,0:T(8,128)(2,1)} %refs_14_.1), channel_id=1, source_target_pairs={{0,4},{4,0},{8,12},{12,8},{1,5},{5,1},{9,13},{13,9},{2,6},{6,2},{1... | collective-permute-start | bytes 786440 | tf_op jit(solution)/shard_map/ppermute | solution.py:25
  0.5 2.6 %collective-permute-start = (bf16[128,1024]{1,0:T(8,128)(2,1)}, bf16[128,1024]{1,0:T(8,128)(2,1)S(1)}, u32[]{:S(2)}, u32[]{:S(2)}) collective-permute-start(bf16[128,1024]{1,0:T(8,128)(2,1)} %refs_14_.1), channel_id=1, source_target_pairs={{0,1},{1,0},{2,3},{3,2},{4,5},{5,4},{6,7},{7,6},{8,9},{9,8},{10,11... | collective-permute-start | bytes 786440 | tf_op jit(solution)/shard_map/ppermute | solution.py:25
  3.1 1.5 %collective-permute-start.3 = (bf16[128,1024]{1,0:T(8,128)(2,1)}, bf16[128,1024]{1,0:T(8,128)(2,1)S(1)}, u32[]{:S(2)}, u32[]{:S(2)}) collective-permute-start(bf16[128,1024]{1,0:T(8,128)(2,1)} %refs_14_.1), channel_id=1, source_target_pairs={{0,8},{4,12},{8,0},{12,4},{1,9},{5,13},{9,1},{13,5},{2,10},{6,14},... | collective-permute-start | bytes 786440 | tf_op jit(solution)/shard_map/ppermute | solution.py:25
  4.6 0.0 collective-permute-done.1.refs_4_.refs_3_
  4.6 0.9 %copy-done.2 = bf16[128,512]{1,0:T(8,128)(2,1)S(1)} copy-done((bf16[128,512]{1,0:T(8,128)(2,1)S(1)}, bf16[128,512]{1,0:T(8,128)(2,1)}, u32[]{:S(2)}) %copy-start.2) | copy-done | bytes 131096
  5.5 0.7 %copy-done.4 = bf16[128]{0:T(256)(128)(2,1)S(1)} copy-done((bf16[128]{0:T(256)(128)(2,1)S(1)}, bf16[128]{0:T(256)(128)(2,1)}, u32[]{:S(2)}) %copy-start.4) | copy-done | bytes 280
  6.1 0.2 shard_map.64.refs_5_.refs_15_
  6.3 0.0 copy-start.3
  6.3 0.1 collective-permute-start.5
  6.4 0.5 %collective-permute-start.2 = (bf16[144,512]{1,0:T(8,128)(2,1)S(1)}, bf16[144,512]{1,0:T(8,128)(2,1)S(1)}, u32[]{:S(2)}, u32[]{:S(2)}) collective-permute-start(bf16[144,512]{1,0:T(8,128)(2,1)S(1)} %shard_map.64.refs_5_.refs_15_), channel_id=1, source_target_pairs={{0,1},{1,0},{2,3},{3,2},{4,5},{5,4},{6,7},{7,6},{8,9},{9,8},{10,11... | collective-permute-start | bytes 442376 | tf_op jit(solution)/shard_map/ppermute | solution.py:25
  6.9 1.3 %collective-permute-start.4 = (bf16[144,512]{1,0:T(8,128)(2,1)S(1)}, bf16[144,512]{1,0:T(8,128)(2,1)S(1)}, u32[]{:S(2)}, u32[]{:S(2)}) collective-permute-start(bf16[144,512]{1,0:T(8,128)(2,1)S(1)} %shard_map.64.refs_5_.refs_15_), channel_id=1, source_target_pairs={{0,8},{4,12},{8,0},{12,4},{1,9},{5,13},{9,1},{13,5},{2,10},{6,14},... | collective-permute-start | bytes 442376 | tf_op jit(solution)/shard_map/ppermute | solution.py:25
  8.2 0.0 collective-permute-done.5.refs_5_.refs_4_
  8.2 2.8 %collective-permute-start.12 = (bf16[128,1024]{1,0:T(8,128)(2,1)}, bf16[128,1024]{1,0:T(8,128)(2,1)S(1)}, u32[]{:S(2)}, u32[]{:S(2)}) collective-permute-start(bf16[128,1024]{1,0:T(8,128)(2,1)} %query_ref.1), channel_id=1, source_target_pairs={{0,3},{1,2},{2,1},{3,0},{4,7},{5,6},{6,5},{7,4},{8,11},{9,10},{10,... | collective-permute-start | bytes 786440 | tf_op jit(solution)/shard_map/ppermute | solution.py:25
  11.1 0.0 collective-permute-done.refs_0_
  11.1 1.4 %collective-permute-done.3.refs_2_ = bf16[128,1024]{1,0:T(8,128)(2,1)S(1)} collective-permute-done((bf16[128,1024]{1,0:T(8,128)(2,1)}, bf16[128,1024]{1,0:T(8,128)(2,1)S(1)}, u32[]{:S(2)}, u32[]{:S(2)}) %collective-permute-start.3) | collective-permute-done | bytes 262176 | tf_op jit(solution)/shard_map/ppermute | solution.py:25
  12.5 1.5 %collective-permute-start.10 = (bf16[128,1024]{1,0:T(8,128)(2,1)S(1)}, bf16[128,1024]{1,0:T(8,128)(2,1)S(1)}, u32[]{:S(2)}, u32[]{:S(2)}) collective-permute-start(bf16[128,1024]{1,0:T(8,128)(2,1)S(1)} %collective-permute-done.refs_0_), channel_id=1, source_target_pairs={{0,8},{4,12},{8,0},{12,4},{1,9},{5,13},{9,1},{13,5},{2,10},{6,14},... | collective-permute-start | bytes 786440 | tf_op jit(solution)/shard_map/ppermute | solution.py:25
  13.9 1.7 %collective-permute-done.4.refs_3_ = bf16[144,512]{1,0:T(8,128)(2,1)S(1)} collective-permute-done((bf16[144,512]{1,0:T(8,128)(2,1)S(1)}, bf16[144,512]{1,0:T(8,128)(2,1)S(1)}, u32[]{:S(2)}, u32[]{:S(2)}) %collective-permute-start.4) | collective-permute-done | bytes 147488 | tf_op jit(solution)/shard_map/ppermute | solution.py:25
  15.6 1.5 %collective-permute-start.11 = (bf16[144,512]{1,0:T(8,128)(2,1)S(1)}, bf16[144,512]{1,0:T(8,128)(2,1)S(1)}, u32[]{:S(2)}, u32[]{:S(2)}) collective-permute-start(bf16[144,512]{1,0:T(8,128)(2,1)S(1)} %collective-permute-done.2.refs_1_), channel_id=1, source_target_pairs={{0,8},{4,12},{8,0},{12,4},{1,9},{5,13},{9,1},{13,5},{2,10},{6,14},... | collective-permute-start | bytes 442376 | tf_op jit(solution)/shard_map/ppermute | solution.py:25
  17.1 0.1 copy.8.lists_ref
  17.2 0.5 %collective-permute-start.6 = (bf16[128,1024]{1,0:T(8,128)(2,1)S(1)}, bf16[128,1024]{1,0:T(8,128)(2,1)S(1)}, u32[]{:S(2)}, u32[]{:S(2)}) collective-permute-start(bf16[128,1024]{1,0:T(8,128)(2,1)S(1)} %collective-permute-done.refs_0_), channel_id=1, source_target_pairs={{0,4},{4,0},{8,12},{12,8},{1,5},{5,1},{9,13},{13,9},{2,6},{6,2},{1... | collective-permute-start | bytes 786440 | tf_op jit(solution)/shard_map/ppermute | solution.py:25
  17.7 3.6 %collective-permute-done.12.query_ref = bf16[128,1024]{1,0:T(8,128)(2,1)S(1)} collective-permute-done((bf16[128,1024]{1,0:T(8,128)(2,1)}, bf16[128,1024]{1,0:T(8,128)(2,1)S(1)}, u32[]{:S(2)}, u32[]{:S(2)}) %collective-permute-start.12) | collective-permute-done | bytes 262176 | tf_op jit(solution)/shard_map/ppermute | solution.py:25
  21.3 0.8 %shard_map.65 = (f32[128,512]{1,0:T(8,128)S(1)}, f32[128,128]{1,0:T(8,128)S(1)}, f32[128,128]{1,0:T(8,128)S(1)}) custom-call(s32[16,4]{1,0:T(8,128)S(1)} %copy.8.lists_ref, s32[16]{0:T(128)S(1)} %copy-done.3, bf16[128,1024]{1,0:T(8,128)(2,1)S(1)} %collective-permute-done.12.query_ref, bf16[128,1024]{1,0:T(8,128)(2,1)S(1)} %collective-permute-done.refs_0_, ...), custom_call_target="tpu_custom_call" | custom-call | flops 268435456 | bytes 4194304 | tf_op jit(solution)/shard_map/pallas_call | solution.py:265
  22.2 1.5 %collective-permute-done.11.refs_11_.refs_10_ = bf16[144,512]{1,0:T(8,128)(2,1)S(1)} collective-permute-done((bf16[144,512]{1,0:T(8,128)(2,1)S(1)}, bf16[144,512]{1,0:T(8,128)(2,1)S(1)}, u32[]{:S(2)}, u32[]{:S(2)}) %collective-permute-start.11) | collective-permute-done | bytes 147488 | tf_op jit(solution)/shard_map/ppermute | solution.py:25
  23.6 0.5 %collective-permute-start.9 = (bf16[144,512]{1,0:T(8,128)(2,1)S(1)}, bf16[144,512]{1,0:T(8,128)(2,1)S(1)}, u32[]{:S(2)}, u32[]{:S(2)}) collective-permute-start(bf16[144,512]{1,0:T(8,128)(2,1)S(1)} %collective-permute-done.4.refs_3_), channel_id=1, source_target_pairs={{0,4},{4,0},{8,12},{12,8},{1,5},{5,1},{9,13},{13,9},{2,6},{6,2},{1... | collective-permute-start | bytes 442376 | tf_op jit(solution)/shard_map/ppermute | solution.py:25
  24.1 0.0 collective-permute-start.14
  24.1 1.2 %collective-permute-done.9.refs_9_.refs_8_ = bf16[144,512]{1,0:T(8,128)(2,1)S(1)} collective-permute-done((bf16[144,512]{1,0:T(8,128)(2,1)S(1)}, bf16[144,512]{1,0:T(8,128)(2,1)S(1)}, u32[]{:S(2)}, u32[]{:S(2)}) %collective-permute-start.9) | collective-permute-done | bytes 147488 | tf_op jit(solution)/shard_map/ppermute | solution.py:25
  25.4 0.2 collective-permute-done.14.refs_13_.refs_12_
  25.6 1.0 %shard_map.67 = bf16[144,512]{1,0:T(8,128)(2,1)S(1)} custom-call(s32[16,4]{1,0:T(8,128)S(1)} %copy.8.lists_ref, s32[16]{0:T(128)S(1)} %copy-done.3, bf16[128,1024]{1,0:T(8,128)(2,1)S(1)} %collective-permute-done.12.query_ref, f32[128,512]{1,0:T(8,128)S(1)} %get-tuple-element.33.refs_0_, f32[128,128]{1,0:T(8,128)S(1)} %get-tuple-element.34.refs_1_, ...), custom_call_target="tpu_custom_call" | custom-call | flops 268435456 | bytes 4194304 | tf_op jit(solution)/shard_map/pallas_call | solution.py:280
  26.6 4.4 %collective-permute-start.15 = (bf16[144,512]{1,0:T(8,128)(2,1)S(1)}, bf16[144,512]{1,0:T(8,128)(2,1)S(1)}, u32[]{:S(2)}, u32[]{:S(2)}) collective-permute-start(bf16[144,512]{1,0:T(8,128)(2,1)S(1)} %shard_map.67), channel_id=1, source_target_pairs={{0,3},{1,2},{2,1},{3,0},{4,7},{5,6},{6,5},{7,4},{8,11},{9,10},{10,... | collective-permute-start | bytes 442376 | tf_op jit(solution)/shard_map/ppermute | solution.py:25
  31.0 1.4 %shard_map.66 = (f32[128,512]{1,0:T(8,128)S(1)}, f32[2,128,128]{2,1,0:T(8,128)S(1)}) custom-call(s32[16,4]{1,0:T(8,128)S(1)} %copy.8.lists_ref, s32[16]{0:T(128)S(1)} %copy-done.3, bf16[128,1024]{1,0:T(8,128)(2,1)S(1)} %copy-done.1, bf16[128,1024]{1,0:T(8,128)(2,1)S(1)} %collective-permute-done.refs_0_, bf16[144,512]{1,0:T(8,128)(2,1)S(1)} %collective-permute-done.2.refs_1_, ...), custom_call_target="tpu_custom_call" | custom-call | flops 268435456 | bytes 4194304 | tf_op jit(solution)/shard_map/pallas_call | solution.py:295
  32.4 2.8 %collective-permute-done.15.refs_0_ = bf16[144,512]{1,0:T(8,128)(2,1)S(1)} collective-permute-done((bf16[144,512]{1,0:T(8,128)(2,1)S(1)}, bf16[144,512]{1,0:T(8,128)(2,1)S(1)}, u32[]{:S(2)}, u32[]{:S(2)}) %collective-permute-start.15) | collective-permute-done | bytes 147488 | tf_op jit(solution)/shard_map/ppermute | solution.py:25
  35.2 0.8 %shard_map.68 = bf16[128,512]{1,0:T(8,128)(2,1)} custom-call(f32[128,512]{1,0:T(8,128)S(1)} %get-tuple-element.31.total_ref, f32[2,128,128]{2,1,0:T(8,128)S(1)} %get-tuple-element.32.stats_ref, bf16[144,512]{1,0:T(8,128)(2,1)S(1)} %collective-permute-done.15.refs_0_), custom_call_target="tpu_custom_call" | custom-call | tf_op jit(solution)/shard_map/pallas_call | solution.py:309
  (18 shorter events, 0.0 us)
Async XLA Ops:
  0.0 21.3 %copy-start = (bf16[128,1024]{1,0:T(8,128)(2,1)S(1)}, bf16[128,1024]{1,0:T(8,128)(2,1)}, u32[]{:S(2)}) copy-start(bf16[128,1024]{1,0:T(8,128)(2,1)} %refs_14_.1) | copy-start | bytes 786436
  0.0 4.6 %collective-permute-start.1 = (bf16[128,1024]{1,0:T(8,128)(2,1)}, bf16[128,1024]{1,0:T(8,128)(2,1)S(1)}, u32[]{:S(2)}, u32[]{:S(2)}) collective-permute-start(bf16[128,1024]{1,0:T(8,128)(2,1)} %refs_14_.1), channel_id=1, source_target_pairs={{0,4},{4,0},{8,12},{12,8},{1,5},{5,1},{9,13},{13,9},{2,6},{6,2},{1... | collective-permute-start | bytes 786440 | tf_op jit(solution)/shard_map/ppermute | solution.py:25
  0.5 10.6 %collective-permute-start = (bf16[128,1024]{1,0:T(8,128)(2,1)}, bf16[128,1024]{1,0:T(8,128)(2,1)S(1)}, u32[]{:S(2)}, u32[]{:S(2)}) collective-permute-start(bf16[128,1024]{1,0:T(8,128)(2,1)} %refs_14_.1), channel_id=1, source_target_pairs={{0,1},{1,0},{2,3},{3,2},{4,5},{5,4},{6,7},{7,6},{8,9},{9,8},{10,11... | collective-permute-start | bytes 786440 | tf_op jit(solution)/shard_map/ppermute | solution.py:25
  3.1 9.4 %collective-permute-start.3 = (bf16[128,1024]{1,0:T(8,128)(2,1)}, bf16[128,1024]{1,0:T(8,128)(2,1)S(1)}, u32[]{:S(2)}, u32[]{:S(2)}) collective-permute-start(bf16[128,1024]{1,0:T(8,128)(2,1)} %refs_14_.1), channel_id=1, source_target_pairs={{0,8},{4,12},{8,0},{12,4},{1,9},{5,13},{9,1},{13,5},{2,10},{6,14},... | collective-permute-start | bytes 786440 | tf_op jit(solution)/shard_map/ppermute | solution.py:25
  4.6 0.9 %copy-start.2 = (bf16[128,512]{1,0:T(8,128)(2,1)S(1)}, bf16[128,512]{1,0:T(8,128)(2,1)}, u32[]{:S(2)}) copy-start(bf16[128,512]{1,0:T(8,128)(2,1)} %values_ref) | copy-start | bytes 393220
  5.5 0.7 %copy-start.4 = (bf16[128]{0:T(256)(128)(2,1)S(1)}, bf16[128]{0:T(256)(128)(2,1)}, u32[]{:S(2)}) copy-start(bf16[128]{0:T(256)(128)(2,1)} %param.9) | copy-start | bytes 772
  6.1 11.0 %copy-start.5 = (s32[16,4]{0,1:T(4,128)S(1)}, s32[16,4]{0,1:T(4,128)}, u32[]{:S(2)}) copy-start(s32[16,4]{0,1:T(4,128)} %param.10) | copy-start | bytes 772
  6.3 15.0 %copy-start.3 = (s32[16]{0:T(128)S(1)}, s32[16]{0:T(128)}, u32[]{:S(2)}) copy-start(s32[16]{0:T(128)} %counts_ref.5) | copy-start | bytes 196
  6.3 1.9 %collective-permute-start.5 = (bf16[144,512]{1,0:T(8,128)(2,1)S(1)}, bf16[144,512]{1,0:T(8,128)(2,1)S(1)}, u32[]{:S(2)}, u32[]{:S(2)}) collective-permute-start(bf16[144,512]{1,0:T(8,128)(2,1)S(1)} %shard_map.64.refs_5_.refs_15_), channel_id=1, source_target_pairs={{0,4},{4,0},{8,12},{12,8},{1,5},{5,1},{9,13},{13,9},{2,6},{6,2},{1... | collective-permute-start | bytes 442376 | tf_op jit(solution)/shard_map/ppermute | solution.py:25
  6.4 7.5 %collective-permute-start.2 = (bf16[144,512]{1,0:T(8,128)(2,1)S(1)}, bf16[144,512]{1,0:T(8,128)(2,1)S(1)}, u32[]{:S(2)}, u32[]{:S(2)}) collective-permute-start(bf16[144,512]{1,0:T(8,128)(2,1)S(1)} %shard_map.64.refs_5_.refs_15_), channel_id=1, source_target_pairs={{0,1},{1,0},{2,3},{3,2},{4,5},{5,4},{6,7},{7,6},{8,9},{9,8},{10,11... | collective-permute-start | bytes 442376 | tf_op jit(solution)/shard_map/ppermute | solution.py:25
  6.9 8.7 %collective-permute-start.4 = (bf16[144,512]{1,0:T(8,128)(2,1)S(1)}, bf16[144,512]{1,0:T(8,128)(2,1)S(1)}, u32[]{:S(2)}, u32[]{:S(2)}) collective-permute-start(bf16[144,512]{1,0:T(8,128)(2,1)S(1)} %shard_map.64.refs_5_.refs_15_), channel_id=1, source_target_pairs={{0,8},{4,12},{8,0},{12,4},{1,9},{5,13},{9,1},{13,5},{2,10},{6,14},... | collective-permute-start | bytes 442376 | tf_op jit(solution)/shard_map/ppermute | solution.py:25
  8.2 13.1 %collective-permute-start.12 = (bf16[128,1024]{1,0:T(8,128)(2,1)}, bf16[128,1024]{1,0:T(8,128)(2,1)S(1)}, u32[]{:S(2)}, u32[]{:S(2)}) collective-permute-start(bf16[128,1024]{1,0:T(8,128)(2,1)} %query_ref.1), channel_id=1, source_target_pairs={{0,3},{1,2},{2,1},{3,0},{4,7},{5,6},{6,5},{7,4},{8,11},{9,10},{10,... | collective-permute-start | bytes 786440 | tf_op jit(solution)/shard_map/ppermute | solution.py:25
  12.5 9.7 %collective-permute-start.10 = (bf16[128,1024]{1,0:T(8,128)(2,1)S(1)}, bf16[128,1024]{1,0:T(8,128)(2,1)S(1)}, u32[]{:S(2)}, u32[]{:S(2)}) collective-permute-start(bf16[128,1024]{1,0:T(8,128)(2,1)S(1)} %collective-permute-done.refs_0_), channel_id=1, source_target_pairs={{0,8},{4,12},{8,0},{12,4},{1,9},{5,13},{9,1},{13,5},{2,10},{6,14},... | collective-permute-start | bytes 786440 | tf_op jit(solution)/shard_map/ppermute | solution.py:25
  15.6 8.0 %collective-permute-start.11 = (bf16[144,512]{1,0:T(8,128)(2,1)S(1)}, bf16[144,512]{1,0:T(8,128)(2,1)S(1)}, u32[]{:S(2)}, u32[]{:S(2)}) collective-permute-start(bf16[144,512]{1,0:T(8,128)(2,1)S(1)} %collective-permute-done.2.refs_1_), channel_id=1, source_target_pairs={{0,8},{4,12},{8,0},{12,4},{1,9},{5,13},{9,1},{13,5},{2,10},{6,14},... | collective-permute-start | bytes 442376 | tf_op jit(solution)/shard_map/ppermute | solution.py:25
  17.1 7.0 %collective-permute-start.7 = (bf16[144,512]{1,0:T(8,128)(2,1)S(1)}, bf16[144,512]{1,0:T(8,128)(2,1)S(1)}, u32[]{:S(2)}, u32[]{:S(2)}) collective-permute-start(bf16[144,512]{1,0:T(8,128)(2,1)S(1)} %collective-permute-done.2.refs_1_), channel_id=1, source_target_pairs={{0,4},{4,0},{8,12},{12,8},{1,5},{5,1},{9,13},{13,9},{2,6},{6,2},{1... | collective-permute-start | bytes 442376 | tf_op jit(solution)/shard_map/ppermute | solution.py:25
  17.2 8.2 %collective-permute-start.6 = (bf16[128,1024]{1,0:T(8,128)(2,1)S(1)}, bf16[128,1024]{1,0:T(8,128)(2,1)S(1)}, u32[]{:S(2)}, u32[]{:S(2)}) collective-permute-start(bf16[128,1024]{1,0:T(8,128)(2,1)S(1)} %collective-permute-done.refs_0_), channel_id=1, source_target_pairs={{0,4},{4,0},{8,12},{12,8},{1,5},{5,1},{9,13},{13,9},{2,6},{6,2},{1... | collective-permute-start | bytes 786440 | tf_op jit(solution)/shard_map/ppermute | solution.py:25
  21.3 4.1 %collective-permute-start.8 = (bf16[128,1024]{1,0:T(8,128)(2,1)S(1)}, bf16[128,1024]{1,0:T(8,128)(2,1)S(1)}, u32[]{:S(2)}, u32[]{:S(2)}) collective-permute-start(bf16[128,1024]{1,0:T(8,128)(2,1)S(1)} %collective-permute-done.3.refs_2_), channel_id=1, source_target_pairs={{0,4},{4,0},{8,12},{12,8},{1,5},{5,1},{9,13},{13,9},{2,6},{6,2},{1... | collective-permute-start | bytes 786440 | tf_op jit(solution)/shard_map/ppermute | solution.py:25
  23.6 2.0 %collective-permute-start.13 = (bf16[128,1024]{1,0:T(8,128)(2,1)S(1)}, bf16[128,1024]{1,0:T(8,128)(2,1)S(1)}, u32[]{:S(2)}, u32[]{:S(2)}) collective-permute-start(bf16[128,1024]{1,0:T(8,128)(2,1)S(1)} %collective-permute-done.10.refs_10_.refs_9_), channel_id=1, source_target_pairs={{0,4},{4,0},{8,12},{12,8},{1,5},{5,1},{9,13},{13,9},{2,6},{6,2},{1... | collective-permute-start | bytes 786440 | tf_op jit(solution)/shard_map/ppermute | solution.py:25
  23.6 1.7 %collective-permute-start.9 = (bf16[144,512]{1,0:T(8,128)(2,1)S(1)}, bf16[144,512]{1,0:T(8,128)(2,1)S(1)}, u32[]{:S(2)}, u32[]{:S(2)}) collective-permute-start(bf16[144,512]{1,0:T(8,128)(2,1)S(1)} %collective-permute-done.4.refs_3_), channel_id=1, source_target_pairs={{0,4},{4,0},{8,12},{12,8},{1,5},{5,1},{9,13},{13,9},{2,6},{6,2},{1... | collective-permute-start | bytes 442376 | tf_op jit(solution)/shard_map/ppermute | solution.py:25
  24.1 1.4 %collective-permute-start.14 = (bf16[144,512]{1,0:T(8,128)(2,1)S(1)}, bf16[144,512]{1,0:T(8,128)(2,1)S(1)}, u32[]{:S(2)}, u32[]{:S(2)}) collective-permute-start(bf16[144,512]{1,0:T(8,128)(2,1)S(1)} %collective-permute-done.11.refs_11_.refs_10_), channel_id=1, source_target_pairs={{0,4},{4,0},{8,12},{12,8},{1,5},{5,1},{9,13},{13,9},{2,6},{6,2},{1... | collective-permute-start | bytes 442376 | tf_op jit(solution)/shard_map/ppermute | solution.py:25
  25.6 5.4 %copy-start.1 = (bf16[128,1024]{1,0:T(8,128)(2,1)S(1)}, bf16[128,1024]{1,0:T(8,128)(2,1)}, u32[]{:S(2)}) copy-start(bf16[128,1024]{1,0:T(8,128)(2,1)} %query_ref.1) | copy-start | bytes 786436
  26.6 8.6 %collective-permute-start.15 = (bf16[144,512]{1,0:T(8,128)(2,1)S(1)}, bf16[144,512]{1,0:T(8,128)(2,1)S(1)}, u32[]{:S(2)}, u32[]{:S(2)}) collective-permute-start(bf16[144,512]{1,0:T(8,128)(2,1)S(1)} %shard_map.67), channel_id=1, source_target_pairs={{0,3},{1,2},{2,1},{3,0},{4,7},{5,6},{6,5},{7,4},{8,11},{9,10},{10,... | collective-permute-start | bytes 442376 | tf_op jit(solution)/shard_map/ppermute | solution.py:25

commit v13 on v12

--- a/solution.py
+++ b/solution.py
@@ -11,6 +11,7 @@
 TILE = 128
 LANES = 128
 EXTRA = 16
+SUBLANES = 8
 MASKED_SCORE = -1e30
 SMEM = pl.BlockSpec(memory_space=pltpu.SMEM)
 VMEM = pl.BlockSpec(memory_space=pltpu.VMEM)
@@ -27,14 +28,6 @@
 
 def tie(*values):
     return lax.optimization_barrier(values)
-
-
-def split_three(value):
-    high = value.astype(jnp.bfloat16)
-    rest = value - high.astype(jnp.float32)
-    middle = rest.astype(jnp.bfloat16)
-    low = (rest - middle.astype(jnp.float32)).astype(jnp.bfloat16)
-    return high, middle, low
 
 
 def pack_kernel(values_ref, scale_ref, packed_ref, row_ref, sems):
@@ -131,9 +124,9 @@
             weight_high = weights.astype(jnp.bfloat16)
             weight_low = (weights - weight_high.astype(jnp.float32)).astype(jnp.bfloat16)
             values = piece.values()
-            added = jnp.dot(weight_high, values, preferred_element_type=jnp.float32)
-            added = added + jnp.dot(weight_low, values, preferred_element_type=jnp.float32)
-            total_ref[...] += added
+            stacked = jnp.concatenate([weight_high, weight_low], axis=0)
+            added = jnp.dot(stacked, values, preferred_element_type=jnp.float32)
+            total_ref[...] += added[0:TILE] + added[TILE:]
 
     return row_max
 
@@ -148,20 +141,13 @@
 def late_kernel(places, panel_mask, lists_ref, counts_ref, query_ref, *refs):
     before, refs = refs[:3], refs[3:]
     pieces, refs = read_pieces(places, refs)
-    packed_ref, score_ref, total_ref, mass_ref = refs
+    partial_ref, lines_ref, score_ref, total_ref, mass_ref = refs
     row_max = attend(pieces, panel_mask, lists_ref, counts_ref, query_ref, score_ref, total_ref, mass_ref, before)
     row_sum = jnp.sum(mass_ref[...], axis=1, keepdims=True)
-    value_width = total_ref.shape[1]
     inverse = 1.0 / jnp.where(row_sum > 0.0, row_sum, 1.0)
-    packed_ref[0:TILE, :] = (total_ref[...] * inverse).astype(jnp.bfloat16)
-    row = lax.broadcasted_iota(jnp.int32, (EXTRA, LANES), 0)
-    packed = jnp.zeros((EXTRA, LANES), jnp.float32)
-    for first, column in ((0, row_max), (3, row_sum)):
-        turned = jnp.transpose(jnp.broadcast_to(column, (TILE, LANES)))[0:EXTRA]
-        for at, part in enumerate(split_three(turned)):
-            packed = jnp.where(row == first + at, part.astype(jnp.float32), packed)
-    packed_ref[TILE:, 0:LANES] = packed.astype(jnp.bfloat16)
-    packed_ref[TILE:, LANES:] = jnp.zeros((EXTRA, value_width - LANES), jnp.bfloat16)
+    partial_ref[...] = (total_ref[...] * inverse).astype(jnp.bfloat16)
+    lane = lax.broadcasted_iota(jnp.int32, (TILE, LANES), 1)
+    lines_ref[...] = jnp.transpose(jnp.where(lane == 0, row_max, row_sum))[0:SUBLANES]
 
 
 def home_kernel(places, lists_ref, counts_ref, query_ref, *refs):
@@ -174,23 +160,23 @@
 
 
 def merge_kernel(total_ref, stats_ref, *refs):
-    packed_refs, out_ref = refs[:-1], refs[-1]
+    returned, out_ref = refs[:-1], refs[-1]
+    partial_refs, lines_refs = returned[0::2], returned[1::2]
     maxima = [stats_ref[0]]
     sums = [stats_ref[1]]
-    for packed_ref in packed_refs:
-        packed = packed_ref[TILE:, 0:LANES].astype(jnp.float32)
-        for first, kept in ((0, maxima), (3, sums)):
-            line = packed[first : first + 1] + packed[first + 1 : first + 2] + packed[first + 2 : first + 3]
-            kept.append(jnp.transpose(jnp.broadcast_to(line, (TILE, LANES))))
+    for lines_ref in lines_refs:
+        turned = jnp.transpose(jnp.concatenate([lines_ref[...]] * (TILE // SUBLANES), axis=0))
+        maxima.append(jnp.broadcast_to(turned[:, 0:1], (TILE, LANES)))
+        sums.append(jnp.broadcast_to(turned[:, 1:2], (TILE, LANES)))
     top = functools.reduce(jnp.maximum, maxima)
     factors = [jnp.exp(row_max - top) for row_max in maxima]
     masses = [factor * row_sum for factor, row_sum in zip(factors, sums)]
     inverse = 1.0 / functools.reduce(jnp.add, masses)
-    scales = [factors[0] * inverse] + [mass * inverse for mass in masses[1:]]
+    shares = [factors[0] * inverse] + [mass * inverse for mass in masses[1:]]
     for at in range(0, total_ref.shape[1], LANES):
-        merged = total_ref[:, at : at + LANES] * scales[0]
-        for packed_ref, scale in zip(packed_refs, scales[1:]):
-            merged = merged + packed_ref[0:TILE, at : at + LANES].astype(jnp.float32) * scale
+        merged = total_ref[:, at : at + LANES] * shares[0]
+        for partial_ref, share in zip(partial_refs, shares[1:]):
+            merged = merged + partial_ref[:, at : at + LANES].astype(jnp.float32) * share
         out_ref[:, at : at + LANES] = merged.astype(jnp.bfloat16)
 
 
@@ -259,6 +245,7 @@
     attend_params = params(pieces_total * piece_rows * value_width * 2)
     own_specs = [pl.BlockSpec(memory_space=pl.ANY), VMEM]
     own_scratch = [pltpu.VMEM(library_keys.shape, library_keys.dtype), pltpu.SemaphoreType.DMA]
+    early = early + [((1, 0), partner_keys, partner_values)]
     early_arrays = arrays_of(early)
     states = []
     for mask, visiting in visitors:
@@ -273,15 +260,18 @@
         )(block_list, block_count, visiting, *early_arrays, library_keys, values)
         states.append(state)
 
-    late = [((1, 0), partner_keys, partner_values)] + cross_cores(early) + relayed + cross_cores(relayed, [state[2] for state in states])
+    late = cross_cores(early[:-1]) + relayed + cross_cores(relayed, [state[2] for state in states])
     late_arrays = arrays_of(late)
     returned = []
     for (mask, visiting), state in zip(visitors, states):
-        packed = pl.pallas_call(
+        partial, lines = pl.pallas_call(
             functools.partial(late_kernel, places_of(late), mask),
-            out_shape=jax.ShapeDtypeStruct((TILE + EXTRA, value_width), jnp.bfloat16),
+            out_shape=(
+                jax.ShapeDtypeStruct((TILE, value_width), jnp.bfloat16),
+                jax.ShapeDtypeStruct((SUBLANES, LANES), jnp.float32),
+            ),
             in_specs=[SMEM, SMEM] + [VMEM] * (4 + len(late_arrays)),
-            out_specs=VMEM,
+            out_specs=(VMEM, VMEM),
             scratch_shapes=[
                 pltpu.VMEM((len(late), TILE, TILE), jnp.float32),
                 pltpu.VMEM((TILE, value_width), jnp.float32),
@@ -290,7 +280,7 @@
             compiler_params=attend_params,
             cost_estimate=cost,
         )(block_list, block_count, visiting, *state, *late_arrays)
-        returned.append(swap(packed, "qry", mask))
+        returned += [swap(partial, "qry", mask), swap(lines, "qry", mask)]
 
     total, stats = pl.pallas_call(
         functools.partial(home_kernel, places_of(early + late)),

time: 36.2 us -> 37.9 us (1.047); the launches traced: 36 us -> 38.2 us
  starting transfers between devices: 17.7 us -> 18.7 us
  Pallas kernels: 4.26 us -> 5.2 us
    ppermute x16 -> x17, starting transfers between devices: 17.7 us -> 18.7 us  [swap(): return lax.ppermute(value, axis, [(i, i ^ mask) for i in range(length)])]
    pallas_call x1, Pallas kernels: 0.83 us -> 1.28 us  [body(): pl.pallas_call(functools.partial(early_kernel, places_of(early), mask), o...]
    pallas_call x1, Pallas kernels: 1.42 us -> 1.85 us  [body(): pl.pallas_call(functools.partial(home_kernel, places_of(early + late)), o...]
    ppermute x16 -> x17, waiting for transfers between devices: 12.4 us -> 12.6 us  [swap(): return lax.ppermute(value, axis, [(i, i ^ mask) for i in range(length)])]
  transfers between devices with their start and end apart: 16 -> 17, of which waited for: 7 -> 7; matrix products, arithmetic and copies ran while one was open for 0% -> 0% of each run, Pallas kernels for 7% -> 9%
where the time goes in v13:
time: 37.9 us; the launch traced here: 38.2 us
  starting transfers between devices  18.7 us (49%)
  waiting for transfers between devices  12.6 us (33%)
  Pallas kernels  5.2 us (14%)
  local copies, waits for them, and re-layouts  1.66 us (4%)
    ppermute x17, starting transfers between devices, swap(): return lax.ppermute(value, axis, [(i, i ^ mask) for i in range(length)])  18.7 us
    ppermute x17, waiting for transfers between devices, swap(): return lax.ppermute(value, axis, [(i, i ^ mask) for i in range(length)])  12.6 us
    pallas_call x1, Pallas kernels, body(): pl.pallas_call(functools.partial(home_kernel, places_of(early + late)), o...  1.85 us
    unnamed x13, local copies, waits for them, and re-layouts  1.66 us
    pallas_call x1, Pallas kernels, body(): pl.pallas_call(functools.partial(early_kernel, places_of(early), mask), o...  1.28 us
    pallas_call x1, Pallas kernels, body(): pl.pallas_call(functools.partial(late_kernel, places_of(late), mask), out...  1.02 us
    pallas_call x1, Pallas kernels, body(): pl.pallas_call(merge_kernel, out_shape=jax.ShapeDtypeStruct((TILE, value_...  0.88 us
  transfers between devices with their start and end apart: 17, of which 7 were waited for; matrix products, arithmetic and copies ran while one was open for 0% of the time, Pallas kernels for 9%

profile of v13, /device:TPU:0, one launch (start us, length us, event | category | flops | bytes accessed | tf_op | source)
XLA Modules:
  0.0 38.2 jit_solution(12713569759669515363)
XLA Ops:
  0.0 0.5 %collective-permute-start.1 = (bf16[128,1024]{1,0:T(8,128)(2,1)}, bf16[128,1024]{1,0:T(8,128)(2,1)S(1)}, u32[]{:S(2)}, u32[]{:S(2)}) collective-permute-start(bf16[128,1024]{1,0:T(8,128)(2,1)} %refs_14_.1), channel_id=1, source_target_pairs={{0,4},{4,0},{8,12},{12,8},{1,5},{5,1},{9,13},{13,9},{2,6},{6,2},{1... | collective-permute-start | bytes 786440 | tf_op jit(solution)/shard_map/ppermute | solution.py:26
  0.5 2.6 %collective-permute-start = (bf16[128,1024]{1,0:T(8,128)(2,1)}, bf16[128,1024]{1,0:T(8,128)(2,1)S(1)}, u32[]{:S(2)}, u32[]{:S(2)}) collective-permute-start(bf16[128,1024]{1,0:T(8,128)(2,1)} %refs_14_.1), channel_id=1, source_target_pairs={{0,1},{1,0},{2,3},{3,2},{4,5},{5,4},{6,7},{7,6},{8,9},{9,8},{10,11... | collective-permute-start | bytes 786440 | tf_op jit(solution)/shard_map/ppermute | solution.py:26
  3.1 1.5 %collective-permute-start.3 = (bf16[128,1024]{1,0:T(8,128)(2,1)}, bf16[128,1024]{1,0:T(8,128)(2,1)S(1)}, u32[]{:S(2)}, u32[]{:S(2)}) collective-permute-start(bf16[128,1024]{1,0:T(8,128)(2,1)} %refs_14_.1), channel_id=1, source_target_pairs={{0,8},{4,12},{8,0},{12,4},{1,9},{5,13},{9,1},{13,5},{2,10},{6,14},... | collective-permute-start | bytes 786440 | tf_op jit(solution)/shard_map/ppermute | solution.py:26
  4.6 0.9 %copy-done.2 = bf16[128,512]{1,0:T(8,128)(2,1)S(1)} copy-done((bf16[128,512]{1,0:T(8,128)(2,1)S(1)}, bf16[128,512]{1,0:T(8,128)(2,1)}, u32[]{:S(2)}) %copy-start.2) | copy-done | bytes 131096
  5.5 0.7 %copy-done.4 = bf16[128]{0:T(256)(128)(2,1)S(1)} copy-done((bf16[128]{0:T(256)(128)(2,1)S(1)}, bf16[128]{0:T(256)(128)(2,1)}, u32[]{:S(2)}) %copy-start.4) | copy-done | bytes 280
  6.1 0.2 shard_map.64.refs_7_.refs_15_
  6.3 0.0 copy-start.3
  6.3 0.1 collective-permute-start.5
  6.4 0.5 %collective-permute-start.2 = (bf16[144,512]{1,0:T(8,128)(2,1)S(1)}, bf16[144,512]{1,0:T(8,128)(2,1)S(1)}, u32[]{:S(2)}, u32[]{:S(2)}) collective-permute-start(bf16[144,512]{1,0:T(8,128)(2,1)S(1)} %shard_map.64.refs_7_.refs_15_), channel_id=1, source_target_pairs={{0,1},{1,0},{2,3},{3,2},{4,5},{5,4},{6,7},{7,6},{8,9},{9,8},{10,11... | collective-permute-start | bytes 442376 | tf_op jit(solution)/shard_map/ppermute | solution.py:26
  6.9 1.3 %collective-permute-start.4 = (bf16[144,512]{1,0:T(8,128)(2,1)S(1)}, bf16[144,512]{1,0:T(8,128)(2,1)S(1)}, u32[]{:S(2)}, u32[]{:S(2)}) collective-permute-start(bf16[144,512]{1,0:T(8,128)(2,1)S(1)} %shard_map.64.refs_7_.refs_15_), channel_id=1, source_target_pairs={{0,8},{4,12},{8,0},{12,4},{1,9},{5,13},{9,1},{13,5},{2,10},{6,14},... | collective-permute-start | bytes 442376 | tf_op jit(solution)/shard_map/ppermute | solution.py:26
  8.2 2.8 %collective-permute-start.12 = (bf16[128,1024]{1,0:T(8,128)(2,1)}, bf16[128,1024]{1,0:T(8,128)(2,1)S(1)}, u32[]{:S(2)}, u32[]{:S(2)}) collective-permute-start(bf16[128,1024]{1,0:T(8,128)(2,1)} %query_ref.1), channel_id=1, source_target_pairs={{0,3},{1,2},{2,1},{3,0},{4,7},{5,6},{6,5},{7,4},{8,11},{9,10},{10,... | collective-permute-start | bytes 786440 | tf_op jit(solution)/shard_map/ppermute | solution.py:26
  11.1 1.4 %collective-permute-done.3.refs_2_ = bf16[128,1024]{1,0:T(8,128)(2,1)S(1)} collective-permute-done((bf16[128,1024]{1,0:T(8,128)(2,1)}, bf16[128,1024]{1,0:T(8,128)(2,1)S(1)}, u32[]{:S(2)}, u32[]{:S(2)}) %collective-permute-start.3) | collective-permute-done | bytes 262176 | tf_op jit(solution)/shard_map/ppermute | solution.py:26
  12.5 1.5 %collective-permute-start.10 = (bf16[128,1024]{1,0:T(8,128)(2,1)S(1)}, bf16[128,1024]{1,0:T(8,128)(2,1)S(1)}, u32[]{:S(2)}, u32[]{:S(2)}) collective-permute-start(bf16[128,1024]{1,0:T(8,128)(2,1)S(1)} %collective-permute-done.refs_0_), channel_id=1, source_target_pairs={{0,8},{4,12},{8,0},{12,4},{1,9},{5,13},{9,1},{13,5},{2,10},{6,14},... | collective-permute-start | bytes 786440 | tf_op jit(solution)/shard_map/ppermute | solution.py:26
  13.9 0.0 collective-permute-done.2.refs_1_
  13.9 1.7 %collective-permute-done.4.refs_3_ = bf16[144,512]{1,0:T(8,128)(2,1)S(1)} collective-permute-done((bf16[144,512]{1,0:T(8,128)(2,1)S(1)}, bf16[144,512]{1,0:T(8,128)(2,1)S(1)}, u32[]{:S(2)}, u32[]{:S(2)}) %collective-permute-start.4) | collective-permute-done | bytes 147488 | tf_op jit(solution)/shard_map/ppermute | solution.py:26
  15.6 1.5 %collective-permute-start.11 = (bf16[144,512]{1,0:T(8,128)(2,1)S(1)}, bf16[144,512]{1,0:T(8,128)(2,1)S(1)}, u32[]{:S(2)}, u32[]{:S(2)}) collective-permute-start(bf16[144,512]{1,0:T(8,128)(2,1)S(1)} %collective-permute-done.2.refs_1_), channel_id=1, source_target_pairs={{0,8},{4,12},{8,0},{12,4},{1,9},{5,13},{9,1},{13,5},{2,10},{6,14},... | collective-permute-start | bytes 442376 | tf_op jit(solution)/shard_map/ppermute | solution.py:26
  17.1 0.0 collective-permute-start.7
  17.1 0.1 copy.8.lists_ref
  17.2 0.5 %collective-permute-start.6 = (bf16[128,1024]{1,0:T(8,128)(2,1)S(1)}, bf16[128,1024]{1,0:T(8,128)(2,1)S(1)}, u32[]{:S(2)}, u32[]{:S(2)}) collective-permute-start(bf16[128,1024]{1,0:T(8,128)(2,1)S(1)} %collective-permute-done.refs_0_), channel_id=1, source_target_pairs={{0,4},{4,0},{8,12},{12,8},{1,5},{5,1},{9,13},{13,9},{2,6},{6,2},{1... | collective-permute-start | bytes 786440 | tf_op jit(solution)/shard_map/ppermute | solution.py:26
  17.7 3.6 %collective-permute-done.12.query_ref = bf16[128,1024]{1,0:T(8,128)(2,1)S(1)} collective-permute-done((bf16[128,1024]{1,0:T(8,128)(2,1)}, bf16[128,1024]{1,0:T(8,128)(2,1)S(1)}, u32[]{:S(2)}, u32[]{:S(2)}) %collective-permute-start.12) | collective-permute-done | bytes 262176 | tf_op jit(solution)/shard_map/ppermute | solution.py:26
  21.3 1.3 %shard_map.65 = (f32[128,512]{1,0:T(8,128)S(1)}, f32[128,128]{1,0:T(8,128)S(1)}, f32[128,128]{1,0:T(8,128)S(1)}) custom-call(s32[16,4]{1,0:T(8,128)S(1)} %copy.8.lists_ref, s32[16]{0:T(128)S(1)} %copy-done.3, bf16[128,1024]{1,0:T(8,128)(2,1)S(1)} %collective-permute-done.12.query_ref, bf16[128,1024]{1,0:T(8,128)(2,1)S(1)} %collective-permute-done.refs_0_, ...), custom_call_target="tpu_custom_call" | custom-call | flops 268435456 | bytes 4194304 | tf_op jit(solution)/shard_map/pallas_call | solution.py:252
  22.6 1.0 %collective-permute-done.11.refs_11_.refs_8_ = bf16[144,512]{1,0:T(8,128)(2,1)S(1)} collective-permute-done((bf16[144,512]{1,0:T(8,128)(2,1)S(1)}, bf16[144,512]{1,0:T(8,128)(2,1)S(1)}, u32[]{:S(2)}, u32[]{:S(2)}) %collective-permute-start.11) | collective-permute-done | bytes 147488 | tf_op jit(solution)/shard_map/ppermute | solution.py:26
  23.6 0.5 %collective-permute-start.9 = (bf16[144,512]{1,0:T(8,128)(2,1)S(1)}, bf16[144,512]{1,0:T(8,128)(2,1)S(1)}, u32[]{:S(2)}, u32[]{:S(2)}) collective-permute-start(bf16[144,512]{1,0:T(8,128)(2,1)S(1)} %collective-permute-done.4.refs_3_), channel_id=1, source_target_pairs={{0,4},{4,0},{8,12},{12,8},{1,5},{5,1},{9,13},{13,9},{2,6},{6,2},{1... | collective-permute-start | bytes 442376 | tf_op jit(solution)/shard_map/ppermute | solution.py:26
  24.1 0.0 collective-permute-start.14
  24.1 1.2 %collective-permute-done.9.refs_9_.refs_6_ = bf16[144,512]{1,0:T(8,128)(2,1)S(1)} collective-permute-done((bf16[144,512]{1,0:T(8,128)(2,1)S(1)}, bf16[144,512]{1,0:T(8,128)(2,1)S(1)}, u32[]{:S(2)}, u32[]{:S(2)}) %collective-permute-start.9) | collective-permute-done | bytes 147488 | tf_op jit(solution)/shard_map/ppermute | solution.py:26
  25.4 0.2 collective-permute-done.14.refs_13_.refs_10_
  25.6 1.0 %shard_map.67 = (bf16[128,512]{1,0:T(8,128)(2,1)S(1)}, f32[8,128]{1,0:T(8,128)S(1)}) custom-call(s32[16,4]{1,0:T(8,128)S(1)} %copy.8.lists_ref, s32[16]{0:T(128)S(1)} %copy-done.3, bf16[128,1024]{1,0:T(8,128)(2,1)S(1)} %collective-permute-done.12.query_ref, f32[128,512]{1,0:T(8,128)S(1)} %get-tuple-element.35.refs_0_, ...), custom_call_target="tpu_custom_call" | custom-call | flops 268435456 | bytes 4194304 | tf_op jit(solution)/shard_map/pallas_call | solution.py:267
  26.6 5.3 %collective-permute-start.15 = (bf16[128,512]{1,0:T(8,128)(2,1)S(1)}, bf16[128,512]{1,0:T(8,128)(2,1)S(1)}, u32[]{:S(2)}, u32[]{:S(2)}) collective-permute-start(bf16[128,512]{1,0:T(8,128)(2,1)S(1)} %get-tuple-element.37), channel_id=1, source_target_pairs={{0,3},{1,2},{2,1},{3,0},{4,7},{5,6},{6,5},{7,4},{8,11},{9,10},{10,... | collective-permute-start | bytes 393224 | tf_op jit(solution)/shard_map/ppermute | solution.py:26
  31.9 0.1 collective-permute-start.16
  32.0 1.9 %shard_map.66 = (f32[128,512]{1,0:T(8,128)S(1)}, f32[2,128,128]{2,1,0:T(8,128)S(1)}) custom-call(s32[16,4]{1,0:T(8,128)S(1)} %copy.8.lists_ref, s32[16]{0:T(128)S(1)} %copy-done.3, bf16[128,1024]{1,0:T(8,128)(2,1)S(1)} %copy-done.1, bf16[128,1024]{1,0:T(8,128)(2,1)S(1)} %collective-permute-done.refs_0_, bf16[144,512]{1,0:T(8,128)(2,1)S(1)} %collective-permute-done.2.refs_1_, ...), custom_call_target="tpu_custom_call" | custom-call | flops 268435456 | bytes 4194304 | tf_op jit(solution)/shard_map/pallas_call | solution.py:285
  33.9 3.5 %collective-permute-done.16.refs_1_ = f32[8,128]{1,0:T(8,128)S(1)} collective-permute-done((f32[8,128]{1,0:T(8,128)S(1)}, f32[8,128]{1,0:T(8,128)S(1)}, u32[]{:S(2)}, u32[]{:S(2)}) %collective-permute-start.16) | collective-permute-done | bytes 4128 | tf_op jit(solution)/shard_map/ppermute | solution.py:26
  37.3 0.9 %shard_map.68 = bf16[128,512]{1,0:T(8,128)(2,1)} custom-call(f32[128,512]{1,0:T(8,128)S(1)} %get-tuple-element.33.total_ref, f32[2,128,128]{2,1,0:T(8,128)S(1)} %get-tuple-element.34.stats_ref, bf16[128,512]{1,0:T(8,128)(2,1)S(1)} %collective-permute-done.15.refs_0_, f32[8,128]{1,0:T(8,128)S(1)} %collective-permute-done.16.refs_1_), custom_call_target="tpu_custom_call" | custom-call | tf_op jit(solution)/shard_map/pallas_call | solution.py:299
  (20 shorter events, 0.0 us)
Async XLA Ops:
  0.0 21.3 %copy-start = (bf16[128,1024]{1,0:T(8,128)(2,1)S(1)}, bf16[128,1024]{1,0:T(8,128)(2,1)}, u32[]{:S(2)}) copy-start(bf16[128,1024]{1,0:T(8,128)(2,1)} %refs_14_.1) | copy-start | bytes 786436
  0.0 4.6 %collective-permute-start.1 = (bf16[128,1024]{1,0:T(8,128)(2,1)}, bf16[128,1024]{1,0:T(8,128)(2,1)S(1)}, u32[]{:S(2)}, u32[]{:S(2)}) collective-permute-start(bf16[128,1024]{1,0:T(8,128)(2,1)} %refs_14_.1), channel_id=1, source_target_pairs={{0,4},{4,0},{8,12},{12,8},{1,5},{5,1},{9,13},{13,9},{2,6},{6,2},{1... | collective-permute-start | bytes 786440 | tf_op jit(solution)/shard_map/ppermute | solution.py:26
  0.5 10.6 %collective-permute-start = (bf16[128,1024]{1,0:T(8,128)(2,1)}, bf16[128,1024]{1,0:T(8,128)(2,1)S(1)}, u32[]{:S(2)}, u32[]{:S(2)}) collective-permute-start(bf16[128,1024]{1,0:T(8,128)(2,1)} %refs_14_.1), channel_id=1, source_target_pairs={{0,1},{1,0},{2,3},{3,2},{4,5},{5,4},{6,7},{7,6},{8,9},{9,8},{10,11... | collective-permute-start | bytes 786440 | tf_op jit(solution)/shard_map/ppermute | solution.py:26
  3.1 9.4 %collective-permute-start.3 = (bf16[128,1024]{1,0:T(8,128)(2,1)}, bf16[128,1024]{1,0:T(8,128)(2,1)S(1)}, u32[]{:S(2)}, u32[]{:S(2)}) collective-permute-start(bf16[128,1024]{1,0:T(8,128)(2,1)} %refs_14_.1), channel_id=1, source_target_pairs={{0,8},{4,12},{8,0},{12,4},{1,9},{5,13},{9,1},{13,5},{2,10},{6,14},... | collective-permute-start | bytes 786440 | tf_op jit(solution)/shard_map/ppermute | solution.py:26
  4.6 0.9 %copy-start.2 = (bf16[128,512]{1,0:T(8,128)(2,1)S(1)}, bf16[128,512]{1,0:T(8,128)(2,1)}, u32[]{:S(2)}) copy-start(bf16[128,512]{1,0:T(8,128)(2,1)} %values_ref) | copy-start | bytes 393220
  5.5 0.7 %copy-start.4 = (bf16[128]{0:T(256)(128)(2,1)S(1)}, bf16[128]{0:T(256)(128)(2,1)}, u32[]{:S(2)}) copy-start(bf16[128]{0:T(256)(128)(2,1)} %param.9) | copy-start | bytes 772
  6.1 11.0 %copy-start.5 = (s32[16,4]{0,1:T(4,128)S(1)}, s32[16,4]{0,1:T(4,128)}, u32[]{:S(2)}) copy-start(s32[16,4]{0,1:T(4,128)} %param.10) | copy-start | bytes 772
  6.3 15.0 %copy-start.3 = (s32[16]{0:T(128)S(1)}, s32[16]{0:T(128)}, u32[]{:S(2)}) copy-start(s32[16]{0:T(128)} %counts_ref.5) | copy-start | bytes 196
  6.3 1.9 %collective-permute-start.5 = (bf16[144,512]{1,0:T(8,128)(2,1)S(1)}, bf16[144,512]{1,0:T(8,128)(2,1)S(1)}, u32[]{:S(2)}, u32[]{:S(2)}) collective-permute-start(bf16[144,512]{1,0:T(8,128)(2,1)S(1)} %shard_map.64.refs_7_.refs_15_), channel_id=1, source_target_pairs={{0,4},{4,0},{8,12},{12,8},{1,5},{5,1},{9,13},{13,9},{2,6},{6,2},{1... | collective-permute-start | bytes 442376 | tf_op jit(solution)/shard_map/ppermute | solution.py:26
  6.4 7.5 %collective-permute-start.2 = (bf16[144,512]{1,0:T(8,128)(2,1)S(1)}, bf16[144,512]{1,0:T(8,128)(2,1)S(1)}, u32[]{:S(2)}, u32[]{:S(2)}) collective-permute-start(bf16[144,512]{1,0:T(8,128)(2,1)S(1)} %shard_map.64.refs_7_.refs_15_), channel_id=1, source_target_pairs={{0,1},{1,0},{2,3},{3,2},{4,5},{5,4},{6,7},{7,6},{8,9},{9,8},{10,11... | collective-permute-start | bytes 442376 | tf_op jit(solution)/shard_map/ppermute | solution.py:26
  6.9 8.7 %collective-permute-start.4 = (bf16[144,512]{1,0:T(8,128)(2,1)S(1)}, bf16[144,512]{1,0:T(8,128)(2,1)S(1)}, u32[]{:S(2)}, u32[]{:S(2)}) collective-permute-start(bf16[144,512]{1,0:T(8,128)(2,1)S(1)} %shard_map.64.refs_7_.refs_15_), channel_id=1, source_target_pairs={{0,8},{4,12},{8,0},{12,4},{1,9},{5,13},{9,1},{13,5},{2,10},{6,14},... | collective-permute-start | bytes 442376 | tf_op jit(solution)/shard_map/ppermute | solution.py:26
  8.2 13.1 %collective-permute-start.12 = (bf16[128,1024]{1,0:T(8,128)(2,1)}, bf16[128,1024]{1,0:T(8,128)(2,1)S(1)}, u32[]{:S(2)}, u32[]{:S(2)}) collective-permute-start(bf16[128,1024]{1,0:T(8,128)(2,1)} %query_ref.1), channel_id=1, source_target_pairs={{0,3},{1,2},{2,1},{3,0},{4,7},{5,6},{6,5},{7,4},{8,11},{9,10},{10,... | collective-permute-start | bytes 786440 | tf_op jit(solution)/shard_map/ppermute | solution.py:26
  12.5 10.1 %collective-permute-start.10 = (bf16[128,1024]{1,0:T(8,128)(2,1)S(1)}, bf16[128,1024]{1,0:T(8,128)(2,1)S(1)}, u32[]{:S(2)}, u32[]{:S(2)}) collective-permute-start(bf16[128,1024]{1,0:T(8,128)(2,1)S(1)} %collective-permute-done.refs_0_), channel_id=1, source_target_pairs={{0,8},{4,12},{8,0},{12,4},{1,9},{5,13},{9,1},{13,5},{2,10},{6,14},... | collective-permute-start | bytes 786440 | tf_op jit(solution)/shard_map/ppermute | solution.py:26
  15.6 8.0 %collective-permute-start.11 = (bf16[144,512]{1,0:T(8,128)(2,1)S(1)}, bf16[144,512]{1,0:T(8,128)(2,1)S(1)}, u32[]{:S(2)}, u32[]{:S(2)}) collective-permute-start(bf16[144,512]{1,0:T(8,128)(2,1)S(1)} %collective-permute-done.2.refs_1_), channel_id=1, source_target_pairs={{0,8},{4,12},{8,0},{12,4},{1,9},{5,13},{9,1},{13,5},{2,10},{6,14},... | collective-permute-start | bytes 442376 | tf_op jit(solution)/shard_map/ppermute | solution.py:26
  17.1 7.0 %collective-permute-start.7 = (bf16[144,512]{1,0:T(8,128)(2,1)S(1)}, bf16[144,512]{1,0:T(8,128)(2,1)S(1)}, u32[]{:S(2)}, u32[]{:S(2)}) collective-permute-start(bf16[144,512]{1,0:T(8,128)(2,1)S(1)} %collective-permute-done.2.refs_1_), channel_id=1, source_target_pairs={{0,4},{4,0},{8,12},{12,8},{1,5},{5,1},{9,13},{13,9},{2,6},{6,2},{1... | collective-permute-start | bytes 442376 | tf_op jit(solution)/shard_map/ppermute | solution.py:26
  17.2 8.2 %collective-permute-start.6 = (bf16[128,1024]{1,0:T(8,128)(2,1)S(1)}, bf16[128,1024]{1,0:T(8,128)(2,1)S(1)}, u32[]{:S(2)}, u32[]{:S(2)}) collective-permute-start(bf16[128,1024]{1,0:T(8,128)(2,1)S(1)} %collective-permute-done.refs_0_), channel_id=1, source_target_pairs={{0,4},{4,0},{8,12},{12,8},{1,5},{5,1},{9,13},{13,9},{2,6},{6,2},{1... | collective-permute-start | bytes 786440 | tf_op jit(solution)/shard_map/ppermute | solution.py:26
  21.3 4.1 %collective-permute-start.8 = (bf16[128,1024]{1,0:T(8,128)(2,1)S(1)}, bf16[128,1024]{1,0:T(8,128)(2,1)S(1)}, u32[]{:S(2)}, u32[]{:S(2)}) collective-permute-start(bf16[128,1024]{1,0:T(8,128)(2,1)S(1)} %collective-permute-done.3.refs_2_), channel_id=1, source_target_pairs={{0,4},{4,0},{8,12},{12,8},{1,5},{5,1},{9,13},{13,9},{2,6},{6,2},{1... | collective-permute-start | bytes 786440 | tf_op jit(solution)/shard_map/ppermute | solution.py:26
  23.6 2.0 %collective-permute-start.13 = (bf16[128,1024]{1,0:T(8,128)(2,1)S(1)}, bf16[128,1024]{1,0:T(8,128)(2,1)S(1)}, u32[]{:S(2)}, u32[]{:S(2)}) collective-permute-start(bf16[128,1024]{1,0:T(8,128)(2,1)S(1)} %collective-permute-done.10.refs_10_.refs_7_), channel_id=1, source_target_pairs={{0,4},{4,0},{8,12},{12,8},{1,5},{5,1},{9,13},{13,9},{2,6},{6,2},{1... | collective-permute-start | bytes 786440 | tf_op jit(solution)/shard_map/ppermute | solution.py:26
  23.6 1.7 %collective-permute-start.9 = (bf16[144,512]{1,0:T(8,128)(2,1)S(1)}, bf16[144,512]{1,0:T(8,128)(2,1)S(1)}, u32[]{:S(2)}, u32[]{:S(2)}) collective-permute-start(bf16[144,512]{1,0:T(8,128)(2,1)S(1)} %collective-permute-done.4.refs_3_), channel_id=1, source_target_pairs={{0,4},{4,0},{8,12},{12,8},{1,5},{5,1},{9,13},{13,9},{2,6},{6,2},{1... | collective-permute-start | bytes 442376 | tf_op jit(solution)/shard_map/ppermute | solution.py:26
  24.1 1.4 %collective-permute-start.14 = (bf16[144,512]{1,0:T(8,128)(2,1)S(1)}, bf16[144,512]{1,0:T(8,128)(2,1)S(1)}, u32[]{:S(2)}, u32[]{:S(2)}) collective-permute-start(bf16[144,512]{1,0:T(8,128)(2,1)S(1)} %collective-permute-done.11.refs_11_.refs_8_), channel_id=1, source_target_pairs={{0,4},{4,0},{8,12},{12,8},{1,5},{5,1},{9,13},{13,9},{2,6},{6,2},{1... | collective-permute-start | bytes 442376 | tf_op jit(solution)/shard_map/ppermute | solution.py:26
  25.6 6.4 %copy-start.1 = (bf16[128,1024]{1,0:T(8,128)(2,1)S(1)}, bf16[128,1024]{1,0:T(8,128)(2,1)}, u32[]{:S(2)}) copy-start(bf16[128,1024]{1,0:T(8,128)(2,1)} %query_ref.1) | copy-start | bytes 786436
  26.6 10.7 %collective-permute-start.15 = (bf16[128,512]{1,0:T(8,128)(2,1)S(1)}, bf16[128,512]{1,0:T(8,128)(2,1)S(1)}, u32[]{:S(2)}, u32[]{:S(2)}) collective-permute-start(bf16[128,512]{1,0:T(8,128)(2,1)S(1)} %get-tuple-element.37), channel_id=1, source_target_pairs={{0,3},{1,2},{2,1},{3,0},{4,7},{5,6},{6,5},{7,4},{8,11},{9,10},{10,... | collective-permute-start | bytes 393224 | tf_op jit(solution)/shard_map/ppermute | solution.py:26
  31.9 5.4 %collective-permute-start.16 = (f32[8,128]{1,0:T(8,128)S(1)}, f32[8,128]{1,0:T(8,128)S(1)}, u32[]{:S(2)}, u32[]{:S(2)}) collective-permute-start(f32[8,128]{1,0:T(8,128)S(1)} %get-tuple-element.38), channel_id=1, source_target_pairs={{0,3},{1,2},{2,1},{3,0},{4,7},{5,6},{6,5},{7,4},{8,11},{9,10},{10,... | collective-permute-start | bytes 12296 | tf_op jit(solution)/shard_map/ppermute | solution.py:26

commit v14 on v12

--- a/solution.py
+++ b/solution.py
@@ -12,7 +12,6 @@
 LANES = 128
 EXTRA = 16
 MASKED_SCORE = -1e30
-SMEM = pl.BlockSpec(memory_space=pltpu.SMEM)
 VMEM = pl.BlockSpec(memory_space=pltpu.VMEM)
 
 
@@ -81,14 +80,21 @@
     return pieces, refs
 
 
+def pick(ref, row, column):
+    rows = lax.broadcasted_iota(jnp.int32, ref.shape, 0)
+    columns = lax.broadcasted_iota(jnp.int32, ref.shape, 1)
+    chosen = jnp.where((rows == row) & (columns == column), ref[...], 0)
+    return jnp.sum(chosen.astype(jnp.float32)).astype(jnp.int32)
+
+
 def attend(pieces, panel_mask, lists_ref, counts_ref, query_ref, score_ref, total_ref, mass_ref, before=None):
     lib_index = lax.axis_index("lib")
     qry_index = lax.axis_index("qry")
     qry_count = lax.axis_size("qry")
     block_total = lax.axis_size("lib") * qry_count
     panel = lib_index * qry_count + lax.bitwise_xor(qry_index, panel_mask)
-    first = lists_ref[panel, 0]
-    count = counts_ref[panel]
+    first = pick(lists_ref, 0, panel)
+    count = pick(counts_ref, 0, panel)
     width = query_ref.shape[1]
     inverse_root = 1.0 / math.sqrt(width)
 
@@ -249,6 +255,8 @@
         compiler_params=params(),
     )(own_values, key_scale.reshape(1, TILE))
 
+    window_lists = block_list.T
+    window_counts = block_count.reshape(1, -1)
     masks = [2 * at + 1 for at in range(1, qry_count // 2)]
     early, relayed, partner_values, visitors = gather_library(library_keys, values, queries, masks)
     piece_rows = (width // value_width + 1) * TILE + EXTRA
@@ -265,12 +273,12 @@
         state = pl.pallas_call(
             functools.partial(early_kernel, places_of(early), mask),
             out_shape=(total_shape, line_shape, line_shape),
-            in_specs=[SMEM, SMEM] + [VMEM] * (1 + len(early_arrays)) + own_specs,
+            in_specs=[VMEM, VMEM] + [VMEM] * (1 + len(early_arrays)) + own_specs,
             out_specs=(VMEM,) * 3,
             scratch_shapes=[pltpu.VMEM((len(early) + 1, TILE, TILE), jnp.float32)] + own_scratch,
             compiler_params=attend_params,
             cost_estimate=cost,
-        )(block_list, block_count, visiting, *early_arrays, library_keys, values)
+        )(window_lists, window_counts, visiting, *early_arrays, library_keys, values)
         states.append(state)
 
     late = [((1, 0), partner_keys, partner_values)] + cross_cores(early) + relayed + cross_cores(relayed, [state[2] for state in states])
@@ -280,7 +288,7 @@
         packed = pl.pallas_call(
             functools.partial(late_kernel, places_of(late), mask),
             out_shape=jax.ShapeDtypeStruct((TILE + EXTRA, value_width), jnp.bfloat16),
-            in_specs=[SMEM, SMEM] + [VMEM] * (4 + len(late_arrays)),
+            in_specs=[VMEM, VMEM] + [VMEM] * (4 + len(late_arrays)),
             out_specs=VMEM,
             scratch_shapes=[
                 pltpu.VMEM((len(late), TILE, TILE), jnp.float32),
@@ -289,13 +297,13 @@
             ],
             compiler_params=attend_params,
             cost_estimate=cost,
-        )(block_list, block_count, visiting, *state, *late_arrays)
+        )(window_lists, window_counts, visiting, *state, *late_arrays)
         returned.append(swap(packed, "qry", mask))
 
     total, stats = pl.pallas_call(
         functools.partial(home_kernel, places_of(early + late)),
         out_shape=(total_shape, jax.ShapeDtypeStruct((2, TILE, LANES), jnp.float32)),
-        in_specs=[SMEM, SMEM] + [VMEM] * (1 + len(early_arrays) + len(late_arrays)) + own_specs,
+        in_specs=[VMEM, VMEM] + [VMEM] * (1 + len(early_arrays) + len(late_arrays)) + own_specs,
         out_specs=(VMEM, VMEM),
         scratch_shapes=[
             pltpu.VMEM((pieces_total, TILE, TILE), jnp.float32),
@@ -304,7 +312,7 @@
         + own_scratch,
         compiler_params=attend_params,
         cost_estimate=cost,
-    )(block_list, block_count, queries, *early_arrays, *late_arrays, library_keys, values)
+    )(window_lists, window_counts, queries, *early_arrays, *late_arrays, library_keys, values)
 
     return pl.pallas_call(
         merge_kernel,

time: 36.2 us -> 36.2 us (level); the launches traced: 36 us -> 36.5 us
  Pallas kernels: 4.26 us -> 3.02 us
  starting transfers between devices: 17.7 us -> 18.7 us
  local copies, waits for them, and re-layouts: 1.66 us -> 2.21 us
    ppermute x16, starting transfers between devices: 17.7 us -> 18.7 us  [swap(): return lax.ppermute(value, axis, [(i, i ^ mask) for i in range(length)])]
    pallas_call x1, Pallas kernels: 0.83 us -> 0.28 us  [body(): pl.pallas_call(functools.partial(early_kernel, places_of(early), mask), o...]
    unnamed x13 -> x12, local copies, waits for them, and re-layouts: 1.66 us -> 2.21 us
    pallas_call x1, Pallas kernels: 1.03 us -> 0.48 us  [body(): pl.pallas_call(functools.partial(late_kernel, places_of(late), mask), out...]
  transfers between devices with their start and end apart: 16 -> 16, of which waited for: 7 -> 7; matrix products, arithmetic and copies ran while one was open for 0% -> 0% of each run, Pallas kernels for 7% -> 5%
where the time goes in v14:
time: 36.2 us; the launch traced here: 36.5 us
  starting transfers between devices  18.7 us (52%)
  waiting for transfers between devices  12.5 us (35%)
  Pallas kernels  3.02 us (8%)
  local copies, waits for them, and re-layouts  2.21 us (6%)
    ppermute x16, starting transfers between devices, swap(): return lax.ppermute(value, axis, [(i, i ^ mask) for i in range(length)])  18.7 us
    ppermute x16, waiting for transfers between devices, swap(): return lax.ppermute(value, axis, [(i, i ^ mask) for i in range(length)])  12.5 us
    unnamed x12, local copies, waits for them, and re-layouts  2.21 us
    pallas_call x1, Pallas kernels, body(): pl.pallas_call(functools.partial(home_kernel, places_of(early + late)), o...  1.29 us
    pallas_call x1, Pallas kernels, body(): pl.pallas_call(merge_kernel, out_shape=jax.ShapeDtypeStruct((TILE, value_...  0.82 us
  transfers between devices with their start and end apart: 16, of which 7 were waited for; matrix products, arithmetic and copies ran while one was open for 0% of the time, Pallas kernels for 5%

profile of v14, /device:TPU:0, one launch (start us, length us, event | category | flops | bytes accessed | tf_op | source)
XLA Modules:
  0.0 36.5 jit_solution(12232295814066726439)
XLA Ops:
  0.0 0.5 %collective-permute-start.1 = (bf16[128,1024]{1,0:T(8,128)(2,1)}, bf16[128,1024]{1,0:T(8,128)(2,1)S(1)}, u32[]{:S(2)}, u32[]{:S(2)}) collective-permute-start(bf16[128,1024]{1,0:T(8,128)(2,1)} %refs_14_.1), channel_id=1, source_target_pairs={{0,4},{4,0},{8,12},{12,8},{1,5},{5,1},{9,13},{13,9},{2,6},{6,2},{1... | collective-permute-start | bytes 786440 | tf_op jit(solution)/shard_map/ppermute | solution.py:24
  0.5 2.6 %collective-permute-start = (bf16[128,1024]{1,0:T(8,128)(2,1)}, bf16[128,1024]{1,0:T(8,128)(2,1)S(1)}, u32[]{:S(2)}, u32[]{:S(2)}) collective-permute-start(bf16[128,1024]{1,0:T(8,128)(2,1)} %refs_14_.1), channel_id=1, source_target_pairs={{0,1},{1,0},{2,3},{3,2},{4,5},{5,4},{6,7},{7,6},{8,9},{9,8},{10,11... | collective-permute-start | bytes 786440 | tf_op jit(solution)/shard_map/ppermute | solution.py:24
  3.1 1.5 %collective-permute-start.3 = (bf16[128,1024]{1,0:T(8,128)(2,1)}, bf16[128,1024]{1,0:T(8,128)(2,1)S(1)}, u32[]{:S(2)}, u32[]{:S(2)}) collective-permute-start(bf16[128,1024]{1,0:T(8,128)(2,1)} %refs_14_.1), channel_id=1, source_target_pairs={{0,8},{4,12},{8,0},{12,4},{1,9},{5,13},{9,1},{13,5},{2,10},{6,14},... | collective-permute-start | bytes 786440 | tf_op jit(solution)/shard_map/ppermute | solution.py:24
  4.6 0.0 collective-permute-done.1.refs_4_.refs_3_
  4.6 0.9 %copy-done.2 = bf16[128,512]{1,0:T(8,128)(2,1)S(1)} copy-done((bf16[128,512]{1,0:T(8,128)(2,1)S(1)}, bf16[128,512]{1,0:T(8,128)(2,1)}, u32[]{:S(2)}) %copy-start.2) | copy-done | bytes 131096
  5.5 0.7 %copy-done.5 = bf16[128]{0:T(256)(128)(2,1)S(1)} copy-done((bf16[128]{0:T(256)(128)(2,1)S(1)}, bf16[128]{0:T(256)(128)(2,1)}, u32[]{:S(2)}) %copy-start.5) | copy-done | bytes 280
  6.1 0.2 shard_map.64.refs_5_.refs_15_
  6.3 0.0 copy-start.3
  6.3 0.1 collective-permute-start.5
  6.4 0.5 %collective-permute-start.2 = (bf16[144,512]{1,0:T(8,128)(2,1)S(1)}, bf16[144,512]{1,0:T(8,128)(2,1)S(1)}, u32[]{:S(2)}, u32[]{:S(2)}) collective-permute-start(bf16[144,512]{1,0:T(8,128)(2,1)S(1)} %shard_map.64.refs_5_.refs_15_), channel_id=1, source_target_pairs={{0,1},{1,0},{2,3},{3,2},{4,5},{5,4},{6,7},{7,6},{8,9},{9,8},{10,11... | collective-permute-start | bytes 442376 | tf_op jit(solution)/shard_map/ppermute | solution.py:24
  6.9 1.3 %collective-permute-start.4 = (bf16[144,512]{1,0:T(8,128)(2,1)S(1)}, bf16[144,512]{1,0:T(8,128)(2,1)S(1)}, u32[]{:S(2)}, u32[]{:S(2)}) collective-permute-start(bf16[144,512]{1,0:T(8,128)(2,1)S(1)} %shard_map.64.refs_5_.refs_15_), channel_id=1, source_target_pairs={{0,8},{4,12},{8,0},{12,4},{1,9},{5,13},{9,1},{13,5},{2,10},{6,14},... | collective-permute-start | bytes 442376 | tf_op jit(solution)/shard_map/ppermute | solution.py:24
  8.2 0.0 collective-permute-done.5.refs_5_.refs_4_
  8.2 2.8 %collective-permute-start.12 = (bf16[128,1024]{1,0:T(8,128)(2,1)}, bf16[128,1024]{1,0:T(8,128)(2,1)S(1)}, u32[]{:S(2)}, u32[]{:S(2)}) collective-permute-start(bf16[128,1024]{1,0:T(8,128)(2,1)} %query_ref.1), channel_id=1, source_target_pairs={{0,3},{1,2},{2,1},{3,0},{4,7},{5,6},{6,5},{7,4},{8,11},{9,10},{10,... | collective-permute-start | bytes 786440 | tf_op jit(solution)/shard_map/ppermute | solution.py:24
  11.1 0.0 collective-permute-done.refs_0_
  11.1 1.4 %collective-permute-done.3.refs_2_ = bf16[128,1024]{1,0:T(8,128)(2,1)S(1)} collective-permute-done((bf16[128,1024]{1,0:T(8,128)(2,1)}, bf16[128,1024]{1,0:T(8,128)(2,1)S(1)}, u32[]{:S(2)}, u32[]{:S(2)}) %collective-permute-start.3) | collective-permute-done | bytes 262176 | tf_op jit(solution)/shard_map/ppermute | solution.py:24
  12.5 1.5 %collective-permute-start.10 = (bf16[128,1024]{1,0:T(8,128)(2,1)S(1)}, bf16[128,1024]{1,0:T(8,128)(2,1)S(1)}, u32[]{:S(2)}, u32[]{:S(2)}) collective-permute-start(bf16[128,1024]{1,0:T(8,128)(2,1)S(1)} %collective-permute-done.refs_0_), channel_id=1, source_target_pairs={{0,8},{4,12},{8,0},{12,4},{1,9},{5,13},{9,1},{13,5},{2,10},{6,14},... | collective-permute-start | bytes 786440 | tf_op jit(solution)/shard_map/ppermute | solution.py:24
  13.9 1.7 %collective-permute-done.4.refs_3_ = bf16[144,512]{1,0:T(8,128)(2,1)S(1)} collective-permute-done((bf16[144,512]{1,0:T(8,128)(2,1)S(1)}, bf16[144,512]{1,0:T(8,128)(2,1)S(1)}, u32[]{:S(2)}, u32[]{:S(2)}) %collective-permute-start.4) | collective-permute-done | bytes 147488 | tf_op jit(solution)/shard_map/ppermute | solution.py:24
  15.6 1.5 %collective-permute-start.11 = (bf16[144,512]{1,0:T(8,128)(2,1)S(1)}, bf16[144,512]{1,0:T(8,128)(2,1)S(1)}, u32[]{:S(2)}, u32[]{:S(2)}) collective-permute-start(bf16[144,512]{1,0:T(8,128)(2,1)S(1)} %collective-permute-done.2.refs_1_), channel_id=1, source_target_pairs={{0,8},{4,12},{8,0},{12,4},{1,9},{5,13},{9,1},{13,5},{2,10},{6,14},... | collective-permute-start | bytes 442376 | tf_op jit(solution)/shard_map/ppermute | solution.py:24
  17.1 0.5 %collective-permute-start.6 = (bf16[128,1024]{1,0:T(8,128)(2,1)S(1)}, bf16[128,1024]{1,0:T(8,128)(2,1)S(1)}, u32[]{:S(2)}, u32[]{:S(2)}) collective-permute-start(bf16[128,1024]{1,0:T(8,128)(2,1)S(1)} %collective-permute-done.refs_0_), channel_id=1, source_target_pairs={{0,4},{4,0},{8,12},{12,8},{1,5},{5,1},{9,13},{13,9},{2,6},{6,2},{1... | collective-permute-start | bytes 786440 | tf_op jit(solution)/shard_map/ppermute | solution.py:24
  17.6 3.7 %collective-permute-done.12.query_ref = bf16[128,1024]{1,0:T(8,128)(2,1)S(1)} collective-permute-done((bf16[128,1024]{1,0:T(8,128)(2,1)}, bf16[128,1024]{1,0:T(8,128)(2,1)S(1)}, u32[]{:S(2)}, u32[]{:S(2)}) %collective-permute-start.12) | collective-permute-done | bytes 262176 | tf_op jit(solution)/shard_map/ppermute | solution.py:24
  21.3 0.6 %copy-done.4 = s32[16]{0:T(128)S(1)} copy-done((s32[16]{0:T(128)S(1)}, s32[16]{0:T(128)}, u32[]{:S(2)}) %copy-start.4) | copy-done | bytes 88
  22.0 0.3 shard_map.65
  22.2 1.4 %collective-permute-done.11.refs_11_.refs_10_ = bf16[144,512]{1,0:T(8,128)(2,1)S(1)} collective-permute-done((bf16[144,512]{1,0:T(8,128)(2,1)S(1)}, bf16[144,512]{1,0:T(8,128)(2,1)S(1)}, u32[]{:S(2)}, u32[]{:S(2)}) %collective-permute-start.11) | collective-permute-done | bytes 147488 | tf_op jit(solution)/shard_map/ppermute | solution.py:24
  23.6 0.5 %collective-permute-start.9 = (bf16[144,512]{1,0:T(8,128)(2,1)S(1)}, bf16[144,512]{1,0:T(8,128)(2,1)S(1)}, u32[]{:S(2)}, u32[]{:S(2)}) collective-permute-start(bf16[144,512]{1,0:T(8,128)(2,1)S(1)} %collective-permute-done.4.refs_3_), channel_id=1, source_target_pairs={{0,4},{4,0},{8,12},{12,8},{1,5},{5,1},{9,13},{13,9},{2,6},{6,2},{1... | collective-permute-start | bytes 442376 | tf_op jit(solution)/shard_map/ppermute | solution.py:24
  24.1 0.0 collective-permute-start.14
  24.1 1.2 %collective-permute-done.9.refs_9_.refs_8_ = bf16[144,512]{1,0:T(8,128)(2,1)S(1)} collective-permute-done((bf16[144,512]{1,0:T(8,128)(2,1)S(1)}, bf16[144,512]{1,0:T(8,128)(2,1)S(1)}, u32[]{:S(2)}, u32[]{:S(2)}) %collective-permute-start.9) | collective-permute-done | bytes 147488 | tf_op jit(solution)/shard_map/ppermute | solution.py:24
  25.4 0.2 collective-permute-done.14.refs_13_.refs_12_
  25.6 0.5 %shard_map.67 = bf16[144,512]{1,0:T(8,128)(2,1)S(1)} custom-call(s32[4,16]{1,0:T(4,128)S(1)} %bitcast.4, s32[1,16]{1,0:T(1,128)S(1)} %bitcast.7, bf16[128,1024]{1,0:T(8,128)(2,1)S(1)} %collective-permute-done.12.query_ref, f32[128,512]{1,0:T(8,128)S(1)} %get-tuple-element.33.refs_0_, f32[128,128]{1,0:T(8,128)S(1)} %get-tuple-element.34.refs_1_, ...), custom_call_target="tpu_custom_call" | custom-call | flops 268435456 | bytes 4194304 | tf_op jit(solution)/shard_map/pallas_call | solution.py:288
  26.1 5.4 %collective-permute-start.15 = (bf16[144,512]{1,0:T(8,128)(2,1)S(1)}, bf16[144,512]{1,0:T(8,128)(2,1)S(1)}, u32[]{:S(2)}, u32[]{:S(2)}) collective-permute-start(bf16[144,512]{1,0:T(8,128)(2,1)S(1)} %shard_map.67), channel_id=1, source_target_pairs={{0,3},{1,2},{2,1},{3,0},{4,7},{5,6},{6,5},{7,4},{8,11},{9,10},{10,... | collective-permute-start | bytes 442376 | tf_op jit(solution)/shard_map/ppermute | solution.py:24
  31.4 1.3 %shard_map.66 = (f32[128,512]{1,0:T(8,128)S(1)}, f32[2,128,128]{2,1,0:T(8,128)S(1)}) custom-call(s32[4,16]{1,0:T(4,128)S(1)} %bitcast.5, s32[1,16]{1,0:T(1,128)S(1)} %bitcast.8, bf16[128,1024]{1,0:T(8,128)(2,1)S(1)} %copy-done.1, bf16[128,1024]{1,0:T(8,128)(2,1)S(1)} %collective-permute-done.refs_0_, bf16[144,512]{1,0:T(8,128)(2,1)S(1)} %collective-permute-done.2.refs_1_, ...), custom_call_target="tpu_custom_call" | custom-call | flops 268435456 | bytes 4194304 | tf_op jit(solution)/shard_map/pallas_call | solution.py:303
  32.7 3.0 %collective-permute-done.15.refs_0_ = bf16[144,512]{1,0:T(8,128)(2,1)S(1)} collective-permute-done((bf16[144,512]{1,0:T(8,128)(2,1)S(1)}, bf16[144,512]{1,0:T(8,128)(2,1)S(1)}, u32[]{:S(2)}, u32[]{:S(2)}) %collective-permute-start.15) | collective-permute-done | bytes 147488 | tf_op jit(solution)/shard_map/ppermute | solution.py:24
  35.7 0.8 %shard_map.68 = bf16[128,512]{1,0:T(8,128)(2,1)} custom-call(f32[128,512]{1,0:T(8,128)S(1)} %get-tuple-element.31.total_ref, f32[2,128,128]{2,1,0:T(8,128)S(1)} %get-tuple-element.32.stats_ref, bf16[144,512]{1,0:T(8,128)(2,1)S(1)} %collective-permute-done.15.refs_0_), custom_call_target="tpu_custom_call" | custom-call | tf_op jit(solution)/shard_map/pallas_call | solution.py:317
  (17 shorter events, 0.0 us)
Async XLA Ops:
  0.0 21.3 %copy-start = (bf16[128,1024]{1,0:T(8,128)(2,1)S(1)}, bf16[128,1024]{1,0:T(8,128)(2,1)}, u32[]{:S(2)}) copy-start(bf16[128,1024]{1,0:T(8,128)(2,1)} %refs_14_.1) | copy-start | bytes 786436
  0.0 4.6 %collective-permute-start.1 = (bf16[128,1024]{1,0:T(8,128)(2,1)}, bf16[128,1024]{1,0:T(8,128)(2,1)S(1)}, u32[]{:S(2)}, u32[]{:S(2)}) collective-permute-start(bf16[128,1024]{1,0:T(8,128)(2,1)} %refs_14_.1), channel_id=1, source_target_pairs={{0,4},{4,0},{8,12},{12,8},{1,5},{5,1},{9,13},{13,9},{2,6},{6,2},{1... | collective-permute-start | bytes 786440 | tf_op jit(solution)/shard_map/ppermute | solution.py:24
  0.5 10.6 %collective-permute-start = (bf16[128,1024]{1,0:T(8,128)(2,1)}, bf16[128,1024]{1,0:T(8,128)(2,1)S(1)}, u32[]{:S(2)}, u32[]{:S(2)}) collective-permute-start(bf16[128,1024]{1,0:T(8,128)(2,1)} %refs_14_.1), channel_id=1, source_target_pairs={{0,1},{1,0},{2,3},{3,2},{4,5},{5,4},{6,7},{7,6},{8,9},{9,8},{10,11... | collective-permute-start | bytes 786440 | tf_op jit(solution)/shard_map/ppermute | solution.py:24
  3.1 9.4 %collective-permute-start.3 = (bf16[128,1024]{1,0:T(8,128)(2,1)}, bf16[128,1024]{1,0:T(8,128)(2,1)S(1)}, u32[]{:S(2)}, u32[]{:S(2)}) collective-permute-start(bf16[128,1024]{1,0:T(8,128)(2,1)} %refs_14_.1), channel_id=1, source_target_pairs={{0,8},{4,12},{8,0},{12,4},{1,9},{5,13},{9,1},{13,5},{2,10},{6,14},... | collective-permute-start | bytes 786440 | tf_op jit(solution)/shard_map/ppermute | solution.py:24
  4.6 0.9 %copy-start.2 = (bf16[128,512]{1,0:T(8,128)(2,1)S(1)}, bf16[128,512]{1,0:T(8,128)(2,1)}, u32[]{:S(2)}) copy-start(bf16[128,512]{1,0:T(8,128)(2,1)} %values_ref) | copy-start | bytes 393220
  5.5 0.7 %copy-start.5 = (bf16[128]{0:T(256)(128)(2,1)S(1)}, bf16[128]{0:T(256)(128)(2,1)}, u32[]{:S(2)}) copy-start(bf16[128]{0:T(256)(128)(2,1)} %param.9) | copy-start | bytes 772
  6.3 15.0 %copy-start.3 = (s32[16,4]{0,1:T(4,128)S(1)}, s32[16,4]{0,1:T(4,128)}, u32[]{:S(2)}) copy-start(s32[16,4]{0,1:T(4,128)} %param.10) | copy-start | bytes 772
  6.3 1.9 %collective-permute-start.5 = (bf16[144,512]{1,0:T(8,128)(2,1)S(1)}, bf16[144,512]{1,0:T(8,128)(2,1)S(1)}, u32[]{:S(2)}, u32[]{:S(2)}) collective-permute-start(bf16[144,512]{1,0:T(8,128)(2,1)S(1)} %shard_map.64.refs_5_.refs_15_), channel_id=1, source_target_pairs={{0,4},{4,0},{8,12},{12,8},{1,5},{5,1},{9,13},{13,9},{2,6},{6,2},{1... | collective-permute-start | bytes 442376 | tf_op jit(solution)/shard_map/ppermute | solution.py:24
  6.4 7.5 %collective-permute-start.2 = (bf16[144,512]{1,0:T(8,128)(2,1)S(1)}, bf16[144,512]{1,0:T(8,128)(2,1)S(1)}, u32[]{:S(2)}, u32[]{:S(2)}) collective-permute-start(bf16[144,512]{1,0:T(8,128)(2,1)S(1)} %shard_map.64.refs_5_.refs_15_), channel_id=1, source_target_pairs={{0,1},{1,0},{2,3},{3,2},{4,5},{5,4},{6,7},{7,6},{8,9},{9,8},{10,11... | collective-permute-start | bytes 442376 | tf_op jit(solution)/shard_map/ppermute | solution.py:24
  6.9 8.7 %collective-permute-start.4 = (bf16[144,512]{1,0:T(8,128)(2,1)S(1)}, bf16[144,512]{1,0:T(8,128)(2,1)S(1)}, u32[]{:S(2)}, u32[]{:S(2)}) collective-permute-start(bf16[144,512]{1,0:T(8,128)(2,1)S(1)} %shard_map.64.refs_5_.refs_15_), channel_id=1, source_target_pairs={{0,8},{4,12},{8,0},{12,4},{1,9},{5,13},{9,1},{13,5},{2,10},{6,14},... | collective-permute-start | bytes 442376 | tf_op jit(solution)/shard_map/ppermute | solution.py:24
  8.2 13.1 %collective-permute-start.12 = (bf16[128,1024]{1,0:T(8,128)(2,1)}, bf16[128,1024]{1,0:T(8,128)(2,1)S(1)}, u32[]{:S(2)}, u32[]{:S(2)}) collective-permute-start(bf16[128,1024]{1,0:T(8,128)(2,1)} %query_ref.1), channel_id=1, source_target_pairs={{0,3},{1,2},{2,1},{3,0},{4,7},{5,6},{6,5},{7,4},{8,11},{9,10},{10,... | collective-permute-start | bytes 786440 | tf_op jit(solution)/shard_map/ppermute | solution.py:24
  12.5 9.8 %collective-permute-start.10 = (bf16[128,1024]{1,0:T(8,128)(2,1)S(1)}, bf16[128,1024]{1,0:T(8,128)(2,1)S(1)}, u32[]{:S(2)}, u32[]{:S(2)}) collective-permute-start(bf16[128,1024]{1,0:T(8,128)(2,1)S(1)} %collective-permute-done.refs_0_), channel_id=1, source_target_pairs={{0,8},{4,12},{8,0},{12,4},{1,9},{5,13},{9,1},{13,5},{2,10},{6,14},... | collective-permute-start | bytes 786440 | tf_op jit(solution)/shard_map/ppermute | solution.py:24
  15.6 8.0 %collective-permute-start.11 = (bf16[144,512]{1,0:T(8,128)(2,1)S(1)}, bf16[144,512]{1,0:T(8,128)(2,1)S(1)}, u32[]{:S(2)}, u32[]{:S(2)}) collective-permute-start(bf16[144,512]{1,0:T(8,128)(2,1)S(1)} %collective-permute-done.2.refs_1_), channel_id=1, source_target_pairs={{0,8},{4,12},{8,0},{12,4},{1,9},{5,13},{9,1},{13,5},{2,10},{6,14},... | collective-permute-start | bytes 442376 | tf_op jit(solution)/shard_map/ppermute | solution.py:24
  17.1 7.0 %collective-permute-start.7 = (bf16[144,512]{1,0:T(8,128)(2,1)S(1)}, bf16[144,512]{1,0:T(8,128)(2,1)S(1)}, u32[]{:S(2)}, u32[]{:S(2)}) collective-permute-start(bf16[144,512]{1,0:T(8,128)(2,1)S(1)} %collective-permute-done.2.refs_1_), channel_id=1, source_target_pairs={{0,4},{4,0},{8,12},{12,8},{1,5},{5,1},{9,13},{13,9},{2,6},{6,2},{1... | collective-permute-start | bytes 442376 | tf_op jit(solution)/shard_map/ppermute | solution.py:24
  17.1 8.3 %collective-permute-start.6 = (bf16[128,1024]{1,0:T(8,128)(2,1)S(1)}, bf16[128,1024]{1,0:T(8,128)(2,1)S(1)}, u32[]{:S(2)}, u32[]{:S(2)}) collective-permute-start(bf16[128,1024]{1,0:T(8,128)(2,1)S(1)} %collective-permute-done.refs_0_), channel_id=1, source_target_pairs={{0,4},{4,0},{8,12},{12,8},{1,5},{5,1},{9,13},{13,9},{2,6},{6,2},{1... | collective-permute-start | bytes 786440 | tf_op jit(solution)/shard_map/ppermute | solution.py:24
  21.3 4.1 %collective-permute-start.8 = (bf16[128,1024]{1,0:T(8,128)(2,1)S(1)}, bf16[128,1024]{1,0:T(8,128)(2,1)S(1)}, u32[]{:S(2)}, u32[]{:S(2)}) collective-permute-start(bf16[128,1024]{1,0:T(8,128)(2,1)S(1)} %collective-permute-done.3.refs_2_), channel_id=1, source_target_pairs={{0,4},{4,0},{8,12},{12,8},{1,5},{5,1},{9,13},{13,9},{2,6},{6,2},{1... | collective-permute-start | bytes 786440 | tf_op jit(solution)/shard_map/ppermute | solution.py:24
  21.3 0.7 %copy-start.4 = (s32[16]{0:T(128)S(1)}, s32[16]{0:T(128)}, u32[]{:S(2)}) copy-start(s32[16]{0:T(128)} %param.11) | copy-start | bytes 196
  23.6 2.0 %collective-permute-start.13 = (bf16[128,1024]{1,0:T(8,128)(2,1)S(1)}, bf16[128,1024]{1,0:T(8,128)(2,1)S(1)}, u32[]{:S(2)}, u32[]{:S(2)}) collective-permute-start(bf16[128,1024]{1,0:T(8,128)(2,1)S(1)} %collective-permute-done.10.refs_10_.refs_9_), channel_id=1, source_target_pairs={{0,4},{4,0},{8,12},{12,8},{1,5},{5,1},{9,13},{13,9},{2,6},{6,2},{1... | collective-permute-start | bytes 786440 | tf_op jit(solution)/shard_map/ppermute | solution.py:24
  23.6 1.7 %collective-permute-start.9 = (bf16[144,512]{1,0:T(8,128)(2,1)S(1)}, bf16[144,512]{1,0:T(8,128)(2,1)S(1)}, u32[]{:S(2)}, u32[]{:S(2)}) collective-permute-start(bf16[144,512]{1,0:T(8,128)(2,1)S(1)} %collective-permute-done.4.refs_3_), channel_id=1, source_target_pairs={{0,4},{4,0},{8,12},{12,8},{1,5},{5,1},{9,13},{13,9},{2,6},{6,2},{1... | collective-permute-start | bytes 442376 | tf_op jit(solution)/shard_map/ppermute | solution.py:24
  24.1 1.4 %collective-permute-start.14 = (bf16[144,512]{1,0:T(8,128)(2,1)S(1)}, bf16[144,512]{1,0:T(8,128)(2,1)S(1)}, u32[]{:S(2)}, u32[]{:S(2)}) collective-permute-start(bf16[144,512]{1,0:T(8,128)(2,1)S(1)} %collective-permute-done.11.refs_11_.refs_10_), channel_id=1, source_target_pairs={{0,4},{4,0},{8,12},{12,8},{1,5},{5,1},{9,13},{13,9},{2,6},{6,2},{1... | collective-permute-start | bytes 442376 | tf_op jit(solution)/shard_map/ppermute | solution.py:24
  25.6 5.8 %copy-start.1 = (bf16[128,1024]{1,0:T(8,128)(2,1)S(1)}, bf16[128,1024]{1,0:T(8,128)(2,1)}, u32[]{:S(2)}) copy-start(bf16[128,1024]{1,0:T(8,128)(2,1)} %query_ref.1) | copy-start | bytes 786436
  26.1 9.6 %collective-permute-start.15 = (bf16[144,512]{1,0:T(8,128)(2,1)S(1)}, bf16[144,512]{1,0:T(8,128)(2,1)S(1)}, u32[]{:S(2)}, u32[]{:S(2)}) collective-permute-start(bf16[144,512]{1,0:T(8,128)(2,1)S(1)} %shard_map.67), channel_id=1, source_target_pairs={{0,3},{1,2},{2,1},{3,0},{4,7},{5,6},{6,5},{7,4},{8,11},{9,10},{10,... | collective-permute-start | bytes 442376 | tf_op jit(solution)/shard_map/ppermute | solution.py:24

commit v15 on v14

--- a/solution.py
+++ b/solution.py
@@ -52,32 +52,47 @@
 
 
 class Piece:
-    def __init__(self, place, keys_ref, values_ref, copy=None):
+    def __init__(self, place, keys_ref, values_ref, row=0, copy=None):
         self.place = place
-        self.refs = (keys_ref, values_ref)
+        self.keys_ref = keys_ref
+        self.values_ref = values_ref
+        self.row = row
         self.copy = copy
 
     def scores(self, query_ref, inverse_root):
-        keys_ref, values_ref = self.refs
         product = lax.dot_general(
-            query_ref[...], keys_ref[...], (((1,), (1,)), ((), ())), preferred_element_type=jnp.float32
+            query_ref[...], self.keys_ref[...], (((1,), (1,)), ((), ())), preferred_element_type=jnp.float32
         )
-        scale = values_ref[TILE : TILE + EXTRA, 0:TILE]
+        scale = self.values_ref[self.row + TILE : self.row + TILE + EXTRA, 0:TILE]
         return product * (scale.astype(jnp.float32)[0:1] * inverse_root)
 
     def values(self):
-        return self.refs[1][0:TILE, :]
-
-
-def read_pieces(places, refs, own=None):
+        return self.values_ref[self.row : self.row + TILE, :]
+
+
+def read_pieces(places, refs, bundled=(), own=None):
     pieces = [Piece(place, refs[2 * at], refs[2 * at + 1]) for at, place in enumerate(places)]
     refs = refs[2 * len(places) :]
+    if bundled:
+        values_ref = refs[len(bundled)]
+        pieces += [
+            Piece(place, refs[at], values_ref, at * (TILE + EXTRA)) for at, place in enumerate(bundled)
+        ]
+        refs = refs[len(bundled) + 1 :]
     if own is not None:
         keys_ref, values_ref, *refs, held_ref, sem = refs
         copy = pltpu.make_async_copy(keys_ref, held_ref, sem)
         copy.start()
-        pieces.append(Piece((0, 0), held_ref, values_ref, copy))
+        pieces.append(Piece((0, 0), held_ref, values_ref, copy=copy))
     return pieces, refs
+
+
+def bundle_kernel(*refs):
+    *refs, bundle_ref = refs
+    row = 0
+    for ref in refs:
+        bundle_ref[row : row + ref.shape[0], :] = ref[...]
+        row += ref.shape[0]
 
 
 def pick(ref, row, column):
@@ -151,9 +166,9 @@
     max_ref[...] = jnp.broadcast_to(row_max, max_ref.shape)
 
 
-def late_kernel(places, panel_mask, lists_ref, counts_ref, query_ref, *refs):
+def late_kernel(places, bundled, panel_mask, lists_ref, counts_ref, query_ref, *refs):
     before, refs = refs[:3], refs[3:]
-    pieces, refs = read_pieces(places, refs)
+    pieces, refs = read_pieces(places, refs, bundled)
     packed_ref, score_ref, total_ref, mass_ref = refs
     row_max = attend(pieces, panel_mask, lists_ref, counts_ref, query_ref, score_ref, total_ref, mass_ref, before)
     row_sum = jnp.sum(mass_ref[...], axis=1, keepdims=True)
@@ -170,8 +185,8 @@
     packed_ref[TILE:, LANES:] = jnp.zeros((EXTRA, value_width - LANES), jnp.bfloat16)
 
 
-def home_kernel(places, lists_ref, counts_ref, query_ref, *refs):
-    pieces, refs = read_pieces(places, refs, own=True)
+def home_kernel(places, bundled, lists_ref, counts_ref, query_ref, *refs):
+    pieces, refs = read_pieces(places, refs, bundled, own=True)
     total_ref, stats_ref, score_ref, mass_ref = refs
     row_max = attend(pieces, 0, lists_ref, counts_ref, query_ref, score_ref, total_ref, mass_ref)
     row_sum = jnp.sum(mass_ref[...], axis=1, keepdims=True)
@@ -281,17 +296,28 @@
         )(window_lists, window_counts, visiting, *early_arrays, library_keys, values)
         states.append(state)
 
-    late = [((1, 0), partner_keys, partner_values)] + cross_cores(early) + relayed + cross_cores(relayed, [state[2] for state in states])
-    late_arrays = arrays_of(late)
+    bundled = [(lib_mask | 1, qry_mask) for lib_mask, qry_mask in places_of(early)]
+    early_values = [piece[2] for piece in early]
+    bundle = pl.pallas_call(
+        bundle_kernel,
+        out_shape=jax.ShapeDtypeStruct((len(early) * (TILE + EXTRA), value_width), jnp.bfloat16),
+        in_specs=[VMEM] * len(early),
+        out_specs=VMEM,
+        compiler_params=params(),
+    )(*early_values)
+    bundled_arrays = [swap(piece[1], "lib", 1) for piece in early] + [swap(bundle, "lib", 1)]
+    late = [((1, 0), partner_keys, partner_values)] + relayed
+    late += cross_cores(relayed, [state[2] for state in states])
+    late_arrays = arrays_of(late) + bundled_arrays
     returned = []
     for (mask, visiting), state in zip(visitors, states):
         packed = pl.pallas_call(
-            functools.partial(late_kernel, places_of(late), mask),
+            functools.partial(late_kernel, places_of(late), bundled, mask),
             out_shape=jax.ShapeDtypeStruct((TILE + EXTRA, value_width), jnp.bfloat16),
             in_specs=[VMEM, VMEM] + [VMEM] * (4 + len(late_arrays)),
             out_specs=VMEM,
             scratch_shapes=[
-                pltpu.VMEM((len(late), TILE, TILE), jnp.float32),
+                pltpu.VMEM((len(late) + len(bundled), TILE, TILE), jnp.float32),
                 pltpu.VMEM((TILE, value_width), jnp.float32),
                 pltpu.VMEM((TILE, TILE), jnp.float32),
             ],
@@ -301,7 +327,7 @@
         returned.append(swap(packed, "qry", mask))
 
     total, stats = pl.pallas_call(
-        functools.partial(home_kernel, places_of(early + late)),
+        functools.partial(home_kernel, places_of(early + late), bundled),
         out_shape=(total_shape, jax.ShapeDtypeStruct((2, TILE, LANES), jnp.float32)),
         in_specs=[VMEM, VMEM] + [VMEM] * (1 + len(early_arrays) + len(late_arrays)) + own_specs,
         out_specs=(VMEM, VMEM),

time: 36.2 us -> 35.5 us (0.981)
  starting transfers between devices: 18.7 us -> 17.2 us
    ppermute x16 -> x15, starting transfers between devices: 18.7 us -> 17.2 us  [swap(): return lax.ppermute(value, axis, [(i, i ^ mask) for i in range(length)])]
    ppermute x16 -> x15, waiting for transfers between devices: 12.5 us -> 12.8 us  [swap(): return lax.ppermute(value, axis, [(i, i ^ mask) for i in range(length)])]
    pallas_call x2 -> x3, Pallas kernels: 1.77 us -> 1.85 us  [the longest x1 0.97 us: body(): pl.pallas_call(functools.partial(late_kernel, places_of(late), bundled, m...]
  transfers between devices with their start and end apart: 16 -> 15, of which waited for: 7 -> 6; matrix products, arithmetic and copies ran while one was open for 0% -> 0% of each run, Pallas kernels for 5% -> 4%
where the time goes in v15:
time: 35.5 us
  starting transfers between devices  17.2 us (48%)
  waiting for transfers between devices  12.8 us (36%)
  Pallas kernels  3.1 us (9%)
  local copies, waits for them, and re-layouts  2.22 us (6%)
    ppermute x15, starting transfers between devices, swap(): return lax.ppermute(value, axis, [(i, i ^ mask) for i in range(length)])  17.2 us
    ppermute x15, waiting for transfers between devices, swap(): return lax.ppermute(value, axis, [(i, i ^ mask) for i in range(length)])  12.8 us
    unnamed x12, local copies, waits for them, and re-layouts  2.22 us
    pallas_call x1, Pallas kernels, body(): pl.pallas_call(functools.partial(late_kernel, places_of(late), bundled, m...  0.97 us
    pallas_call x1, Pallas kernels, body(): pl.pallas_call(functools.partial(home_kernel, places_of(early + late), bu...  0.86 us
    pallas_call x1, Pallas kernels, body(): pl.pallas_call(merge_kernel, out_shape=jax.ShapeDtypeStruct((TILE, value_...  0.81 us
  transfers between devices with their start and end apart: 15, of which 6 were waited for; matrix products, arithmetic and copies ran while one was open for 0% of the time, Pallas kernels for 4%

profile of v15, /device:TPU:0, one launch (start us, length us, event | category | flops | bytes accessed | tf_op | source)
XLA Modules:
  0.0 35.5 jit_solution(16961721473631356460)
XLA Ops:
  0.0 0.5 %collective-permute-start.1 = (bf16[128,1024]{1,0:T(8,128)(2,1)}, bf16[128,1024]{1,0:T(8,128)(2,1)S(1)}, u32[]{:S(2)}, u32[]{:S(2)}) collective-permute-start(bf16[128,1024]{1,0:T(8,128)(2,1)} %refs_13_.1), channel_id=1, source_target_pairs={{0,4},{4,0},{8,12},{12,8},{1,5},{5,1},{9,13},{13,9},{2,6},{6,2},{1... | collective-permute-start | bytes 786440 | tf_op jit(solution)/shard_map/ppermute | solution.py:24
  0.5 2.6 %collective-permute-start = (bf16[128,1024]{1,0:T(8,128)(2,1)}, bf16[128,1024]{1,0:T(8,128)(2,1)S(1)}, u32[]{:S(2)}, u32[]{:S(2)}) collective-permute-start(bf16[128,1024]{1,0:T(8,128)(2,1)} %refs_13_.1), channel_id=1, source_target_pairs={{0,1},{1,0},{2,3},{3,2},{4,5},{5,4},{6,7},{7,6},{8,9},{9,8},{10,11... | collective-permute-start | bytes 786440 | tf_op jit(solution)/shard_map/ppermute | solution.py:24
  3.1 1.5 %collective-permute-start.3 = (bf16[128,1024]{1,0:T(8,128)(2,1)}, bf16[128,1024]{1,0:T(8,128)(2,1)S(1)}, u32[]{:S(2)}, u32[]{:S(2)}) collective-permute-start(bf16[128,1024]{1,0:T(8,128)(2,1)} %refs_13_.1), channel_id=1, source_target_pairs={{0,8},{4,12},{8,0},{12,4},{1,9},{5,13},{9,1},{13,5},{2,10},{6,14},... | collective-permute-start | bytes 786440 | tf_op jit(solution)/shard_map/ppermute | solution.py:24
  4.6 0.0 collective-permute-done.1.refs_4_.refs_3_
  4.6 0.9 %copy-done.2 = bf16[128,512]{1,0:T(8,128)(2,1)S(1)} copy-done((bf16[128,512]{1,0:T(8,128)(2,1)S(1)}, bf16[128,512]{1,0:T(8,128)(2,1)}, u32[]{:S(2)}) %copy-start.2) | copy-done | bytes 131096
  5.5 0.7 %copy-done.5 = bf16[128]{0:T(256)(128)(2,1)S(1)} copy-done((bf16[128]{0:T(256)(128)(2,1)S(1)}, bf16[128]{0:T(256)(128)(2,1)}, u32[]{:S(2)}) %copy-start.5) | copy-done | bytes 280
  6.1 0.2 shard_map.64.refs_5_.refs_14_
  6.3 0.0 copy-start
  6.3 0.1 collective-permute-start.5
  6.4 0.5 %collective-permute-start.2 = (bf16[144,512]{1,0:T(8,128)(2,1)S(1)}, bf16[144,512]{1,0:T(8,128)(2,1)S(1)}, u32[]{:S(2)}, u32[]{:S(2)}) collective-permute-start(bf16[144,512]{1,0:T(8,128)(2,1)S(1)} %shard_map.64.refs_5_.refs_14_), channel_id=1, source_target_pairs={{0,1},{1,0},{2,3},{3,2},{4,5},{5,4},{6,7},{7,6},{8,9},{9,8},{10,11... | collective-permute-start | bytes 442376 | tf_op jit(solution)/shard_map/ppermute | solution.py:24
  6.9 1.3 %collective-permute-start.4 = (bf16[144,512]{1,0:T(8,128)(2,1)S(1)}, bf16[144,512]{1,0:T(8,128)(2,1)S(1)}, u32[]{:S(2)}, u32[]{:S(2)}) collective-permute-start(bf16[144,512]{1,0:T(8,128)(2,1)S(1)} %shard_map.64.refs_5_.refs_14_), channel_id=1, source_target_pairs={{0,8},{4,12},{8,0},{12,4},{1,9},{5,13},{9,1},{13,5},{2,10},{6,14},... | collective-permute-start | bytes 442376 | tf_op jit(solution)/shard_map/ppermute | solution.py:24
  8.2 0.0 collective-permute-done.5.refs_5_.refs_4_
  8.2 2.8 %collective-permute-start.8 = (bf16[128,1024]{1,0:T(8,128)(2,1)S(1)}, bf16[128,1024]{1,0:T(8,128)(2,1)S(1)}, u32[]{:S(2)}, u32[]{:S(2)}) collective-permute-start(bf16[128,1024]{1,0:T(8,128)(2,1)S(1)} %copy-done.1), channel_id=1, source_target_pairs={{0,3},{1,2},{2,1},{3,0},{4,7},{5,6},{6,5},{7,4},{8,11},{9,10},{10,... | collective-permute-start | bytes 786440 | tf_op jit(solution)/shard_map/ppermute | solution.py:24
  11.1 1.4 %collective-permute-done.3.refs_2_ = bf16[128,1024]{1,0:T(8,128)(2,1)S(1)} collective-permute-done((bf16[128,1024]{1,0:T(8,128)(2,1)}, bf16[128,1024]{1,0:T(8,128)(2,1)S(1)}, u32[]{:S(2)}, u32[]{:S(2)}) %collective-permute-start.3) | collective-permute-done | bytes 262176 | tf_op jit(solution)/shard_map/ppermute | solution.py:24
  12.5 1.5 %collective-permute-start.6 = (bf16[128,1024]{1,0:T(8,128)(2,1)S(1)}, bf16[128,1024]{1,0:T(8,128)(2,1)S(1)}, u32[]{:S(2)}, u32[]{:S(2)}) collective-permute-start(bf16[128,1024]{1,0:T(8,128)(2,1)S(1)} %collective-permute-done.refs_0_), channel_id=1, source_target_pairs={{0,8},{4,12},{8,0},{12,4},{1,9},{5,13},{9,1},{13,5},{2,10},{6,14},... | collective-permute-start | bytes 786440 | tf_op jit(solution)/shard_map/ppermute | solution.py:24
  13.9 1.7 %collective-permute-done.4.refs_3_.refs_1_ = bf16[144,512]{1,0:T(8,128)(2,1)S(1)} collective-permute-done((bf16[144,512]{1,0:T(8,128)(2,1)S(1)}, bf16[144,512]{1,0:T(8,128)(2,1)S(1)}, u32[]{:S(2)}, u32[]{:S(2)}) %collective-permute-start.4) | collective-permute-done | bytes 147488 | tf_op jit(solution)/shard_map/ppermute | solution.py:24
  15.6 1.5 %collective-permute-start.7 = (bf16[144,512]{1,0:T(8,128)(2,1)S(1)}, bf16[144,512]{1,0:T(8,128)(2,1)S(1)}, u32[]{:S(2)}, u32[]{:S(2)}) collective-permute-start(bf16[144,512]{1,0:T(8,128)(2,1)S(1)} %collective-permute-done.2.refs_1_.refs_0_), channel_id=1, source_target_pairs={{0,8},{4,12},{8,0},{12,4},{1,9},{5,13},{9,1},{13,5},{2,10},{6,14},... | collective-permute-start | bytes 442376 | tf_op jit(solution)/shard_map/ppermute | solution.py:24
  17.1 0.0 copy-start.3
  17.1 0.1 collective-permute-start.13
  17.2 0.5 %collective-permute-start.11 = (bf16[128,1024]{1,0:T(8,128)(2,1)S(1)}, bf16[128,1024]{1,0:T(8,128)(2,1)S(1)}, u32[]{:S(2)}, u32[]{:S(2)}) collective-permute-start(bf16[128,1024]{1,0:T(8,128)(2,1)S(1)} %collective-permute-done.refs_0_), channel_id=1, source_target_pairs={{0,4},{4,0},{8,12},{12,8},{1,5},{5,1},{9,13},{13,9},{2,6},{6,2},{1... | collective-permute-start | bytes 786440 | tf_op jit(solution)/shard_map/ppermute | solution.py:24
  17.7 3.6 %collective-permute-done.8.query_ref = bf16[128,1024]{1,0:T(8,128)(2,1)S(1)} collective-permute-done((bf16[128,1024]{1,0:T(8,128)(2,1)S(1)}, bf16[128,1024]{1,0:T(8,128)(2,1)S(1)}, u32[]{:S(2)}, u32[]{:S(2)}) %collective-permute-start.8) | collective-permute-done | bytes 262176 | tf_op jit(solution)/shard_map/ppermute | solution.py:24
  21.3 0.0 collective-permute-start.12
  21.3 0.6 %copy-done.4 = s32[16]{0:T(128)S(1)} copy-done((s32[16]{0:T(128)S(1)}, s32[16]{0:T(128)}, u32[]{:S(2)}) %copy-start.4) | copy-done | bytes 88
  21.9 0.3 shard_map.65
  22.2 1.4 %collective-permute-done.7.refs_7_.refs_6_ = bf16[144,512]{1,0:T(8,128)(2,1)S(1)} collective-permute-done((bf16[144,512]{1,0:T(8,128)(2,1)S(1)}, bf16[144,512]{1,0:T(8,128)(2,1)S(1)}, u32[]{:S(2)}, u32[]{:S(2)}) %collective-permute-start.7) | collective-permute-done | bytes 147488 | tf_op jit(solution)/shard_map/ppermute | solution.py:24
  23.6 0.5 %collective-permute-start.10 = (bf16[144,512]{1,0:T(8,128)(2,1)S(1)}, bf16[144,512]{1,0:T(8,128)(2,1)S(1)}, u32[]{:S(2)}, u32[]{:S(2)}) collective-permute-start(bf16[144,512]{1,0:T(8,128)(2,1)S(1)} %collective-permute-done.7.refs_7_.refs_6_), channel_id=1, source_target_pairs={{0,4},{4,0},{8,12},{12,8},{1,5},{5,1},{9,13},{13,9},{2,6},{6,2},{1... | collective-permute-start | bytes 442376 | tf_op jit(solution)/shard_map/ppermute | solution.py:24
  24.1 1.2 %collective-permute-done.10.refs_9_.refs_8_ = bf16[144,512]{1,0:T(8,128)(2,1)S(1)} collective-permute-done((bf16[144,512]{1,0:T(8,128)(2,1)S(1)}, bf16[144,512]{1,0:T(8,128)(2,1)S(1)}, u32[]{:S(2)}, u32[]{:S(2)}) %collective-permute-start.10) | collective-permute-done | bytes 147488 | tf_op jit(solution)/shard_map/ppermute | solution.py:24
  25.4 1.0 %shard_map.68 = bf16[144,512]{1,0:T(8,128)(2,1)S(1)} custom-call(s32[4,16]{1,0:T(4,128)S(1)} %bitcast.4, s32[1,16]{1,0:T(1,128)S(1)} %bitcast.7, bf16[128,1024]{1,0:T(8,128)(2,1)S(1)} %collective-permute-done.8.query_ref, f32[128,512]{1,0:T(8,128)S(1)} %get-tuple-element.25.refs_0_, f32[128,128]{1,0:T(8,128)S(1)} %get-tuple-element.26.refs_1_, ...), custom_call_target="tpu_custom_call" | custom-call | flops 268435456 | bytes 4194304 | tf_op jit(solution)/shard_map/pallas_call | solution.py:314
  26.3 3.9 %collective-permute-start.14 = (bf16[144,512]{1,0:T(8,128)(2,1)S(1)}, bf16[144,512]{1,0:T(8,128)(2,1)S(1)}, u32[]{:S(2)}, u32[]{:S(2)}) collective-permute-start(bf16[144,512]{1,0:T(8,128)(2,1)S(1)} %shard_map.68), channel_id=1, source_target_pairs={{0,3},{1,2},{2,1},{3,0},{4,7},{5,6},{6,5},{7,4},{8,11},{9,10},{10,... | collective-permute-start | bytes 442376 | tf_op jit(solution)/shard_map/ppermute | solution.py:24
  30.2 0.9 %shard_map.67 = (f32[128,512]{1,0:T(8,128)S(1)}, f32[2,128,128]{2,1,0:T(8,128)S(1)}) custom-call(s32[4,16]{1,0:T(4,128)S(1)} %bitcast.5, s32[1,16]{1,0:T(1,128)S(1)} %bitcast.8, bf16[128,1024]{1,0:T(8,128)(2,1)S(1)} %copy-done.1, bf16[128,1024]{1,0:T(8,128)(2,1)S(1)} %collective-permute-done.refs_0_, ...), custom_call_target="tpu_custom_call" | custom-call | flops 268435456 | bytes 4194304 | tf_op jit(solution)/shard_map/pallas_call | solution.py:329
  31.1 3.6 %collective-permute-done.14.refs_0_ = bf16[144,512]{1,0:T(8,128)(2,1)S(1)} collective-permute-done((bf16[144,512]{1,0:T(8,128)(2,1)S(1)}, bf16[144,512]{1,0:T(8,128)(2,1)S(1)}, u32[]{:S(2)}, u32[]{:S(2)}) %collective-permute-start.14) | collective-permute-done | bytes 147488 | tf_op jit(solution)/shard_map/ppermute | solution.py:24
  34.7 0.8 %shard_map.69 = bf16[128,512]{1,0:T(8,128)(2,1)} custom-call(f32[128,512]{1,0:T(8,128)S(1)} %get-tuple-element.23.total_ref, f32[2,128,128]{2,1,0:T(8,128)S(1)} %get-tuple-element.24.stats_ref, bf16[144,512]{1,0:T(8,128)(2,1)S(1)} %collective-permute-done.14.refs_0_), custom_call_target="tpu_custom_call" | custom-call | tf_op jit(solution)/shard_map/pallas_call | solution.py:343
  (16 shorter events, 0.1 us)
Async XLA Ops:
  0.0 8.2 %copy-start.1 = (bf16[128,1024]{1,0:T(8,128)(2,1)S(1)}, bf16[128,1024]{1,0:T(8,128)(2,1)}, u32[]{:S(2)}) copy-start(bf16[128,1024]{1,0:T(8,128)(2,1)} %query_ref.1) | copy-start | bytes 786436
  0.0 4.6 %collective-permute-start.1 = (bf16[128,1024]{1,0:T(8,128)(2,1)}, bf16[128,1024]{1,0:T(8,128)(2,1)S(1)}, u32[]{:S(2)}, u32[]{:S(2)}) collective-permute-start(bf16[128,1024]{1,0:T(8,128)(2,1)} %refs_13_.1), channel_id=1, source_target_pairs={{0,4},{4,0},{8,12},{12,8},{1,5},{5,1},{9,13},{13,9},{2,6},{6,2},{1... | collective-permute-start | bytes 786440 | tf_op jit(solution)/shard_map/ppermute | solution.py:24
  0.5 10.6 %collective-permute-start = (bf16[128,1024]{1,0:T(8,128)(2,1)}, bf16[128,1024]{1,0:T(8,128)(2,1)S(1)}, u32[]{:S(2)}, u32[]{:S(2)}) collective-permute-start(bf16[128,1024]{1,0:T(8,128)(2,1)} %refs_13_.1), channel_id=1, source_target_pairs={{0,1},{1,0},{2,3},{3,2},{4,5},{5,4},{6,7},{7,6},{8,9},{9,8},{10,11... | collective-permute-start | bytes 786440 | tf_op jit(solution)/shard_map/ppermute | solution.py:24
  3.1 9.4 %collective-permute-start.3 = (bf16[128,1024]{1,0:T(8,128)(2,1)}, bf16[128,1024]{1,0:T(8,128)(2,1)S(1)}, u32[]{:S(2)}, u32[]{:S(2)}) collective-permute-start(bf16[128,1024]{1,0:T(8,128)(2,1)} %refs_13_.1), channel_id=1, source_target_pairs={{0,8},{4,12},{8,0},{12,4},{1,9},{5,13},{9,1},{13,5},{2,10},{6,14},... | collective-permute-start | bytes 786440 | tf_op jit(solution)/shard_map/ppermute | solution.py:24
  4.6 0.9 %copy-start.2 = (bf16[128,512]{1,0:T(8,128)(2,1)S(1)}, bf16[128,512]{1,0:T(8,128)(2,1)}, u32[]{:S(2)}) copy-start(bf16[128,512]{1,0:T(8,128)(2,1)} %values_ref) | copy-start | bytes 393220
  5.5 0.7 %copy-start.5 = (bf16[128]{0:T(256)(128)(2,1)S(1)}, bf16[128]{0:T(256)(128)(2,1)}, u32[]{:S(2)}) copy-start(bf16[128]{0:T(256)(128)(2,1)} %param.9) | copy-start | bytes 772
  6.3 15.0 %copy-start = (bf16[128,1024]{1,0:T(8,128)(2,1)S(1)}, bf16[128,1024]{1,0:T(8,128)(2,1)}, u32[]{:S(2)}) copy-start(bf16[128,1024]{1,0:T(8,128)(2,1)} %refs_13_.1) | copy-start | bytes 786436
  6.3 1.9 %collective-permute-start.5 = (bf16[144,512]{1,0:T(8,128)(2,1)S(1)}, bf16[144,512]{1,0:T(8,128)(2,1)S(1)}, u32[]{:S(2)}, u32[]{:S(2)}) collective-permute-start(bf16[144,512]{1,0:T(8,128)(2,1)S(1)} %shard_map.64.refs_5_.refs_14_), channel_id=1, source_target_pairs={{0,4},{4,0},{8,12},{12,8},{1,5},{5,1},{9,13},{13,9},{2,6},{6,2},{1... | collective-permute-start | bytes 442376 | tf_op jit(solution)/shard_map/ppermute | solution.py:24
  6.4 7.5 %collective-permute-start.2 = (bf16[144,512]{1,0:T(8,128)(2,1)S(1)}, bf16[144,512]{1,0:T(8,128)(2,1)S(1)}, u32[]{:S(2)}, u32[]{:S(2)}) collective-permute-start(bf16[144,512]{1,0:T(8,128)(2,1)S(1)} %shard_map.64.refs_5_.refs_14_), channel_id=1, source_target_pairs={{0,1},{1,0},{2,3},{3,2},{4,5},{5,4},{6,7},{7,6},{8,9},{9,8},{10,11... | collective-permute-start | bytes 442376 | tf_op jit(solution)/shard_map/ppermute | solution.py:24
  6.9 8.7 %collective-permute-start.4 = (bf16[144,512]{1,0:T(8,128)(2,1)S(1)}, bf16[144,512]{1,0:T(8,128)(2,1)S(1)}, u32[]{:S(2)}, u32[]{:S(2)}) collective-permute-start(bf16[144,512]{1,0:T(8,128)(2,1)S(1)} %shard_map.64.refs_5_.refs_14_), channel_id=1, source_target_pairs={{0,8},{4,12},{8,0},{12,4},{1,9},{5,13},{9,1},{13,5},{2,10},{6,14},... | collective-permute-start | bytes 442376 | tf_op jit(solution)/shard_map/ppermute | solution.py:24
  8.2 13.1 %collective-permute-start.8 = (bf16[128,1024]{1,0:T(8,128)(2,1)S(1)}, bf16[128,1024]{1,0:T(8,128)(2,1)S(1)}, u32[]{:S(2)}, u32[]{:S(2)}) collective-permute-start(bf16[128,1024]{1,0:T(8,128)(2,1)S(1)} %copy-done.1), channel_id=1, source_target_pairs={{0,3},{1,2},{2,1},{3,0},{4,7},{5,6},{6,5},{7,4},{8,11},{9,10},{10,... | collective-permute-start | bytes 786440 | tf_op jit(solution)/shard_map/ppermute | solution.py:24
  12.5 9.8 %collective-permute-start.6 = (bf16[128,1024]{1,0:T(8,128)(2,1)S(1)}, bf16[128,1024]{1,0:T(8,128)(2,1)S(1)}, u32[]{:S(2)}, u32[]{:S(2)}) collective-permute-start(bf16[128,1024]{1,0:T(8,128)(2,1)S(1)} %collective-permute-done.refs_0_), channel_id=1, source_target_pairs={{0,8},{4,12},{8,0},{12,4},{1,9},{5,13},{9,1},{13,5},{2,10},{6,14},... | collective-permute-start | bytes 786440 | tf_op jit(solution)/shard_map/ppermute | solution.py:24
  15.6 8.0 %collective-permute-start.7 = (bf16[144,512]{1,0:T(8,128)(2,1)S(1)}, bf16[144,512]{1,0:T(8,128)(2,1)S(1)}, u32[]{:S(2)}, u32[]{:S(2)}) collective-permute-start(bf16[144,512]{1,0:T(8,128)(2,1)S(1)} %collective-permute-done.2.refs_1_.refs_0_), channel_id=1, source_target_pairs={{0,8},{4,12},{8,0},{12,4},{1,9},{5,13},{9,1},{13,5},{2,10},{6,14},... | collective-permute-start | bytes 442376 | tf_op jit(solution)/shard_map/ppermute | solution.py:24
  17.1 4.2 %copy-start.3 = (s32[16,4]{0,1:T(4,128)S(1)}, s32[16,4]{0,1:T(4,128)}, u32[]{:S(2)}) copy-start(s32[16,4]{0,1:T(4,128)} %param.10) | copy-start | bytes 772
  17.1 7.0 %collective-permute-start.13 = (bf16[288,512]{1,0:T(8,128)(2,1)S(1)}, bf16[288,512]{1,0:T(8,128)(2,1)S(1)}, u32[]{:S(2)}, u32[]{:S(2)}) collective-permute-start(bf16[288,512]{1,0:T(8,128)(2,1)S(1)} %shard_map.66), channel_id=1, source_target_pairs={{0,4},{4,0},{8,12},{12,8},{1,5},{5,1},{9,13},{13,9},{2,6},{6,2},{1... | collective-permute-start | bytes 884744 | tf_op jit(solution)/shard_map/ppermute | solution.py:24
  17.2 6.9 %collective-permute-start.11 = (bf16[128,1024]{1,0:T(8,128)(2,1)S(1)}, bf16[128,1024]{1,0:T(8,128)(2,1)S(1)}, u32[]{:S(2)}, u32[]{:S(2)}) collective-permute-start(bf16[128,1024]{1,0:T(8,128)(2,1)S(1)} %collective-permute-done.refs_0_), channel_id=1, source_target_pairs={{0,4},{4,0},{8,12},{12,8},{1,5},{5,1},{9,13},{13,9},{2,6},{6,2},{1... | collective-permute-start | bytes 786440 | tf_op jit(solution)/shard_map/ppermute | solution.py:24
  21.3 2.8 %collective-permute-start.12 = (bf16[128,1024]{1,0:T(8,128)(2,1)S(1)}, bf16[128,1024]{1,0:T(8,128)(2,1)S(1)}, u32[]{:S(2)}, u32[]{:S(2)}) collective-permute-start(bf16[128,1024]{1,0:T(8,128)(2,1)S(1)} %collective-permute-done.3.refs_2_), channel_id=1, source_target_pairs={{0,4},{4,0},{8,12},{12,8},{1,5},{5,1},{9,13},{13,9},{2,6},{6,2},{1... | collective-permute-start | bytes 786440 | tf_op jit(solution)/shard_map/ppermute | solution.py:24
  21.3 0.7 %copy-start.4 = (s32[16]{0:T(128)S(1)}, s32[16]{0:T(128)}, u32[]{:S(2)}) copy-start(s32[16]{0:T(128)} %param.11) | copy-start | bytes 196
  23.6 1.8 %collective-permute-start.9 = (bf16[128,1024]{1,0:T(8,128)(2,1)S(1)}, bf16[128,1024]{1,0:T(8,128)(2,1)S(1)}, u32[]{:S(2)}, u32[]{:S(2)}) collective-permute-start(bf16[128,1024]{1,0:T(8,128)(2,1)S(1)} %collective-permute-done.6.refs_6_.refs_5_), channel_id=1, source_target_pairs={{0,4},{4,0},{8,12},{12,8},{1,5},{5,1},{9,13},{13,9},{2,6},{6,2},{1... | collective-permute-start | bytes 786440 | tf_op jit(solution)/shard_map/ppermute | solution.py:24
  23.6 1.7 %collective-permute-start.10 = (bf16[144,512]{1,0:T(8,128)(2,1)S(1)}, bf16[144,512]{1,0:T(8,128)(2,1)S(1)}, u32[]{:S(2)}, u32[]{:S(2)}) collective-permute-start(bf16[144,512]{1,0:T(8,128)(2,1)S(1)} %collective-permute-done.7.refs_7_.refs_6_), channel_id=1, source_target_pairs={{0,4},{4,0},{8,12},{12,8},{1,5},{5,1},{9,13},{13,9},{2,6},{6,2},{1... | collective-permute-start | bytes 442376 | tf_op jit(solution)/shard_map/ppermute | solution.py:24
  26.3 8.3 %collective-permute-start.14 = (bf16[144,512]{1,0:T(8,128)(2,1)S(1)}, bf16[144,512]{1,0:T(8,128)(2,1)S(1)}, u32[]{:S(2)}, u32[]{:S(2)}) collective-permute-start(bf16[144,512]{1,0:T(8,128)(2,1)S(1)} %shard_map.68), channel_id=1, source_target_pairs={{0,3},{1,2},{2,1},{3,0},{4,7},{5,6},{6,5},{7,4},{8,11},{9,10},{10,... | collective-permute-start | bytes 442376 | tf_op jit(solution)/shard_map/ppermute | solution.py:24

commit v16 on v15

--- a/solution.py
+++ b/solution.py
@@ -11,6 +11,7 @@
 TILE = 128
 LANES = 128
 EXTRA = 16
+SUBLANES = 8
 MASKED_SCORE = -1e30
 VMEM = pl.BlockSpec(memory_space=pltpu.VMEM)
 
@@ -26,14 +27,6 @@
 
 def tie(*values):
     return lax.optimization_barrier(values)
-
-
-def split_three(value):
-    high = value.astype(jnp.bfloat16)
-    rest = value - high.astype(jnp.float32)
-    middle = rest.astype(jnp.bfloat16)
-    low = (rest - middle.astype(jnp.float32)).astype(jnp.bfloat16)
-    return high, middle, low
 
 
 def pack_kernel(values_ref, scale_ref, packed_ref, row_ref, sems):
@@ -169,20 +162,13 @@
 def late_kernel(places, bundled, panel_mask, lists_ref, counts_ref, query_ref, *refs):
     before, refs = refs[:3], refs[3:]
     pieces, refs = read_pieces(places, refs, bundled)
-    packed_ref, score_ref, total_ref, mass_ref = refs
+    partial_ref, lines_ref, score_ref, total_ref, mass_ref = refs
     row_max = attend(pieces, panel_mask, lists_ref, counts_ref, query_ref, score_ref, total_ref, mass_ref, before)
     row_sum = jnp.sum(mass_ref[...], axis=1, keepdims=True)
-    value_width = total_ref.shape[1]
     inverse = 1.0 / jnp.where(row_sum > 0.0, row_sum, 1.0)
-    packed_ref[0:TILE, :] = (total_ref[...] * inverse).astype(jnp.bfloat16)
-    row = lax.broadcasted_iota(jnp.int32, (EXTRA, LANES), 0)
-    packed = jnp.zeros((EXTRA, LANES), jnp.float32)
-    for first, column in ((0, row_max), (3, row_sum)):
-        turned = jnp.transpose(jnp.broadcast_to(column, (TILE, LANES)))[0:EXTRA]
-        for at, part in enumerate(split_three(turned)):
-            packed = jnp.where(row == first + at, part.astype(jnp.float32), packed)
-    packed_ref[TILE:, 0:LANES] = packed.astype(jnp.bfloat16)
-    packed_ref[TILE:, LANES:] = jnp.zeros((EXTRA, value_width - LANES), jnp.bfloat16)
+    partial_ref[...] = (total_ref[...] * inverse).astype(jnp.bfloat16)
+    lane = lax.broadcasted_iota(jnp.int32, (TILE, LANES), 1)
+    lines_ref[...] = jnp.transpose(jnp.where(lane == 0, row_max, row_sum))[0:SUBLANES]
 
 
 def home_kernel(places, bundled, lists_ref, counts_ref, query_ref, *refs):
@@ -195,23 +181,23 @@
 
 
 def merge_kernel(total_ref, stats_ref, *refs):
-    packed_refs, out_ref = refs[:-1], refs[-1]
+    returned, out_ref = refs[:-1], refs[-1]
+    partial_refs, lines_refs = returned[0::2], returned[1::2]
     maxima = [stats_ref[0]]
     sums = [stats_ref[1]]
-    for packed_ref in packed_refs:
-        packed = packed_ref[TILE:, 0:LANES].astype(jnp.float32)
-        for first, kept in ((0, maxima), (3, sums)):
-            line = packed[first : first + 1] + packed[first + 1 : first + 2] + packed[first + 2 : first + 3]
-            kept.append(jnp.transpose(jnp.broadcast_to(line, (TILE, LANES))))
+    for lines_ref in lines_refs:
+        turned = jnp.transpose(jnp.concatenate([lines_ref[...]] * (TILE // SUBLANES), axis=0))
+        maxima.append(jnp.broadcast_to(turned[:, 0:1], (TILE, LANES)))
+        sums.append(jnp.broadcast_to(turned[:, 1:2], (TILE, LANES)))
     top = functools.reduce(jnp.maximum, maxima)
     factors = [jnp.exp(row_max - top) for row_max in maxima]
     masses = [factor * row_sum for factor, row_sum in zip(factors, sums)]
     inverse = 1.0 / functools.reduce(jnp.add, masses)
-    scales = [factors[0] * inverse] + [mass * inverse for mass in masses[1:]]
+    shares = [factors[0] * inverse] + [mass * inverse for mass in masses[1:]]
     for at in range(0, total_ref.shape[1], LANES):
-        merged = total_ref[:, at : at + LANES] * scales[0]
-        for packed_ref, scale in zip(packed_refs, scales[1:]):
-            merged = merged + packed_ref[0:TILE, at : at + LANES].astype(jnp.float32) * scale
+        merged = total_ref[:, at : at + LANES] * shares[0]
+        for partial_ref, share in zip(partial_refs, shares[1:]):
+            merged = merged + partial_ref[:, at : at + LANES].astype(jnp.float32) * share
         out_ref[:, at : at + LANES] = merged.astype(jnp.bfloat16)
 
 
@@ -311,11 +297,14 @@
     late_arrays = arrays_of(late) + bundled_arrays
     returned = []
     for (mask, visiting), state in zip(visitors, states):
-        packed = pl.pallas_call(
+        partial, lines = pl.pallas_call(
             functools.partial(late_kernel, places_of(late), bundled, mask),
-            out_shape=jax.ShapeDtypeStruct((TILE + EXTRA, value_width), jnp.bfloat16),
+            out_shape=(
+                jax.ShapeDtypeStruct((TILE, value_width), jnp.bfloat16),
+                jax.ShapeDtypeStruct((SUBLANES, LANES), jnp.float32),
+            ),
             in_specs=[VMEM, VMEM] + [VMEM] * (4 + len(late_arrays)),
-            out_specs=VMEM,
+            out_specs=(VMEM, VMEM),
             scratch_shapes=[
                 pltpu.VMEM((len(late) + len(bundled), TILE, TILE), jnp.float32),
                 pltpu.VMEM((TILE, value_width), jnp.float32),
@@ -324,7 +313,7 @@
             compiler_params=attend_params,
             cost_estimate=cost,
         )(window_lists, window_counts, visiting, *state, *late_arrays)
-        returned.append(swap(packed, "qry", mask))
+        returned += [swap(partial, "qry", mask), swap(lines, "qry", mask)]
 
     total, stats = pl.pallas_call(
         functools.partial(home_kernel, places_of(early + late), bundled),

time: 35.5 us -> 37.4 us (1.054)
  starting transfers between devices: 17.2 us -> 18.3 us
  waiting for transfers between devices: 12.8 us -> 13.7 us
    ppermute x15 -> x16, starting transfers between devices: 17.2 us -> 18.3 us  [swap(): return lax.ppermute(value, axis, [(i, i ^ mask) for i in range(length)])]
    ppermute x15 -> x16, waiting for transfers between devices: 12.8 us -> 13.7 us  [swap(): return lax.ppermute(value, axis, [(i, i ^ mask) for i in range(length)])]
    pallas_call x1, Pallas kernels: 0.28 us -> 0.72 us  [body(): pl.pallas_call(functools.partial(early_kernel, places_of(early), mask), o...]
    pallas_call x1, Pallas kernels: 0.86 us -> 0.43 us  [body(): pl.pallas_call(functools.partial(home_kernel, places_of(early + late), bu...]
  transfers between devices with their start and end apart: 15 -> 16, of which waited for: 6 -> 6; matrix products, arithmetic and copies ran while one was open for 0% -> 0% of each run, Pallas kernels for 4% -> 4%
where the time goes in v16:
time: 37.4 us; the launch traced here: 37.5 us
  starting transfers between devices  18.3 us (49%)
  waiting for transfers between devices  13.7 us (37%)
  Pallas kernels  3.18 us (9%)
  local copies, waits for them, and re-layouts  2.22 us (6%)
    ppermute x16, starting transfers between devices, swap(): return lax.ppermute(value, axis, [(i, i ^ mask) for i in range(length)])  18.3 us
    ppermute x16, waiting for transfers between devices, swap(): return lax.ppermute(value, axis, [(i, i ^ mask) for i in range(length)])  13.7 us
    unnamed x12, local copies, waits for them, and re-layouts  2.22 us
    pallas_call x1, Pallas kernels, body(): pl.pallas_call(functools.partial(late_kernel, places_of(late), bundled, m...  0.98 us
    pallas_call x1, Pallas kernels, body(): pl.pallas_call(merge_kernel, out_shape=jax.ShapeDtypeStruct((TILE, value_...  0.88 us
  transfers between devices with their start and end apart: 16, of which 6 were waited for; matrix products, arithmetic and copies ran while one was open for 0% of the time, Pallas kernels for 4%

profile of v16, /device:TPU:0, one launch (start us, length us, event | category | flops | bytes accessed | tf_op | source)
XLA Modules:
  0.0 37.5 jit_solution(17019151206841723316)
XLA Ops:
  0.0 0.5 %collective-permute-start.1 = (bf16[128,1024]{1,0:T(8,128)(2,1)}, bf16[128,1024]{1,0:T(8,128)(2,1)S(1)}, u32[]{:S(2)}, u32[]{:S(2)}) collective-permute-start(bf16[128,1024]{1,0:T(8,128)(2,1)} %refs_13_.1), channel_id=1, source_target_pairs={{0,4},{4,0},{8,12},{12,8},{1,5},{5,1},{9,13},{13,9},{2,6},{6,2},{1... | collective-permute-start | bytes 786440 | tf_op jit(solution)/shard_map/ppermute | solution.py:25
  0.5 2.6 %collective-permute-start = (bf16[128,1024]{1,0:T(8,128)(2,1)}, bf16[128,1024]{1,0:T(8,128)(2,1)S(1)}, u32[]{:S(2)}, u32[]{:S(2)}) collective-permute-start(bf16[128,1024]{1,0:T(8,128)(2,1)} %refs_13_.1), channel_id=1, source_target_pairs={{0,1},{1,0},{2,3},{3,2},{4,5},{5,4},{6,7},{7,6},{8,9},{9,8},{10,11... | collective-permute-start | bytes 786440 | tf_op jit(solution)/shard_map/ppermute | solution.py:25
  3.1 1.5 %collective-permute-start.3 = (bf16[128,1024]{1,0:T(8,128)(2,1)}, bf16[128,1024]{1,0:T(8,128)(2,1)S(1)}, u32[]{:S(2)}, u32[]{:S(2)}) collective-permute-start(bf16[128,1024]{1,0:T(8,128)(2,1)} %refs_13_.1), channel_id=1, source_target_pairs={{0,8},{4,12},{8,0},{12,4},{1,9},{5,13},{9,1},{13,5},{2,10},{6,14},... | collective-permute-start | bytes 786440 | tf_op jit(solution)/shard_map/ppermute | solution.py:25
  4.6 0.0 collective-permute-done.1.refs_4_.refs_3_
  4.6 0.9 %copy-done.2 = bf16[128,512]{1,0:T(8,128)(2,1)S(1)} copy-done((bf16[128,512]{1,0:T(8,128)(2,1)S(1)}, bf16[128,512]{1,0:T(8,128)(2,1)}, u32[]{:S(2)}) %copy-start.2) | copy-done | bytes 131096
  5.5 0.7 %copy-done.5 = bf16[128]{0:T(256)(128)(2,1)S(1)} copy-done((bf16[128]{0:T(256)(128)(2,1)S(1)}, bf16[128]{0:T(256)(128)(2,1)}, u32[]{:S(2)}) %copy-start.5) | copy-done | bytes 280
  6.1 0.2 shard_map.64.refs_5_.refs_14_
  6.3 0.0 copy-start
  6.3 0.1 collective-permute-start.5
  6.4 0.5 %collective-permute-start.2 = (bf16[144,512]{1,0:T(8,128)(2,1)S(1)}, bf16[144,512]{1,0:T(8,128)(2,1)S(1)}, u32[]{:S(2)}, u32[]{:S(2)}) collective-permute-start(bf16[144,512]{1,0:T(8,128)(2,1)S(1)} %shard_map.64.refs_5_.refs_14_), channel_id=1, source_target_pairs={{0,1},{1,0},{2,3},{3,2},{4,5},{5,4},{6,7},{7,6},{8,9},{9,8},{10,11... | collective-permute-start | bytes 442376 | tf_op jit(solution)/shard_map/ppermute | solution.py:25
  6.9 1.3 %collective-permute-start.4 = (bf16[144,512]{1,0:T(8,128)(2,1)S(1)}, bf16[144,512]{1,0:T(8,128)(2,1)S(1)}, u32[]{:S(2)}, u32[]{:S(2)}) collective-permute-start(bf16[144,512]{1,0:T(8,128)(2,1)S(1)} %shard_map.64.refs_5_.refs_14_), channel_id=1, source_target_pairs={{0,8},{4,12},{8,0},{12,4},{1,9},{5,13},{9,1},{13,5},{2,10},{6,14},... | collective-permute-start | bytes 442376 | tf_op jit(solution)/shard_map/ppermute | solution.py:25
  8.2 0.0 collective-permute-done.5.refs_5_.refs_4_
  8.2 2.8 %collective-permute-start.8 = (bf16[128,1024]{1,0:T(8,128)(2,1)S(1)}, bf16[128,1024]{1,0:T(8,128)(2,1)S(1)}, u32[]{:S(2)}, u32[]{:S(2)}) collective-permute-start(bf16[128,1024]{1,0:T(8,128)(2,1)S(1)} %copy-done.1), channel_id=1, source_target_pairs={{0,3},{1,2},{2,1},{3,0},{4,7},{5,6},{6,5},{7,4},{8,11},{9,10},{10,... | collective-permute-start | bytes 786440 | tf_op jit(solution)/shard_map/ppermute | solution.py:25
  11.1 1.4 %collective-permute-done.3.refs_2_ = bf16[128,1024]{1,0:T(8,128)(2,1)S(1)} collective-permute-done((bf16[128,1024]{1,0:T(8,128)(2,1)}, bf16[128,1024]{1,0:T(8,128)(2,1)S(1)}, u32[]{:S(2)}, u32[]{:S(2)}) %collective-permute-start.3) | collective-permute-done | bytes 262176 | tf_op jit(solution)/shard_map/ppermute | solution.py:25
  12.5 1.5 %collective-permute-start.6 = (bf16[128,1024]{1,0:T(8,128)(2,1)S(1)}, bf16[128,1024]{1,0:T(8,128)(2,1)S(1)}, u32[]{:S(2)}, u32[]{:S(2)}) collective-permute-start(bf16[128,1024]{1,0:T(8,128)(2,1)S(1)} %collective-permute-done.refs_0_), channel_id=1, source_target_pairs={{0,8},{4,12},{8,0},{12,4},{1,9},{5,13},{9,1},{13,5},{2,10},{6,14},... | collective-permute-start | bytes 786440 | tf_op jit(solution)/shard_map/ppermute | solution.py:25
  13.9 1.7 %collective-permute-done.4.refs_3_.refs_1_ = bf16[144,512]{1,0:T(8,128)(2,1)S(1)} collective-permute-done((bf16[144,512]{1,0:T(8,128)(2,1)S(1)}, bf16[144,512]{1,0:T(8,128)(2,1)S(1)}, u32[]{:S(2)}, u32[]{:S(2)}) %collective-permute-start.4) | collective-permute-done | bytes 147488 | tf_op jit(solution)/shard_map/ppermute | solution.py:25
  15.6 1.5 %collective-permute-start.7 = (bf16[144,512]{1,0:T(8,128)(2,1)S(1)}, bf16[144,512]{1,0:T(8,128)(2,1)S(1)}, u32[]{:S(2)}, u32[]{:S(2)}) collective-permute-start(bf16[144,512]{1,0:T(8,128)(2,1)S(1)} %collective-permute-done.2.refs_1_.refs_0_), channel_id=1, source_target_pairs={{0,8},{4,12},{8,0},{12,4},{1,9},{5,13},{9,1},{13,5},{2,10},{6,14},... | collective-permute-start | bytes 442376 | tf_op jit(solution)/shard_map/ppermute | solution.py:25
  17.1 0.0 copy-start.3
  17.1 0.1 collective-permute-start.13
  17.2 0.5 %collective-permute-start.11 = (bf16[128,1024]{1,0:T(8,128)(2,1)S(1)}, bf16[128,1024]{1,0:T(8,128)(2,1)S(1)}, u32[]{:S(2)}, u32[]{:S(2)}) collective-permute-start(bf16[128,1024]{1,0:T(8,128)(2,1)S(1)} %collective-permute-done.refs_0_), channel_id=1, source_target_pairs={{0,4},{4,0},{8,12},{12,8},{1,5},{5,1},{9,13},{13,9},{2,6},{6,2},{1... | collective-permute-start | bytes 786440 | tf_op jit(solution)/shard_map/ppermute | solution.py:25
  17.7 3.6 %collective-permute-done.8.query_ref = bf16[128,1024]{1,0:T(8,128)(2,1)S(1)} collective-permute-done((bf16[128,1024]{1,0:T(8,128)(2,1)S(1)}, bf16[128,1024]{1,0:T(8,128)(2,1)S(1)}, u32[]{:S(2)}, u32[]{:S(2)}) %collective-permute-start.8) | collective-permute-done | bytes 262176 | tf_op jit(solution)/shard_map/ppermute | solution.py:25
  21.3 0.6 %copy-done.4 = s32[16]{0:T(128)S(1)} copy-done((s32[16]{0:T(128)S(1)}, s32[16]{0:T(128)}, u32[]{:S(2)}) %copy-start.4) | copy-done | bytes 88
  21.9 0.7 %shard_map.65 = (f32[128,512]{1,0:T(8,128)S(1)}, f32[128,128]{1,0:T(8,128)S(1)}, f32[128,128]{1,0:T(8,128)S(1)}) custom-call(s32[4,16]{1,0:T(4,128)S(1)} %bitcast.3, s32[1,16]{1,0:T(1,128)S(1)} %bitcast.6, bf16[128,1024]{1,0:T(8,128)(2,1)S(1)} %collective-permute-done.8.query_ref, bf16[128,1024]{1,0:T(8,128)(2,1)S(1)} %collective-permute-done.refs_0_, ...), custom_call_target="tpu_custom_call" | custom-call | flops 268435456 | bytes 4194304 | tf_op jit(solution)/shard_map/pallas_call | solution.py:274
  22.7 0.9 %collective-permute-done.7.refs_7_.refs_6_ = bf16[144,512]{1,0:T(8,128)(2,1)S(1)} collective-permute-done((bf16[144,512]{1,0:T(8,128)(2,1)S(1)}, bf16[144,512]{1,0:T(8,128)(2,1)S(1)}, u32[]{:S(2)}, u32[]{:S(2)}) %collective-permute-start.7) | collective-permute-done | bytes 147488 | tf_op jit(solution)/shard_map/ppermute | solution.py:25
  23.6 0.5 %collective-permute-start.10 = (bf16[144,512]{1,0:T(8,128)(2,1)S(1)}, bf16[144,512]{1,0:T(8,128)(2,1)S(1)}, u32[]{:S(2)}, u32[]{:S(2)}) collective-permute-start(bf16[144,512]{1,0:T(8,128)(2,1)S(1)} %collective-permute-done.7.refs_7_.refs_6_), channel_id=1, source_target_pairs={{0,4},{4,0},{8,12},{12,8},{1,5},{5,1},{9,13},{13,9},{2,6},{6,2},{1... | collective-permute-start | bytes 442376 | tf_op jit(solution)/shard_map/ppermute | solution.py:25
  24.1 1.2 %collective-permute-done.10.refs_9_.refs_8_ = bf16[144,512]{1,0:T(8,128)(2,1)S(1)} collective-permute-done((bf16[144,512]{1,0:T(8,128)(2,1)S(1)}, bf16[144,512]{1,0:T(8,128)(2,1)S(1)}, u32[]{:S(2)}, u32[]{:S(2)}) %collective-permute-start.10) | collective-permute-done | bytes 147488 | tf_op jit(solution)/shard_map/ppermute | solution.py:25
  25.4 1.0 %shard_map.68 = (bf16[128,512]{1,0:T(8,128)(2,1)S(1)}, f32[8,128]{1,0:T(8,128)S(1)}) custom-call(s32[4,16]{1,0:T(4,128)S(1)} %bitcast.4, s32[1,16]{1,0:T(1,128)S(1)} %bitcast.7, bf16[128,1024]{1,0:T(8,128)(2,1)S(1)} %collective-permute-done.8.query_ref, f32[128,512]{1,0:T(8,128)S(1)} %get-tuple-element.27.refs_0_, f32[128,128]{1,0:T(8,128)S(1)} %get-tuple-element.28.refs_1_, ...), custom_call_target="tpu_custom_call" | custom-call | flops 268435456 | bytes 4194304 | tf_op jit(solution)/shard_map/pallas_call | solution.py:300
  26.3 4.8 %collective-permute-start.14 = (bf16[128,512]{1,0:T(8,128)(2,1)S(1)}, bf16[128,512]{1,0:T(8,128)(2,1)S(1)}, u32[]{:S(2)}, u32[]{:S(2)}) collective-permute-start(bf16[128,512]{1,0:T(8,128)(2,1)S(1)} %get-tuple-element.29), channel_id=1, source_target_pairs={{0,3},{1,2},{2,1},{3,0},{4,7},{5,6},{6,5},{7,4},{8,11},{9,10},{10,... | collective-permute-start | bytes 393224 | tf_op jit(solution)/shard_map/ppermute | solution.py:25
  31.2 0.1 collective-permute-start.15
  31.3 0.4 %shard_map.67 = (f32[128,512]{1,0:T(8,128)S(1)}, f32[2,128,128]{2,1,0:T(8,128)S(1)}) custom-call(s32[4,16]{1,0:T(4,128)S(1)} %bitcast.5, s32[1,16]{1,0:T(1,128)S(1)} %bitcast.8, bf16[128,1024]{1,0:T(8,128)(2,1)S(1)} %copy-done.1, bf16[128,1024]{1,0:T(8,128)(2,1)S(1)} %collective-permute-done.refs_0_, ...), custom_call_target="tpu_custom_call" | custom-call | flops 268435456 | bytes 4194304 | tf_op jit(solution)/shard_map/pallas_call | solution.py:318
  31.7 4.9 %collective-permute-done.15.refs_1_ = f32[8,128]{1,0:T(8,128)S(1)} collective-permute-done((f32[8,128]{1,0:T(8,128)S(1)}, f32[8,128]{1,0:T(8,128)S(1)}, u32[]{:S(2)}, u32[]{:S(2)}) %collective-permute-start.15) | collective-permute-done | bytes 4128 | tf_op jit(solution)/shard_map/ppermute | solution.py:25
  36.6 0.9 %shard_map.69 = bf16[128,512]{1,0:T(8,128)(2,1)} custom-call(f32[128,512]{1,0:T(8,128)S(1)} %get-tuple-element.25.total_ref, f32[2,128,128]{2,1,0:T(8,128)S(1)} %get-tuple-element.26.stats_ref, bf16[128,512]{1,0:T(8,128)(2,1)S(1)} %collective-permute-done.14.refs_0_, f32[8,128]{1,0:T(8,128)S(1)} %collective-permute-done.15.refs_1_), custom_call_target="tpu_custom_call" | custom-call | tf_op jit(solution)/shard_map/pallas_call | solution.py:332
  (18 shorter events, 0.1 us)
Async XLA Ops:
  0.0 8.2 %copy-start.1 = (bf16[128,1024]{1,0:T(8,128)(2,1)S(1)}, bf16[128,1024]{1,0:T(8,128)(2,1)}, u32[]{:S(2)}) copy-start(bf16[128,1024]{1,0:T(8,128)(2,1)} %query_ref.1) | copy-start | bytes 786436
  0.0 4.6 %collective-permute-start.1 = (bf16[128,1024]{1,0:T(8,128)(2,1)}, bf16[128,1024]{1,0:T(8,128)(2,1)S(1)}, u32[]{:S(2)}, u32[]{:S(2)}) collective-permute-start(bf16[128,1024]{1,0:T(8,128)(2,1)} %refs_13_.1), channel_id=1, source_target_pairs={{0,4},{4,0},{8,12},{12,8},{1,5},{5,1},{9,13},{13,9},{2,6},{6,2},{1... | collective-permute-start | bytes 786440 | tf_op jit(solution)/shard_map/ppermute | solution.py:25
  0.5 10.6 %collective-permute-start = (bf16[128,1024]{1,0:T(8,128)(2,1)}, bf16[128,1024]{1,0:T(8,128)(2,1)S(1)}, u32[]{:S(2)}, u32[]{:S(2)}) collective-permute-start(bf16[128,1024]{1,0:T(8,128)(2,1)} %refs_13_.1), channel_id=1, source_target_pairs={{0,1},{1,0},{2,3},{3,2},{4,5},{5,4},{6,7},{7,6},{8,9},{9,8},{10,11... | collective-permute-start | bytes 786440 | tf_op jit(solution)/shard_map/ppermute | solution.py:25
  3.1 9.4 %collective-permute-start.3 = (bf16[128,1024]{1,0:T(8,128)(2,1)}, bf16[128,1024]{1,0:T(8,128)(2,1)S(1)}, u32[]{:S(2)}, u32[]{:S(2)}) collective-permute-start(bf16[128,1024]{1,0:T(8,128)(2,1)} %refs_13_.1), channel_id=1, source_target_pairs={{0,8},{4,12},{8,0},{12,4},{1,9},{5,13},{9,1},{13,5},{2,10},{6,14},... | collective-permute-start | bytes 786440 | tf_op jit(solution)/shard_map/ppermute | solution.py:25
  4.6 0.9 %copy-start.2 = (bf16[128,512]{1,0:T(8,128)(2,1)S(1)}, bf16[128,512]{1,0:T(8,128)(2,1)}, u32[]{:S(2)}) copy-start(bf16[128,512]{1,0:T(8,128)(2,1)} %values_ref) | copy-start | bytes 393220
  5.5 0.7 %copy-start.5 = (bf16[128]{0:T(256)(128)(2,1)S(1)}, bf16[128]{0:T(256)(128)(2,1)}, u32[]{:S(2)}) copy-start(bf16[128]{0:T(256)(128)(2,1)} %param.9) | copy-start | bytes 772
  6.3 15.0 %copy-start = (bf16[128,1024]{1,0:T(8,128)(2,1)S(1)}, bf16[128,1024]{1,0:T(8,128)(2,1)}, u32[]{:S(2)}) copy-start(bf16[128,1024]{1,0:T(8,128)(2,1)} %refs_13_.1) | copy-start | bytes 786436
  6.3 1.9 %collective-permute-start.5 = (bf16[144,512]{1,0:T(8,128)(2,1)S(1)}, bf16[144,512]{1,0:T(8,128)(2,1)S(1)}, u32[]{:S(2)}, u32[]{:S(2)}) collective-permute-start(bf16[144,512]{1,0:T(8,128)(2,1)S(1)} %shard_map.64.refs_5_.refs_14_), channel_id=1, source_target_pairs={{0,4},{4,0},{8,12},{12,8},{1,5},{5,1},{9,13},{13,9},{2,6},{6,2},{1... | collective-permute-start | bytes 442376 | tf_op jit(solution)/shard_map/ppermute | solution.py:25
  6.4 7.5 %collective-permute-start.2 = (bf16[144,512]{1,0:T(8,128)(2,1)S(1)}, bf16[144,512]{1,0:T(8,128)(2,1)S(1)}, u32[]{:S(2)}, u32[]{:S(2)}) collective-permute-start(bf16[144,512]{1,0:T(8,128)(2,1)S(1)} %shard_map.64.refs_5_.refs_14_), channel_id=1, source_target_pairs={{0,1},{1,0},{2,3},{3,2},{4,5},{5,4},{6,7},{7,6},{8,9},{9,8},{10,11... | collective-permute-start | bytes 442376 | tf_op jit(solution)/shard_map/ppermute | solution.py:25
  6.9 8.7 %collective-permute-start.4 = (bf16[144,512]{1,0:T(8,128)(2,1)S(1)}, bf16[144,512]{1,0:T(8,128)(2,1)S(1)}, u32[]{:S(2)}, u32[]{:S(2)}) collective-permute-start(bf16[144,512]{1,0:T(8,128)(2,1)S(1)} %shard_map.64.refs_5_.refs_14_), channel_id=1, source_target_pairs={{0,8},{4,12},{8,0},{12,4},{1,9},{5,13},{9,1},{13,5},{2,10},{6,14},... | collective-permute-start | bytes 442376 | tf_op jit(solution)/shard_map/ppermute | solution.py:25
  8.2 13.1 %collective-permute-start.8 = (bf16[128,1024]{1,0:T(8,128)(2,1)S(1)}, bf16[128,1024]{1,0:T(8,128)(2,1)S(1)}, u32[]{:S(2)}, u32[]{:S(2)}) collective-permute-start(bf16[128,1024]{1,0:T(8,128)(2,1)S(1)} %copy-done.1), channel_id=1, source_target_pairs={{0,3},{1,2},{2,1},{3,0},{4,7},{5,6},{6,5},{7,4},{8,11},{9,10},{10,... | collective-permute-start | bytes 786440 | tf_op jit(solution)/shard_map/ppermute | solution.py:25
  12.5 10.2 %collective-permute-start.6 = (bf16[128,1024]{1,0:T(8,128)(2,1)S(1)}, bf16[128,1024]{1,0:T(8,128)(2,1)S(1)}, u32[]{:S(2)}, u32[]{:S(2)}) collective-permute-start(bf16[128,1024]{1,0:T(8,128)(2,1)S(1)} %collective-permute-done.refs_0_), channel_id=1, source_target_pairs={{0,8},{4,12},{8,0},{12,4},{1,9},{5,13},{9,1},{13,5},{2,10},{6,14},... | collective-permute-start | bytes 786440 | tf_op jit(solution)/shard_map/ppermute | solution.py:25
  15.6 8.0 %collective-permute-start.7 = (bf16[144,512]{1,0:T(8,128)(2,1)S(1)}, bf16[144,512]{1,0:T(8,128)(2,1)S(1)}, u32[]{:S(2)}, u32[]{:S(2)}) collective-permute-start(bf16[144,512]{1,0:T(8,128)(2,1)S(1)} %collective-permute-done.2.refs_1_.refs_0_), channel_id=1, source_target_pairs={{0,8},{4,12},{8,0},{12,4},{1,9},{5,13},{9,1},{13,5},{2,10},{6,14},... | collective-permute-start | bytes 442376 | tf_op jit(solution)/shard_map/ppermute | solution.py:25
  17.1 4.2 %copy-start.3 = (s32[16,4]{0,1:T(4,128)S(1)}, s32[16,4]{0,1:T(4,128)}, u32[]{:S(2)}) copy-start(s32[16,4]{0,1:T(4,128)} %param.10) | copy-start | bytes 772
  17.1 7.0 %collective-permute-start.13 = (bf16[288,512]{1,0:T(8,128)(2,1)S(1)}, bf16[288,512]{1,0:T(8,128)(2,1)S(1)}, u32[]{:S(2)}, u32[]{:S(2)}) collective-permute-start(bf16[288,512]{1,0:T(8,128)(2,1)S(1)} %shard_map.66), channel_id=1, source_target_pairs={{0,4},{4,0},{8,12},{12,8},{1,5},{5,1},{9,13},{13,9},{2,6},{6,2},{1... | collective-permute-start | bytes 884744 | tf_op jit(solution)/shard_map/ppermute | solution.py:25
  17.2 6.9 %collective-permute-start.11 = (bf16[128,1024]{1,0:T(8,128)(2,1)S(1)}, bf16[128,1024]{1,0:T(8,128)(2,1)S(1)}, u32[]{:S(2)}, u32[]{:S(2)}) collective-permute-start(bf16[128,1024]{1,0:T(8,128)(2,1)S(1)} %collective-permute-done.refs_0_), channel_id=1, source_target_pairs={{0,4},{4,0},{8,12},{12,8},{1,5},{5,1},{9,13},{13,9},{2,6},{6,2},{1... | collective-permute-start | bytes 786440 | tf_op jit(solution)/shard_map/ppermute | solution.py:25
  21.3 2.8 %collective-permute-start.12 = (bf16[128,1024]{1,0:T(8,128)(2,1)S(1)}, bf16[128,1024]{1,0:T(8,128)(2,1)S(1)}, u32[]{:S(2)}, u32[]{:S(2)}) collective-permute-start(bf16[128,1024]{1,0:T(8,128)(2,1)S(1)} %collective-permute-done.3.refs_2_), channel_id=1, source_target_pairs={{0,4},{4,0},{8,12},{12,8},{1,5},{5,1},{9,13},{13,9},{2,6},{6,2},{1... | collective-permute-start | bytes 786440 | tf_op jit(solution)/shard_map/ppermute | solution.py:25
  21.3 0.7 %copy-start.4 = (s32[16]{0:T(128)S(1)}, s32[16]{0:T(128)}, u32[]{:S(2)}) copy-start(s32[16]{0:T(128)} %param.11) | copy-start | bytes 196
  23.6 1.8 %collective-permute-start.9 = (bf16[128,1024]{1,0:T(8,128)(2,1)S(1)}, bf16[128,1024]{1,0:T(8,128)(2,1)S(1)}, u32[]{:S(2)}, u32[]{:S(2)}) collective-permute-start(bf16[128,1024]{1,0:T(8,128)(2,1)S(1)} %collective-permute-done.6.refs_6_.refs_5_), channel_id=1, source_target_pairs={{0,4},{4,0},{8,12},{12,8},{1,5},{5,1},{9,13},{13,9},{2,6},{6,2},{1... | collective-permute-start | bytes 786440 | tf_op jit(solution)/shard_map/ppermute | solution.py:25
  23.6 1.7 %collective-permute-start.10 = (bf16[144,512]{1,0:T(8,128)(2,1)S(1)}, bf16[144,512]{1,0:T(8,128)(2,1)S(1)}, u32[]{:S(2)}, u32[]{:S(2)}) collective-permute-start(bf16[144,512]{1,0:T(8,128)(2,1)S(1)} %collective-permute-done.7.refs_7_.refs_6_), channel_id=1, source_target_pairs={{0,4},{4,0},{8,12},{12,8},{1,5},{5,1},{9,13},{13,9},{2,6},{6,2},{1... | collective-permute-start | bytes 442376 | tf_op jit(solution)/shard_map/ppermute | solution.py:25
  26.3 10.2 %collective-permute-start.14 = (bf16[128,512]{1,0:T(8,128)(2,1)S(1)}, bf16[128,512]{1,0:T(8,128)(2,1)S(1)}, u32[]{:S(2)}, u32[]{:S(2)}) collective-permute-start(bf16[128,512]{1,0:T(8,128)(2,1)S(1)} %get-tuple-element.29), channel_id=1, source_target_pairs={{0,3},{1,2},{2,1},{3,0},{4,7},{5,6},{6,5},{7,4},{8,11},{9,10},{10,... | collective-permute-start | bytes 393224 | tf_op jit(solution)/shard_map/ppermute | solution.py:25
  31.2 5.4 %collective-permute-start.15 = (f32[8,128]{1,0:T(8,128)S(1)}, f32[8,128]{1,0:T(8,128)S(1)}, u32[]{:S(2)}, u32[]{:S(2)}) collective-permute-start(f32[8,128]{1,0:T(8,128)S(1)} %get-tuple-element.30), channel_id=1, source_target_pairs={{0,3},{1,2},{2,1},{3,0},{4,7},{5,6},{6,5},{7,4},{8,11},{9,10},{10,... | collective-permute-start | bytes 12296 | tf_op jit(solution)/shard_map/ppermute | solution.py:25

commit v17 on v15

--- a/solution.py
+++ b/solution.py
@@ -11,6 +11,7 @@
 TILE = 128
 LANES = 128
 EXTRA = 16
+LINES = 8
 MASKED_SCORE = -1e30
 VMEM = pl.BlockSpec(memory_space=pltpu.VMEM)
 
@@ -175,14 +176,14 @@
     value_width = total_ref.shape[1]
     inverse = 1.0 / jnp.where(row_sum > 0.0, row_sum, 1.0)
     packed_ref[0:TILE, :] = (total_ref[...] * inverse).astype(jnp.bfloat16)
-    row = lax.broadcasted_iota(jnp.int32, (EXTRA, LANES), 0)
-    packed = jnp.zeros((EXTRA, LANES), jnp.float32)
+    row = lax.broadcasted_iota(jnp.int32, (LINES, LANES), 0)
+    packed = jnp.zeros((LINES, LANES), jnp.float32)
     for first, column in ((0, row_max), (3, row_sum)):
-        turned = jnp.transpose(jnp.broadcast_to(column, (TILE, LANES)))[0:EXTRA]
+        turned = jnp.transpose(jnp.broadcast_to(column, (TILE, LANES)))[0:LINES]
         for at, part in enumerate(split_three(turned)):
             packed = jnp.where(row == first + at, part.astype(jnp.float32), packed)
     packed_ref[TILE:, 0:LANES] = packed.astype(jnp.bfloat16)
-    packed_ref[TILE:, LANES:] = jnp.zeros((EXTRA, value_width - LANES), jnp.bfloat16)
+    packed_ref[TILE:, LANES:] = jnp.zeros((LINES, value_width - LANES), jnp.bfloat16)
 
 
 def home_kernel(places, bundled, lists_ref, counts_ref, query_ref, *refs):
@@ -313,7 +314,7 @@
     for (mask, visiting), state in zip(visitors, states):
         packed = pl.pallas_call(
             functools.partial(late_kernel, places_of(late), bundled, mask),
-            out_shape=jax.ShapeDtypeStruct((TILE + EXTRA, value_width), jnp.bfloat16),
+            out_shape=jax.ShapeDtypeStruct((TILE + LINES, value_width), jnp.bfloat16),
             in_specs=[VMEM, VMEM] + [VMEM] * (4 + len(late_arrays)),
             out_specs=VMEM,
             scratch_shapes=[

time: 35.5 us -> 35.5 us (level); the launches traced: 35.5 us -> 35.1 us
  starting transfers between devices: 17.2 us -> 18.2 us
  waiting for transfers between devices: 12.8 us -> 11.9 us
  Pallas kernels: 3.1 us -> 2.61 us
    ppermute x15, starting transfers between devices: 17.2 us -> 18.2 us  [swap(): return lax.ppermute(value, axis, [(i, i ^ mask) for i in range(length)])]
    ppermute x15, waiting for transfers between devices: 12.8 us -> 11.9 us  [swap(): return lax.ppermute(value, axis, [(i, i ^ mask) for i in range(length)])]
    pallas_call x1, Pallas kernels: 0.97 us -> 0.48 us  [body(): pl.pallas_call(functools.partial(late_kernel, places_of(late), bundled, m...]
where the time goes in v17:
time: 35.5 us; the launch traced here: 35.1 us
  starting transfers between devices  18.2 us (51%)
  waiting for transfers between devices  11.9 us (34%)
  Pallas kernels  2.61 us (7%)
  local copies, waits for them, and re-layouts  2.22 us (6%)
    ppermute x15, starting transfers between devices, swap(): return lax.ppermute(value, axis, [(i, i ^ mask) for i in range(length)])  18.2 us
    ppermute x15, waiting for transfers between devices, swap(): return lax.ppermute(value, axis, [(i, i ^ mask) for i in range(length)])  11.9 us
    unnamed x12, local copies, waits for them, and re-layouts  2.22 us
    pallas_call x1, Pallas kernels, body(): pl.pallas_call(functools.partial(home_kernel, places_of(early + late), bu...  0.87 us
    pallas_call x1, Pallas kernels, body(): pl.pallas_call(merge_kernel, out_shape=jax.ShapeDtypeStruct((TILE, value_...  0.81 us
  transfers between devices with their start and end apart: 15, of which 6 were waited for; matrix products, arithmetic and copies ran while one was open for 0% of the time, Pallas kernels for 4%

profile of v17, /device:TPU:0, one launch (start us, length us, event | category | flops | bytes accessed | tf_op | source)
XLA Modules:
  0.0 35.1 jit_solution(9479338846460425393)
XLA Ops:
  0.0 0.5 %collective-permute-start.1 = (bf16[128,1024]{1,0:T(8,128)(2,1)}, bf16[128,1024]{1,0:T(8,128)(2,1)S(1)}, u32[]{:S(2)}, u32[]{:S(2)}) collective-permute-start(bf16[128,1024]{1,0:T(8,128)(2,1)} %refs_13_.1), channel_id=1, source_target_pairs={{0,4},{4,0},{8,12},{12,8},{1,5},{5,1},{9,13},{13,9},{2,6},{6,2},{1... | collective-permute-start | bytes 786440 | tf_op jit(solution)/shard_map/ppermute | solution.py:25
  0.5 2.6 %collective-permute-start = (bf16[128,1024]{1,0:T(8,128)(2,1)}, bf16[128,1024]{1,0:T(8,128)(2,1)S(1)}, u32[]{:S(2)}, u32[]{:S(2)}) collective-permute-start(bf16[128,1024]{1,0:T(8,128)(2,1)} %refs_13_.1), channel_id=1, source_target_pairs={{0,1},{1,0},{2,3},{3,2},{4,5},{5,4},{6,7},{7,6},{8,9},{9,8},{10,11... | collective-permute-start | bytes 786440 | tf_op jit(solution)/shard_map/ppermute | solution.py:25
  3.1 1.5 %collective-permute-start.3 = (bf16[128,1024]{1,0:T(8,128)(2,1)}, bf16[128,1024]{1,0:T(8,128)(2,1)S(1)}, u32[]{:S(2)}, u32[]{:S(2)}) collective-permute-start(bf16[128,1024]{1,0:T(8,128)(2,1)} %refs_13_.1), channel_id=1, source_target_pairs={{0,8},{4,12},{8,0},{12,4},{1,9},{5,13},{9,1},{13,5},{2,10},{6,14},... | collective-permute-start | bytes 786440 | tf_op jit(solution)/shard_map/ppermute | solution.py:25
  4.6 0.0 collective-permute-done.1.refs_4_.refs_3_
  4.6 0.9 %copy-done.2 = bf16[128,512]{1,0:T(8,128)(2,1)S(1)} copy-done((bf16[128,512]{1,0:T(8,128)(2,1)S(1)}, bf16[128,512]{1,0:T(8,128)(2,1)}, u32[]{:S(2)}) %copy-start.2) | copy-done | bytes 131096
  5.5 0.7 %copy-done.5 = bf16[128]{0:T(256)(128)(2,1)S(1)} copy-done((bf16[128]{0:T(256)(128)(2,1)S(1)}, bf16[128]{0:T(256)(128)(2,1)}, u32[]{:S(2)}) %copy-start.5) | copy-done | bytes 280
  6.1 0.2 shard_map.64.refs_5_.refs_14_
  6.3 0.0 copy-start
  6.3 0.1 collective-permute-start.5
  6.4 0.5 %collective-permute-start.2 = (bf16[144,512]{1,0:T(8,128)(2,1)S(1)}, bf16[144,512]{1,0:T(8,128)(2,1)S(1)}, u32[]{:S(2)}, u32[]{:S(2)}) collective-permute-start(bf16[144,512]{1,0:T(8,128)(2,1)S(1)} %shard_map.64.refs_5_.refs_14_), channel_id=1, source_target_pairs={{0,1},{1,0},{2,3},{3,2},{4,5},{5,4},{6,7},{7,6},{8,9},{9,8},{10,11... | collective-permute-start | bytes 442376 | tf_op jit(solution)/shard_map/ppermute | solution.py:25
  6.9 1.3 %collective-permute-start.4 = (bf16[144,512]{1,0:T(8,128)(2,1)S(1)}, bf16[144,512]{1,0:T(8,128)(2,1)S(1)}, u32[]{:S(2)}, u32[]{:S(2)}) collective-permute-start(bf16[144,512]{1,0:T(8,128)(2,1)S(1)} %shard_map.64.refs_5_.refs_14_), channel_id=1, source_target_pairs={{0,8},{4,12},{8,0},{12,4},{1,9},{5,13},{9,1},{13,5},{2,10},{6,14},... | collective-permute-start | bytes 442376 | tf_op jit(solution)/shard_map/ppermute | solution.py:25
  8.2 0.0 collective-permute-done.5.refs_5_.refs_4_
  8.2 2.8 %collective-permute-start.8 = (bf16[128,1024]{1,0:T(8,128)(2,1)S(1)}, bf16[128,1024]{1,0:T(8,128)(2,1)S(1)}, u32[]{:S(2)}, u32[]{:S(2)}) collective-permute-start(bf16[128,1024]{1,0:T(8,128)(2,1)S(1)} %copy-done.1), channel_id=1, source_target_pairs={{0,3},{1,2},{2,1},{3,0},{4,7},{5,6},{6,5},{7,4},{8,11},{9,10},{10,... | collective-permute-start | bytes 786440 | tf_op jit(solution)/shard_map/ppermute | solution.py:25
  11.1 0.0 collective-permute-done.refs_0_
  11.1 1.4 %collective-permute-done.3.refs_2_ = bf16[128,1024]{1,0:T(8,128)(2,1)S(1)} collective-permute-done((bf16[128,1024]{1,0:T(8,128)(2,1)}, bf16[128,1024]{1,0:T(8,128)(2,1)S(1)}, u32[]{:S(2)}, u32[]{:S(2)}) %collective-permute-start.3) | collective-permute-done | bytes 262176 | tf_op jit(solution)/shard_map/ppermute | solution.py:25
  12.5 1.5 %collective-permute-start.6 = (bf16[128,1024]{1,0:T(8,128)(2,1)S(1)}, bf16[128,1024]{1,0:T(8,128)(2,1)S(1)}, u32[]{:S(2)}, u32[]{:S(2)}) collective-permute-start(bf16[128,1024]{1,0:T(8,128)(2,1)S(1)} %collective-permute-done.refs_0_), channel_id=1, source_target_pairs={{0,8},{4,12},{8,0},{12,4},{1,9},{5,13},{9,1},{13,5},{2,10},{6,14},... | collective-permute-start | bytes 786440 | tf_op jit(solution)/shard_map/ppermute | solution.py:25
  13.9 1.7 %collective-permute-done.4.refs_3_.refs_1_ = bf16[144,512]{1,0:T(8,128)(2,1)S(1)} collective-permute-done((bf16[144,512]{1,0:T(8,128)(2,1)S(1)}, bf16[144,512]{1,0:T(8,128)(2,1)S(1)}, u32[]{:S(2)}, u32[]{:S(2)}) %collective-permute-start.4) | collective-permute-done | bytes 147488 | tf_op jit(solution)/shard_map/ppermute | solution.py:25
  15.6 1.5 %collective-permute-start.7 = (bf16[144,512]{1,0:T(8,128)(2,1)S(1)}, bf16[144,512]{1,0:T(8,128)(2,1)S(1)}, u32[]{:S(2)}, u32[]{:S(2)}) collective-permute-start(bf16[144,512]{1,0:T(8,128)(2,1)S(1)} %collective-permute-done.2.refs_1_.refs_0_), channel_id=1, source_target_pairs={{0,8},{4,12},{8,0},{12,4},{1,9},{5,13},{9,1},{13,5},{2,10},{6,14},... | collective-permute-start | bytes 442376 | tf_op jit(solution)/shard_map/ppermute | solution.py:25
  17.1 0.0 copy-start.3
  17.1 0.1 collective-permute-start.13
  17.2 0.5 %collective-permute-start.11 = (bf16[128,1024]{1,0:T(8,128)(2,1)S(1)}, bf16[128,1024]{1,0:T(8,128)(2,1)S(1)}, u32[]{:S(2)}, u32[]{:S(2)}) collective-permute-start(bf16[128,1024]{1,0:T(8,128)(2,1)S(1)} %collective-permute-done.refs_0_), channel_id=1, source_target_pairs={{0,4},{4,0},{8,12},{12,8},{1,5},{5,1},{9,13},{13,9},{2,6},{6,2},{1... | collective-permute-start | bytes 786440 | tf_op jit(solution)/shard_map/ppermute | solution.py:25
  17.7 3.6 %collective-permute-done.8.query_ref = bf16[128,1024]{1,0:T(8,128)(2,1)S(1)} collective-permute-done((bf16[128,1024]{1,0:T(8,128)(2,1)S(1)}, bf16[128,1024]{1,0:T(8,128)(2,1)S(1)}, u32[]{:S(2)}, u32[]{:S(2)}) %collective-permute-start.8) | collective-permute-done | bytes 262176 | tf_op jit(solution)/shard_map/ppermute | solution.py:25
  21.3 0.6 %copy-done.4 = s32[16]{0:T(128)S(1)} copy-done((s32[16]{0:T(128)S(1)}, s32[16]{0:T(128)}, u32[]{:S(2)}) %copy-start.4) | copy-done | bytes 88
  21.9 0.3 shard_map.65
  22.2 1.4 %collective-permute-done.7.refs_7_.refs_6_ = bf16[144,512]{1,0:T(8,128)(2,1)S(1)} collective-permute-done((bf16[144,512]{1,0:T(8,128)(2,1)S(1)}, bf16[144,512]{1,0:T(8,128)(2,1)S(1)}, u32[]{:S(2)}, u32[]{:S(2)}) %collective-permute-start.7) | collective-permute-done | bytes 147488 | tf_op jit(solution)/shard_map/ppermute | solution.py:25
  23.6 0.5 %collective-permute-start.10 = (bf16[144,512]{1,0:T(8,128)(2,1)S(1)}, bf16[144,512]{1,0:T(8,128)(2,1)S(1)}, u32[]{:S(2)}, u32[]{:S(2)}) collective-permute-start(bf16[144,512]{1,0:T(8,128)(2,1)S(1)} %collective-permute-done.7.refs_7_.refs_6_), channel_id=1, source_target_pairs={{0,4},{4,0},{8,12},{12,8},{1,5},{5,1},{9,13},{13,9},{2,6},{6,2},{1... | collective-permute-start | bytes 442376 | tf_op jit(solution)/shard_map/ppermute | solution.py:25
  24.1 1.2 %collective-permute-done.10.refs_9_.refs_8_ = bf16[144,512]{1,0:T(8,128)(2,1)S(1)} collective-permute-done((bf16[144,512]{1,0:T(8,128)(2,1)S(1)}, bf16[144,512]{1,0:T(8,128)(2,1)S(1)}, u32[]{:S(2)}, u32[]{:S(2)}) %collective-permute-start.10) | collective-permute-done | bytes 147488 | tf_op jit(solution)/shard_map/ppermute | solution.py:25
  25.4 0.5 %shard_map.68 = bf16[136,512]{1,0:T(8,128)(2,1)S(1)} custom-call(s32[4,16]{1,0:T(4,128)S(1)} %bitcast.4, s32[1,16]{1,0:T(1,128)S(1)} %bitcast.7, bf16[128,1024]{1,0:T(8,128)(2,1)S(1)} %collective-permute-done.8.query_ref, f32[128,512]{1,0:T(8,128)S(1)} %get-tuple-element.25.refs_0_, f32[128,128]{1,0:T(8,128)S(1)} %get-tuple-element.26.refs_1_, ...), custom_call_target="tpu_custom_call" | custom-call | flops 268435456 | bytes 4194304 | tf_op jit(solution)/shard_map/pallas_call | solution.py:315
  25.8 4.9 %collective-permute-start.14 = (bf16[136,512]{1,0:T(8,128)(2,1)S(1)}, bf16[136,512]{1,0:T(8,128)(2,1)S(1)}, u32[]{:S(2)}, u32[]{:S(2)}) collective-permute-start(bf16[136,512]{1,0:T(8,128)(2,1)S(1)} %shard_map.68), channel_id=1, source_target_pairs={{0,3},{1,2},{2,1},{3,0},{4,7},{5,6},{6,5},{7,4},{8,11},{9,10},{10,... | collective-permute-start | bytes 417800 | tf_op jit(solution)/shard_map/ppermute | solution.py:25
  30.7 0.9 %shard_map.67 = (f32[128,512]{1,0:T(8,128)S(1)}, f32[2,128,128]{2,1,0:T(8,128)S(1)}) custom-call(s32[4,16]{1,0:T(4,128)S(1)} %bitcast.5, s32[1,16]{1,0:T(1,128)S(1)} %bitcast.8, bf16[128,1024]{1,0:T(8,128)(2,1)S(1)} %copy-done.1, bf16[128,1024]{1,0:T(8,128)(2,1)S(1)} %collective-permute-done.refs_0_, ...), custom_call_target="tpu_custom_call" | custom-call | flops 268435456 | bytes 4194304 | tf_op jit(solution)/shard_map/pallas_call | solution.py:330
  31.6 2.7 %collective-permute-done.14.refs_0_ = bf16[136,512]{1,0:T(8,128)(2,1)S(1)} collective-permute-done((bf16[136,512]{1,0:T(8,128)(2,1)S(1)}, bf16[136,512]{1,0:T(8,128)(2,1)S(1)}, u32[]{:S(2)}, u32[]{:S(2)}) %collective-permute-start.14) | collective-permute-done | bytes 139296 | tf_op jit(solution)/shard_map/ppermute | solution.py:25
  34.3 0.8 %shard_map.69 = bf16[128,512]{1,0:T(8,128)(2,1)} custom-call(f32[128,512]{1,0:T(8,128)S(1)} %get-tuple-element.23.total_ref, f32[2,128,128]{2,1,0:T(8,128)S(1)} %get-tuple-element.24.stats_ref, bf16[136,512]{1,0:T(8,128)(2,1)S(1)} %collective-permute-done.14.refs_0_), custom_call_target="tpu_custom_call" | custom-call | tf_op jit(solution)/shard_map/pallas_call | solution.py:344
  (16 shorter events, 0.1 us)
Async XLA Ops:
  0.0 8.2 %copy-start.1 = (bf16[128,1024]{1,0:T(8,128)(2,1)S(1)}, bf16[128,1024]{1,0:T(8,128)(2,1)}, u32[]{:S(2)}) copy-start(bf16[128,1024]{1,0:T(8,128)(2,1)} %query_ref.1) | copy-start | bytes 786436
  0.0 4.6 %collective-permute-start.1 = (bf16[128,1024]{1,0:T(8,128)(2,1)}, bf16[128,1024]{1,0:T(8,128)(2,1)S(1)}, u32[]{:S(2)}, u32[]{:S(2)}) collective-permute-start(bf16[128,1024]{1,0:T(8,128)(2,1)} %refs_13_.1), channel_id=1, source_target_pairs={{0,4},{4,0},{8,12},{12,8},{1,5},{5,1},{9,13},{13,9},{2,6},{6,2},{1... | collective-permute-start | bytes 786440 | tf_op jit(solution)/shard_map/ppermute | solution.py:25
  0.5 10.6 %collective-permute-start = (bf16[128,1024]{1,0:T(8,128)(2,1)}, bf16[128,1024]{1,0:T(8,128)(2,1)S(1)}, u32[]{:S(2)}, u32[]{:S(2)}) collective-permute-start(bf16[128,1024]{1,0:T(8,128)(2,1)} %refs_13_.1), channel_id=1, source_target_pairs={{0,1},{1,0},{2,3},{3,2},{4,5},{5,4},{6,7},{7,6},{8,9},{9,8},{10,11... | collective-permute-start | bytes 786440 | tf_op jit(solution)/shard_map/ppermute | solution.py:25
  3.1 9.4 %collective-permute-start.3 = (bf16[128,1024]{1,0:T(8,128)(2,1)}, bf16[128,1024]{1,0:T(8,128)(2,1)S(1)}, u32[]{:S(2)}, u32[]{:S(2)}) collective-permute-start(bf16[128,1024]{1,0:T(8,128)(2,1)} %refs_13_.1), channel_id=1, source_target_pairs={{0,8},{4,12},{8,0},{12,4},{1,9},{5,13},{9,1},{13,5},{2,10},{6,14},... | collective-permute-start | bytes 786440 | tf_op jit(solution)/shard_map/ppermute | solution.py:25
  4.6 0.9 %copy-start.2 = (bf16[128,512]{1,0:T(8,128)(2,1)S(1)}, bf16[128,512]{1,0:T(8,128)(2,1)}, u32[]{:S(2)}) copy-start(bf16[128,512]{1,0:T(8,128)(2,1)} %values_ref) | copy-start | bytes 393220
  5.5 0.7 %copy-start.5 = (bf16[128]{0:T(256)(128)(2,1)S(1)}, bf16[128]{0:T(256)(128)(2,1)}, u32[]{:S(2)}) copy-start(bf16[128]{0:T(256)(128)(2,1)} %param.9) | copy-start | bytes 772
  6.3 15.0 %copy-start = (bf16[128,1024]{1,0:T(8,128)(2,1)S(1)}, bf16[128,1024]{1,0:T(8,128)(2,1)}, u32[]{:S(2)}) copy-start(bf16[128,1024]{1,0:T(8,128)(2,1)} %refs_13_.1) | copy-start | bytes 786436
  6.3 1.9 %collective-permute-start.5 = (bf16[144,512]{1,0:T(8,128)(2,1)S(1)}, bf16[144,512]{1,0:T(8,128)(2,1)S(1)}, u32[]{:S(2)}, u32[]{:S(2)}) collective-permute-start(bf16[144,512]{1,0:T(8,128)(2,1)S(1)} %shard_map.64.refs_5_.refs_14_), channel_id=1, source_target_pairs={{0,4},{4,0},{8,12},{12,8},{1,5},{5,1},{9,13},{13,9},{2,6},{6,2},{1... | collective-permute-start | bytes 442376 | tf_op jit(solution)/shard_map/ppermute | solution.py:25
  6.4 7.5 %collective-permute-start.2 = (bf16[144,512]{1,0:T(8,128)(2,1)S(1)}, bf16[144,512]{1,0:T(8,128)(2,1)S(1)}, u32[]{:S(2)}, u32[]{:S(2)}) collective-permute-start(bf16[144,512]{1,0:T(8,128)(2,1)S(1)} %shard_map.64.refs_5_.refs_14_), channel_id=1, source_target_pairs={{0,1},{1,0},{2,3},{3,2},{4,5},{5,4},{6,7},{7,6},{8,9},{9,8},{10,11... | collective-permute-start | bytes 442376 | tf_op jit(solution)/shard_map/ppermute | solution.py:25
  6.9 8.7 %collective-permute-start.4 = (bf16[144,512]{1,0:T(8,128)(2,1)S(1)}, bf16[144,512]{1,0:T(8,128)(2,1)S(1)}, u32[]{:S(2)}, u32[]{:S(2)}) collective-permute-start(bf16[144,512]{1,0:T(8,128)(2,1)S(1)} %shard_map.64.refs_5_.refs_14_), channel_id=1, source_target_pairs={{0,8},{4,12},{8,0},{12,4},{1,9},{5,13},{9,1},{13,5},{2,10},{6,14},... | collective-permute-start | bytes 442376 | tf_op jit(solution)/shard_map/ppermute | solution.py:25
  8.2 13.1 %collective-permute-start.8 = (bf16[128,1024]{1,0:T(8,128)(2,1)S(1)}, bf16[128,1024]{1,0:T(8,128)(2,1)S(1)}, u32[]{:S(2)}, u32[]{:S(2)}) collective-permute-start(bf16[128,1024]{1,0:T(8,128)(2,1)S(1)} %copy-done.1), channel_id=1, source_target_pairs={{0,3},{1,2},{2,1},{3,0},{4,7},{5,6},{6,5},{7,4},{8,11},{9,10},{10,... | collective-permute-start | bytes 786440 | tf_op jit(solution)/shard_map/ppermute | solution.py:25
  12.5 9.8 %collective-permute-start.6 = (bf16[128,1024]{1,0:T(8,128)(2,1)S(1)}, bf16[128,1024]{1,0:T(8,128)(2,1)S(1)}, u32[]{:S(2)}, u32[]{:S(2)}) collective-permute-start(bf16[128,1024]{1,0:T(8,128)(2,1)S(1)} %collective-permute-done.refs_0_), channel_id=1, source_target_pairs={{0,8},{4,12},{8,0},{12,4},{1,9},{5,13},{9,1},{13,5},{2,10},{6,14},... | collective-permute-start | bytes 786440 | tf_op jit(solution)/shard_map/ppermute | solution.py:25
  15.6 8.0 %collective-permute-start.7 = (bf16[144,512]{1,0:T(8,128)(2,1)S(1)}, bf16[144,512]{1,0:T(8,128)(2,1)S(1)}, u32[]{:S(2)}, u32[]{:S(2)}) collective-permute-start(bf16[144,512]{1,0:T(8,128)(2,1)S(1)} %collective-permute-done.2.refs_1_.refs_0_), channel_id=1, source_target_pairs={{0,8},{4,12},{8,0},{12,4},{1,9},{5,13},{9,1},{13,5},{2,10},{6,14},... | collective-permute-start | bytes 442376 | tf_op jit(solution)/shard_map/ppermute | solution.py:25
  17.1 4.2 %copy-start.3 = (s32[16,4]{0,1:T(4,128)S(1)}, s32[16,4]{0,1:T(4,128)}, u32[]{:S(2)}) copy-start(s32[16,4]{0,1:T(4,128)} %param.10) | copy-start | bytes 772
  17.1 7.0 %collective-permute-start.13 = (bf16[288,512]{1,0:T(8,128)(2,1)S(1)}, bf16[288,512]{1,0:T(8,128)(2,1)S(1)}, u32[]{:S(2)}, u32[]{:S(2)}) collective-permute-start(bf16[288,512]{1,0:T(8,128)(2,1)S(1)} %shard_map.66), channel_id=1, source_target_pairs={{0,4},{4,0},{8,12},{12,8},{1,5},{5,1},{9,13},{13,9},{2,6},{6,2},{1... | collective-permute-start | bytes 884744 | tf_op jit(solution)/shard_map/ppermute | solution.py:25
  17.2 6.9 %collective-permute-start.11 = (bf16[128,1024]{1,0:T(8,128)(2,1)S(1)}, bf16[128,1024]{1,0:T(8,128)(2,1)S(1)}, u32[]{:S(2)}, u32[]{:S(2)}) collective-permute-start(bf16[128,1024]{1,0:T(8,128)(2,1)S(1)} %collective-permute-done.refs_0_), channel_id=1, source_target_pairs={{0,4},{4,0},{8,12},{12,8},{1,5},{5,1},{9,13},{13,9},{2,6},{6,2},{1... | collective-permute-start | bytes 786440 | tf_op jit(solution)/shard_map/ppermute | solution.py:25
  21.3 2.8 %collective-permute-start.12 = (bf16[128,1024]{1,0:T(8,128)(2,1)S(1)}, bf16[128,1024]{1,0:T(8,128)(2,1)S(1)}, u32[]{:S(2)}, u32[]{:S(2)}) collective-permute-start(bf16[128,1024]{1,0:T(8,128)(2,1)S(1)} %collective-permute-done.3.refs_2_), channel_id=1, source_target_pairs={{0,4},{4,0},{8,12},{12,8},{1,5},{5,1},{9,13},{13,9},{2,6},{6,2},{1... | collective-permute-start | bytes 786440 | tf_op jit(solution)/shard_map/ppermute | solution.py:25
  21.3 0.7 %copy-start.4 = (s32[16]{0:T(128)S(1)}, s32[16]{0:T(128)}, u32[]{:S(2)}) copy-start(s32[16]{0:T(128)} %param.11) | copy-start | bytes 196
  23.6 1.8 %collective-permute-start.9 = (bf16[128,1024]{1,0:T(8,128)(2,1)S(1)}, bf16[128,1024]{1,0:T(8,128)(2,1)S(1)}, u32[]{:S(2)}, u32[]{:S(2)}) collective-permute-start(bf16[128,1024]{1,0:T(8,128)(2,1)S(1)} %collective-permute-done.6.refs_6_.refs_5_), channel_id=1, source_target_pairs={{0,4},{4,0},{8,12},{12,8},{1,5},{5,1},{9,13},{13,9},{2,6},{6,2},{1... | collective-permute-start | bytes 786440 | tf_op jit(solution)/shard_map/ppermute | solution.py:25
  23.6 1.7 %collective-permute-start.10 = (bf16[144,512]{1,0:T(8,128)(2,1)S(1)}, bf16[144,512]{1,0:T(8,128)(2,1)S(1)}, u32[]{:S(2)}, u32[]{:S(2)}) collective-permute-start(bf16[144,512]{1,0:T(8,128)(2,1)S(1)} %collective-permute-done.7.refs_7_.refs_6_), channel_id=1, source_target_pairs={{0,4},{4,0},{8,12},{12,8},{1,5},{5,1},{9,13},{13,9},{2,6},{6,2},{1... | collective-permute-start | bytes 442376 | tf_op jit(solution)/shard_map/ppermute | solution.py:25
  25.8 8.4 %collective-permute-start.14 = (bf16[136,512]{1,0:T(8,128)(2,1)S(1)}, bf16[136,512]{1,0:T(8,128)(2,1)S(1)}, u32[]{:S(2)}, u32[]{:S(2)}) collective-permute-start(bf16[136,512]{1,0:T(8,128)(2,1)S(1)} %shard_map.68), channel_id=1, source_target_pairs={{0,3},{1,2},{2,1},{3,0},{4,7},{5,6},{6,5},{7,4},{8,11},{9,10},{10,... | collective-permute-start | bytes 417800 | tf_op jit(solution)/shard_map/ppermute | solution.py:25

commit v18 on v15

--- a/solution.py
+++ b/solution.py
@@ -63,6 +63,11 @@
         product = lax.dot_general(
             query_ref[...], self.keys_ref[...], (((1,), (1,)), ((), ())), preferred_element_type=jnp.float32
         )
+        scale = self.values_ref[self.row + TILE : self.row + TILE + EXTRA, 0:TILE]
+        return product * (scale.astype(jnp.float32)[0:1] * inverse_root)
+
+    def turned_scores(self, turned_ref, inverse_root):
+        product = jnp.transpose(jnp.dot(self.keys_ref[...], turned_ref[...], preferred_element_type=jnp.float32))
         scale = self.values_ref[self.row + TILE : self.row + TILE + EXTRA, 0:TILE]
         return product * (scale.astype(jnp.float32)[0:1] * inverse_root)
 
@@ -110,8 +115,7 @@
     panel = lib_index * qry_count + lax.bitwise_xor(qry_index, panel_mask)
     first = pick(lists_ref, 0, panel)
     count = pick(counts_ref, 0, panel)
-    width = query_ref.shape[1]
-    inverse_root = 1.0 / math.sqrt(width)
+    inverse_root = 1.0 / math.sqrt(pieces[0].keys_ref.shape[1])
 
     def active(lib_mask, qry_mask):
         block = lax.bitwise_xor(lib_index, lib_mask) * qry_count + lax.bitwise_xor(qry_index, qry_mask)
@@ -125,7 +129,8 @@
 
         @pl.when(flag)
         def _(at=at, piece=piece):
-            score_ref[at] = piece.scores(query_ref, inverse_root)
+            scores = piece.scores if before is None else piece.turned_scores
+            score_ref[at] = scores(query_ref, inverse_root)
 
     largest = score_ref[0]
     for at in range(1, len(flags)):
@@ -161,16 +166,17 @@
 
 def early_kernel(places, panel_mask, lists_ref, counts_ref, query_ref, *refs):
     pieces, refs = read_pieces(places, refs, own=True)
-    total_ref, mass_ref, max_ref, score_ref = refs
+    turned_ref, total_ref, mass_ref, max_ref, score_ref = refs
     row_max = attend(pieces, panel_mask, lists_ref, counts_ref, query_ref, score_ref, total_ref, mass_ref)
     max_ref[...] = jnp.broadcast_to(row_max, max_ref.shape)
-
-
-def late_kernel(places, bundled, panel_mask, lists_ref, counts_ref, query_ref, *refs):
+    turned_ref[...] = jnp.transpose(query_ref[...])
+
+
+def late_kernel(places, bundled, panel_mask, lists_ref, counts_ref, turned_ref, *refs):
     before, refs = refs[:3], refs[3:]
     pieces, refs = read_pieces(places, refs, bundled)
     packed_ref, score_ref, total_ref, mass_ref = refs
-    row_max = attend(pieces, panel_mask, lists_ref, counts_ref, query_ref, score_ref, total_ref, mass_ref, before)
+    row_max = attend(pieces, panel_mask, lists_ref, counts_ref, turned_ref, score_ref, total_ref, mass_ref, before)
     row_sum = jnp.sum(mass_ref[...], axis=1, keepdims=True)
     value_width = total_ref.shape[1]
     inverse = 1.0 / jnp.where(row_sum > 0.0, row_sum, 1.0)
@@ -287,9 +293,9 @@
     for mask, visiting in visitors:
         state = pl.pallas_call(
             functools.partial(early_kernel, places_of(early), mask),
-            out_shape=(total_shape, line_shape, line_shape),
+            out_shape=(jax.ShapeDtypeStruct(queries.shape[::-1], queries.dtype), total_shape, line_shape, line_shape),
             in_specs=[VMEM, VMEM] + [VMEM] * (1 + len(early_arrays)) + own_specs,
-            out_specs=(VMEM,) * 3,
+            out_specs=(VMEM,) * 4,
             scratch_shapes=[pltpu.VMEM((len(early) + 1, TILE, TILE), jnp.float32)] + own_scratch,
             compiler_params=attend_params,
             cost_estimate=cost,
@@ -307,10 +313,10 @@
     )(*early_values)
     bundled_arrays = [swap(piece[1], "lib", 1) for piece in early] + [swap(bundle, "lib", 1)]
     late = [((1, 0), partner_keys, partner_values)] + relayed
-    late += cross_cores(relayed, [state[2] for state in states])
+    late += cross_cores(relayed, [state[3] for state in states])
     late_arrays = arrays_of(late) + bundled_arrays
     returned = []
-    for (mask, visiting), state in zip(visitors, states):
+    for (mask, _), state in zip(visitors, states):
         packed = pl.pallas_call(
             functools.partial(late_kernel, places_of(late), bundled, mask),
             out_shape=jax.ShapeDtypeStruct((TILE + EXTRA, value_width), jnp.bfloat16),
@@ -323,7 +329,7 @@
             ],
             compiler_params=attend_params,
             cost_estimate=cost,
-        )(window_lists, window_counts, visiting, *state, *late_arrays)
+        )(window_lists, window_counts, *state, *late_arrays)
         returned.append(swap(packed, "qry", mask))
 
     total, stats = pl.pallas_call(

time: 35.5 us -> 36 us (1.014)
  waiting for transfers between devices: 12.8 us -> 11.2 us
  starting transfers between devices: 17.2 us -> 18.3 us
  Pallas kernels: 3.1 us -> 4.04 us
    ppermute x15, waiting for transfers between devices: 12.8 us -> 11.2 us  [swap(): return lax.ppermute(value, axis, [(i, i ^ mask) for i in range(length)])]
    ppermute x15, starting transfers between devices: 17.2 us -> 18.3 us  [swap(): return lax.ppermute(value, axis, [(i, i ^ mask) for i in range(length)])]
    pallas_call x1, Pallas kernels: 0.28 us -> 1.27 us  [body(): pl.pallas_call(functools.partial(early_kernel, places_of(early), mask), o...]
    pallas_call x1, Pallas kernels: 0.97 us -> 0.48 us  [body(): pl.pallas_call(functools.partial(late_kernel, places_of(late), bundled, m...]
    pallas_call x1, Pallas kernels: 0.86 us -> 1.3 us  [body(): pl.pallas_call(functools.partial(home_kernel, places_of(early + late), bu...]
  transfers between devices with their start and end apart: 15 -> 15, of which waited for: 6 -> 6; matrix products, arithmetic and copies ran while one was open for 0% -> 0% of each run, Pallas kernels for 4% -> 8%
where the time goes in v18:
time: 36 us; the launch traced here: 35.8 us
  starting transfers between devices  18.3 us (51%)
  waiting for transfers between devices  11.2 us (31%)
  Pallas kernels  4.04 us (11%)
  local copies, waits for them, and re-layouts  2.22 us (6%)
    ppermute x15, starting transfers between devices, swap(): return lax.ppermute(value, axis, [(i, i ^ mask) for i in range(length)])  18.3 us
    ppermute x15, waiting for transfers between devices, swap(): return lax.ppermute(value, axis, [(i, i ^ mask) for i in range(length)])  11.2 us
    unnamed x12, local copies, waits for them, and re-layouts  2.22 us
    pallas_call x1, Pallas kernels, body(): pl.pallas_call(functools.partial(home_kernel, places_of(early + late), bu...  1.3 us
    pallas_call x1, Pallas kernels, body(): pl.pallas_call(functools.partial(early_kernel, places_of(early), mask), o...  1.27 us
    pallas_call x1, Pallas kernels, body(): pl.pallas_call(merge_kernel, out_shape=jax.ShapeDtypeStruct((TILE, value_...  0.81 us
  transfers between devices with their start and end apart: 15, of which 6 were waited for; matrix products, arithmetic and copies ran while one was open for 0% of the time, Pallas kernels for 8%

profile of v18, /device:TPU:0, one launch (start us, length us, event | category | flops | bytes accessed | tf_op | source)
XLA Modules:
  0.0 35.8 jit_solution(17526733156199745867)
XLA Ops:
  0.0 0.5 %collective-permute-start.1 = (bf16[128,1024]{1,0:T(8,128)(2,1)}, bf16[128,1024]{1,0:T(8,128)(2,1)S(1)}, u32[]{:S(2)}, u32[]{:S(2)}) collective-permute-start(bf16[128,1024]{1,0:T(8,128)(2,1)} %refs_13_.1), channel_id=1, source_target_pairs={{0,4},{4,0},{8,12},{12,8},{1,5},{5,1},{9,13},{13,9},{2,6},{6,2},{1... | collective-permute-start | bytes 786440 | tf_op jit(solution)/shard_map/ppermute | solution.py:24
  0.5 2.6 %collective-permute-start = (bf16[128,1024]{1,0:T(8,128)(2,1)}, bf16[128,1024]{1,0:T(8,128)(2,1)S(1)}, u32[]{:S(2)}, u32[]{:S(2)}) collective-permute-start(bf16[128,1024]{1,0:T(8,128)(2,1)} %refs_13_.1), channel_id=1, source_target_pairs={{0,1},{1,0},{2,3},{3,2},{4,5},{5,4},{6,7},{7,6},{8,9},{9,8},{10,11... | collective-permute-start | bytes 786440 | tf_op jit(solution)/shard_map/ppermute | solution.py:24
  3.1 1.5 %collective-permute-start.3 = (bf16[128,1024]{1,0:T(8,128)(2,1)}, bf16[128,1024]{1,0:T(8,128)(2,1)S(1)}, u32[]{:S(2)}, u32[]{:S(2)}) collective-permute-start(bf16[128,1024]{1,0:T(8,128)(2,1)} %refs_13_.1), channel_id=1, source_target_pairs={{0,8},{4,12},{8,0},{12,4},{1,9},{5,13},{9,1},{13,5},{2,10},{6,14},... | collective-permute-start | bytes 786440 | tf_op jit(solution)/shard_map/ppermute | solution.py:24
  4.6 0.9 %copy-done.2 = bf16[128,512]{1,0:T(8,128)(2,1)S(1)} copy-done((bf16[128,512]{1,0:T(8,128)(2,1)S(1)}, bf16[128,512]{1,0:T(8,128)(2,1)}, u32[]{:S(2)}) %copy-start.2) | copy-done | bytes 131096
  5.5 0.7 %copy-done.5 = bf16[128]{0:T(256)(128)(2,1)S(1)} copy-done((bf16[128]{0:T(256)(128)(2,1)S(1)}, bf16[128]{0:T(256)(128)(2,1)}, u32[]{:S(2)}) %copy-start.5) | copy-done | bytes 280
  6.1 0.2 shard_map.64.refs_5_.refs_14_
  6.3 0.0 copy-start
  6.3 0.1 collective-permute-start.5
  6.4 0.5 %collective-permute-start.2 = (bf16[144,512]{1,0:T(8,128)(2,1)S(1)}, bf16[144,512]{1,0:T(8,128)(2,1)S(1)}, u32[]{:S(2)}, u32[]{:S(2)}) collective-permute-start(bf16[144,512]{1,0:T(8,128)(2,1)S(1)} %shard_map.64.refs_5_.refs_14_), channel_id=1, source_target_pairs={{0,1},{1,0},{2,3},{3,2},{4,5},{5,4},{6,7},{7,6},{8,9},{9,8},{10,11... | collective-permute-start | bytes 442376 | tf_op jit(solution)/shard_map/ppermute | solution.py:24
  6.9 1.3 %collective-permute-start.4 = (bf16[144,512]{1,0:T(8,128)(2,1)S(1)}, bf16[144,512]{1,0:T(8,128)(2,1)S(1)}, u32[]{:S(2)}, u32[]{:S(2)}) collective-permute-start(bf16[144,512]{1,0:T(8,128)(2,1)S(1)} %shard_map.64.refs_5_.refs_14_), channel_id=1, source_target_pairs={{0,8},{4,12},{8,0},{12,4},{1,9},{5,13},{9,1},{13,5},{2,10},{6,14},... | collective-permute-start | bytes 442376 | tf_op jit(solution)/shard_map/ppermute | solution.py:24
  8.2 0.0 collective-permute-done.5.refs_5_.refs_4_
  8.2 2.8 %collective-permute-start.8 = (bf16[128,1024]{1,0:T(8,128)(2,1)S(1)}, bf16[128,1024]{1,0:T(8,128)(2,1)S(1)}, u32[]{:S(2)}, u32[]{:S(2)}) collective-permute-start(bf16[128,1024]{1,0:T(8,128)(2,1)S(1)} %copy-done.1), channel_id=1, source_target_pairs={{0,3},{1,2},{2,1},{3,0},{4,7},{5,6},{6,5},{7,4},{8,11},{9,10},{10,... | collective-permute-start | bytes 786440 | tf_op jit(solution)/shard_map/ppermute | solution.py:24
  11.1 0.0 collective-permute-done.refs_0_
  11.1 1.4 %collective-permute-done.3.refs_2_ = bf16[128,1024]{1,0:T(8,128)(2,1)S(1)} collective-permute-done((bf16[128,1024]{1,0:T(8,128)(2,1)}, bf16[128,1024]{1,0:T(8,128)(2,1)S(1)}, u32[]{:S(2)}, u32[]{:S(2)}) %collective-permute-start.3) | collective-permute-done | bytes 262176 | tf_op jit(solution)/shard_map/ppermute | solution.py:24
  12.5 1.5 %collective-permute-start.6 = (bf16[128,1024]{1,0:T(8,128)(2,1)S(1)}, bf16[128,1024]{1,0:T(8,128)(2,1)S(1)}, u32[]{:S(2)}, u32[]{:S(2)}) collective-permute-start(bf16[128,1024]{1,0:T(8,128)(2,1)S(1)} %collective-permute-done.refs_0_), channel_id=1, source_target_pairs={{0,8},{4,12},{8,0},{12,4},{1,9},{5,13},{9,1},{13,5},{2,10},{6,14},... | collective-permute-start | bytes 786440 | tf_op jit(solution)/shard_map/ppermute | solution.py:24
  13.9 0.0 collective-permute-done.2.refs_1_.refs_0_
  13.9 1.7 %collective-permute-done.4.refs_3_.refs_1_ = bf16[144,512]{1,0:T(8,128)(2,1)S(1)} collective-permute-done((bf16[144,512]{1,0:T(8,128)(2,1)S(1)}, bf16[144,512]{1,0:T(8,128)(2,1)S(1)}, u32[]{:S(2)}, u32[]{:S(2)}) %collective-permute-start.4) | collective-permute-done | bytes 147488 | tf_op jit(solution)/shard_map/ppermute | solution.py:24
  15.6 1.5 %collective-permute-start.7 = (bf16[144,512]{1,0:T(8,128)(2,1)S(1)}, bf16[144,512]{1,0:T(8,128)(2,1)S(1)}, u32[]{:S(2)}, u32[]{:S(2)}) collective-permute-start(bf16[144,512]{1,0:T(8,128)(2,1)S(1)} %collective-permute-done.2.refs_1_.refs_0_), channel_id=1, source_target_pairs={{0,8},{4,12},{8,0},{12,4},{1,9},{5,13},{9,1},{13,5},{2,10},{6,14},... | collective-permute-start | bytes 442376 | tf_op jit(solution)/shard_map/ppermute | solution.py:24
  17.1 0.0 copy-start.3
  17.1 0.1 collective-permute-start.13
  17.2 0.5 %collective-permute-start.11 = (bf16[128,1024]{1,0:T(8,128)(2,1)S(1)}, bf16[128,1024]{1,0:T(8,128)(2,1)S(1)}, u32[]{:S(2)}, u32[]{:S(2)}) collective-permute-start(bf16[128,1024]{1,0:T(8,128)(2,1)S(1)} %collective-permute-done.refs_0_), channel_id=1, source_target_pairs={{0,4},{4,0},{8,12},{12,8},{1,5},{5,1},{9,13},{13,9},{2,6},{6,2},{1... | collective-permute-start | bytes 786440 | tf_op jit(solution)/shard_map/ppermute | solution.py:24
  17.7 3.6 %collective-permute-done.8.query_ref = bf16[128,1024]{1,0:T(8,128)(2,1)S(1)} collective-permute-done((bf16[128,1024]{1,0:T(8,128)(2,1)S(1)}, bf16[128,1024]{1,0:T(8,128)(2,1)S(1)}, u32[]{:S(2)}, u32[]{:S(2)}) %collective-permute-start.8) | collective-permute-done | bytes 262176 | tf_op jit(solution)/shard_map/ppermute | solution.py:24
  21.3 0.6 %copy-done.4 = s32[16]{0:T(128)S(1)} copy-done((s32[16]{0:T(128)S(1)}, s32[16]{0:T(128)}, u32[]{:S(2)}) %copy-start.4) | copy-done | bytes 88
  21.9 1.3 %shard_map.65 = (bf16[1024,128]{1,0:T(8,128)(2,1)S(1)}, f32[128,512]{1,0:T(8,128)S(1)}, f32[128,128]{1,0:T(8,128)S(1)}, f32[128,128]{1,0:T(8,128)S(1)}) custom-call(s32[4,16]{1,0:T(4,128)S(1)} %bitcast.3, s32[1,16]{1,0:T(1,128)S(1)} %bitcast.6, bf16[128,1024]{1,0:T(8,128)(2,1)S(1)} %collective-permute-done.8.query_ref, ...), custom_call_target="tpu_custom_call" | custom-call | flops 268435456 | bytes 4194304 | tf_op jit(solution)/shard_map/pallas_call | solution.py:294
  23.2 0.4 %collective-permute-done.7.refs_7_.refs_6_ = bf16[144,512]{1,0:T(8,128)(2,1)S(1)} collective-permute-done((bf16[144,512]{1,0:T(8,128)(2,1)S(1)}, bf16[144,512]{1,0:T(8,128)(2,1)S(1)}, u32[]{:S(2)}, u32[]{:S(2)}) %collective-permute-start.7) | collective-permute-done | bytes 147488 | tf_op jit(solution)/shard_map/ppermute | solution.py:24
  23.6 0.5 %collective-permute-start.10 = (bf16[144,512]{1,0:T(8,128)(2,1)S(1)}, bf16[144,512]{1,0:T(8,128)(2,1)S(1)}, u32[]{:S(2)}, u32[]{:S(2)}) collective-permute-start(bf16[144,512]{1,0:T(8,128)(2,1)S(1)} %collective-permute-done.7.refs_7_.refs_6_), channel_id=1, source_target_pairs={{0,4},{4,0},{8,12},{12,8},{1,5},{5,1},{9,13},{13,9},{2,6},{6,2},{1... | collective-permute-start | bytes 442376 | tf_op jit(solution)/shard_map/ppermute | solution.py:24
  24.1 1.2 %collective-permute-done.10.refs_9_.refs_8_ = bf16[144,512]{1,0:T(8,128)(2,1)S(1)} collective-permute-done((bf16[144,512]{1,0:T(8,128)(2,1)S(1)}, bf16[144,512]{1,0:T(8,128)(2,1)S(1)}, u32[]{:S(2)}, u32[]{:S(2)}) %collective-permute-start.10) | collective-permute-done | bytes 147488 | tf_op jit(solution)/shard_map/ppermute | solution.py:24
  25.4 0.5 %shard_map.68 = bf16[144,512]{1,0:T(8,128)(2,1)S(1)} custom-call(s32[4,16]{1,0:T(4,128)S(1)} %bitcast.4, s32[1,16]{1,0:T(1,128)S(1)} %bitcast.7, bf16[1024,128]{1,0:T(8,128)(2,1)S(1)} %get-tuple-element.26.turned_ref, f32[128,512]{1,0:T(8,128)S(1)} %get-tuple-element.27.refs_0_, f32[128,128]{1,0:T(8,128)S(1)} %get-tuple-element.28.refs_1_, ...), custom_call_target="tpu_custom_call" | custom-call | flops 268435456 | bytes 4194304 | tf_op jit(solution)/shard_map/pallas_call | solution.py:320
  25.9 4.9 %collective-permute-start.14 = (bf16[144,512]{1,0:T(8,128)(2,1)S(1)}, bf16[144,512]{1,0:T(8,128)(2,1)S(1)}, u32[]{:S(2)}, u32[]{:S(2)}) collective-permute-start(bf16[144,512]{1,0:T(8,128)(2,1)S(1)} %shard_map.68), channel_id=1, source_target_pairs={{0,3},{1,2},{2,1},{3,0},{4,7},{5,6},{6,5},{7,4},{8,11},{9,10},{10,... | collective-permute-start | bytes 442376 | tf_op jit(solution)/shard_map/ppermute | solution.py:24
  30.8 1.3 %shard_map.67 = (f32[128,512]{1,0:T(8,128)S(1)}, f32[2,128,128]{2,1,0:T(8,128)S(1)}) custom-call(s32[4,16]{1,0:T(4,128)S(1)} %bitcast.5, s32[1,16]{1,0:T(1,128)S(1)} %bitcast.8, bf16[128,1024]{1,0:T(8,128)(2,1)S(1)} %copy-done.1, bf16[128,1024]{1,0:T(8,128)(2,1)S(1)} %collective-permute-done.refs_0_, ...), custom_call_target="tpu_custom_call" | custom-call | flops 268435456 | bytes 4194304 | tf_op jit(solution)/shard_map/pallas_call | solution.py:335
  32.1 2.9 %collective-permute-done.14.refs_0_ = bf16[144,512]{1,0:T(8,128)(2,1)S(1)} collective-permute-done((bf16[144,512]{1,0:T(8,128)(2,1)S(1)}, bf16[144,512]{1,0:T(8,128)(2,1)S(1)}, u32[]{:S(2)}, u32[]{:S(2)}) %collective-permute-start.14) | collective-permute-done | bytes 147488 | tf_op jit(solution)/shard_map/ppermute | solution.py:24
  35.0 0.8 %shard_map.69 = bf16[128,512]{1,0:T(8,128)(2,1)} custom-call(f32[128,512]{1,0:T(8,128)S(1)} %get-tuple-element.24.total_ref, f32[2,128,128]{2,1,0:T(8,128)S(1)} %get-tuple-element.25.stats_ref, bf16[144,512]{1,0:T(8,128)(2,1)S(1)} %collective-permute-done.14.refs_0_), custom_call_target="tpu_custom_call" | custom-call | tf_op jit(solution)/shard_map/pallas_call | solution.py:349
  (16 shorter events, 0.1 us)
Async XLA Ops:
  0.0 8.2 %copy-start.1 = (bf16[128,1024]{1,0:T(8,128)(2,1)S(1)}, bf16[128,1024]{1,0:T(8,128)(2,1)}, u32[]{:S(2)}) copy-start(bf16[128,1024]{1,0:T(8,128)(2,1)} %query_ref.1) | copy-start | bytes 786436
  0.0 4.6 %collective-permute-start.1 = (bf16[128,1024]{1,0:T(8,128)(2,1)}, bf16[128,1024]{1,0:T(8,128)(2,1)S(1)}, u32[]{:S(2)}, u32[]{:S(2)}) collective-permute-start(bf16[128,1024]{1,0:T(8,128)(2,1)} %refs_13_.1), channel_id=1, source_target_pairs={{0,4},{4,0},{8,12},{12,8},{1,5},{5,1},{9,13},{13,9},{2,6},{6,2},{1... | collective-permute-start | bytes 786440 | tf_op jit(solution)/shard_map/ppermute | solution.py:24
  0.5 10.6 %collective-permute-start = (bf16[128,1024]{1,0:T(8,128)(2,1)}, bf16[128,1024]{1,0:T(8,128)(2,1)S(1)}, u32[]{:S(2)}, u32[]{:S(2)}) collective-permute-start(bf16[128,1024]{1,0:T(8,128)(2,1)} %refs_13_.1), channel_id=1, source_target_pairs={{0,1},{1,0},{2,3},{3,2},{4,5},{5,4},{6,7},{7,6},{8,9},{9,8},{10,11... | collective-permute-start | bytes 786440 | tf_op jit(solution)/shard_map/ppermute | solution.py:24
  3.1 9.4 %collective-permute-start.3 = (bf16[128,1024]{1,0:T(8,128)(2,1)}, bf16[128,1024]{1,0:T(8,128)(2,1)S(1)}, u32[]{:S(2)}, u32[]{:S(2)}) collective-permute-start(bf16[128,1024]{1,0:T(8,128)(2,1)} %refs_13_.1), channel_id=1, source_target_pairs={{0,8},{4,12},{8,0},{12,4},{1,9},{5,13},{9,1},{13,5},{2,10},{6,14},... | collective-permute-start | bytes 786440 | tf_op jit(solution)/shard_map/ppermute | solution.py:24
  4.6 0.9 %copy-start.2 = (bf16[128,512]{1,0:T(8,128)(2,1)S(1)}, bf16[128,512]{1,0:T(8,128)(2,1)}, u32[]{:S(2)}) copy-start(bf16[128,512]{1,0:T(8,128)(2,1)} %values_ref) | copy-start | bytes 393220
  5.5 0.7 %copy-start.5 = (bf16[128]{0:T(256)(128)(2,1)S(1)}, bf16[128]{0:T(256)(128)(2,1)}, u32[]{:S(2)}) copy-start(bf16[128]{0:T(256)(128)(2,1)} %param.9) | copy-start | bytes 772
  6.3 15.0 %copy-start = (bf16[128,1024]{1,0:T(8,128)(2,1)S(1)}, bf16[128,1024]{1,0:T(8,128)(2,1)}, u32[]{:S(2)}) copy-start(bf16[128,1024]{1,0:T(8,128)(2,1)} %refs_13_.1) | copy-start | bytes 786436
  6.3 1.9 %collective-permute-start.5 = (bf16[144,512]{1,0:T(8,128)(2,1)S(1)}, bf16[144,512]{1,0:T(8,128)(2,1)S(1)}, u32[]{:S(2)}, u32[]{:S(2)}) collective-permute-start(bf16[144,512]{1,0:T(8,128)(2,1)S(1)} %shard_map.64.refs_5_.refs_14_), channel_id=1, source_target_pairs={{0,4},{4,0},{8,12},{12,8},{1,5},{5,1},{9,13},{13,9},{2,6},{6,2},{1... | collective-permute-start | bytes 442376 | tf_op jit(solution)/shard_map/ppermute | solution.py:24
  6.4 7.5 %collective-permute-start.2 = (bf16[144,512]{1,0:T(8,128)(2,1)S(1)}, bf16[144,512]{1,0:T(8,128)(2,1)S(1)}, u32[]{:S(2)}, u32[]{:S(2)}) collective-permute-start(bf16[144,512]{1,0:T(8,128)(2,1)S(1)} %shard_map.64.refs_5_.refs_14_), channel_id=1, source_target_pairs={{0,1},{1,0},{2,3},{3,2},{4,5},{5,4},{6,7},{7,6},{8,9},{9,8},{10,11... | collective-permute-start | bytes 442376 | tf_op jit(solution)/shard_map/ppermute | solution.py:24
  6.9 8.7 %collective-permute-start.4 = (bf16[144,512]{1,0:T(8,128)(2,1)S(1)}, bf16[144,512]{1,0:T(8,128)(2,1)S(1)}, u32[]{:S(2)}, u32[]{:S(2)}) collective-permute-start(bf16[144,512]{1,0:T(8,128)(2,1)S(1)} %shard_map.64.refs_5_.refs_14_), channel_id=1, source_target_pairs={{0,8},{4,12},{8,0},{12,4},{1,9},{5,13},{9,1},{13,5},{2,10},{6,14},... | collective-permute-start | bytes 442376 | tf_op jit(solution)/shard_map/ppermute | solution.py:24
  8.2 13.1 %collective-permute-start.8 = (bf16[128,1024]{1,0:T(8,128)(2,1)S(1)}, bf16[128,1024]{1,0:T(8,128)(2,1)S(1)}, u32[]{:S(2)}, u32[]{:S(2)}) collective-permute-start(bf16[128,1024]{1,0:T(8,128)(2,1)S(1)} %copy-done.1), channel_id=1, source_target_pairs={{0,3},{1,2},{2,1},{3,0},{4,7},{5,6},{6,5},{7,4},{8,11},{9,10},{10,... | collective-permute-start | bytes 786440 | tf_op jit(solution)/shard_map/ppermute | solution.py:24
  12.5 10.8 %collective-permute-start.6 = (bf16[128,1024]{1,0:T(8,128)(2,1)S(1)}, bf16[128,1024]{1,0:T(8,128)(2,1)S(1)}, u32[]{:S(2)}, u32[]{:S(2)}) collective-permute-start(bf16[128,1024]{1,0:T(8,128)(2,1)S(1)} %collective-permute-done.refs_0_), channel_id=1, source_target_pairs={{0,8},{4,12},{8,0},{12,4},{1,9},{5,13},{9,1},{13,5},{2,10},{6,14},... | collective-permute-start | bytes 786440 | tf_op jit(solution)/shard_map/ppermute | solution.py:24
  15.6 8.0 %collective-permute-start.7 = (bf16[144,512]{1,0:T(8,128)(2,1)S(1)}, bf16[144,512]{1,0:T(8,128)(2,1)S(1)}, u32[]{:S(2)}, u32[]{:S(2)}) collective-permute-start(bf16[144,512]{1,0:T(8,128)(2,1)S(1)} %collective-permute-done.2.refs_1_.refs_0_), channel_id=1, source_target_pairs={{0,8},{4,12},{8,0},{12,4},{1,9},{5,13},{9,1},{13,5},{2,10},{6,14},... | collective-permute-start | bytes 442376 | tf_op jit(solution)/shard_map/ppermute | solution.py:24
  17.1 4.2 %copy-start.3 = (s32[16,4]{0,1:T(4,128)S(1)}, s32[16,4]{0,1:T(4,128)}, u32[]{:S(2)}) copy-start(s32[16,4]{0,1:T(4,128)} %param.10) | copy-start | bytes 772
  17.1 7.0 %collective-permute-start.13 = (bf16[288,512]{1,0:T(8,128)(2,1)S(1)}, bf16[288,512]{1,0:T(8,128)(2,1)S(1)}, u32[]{:S(2)}, u32[]{:S(2)}) collective-permute-start(bf16[288,512]{1,0:T(8,128)(2,1)S(1)} %shard_map.66), channel_id=1, source_target_pairs={{0,4},{4,0},{8,12},{12,8},{1,5},{5,1},{9,13},{13,9},{2,6},{6,2},{1... | collective-permute-start | bytes 884744 | tf_op jit(solution)/shard_map/ppermute | solution.py:24
  17.2 6.9 %collective-permute-start.11 = (bf16[128,1024]{1,0:T(8,128)(2,1)S(1)}, bf16[128,1024]{1,0:T(8,128)(2,1)S(1)}, u32[]{:S(2)}, u32[]{:S(2)}) collective-permute-start(bf16[128,1024]{1,0:T(8,128)(2,1)S(1)} %collective-permute-done.refs_0_), channel_id=1, source_target_pairs={{0,4},{4,0},{8,12},{12,8},{1,5},{5,1},{9,13},{13,9},{2,6},{6,2},{1... | collective-permute-start | bytes 786440 | tf_op jit(solution)/shard_map/ppermute | solution.py:24
  21.3 2.8 %collective-permute-start.12 = (bf16[128,1024]{1,0:T(8,128)(2,1)S(1)}, bf16[128,1024]{1,0:T(8,128)(2,1)S(1)}, u32[]{:S(2)}, u32[]{:S(2)}) collective-permute-start(bf16[128,1024]{1,0:T(8,128)(2,1)S(1)} %collective-permute-done.3.refs_2_), channel_id=1, source_target_pairs={{0,4},{4,0},{8,12},{12,8},{1,5},{5,1},{9,13},{13,9},{2,6},{6,2},{1... | collective-permute-start | bytes 786440 | tf_op jit(solution)/shard_map/ppermute | solution.py:24
  21.3 0.7 %copy-start.4 = (s32[16]{0:T(128)S(1)}, s32[16]{0:T(128)}, u32[]{:S(2)}) copy-start(s32[16]{0:T(128)} %param.11) | copy-start | bytes 196
  23.6 1.8 %collective-permute-start.9 = (bf16[128,1024]{1,0:T(8,128)(2,1)S(1)}, bf16[128,1024]{1,0:T(8,128)(2,1)S(1)}, u32[]{:S(2)}, u32[]{:S(2)}) collective-permute-start(bf16[128,1024]{1,0:T(8,128)(2,1)S(1)} %collective-permute-done.6.refs_6_.refs_5_), channel_id=1, source_target_pairs={{0,4},{4,0},{8,12},{12,8},{1,5},{5,1},{9,13},{13,9},{2,6},{6,2},{1... | collective-permute-start | bytes 786440 | tf_op jit(solution)/shard_map/ppermute | solution.py:24
  23.6 1.7 %collective-permute-start.10 = (bf16[144,512]{1,0:T(8,128)(2,1)S(1)}, bf16[144,512]{1,0:T(8,128)(2,1)S(1)}, u32[]{:S(2)}, u32[]{:S(2)}) collective-permute-start(bf16[144,512]{1,0:T(8,128)(2,1)S(1)} %collective-permute-done.7.refs_7_.refs_6_), channel_id=1, source_target_pairs={{0,4},{4,0},{8,12},{12,8},{1,5},{5,1},{9,13},{13,9},{2,6},{6,2},{1... | collective-permute-start | bytes 442376 | tf_op jit(solution)/shard_map/ppermute | solution.py:24
  25.9 9.2 %collective-permute-start.14 = (bf16[144,512]{1,0:T(8,128)(2,1)S(1)}, bf16[144,512]{1,0:T(8,128)(2,1)S(1)}, u32[]{:S(2)}, u32[]{:S(2)}) collective-permute-start(bf16[144,512]{1,0:T(8,128)(2,1)S(1)} %shard_map.68), channel_id=1, source_target_pairs={{0,3},{1,2},{2,1},{3,0},{4,7},{5,6},{6,5},{7,4},{8,11},{9,10},{10,... | collective-permute-start | bytes 442376 | tf_op jit(solution)/shard_map/ppermute | solution.py:24

commit v19 on v18

--- a/solution.py
+++ b/solution.py
@@ -201,7 +201,7 @@
 
 
 def merge_kernel(total_ref, stats_ref, *refs):
-    packed_refs, out_ref = refs[:-1], refs[-1]
+    *packed_refs, out_ref, held_ref, sems = refs
     maxima = [stats_ref[0]]
     sums = [stats_ref[1]]
     for packed_ref in packed_refs:
@@ -214,11 +214,20 @@
     masses = [factor * row_sum for factor, row_sum in zip(factors, sums)]
     inverse = 1.0 / functools.reduce(jnp.add, masses)
     scales = [factors[0] * inverse] + [mass * inverse for mass in masses[1:]]
-    for at in range(0, total_ref.shape[1], LANES):
-        merged = total_ref[:, at : at + LANES] * scales[0]
-        for packed_ref, scale in zip(packed_refs, scales[1:]):
-            merged = merged + packed_ref[0:TILE, at : at + LANES].astype(jnp.float32) * scale
-        out_ref[:, at : at + LANES] = merged.astype(jnp.bfloat16)
+    rows = TILE // sems.shape[0]
+    copies = []
+    for group in range(sems.shape[0]):
+        low, high = group * rows, (group + 1) * rows
+        for at in range(0, total_ref.shape[1], LANES):
+            merged = total_ref[low:high, at : at + LANES] * scales[0][low:high]
+            for packed_ref, scale in zip(packed_refs, scales[1:]):
+                merged = merged + packed_ref[low:high, at : at + LANES].astype(jnp.float32) * scale[low:high]
+            held_ref[low:high, at : at + LANES] = merged.astype(jnp.bfloat16)
+        span = pl.ds(low, rows)
+        copies.append(pltpu.make_async_copy(held_ref.at[span], out_ref.at[span], sems.at[group]))
+        copies[-1].start()
+    for copy in copies:
+        copy.wait()
 
 
 def gather_library(keys, values, queries, masks):
@@ -350,7 +359,8 @@
         merge_kernel,
         out_shape=jax.ShapeDtypeStruct((TILE, value_width), jnp.bfloat16),
         in_specs=[VMEM] * (2 + len(returned)),
-        out_specs=VMEM,
+        out_specs=pl.BlockSpec(memory_space=pl.ANY),
+        scratch_shapes=[pltpu.VMEM((TILE, value_width), jnp.bfloat16), pltpu.SemaphoreType.DMA((4,))],
         compiler_params=params(),
     )(total, stats, *returned)
 

time: 36 us -> 35.8 us (level)
  Pallas kernels: 4.04 us -> 2.72 us
  starting transfers between devices: 18.3 us -> 18.8 us
    pallas_call x1, Pallas kernels: 1.27 us -> 0.4 us  [body(): pl.pallas_call(functools.partial(early_kernel, places_of(early), mask), o...]
    ppermute x15, starting transfers between devices: 18.3 us -> 18.8 us  [swap(): return lax.ppermute(value, axis, [(i, i ^ mask) for i in range(length)])]
    pallas_call x1, Pallas kernels: 1.3 us -> 0.86 us  [body(): pl.pallas_call(functools.partial(home_kernel, places_of(early + late), bu...]
  transfers between devices with their start and end apart: 15 -> 15, of which waited for: 6 -> 6; matrix products, arithmetic and copies ran while one was open for 0% -> 0% of each run, Pallas kernels for 8% -> 4%
where the time goes in v19:
time: 35.8 us; the launch traced here: 35.3 us
  starting transfers between devices  18.8 us (53%)
  waiting for transfers between devices  11.4 us (32%)
  Pallas kernels  2.72 us (8%)
  local copies, waits for them, and re-layouts  2.22 us (6%)
    ppermute x15, starting transfers between devices, swap(): return lax.ppermute(value, axis, [(i, i ^ mask) for i in range(length)])  18.8 us
    ppermute x15, waiting for transfers between devices, swap(): return lax.ppermute(value, axis, [(i, i ^ mask) for i in range(length)])  11.4 us
    unnamed x12, local copies, waits for them, and re-layouts  2.22 us
    pallas_call x1, Pallas kernels, body(): pl.pallas_call(functools.partial(home_kernel, places_of(early + late), bu...  0.86 us
    pallas_call x1, Pallas kernels, body(): pl.pallas_call(merge_kernel, out_shape=jax.ShapeDtypeStruct((TILE, value_...  0.81 us
  transfers between devices with their start and end apart: 15, of which 6 were waited for; matrix products, arithmetic and copies ran while one was open for 0% of the time, Pallas kernels for 4%

profile of v19, /device:TPU:0, one launch (start us, length us, event | category | flops | bytes accessed | tf_op | source)
XLA Modules:
  0.0 35.3 jit_solution(4302591778786867548)
XLA Ops:
  0.0 0.5 %collective-permute-start.1 = (bf16[128,1024]{1,0:T(8,128)(2,1)}, bf16[128,1024]{1,0:T(8,128)(2,1)S(1)}, u32[]{:S(2)}, u32[]{:S(2)}) collective-permute-start(bf16[128,1024]{1,0:T(8,128)(2,1)} %refs_13_.1), channel_id=1, source_target_pairs={{0,4},{4,0},{8,12},{12,8},{1,5},{5,1},{9,13},{13,9},{2,6},{6,2},{1... | collective-permute-start | bytes 786440 | tf_op jit(solution)/shard_map/ppermute | solution.py:24
  0.5 2.6 %collective-permute-start = (bf16[128,1024]{1,0:T(8,128)(2,1)}, bf16[128,1024]{1,0:T(8,128)(2,1)S(1)}, u32[]{:S(2)}, u32[]{:S(2)}) collective-permute-start(bf16[128,1024]{1,0:T(8,128)(2,1)} %refs_13_.1), channel_id=1, source_target_pairs={{0,1},{1,0},{2,3},{3,2},{4,5},{5,4},{6,7},{7,6},{8,9},{9,8},{10,11... | collective-permute-start | bytes 786440 | tf_op jit(solution)/shard_map/ppermute | solution.py:24
  3.1 1.5 %collective-permute-start.3 = (bf16[128,1024]{1,0:T(8,128)(2,1)}, bf16[128,1024]{1,0:T(8,128)(2,1)S(1)}, u32[]{:S(2)}, u32[]{:S(2)}) collective-permute-start(bf16[128,1024]{1,0:T(8,128)(2,1)} %refs_13_.1), channel_id=1, source_target_pairs={{0,8},{4,12},{8,0},{12,4},{1,9},{5,13},{9,1},{13,5},{2,10},{6,14},... | collective-permute-start | bytes 786440 | tf_op jit(solution)/shard_map/ppermute | solution.py:24
  4.6 0.0 collective-permute-done.1.refs_4_.refs_3_
  4.6 0.9 %copy-done.2 = bf16[128,512]{1,0:T(8,128)(2,1)S(1)} copy-done((bf16[128,512]{1,0:T(8,128)(2,1)S(1)}, bf16[128,512]{1,0:T(8,128)(2,1)}, u32[]{:S(2)}) %copy-start.2) | copy-done | bytes 131096
  5.5 0.7 %copy-done.5 = bf16[128]{0:T(256)(128)(2,1)S(1)} copy-done((bf16[128]{0:T(256)(128)(2,1)S(1)}, bf16[128]{0:T(256)(128)(2,1)}, u32[]{:S(2)}) %copy-start.5) | copy-done | bytes 280
  6.1 0.2 shard_map.64.refs_5_.refs_14_
  6.3 0.0 copy-start
  6.3 0.1 collective-permute-start.5
  6.4 0.5 %collective-permute-start.2 = (bf16[144,512]{1,0:T(8,128)(2,1)S(1)}, bf16[144,512]{1,0:T(8,128)(2,1)S(1)}, u32[]{:S(2)}, u32[]{:S(2)}) collective-permute-start(bf16[144,512]{1,0:T(8,128)(2,1)S(1)} %shard_map.64.refs_5_.refs_14_), channel_id=1, source_target_pairs={{0,1},{1,0},{2,3},{3,2},{4,5},{5,4},{6,7},{7,6},{8,9},{9,8},{10,11... | collective-permute-start | bytes 442376 | tf_op jit(solution)/shard_map/ppermute | solution.py:24
  6.9 1.3 %collective-permute-start.4 = (bf16[144,512]{1,0:T(8,128)(2,1)S(1)}, bf16[144,512]{1,0:T(8,128)(2,1)S(1)}, u32[]{:S(2)}, u32[]{:S(2)}) collective-permute-start(bf16[144,512]{1,0:T(8,128)(2,1)S(1)} %shard_map.64.refs_5_.refs_14_), channel_id=1, source_target_pairs={{0,8},{4,12},{8,0},{12,4},{1,9},{5,13},{9,1},{13,5},{2,10},{6,14},... | collective-permute-start | bytes 442376 | tf_op jit(solution)/shard_map/ppermute | solution.py:24
  8.2 0.0 collective-permute-done.5.refs_5_.refs_4_
  8.2 2.8 %collective-permute-start.8 = (bf16[128,1024]{1,0:T(8,128)(2,1)S(1)}, bf16[128,1024]{1,0:T(8,128)(2,1)S(1)}, u32[]{:S(2)}, u32[]{:S(2)}) collective-permute-start(bf16[128,1024]{1,0:T(8,128)(2,1)S(1)} %copy-done.1), channel_id=1, source_target_pairs={{0,3},{1,2},{2,1},{3,0},{4,7},{5,6},{6,5},{7,4},{8,11},{9,10},{10,... | collective-permute-start | bytes 786440 | tf_op jit(solution)/shard_map/ppermute | solution.py:24
  11.1 1.4 %collective-permute-done.3.refs_2_ = bf16[128,1024]{1,0:T(8,128)(2,1)S(1)} collective-permute-done((bf16[128,1024]{1,0:T(8,128)(2,1)}, bf16[128,1024]{1,0:T(8,128)(2,1)S(1)}, u32[]{:S(2)}, u32[]{:S(2)}) %collective-permute-start.3) | collective-permute-done | bytes 262176 | tf_op jit(solution)/shard_map/ppermute | solution.py:24
  12.5 1.5 %collective-permute-start.6 = (bf16[128,1024]{1,0:T(8,128)(2,1)S(1)}, bf16[128,1024]{1,0:T(8,128)(2,1)S(1)}, u32[]{:S(2)}, u32[]{:S(2)}) collective-permute-start(bf16[128,1024]{1,0:T(8,128)(2,1)S(1)} %collective-permute-done.refs_0_), channel_id=1, source_target_pairs={{0,8},{4,12},{8,0},{12,4},{1,9},{5,13},{9,1},{13,5},{2,10},{6,14},... | collective-permute-start | bytes 786440 | tf_op jit(solution)/shard_map/ppermute | solution.py:24
  13.9 1.7 %collective-permute-done.4.refs_3_.refs_1_ = bf16[144,512]{1,0:T(8,128)(2,1)S(1)} collective-permute-done((bf16[144,512]{1,0:T(8,128)(2,1)S(1)}, bf16[144,512]{1,0:T(8,128)(2,1)S(1)}, u32[]{:S(2)}, u32[]{:S(2)}) %collective-permute-start.4) | collective-permute-done | bytes 147488 | tf_op jit(solution)/shard_map/ppermute | solution.py:24
  15.6 1.5 %collective-permute-start.7 = (bf16[144,512]{1,0:T(8,128)(2,1)S(1)}, bf16[144,512]{1,0:T(8,128)(2,1)S(1)}, u32[]{:S(2)}, u32[]{:S(2)}) collective-permute-start(bf16[144,512]{1,0:T(8,128)(2,1)S(1)} %collective-permute-done.2.refs_1_.refs_0_), channel_id=1, source_target_pairs={{0,8},{4,12},{8,0},{12,4},{1,9},{5,13},{9,1},{13,5},{2,10},{6,14},... | collective-permute-start | bytes 442376 | tf_op jit(solution)/shard_map/ppermute | solution.py:24
  17.1 0.0 copy-start.3
  17.1 0.1 collective-permute-start.13
  17.2 0.5 %collective-permute-start.11 = (bf16[128,1024]{1,0:T(8,128)(2,1)S(1)}, bf16[128,1024]{1,0:T(8,128)(2,1)S(1)}, u32[]{:S(2)}, u32[]{:S(2)}) collective-permute-start(bf16[128,1024]{1,0:T(8,128)(2,1)S(1)} %collective-permute-done.refs_0_), channel_id=1, source_target_pairs={{0,4},{4,0},{8,12},{12,8},{1,5},{5,1},{9,13},{13,9},{2,6},{6,2},{1... | collective-permute-start | bytes 786440 | tf_op jit(solution)/shard_map/ppermute | solution.py:24
  17.7 3.6 %collective-permute-done.8.query_ref = bf16[128,1024]{1,0:T(8,128)(2,1)S(1)} collective-permute-done((bf16[128,1024]{1,0:T(8,128)(2,1)S(1)}, bf16[128,1024]{1,0:T(8,128)(2,1)S(1)}, u32[]{:S(2)}, u32[]{:S(2)}) %collective-permute-start.8) | collective-permute-done | bytes 262176 | tf_op jit(solution)/shard_map/ppermute | solution.py:24
  21.3 0.6 %copy-done.4 = s32[16]{0:T(128)S(1)} copy-done((s32[16]{0:T(128)S(1)}, s32[16]{0:T(128)}, u32[]{:S(2)}) %copy-start.4) | copy-done | bytes 88
  21.9 0.4 %shard_map.65 = (bf16[1024,128]{1,0:T(8,128)(2,1)S(1)}, f32[128,512]{1,0:T(8,128)S(1)}, f32[128,128]{1,0:T(8,128)S(1)}, f32[128,128]{1,0:T(8,128)S(1)}) custom-call(s32[4,16]{1,0:T(4,128)S(1)} %bitcast.3, s32[1,16]{1,0:T(1,128)S(1)} %bitcast.6, bf16[128,1024]{1,0:T(8,128)(2,1)S(1)} %collective-permute-done.8.query_ref, ...), custom_call_target="tpu_custom_call" | custom-call | flops 268435456 | bytes 4194304 | tf_op jit(solution)/shard_map/pallas_call | solution.py:303
  22.4 1.3 %collective-permute-done.7.refs_7_.refs_6_ = bf16[144,512]{1,0:T(8,128)(2,1)S(1)} collective-permute-done((bf16[144,512]{1,0:T(8,128)(2,1)S(1)}, bf16[144,512]{1,0:T(8,128)(2,1)S(1)}, u32[]{:S(2)}, u32[]{:S(2)}) %collective-permute-start.7) | collective-permute-done | bytes 147488 | tf_op jit(solution)/shard_map/ppermute | solution.py:24
  23.6 0.0 collective-permute-start.9
  23.6 0.5 %collective-permute-start.10 = (bf16[144,512]{1,0:T(8,128)(2,1)S(1)}, bf16[144,512]{1,0:T(8,128)(2,1)S(1)}, u32[]{:S(2)}, u32[]{:S(2)}) collective-permute-start(bf16[144,512]{1,0:T(8,128)(2,1)S(1)} %collective-permute-done.7.refs_7_.refs_6_), channel_id=1, source_target_pairs={{0,4},{4,0},{8,12},{12,8},{1,5},{5,1},{9,13},{13,9},{2,6},{6,2},{1... | collective-permute-start | bytes 442376 | tf_op jit(solution)/shard_map/ppermute | solution.py:24
  24.1 1.2 %collective-permute-done.10.refs_9_.refs_8_ = bf16[144,512]{1,0:T(8,128)(2,1)S(1)} collective-permute-done((bf16[144,512]{1,0:T(8,128)(2,1)S(1)}, bf16[144,512]{1,0:T(8,128)(2,1)S(1)}, u32[]{:S(2)}, u32[]{:S(2)}) %collective-permute-start.10) | collective-permute-done | bytes 147488 | tf_op jit(solution)/shard_map/ppermute | solution.py:24
  25.4 0.5 %shard_map.68 = bf16[144,512]{1,0:T(8,128)(2,1)S(1)} custom-call(s32[4,16]{1,0:T(4,128)S(1)} %bitcast.4, s32[1,16]{1,0:T(1,128)S(1)} %bitcast.7, bf16[1024,128]{1,0:T(8,128)(2,1)S(1)} %get-tuple-element.26.turned_ref, f32[128,512]{1,0:T(8,128)S(1)} %get-tuple-element.27.refs_0_, f32[128,128]{1,0:T(8,128)S(1)} %get-tuple-element.28.refs_1_, ...), custom_call_target="tpu_custom_call" | custom-call | flops 268435456 | bytes 4194304 | tf_op jit(solution)/shard_map/pallas_call | solution.py:329
  25.9 5.5 %collective-permute-start.14 = (bf16[144,512]{1,0:T(8,128)(2,1)S(1)}, bf16[144,512]{1,0:T(8,128)(2,1)S(1)}, u32[]{:S(2)}, u32[]{:S(2)}) collective-permute-start(bf16[144,512]{1,0:T(8,128)(2,1)S(1)} %shard_map.68), channel_id=1, source_target_pairs={{0,3},{1,2},{2,1},{3,0},{4,7},{5,6},{6,5},{7,4},{8,11},{9,10},{10,... | collective-permute-start | bytes 442376 | tf_op jit(solution)/shard_map/ppermute | solution.py:24
  31.3 0.9 %shard_map.67 = (f32[128,512]{1,0:T(8,128)S(1)}, f32[2,128,128]{2,1,0:T(8,128)S(1)}) custom-call(s32[4,16]{1,0:T(4,128)S(1)} %bitcast.5, s32[1,16]{1,0:T(1,128)S(1)} %bitcast.8, bf16[128,1024]{1,0:T(8,128)(2,1)S(1)} %copy-done.1, bf16[128,1024]{1,0:T(8,128)(2,1)S(1)} %collective-permute-done.refs_0_, ...), custom_call_target="tpu_custom_call" | custom-call | flops 268435456 | bytes 4194304 | tf_op jit(solution)/shard_map/pallas_call | solution.py:344
  32.2 2.3 %collective-permute-done.14.refs_0_ = bf16[144,512]{1,0:T(8,128)(2,1)S(1)} collective-permute-done((bf16[144,512]{1,0:T(8,128)(2,1)S(1)}, bf16[144,512]{1,0:T(8,128)(2,1)S(1)}, u32[]{:S(2)}, u32[]{:S(2)}) %collective-permute-start.14) | collective-permute-done | bytes 147488 | tf_op jit(solution)/shard_map/ppermute | solution.py:24
  34.5 0.8 %shard_map.69 = bf16[128,512]{1,0:T(8,128)(2,1)} custom-call(f32[128,512]{1,0:T(8,128)S(1)} %get-tuple-element.24.total_ref, f32[2,128,128]{2,1,0:T(8,128)S(1)} %get-tuple-element.25.stats_ref, bf16[144,512]{1,0:T(8,128)(2,1)S(1)} %collective-permute-done.14.refs_0_), custom_call_target="tpu_custom_call" | custom-call | tf_op jit(solution)/shard_map/pallas_call | solution.py:358
  (16 shorter events, 0.1 us)
Async XLA Ops:
  0.0 8.2 %copy-start.1 = (bf16[128,1024]{1,0:T(8,128)(2,1)S(1)}, bf16[128,1024]{1,0:T(8,128)(2,1)}, u32[]{:S(2)}) copy-start(bf16[128,1024]{1,0:T(8,128)(2,1)} %query_ref.1) | copy-start | bytes 786436
  0.0 4.6 %collective-permute-start.1 = (bf16[128,1024]{1,0:T(8,128)(2,1)}, bf16[128,1024]{1,0:T(8,128)(2,1)S(1)}, u32[]{:S(2)}, u32[]{:S(2)}) collective-permute-start(bf16[128,1024]{1,0:T(8,128)(2,1)} %refs_13_.1), channel_id=1, source_target_pairs={{0,4},{4,0},{8,12},{12,8},{1,5},{5,1},{9,13},{13,9},{2,6},{6,2},{1... | collective-permute-start | bytes 786440 | tf_op jit(solution)/shard_map/ppermute | solution.py:24
  0.5 10.6 %collective-permute-start = (bf16[128,1024]{1,0:T(8,128)(2,1)}, bf16[128,1024]{1,0:T(8,128)(2,1)S(1)}, u32[]{:S(2)}, u32[]{:S(2)}) collective-permute-start(bf16[128,1024]{1,0:T(8,128)(2,1)} %refs_13_.1), channel_id=1, source_target_pairs={{0,1},{1,0},{2,3},{3,2},{4,5},{5,4},{6,7},{7,6},{8,9},{9,8},{10,11... | collective-permute-start | bytes 786440 | tf_op jit(solution)/shard_map/ppermute | solution.py:24
  3.1 9.4 %collective-permute-start.3 = (bf16[128,1024]{1,0:T(8,128)(2,1)}, bf16[128,1024]{1,0:T(8,128)(2,1)S(1)}, u32[]{:S(2)}, u32[]{:S(2)}) collective-permute-start(bf16[128,1024]{1,0:T(8,128)(2,1)} %refs_13_.1), channel_id=1, source_target_pairs={{0,8},{4,12},{8,0},{12,4},{1,9},{5,13},{9,1},{13,5},{2,10},{6,14},... | collective-permute-start | bytes 786440 | tf_op jit(solution)/shard_map/ppermute | solution.py:24
  4.6 0.9 %copy-start.2 = (bf16[128,512]{1,0:T(8,128)(2,1)S(1)}, bf16[128,512]{1,0:T(8,128)(2,1)}, u32[]{:S(2)}) copy-start(bf16[128,512]{1,0:T(8,128)(2,1)} %values_ref) | copy-start | bytes 393220
  5.5 0.7 %copy-start.5 = (bf16[128]{0:T(256)(128)(2,1)S(1)}, bf16[128]{0:T(256)(128)(2,1)}, u32[]{:S(2)}) copy-start(bf16[128]{0:T(256)(128)(2,1)} %param.9) | copy-start | bytes 772
  6.3 15.0 %copy-start = (bf16[128,1024]{1,0:T(8,128)(2,1)S(1)}, bf16[128,1024]{1,0:T(8,128)(2,1)}, u32[]{:S(2)}) copy-start(bf16[128,1024]{1,0:T(8,128)(2,1)} %refs_13_.1) | copy-start | bytes 786436
  6.3 1.9 %collective-permute-start.5 = (bf16[144,512]{1,0:T(8,128)(2,1)S(1)}, bf16[144,512]{1,0:T(8,128)(2,1)S(1)}, u32[]{:S(2)}, u32[]{:S(2)}) collective-permute-start(bf16[144,512]{1,0:T(8,128)(2,1)S(1)} %shard_map.64.refs_5_.refs_14_), channel_id=1, source_target_pairs={{0,4},{4,0},{8,12},{12,8},{1,5},{5,1},{9,13},{13,9},{2,6},{6,2},{1... | collective-permute-start | bytes 442376 | tf_op jit(solution)/shard_map/ppermute | solution.py:24
  6.4 7.5 %collective-permute-start.2 = (bf16[144,512]{1,0:T(8,128)(2,1)S(1)}, bf16[144,512]{1,0:T(8,128)(2,1)S(1)}, u32[]{:S(2)}, u32[]{:S(2)}) collective-permute-start(bf16[144,512]{1,0:T(8,128)(2,1)S(1)} %shard_map.64.refs_5_.refs_14_), channel_id=1, source_target_pairs={{0,1},{1,0},{2,3},{3,2},{4,5},{5,4},{6,7},{7,6},{8,9},{9,8},{10,11... | collective-permute-start | bytes 442376 | tf_op jit(solution)/shard_map/ppermute | solution.py:24
  6.9 8.7 %collective-permute-start.4 = (bf16[144,512]{1,0:T(8,128)(2,1)S(1)}, bf16[144,512]{1,0:T(8,128)(2,1)S(1)}, u32[]{:S(2)}, u32[]{:S(2)}) collective-permute-start(bf16[144,512]{1,0:T(8,128)(2,1)S(1)} %shard_map.64.refs_5_.refs_14_), channel_id=1, source_target_pairs={{0,8},{4,12},{8,0},{12,4},{1,9},{5,13},{9,1},{13,5},{2,10},{6,14},... | collective-permute-start | bytes 442376 | tf_op jit(solution)/shard_map/ppermute | solution.py:24
  8.2 13.1 %collective-permute-start.8 = (bf16[128,1024]{1,0:T(8,128)(2,1)S(1)}, bf16[128,1024]{1,0:T(8,128)(2,1)S(1)}, u32[]{:S(2)}, u32[]{:S(2)}) collective-permute-start(bf16[128,1024]{1,0:T(8,128)(2,1)S(1)} %copy-done.1), channel_id=1, source_target_pairs={{0,3},{1,2},{2,1},{3,0},{4,7},{5,6},{6,5},{7,4},{8,11},{9,10},{10,... | collective-permute-start | bytes 786440 | tf_op jit(solution)/shard_map/ppermute | solution.py:24
  12.5 9.9 %collective-permute-start.6 = (bf16[128,1024]{1,0:T(8,128)(2,1)S(1)}, bf16[128,1024]{1,0:T(8,128)(2,1)S(1)}, u32[]{:S(2)}, u32[]{:S(2)}) collective-permute-start(bf16[128,1024]{1,0:T(8,128)(2,1)S(1)} %collective-permute-done.refs_0_), channel_id=1, source_target_pairs={{0,8},{4,12},{8,0},{12,4},{1,9},{5,13},{9,1},{13,5},{2,10},{6,14},... | collective-permute-start | bytes 786440 | tf_op jit(solution)/shard_map/ppermute | solution.py:24
  15.6 8.0 %collective-permute-start.7 = (bf16[144,512]{1,0:T(8,128)(2,1)S(1)}, bf16[144,512]{1,0:T(8,128)(2,1)S(1)}, u32[]{:S(2)}, u32[]{:S(2)}) collective-permute-start(bf16[144,512]{1,0:T(8,128)(2,1)S(1)} %collective-permute-done.2.refs_1_.refs_0_), channel_id=1, source_target_pairs={{0,8},{4,12},{8,0},{12,4},{1,9},{5,13},{9,1},{13,5},{2,10},{6,14},... | collective-permute-start | bytes 442376 | tf_op jit(solution)/shard_map/ppermute | solution.py:24
  17.1 4.2 %copy-start.3 = (s32[16,4]{0,1:T(4,128)S(1)}, s32[16,4]{0,1:T(4,128)}, u32[]{:S(2)}) copy-start(s32[16,4]{0,1:T(4,128)} %param.10) | copy-start | bytes 772
  17.1 7.0 %collective-permute-start.13 = (bf16[288,512]{1,0:T(8,128)(2,1)S(1)}, bf16[288,512]{1,0:T(8,128)(2,1)S(1)}, u32[]{:S(2)}, u32[]{:S(2)}) collective-permute-start(bf16[288,512]{1,0:T(8,128)(2,1)S(1)} %shard_map.66), channel_id=1, source_target_pairs={{0,4},{4,0},{8,12},{12,8},{1,5},{5,1},{9,13},{13,9},{2,6},{6,2},{1... | collective-permute-start | bytes 884744 | tf_op jit(solution)/shard_map/ppermute | solution.py:24
  17.2 6.9 %collective-permute-start.11 = (bf16[128,1024]{1,0:T(8,128)(2,1)S(1)}, bf16[128,1024]{1,0:T(8,128)(2,1)S(1)}, u32[]{:S(2)}, u32[]{:S(2)}) collective-permute-start(bf16[128,1024]{1,0:T(8,128)(2,1)S(1)} %collective-permute-done.refs_0_), channel_id=1, source_target_pairs={{0,4},{4,0},{8,12},{12,8},{1,5},{5,1},{9,13},{13,9},{2,6},{6,2},{1... | collective-permute-start | bytes 786440 | tf_op jit(solution)/shard_map/ppermute | solution.py:24
  21.3 2.8 %collective-permute-start.12 = (bf16[128,1024]{1,0:T(8,128)(2,1)S(1)}, bf16[128,1024]{1,0:T(8,128)(2,1)S(1)}, u32[]{:S(2)}, u32[]{:S(2)}) collective-permute-start(bf16[128,1024]{1,0:T(8,128)(2,1)S(1)} %collective-permute-done.3.refs_2_), channel_id=1, source_target_pairs={{0,4},{4,0},{8,12},{12,8},{1,5},{5,1},{9,13},{13,9},{2,6},{6,2},{1... | collective-permute-start | bytes 786440 | tf_op jit(solution)/shard_map/ppermute | solution.py:24
  21.3 0.7 %copy-start.4 = (s32[16]{0:T(128)S(1)}, s32[16]{0:T(128)}, u32[]{:S(2)}) copy-start(s32[16]{0:T(128)} %param.11) | copy-start | bytes 196
  23.6 1.8 %collective-permute-start.9 = (bf16[128,1024]{1,0:T(8,128)(2,1)S(1)}, bf16[128,1024]{1,0:T(8,128)(2,1)S(1)}, u32[]{:S(2)}, u32[]{:S(2)}) collective-permute-start(bf16[128,1024]{1,0:T(8,128)(2,1)S(1)} %collective-permute-done.6.refs_6_.refs_5_), channel_id=1, source_target_pairs={{0,4},{4,0},{8,12},{12,8},{1,5},{5,1},{9,13},{13,9},{2,6},{6,2},{1... | collective-permute-start | bytes 786440 | tf_op jit(solution)/shard_map/ppermute | solution.py:24
  23.6 1.7 %collective-permute-start.10 = (bf16[144,512]{1,0:T(8,128)(2,1)S(1)}, bf16[144,512]{1,0:T(8,128)(2,1)S(1)}, u32[]{:S(2)}, u32[]{:S(2)}) collective-permute-start(bf16[144,512]{1,0:T(8,128)(2,1)S(1)} %collective-permute-done.7.refs_7_.refs_6_), channel_id=1, source_target_pairs={{0,4},{4,0},{8,12},{12,8},{1,5},{5,1},{9,13},{13,9},{2,6},{6,2},{1... | collective-permute-start | bytes 442376 | tf_op jit(solution)/shard_map/ppermute | solution.py:24
  25.9 8.6 %collective-permute-start.14 = (bf16[144,512]{1,0:T(8,128)(2,1)S(1)}, bf16[144,512]{1,0:T(8,128)(2,1)S(1)}, u32[]{:S(2)}, u32[]{:S(2)}) collective-permute-start(bf16[144,512]{1,0:T(8,128)(2,1)S(1)} %shard_map.68), channel_id=1, source_target_pairs={{0,3},{1,2},{2,1},{3,0},{4,7},{5,6},{6,5},{7,4},{8,11},{9,10},{10,... | collective-permute-start | bytes 442376 | tf_op jit(solution)/shard_map/ppermute | solution.py:24

commit v20 on v18

--- a/solution.py
+++ b/solution.py
@@ -100,6 +100,11 @@
         row += ref.shape[0]
 
 
+def window_kernel(lists_ref, counts_ref, windows_ref):
+    windows_ref[0:1, :] = lists_ref[0:1, :]
+    windows_ref[1:2, :] = counts_ref[...]
+
+
 def pick(ref, row, column):
     rows = lax.broadcasted_iota(jnp.int32, ref.shape, 0)
     columns = lax.broadcasted_iota(jnp.int32, ref.shape, 1)
@@ -107,14 +112,14 @@
     return jnp.sum(chosen.astype(jnp.float32)).astype(jnp.int32)
 
 
-def attend(pieces, panel_mask, lists_ref, counts_ref, query_ref, score_ref, total_ref, mass_ref, before=None):
+def attend(pieces, panel_mask, windows_ref, query_ref, score_ref, total_ref, mass_ref, before=None):
     lib_index = lax.axis_index("lib")
     qry_index = lax.axis_index("qry")
     qry_count = lax.axis_size("qry")
     block_total = lax.axis_size("lib") * qry_count
     panel = lib_index * qry_count + lax.bitwise_xor(qry_index, panel_mask)
-    first = pick(lists_ref, 0, panel)
-    count = pick(counts_ref, 0, panel)
+    first = pick(windows_ref, 0, panel)
+    count = pick(windows_ref, 1, panel)
     inverse_root = 1.0 / math.sqrt(pieces[0].keys_ref.shape[1])
 
     def active(lib_mask, qry_mask):
@@ -164,19 +169,19 @@
     return row_max
 
 
-def early_kernel(places, panel_mask, lists_ref, counts_ref, query_ref, *refs):
+def early_kernel(places, panel_mask, windows_ref, query_ref, *refs):
     pieces, refs = read_pieces(places, refs, own=True)
     turned_ref, total_ref, mass_ref, max_ref, score_ref = refs
-    row_max = attend(pieces, panel_mask, lists_ref, counts_ref, query_ref, score_ref, total_ref, mass_ref)
+    row_max = attend(pieces, panel_mask, windows_ref, query_ref, score_ref, total_ref, mass_ref)
     max_ref[...] = jnp.broadcast_to(row_max, max_ref.shape)
     turned_ref[...] = jnp.transpose(query_ref[...])
 
 
-def late_kernel(places, bundled, panel_mask, lists_ref, counts_ref, turned_ref, *refs):
+def late_kernel(places, bundled, panel_mask, windows_ref, turned_ref, *refs):
     before, refs = refs[:3], refs[3:]
     pieces, refs = read_pieces(places, refs, bundled)
     packed_ref, score_ref, total_ref, mass_ref = refs
-    row_max = attend(pieces, panel_mask, lists_ref, counts_ref, turned_ref, score_ref, total_ref, mass_ref, before)
+    row_max = attend(pieces, panel_mask, windows_ref, turned_ref, score_ref, total_ref, mass_ref, before)
     row_sum = jnp.sum(mass_ref[...], axis=1, keepdims=True)
     value_width = total_ref.shape[1]
     inverse = 1.0 / jnp.where(row_sum > 0.0, row_sum, 1.0)
@@ -191,10 +196,10 @@
     packed_ref[TILE:, LANES:] = jnp.zeros((EXTRA, value_width - LANES), jnp.bfloat16)
 
 
-def home_kernel(places, bundled, lists_ref, counts_ref, query_ref, *refs):
+def home_kernel(places, bundled, windows_ref, query_ref, *refs):
     pieces, refs = read_pieces(places, refs, bundled, own=True)
     total_ref, stats_ref, score_ref, mass_ref = refs
-    row_max = attend(pieces, 0, lists_ref, counts_ref, query_ref, score_ref, total_ref, mass_ref)
+    row_max = attend(pieces, 0, windows_ref, query_ref, score_ref, total_ref, mass_ref)
     row_sum = jnp.sum(mass_ref[...], axis=1, keepdims=True)
     stats_ref[0] = jnp.broadcast_to(row_max, (TILE, LANES))
     stats_ref[1] = jnp.broadcast_to(row_sum, (TILE, LANES))
@@ -221,14 +226,14 @@
         out_ref[:, at : at + LANES] = merged.astype(jnp.bfloat16)
 
 
-def gather_library(keys, values, queries, masks):
+def gather_library(keys, values, queries, windows, masks):
     steps = [("qry", 1)]
     mask = lax.axis_size("lib") // 2
     while mask > 1:
         steps.append(("lib", mask))
         mask //= 2
     partner_values = swap(values, "lib", 1)
-    leaving, _ = tie(queries, partner_values)
+    leaving, *_ = tie(queries, partner_values, windows)
     visitors = [swap(leaving, "qry", mask) for mask in masks]
     early, late = [], []
     for axis, mask in steps:
@@ -276,10 +281,15 @@
         compiler_params=params(),
     )(own_values, key_scale.reshape(1, TILE))
 
-    window_lists = block_list.T
-    window_counts = block_count.reshape(1, -1)
+    windows = pl.pallas_call(
+        window_kernel,
+        out_shape=jax.ShapeDtypeStruct((2, block_list.shape[0]), jnp.int32),
+        in_specs=[VMEM, VMEM],
+        out_specs=VMEM,
+        compiler_params=params(),
+    )(block_list.T, block_count.reshape(1, -1))
     masks = [2 * at + 1 for at in range(1, qry_count // 2)]
-    early, relayed, partner_values, visitors = gather_library(library_keys, values, queries, masks)
+    early, relayed, partner_values, visitors = gather_library(library_keys, values, queries, windows, masks)
     piece_rows = (width // value_width + 1) * TILE + EXTRA
     cost = pl.CostEstimate(flops=2 * TILE * 4 * TILE * width * 2, bytes_accessed=4 * 1024 * 1024, transcendentals=0)
     total_shape = jax.ShapeDtypeStruct((TILE, value_width), jnp.float32)
@@ -294,12 +304,12 @@
         state = pl.pallas_call(
             functools.partial(early_kernel, places_of(early), mask),
             out_shape=(jax.ShapeDtypeStruct(queries.shape[::-1], queries.dtype), total_shape, line_shape, line_shape),
-            in_specs=[VMEM, VMEM] + [VMEM] * (1 + len(early_arrays)) + own_specs,
+            in_specs=[VMEM] * (2 + len(early_arrays)) + own_specs,
             out_specs=(VMEM,) * 4,
             scratch_shapes=[pltpu.VMEM((len(early) + 1, TILE, TILE), jnp.float32)] + own_scratch,
             compiler_params=attend_params,
             cost_estimate=cost,
-        )(window_lists, window_counts, visiting, *early_arrays, library_keys, values)
+        )(windows, visiting, *early_arrays, library_keys, values)
         states.append(state)
 
     bundled = [(lib_mask | 1, qry_mask) for lib_mask, qry_mask in places_of(early)]
@@ -320,7 +330,7 @@
         packed = pl.pallas_call(
             functools.partial(late_kernel, places_of(late), bundled, mask),
             out_shape=jax.ShapeDtypeStruct((TILE + EXTRA, value_width), jnp.bfloat16),
-            in_specs=[VMEM, VMEM] + [VMEM] * (4 + len(late_arrays)),
+            in_specs=[VMEM] * (5 + len(late_arrays)),
             out_specs=VMEM,
             scratch_shapes=[
                 pltpu.VMEM((len(late) + len(bundled), TILE, TILE), jnp.float32),
@@ -329,13 +339,13 @@
             ],
             compiler_params=attend_params,
             cost_estimate=cost,
-        )(window_lists, window_counts, *state, *late_arrays)
+        )(windows, *state, *late_arrays)
         returned.append(swap(packed, "qry", mask))
 
     total, stats = pl.pallas_call(
         functools.partial(home_kernel, places_of(early + late), bundled),
         out_shape=(total_shape, jax.ShapeDtypeStruct((2, TILE, LANES), jnp.float32)),
-        in_specs=[VMEM, VMEM] + [VMEM] * (1 + len(early_arrays) + len(late_arrays)) + own_specs,
+        in_specs=[VMEM] * (2 + len(early_arrays) + len(late_arrays)) + own_specs,
         out_specs=(VMEM, VMEM),
         scratch_shapes=[
             pltpu.VMEM((pieces_total, TILE, TILE), jnp.float32),
@@ -344,7 +354,7 @@
         + own_scratch,
         compiler_params=attend_params,
         cost_estimate=cost,
-    )(window_lists, window_counts, queries, *early_arrays, *late_arrays, library_keys, values)
+    )(windows, queries, *early_arrays, *late_arrays, library_keys, values)
 
     return pl.pallas_call(
         merge_kernel,

time: 36 us -> 35.8 us (level)
    pallas_call x1, Pallas kernels: 1.27 us -> 0.4 us  [body(): pl.pallas_call(functools.partial(early_kernel, places_of(early), mask), o...]
    pallas_call x1, Pallas kernels: 0.48 us -> 1.02 us  [body(): pl.pallas_call(functools.partial(late_kernel, places_of(late), bundled, m...]
  transfers between devices with their start and end apart: 15 -> 15, of which waited for: 6 -> 6; matrix products, arithmetic and copies ran while one was open for 0% -> 0% of each run, Pallas kernels for 8% -> 5%
where the time goes in v20:
time: 35.8 us
  starting transfers between devices  18.3 us (51%)
  waiting for transfers between devices  11.4 us (32%)
  Pallas kernels  3.73 us (10%)
  local copies, waits for them, and re-layouts  2.23 us (6%)
    ppermute x15, starting transfers between devices, swap(): return lax.ppermute(value, axis, [(i, i ^ mask) for i in range(length)])  18.3 us
    ppermute x15, waiting for transfers between devices, swap(): return lax.ppermute(value, axis, [(i, i ^ mask) for i in range(length)])  11.4 us
    unnamed x12, local copies, waits for them, and re-layouts  2.23 us
    pallas_call x1, Pallas kernels, body(): pl.pallas_call(functools.partial(home_kernel, places_of(early + late), bu...  1.31 us
    pallas_call x1, Pallas kernels, body(): pl.pallas_call(functools.partial(late_kernel, places_of(late), bundled, m...  1.02 us
    pallas_call x1, Pallas kernels, body(): pl.pallas_call(merge_kernel, out_shape=jax.ShapeDtypeStruct((TILE, value_...  0.81 us
  transfers between devices with their start and end apart: 15, of which 6 were waited for; matrix products, arithmetic and copies ran while one was open for 0% of the time, Pallas kernels for 5%

profile of v20, /device:TPU:0, one launch (start us, length us, event | category | flops | bytes accessed | tf_op | source)
XLA Modules:
  0.0 35.8 jit_solution(9153467437711874620)
XLA Ops:
  0.0 0.5 %collective-permute-start.1 = (bf16[128,1024]{1,0:T(8,128)(2,1)}, bf16[128,1024]{1,0:T(8,128)(2,1)S(1)}, u32[]{:S(2)}, u32[]{:S(2)}) collective-permute-start(bf16[128,1024]{1,0:T(8,128)(2,1)} %refs_13_.1), channel_id=1, source_target_pairs={{0,4},{4,0},{8,12},{12,8},{1,5},{5,1},{9,13},{13,9},{2,6},{6,2},{1... | collective-permute-start | bytes 786440 | tf_op jit(solution)/shard_map/ppermute | solution.py:24
  0.5 2.6 %collective-permute-start = (bf16[128,1024]{1,0:T(8,128)(2,1)}, bf16[128,1024]{1,0:T(8,128)(2,1)S(1)}, u32[]{:S(2)}, u32[]{:S(2)}) collective-permute-start(bf16[128,1024]{1,0:T(8,128)(2,1)} %refs_13_.1), channel_id=1, source_target_pairs={{0,1},{1,0},{2,3},{3,2},{4,5},{5,4},{6,7},{7,6},{8,9},{9,8},{10,11... | collective-permute-start | bytes 786440 | tf_op jit(solution)/shard_map/ppermute | solution.py:24
  3.1 1.5 %collective-permute-start.3 = (bf16[128,1024]{1,0:T(8,128)(2,1)}, bf16[128,1024]{1,0:T(8,128)(2,1)S(1)}, u32[]{:S(2)}, u32[]{:S(2)}) collective-permute-start(bf16[128,1024]{1,0:T(8,128)(2,1)} %refs_13_.1), channel_id=1, source_target_pairs={{0,8},{4,12},{8,0},{12,4},{1,9},{5,13},{9,1},{13,5},{2,10},{6,14},... | collective-permute-start | bytes 786440 | tf_op jit(solution)/shard_map/ppermute | solution.py:24
  4.6 0.9 %copy-done.2 = bf16[128,512]{1,0:T(8,128)(2,1)S(1)} copy-done((bf16[128,512]{1,0:T(8,128)(2,1)S(1)}, bf16[128,512]{1,0:T(8,128)(2,1)}, u32[]{:S(2)}) %copy-start.2) | copy-done | bytes 131096
  5.5 0.7 %copy-done.4 = bf16[128]{0:T(256)(128)(2,1)S(1)} copy-done((bf16[128]{0:T(256)(128)(2,1)S(1)}, bf16[128]{0:T(256)(128)(2,1)}, u32[]{:S(2)}) %copy-start.4) | copy-done | bytes 280
  6.1 0.2 shard_map.65.refs_5_.refs_14_
  6.3 0.0 copy-start.3
  6.3 0.1 collective-permute-start.5
  6.4 0.5 %collective-permute-start.2 = (bf16[144,512]{1,0:T(8,128)(2,1)S(1)}, bf16[144,512]{1,0:T(8,128)(2,1)S(1)}, u32[]{:S(2)}, u32[]{:S(2)}) collective-permute-start(bf16[144,512]{1,0:T(8,128)(2,1)S(1)} %shard_map.65.refs_5_.refs_14_), channel_id=1, source_target_pairs={{0,1},{1,0},{2,3},{3,2},{4,5},{5,4},{6,7},{7,6},{8,9},{9,8},{10,11... | collective-permute-start | bytes 442376 | tf_op jit(solution)/shard_map/ppermute | solution.py:24
  6.9 1.3 %collective-permute-start.4 = (bf16[144,512]{1,0:T(8,128)(2,1)S(1)}, bf16[144,512]{1,0:T(8,128)(2,1)S(1)}, u32[]{:S(2)}, u32[]{:S(2)}) collective-permute-start(bf16[144,512]{1,0:T(8,128)(2,1)S(1)} %shard_map.65.refs_5_.refs_14_), channel_id=1, source_target_pairs={{0,8},{4,12},{8,0},{12,4},{1,9},{5,13},{9,1},{13,5},{2,10},{6,14},... | collective-permute-start | bytes 442376 | tf_op jit(solution)/shard_map/ppermute | solution.py:24
  8.2 0.7 %copy-done.5 = s32[16]{0:T(128)S(1)} copy-done((s32[16]{0:T(128)S(1)}, s32[16]{0:T(128)}, u32[]{:S(2)}) %copy-start.5) | copy-done | bytes 88
  8.9 0.0 collective-permute-done.5.refs_5_.refs_4_
  8.9 2.9 %collective-permute-start.8 = (bf16[128,1024]{1,0:T(8,128)(2,1)S(1)}, bf16[128,1024]{1,0:T(8,128)(2,1)S(1)}, u32[]{:S(2)}, u32[]{:S(2)}) collective-permute-start(bf16[128,1024]{1,0:T(8,128)(2,1)S(1)} %copy-done.1), channel_id=1, source_target_pairs={{0,3},{1,2},{2,1},{3,0},{4,7},{5,6},{6,5},{7,4},{8,11},{9,10},{10,... | collective-permute-start | bytes 786440 | tf_op jit(solution)/shard_map/ppermute | solution.py:24
  11.8 0.0 collective-permute-done.refs_0_
  11.8 0.6 %collective-permute-done.3.refs_2_ = bf16[128,1024]{1,0:T(8,128)(2,1)S(1)} collective-permute-done((bf16[128,1024]{1,0:T(8,128)(2,1)}, bf16[128,1024]{1,0:T(8,128)(2,1)S(1)}, u32[]{:S(2)}, u32[]{:S(2)}) %collective-permute-start.3) | collective-permute-done | bytes 262176 | tf_op jit(solution)/shard_map/ppermute | solution.py:24
  12.5 1.5 %collective-permute-start.6 = (bf16[128,1024]{1,0:T(8,128)(2,1)S(1)}, bf16[128,1024]{1,0:T(8,128)(2,1)S(1)}, u32[]{:S(2)}, u32[]{:S(2)}) collective-permute-start(bf16[128,1024]{1,0:T(8,128)(2,1)S(1)} %collective-permute-done.refs_0_), channel_id=1, source_target_pairs={{0,8},{4,12},{8,0},{12,4},{1,9},{5,13},{9,1},{13,5},{2,10},{6,14},... | collective-permute-start | bytes 786440 | tf_op jit(solution)/shard_map/ppermute | solution.py:24
  13.9 0.0 collective-permute-done.2.refs_1_.refs_0_
  13.9 1.7 %collective-permute-done.4.refs_3_.refs_1_ = bf16[144,512]{1,0:T(8,128)(2,1)S(1)} collective-permute-done((bf16[144,512]{1,0:T(8,128)(2,1)S(1)}, bf16[144,512]{1,0:T(8,128)(2,1)S(1)}, u32[]{:S(2)}, u32[]{:S(2)}) %collective-permute-start.4) | collective-permute-done | bytes 147488 | tf_op jit(solution)/shard_map/ppermute | solution.py:24
  15.6 1.5 %collective-permute-start.7 = (bf16[144,512]{1,0:T(8,128)(2,1)S(1)}, bf16[144,512]{1,0:T(8,128)(2,1)S(1)}, u32[]{:S(2)}, u32[]{:S(2)}) collective-permute-start(bf16[144,512]{1,0:T(8,128)(2,1)S(1)} %collective-permute-done.2.refs_1_.refs_0_), channel_id=1, source_target_pairs={{0,8},{4,12},{8,0},{12,4},{1,9},{5,13},{9,1},{13,5},{2,10},{6,14},... | collective-permute-start | bytes 442376 | tf_op jit(solution)/shard_map/ppermute | solution.py:24
  17.1 0.1 collective-permute-start.13
  17.2 0.5 %collective-permute-start.11 = (bf16[128,1024]{1,0:T(8,128)(2,1)S(1)}, bf16[128,1024]{1,0:T(8,128)(2,1)S(1)}, u32[]{:S(2)}, u32[]{:S(2)}) collective-permute-start(bf16[128,1024]{1,0:T(8,128)(2,1)S(1)} %collective-permute-done.refs_0_), channel_id=1, source_target_pairs={{0,4},{4,0},{8,12},{12,8},{1,5},{5,1},{9,13},{13,9},{2,6},{6,2},{1... | collective-permute-start | bytes 786440 | tf_op jit(solution)/shard_map/ppermute | solution.py:24
  17.7 3.6 %collective-permute-done.8.query_ref = bf16[128,1024]{1,0:T(8,128)(2,1)S(1)} collective-permute-done((bf16[128,1024]{1,0:T(8,128)(2,1)S(1)}, bf16[128,1024]{1,0:T(8,128)(2,1)S(1)}, u32[]{:S(2)}, u32[]{:S(2)}) %collective-permute-start.8) | collective-permute-done | bytes 262176 | tf_op jit(solution)/shard_map/ppermute | solution.py:24
  21.3 0.0 collective-permute-start.12
  21.3 0.4 %shard_map.66 = (bf16[1024,128]{1,0:T(8,128)(2,1)S(1)}, f32[128,512]{1,0:T(8,128)S(1)}, f32[128,128]{1,0:T(8,128)S(1)}, f32[128,128]{1,0:T(8,128)S(1)}) custom-call(s32[2,16]{1,0:T(2,128)S(1)} %shard_map.64.windows_ref, bf16[128,1024]{1,0:T(8,128)(2,1)S(1)} %collective-permute-done.8.query_ref, bf16[128,1024]{1,0:T(8,128)(2,1)S(1)} %collective-permute-done.refs_0_, ...), custom_call_target="tpu_custom_call" | custom-call | flops 268435456 | bytes 4194304 | tf_op jit(solution)/shard_map/pallas_call | solution.py:304
  21.7 1.9 %collective-permute-done.7.refs_7_.refs_6_ = bf16[144,512]{1,0:T(8,128)(2,1)S(1)} collective-permute-done((bf16[144,512]{1,0:T(8,128)(2,1)S(1)}, bf16[144,512]{1,0:T(8,128)(2,1)S(1)}, u32[]{:S(2)}, u32[]{:S(2)}) %collective-permute-start.7) | collective-permute-done | bytes 147488 | tf_op jit(solution)/shard_map/ppermute | solution.py:24
  23.6 0.5 %collective-permute-start.10 = (bf16[144,512]{1,0:T(8,128)(2,1)S(1)}, bf16[144,512]{1,0:T(8,128)(2,1)S(1)}, u32[]{:S(2)}, u32[]{:S(2)}) collective-permute-start(bf16[144,512]{1,0:T(8,128)(2,1)S(1)} %collective-permute-done.7.refs_7_.refs_6_), channel_id=1, source_target_pairs={{0,4},{4,0},{8,12},{12,8},{1,5},{5,1},{9,13},{13,9},{2,6},{6,2},{1... | collective-permute-start | bytes 442376 | tf_op jit(solution)/shard_map/ppermute | solution.py:24
  24.1 1.2 %collective-permute-done.10.refs_9_.refs_8_ = bf16[144,512]{1,0:T(8,128)(2,1)S(1)} collective-permute-done((bf16[144,512]{1,0:T(8,128)(2,1)S(1)}, bf16[144,512]{1,0:T(8,128)(2,1)S(1)}, u32[]{:S(2)}, u32[]{:S(2)}) %collective-permute-start.10) | collective-permute-done | bytes 147488 | tf_op jit(solution)/shard_map/ppermute | solution.py:24
  25.4 1.0 %shard_map.69 = bf16[144,512]{1,0:T(8,128)(2,1)S(1)} custom-call(s32[2,16]{1,0:T(2,128)S(1)} %shard_map.64.windows_ref, bf16[1024,128]{1,0:T(8,128)(2,1)S(1)} %get-tuple-element.26.turned_ref, f32[128,512]{1,0:T(8,128)S(1)} %get-tuple-element.27.refs_0_, f32[128,128]{1,0:T(8,128)S(1)} %get-tuple-element.28.refs_1_, ...), custom_call_target="tpu_custom_call" | custom-call | flops 268435456 | bytes 4194304 | tf_op jit(solution)/shard_map/pallas_call | solution.py:330
  26.4 4.9 %collective-permute-start.14 = (bf16[144,512]{1,0:T(8,128)(2,1)S(1)}, bf16[144,512]{1,0:T(8,128)(2,1)S(1)}, u32[]{:S(2)}, u32[]{:S(2)}) collective-permute-start(bf16[144,512]{1,0:T(8,128)(2,1)S(1)} %shard_map.69), channel_id=1, source_target_pairs={{0,3},{1,2},{2,1},{3,0},{4,7},{5,6},{6,5},{7,4},{8,11},{9,10},{10,... | collective-permute-start | bytes 442376 | tf_op jit(solution)/shard_map/ppermute | solution.py:24
  31.3 1.3 %shard_map.68 = (f32[128,512]{1,0:T(8,128)S(1)}, f32[2,128,128]{2,1,0:T(8,128)S(1)}) custom-call(s32[2,16]{1,0:T(2,128)S(1)} %shard_map.64.windows_ref, bf16[128,1024]{1,0:T(8,128)(2,1)S(1)} %copy-done.1, bf16[128,1024]{1,0:T(8,128)(2,1)S(1)} %collective-permute-done.refs_0_, bf16[144,512]{1,0:T(8,128)(2,1)S(1)} %collective-permute-done.2.refs_1_.refs_0_, ...), custom_call_target="tpu_custom_call" | custom-call | flops 268435456 | bytes 4194304 | tf_op jit(solution)/shard_map/pallas_call | solution.py:345
  32.6 2.4 %collective-permute-done.14.refs_0_ = bf16[144,512]{1,0:T(8,128)(2,1)S(1)} collective-permute-done((bf16[144,512]{1,0:T(8,128)(2,1)S(1)}, bf16[144,512]{1,0:T(8,128)(2,1)S(1)}, u32[]{:S(2)}, u32[]{:S(2)}) %collective-permute-start.14) | collective-permute-done | bytes 147488 | tf_op jit(solution)/shard_map/ppermute | solution.py:24
  35.0 0.8 %shard_map.70 = bf16[128,512]{1,0:T(8,128)(2,1)} custom-call(f32[128,512]{1,0:T(8,128)S(1)} %get-tuple-element.24.total_ref, f32[2,128,128]{2,1,0:T(8,128)S(1)} %get-tuple-element.25.stats_ref, bf16[144,512]{1,0:T(8,128)(2,1)S(1)} %collective-permute-done.14.refs_0_), custom_call_target="tpu_custom_call" | custom-call | tf_op jit(solution)/shard_map/pallas_call | solution.py:359
  (17 shorter events, 0.1 us)
Async XLA Ops:
  0.0 8.9 %copy-start.1 = (bf16[128,1024]{1,0:T(8,128)(2,1)S(1)}, bf16[128,1024]{1,0:T(8,128)(2,1)}, u32[]{:S(2)}) copy-start(bf16[128,1024]{1,0:T(8,128)(2,1)} %query_ref.1) | copy-start | bytes 786436
  0.0 4.6 %collective-permute-start.1 = (bf16[128,1024]{1,0:T(8,128)(2,1)}, bf16[128,1024]{1,0:T(8,128)(2,1)S(1)}, u32[]{:S(2)}, u32[]{:S(2)}) collective-permute-start(bf16[128,1024]{1,0:T(8,128)(2,1)} %refs_13_.1), channel_id=1, source_target_pairs={{0,4},{4,0},{8,12},{12,8},{1,5},{5,1},{9,13},{13,9},{2,6},{6,2},{1... | collective-permute-start | bytes 786440 | tf_op jit(solution)/shard_map/ppermute | solution.py:24
  0.5 11.3 %collective-permute-start = (bf16[128,1024]{1,0:T(8,128)(2,1)}, bf16[128,1024]{1,0:T(8,128)(2,1)S(1)}, u32[]{:S(2)}, u32[]{:S(2)}) collective-permute-start(bf16[128,1024]{1,0:T(8,128)(2,1)} %refs_13_.1), channel_id=1, source_target_pairs={{0,1},{1,0},{2,3},{3,2},{4,5},{5,4},{6,7},{7,6},{8,9},{9,8},{10,11... | collective-permute-start | bytes 786440 | tf_op jit(solution)/shard_map/ppermute | solution.py:24
  3.1 9.4 %collective-permute-start.3 = (bf16[128,1024]{1,0:T(8,128)(2,1)}, bf16[128,1024]{1,0:T(8,128)(2,1)S(1)}, u32[]{:S(2)}, u32[]{:S(2)}) collective-permute-start(bf16[128,1024]{1,0:T(8,128)(2,1)} %refs_13_.1), channel_id=1, source_target_pairs={{0,8},{4,12},{8,0},{12,4},{1,9},{5,13},{9,1},{13,5},{2,10},{6,14},... | collective-permute-start | bytes 786440 | tf_op jit(solution)/shard_map/ppermute | solution.py:24
  4.6 0.9 %copy-start.2 = (bf16[128,512]{1,0:T(8,128)(2,1)S(1)}, bf16[128,512]{1,0:T(8,128)(2,1)}, u32[]{:S(2)}) copy-start(bf16[128,512]{1,0:T(8,128)(2,1)} %values_ref) | copy-start | bytes 393220
  5.5 0.7 %copy-start.4 = (bf16[128]{0:T(256)(128)(2,1)S(1)}, bf16[128]{0:T(256)(128)(2,1)}, u32[]{:S(2)}) copy-start(bf16[128]{0:T(256)(128)(2,1)} %param.9) | copy-start | bytes 772
  6.3 1.9 %copy-start.3 = (s32[16,4]{0,1:T(4,128)S(1)}, s32[16,4]{0,1:T(4,128)}, u32[]{:S(2)}) copy-start(s32[16,4]{0,1:T(4,128)} %param.10) | copy-start | bytes 772
  6.3 2.6 %collective-permute-start.5 = (bf16[144,512]{1,0:T(8,128)(2,1)S(1)}, bf16[144,512]{1,0:T(8,128)(2,1)S(1)}, u32[]{:S(2)}, u32[]{:S(2)}) collective-permute-start(bf16[144,512]{1,0:T(8,128)(2,1)S(1)} %shard_map.65.refs_5_.refs_14_), channel_id=1, source_target_pairs={{0,4},{4,0},{8,12},{12,8},{1,5},{5,1},{9,13},{13,9},{2,6},{6,2},{1... | collective-permute-start | bytes 442376 | tf_op jit(solution)/shard_map/ppermute | solution.py:24
  6.4 7.5 %collective-permute-start.2 = (bf16[144,512]{1,0:T(8,128)(2,1)S(1)}, bf16[144,512]{1,0:T(8,128)(2,1)S(1)}, u32[]{:S(2)}, u32[]{:S(2)}) collective-permute-start(bf16[144,512]{1,0:T(8,128)(2,1)S(1)} %shard_map.65.refs_5_.refs_14_), channel_id=1, source_target_pairs={{0,1},{1,0},{2,3},{3,2},{4,5},{5,4},{6,7},{7,6},{8,9},{9,8},{10,11... | collective-permute-start | bytes 442376 | tf_op jit(solution)/shard_map/ppermute | solution.py:24
  6.9 8.7 %collective-permute-start.4 = (bf16[144,512]{1,0:T(8,128)(2,1)S(1)}, bf16[144,512]{1,0:T(8,128)(2,1)S(1)}, u32[]{:S(2)}, u32[]{:S(2)}) collective-permute-start(bf16[144,512]{1,0:T(8,128)(2,1)S(1)} %shard_map.65.refs_5_.refs_14_), channel_id=1, source_target_pairs={{0,8},{4,12},{8,0},{12,4},{1,9},{5,13},{9,1},{13,5},{2,10},{6,14},... | collective-permute-start | bytes 442376 | tf_op jit(solution)/shard_map/ppermute | solution.py:24
  8.2 0.7 %copy-start.5 = (s32[16]{0:T(128)S(1)}, s32[16]{0:T(128)}, u32[]{:S(2)}) copy-start(s32[16]{0:T(128)} %param.11) | copy-start | bytes 196
  8.9 12.4 %copy-start = (bf16[128,1024]{1,0:T(8,128)(2,1)S(1)}, bf16[128,1024]{1,0:T(8,128)(2,1)}, u32[]{:S(2)}) copy-start(bf16[128,1024]{1,0:T(8,128)(2,1)} %refs_13_.1) | copy-start | bytes 786436
  8.9 12.4 %collective-permute-start.8 = (bf16[128,1024]{1,0:T(8,128)(2,1)S(1)}, bf16[128,1024]{1,0:T(8,128)(2,1)S(1)}, u32[]{:S(2)}, u32[]{:S(2)}) collective-permute-start(bf16[128,1024]{1,0:T(8,128)(2,1)S(1)} %copy-done.1), channel_id=1, source_target_pairs={{0,3},{1,2},{2,1},{3,0},{4,7},{5,6},{6,5},{7,4},{8,11},{9,10},{10,... | collective-permute-start | bytes 786440 | tf_op jit(solution)/shard_map/ppermute | solution.py:24
  12.5 9.3 %collective-permute-start.6 = (bf16[128,1024]{1,0:T(8,128)(2,1)S(1)}, bf16[128,1024]{1,0:T(8,128)(2,1)S(1)}, u32[]{:S(2)}, u32[]{:S(2)}) collective-permute-start(bf16[128,1024]{1,0:T(8,128)(2,1)S(1)} %collective-permute-done.refs_0_), channel_id=1, source_target_pairs={{0,8},{4,12},{8,0},{12,4},{1,9},{5,13},{9,1},{13,5},{2,10},{6,14},... | collective-permute-start | bytes 786440 | tf_op jit(solution)/shard_map/ppermute | solution.py:24
  15.6 8.0 %collective-permute-start.7 = (bf16[144,512]{1,0:T(8,128)(2,1)S(1)}, bf16[144,512]{1,0:T(8,128)(2,1)S(1)}, u32[]{:S(2)}, u32[]{:S(2)}) collective-permute-start(bf16[144,512]{1,0:T(8,128)(2,1)S(1)} %collective-permute-done.2.refs_1_.refs_0_), channel_id=1, source_target_pairs={{0,8},{4,12},{8,0},{12,4},{1,9},{5,13},{9,1},{13,5},{2,10},{6,14},... | collective-permute-start | bytes 442376 | tf_op jit(solution)/shard_map/ppermute | solution.py:24
  17.1 7.0 %collective-permute-start.13 = (bf16[288,512]{1,0:T(8,128)(2,1)S(1)}, bf16[288,512]{1,0:T(8,128)(2,1)S(1)}, u32[]{:S(2)}, u32[]{:S(2)}) collective-permute-start(bf16[288,512]{1,0:T(8,128)(2,1)S(1)} %shard_map.67), channel_id=1, source_target_pairs={{0,4},{4,0},{8,12},{12,8},{1,5},{5,1},{9,13},{13,9},{2,6},{6,2},{1... | collective-permute-start | bytes 884744 | tf_op jit(solution)/shard_map/ppermute | solution.py:24
  17.2 6.9 %collective-permute-start.11 = (bf16[128,1024]{1,0:T(8,128)(2,1)S(1)}, bf16[128,1024]{1,0:T(8,128)(2,1)S(1)}, u32[]{:S(2)}, u32[]{:S(2)}) collective-permute-start(bf16[128,1024]{1,0:T(8,128)(2,1)S(1)} %collective-permute-done.refs_0_), channel_id=1, source_target_pairs={{0,4},{4,0},{8,12},{12,8},{1,5},{5,1},{9,13},{13,9},{2,6},{6,2},{1... | collective-permute-start | bytes 786440 | tf_op jit(solution)/shard_map/ppermute | solution.py:24
  21.3 2.8 %collective-permute-start.12 = (bf16[128,1024]{1,0:T(8,128)(2,1)S(1)}, bf16[128,1024]{1,0:T(8,128)(2,1)S(1)}, u32[]{:S(2)}, u32[]{:S(2)}) collective-permute-start(bf16[128,1024]{1,0:T(8,128)(2,1)S(1)} %collective-permute-done.3.refs_2_), channel_id=1, source_target_pairs={{0,4},{4,0},{8,12},{12,8},{1,5},{5,1},{9,13},{13,9},{2,6},{6,2},{1... | collective-permute-start | bytes 786440 | tf_op jit(solution)/shard_map/ppermute | solution.py:24
  23.6 1.8 %collective-permute-start.9 = (bf16[128,1024]{1,0:T(8,128)(2,1)S(1)}, bf16[128,1024]{1,0:T(8,128)(2,1)S(1)}, u32[]{:S(2)}, u32[]{:S(2)}) collective-permute-start(bf16[128,1024]{1,0:T(8,128)(2,1)S(1)} %collective-permute-done.6.refs_6_.refs_5_), channel_id=1, source_target_pairs={{0,4},{4,0},{8,12},{12,8},{1,5},{5,1},{9,13},{13,9},{2,6},{6,2},{1... | collective-permute-start | bytes 786440 | tf_op jit(solution)/shard_map/ppermute | solution.py:24
  23.6 1.7 %collective-permute-start.10 = (bf16[144,512]{1,0:T(8,128)(2,1)S(1)}, bf16[144,512]{1,0:T(8,128)(2,1)S(1)}, u32[]{:S(2)}, u32[]{:S(2)}) collective-permute-start(bf16[144,512]{1,0:T(8,128)(2,1)S(1)} %collective-permute-done.7.refs_7_.refs_6_), channel_id=1, source_target_pairs={{0,4},{4,0},{8,12},{12,8},{1,5},{5,1},{9,13},{13,9},{2,6},{6,2},{1... | collective-permute-start | bytes 442376 | tf_op jit(solution)/shard_map/ppermute | solution.py:24
  26.4 8.6 %collective-permute-start.14 = (bf16[144,512]{1,0:T(8,128)(2,1)S(1)}, bf16[144,512]{1,0:T(8,128)(2,1)S(1)}, u32[]{:S(2)}, u32[]{:S(2)}) collective-permute-start(bf16[144,512]{1,0:T(8,128)(2,1)S(1)} %shard_map.69), channel_id=1, source_target_pairs={{0,3},{1,2},{2,1},{3,0},{4,7},{5,6},{6,5},{7,4},{8,11},{9,10},{10,... | collective-permute-start | bytes 442376 | tf_op jit(solution)/shard_map/ppermute | solution.py:24

commit v21 on v20

--- a/solution.py
+++ b/solution.py
@@ -323,7 +323,7 @@
     )(*early_values)
     bundled_arrays = [swap(piece[1], "lib", 1) for piece in early] + [swap(bundle, "lib", 1)]
     late = [((1, 0), partner_keys, partner_values)] + relayed
-    late += cross_cores(relayed, [state[3] for state in states])
+    late += cross_cores(relayed)
     late_arrays = arrays_of(late) + bundled_arrays
     returned = []
     for (mask, _), state in zip(visitors, states):

time: 35.8 us -> 36.5 us (1.020)
  the two profiles are of different devices: /device:TPU:0 before, /device:TPU:11 now
where the time goes in v21:
time: 36.5 us; the launch traced here: 35.9 us
  starting transfers between devices  18 us (49%)
  waiting for transfers between devices  13.2 us (36%)
  Pallas kernels  2.29 us (6%)
  local copies, waits for them, and re-layouts  2.22 us (6%)
    ppermute x15, starting transfers between devices, swap(): return lax.ppermute(value, axis, [(i, i ^ mask) for i in range(length)])  18 us
    ppermute x15, waiting for transfers between devices, swap(): return lax.ppermute(value, axis, [(i, i ^ mask) for i in range(length)])  13.2 us
    unnamed x12, local copies, waits for them, and re-layouts  2.22 us
    pallas_call x1, Pallas kernels, body(): pl.pallas_call(merge_kernel, out_shape=jax.ShapeDtypeStruct((TILE, value_...  0.81 us
  transfers between devices with their start and end apart: 15, of which 7 were waited for; matrix products, arithmetic and copies ran while one was open for 0% of the time, Pallas kernels for 3%

profile of v21, /device:TPU:11, one launch (start us, length us, event | category | flops | bytes accessed | tf_op | source)
XLA Modules:
  0.0 35.9 jit_solution(1638555568211751163)
XLA Ops:
  0.0 0.7 %collective-permute-start.1 = (bf16[128,1024]{1,0:T(8,128)(2,1)}, bf16[128,1024]{1,0:T(8,128)(2,1)S(1)}, u32[]{:S(2)}, u32[]{:S(2)}) collective-permute-start(bf16[128,1024]{1,0:T(8,128)(2,1)} %refs_4_.1), channel_id=1, source_target_pairs={{0,4},{4,0},{8,12},{12,8},{1,5},{5,1},{9,13},{13,9},{2,6},{6,2},{1... | collective-permute-start | bytes 786440 | tf_op jit(solution)/shard_map/ppermute | solution.py:24
  0.7 0.2 collective-permute-start
  0.8 0.1 collective-permute-start.3
  0.9 1.1 %collective-permute-done.1.refs_4_.refs_3_ = bf16[128,1024]{1,0:T(8,128)(2,1)S(1)} collective-permute-done((bf16[128,1024]{1,0:T(8,128)(2,1)}, bf16[128,1024]{1,0:T(8,128)(2,1)S(1)}, u32[]{:S(2)}, u32[]{:S(2)}) %collective-permute-start.1) | collective-permute-done | bytes 262176 | tf_op jit(solution)/shard_map/ppermute | solution.py:24
  2.1 0.9 %copy-done.2 = bf16[128,512]{1,0:T(8,128)(2,1)S(1)} copy-done((bf16[128,512]{1,0:T(8,128)(2,1)S(1)}, bf16[128,512]{1,0:T(8,128)(2,1)}, u32[]{:S(2)}) %copy-start.2) | copy-done | bytes 131096
  3.0 0.7 %copy-done.4 = bf16[128]{0:T(256)(128)(2,1)S(1)} copy-done((bf16[128]{0:T(256)(128)(2,1)S(1)}, bf16[128]{0:T(256)(128)(2,1)}, u32[]{:S(2)}) %copy-start.4) | copy-done | bytes 280
  3.6 0.2 shard_map.65.refs_14_.refs_5_
  3.8 0.0 copy-start.3
  3.8 0.4 %collective-permute-start.5 = (bf16[144,512]{1,0:T(8,128)(2,1)S(1)}, bf16[144,512]{1,0:T(8,128)(2,1)S(1)}, u32[]{:S(2)}, u32[]{:S(2)}) collective-permute-start(bf16[144,512]{1,0:T(8,128)(2,1)S(1)} %shard_map.65.refs_14_.refs_5_), channel_id=1, source_target_pairs={{0,4},{4,0},{8,12},{12,8},{1,5},{5,1},{9,13},{13,9},{2,6},{6,2},{1... | collective-permute-start | bytes 442376 | tf_op jit(solution)/shard_map/ppermute | solution.py:24
  4.2 0.6 %collective-permute-start.2 = (bf16[144,512]{1,0:T(8,128)(2,1)S(1)}, bf16[144,512]{1,0:T(8,128)(2,1)S(1)}, u32[]{:S(2)}, u32[]{:S(2)}) collective-permute-start(bf16[144,512]{1,0:T(8,128)(2,1)S(1)} %shard_map.65.refs_14_.refs_5_), channel_id=1, source_target_pairs={{0,1},{1,0},{2,3},{3,2},{4,5},{5,4},{6,7},{7,6},{8,9},{9,8},{10,11... | collective-permute-start | bytes 442376 | tf_op jit(solution)/shard_map/ppermute | solution.py:24
  4.8 1.2 %collective-permute-start.4 = (bf16[144,512]{1,0:T(8,128)(2,1)S(1)}, bf16[144,512]{1,0:T(8,128)(2,1)S(1)}, u32[]{:S(2)}, u32[]{:S(2)}) collective-permute-start(bf16[144,512]{1,0:T(8,128)(2,1)S(1)} %shard_map.65.refs_14_.refs_5_), channel_id=1, source_target_pairs={{0,8},{4,12},{8,0},{12,4},{1,9},{5,13},{9,1},{13,5},{2,10},{6,14},... | collective-permute-start | bytes 442376 | tf_op jit(solution)/shard_map/ppermute | solution.py:24
  6.1 2.7 %collective-permute-done.refs_0_ = bf16[128,1024]{1,0:T(8,128)(2,1)S(1)} collective-permute-done((bf16[128,1024]{1,0:T(8,128)(2,1)}, bf16[128,1024]{1,0:T(8,128)(2,1)S(1)}, u32[]{:S(2)}, u32[]{:S(2)}) %collective-permute-start) | collective-permute-done | bytes 262176 | tf_op jit(solution)/shard_map/ppermute | solution.py:24
  8.8 0.0 collective-permute-done.3.refs_2_
  8.8 0.3 collective-permute-start.6
  9.0 0.7 %copy-done.5 = s32[16]{0:T(128)S(1)} copy-done((s32[16]{0:T(128)S(1)}, s32[16]{0:T(128)}, u32[]{:S(2)}) %copy-start.5) | copy-done | bytes 88
  9.7 2.3 %collective-permute-start.13 = (bf16[128,1024]{1,0:T(8,128)(2,1)S(1)}, bf16[128,1024]{1,0:T(8,128)(2,1)S(1)}, u32[]{:S(2)}, u32[]{:S(2)}) collective-permute-start(bf16[128,1024]{1,0:T(8,128)(2,1)S(1)} %copy-done.1), channel_id=1, source_target_pairs={{0,3},{1,2},{2,1},{3,0},{4,7},{5,6},{6,5},{7,4},{8,11},{9,10},{10,... | collective-permute-start | bytes 786440 | tf_op jit(solution)/shard_map/ppermute | solution.py:24
  12.0 1.2 %collective-permute-start.7 = (bf16[144,512]{1,0:T(8,128)(2,1)S(1)}, bf16[144,512]{1,0:T(8,128)(2,1)S(1)}, u32[]{:S(2)}, u32[]{:S(2)}) collective-permute-start(bf16[144,512]{1,0:T(8,128)(2,1)S(1)} %collective-permute-done.2.refs_0_.refs_1_), channel_id=1, source_target_pairs={{0,8},{4,12},{8,0},{12,4},{1,9},{5,13},{9,1},{13,5},{2,10},{6,14},... | collective-permute-start | bytes 442376 | tf_op jit(solution)/shard_map/ppermute | solution.py:24
  13.3 2.9 %collective-permute-start.12 = (bf16[288,512]{1,0:T(8,128)(2,1)S(1)}, bf16[288,512]{1,0:T(8,128)(2,1)S(1)}, u32[]{:S(2)}, u32[]{:S(2)}) collective-permute-start(bf16[288,512]{1,0:T(8,128)(2,1)S(1)} %shard_map.66), channel_id=1, source_target_pairs={{0,4},{4,0},{8,12},{12,8},{1,5},{5,1},{9,13},{13,9},{2,6},{6,2},{1... | collective-permute-start | bytes 884744 | tf_op jit(solution)/shard_map/ppermute | solution.py:24
  16.1 0.1 collective-permute-start.10
  16.2 0.7 %collective-permute-done.6.refs_6_.refs_5_ = bf16[128,1024]{1,0:T(8,128)(2,1)S(1)} collective-permute-done((bf16[128,1024]{1,0:T(8,128)(2,1)S(1)}, bf16[128,1024]{1,0:T(8,128)(2,1)S(1)}, u32[]{:S(2)}, u32[]{:S(2)}) %collective-permute-start.6) | collective-permute-done | bytes 262176 | tf_op jit(solution)/shard_map/ppermute | solution.py:24
  16.9 2.9 %collective-permute-start.11 = (bf16[128,1024]{1,0:T(8,128)(2,1)S(1)}, bf16[128,1024]{1,0:T(8,128)(2,1)S(1)}, u32[]{:S(2)}, u32[]{:S(2)}) collective-permute-start(bf16[128,1024]{1,0:T(8,128)(2,1)S(1)} %collective-permute-done.3.refs_2_), channel_id=1, source_target_pairs={{0,4},{4,0},{8,12},{12,8},{1,5},{5,1},{9,13},{13,9},{2,6},{6,2},{1... | collective-permute-start | bytes 786440 | tf_op jit(solution)/shard_map/ppermute | solution.py:24
  19.8 0.3 collective-permute-done.7.refs_7_.refs_6_
  20.1 1.6 %collective-permute-start.8 = (bf16[128,1024]{1,0:T(8,128)(2,1)S(1)}, bf16[128,1024]{1,0:T(8,128)(2,1)S(1)}, u32[]{:S(2)}, u32[]{:S(2)}) collective-permute-start(bf16[128,1024]{1,0:T(8,128)(2,1)S(1)} %collective-permute-done.6.refs_6_.refs_5_), channel_id=1, source_target_pairs={{0,4},{4,0},{8,12},{12,8},{1,5},{5,1},{9,13},{13,9},{2,6},{6,2},{1... | collective-permute-start | bytes 786440 | tf_op jit(solution)/shard_map/ppermute | solution.py:24
  21.7 1.7 %collective-permute-done.13.query_ref = bf16[128,1024]{1,0:T(8,128)(2,1)S(1)} collective-permute-done((bf16[128,1024]{1,0:T(8,128)(2,1)S(1)}, bf16[128,1024]{1,0:T(8,128)(2,1)S(1)}, u32[]{:S(2)}, u32[]{:S(2)}) %collective-permute-start.13) | collective-permute-done | bytes 262176 | tf_op jit(solution)/shard_map/ppermute | solution.py:24
  23.4 1.5 %collective-permute-start.9 = (bf16[144,512]{1,0:T(8,128)(2,1)S(1)}, bf16[144,512]{1,0:T(8,128)(2,1)S(1)}, u32[]{:S(2)}, u32[]{:S(2)}) collective-permute-start(bf16[144,512]{1,0:T(8,128)(2,1)S(1)} %collective-permute-done.7.refs_7_.refs_6_), channel_id=1, source_target_pairs={{0,4},{4,0},{8,12},{12,8},{1,5},{5,1},{9,13},{13,9},{2,6},{6,2},{1... | collective-permute-start | bytes 442376 | tf_op jit(solution)/shard_map/ppermute | solution.py:24
  24.9 0.4 %shard_map.68 = (bf16[1024,128]{1,0:T(8,128)(2,1)S(1)}, f32[128,512]{1,0:T(8,128)S(1)}, f32[128,128]{1,0:T(8,128)S(1)}, f32[128,128]{1,0:T(8,128)S(1)}) custom-call(s32[2,16]{1,0:T(2,128)S(1)} %shard_map.64.windows_ref, bf16[128,1024]{1,0:T(8,128)(2,1)S(1)} %collective-permute-done.13.query_ref, bf16[128,1024]{1,0:T(8,128)(2,1)S(1)} %collective-permute-done.refs_0_, ...), custom_call_target="tpu_custom_call" | custom-call | flops 268435456 | bytes 4194304 | tf_op jit(solution)/shard_map/pallas_call | solution.py:304
  25.3 0.6 %collective-permute-done.9.refs_9_.refs_8_ = bf16[144,512]{1,0:T(8,128)(2,1)S(1)} collective-permute-done((bf16[144,512]{1,0:T(8,128)(2,1)S(1)}, bf16[144,512]{1,0:T(8,128)(2,1)S(1)}, u32[]{:S(2)}, u32[]{:S(2)}) %collective-permute-start.9) | collective-permute-done | bytes 147488 | tf_op jit(solution)/shard_map/ppermute | solution.py:24
  25.9 0.5 %shard_map.69 = bf16[144,512]{1,0:T(8,128)(2,1)S(1)} custom-call(s32[2,16]{1,0:T(2,128)S(1)} %shard_map.64.windows_ref, bf16[1024,128]{1,0:T(8,128)(2,1)S(1)} %get-tuple-element.25.turned_ref, f32[128,512]{1,0:T(8,128)S(1)} %get-tuple-element.26.refs_0_, f32[128,128]{1,0:T(8,128)S(1)} %get-tuple-element.27.refs_1_, ...), custom_call_target="tpu_custom_call" | custom-call | flops 268435456 | bytes 4194304 | tf_op jit(solution)/shard_map/pallas_call | solution.py:330
  26.4 2.1 %collective-permute-start.14 = (bf16[144,512]{1,0:T(8,128)(2,1)S(1)}, bf16[144,512]{1,0:T(8,128)(2,1)S(1)}, u32[]{:S(2)}, u32[]{:S(2)}) collective-permute-start(bf16[144,512]{1,0:T(8,128)(2,1)S(1)} %shard_map.69), channel_id=1, source_target_pairs={{0,3},{1,2},{2,1},{3,0},{4,7},{5,6},{6,5},{7,4},{8,11},{9,10},{10,... | collective-permute-start | bytes 442376 | tf_op jit(solution)/shard_map/ppermute | solution.py:24
  28.5 0.4 %shard_map.67 = (f32[128,512]{1,0:T(8,128)S(1)}, f32[2,128,128]{2,1,0:T(8,128)S(1)}) custom-call(s32[2,16]{1,0:T(2,128)S(1)} %shard_map.64.windows_ref, bf16[128,1024]{1,0:T(8,128)(2,1)S(1)} %copy-done.1, bf16[128,1024]{1,0:T(8,128)(2,1)S(1)} %collective-permute-done.refs_0_, bf16[144,512]{1,0:T(8,128)(2,1)S(1)} %collective-permute-done.2.refs_0_.refs_1_, ...), custom_call_target="tpu_custom_call" | custom-call | flops 268435456 | bytes 4194304 | tf_op jit(solution)/shard_map/pallas_call | solution.py:345
  28.9 6.1 %collective-permute-done.14.refs_0_ = bf16[144,512]{1,0:T(8,128)(2,1)S(1)} collective-permute-done((bf16[144,512]{1,0:T(8,128)(2,1)S(1)}, bf16[144,512]{1,0:T(8,128)(2,1)S(1)}, u32[]{:S(2)}, u32[]{:S(2)}) %collective-permute-start.14) | collective-permute-done | bytes 147488 | tf_op jit(solution)/shard_map/ppermute | solution.py:24
  35.1 0.8 %shard_map.70 = bf16[128,512]{1,0:T(8,128)(2,1)} custom-call(f32[128,512]{1,0:T(8,128)S(1)} %get-tuple-element.22.total_ref, f32[2,128,128]{2,1,0:T(8,128)S(1)} %get-tuple-element.23.stats_ref, bf16[144,512]{1,0:T(8,128)(2,1)S(1)} %collective-permute-done.14.refs_0_), custom_call_target="tpu_custom_call" | custom-call | tf_op jit(solution)/shard_map/pallas_call | solution.py:359
  (17 shorter events, 0.1 us)
Async XLA Ops:
  0.0 9.7 %copy-start.1 = (bf16[128,1024]{1,0:T(8,128)(2,1)S(1)}, bf16[128,1024]{1,0:T(8,128)(2,1)}, u32[]{:S(2)}) copy-start(bf16[128,1024]{1,0:T(8,128)(2,1)} %query_ref.1) | copy-start | bytes 786436
  0.0 2.0 %collective-permute-start.1 = (bf16[128,1024]{1,0:T(8,128)(2,1)}, bf16[128,1024]{1,0:T(8,128)(2,1)S(1)}, u32[]{:S(2)}, u32[]{:S(2)}) collective-permute-start(bf16[128,1024]{1,0:T(8,128)(2,1)} %refs_4_.1), channel_id=1, source_target_pairs={{0,4},{4,0},{8,12},{12,8},{1,5},{5,1},{9,13},{13,9},{2,6},{6,2},{1... | collective-permute-start | bytes 786440 | tf_op jit(solution)/shard_map/ppermute | solution.py:24
  0.7 8.1 %collective-permute-start = (bf16[128,1024]{1,0:T(8,128)(2,1)}, bf16[128,1024]{1,0:T(8,128)(2,1)S(1)}, u32[]{:S(2)}, u32[]{:S(2)}) collective-permute-start(bf16[128,1024]{1,0:T(8,128)(2,1)} %refs_4_.1), channel_id=1, source_target_pairs={{0,1},{1,0},{2,3},{3,2},{4,5},{5,4},{6,7},{7,6},{8,9},{9,8},{10,11... | collective-permute-start | bytes 786440 | tf_op jit(solution)/shard_map/ppermute | solution.py:24
  0.8 7.9 %collective-permute-start.3 = (bf16[128,1024]{1,0:T(8,128)(2,1)}, bf16[128,1024]{1,0:T(8,128)(2,1)S(1)}, u32[]{:S(2)}, u32[]{:S(2)}) collective-permute-start(bf16[128,1024]{1,0:T(8,128)(2,1)} %refs_4_.1), channel_id=1, source_target_pairs={{0,8},{4,12},{8,0},{12,4},{1,9},{5,13},{9,1},{13,5},{2,10},{6,14},... | collective-permute-start | bytes 786440 | tf_op jit(solution)/shard_map/ppermute | solution.py:24
  2.1 0.9 %copy-start.2 = (bf16[128,512]{1,0:T(8,128)(2,1)S(1)}, bf16[128,512]{1,0:T(8,128)(2,1)}, u32[]{:S(2)}) copy-start(bf16[128,512]{1,0:T(8,128)(2,1)} %values_ref) | copy-start | bytes 393220
  3.0 0.7 %copy-start.4 = (bf16[128]{0:T(256)(128)(2,1)S(1)}, bf16[128]{0:T(256)(128)(2,1)}, u32[]{:S(2)}) copy-start(bf16[128]{0:T(256)(128)(2,1)} %param.9) | copy-start | bytes 772
  3.8 5.2 %copy-start.3 = (s32[16,4]{0,1:T(4,128)S(1)}, s32[16,4]{0,1:T(4,128)}, u32[]{:S(2)}) copy-start(s32[16,4]{0,1:T(4,128)} %param.10) | copy-start | bytes 772
  3.8 5.9 %collective-permute-start.5 = (bf16[144,512]{1,0:T(8,128)(2,1)S(1)}, bf16[144,512]{1,0:T(8,128)(2,1)S(1)}, u32[]{:S(2)}, u32[]{:S(2)}) collective-permute-start(bf16[144,512]{1,0:T(8,128)(2,1)S(1)} %shard_map.65.refs_14_.refs_5_), channel_id=1, source_target_pairs={{0,4},{4,0},{8,12},{12,8},{1,5},{5,1},{9,13},{13,9},{2,6},{6,2},{1... | collective-permute-start | bytes 442376 | tf_op jit(solution)/shard_map/ppermute | solution.py:24
  4.2 7.8 %collective-permute-start.2 = (bf16[144,512]{1,0:T(8,128)(2,1)S(1)}, bf16[144,512]{1,0:T(8,128)(2,1)S(1)}, u32[]{:S(2)}, u32[]{:S(2)}) collective-permute-start(bf16[144,512]{1,0:T(8,128)(2,1)S(1)} %shard_map.65.refs_14_.refs_5_), channel_id=1, source_target_pairs={{0,1},{1,0},{2,3},{3,2},{4,5},{5,4},{6,7},{7,6},{8,9},{9,8},{10,11... | collective-permute-start | bytes 442376 | tf_op jit(solution)/shard_map/ppermute | solution.py:24
  4.8 7.2 %collective-permute-start.4 = (bf16[144,512]{1,0:T(8,128)(2,1)S(1)}, bf16[144,512]{1,0:T(8,128)(2,1)S(1)}, u32[]{:S(2)}, u32[]{:S(2)}) collective-permute-start(bf16[144,512]{1,0:T(8,128)(2,1)S(1)} %shard_map.65.refs_14_.refs_5_), channel_id=1, source_target_pairs={{0,8},{4,12},{8,0},{12,4},{1,9},{5,13},{9,1},{13,5},{2,10},{6,14},... | collective-permute-start | bytes 442376 | tf_op jit(solution)/shard_map/ppermute | solution.py:24
  8.8 8.2 %collective-permute-start.6 = (bf16[128,1024]{1,0:T(8,128)(2,1)S(1)}, bf16[128,1024]{1,0:T(8,128)(2,1)S(1)}, u32[]{:S(2)}, u32[]{:S(2)}) collective-permute-start(bf16[128,1024]{1,0:T(8,128)(2,1)S(1)} %collective-permute-done.refs_0_), channel_id=1, source_target_pairs={{0,8},{4,12},{8,0},{12,4},{1,9},{5,13},{9,1},{13,5},{2,10},{6,14},... | collective-permute-start | bytes 786440 | tf_op jit(solution)/shard_map/ppermute | solution.py:24
  9.0 0.7 %copy-start.5 = (s32[16]{0:T(128)S(1)}, s32[16]{0:T(128)}, u32[]{:S(2)}) copy-start(s32[16]{0:T(128)} %param.11) | copy-start | bytes 196
  9.7 15.2 %copy-start = (bf16[128,1024]{1,0:T(8,128)(2,1)S(1)}, bf16[128,1024]{1,0:T(8,128)(2,1)}, u32[]{:S(2)}) copy-start(bf16[128,1024]{1,0:T(8,128)(2,1)} %refs_4_.1) | copy-start | bytes 786436
  9.7 13.7 %collective-permute-start.13 = (bf16[128,1024]{1,0:T(8,128)(2,1)S(1)}, bf16[128,1024]{1,0:T(8,128)(2,1)S(1)}, u32[]{:S(2)}, u32[]{:S(2)}) collective-permute-start(bf16[128,1024]{1,0:T(8,128)(2,1)S(1)} %copy-done.1), channel_id=1, source_target_pairs={{0,3},{1,2},{2,1},{3,0},{4,7},{5,6},{6,5},{7,4},{8,11},{9,10},{10,... | collective-permute-start | bytes 786440 | tf_op jit(solution)/shard_map/ppermute | solution.py:24
  12.0 8.0 %collective-permute-start.7 = (bf16[144,512]{1,0:T(8,128)(2,1)S(1)}, bf16[144,512]{1,0:T(8,128)(2,1)S(1)}, u32[]{:S(2)}, u32[]{:S(2)}) collective-permute-start(bf16[144,512]{1,0:T(8,128)(2,1)S(1)} %collective-permute-done.2.refs_0_.refs_1_), channel_id=1, source_target_pairs={{0,8},{4,12},{8,0},{12,4},{1,9},{5,13},{9,1},{13,5},{2,10},{6,14},... | collective-permute-start | bytes 442376 | tf_op jit(solution)/shard_map/ppermute | solution.py:24
  13.3 12.6 %collective-permute-start.12 = (bf16[288,512]{1,0:T(8,128)(2,1)S(1)}, bf16[288,512]{1,0:T(8,128)(2,1)S(1)}, u32[]{:S(2)}, u32[]{:S(2)}) collective-permute-start(bf16[288,512]{1,0:T(8,128)(2,1)S(1)} %shard_map.66), channel_id=1, source_target_pairs={{0,4},{4,0},{8,12},{12,8},{1,5},{5,1},{9,13},{13,9},{2,6},{6,2},{1... | collective-permute-start | bytes 884744 | tf_op jit(solution)/shard_map/ppermute | solution.py:24
  16.1 9.2 %collective-permute-start.10 = (bf16[128,1024]{1,0:T(8,128)(2,1)S(1)}, bf16[128,1024]{1,0:T(8,128)(2,1)S(1)}, u32[]{:S(2)}, u32[]{:S(2)}) collective-permute-start(bf16[128,1024]{1,0:T(8,128)(2,1)S(1)} %collective-permute-done.refs_0_), channel_id=1, source_target_pairs={{0,4},{4,0},{8,12},{12,8},{1,5},{5,1},{9,13},{13,9},{2,6},{6,2},{1... | collective-permute-start | bytes 786440 | tf_op jit(solution)/shard_map/ppermute | solution.py:24
  16.9 8.4 %collective-permute-start.11 = (bf16[128,1024]{1,0:T(8,128)(2,1)S(1)}, bf16[128,1024]{1,0:T(8,128)(2,1)S(1)}, u32[]{:S(2)}, u32[]{:S(2)}) collective-permute-start(bf16[128,1024]{1,0:T(8,128)(2,1)S(1)} %collective-permute-done.3.refs_2_), channel_id=1, source_target_pairs={{0,4},{4,0},{8,12},{12,8},{1,5},{5,1},{9,13},{13,9},{2,6},{6,2},{1... | collective-permute-start | bytes 786440 | tf_op jit(solution)/shard_map/ppermute | solution.py:24
  20.1 5.8 %collective-permute-start.8 = (bf16[128,1024]{1,0:T(8,128)(2,1)S(1)}, bf16[128,1024]{1,0:T(8,128)(2,1)S(1)}, u32[]{:S(2)}, u32[]{:S(2)}) collective-permute-start(bf16[128,1024]{1,0:T(8,128)(2,1)S(1)} %collective-permute-done.6.refs_6_.refs_5_), channel_id=1, source_target_pairs={{0,4},{4,0},{8,12},{12,8},{1,5},{5,1},{9,13},{13,9},{2,6},{6,2},{1... | collective-permute-start | bytes 786440 | tf_op jit(solution)/shard_map/ppermute | solution.py:24
  23.4 2.5 %collective-permute-start.9 = (bf16[144,512]{1,0:T(8,128)(2,1)S(1)}, bf16[144,512]{1,0:T(8,128)(2,1)S(1)}, u32[]{:S(2)}, u32[]{:S(2)}) collective-permute-start(bf16[144,512]{1,0:T(8,128)(2,1)S(1)} %collective-permute-done.7.refs_7_.refs_6_), channel_id=1, source_target_pairs={{0,4},{4,0},{8,12},{12,8},{1,5},{5,1},{9,13},{13,9},{2,6},{6,2},{1... | collective-permute-start | bytes 442376 | tf_op jit(solution)/shard_map/ppermute | solution.py:24
  26.4 8.7 %collective-permute-start.14 = (bf16[144,512]{1,0:T(8,128)(2,1)S(1)}, bf16[144,512]{1,0:T(8,128)(2,1)S(1)}, u32[]{:S(2)}, u32[]{:S(2)}) collective-permute-start(bf16[144,512]{1,0:T(8,128)(2,1)S(1)} %shard_map.69), channel_id=1, source_target_pairs={{0,3},{1,2},{2,1},{3,0},{4,7},{5,6},{6,5},{7,4},{8,11},{9,10},{10,... | collective-permute-start | bytes 442376 | tf_op jit(solution)/shard_map/ppermute | solution.py:24

commit v22 on v20

--- a/solution.py
+++ b/solution.py
@@ -233,8 +233,6 @@
         steps.append(("lib", mask))
         mask //= 2
     partner_values = swap(values, "lib", 1)
-    leaving, *_ = tie(queries, partner_values, windows)
-    visitors = [swap(leaving, "qry", mask) for mask in masks]
     early, late = [], []
     for axis, mask in steps:
         place = (0, mask) if axis == "qry" else (mask, 0)
@@ -246,6 +244,8 @@
             place = (lib_mask | mask, qry_mask)
             relayed.append((place, swap(far_keys, axis, mask), swap(far_values, axis, mask)))
         early, late = early + late + [near], relayed
+    leaving, *_ = tie(queries, partner_values, windows, early[-1][1])
+    visitors = [swap(leaving, "qry", mask) for mask in masks]
     return early, late, partner_values, list(zip(masks, visitors))
 
 

time: 35.8 us -> 37.1 us (1.036)
  waiting for transfers between devices: 11.4 us -> 13.5 us
  Pallas kernels: 3.73 us -> 3.19 us
    ppermute x15, waiting for transfers between devices: 11.4 us -> 13.5 us  [swap(): return lax.ppermute(value, axis, [(i, i ^ mask) for i in range(length)])]
    pallas_call x1, Pallas kernels: 1.02 us -> 0.48 us  [body(): pl.pallas_call(functools.partial(late_kernel, places_of(late), bundled, m...]
    pallas_call x1, Pallas kernels: 0.4 us -> 0.85 us  [body(): pl.pallas_call(functools.partial(early_kernel, places_of(early), mask), o...]
    pallas_call x1, Pallas kernels: 1.31 us -> 0.88 us  [body(): pl.pallas_call(functools.partial(home_kernel, places_of(early + late), bu...]
  transfers between devices with their start and end apart: 15 -> 15, of which waited for: 6 -> 5; matrix products, arithmetic and copies ran while one was open for 0% -> 0% of each run, Pallas kernels for 5% -> 5%
where the time goes in v22:
time: 37.1 us; the launch traced here: 37 us
  starting transfers between devices  18.1 us (49%)
  waiting for transfers between devices  13.5 us (36%)
  Pallas kernels  3.19 us (9%)
  local copies, waits for them, and re-layouts  2.23 us (6%)
    ppermute x15, starting transfers between devices, swap(): return lax.ppermute(value, axis, [(i, i ^ mask) for i in range(length)])  18.1 us
    ppermute x15, waiting for transfers between devices, swap(): return lax.ppermute(value, axis, [(i, i ^ mask) for i in range(length)])  13.5 us
    unnamed x12, local copies, waits for them, and re-layouts  2.23 us
    pallas_call x1, Pallas kernels, body(): pl.pallas_call(functools.partial(home_kernel, places_of(early + late), bu...  0.88 us
    pallas_call x1, Pallas kernels, body(): pl.pallas_call(functools.partial(early_kernel, places_of(early), mask), o...  0.85 us
    pallas_call x1, Pallas kernels, body(): pl.pallas_call(merge_kernel, out_shape=jax.ShapeDtypeStruct((TILE, value_...  0.81 us
  transfers between devices with their start and end apart: 15, of which 5 were waited for; matrix products, arithmetic and copies ran while one was open for 0% of the time, Pallas kernels for 5%

profile of v22, /device:TPU:0, one launch (start us, length us, event | category | flops | bytes accessed | tf_op | source)
XLA Modules:
  0.0 37.0 jit_solution(15516430841202764567)
XLA Ops:
  0.0 0.5 %collective-permute-start.1 = (bf16[128,1024]{1,0:T(8,128)(2,1)}, bf16[128,1024]{1,0:T(8,128)(2,1)S(1)}, u32[]{:S(2)}, u32[]{:S(2)}) collective-permute-start(bf16[128,1024]{1,0:T(8,128)(2,1)} %refs_13_.1), channel_id=1, source_target_pairs={{0,4},{4,0},{8,12},{12,8},{1,5},{5,1},{9,13},{13,9},{2,6},{6,2},{1... | collective-permute-start | bytes 786440 | tf_op jit(solution)/shard_map/ppermute | solution.py:24
  0.5 2.5 %collective-permute-start.3 = (bf16[128,1024]{1,0:T(8,128)(2,1)}, bf16[128,1024]{1,0:T(8,128)(2,1)S(1)}, u32[]{:S(2)}, u32[]{:S(2)}) collective-permute-start(bf16[128,1024]{1,0:T(8,128)(2,1)} %refs_13_.1), channel_id=1, source_target_pairs={{0,8},{4,12},{8,0},{12,4},{1,9},{5,13},{9,1},{13,5},{2,10},{6,14},... | collective-permute-start | bytes 786440 | tf_op jit(solution)/shard_map/ppermute | solution.py:24
  3.0 1.6 %collective-permute-start = (bf16[128,1024]{1,0:T(8,128)(2,1)}, bf16[128,1024]{1,0:T(8,128)(2,1)S(1)}, u32[]{:S(2)}, u32[]{:S(2)}) collective-permute-start(bf16[128,1024]{1,0:T(8,128)(2,1)} %refs_13_.1), channel_id=1, source_target_pairs={{0,1},{1,0},{2,3},{3,2},{4,5},{5,4},{6,7},{7,6},{8,9},{9,8},{10,11... | collective-permute-start | bytes 786440 | tf_op jit(solution)/shard_map/ppermute | solution.py:24
  4.6 0.0 collective-permute-done.1.refs_4_.refs_3_
  4.6 0.9 %copy-done.2 = bf16[128,512]{1,0:T(8,128)(2,1)S(1)} copy-done((bf16[128,512]{1,0:T(8,128)(2,1)S(1)}, bf16[128,512]{1,0:T(8,128)(2,1)}, u32[]{:S(2)}) %copy-start.2) | copy-done | bytes 131096
  5.5 0.7 %copy-done.4 = bf16[128]{0:T(256)(128)(2,1)S(1)} copy-done((bf16[128]{0:T(256)(128)(2,1)S(1)}, bf16[128]{0:T(256)(128)(2,1)}, u32[]{:S(2)}) %copy-start.4) | copy-done | bytes 280
  6.1 0.2 shard_map.65.refs_5_.refs_14_
  6.3 0.0 copy-start.3
  6.3 0.1 collective-permute-start.5
  6.4 0.5 %collective-permute-start.2 = (bf16[144,512]{1,0:T(8,128)(2,1)S(1)}, bf16[144,512]{1,0:T(8,128)(2,1)S(1)}, u32[]{:S(2)}, u32[]{:S(2)}) collective-permute-start(bf16[144,512]{1,0:T(8,128)(2,1)S(1)} %shard_map.65.refs_5_.refs_14_), channel_id=1, source_target_pairs={{0,1},{1,0},{2,3},{3,2},{4,5},{5,4},{6,7},{7,6},{8,9},{9,8},{10,11... | collective-permute-start | bytes 442376 | tf_op jit(solution)/shard_map/ppermute | solution.py:24
  6.9 1.3 %collective-permute-start.4 = (bf16[144,512]{1,0:T(8,128)(2,1)S(1)}, bf16[144,512]{1,0:T(8,128)(2,1)S(1)}, u32[]{:S(2)}, u32[]{:S(2)}) collective-permute-start(bf16[144,512]{1,0:T(8,128)(2,1)S(1)} %shard_map.65.refs_5_.refs_14_), channel_id=1, source_target_pairs={{0,8},{4,12},{8,0},{12,4},{1,9},{5,13},{9,1},{13,5},{2,10},{6,14},... | collective-permute-start | bytes 442376 | tf_op jit(solution)/shard_map/ppermute | solution.py:24
  8.2 0.7 %copy-done.5 = s32[16]{0:T(128)S(1)} copy-done((s32[16]{0:T(128)S(1)}, s32[16]{0:T(128)}, u32[]{:S(2)}) %copy-start.5) | copy-done | bytes 88
  8.9 1.5 %collective-permute-done.3.refs_2_ = bf16[128,1024]{1,0:T(8,128)(2,1)S(1)} collective-permute-done((bf16[128,1024]{1,0:T(8,128)(2,1)}, bf16[128,1024]{1,0:T(8,128)(2,1)S(1)}, u32[]{:S(2)}, u32[]{:S(2)}) %collective-permute-start.3) | collective-permute-done | bytes 262176 | tf_op jit(solution)/shard_map/ppermute | solution.py:24
  10.4 0.0 collective-permute-done.5.refs_5_.refs_4_
  10.4 4.1 %collective-permute-start.8 = (bf16[128,1024]{1,0:T(8,128)(2,1)S(1)}, bf16[128,1024]{1,0:T(8,128)(2,1)S(1)}, u32[]{:S(2)}, u32[]{:S(2)}) collective-permute-start(bf16[128,1024]{1,0:T(8,128)(2,1)S(1)} %copy-done.1), channel_id=1, source_target_pairs={{0,3},{1,2},{2,1},{3,0},{4,7},{5,6},{6,5},{7,4},{8,11},{9,10},{10,... | collective-permute-start | bytes 786440 | tf_op jit(solution)/shard_map/ppermute | solution.py:24
  14.4 0.0 collective-permute-done.refs_0_
  14.4 1.5 %collective-permute-start.6 = (bf16[128,1024]{1,0:T(8,128)(2,1)S(1)}, bf16[128,1024]{1,0:T(8,128)(2,1)S(1)}, u32[]{:S(2)}, u32[]{:S(2)}) collective-permute-start(bf16[128,1024]{1,0:T(8,128)(2,1)S(1)} %collective-permute-done.refs_0_), channel_id=1, source_target_pairs={{0,8},{4,12},{8,0},{12,4},{1,9},{5,13},{9,1},{13,5},{2,10},{6,14},... | collective-permute-start | bytes 786440 | tf_op jit(solution)/shard_map/ppermute | solution.py:24
  15.9 0.0 collective-permute-done.2.refs_1_.refs_0_
  15.9 0.0 collective-permute-done.4.refs_3_.refs_1_
  15.9 0.5 %collective-permute-start.7 = (bf16[144,512]{1,0:T(8,128)(2,1)S(1)}, bf16[144,512]{1,0:T(8,128)(2,1)S(1)}, u32[]{:S(2)}, u32[]{:S(2)}) collective-permute-start(bf16[144,512]{1,0:T(8,128)(2,1)S(1)} %collective-permute-done.2.refs_1_.refs_0_), channel_id=1, source_target_pairs={{0,8},{4,12},{8,0},{12,4},{1,9},{5,13},{9,1},{13,5},{2,10},{6,14},... | collective-permute-start | bytes 442376 | tf_op jit(solution)/shard_map/ppermute | solution.py:24
  16.5 0.1 collective-permute-start.13
  16.6 0.5 %collective-permute-start.12 = (bf16[128,1024]{1,0:T(8,128)(2,1)S(1)}, bf16[128,1024]{1,0:T(8,128)(2,1)S(1)}, u32[]{:S(2)}, u32[]{:S(2)}) collective-permute-start(bf16[128,1024]{1,0:T(8,128)(2,1)S(1)} %collective-permute-done.3.refs_2_), channel_id=1, source_target_pairs={{0,4},{4,0},{8,12},{12,8},{1,5},{5,1},{9,13},{13,9},{2,6},{6,2},{1... | collective-permute-start | bytes 786440 | tf_op jit(solution)/shard_map/ppermute | solution.py:24
  17.1 5.4 %collective-permute-done.8.query_ref = bf16[128,1024]{1,0:T(8,128)(2,1)S(1)} collective-permute-done((bf16[128,1024]{1,0:T(8,128)(2,1)S(1)}, bf16[128,1024]{1,0:T(8,128)(2,1)S(1)}, u32[]{:S(2)}, u32[]{:S(2)}) %collective-permute-start.8) | collective-permute-done | bytes 262176 | tf_op jit(solution)/shard_map/ppermute | solution.py:24
  22.5 0.8 %shard_map.66 = (bf16[1024,128]{1,0:T(8,128)(2,1)S(1)}, f32[128,512]{1,0:T(8,128)S(1)}, f32[128,128]{1,0:T(8,128)S(1)}, f32[128,128]{1,0:T(8,128)S(1)}) custom-call(s32[2,16]{1,0:T(2,128)S(1)} %shard_map.64.windows_ref, bf16[128,1024]{1,0:T(8,128)(2,1)S(1)} %collective-permute-done.8.query_ref, bf16[128,1024]{1,0:T(8,128)(2,1)S(1)} %collective-permute-done.refs_0_, ...), custom_call_target="tpu_custom_call" | custom-call | flops 268435456 | bytes 4194304 | tf_op jit(solution)/shard_map/pallas_call | solution.py:304
  23.4 1.4 %collective-permute-done.7.refs_7_.refs_6_ = bf16[144,512]{1,0:T(8,128)(2,1)S(1)} collective-permute-done((bf16[144,512]{1,0:T(8,128)(2,1)S(1)}, bf16[144,512]{1,0:T(8,128)(2,1)S(1)}, u32[]{:S(2)}, u32[]{:S(2)}) %collective-permute-start.7) | collective-permute-done | bytes 147488 | tf_op jit(solution)/shard_map/ppermute | solution.py:24
  24.8 0.5 %collective-permute-start.10 = (bf16[144,512]{1,0:T(8,128)(2,1)S(1)}, bf16[144,512]{1,0:T(8,128)(2,1)S(1)}, u32[]{:S(2)}, u32[]{:S(2)}) collective-permute-start(bf16[144,512]{1,0:T(8,128)(2,1)S(1)} %collective-permute-done.7.refs_7_.refs_6_), channel_id=1, source_target_pairs={{0,4},{4,0},{8,12},{12,8},{1,5},{5,1},{9,13},{13,9},{2,6},{6,2},{1... | collective-permute-start | bytes 442376 | tf_op jit(solution)/shard_map/ppermute | solution.py:24
  25.3 1.2 %collective-permute-done.10.refs_9_.refs_8_ = bf16[144,512]{1,0:T(8,128)(2,1)S(1)} collective-permute-done((bf16[144,512]{1,0:T(8,128)(2,1)S(1)}, bf16[144,512]{1,0:T(8,128)(2,1)S(1)}, u32[]{:S(2)}, u32[]{:S(2)}) %collective-permute-start.10) | collective-permute-done | bytes 147488 | tf_op jit(solution)/shard_map/ppermute | solution.py:24
  26.5 0.5 %shard_map.69 = bf16[144,512]{1,0:T(8,128)(2,1)S(1)} custom-call(s32[2,16]{1,0:T(2,128)S(1)} %shard_map.64.windows_ref, bf16[1024,128]{1,0:T(8,128)(2,1)S(1)} %get-tuple-element.26.turned_ref, f32[128,512]{1,0:T(8,128)S(1)} %get-tuple-element.27.refs_0_, f32[128,128]{1,0:T(8,128)S(1)} %get-tuple-element.28.refs_1_, ...), custom_call_target="tpu_custom_call" | custom-call | flops 268435456 | bytes 4194304 | tf_op jit(solution)/shard_map/pallas_call | solution.py:330
  27.0 4.4 %collective-permute-start.14 = (bf16[144,512]{1,0:T(8,128)(2,1)S(1)}, bf16[144,512]{1,0:T(8,128)(2,1)S(1)}, u32[]{:S(2)}, u32[]{:S(2)}) collective-permute-start(bf16[144,512]{1,0:T(8,128)(2,1)S(1)} %shard_map.69), channel_id=1, source_target_pairs={{0,3},{1,2},{2,1},{3,0},{4,7},{5,6},{6,5},{7,4},{8,11},{9,10},{10,... | collective-permute-start | bytes 442376 | tf_op jit(solution)/shard_map/ppermute | solution.py:24
  31.4 0.9 %shard_map.68 = (f32[128,512]{1,0:T(8,128)S(1)}, f32[2,128,128]{2,1,0:T(8,128)S(1)}) custom-call(s32[2,16]{1,0:T(2,128)S(1)} %shard_map.64.windows_ref, bf16[128,1024]{1,0:T(8,128)(2,1)S(1)} %copy-done.1, bf16[128,1024]{1,0:T(8,128)(2,1)S(1)} %collective-permute-done.refs_0_, bf16[144,512]{1,0:T(8,128)(2,1)S(1)} %collective-permute-done.2.refs_1_.refs_0_, ...), custom_call_target="tpu_custom_call" | custom-call | flops 268435456 | bytes 4194304 | tf_op jit(solution)/shard_map/pallas_call | solution.py:345
  32.3 3.9 %collective-permute-done.14.refs_0_ = bf16[144,512]{1,0:T(8,128)(2,1)S(1)} collective-permute-done((bf16[144,512]{1,0:T(8,128)(2,1)S(1)}, bf16[144,512]{1,0:T(8,128)(2,1)S(1)}, u32[]{:S(2)}, u32[]{:S(2)}) %collective-permute-start.14) | collective-permute-done | bytes 147488 | tf_op jit(solution)/shard_map/ppermute | solution.py:24
  36.2 0.8 %shard_map.70 = bf16[128,512]{1,0:T(8,128)(2,1)} custom-call(f32[128,512]{1,0:T(8,128)S(1)} %get-tuple-element.24.total_ref, f32[2,128,128]{2,1,0:T(8,128)S(1)} %get-tuple-element.25.stats_ref, bf16[144,512]{1,0:T(8,128)(2,1)S(1)} %collective-permute-done.14.refs_0_), custom_call_target="tpu_custom_call" | custom-call | tf_op jit(solution)/shard_map/pallas_call | solution.py:359
  (17 shorter events, 0.1 us)
Async XLA Ops:
  0.0 10.4 %copy-start.1 = (bf16[128,1024]{1,0:T(8,128)(2,1)S(1)}, bf16[128,1024]{1,0:T(8,128)(2,1)}, u32[]{:S(2)}) copy-start(bf16[128,1024]{1,0:T(8,128)(2,1)} %query_ref.1) | copy-start | bytes 786436
  0.0 4.6 %collective-permute-start.1 = (bf16[128,1024]{1,0:T(8,128)(2,1)}, bf16[128,1024]{1,0:T(8,128)(2,1)S(1)}, u32[]{:S(2)}, u32[]{:S(2)}) collective-permute-start(bf16[128,1024]{1,0:T(8,128)(2,1)} %refs_13_.1), channel_id=1, source_target_pairs={{0,4},{4,0},{8,12},{12,8},{1,5},{5,1},{9,13},{13,9},{2,6},{6,2},{1... | collective-permute-start | bytes 786440 | tf_op jit(solution)/shard_map/ppermute | solution.py:24
  0.5 9.9 %collective-permute-start.3 = (bf16[128,1024]{1,0:T(8,128)(2,1)}, bf16[128,1024]{1,0:T(8,128)(2,1)S(1)}, u32[]{:S(2)}, u32[]{:S(2)}) collective-permute-start(bf16[128,1024]{1,0:T(8,128)(2,1)} %refs_13_.1), channel_id=1, source_target_pairs={{0,8},{4,12},{8,0},{12,4},{1,9},{5,13},{9,1},{13,5},{2,10},{6,14},... | collective-permute-start | bytes 786440 | tf_op jit(solution)/shard_map/ppermute | solution.py:24
  3.0 11.4 %collective-permute-start = (bf16[128,1024]{1,0:T(8,128)(2,1)}, bf16[128,1024]{1,0:T(8,128)(2,1)S(1)}, u32[]{:S(2)}, u32[]{:S(2)}) collective-permute-start(bf16[128,1024]{1,0:T(8,128)(2,1)} %refs_13_.1), channel_id=1, source_target_pairs={{0,1},{1,0},{2,3},{3,2},{4,5},{5,4},{6,7},{7,6},{8,9},{9,8},{10,11... | collective-permute-start | bytes 786440 | tf_op jit(solution)/shard_map/ppermute | solution.py:24
  4.6 0.9 %copy-start.2 = (bf16[128,512]{1,0:T(8,128)(2,1)S(1)}, bf16[128,512]{1,0:T(8,128)(2,1)}, u32[]{:S(2)}) copy-start(bf16[128,512]{1,0:T(8,128)(2,1)} %values_ref) | copy-start | bytes 393220
  5.5 0.7 %copy-start.4 = (bf16[128]{0:T(256)(128)(2,1)S(1)}, bf16[128]{0:T(256)(128)(2,1)}, u32[]{:S(2)}) copy-start(bf16[128]{0:T(256)(128)(2,1)} %param.9) | copy-start | bytes 772
  6.3 1.9 %copy-start.3 = (s32[16,4]{0,1:T(4,128)S(1)}, s32[16,4]{0,1:T(4,128)}, u32[]{:S(2)}) copy-start(s32[16,4]{0,1:T(4,128)} %param.10) | copy-start | bytes 772
  6.3 4.1 %collective-permute-start.5 = (bf16[144,512]{1,0:T(8,128)(2,1)S(1)}, bf16[144,512]{1,0:T(8,128)(2,1)S(1)}, u32[]{:S(2)}, u32[]{:S(2)}) collective-permute-start(bf16[144,512]{1,0:T(8,128)(2,1)S(1)} %shard_map.65.refs_5_.refs_14_), channel_id=1, source_target_pairs={{0,4},{4,0},{8,12},{12,8},{1,5},{5,1},{9,13},{13,9},{2,6},{6,2},{1... | collective-permute-start | bytes 442376 | tf_op jit(solution)/shard_map/ppermute | solution.py:24
  6.4 9.5 %collective-permute-start.2 = (bf16[144,512]{1,0:T(8,128)(2,1)S(1)}, bf16[144,512]{1,0:T(8,128)(2,1)S(1)}, u32[]{:S(2)}, u32[]{:S(2)}) collective-permute-start(bf16[144,512]{1,0:T(8,128)(2,1)S(1)} %shard_map.65.refs_5_.refs_14_), channel_id=1, source_target_pairs={{0,1},{1,0},{2,3},{3,2},{4,5},{5,4},{6,7},{7,6},{8,9},{9,8},{10,11... | collective-permute-start | bytes 442376 | tf_op jit(solution)/shard_map/ppermute | solution.py:24
  6.9 9.0 %collective-permute-start.4 = (bf16[144,512]{1,0:T(8,128)(2,1)S(1)}, bf16[144,512]{1,0:T(8,128)(2,1)S(1)}, u32[]{:S(2)}, u32[]{:S(2)}) collective-permute-start(bf16[144,512]{1,0:T(8,128)(2,1)S(1)} %shard_map.65.refs_5_.refs_14_), channel_id=1, source_target_pairs={{0,8},{4,12},{8,0},{12,4},{1,9},{5,13},{9,1},{13,5},{2,10},{6,14},... | collective-permute-start | bytes 442376 | tf_op jit(solution)/shard_map/ppermute | solution.py:24
  8.2 0.7 %copy-start.5 = (s32[16]{0:T(128)S(1)}, s32[16]{0:T(128)}, u32[]{:S(2)}) copy-start(s32[16]{0:T(128)} %param.11) | copy-start | bytes 196
  8.9 13.6 %copy-start = (bf16[128,1024]{1,0:T(8,128)(2,1)S(1)}, bf16[128,1024]{1,0:T(8,128)(2,1)}, u32[]{:S(2)}) copy-start(bf16[128,1024]{1,0:T(8,128)(2,1)} %refs_13_.1) | copy-start | bytes 786436
  10.4 12.1 %collective-permute-start.8 = (bf16[128,1024]{1,0:T(8,128)(2,1)S(1)}, bf16[128,1024]{1,0:T(8,128)(2,1)S(1)}, u32[]{:S(2)}, u32[]{:S(2)}) collective-permute-start(bf16[128,1024]{1,0:T(8,128)(2,1)S(1)} %copy-done.1), channel_id=1, source_target_pairs={{0,3},{1,2},{2,1},{3,0},{4,7},{5,6},{6,5},{7,4},{8,11},{9,10},{10,... | collective-permute-start | bytes 786440 | tf_op jit(solution)/shard_map/ppermute | solution.py:24
  14.4 8.9 %collective-permute-start.6 = (bf16[128,1024]{1,0:T(8,128)(2,1)S(1)}, bf16[128,1024]{1,0:T(8,128)(2,1)S(1)}, u32[]{:S(2)}, u32[]{:S(2)}) collective-permute-start(bf16[128,1024]{1,0:T(8,128)(2,1)S(1)} %collective-permute-done.refs_0_), channel_id=1, source_target_pairs={{0,8},{4,12},{8,0},{12,4},{1,9},{5,13},{9,1},{13,5},{2,10},{6,14},... | collective-permute-start | bytes 786440 | tf_op jit(solution)/shard_map/ppermute | solution.py:24
  15.9 8.8 %collective-permute-start.7 = (bf16[144,512]{1,0:T(8,128)(2,1)S(1)}, bf16[144,512]{1,0:T(8,128)(2,1)S(1)}, u32[]{:S(2)}, u32[]{:S(2)}) collective-permute-start(bf16[144,512]{1,0:T(8,128)(2,1)S(1)} %collective-permute-done.2.refs_1_.refs_0_), channel_id=1, source_target_pairs={{0,8},{4,12},{8,0},{12,4},{1,9},{5,13},{9,1},{13,5},{2,10},{6,14},... | collective-permute-start | bytes 442376 | tf_op jit(solution)/shard_map/ppermute | solution.py:24
  16.5 8.8 %collective-permute-start.13 = (bf16[288,512]{1,0:T(8,128)(2,1)S(1)}, bf16[288,512]{1,0:T(8,128)(2,1)S(1)}, u32[]{:S(2)}, u32[]{:S(2)}) collective-permute-start(bf16[288,512]{1,0:T(8,128)(2,1)S(1)} %shard_map.67), channel_id=1, source_target_pairs={{0,4},{4,0},{8,12},{12,8},{1,5},{5,1},{9,13},{13,9},{2,6},{6,2},{1... | collective-permute-start | bytes 884744 | tf_op jit(solution)/shard_map/ppermute | solution.py:24
  16.6 8.7 %collective-permute-start.12 = (bf16[128,1024]{1,0:T(8,128)(2,1)S(1)}, bf16[128,1024]{1,0:T(8,128)(2,1)S(1)}, u32[]{:S(2)}, u32[]{:S(2)}) collective-permute-start(bf16[128,1024]{1,0:T(8,128)(2,1)S(1)} %collective-permute-done.3.refs_2_), channel_id=1, source_target_pairs={{0,4},{4,0},{8,12},{12,8},{1,5},{5,1},{9,13},{13,9},{2,6},{6,2},{1... | collective-permute-start | bytes 786440 | tf_op jit(solution)/shard_map/ppermute | solution.py:24
  22.5 2.8 %collective-permute-start.11 = (bf16[128,1024]{1,0:T(8,128)(2,1)S(1)}, bf16[128,1024]{1,0:T(8,128)(2,1)S(1)}, u32[]{:S(2)}, u32[]{:S(2)}) collective-permute-start(bf16[128,1024]{1,0:T(8,128)(2,1)S(1)} %collective-permute-done.refs_0_), channel_id=1, source_target_pairs={{0,4},{4,0},{8,12},{12,8},{1,5},{5,1},{9,13},{13,9},{2,6},{6,2},{1... | collective-permute-start | bytes 786440 | tf_op jit(solution)/shard_map/ppermute | solution.py:24
  24.7 1.8 %collective-permute-start.9 = (bf16[128,1024]{1,0:T(8,128)(2,1)S(1)}, bf16[128,1024]{1,0:T(8,128)(2,1)S(1)}, u32[]{:S(2)}, u32[]{:S(2)}) collective-permute-start(bf16[128,1024]{1,0:T(8,128)(2,1)S(1)} %collective-permute-done.6.refs_6_.refs_5_), channel_id=1, source_target_pairs={{0,4},{4,0},{8,12},{12,8},{1,5},{5,1},{9,13},{13,9},{2,6},{6,2},{1... | collective-permute-start | bytes 786440 | tf_op jit(solution)/shard_map/ppermute | solution.py:24
  24.8 1.7 %collective-permute-start.10 = (bf16[144,512]{1,0:T(8,128)(2,1)S(1)}, bf16[144,512]{1,0:T(8,128)(2,1)S(1)}, u32[]{:S(2)}, u32[]{:S(2)}) collective-permute-start(bf16[144,512]{1,0:T(8,128)(2,1)S(1)} %collective-permute-done.7.refs_7_.refs_6_), channel_id=1, source_target_pairs={{0,4},{4,0},{8,12},{12,8},{1,5},{5,1},{9,13},{13,9},{2,6},{6,2},{1... | collective-permute-start | bytes 442376 | tf_op jit(solution)/shard_map/ppermute | solution.py:24
  27.0 9.2 %collective-permute-start.14 = (bf16[144,512]{1,0:T(8,128)(2,1)S(1)}, bf16[144,512]{1,0:T(8,128)(2,1)S(1)}, u32[]{:S(2)}, u32[]{:S(2)}) collective-permute-start(bf16[144,512]{1,0:T(8,128)(2,1)S(1)} %shard_map.69), channel_id=1, source_target_pairs={{0,3},{1,2},{2,1},{3,0},{4,7},{5,6},{6,5},{7,4},{8,11},{9,10},{10,... | collective-permute-start | bytes 442376 | tf_op jit(solution)/shard_map/ppermute | solution.py:24

commit v23 on v20

--- a/solution.py
+++ b/solution.py
@@ -11,6 +11,7 @@
 TILE = 128
 LANES = 128
 EXTRA = 16
+LINES = 8
 MASKED_SCORE = -1e30
 VMEM = pl.BlockSpec(memory_space=pltpu.VMEM)
 
@@ -186,14 +187,14 @@
     value_width = total_ref.shape[1]
     inverse = 1.0 / jnp.where(row_sum > 0.0, row_sum, 1.0)
     packed_ref[0:TILE, :] = (total_ref[...] * inverse).astype(jnp.bfloat16)
-    row = lax.broadcasted_iota(jnp.int32, (EXTRA, LANES), 0)
-    packed = jnp.zeros((EXTRA, LANES), jnp.float32)
+    row = lax.broadcasted_iota(jnp.int32, (LINES, LANES), 0)
+    packed = jnp.zeros((LINES, LANES), jnp.float32)
     for first, column in ((0, row_max), (3, row_sum)):
-        turned = jnp.transpose(jnp.broadcast_to(column, (TILE, LANES)))[0:EXTRA]
+        turned = jnp.transpose(jnp.broadcast_to(column, (TILE, LANES)))[0:LINES]
         for at, part in enumerate(split_three(turned)):
             packed = jnp.where(row == first + at, part.astype(jnp.float32), packed)
     packed_ref[TILE:, 0:LANES] = packed.astype(jnp.bfloat16)
-    packed_ref[TILE:, LANES:] = jnp.zeros((EXTRA, value_width - LANES), jnp.bfloat16)
+    packed_ref[TILE:, LANES:] = jnp.zeros((LINES, value_width - LANES), jnp.bfloat16)
 
 
 def home_kernel(places, bundled, windows_ref, query_ref, *refs):
@@ -329,7 +330,7 @@
     for (mask, _), state in zip(visitors, states):
         packed = pl.pallas_call(
             functools.partial(late_kernel, places_of(late), bundled, mask),
-            out_shape=jax.ShapeDtypeStruct((TILE + EXTRA, value_width), jnp.bfloat16),
+            out_shape=jax.ShapeDtypeStruct((TILE + LINES, value_width), jnp.bfloat16),
             in_specs=[VMEM] * (5 + len(late_arrays)),
             out_specs=VMEM,
             scratch_shapes=[

time: 35.8 us -> 35.5 us (level); the launches traced: 35.8 us -> 35.1 us
  Pallas kernels: 3.73 us -> 3.16 us
    pallas_call x1, Pallas kernels: 1.02 us -> 0.48 us  [body(): pl.pallas_call(functools.partial(late_kernel, places_of(late), bundled, m...]
where the time goes in v23:
time: 35.5 us; the launch traced here: 35.1 us
  starting transfers between devices  18.4 us (52%)
  waiting for transfers between devices  11.3 us (32%)
  Pallas kernels  3.16 us (9%)
  local copies, waits for them, and re-layouts  2.23 us (6%)
    ppermute x15, starting transfers between devices, swap(): return lax.ppermute(value, axis, [(i, i ^ mask) for i in range(length)])  18.4 us
    ppermute x15, waiting for transfers between devices, swap(): return lax.ppermute(value, axis, [(i, i ^ mask) for i in range(length)])  11.3 us
    unnamed x12, local copies, waits for them, and re-layouts  2.23 us
    pallas_call x1, Pallas kernels, body(): pl.pallas_call(functools.partial(home_kernel, places_of(early + late), bu...  1.29 us
    pallas_call x1, Pallas kernels, body(): pl.pallas_call(merge_kernel, out_shape=jax.ShapeDtypeStruct((TILE, value_...  0.81 us
  transfers between devices with their start and end apart: 15, of which 6 were waited for; matrix products, arithmetic and copies ran while one was open for 0% of the time, Pallas kernels for 5%

profile of v23, /device:TPU:0, one launch (start us, length us, event | category | flops | bytes accessed | tf_op | source)
XLA Modules:
  0.0 35.1 jit_solution(13941334622279764160)
XLA Ops:
  0.0 0.5 %collective-permute-start.1 = (bf16[128,1024]{1,0:T(8,128)(2,1)}, bf16[128,1024]{1,0:T(8,128)(2,1)S(1)}, u32[]{:S(2)}, u32[]{:S(2)}) collective-permute-start(bf16[128,1024]{1,0:T(8,128)(2,1)} %refs_13_.1), channel_id=1, source_target_pairs={{0,4},{4,0},{8,12},{12,8},{1,5},{5,1},{9,13},{13,9},{2,6},{6,2},{1... | collective-permute-start | bytes 786440 | tf_op jit(solution)/shard_map/ppermute | solution.py:25
  0.5 2.6 %collective-permute-start = (bf16[128,1024]{1,0:T(8,128)(2,1)}, bf16[128,1024]{1,0:T(8,128)(2,1)S(1)}, u32[]{:S(2)}, u32[]{:S(2)}) collective-permute-start(bf16[128,1024]{1,0:T(8,128)(2,1)} %refs_13_.1), channel_id=1, source_target_pairs={{0,1},{1,0},{2,3},{3,2},{4,5},{5,4},{6,7},{7,6},{8,9},{9,8},{10,11... | collective-permute-start | bytes 786440 | tf_op jit(solution)/shard_map/ppermute | solution.py:25
  3.1 1.5 %collective-permute-start.3 = (bf16[128,1024]{1,0:T(8,128)(2,1)}, bf16[128,1024]{1,0:T(8,128)(2,1)S(1)}, u32[]{:S(2)}, u32[]{:S(2)}) collective-permute-start(bf16[128,1024]{1,0:T(8,128)(2,1)} %refs_13_.1), channel_id=1, source_target_pairs={{0,8},{4,12},{8,0},{12,4},{1,9},{5,13},{9,1},{13,5},{2,10},{6,14},... | collective-permute-start | bytes 786440 | tf_op jit(solution)/shard_map/ppermute | solution.py:25
  4.6 0.0 collective-permute-done.1.refs_4_.refs_3_
  4.6 0.9 %copy-done.2 = bf16[128,512]{1,0:T(8,128)(2,1)S(1)} copy-done((bf16[128,512]{1,0:T(8,128)(2,1)S(1)}, bf16[128,512]{1,0:T(8,128)(2,1)}, u32[]{:S(2)}) %copy-start.2) | copy-done | bytes 131096
  5.5 0.7 %copy-done.4 = bf16[128]{0:T(256)(128)(2,1)S(1)} copy-done((bf16[128]{0:T(256)(128)(2,1)S(1)}, bf16[128]{0:T(256)(128)(2,1)}, u32[]{:S(2)}) %copy-start.4) | copy-done | bytes 280
  6.1 0.2 shard_map.65.refs_5_.refs_14_
  6.3 0.0 copy-start.3
  6.3 0.1 collective-permute-start.5
  6.4 0.5 %collective-permute-start.2 = (bf16[144,512]{1,0:T(8,128)(2,1)S(1)}, bf16[144,512]{1,0:T(8,128)(2,1)S(1)}, u32[]{:S(2)}, u32[]{:S(2)}) collective-permute-start(bf16[144,512]{1,0:T(8,128)(2,1)S(1)} %shard_map.65.refs_5_.refs_14_), channel_id=1, source_target_pairs={{0,1},{1,0},{2,3},{3,2},{4,5},{5,4},{6,7},{7,6},{8,9},{9,8},{10,11... | collective-permute-start | bytes 442376 | tf_op jit(solution)/shard_map/ppermute | solution.py:25
  6.9 1.3 %collective-permute-start.4 = (bf16[144,512]{1,0:T(8,128)(2,1)S(1)}, bf16[144,512]{1,0:T(8,128)(2,1)S(1)}, u32[]{:S(2)}, u32[]{:S(2)}) collective-permute-start(bf16[144,512]{1,0:T(8,128)(2,1)S(1)} %shard_map.65.refs_5_.refs_14_), channel_id=1, source_target_pairs={{0,8},{4,12},{8,0},{12,4},{1,9},{5,13},{9,1},{13,5},{2,10},{6,14},... | collective-permute-start | bytes 442376 | tf_op jit(solution)/shard_map/ppermute | solution.py:25
  8.2 0.7 %copy-done.5 = s32[16]{0:T(128)S(1)} copy-done((s32[16]{0:T(128)S(1)}, s32[16]{0:T(128)}, u32[]{:S(2)}) %copy-start.5) | copy-done | bytes 88
  8.9 0.0 collective-permute-done.5.refs_5_.refs_4_
  8.9 2.9 %collective-permute-start.8 = (bf16[128,1024]{1,0:T(8,128)(2,1)S(1)}, bf16[128,1024]{1,0:T(8,128)(2,1)S(1)}, u32[]{:S(2)}, u32[]{:S(2)}) collective-permute-start(bf16[128,1024]{1,0:T(8,128)(2,1)S(1)} %copy-done.1), channel_id=1, source_target_pairs={{0,3},{1,2},{2,1},{3,0},{4,7},{5,6},{6,5},{7,4},{8,11},{9,10},{10,... | collective-permute-start | bytes 786440 | tf_op jit(solution)/shard_map/ppermute | solution.py:25
  11.8 0.0 collective-permute-done.refs_0_
  11.8 0.6 %collective-permute-done.3.refs_2_ = bf16[128,1024]{1,0:T(8,128)(2,1)S(1)} collective-permute-done((bf16[128,1024]{1,0:T(8,128)(2,1)}, bf16[128,1024]{1,0:T(8,128)(2,1)S(1)}, u32[]{:S(2)}, u32[]{:S(2)}) %collective-permute-start.3) | collective-permute-done | bytes 262176 | tf_op jit(solution)/shard_map/ppermute | solution.py:25
  12.5 1.5 %collective-permute-start.6 = (bf16[128,1024]{1,0:T(8,128)(2,1)S(1)}, bf16[128,1024]{1,0:T(8,128)(2,1)S(1)}, u32[]{:S(2)}, u32[]{:S(2)}) collective-permute-start(bf16[128,1024]{1,0:T(8,128)(2,1)S(1)} %collective-permute-done.refs_0_), channel_id=1, source_target_pairs={{0,8},{4,12},{8,0},{12,4},{1,9},{5,13},{9,1},{13,5},{2,10},{6,14},... | collective-permute-start | bytes 786440 | tf_op jit(solution)/shard_map/ppermute | solution.py:25
  13.9 1.7 %collective-permute-done.4.refs_3_.refs_1_ = bf16[144,512]{1,0:T(8,128)(2,1)S(1)} collective-permute-done((bf16[144,512]{1,0:T(8,128)(2,1)S(1)}, bf16[144,512]{1,0:T(8,128)(2,1)S(1)}, u32[]{:S(2)}, u32[]{:S(2)}) %collective-permute-start.4) | collective-permute-done | bytes 147488 | tf_op jit(solution)/shard_map/ppermute | solution.py:25
  15.6 1.5 %collective-permute-start.7 = (bf16[144,512]{1,0:T(8,128)(2,1)S(1)}, bf16[144,512]{1,0:T(8,128)(2,1)S(1)}, u32[]{:S(2)}, u32[]{:S(2)}) collective-permute-start(bf16[144,512]{1,0:T(8,128)(2,1)S(1)} %collective-permute-done.2.refs_1_.refs_0_), channel_id=1, source_target_pairs={{0,8},{4,12},{8,0},{12,4},{1,9},{5,13},{9,1},{13,5},{2,10},{6,14},... | collective-permute-start | bytes 442376 | tf_op jit(solution)/shard_map/ppermute | solution.py:25
  17.1 0.1 collective-permute-start.13
  17.2 0.5 %collective-permute-start.11 = (bf16[128,1024]{1,0:T(8,128)(2,1)S(1)}, bf16[128,1024]{1,0:T(8,128)(2,1)S(1)}, u32[]{:S(2)}, u32[]{:S(2)}) collective-permute-start(bf16[128,1024]{1,0:T(8,128)(2,1)S(1)} %collective-permute-done.refs_0_), channel_id=1, source_target_pairs={{0,4},{4,0},{8,12},{12,8},{1,5},{5,1},{9,13},{13,9},{2,6},{6,2},{1... | collective-permute-start | bytes 786440 | tf_op jit(solution)/shard_map/ppermute | solution.py:25
  17.7 3.6 %collective-permute-done.8.query_ref = bf16[128,1024]{1,0:T(8,128)(2,1)S(1)} collective-permute-done((bf16[128,1024]{1,0:T(8,128)(2,1)S(1)}, bf16[128,1024]{1,0:T(8,128)(2,1)S(1)}, u32[]{:S(2)}, u32[]{:S(2)}) %collective-permute-start.8) | collective-permute-done | bytes 262176 | tf_op jit(solution)/shard_map/ppermute | solution.py:25
  21.3 0.4 %shard_map.66 = (bf16[1024,128]{1,0:T(8,128)(2,1)S(1)}, f32[128,512]{1,0:T(8,128)S(1)}, f32[128,128]{1,0:T(8,128)S(1)}, f32[128,128]{1,0:T(8,128)S(1)}) custom-call(s32[2,16]{1,0:T(2,128)S(1)} %shard_map.64.windows_ref, bf16[128,1024]{1,0:T(8,128)(2,1)S(1)} %collective-permute-done.8.query_ref, bf16[128,1024]{1,0:T(8,128)(2,1)S(1)} %collective-permute-done.refs_0_, ...), custom_call_target="tpu_custom_call" | custom-call | flops 268435456 | bytes 4194304 | tf_op jit(solution)/shard_map/pallas_call | solution.py:305
  21.7 1.9 %collective-permute-done.7.refs_7_.refs_6_ = bf16[144,512]{1,0:T(8,128)(2,1)S(1)} collective-permute-done((bf16[144,512]{1,0:T(8,128)(2,1)S(1)}, bf16[144,512]{1,0:T(8,128)(2,1)S(1)}, u32[]{:S(2)}, u32[]{:S(2)}) %collective-permute-start.7) | collective-permute-done | bytes 147488 | tf_op jit(solution)/shard_map/ppermute | solution.py:25
  23.6 0.0 collective-permute-start.9
  23.6 0.5 %collective-permute-start.10 = (bf16[144,512]{1,0:T(8,128)(2,1)S(1)}, bf16[144,512]{1,0:T(8,128)(2,1)S(1)}, u32[]{:S(2)}, u32[]{:S(2)}) collective-permute-start(bf16[144,512]{1,0:T(8,128)(2,1)S(1)} %collective-permute-done.7.refs_7_.refs_6_), channel_id=1, source_target_pairs={{0,4},{4,0},{8,12},{12,8},{1,5},{5,1},{9,13},{13,9},{2,6},{6,2},{1... | collective-permute-start | bytes 442376 | tf_op jit(solution)/shard_map/ppermute | solution.py:25
  24.1 1.2 %collective-permute-done.10.refs_9_.refs_8_ = bf16[144,512]{1,0:T(8,128)(2,1)S(1)} collective-permute-done((bf16[144,512]{1,0:T(8,128)(2,1)S(1)}, bf16[144,512]{1,0:T(8,128)(2,1)S(1)}, u32[]{:S(2)}, u32[]{:S(2)}) %collective-permute-start.10) | collective-permute-done | bytes 147488 | tf_op jit(solution)/shard_map/ppermute | solution.py:25
  25.4 0.5 %shard_map.69 = bf16[136,512]{1,0:T(8,128)(2,1)S(1)} custom-call(s32[2,16]{1,0:T(2,128)S(1)} %shard_map.64.windows_ref, bf16[1024,128]{1,0:T(8,128)(2,1)S(1)} %get-tuple-element.26.turned_ref, f32[128,512]{1,0:T(8,128)S(1)} %get-tuple-element.27.refs_0_, f32[128,128]{1,0:T(8,128)S(1)} %get-tuple-element.28.refs_1_, ...), custom_call_target="tpu_custom_call" | custom-call | flops 268435456 | bytes 4194304 | tf_op jit(solution)/shard_map/pallas_call | solution.py:331
  25.8 4.9 %collective-permute-start.14 = (bf16[136,512]{1,0:T(8,128)(2,1)S(1)}, bf16[136,512]{1,0:T(8,128)(2,1)S(1)}, u32[]{:S(2)}, u32[]{:S(2)}) collective-permute-start(bf16[136,512]{1,0:T(8,128)(2,1)S(1)} %shard_map.69), channel_id=1, source_target_pairs={{0,3},{1,2},{2,1},{3,0},{4,7},{5,6},{6,5},{7,4},{8,11},{9,10},{10,... | collective-permute-start | bytes 417800 | tf_op jit(solution)/shard_map/ppermute | solution.py:25
  30.8 1.3 %shard_map.68 = (f32[128,512]{1,0:T(8,128)S(1)}, f32[2,128,128]{2,1,0:T(8,128)S(1)}) custom-call(s32[2,16]{1,0:T(2,128)S(1)} %shard_map.64.windows_ref, bf16[128,1024]{1,0:T(8,128)(2,1)S(1)} %copy-done.1, bf16[128,1024]{1,0:T(8,128)(2,1)S(1)} %collective-permute-done.refs_0_, bf16[144,512]{1,0:T(8,128)(2,1)S(1)} %collective-permute-done.2.refs_1_.refs_0_, ...), custom_call_target="tpu_custom_call" | custom-call | flops 268435456 | bytes 4194304 | tf_op jit(solution)/shard_map/pallas_call | solution.py:346
  32.1 2.2 %collective-permute-done.14.refs_0_ = bf16[136,512]{1,0:T(8,128)(2,1)S(1)} collective-permute-done((bf16[136,512]{1,0:T(8,128)(2,1)S(1)}, bf16[136,512]{1,0:T(8,128)(2,1)S(1)}, u32[]{:S(2)}, u32[]{:S(2)}) %collective-permute-start.14) | collective-permute-done | bytes 139296 | tf_op jit(solution)/shard_map/ppermute | solution.py:25
  34.3 0.8 %shard_map.70 = bf16[128,512]{1,0:T(8,128)(2,1)} custom-call(f32[128,512]{1,0:T(8,128)S(1)} %get-tuple-element.24.total_ref, f32[2,128,128]{2,1,0:T(8,128)S(1)} %get-tuple-element.25.stats_ref, bf16[136,512]{1,0:T(8,128)(2,1)S(1)} %collective-permute-done.14.refs_0_), custom_call_target="tpu_custom_call" | custom-call | tf_op jit(solution)/shard_map/pallas_call | solution.py:360
  (17 shorter events, 0.1 us)
Async XLA Ops:
  0.0 8.9 %copy-start.1 = (bf16[128,1024]{1,0:T(8,128)(2,1)S(1)}, bf16[128,1024]{1,0:T(8,128)(2,1)}, u32[]{:S(2)}) copy-start(bf16[128,1024]{1,0:T(8,128)(2,1)} %query_ref.1) | copy-start | bytes 786436
  0.0 4.6 %collective-permute-start.1 = (bf16[128,1024]{1,0:T(8,128)(2,1)}, bf16[128,1024]{1,0:T(8,128)(2,1)S(1)}, u32[]{:S(2)}, u32[]{:S(2)}) collective-permute-start(bf16[128,1024]{1,0:T(8,128)(2,1)} %refs_13_.1), channel_id=1, source_target_pairs={{0,4},{4,0},{8,12},{12,8},{1,5},{5,1},{9,13},{13,9},{2,6},{6,2},{1... | collective-permute-start | bytes 786440 | tf_op jit(solution)/shard_map/ppermute | solution.py:25
  0.5 11.3 %collective-permute-start = (bf16[128,1024]{1,0:T(8,128)(2,1)}, bf16[128,1024]{1,0:T(8,128)(2,1)S(1)}, u32[]{:S(2)}, u32[]{:S(2)}) collective-permute-start(bf16[128,1024]{1,0:T(8,128)(2,1)} %refs_13_.1), channel_id=1, source_target_pairs={{0,1},{1,0},{2,3},{3,2},{4,5},{5,4},{6,7},{7,6},{8,9},{9,8},{10,11... | collective-permute-start | bytes 786440 | tf_op jit(solution)/shard_map/ppermute | solution.py:25
  3.1 9.4 %collective-permute-start.3 = (bf16[128,1024]{1,0:T(8,128)(2,1)}, bf16[128,1024]{1,0:T(8,128)(2,1)S(1)}, u32[]{:S(2)}, u32[]{:S(2)}) collective-permute-start(bf16[128,1024]{1,0:T(8,128)(2,1)} %refs_13_.1), channel_id=1, source_target_pairs={{0,8},{4,12},{8,0},{12,4},{1,9},{5,13},{9,1},{13,5},{2,10},{6,14},... | collective-permute-start | bytes 786440 | tf_op jit(solution)/shard_map/ppermute | solution.py:25
  4.6 0.9 %copy-start.2 = (bf16[128,512]{1,0:T(8,128)(2,1)S(1)}, bf16[128,512]{1,0:T(8,128)(2,1)}, u32[]{:S(2)}) copy-start(bf16[128,512]{1,0:T(8,128)(2,1)} %values_ref) | copy-start | bytes 393220
  5.5 0.7 %copy-start.4 = (bf16[128]{0:T(256)(128)(2,1)S(1)}, bf16[128]{0:T(256)(128)(2,1)}, u32[]{:S(2)}) copy-start(bf16[128]{0:T(256)(128)(2,1)} %param.9) | copy-start | bytes 772
  6.3 1.9 %copy-start.3 = (s32[16,4]{0,1:T(4,128)S(1)}, s32[16,4]{0,1:T(4,128)}, u32[]{:S(2)}) copy-start(s32[16,4]{0,1:T(4,128)} %param.10) | copy-start | bytes 772
  6.3 2.6 %collective-permute-start.5 = (bf16[144,512]{1,0:T(8,128)(2,1)S(1)}, bf16[144,512]{1,0:T(8,128)(2,1)S(1)}, u32[]{:S(2)}, u32[]{:S(2)}) collective-permute-start(bf16[144,512]{1,0:T(8,128)(2,1)S(1)} %shard_map.65.refs_5_.refs_14_), channel_id=1, source_target_pairs={{0,4},{4,0},{8,12},{12,8},{1,5},{5,1},{9,13},{13,9},{2,6},{6,2},{1... | collective-permute-start | bytes 442376 | tf_op jit(solution)/shard_map/ppermute | solution.py:25
  6.4 7.5 %collective-permute-start.2 = (bf16[144,512]{1,0:T(8,128)(2,1)S(1)}, bf16[144,512]{1,0:T(8,128)(2,1)S(1)}, u32[]{:S(2)}, u32[]{:S(2)}) collective-permute-start(bf16[144,512]{1,0:T(8,128)(2,1)S(1)} %shard_map.65.refs_5_.refs_14_), channel_id=1, source_target_pairs={{0,1},{1,0},{2,3},{3,2},{4,5},{5,4},{6,7},{7,6},{8,9},{9,8},{10,11... | collective-permute-start | bytes 442376 | tf_op jit(solution)/shard_map/ppermute | solution.py:25
  6.9 8.7 %collective-permute-start.4 = (bf16[144,512]{1,0:T(8,128)(2,1)S(1)}, bf16[144,512]{1,0:T(8,128)(2,1)S(1)}, u32[]{:S(2)}, u32[]{:S(2)}) collective-permute-start(bf16[144,512]{1,0:T(8,128)(2,1)S(1)} %shard_map.65.refs_5_.refs_14_), channel_id=1, source_target_pairs={{0,8},{4,12},{8,0},{12,4},{1,9},{5,13},{9,1},{13,5},{2,10},{6,14},... | collective-permute-start | bytes 442376 | tf_op jit(solution)/shard_map/ppermute | solution.py:25
  8.2 0.7 %copy-start.5 = (s32[16]{0:T(128)S(1)}, s32[16]{0:T(128)}, u32[]{:S(2)}) copy-start(s32[16]{0:T(128)} %param.11) | copy-start | bytes 196
  8.9 12.4 %copy-start = (bf16[128,1024]{1,0:T(8,128)(2,1)S(1)}, bf16[128,1024]{1,0:T(8,128)(2,1)}, u32[]{:S(2)}) copy-start(bf16[128,1024]{1,0:T(8,128)(2,1)} %refs_13_.1) | copy-start | bytes 786436
  8.9 12.4 %collective-permute-start.8 = (bf16[128,1024]{1,0:T(8,128)(2,1)S(1)}, bf16[128,1024]{1,0:T(8,128)(2,1)S(1)}, u32[]{:S(2)}, u32[]{:S(2)}) collective-permute-start(bf16[128,1024]{1,0:T(8,128)(2,1)S(1)} %copy-done.1), channel_id=1, source_target_pairs={{0,3},{1,2},{2,1},{3,0},{4,7},{5,6},{6,5},{7,4},{8,11},{9,10},{10,... | collective-permute-start | bytes 786440 | tf_op jit(solution)/shard_map/ppermute | solution.py:25
  12.5 9.3 %collective-permute-start.6 = (bf16[128,1024]{1,0:T(8,128)(2,1)S(1)}, bf16[128,1024]{1,0:T(8,128)(2,1)S(1)}, u32[]{:S(2)}, u32[]{:S(2)}) collective-permute-start(bf16[128,1024]{1,0:T(8,128)(2,1)S(1)} %collective-permute-done.refs_0_), channel_id=1, source_target_pairs={{0,8},{4,12},{8,0},{12,4},{1,9},{5,13},{9,1},{13,5},{2,10},{6,14},... | collective-permute-start | bytes 786440 | tf_op jit(solution)/shard_map/ppermute | solution.py:25
  15.6 8.0 %collective-permute-start.7 = (bf16[144,512]{1,0:T(8,128)(2,1)S(1)}, bf16[144,512]{1,0:T(8,128)(2,1)S(1)}, u32[]{:S(2)}, u32[]{:S(2)}) collective-permute-start(bf16[144,512]{1,0:T(8,128)(2,1)S(1)} %collective-permute-done.2.refs_1_.refs_0_), channel_id=1, source_target_pairs={{0,8},{4,12},{8,0},{12,4},{1,9},{5,13},{9,1},{13,5},{2,10},{6,14},... | collective-permute-start | bytes 442376 | tf_op jit(solution)/shard_map/ppermute | solution.py:25
  17.1 7.0 %collective-permute-start.13 = (bf16[288,512]{1,0:T(8,128)(2,1)S(1)}, bf16[288,512]{1,0:T(8,128)(2,1)S(1)}, u32[]{:S(2)}, u32[]{:S(2)}) collective-permute-start(bf16[288,512]{1,0:T(8,128)(2,1)S(1)} %shard_map.67), channel_id=1, source_target_pairs={{0,4},{4,0},{8,12},{12,8},{1,5},{5,1},{9,13},{13,9},{2,6},{6,2},{1... | collective-permute-start | bytes 884744 | tf_op jit(solution)/shard_map/ppermute | solution.py:25
  17.2 6.9 %collective-permute-start.11 = (bf16[128,1024]{1,0:T(8,128)(2,1)S(1)}, bf16[128,1024]{1,0:T(8,128)(2,1)S(1)}, u32[]{:S(2)}, u32[]{:S(2)}) collective-permute-start(bf16[128,1024]{1,0:T(8,128)(2,1)S(1)} %collective-permute-done.refs_0_), channel_id=1, source_target_pairs={{0,4},{4,0},{8,12},{12,8},{1,5},{5,1},{9,13},{13,9},{2,6},{6,2},{1... | collective-permute-start | bytes 786440 | tf_op jit(solution)/shard_map/ppermute | solution.py:25
  21.3 2.8 %collective-permute-start.12 = (bf16[128,1024]{1,0:T(8,128)(2,1)S(1)}, bf16[128,1024]{1,0:T(8,128)(2,1)S(1)}, u32[]{:S(2)}, u32[]{:S(2)}) collective-permute-start(bf16[128,1024]{1,0:T(8,128)(2,1)S(1)} %collective-permute-done.3.refs_2_), channel_id=1, source_target_pairs={{0,4},{4,0},{8,12},{12,8},{1,5},{5,1},{9,13},{13,9},{2,6},{6,2},{1... | collective-permute-start | bytes 786440 | tf_op jit(solution)/shard_map/ppermute | solution.py:25
  23.6 1.8 %collective-permute-start.9 = (bf16[128,1024]{1,0:T(8,128)(2,1)S(1)}, bf16[128,1024]{1,0:T(8,128)(2,1)S(1)}, u32[]{:S(2)}, u32[]{:S(2)}) collective-permute-start(bf16[128,1024]{1,0:T(8,128)(2,1)S(1)} %collective-permute-done.6.refs_6_.refs_5_), channel_id=1, source_target_pairs={{0,4},{4,0},{8,12},{12,8},{1,5},{5,1},{9,13},{13,9},{2,6},{6,2},{1... | collective-permute-start | bytes 786440 | tf_op jit(solution)/shard_map/ppermute | solution.py:25
  23.6 1.7 %collective-permute-start.10 = (bf16[144,512]{1,0:T(8,128)(2,1)S(1)}, bf16[144,512]{1,0:T(8,128)(2,1)S(1)}, u32[]{:S(2)}, u32[]{:S(2)}) collective-permute-start(bf16[144,512]{1,0:T(8,128)(2,1)S(1)} %collective-permute-done.7.refs_7_.refs_6_), channel_id=1, source_target_pairs={{0,4},{4,0},{8,12},{12,8},{1,5},{5,1},{9,13},{13,9},{2,6},{6,2},{1... | collective-permute-start | bytes 442376 | tf_op jit(solution)/shard_map/ppermute | solution.py:25
  25.8 8.4 %collective-permute-start.14 = (bf16[136,512]{1,0:T(8,128)(2,1)S(1)}, bf16[136,512]{1,0:T(8,128)(2,1)S(1)}, u32[]{:S(2)}, u32[]{:S(2)}) collective-permute-start(bf16[136,512]{1,0:T(8,128)(2,1)S(1)} %shard_map.69), channel_id=1, source_target_pairs={{0,3},{1,2},{2,1},{3,0},{4,7},{5,6},{6,5},{7,4},{8,11},{9,10},{10,... | collective-permute-start | bytes 417800 | tf_op jit(solution)/shard_map/ppermute | solution.py:25
